TPU v7x, 32 devices: a whole 2x2x4 slice. The times are simulated.
32 devices in a mesh: groups: 2 (over y), leaf: 2 (over x), sub: 4 (over z), rep: 2 (over core).
Axes of the slice: x: 2, y: 2, z: 4, core: 2. Of those that a mesh axis runs over, the one named last changes fastest.
Arguments:
- points: float32 [16384, 64], P(('groups', 'leaf', 'sub')), parts along dimension 0, may hold values from -12 to 12
- weights: float32 [16384, 256], P(('groups', 'leaf', 'sub'), 'rep'), parts along dimension 0, may hold values from -6 to 6
- tree_slot: int32 [16384], P(('groups', 'leaf', 'sub')), parts along dimension 0, may hold values from 0 to 8191, as said below
- near_count: int32 [4, 8], P(('groups', 'leaf')), parts along dimension 0, may hold values from 1 to 16, 32 in all within a row
- near_list: int32 [4, 8, 16], P(('groups', 'leaf')), parts along dimension 0, may hold values from 0 to 7
- skeleton_base: int32 [16, 128], P(('groups', 'leaf', 'sub')), parts along dimension 0, may hold values from 0 to 1023, as said below
- skeleton_upper: int32 [12, 128], P('groups'), parts along dimension 0, may hold values from 0 to 255, as said below
- far_use: int32 [32, 3], P(('groups', 'leaf', 'sub')), parts along dimension 0, may hold values 0 or 1
Outputs:
- result: float32 [16384, 256], P(('groups', 'leaf', 'sub'), 'rep'), parts along dimension 0
There are 2 independent parts, one for each index of `groups`. A program takes and returns all parts, laid end to end along the dimension named above; each array names one. Nothing has to cross between parts.
Inputs may be any that keep to these rules, and one draw needn't show every extreme that they name: `tree_slot`: A permutation; each device block's input rows hold exactly 128 points of every device block of the tree. `near_count`: the counts of one subtree sum to 32. `near_list`: only the first near_count slots of a leaf are read; entries may repeat. `skeleton_base`: entries of a row are distinct. `skeleton_upper`: entries of a row are distinct; node j of level l is row 8 - (8 >> (l - 1)) + j.
All inputs are finite; a program needn't handle non-finite values. No bound on the sum of `far_use` on one device may be relied on, other than what follows from the above.
Results may differ from a plain program's by a relative error of at most 0.0028.
Values sent between devices are 32-bit elements; how exact they have to be, the bound alone decides.
No kernel may reach another device: no remote copies, remote signals or barrier semaphores. Data moves between devices by JAX's collectives and lax.ppermute only.
A program may use at most 64 MiB of HBM per device.

v0:
```python
import jax
import jax.numpy as jnp
from jax import lax
from jax.sharding import PartitionSpec as P

DIM = 64
LEAF = 512


highest = lax.Precision.HIGHEST
kernel_scale = 1.0 / 32.0
ridge = 0.5


def from_partner(value, axis, stride):
    return lax.ppermute(value, axis, [(i, i ^ 1 << stride) for i in range(lax.axis_size(axis))])


def kernel(targets, sources):
    inner = jnp.dot(targets, sources.T, precision=highest, preferred_element_type=jnp.float32)
    distance = (
        jnp.sum(targets * targets, axis=1)[:, None]
        + jnp.sum(sources * sources, axis=1)[None, :]
        - 2.0 * inner
    )
    return jnp.exp(-kernel_scale * distance)


def body(points, weights, tree_slot, near_count, near_list, skeleton_base, skeleton_upper, far_use):
    devices = lax.axis_size(("leaf", "sub"))
    rows = points.shape[0]
    per_peer = rows // devices
    leaves = rows // LEAF
    levels = devices.bit_length() - 1
    order = jnp.argsort(tree_slot // rows, stable=True)
    send_points = points[order].reshape(devices, per_peer, DIM)
    send_weights = weights[order].reshape(devices, per_peer, weights.shape[1])
    send_slots = (tree_slot[order] % rows).astype(jnp.float32).reshape(devices, per_peer)
    got_points, got_weights, got_slots = (
        lax.all_to_all(send_points, ("leaf", "sub"), split_axis=0, concat_axis=0, tiled=True),
        lax.all_to_all(send_weights, ("leaf", "sub"), split_axis=0, concat_axis=0, tiled=True),
        lax.all_to_all(send_slots, ("leaf", "sub"), split_axis=0, concat_axis=0, tiled=True),
    )
    places = got_slots.reshape(rows).astype(jnp.int32)
    tree_points = jnp.zeros((rows, DIM), jnp.float32).at[places].set(got_points.reshape(rows, DIM))
    tree_weights = (
        jnp.zeros((rows, weights.shape[1]), jnp.float32)
        .at[places]
        .set(got_weights.reshape(rows, weights.shape[1]))
    )
    span = LEAF
    columns = tree_weights.shape[1]
    light = tree_weights.astype(jnp.bfloat16)

    def pick(array):
        return array.reshape(leaves, LEAF, array.shape[-1])

    sub_points, sub_weights = (
        lax.all_gather(tree_points, "sub", axis=0, tiled=True),
        lax.all_gather(tree_weights, "sub", axis=0, tiled=True),
    )
    sub_light = sub_weights.astype(jnp.bfloat16)
    my_sub = lax.axis_index("sub")
    first_leaf = my_sub * leaves
    counts = near_count[0]
    lists = near_list[0]
    own_blocks = tree_points.reshape(leaves, LEAF, DIM)
    target_blocks = pick(tree_points)

    def leaf_term(target_points, source_leaf):
        sources = lax.dynamic_slice_in_dim(sub_points, source_leaf * LEAF, LEAF, 0)
        source_light = lax.dynamic_slice_in_dim(sub_light, source_leaf * LEAF, LEAF, 0)
        block = kernel(target_points, sources).astype(jnp.bfloat16)
        return jnp.dot(block, source_light, preferred_element_type=jnp.float32)

    def self_term(target_points, place, value):
        block = kernel(target_points, place).astype(jnp.bfloat16)
        return jnp.dot(block, value, preferred_element_type=jnp.float32)

    self_part = jax.vmap(self_term)(target_blocks, own_blocks, light.reshape(leaves, LEAF, columns))
    mine = lax.dynamic_slice_in_dim(counts, first_leaf, leaves, 0)
    my_lists = lax.dynamic_slice_in_dim(lists, first_leaf, leaves, 0)

    def one_slot(slot, total):
        sources = lax.dynamic_index_in_dim(my_lists, slot, 1, keepdims=False)
        terms = jax.vmap(leaf_term)(target_blocks, sources)
        live = (slot < mine).astype(jnp.float32)[:, None, None]
        return total + terms * live

    near = lax.fori_loop(
        0, jnp.max(mine), one_slot, jnp.zeros((leaves, span, columns), jnp.float32)
    )
    device = lax.axis_index(("leaf", "sub"))
    own_points = tree_points[skeleton_base[0]]
    own_coefs = jnp.dot(
        kernel(own_points, tree_points).astype(jnp.bfloat16),
        light,
        preferred_element_type=jnp.float32,
    )
    flags = far_use.astype(jnp.float32)
    target_flat = target_blocks.reshape(leaves * span, DIM)
    far = jnp.zeros((leaves * span, columns), jnp.float32)
    offset = 0
    for level in range(levels):
        other_points, other_coefs = from_partner((own_points, own_coefs), ("leaf", "sub"), level)
        block = kernel(target_flat, other_points)
        term = jnp.dot(block, other_coefs, precision=highest, preferred_element_type=jnp.float32)
        far = far + term * jnp.repeat(flags[:, level], span)[:, None]
        if level + 1 < levels:
            second = device >> level & 1 == 1
            pair_points = jnp.where(
                second,
                jnp.concatenate([other_points, own_points], 0),
                jnp.concatenate([own_points, other_points], 0),
            )
            pair_coefs = jnp.where(
                second,
                jnp.concatenate([other_coefs, own_coefs], 0),
                jnp.concatenate([own_coefs, other_coefs], 0),
            )
            chosen = skeleton_upper[offset + (device >> level + 1)]
            offset += devices >> level + 1
            own_points = pair_points[chosen]
            own_coefs = jnp.dot(
                kernel(own_points, pair_points),
                pair_coefs,
                precision=highest,
                preferred_element_type=jnp.float32,
            )
    partial_result = (
        ridge * pick(tree_weights) + self_part + near + far.reshape(leaves, span, columns)
    )
    tree_result = partial_result.reshape(rows, columns)
    narrow = tree_result.shape[1]
    leaving = tree_result[places].reshape(devices, per_peer, narrow)
    back = lax.all_to_all(leaving, ("leaf", "sub"), split_axis=0, concat_axis=0, tiled=True)
    return jnp.zeros((rows, narrow), jnp.float32).at[order].set(back.reshape(rows, narrow))


def solution(mesh):
    in_specs = (
        P(("groups", "leaf", "sub"), None),
        P(("groups", "leaf", "sub"), "rep"),
        P(("groups", "leaf", "sub")),
        P(("groups", "leaf"), None),
        P(("groups", "leaf"), None, None),
        P(("groups", "leaf", "sub"), None),
        P("groups", None),
        P(("groups", "leaf", "sub"), None),
    )
    out_specs = P(("groups", "leaf", "sub"), "rep")
    return jax.shard_map(body, mesh=mesh, in_specs=in_specs, out_specs=out_specs, check_vma=False)
```

profile of v0, /device:TPU:0, one launch (start us, length us, event | category | flops | bytes accessed | tf_op | source)
XLA Modules:
  0.0 310.0 jit_solution(3154496878285650360)
XLA Ops:
  7.3 4.4 %sort.17 = (s32[1024]{0:T(1024)}, s32[1024]{0:T(1024)S(1)}) sort(s32[1024]{0:T(1024)S(1)} %add_select_fusion, s32[1024]{0:T(1024)S(1)} %iota.4), dimensions={0}, to_apply=%region_0.1 | sort | flops 10240 | bytes 16384 | tf_op jit(solution)/shard_map/jit(argsort)/sort | solution.py:35
  11.7 4.5 %gather_fusion = s32[1024]{0:T(1024)S(1)} fusion(s32[1024]{0:T(1024)S(1)} %copy-done.1, s32[1024]{0:T(1024)S(1)} %get-tuple-element.180), kind=kCustom, calls=%fused_computation | custom fusion | bytes 12288 | tf_op jit(solution)/shard_map/gather | solution.py:38
  16.8 7.3 %all-to-all-start = ((f32[8,1,128]{2,1,0:T(1,128)}), f32[8,1,128]{2,1,0:T(1,128)S(1)}, u32[]{:S(2)}, u32[]{:S(2)}) async-start(f32[8,1,128]{2,1,0:T(1,128)} %fusion.59), calls=%async_computation | async-start | bytes 8192 | tf_op jit(solution)/shard_map/all_to_all | solution.py:42
  24.1 4.0 %gather_fusion.1 = f32[1024,128]{1,0:T(8,128)} fusion(f32[1024,128]{1,0:T(8,128)S(1)} %copy-done, s32[1024]{0:T(1024)S(1)} %get-tuple-element.180), kind=kCustom, calls=%fused_computation.1 | custom fusion | bytes 1052672 | tf_op jit(solution)/shard_map/gather | solution.py:37
  30.5 3.7 %all-to-all-start.1 = ((f32[8,128,128]{2,1,0:T(8,128)}), f32[8,128,128]{2,1,0:T(8,128)S(1)}, u32[]{:S(2)}, u32[]{:S(2)}) async-start(f32[8,128,128]{2,1,0:T(8,128)} %bitcast.4), calls=%async_computation.1 | async-start | bytes 1048576 | tf_op jit(solution)/shard_map/all_to_all | solution.py:41
  34.3 14.8 %all-to-all-done.1 = f32[8,128,128]{2,1,0:T(8,128)S(1)} async-done(((f32[8,128,128]{2,1,0:T(8,128)}), f32[8,128,128]{2,1,0:T(8,128)S(1)}, u32[]{:S(2)}, u32[]{:S(2)}) %all-to-all-start.1) | async-done | bytes 524320 | tf_op jit(solution)/shard_map/all_to_all | solution.py:41
  49.1 3.9 %scatter_custom_fusion = f32[1024,128]{1,0:T(8,128)} fusion(s32[1024]{0:T(1024)S(1)} %bitcast.129, f32[1024,128]{1,0:T(8,128)S(1)} %bitcast.122, f32[]{:T(128)} %constant.95.clone.1), kind=kCustom, calls=%fused_computation.74 | custom fusion | bytes 524292 | tf_op jit(solution)/shard_map/scatter | solution.py:49
  53.2 2.8 gather_fusion.2
  56.9 3.4 %all-to-all-start.2 = ((f32[8,128,64]{1,2,0:T(8,128)}), f32[8,128,64]{1,2,0:T(8,128)S(1)}, u32[]{:S(2)}, u32[]{:S(2)}) async-start(f32[8,128,64]{1,2,0:T(8,128)} %copy.14), calls=%async_computation.2 | async-start | bytes 524288 | tf_op jit(solution)/shard_map/all_to_all | solution.py:40
  63.1 15.0 %all-to-all-done.2 = f32[8,128,64]{1,2,0:T(8,128)S(1)} async-done(((f32[8,128,64]{1,2,0:T(8,128)}), f32[8,128,64]{1,2,0:T(8,128)S(1)}, u32[]{:S(2)}, u32[]{:S(2)}) %all-to-all-start.2) | async-done | bytes 262176 | tf_op jit(solution)/shard_map/all_to_all | solution.py:40
  78.3 3.4 %scatter_custom_fusion.1 = f32[1024,64]{1,0:T(8,128)S(1)} fusion(s32[1024]{0:T(1024)S(1)} %bitcast.131, f32[1024,64]{1,0:T(8,128)S(1)} %bitcast.121, f32[]{:T(128)} %constant.95.clone.1), kind=kCustom, calls=%fused_computation.69 | custom fusion | bytes 262148 | tf_op jit(solution)/shard_map/scatter | solution.py:45
  82.8 4.4 %exponential_convert_fusion = bf16[2,512,512]{2,1,0:T(8,128)(2,1)} fusion(f32[2,512,64]{2,1,0:T(8,128)} %bitcast.113, f32[2,512]{1,0:T(2,128)S(1)} %add.235), kind=kOutput, calls=%fused_computation.23 | convolution fusion | flops 405274624 | bytes 1314816 | tf_op jit(solution)/shard_map/vmap()/dot_general | solution.py:20
  88.7 2.5 collective-permute-done
  93.3 7.3 %collective-permute-done.2 = f32[128,64]{1,0:T(8,128)S(1)} collective-permute-done((f32[128,64]{1,0:T(8,128)S(1)}, f32[128,64]{1,0:T(8,128)S(1)}, u32[]{:S(2)}, u32[]{:S(2)}) %collective-permute-start.2) | collective-permute-done | bytes 32800 | tf_op jit(solution)/shard_map/ppermute | solution.py:16
  106.4 2.6 collective-permute-done.1
  109.5 5.6 %collective-permute-done.3 = f32[128,128]{1,0:T(8,128)S(1)} collective-permute-done((f32[128,128]{1,0:T(8,128)S(1)}, f32[128,128]{1,0:T(8,128)S(1)}, u32[]{:S(2)}, u32[]{:S(2)}) %collective-permute-start.3) | collective-permute-done | bytes 65568 | tf_op jit(solution)/shard_map/ppermute | solution.py:16
  116.8 2.9 collective-permute-done.5
  123.5 27.5 %all-gather.3.cloned.1.call-done = f32[4096,64]{1,0:T(8,128)} async-done(((f32[1024,64]{1,0:T(8,128)}), f32[4096,64]{1,0:T(8,128)}) %all-gather.3.cloned.1.call-update) | async-done | bytes 1048592 | tf_op jit(solution)/shard_map/all_gather | solution.py:59
  151.1 16.2 %while.18 = (s32[]{:T(128)}, f32[2,512,128]{2,1,0:T(8,128)S(1)}, s32[]{:T(128)}, f32[2,512]{1,0:T(2,128)S(1)}, s32[2,16]{1,0:T(2,128)S(1)}, /*index=5*/f32[4096,...) while((s32[]{:T(128)}, f32[2,512,128]{2,1,0:T(8,128)S(1)}, ...), condition=%wide.region_7.8_spmd, body=%wide.region_5.7_spmd.sunk | while | flops 539884544 | bytes 5912113 | solution.py:90
  154.8 3.2 %fusion.113 = bf16[2,512,512]{1,2,0:T(8,128)(2,1)S(1)} fusion(f32[2,512,64]{2,1,0:T(8,128)} %copy-done.4, f32[2,512,64]{1,2,0:T(8,128)} %get-tuple-element.377, f32[2,512]{1,0:T(2,128)S(1)} %multiply_reduce_fusion.11, f32[2,512]{1,0:T(2,128)S(1)} %get-tuple-element.374), kind=kOutput, calls=%fused_computation.17.clone.1 | convolution fusion | flops 405274624 | bytes 1581056 | tf_op jit(solution)/shard_map/while/body/vmap()/dot_general | solution.py:20
  162.5 3.2 %fusion.113 = bf16[2,512,512]{1,2,0:T(8,128)(2,1)S(1)} fusion(f32[2,512,64]{2,1,0:T(8,128)} %copy-done.4, f32[2,512,64]{1,2,0:T(8,128)} %get-tuple-element.377, f32[2,512]{1,0:T(2,128)S(1)} %multiply_reduce_fusion.11, f32[2,512]{1,0:T(2,128)S(1)} %get-tuple-element.374), kind=kOutput, calls=%fused_computation.17.clone.1 | convolution fusion | flops 405274624 | bytes 1581056 | tf_op jit(solution)/shard_map/while/body/vmap()/dot_general | solution.py:20
  169.3 2.8 gather_fusion.6
  172.1 127.1 %all_to_all.21 = f32[8,128,128]{2,1,0:T(8,128)S(1)} all-to-all(f32[8,128,128]{2,1,0:T(8,128)S(1)} %bitcast.120), channel_id=1, replica_groups=mesh['groups'=2,'leaf'=2,'sub'=4,'rep'=2] {'leaf','sub'}, dimensions={0} | all-to-all | bytes 1048576 | tf_op jit(solution)/shard_map/all_to_all | solution.py:136
  299.3 3.9 %scatter_custom_fusion.2 = f32[1024,128]{1,0:T(8,128)} fusion(s32[1024]{0:T(1024)S(1)} %get-tuple-element.181, f32[1024,128]{1,0:T(8,128)S(1)} %bitcast.123, f32[]{:T(128)} %constant.95.clone.1), kind=kCustom, calls=%fused_computation.72 | custom fusion | bytes 524292 | tf_op jit(solution)/shard_map/scatter | solution.py:137
  (127 shorter events, 38.2 us)
Async XLA Ops:
  6.5 17.5 %copy-start = (f32[1024,128]{1,0:T(8,128)S(1)}, f32[1024,128]{1,0:T(8,128)}, u32[]{:S(2)}) copy-start(f32[1024,128]{1,0:T(8,128)} %param.11) | copy-start | bytes 1572868
  6.5 5.1 %copy-start.1 = (s32[1024]{0:T(1024)S(1)}, s32[1024]{0:T(1024)}, u32[]{:S(2)}) copy-start(s32[1024]{0:T(1024)} %param.12) | copy-start | bytes 12292
  16.8 13.7 %all-to-all-start = ((f32[8,1,128]{2,1,0:T(1,128)}), f32[8,1,128]{2,1,0:T(1,128)S(1)}, u32[]{:S(2)}, u32[]{:S(2)}) async-start(f32[8,1,128]{2,1,0:T(1,128)} %fusion.59), calls=%async_computation | async-start | bytes 8192 | tf_op jit(solution)/shard_map/all_to_all | solution.py:42
  28.1 24.9 %copy-start.8 = (f32[1024,64]{0,1:T(8,128)S(1)}, f32[1024,64]{0,1:T(8,128)}, u32[]{:S(2)}) copy-start(f32[1024,64]{0,1:T(8,128)} %param.10) | copy-start | bytes 786436
  30.5 18.5 %all-to-all-start.1 = ((f32[8,128,128]{2,1,0:T(8,128)}), f32[8,128,128]{2,1,0:T(8,128)S(1)}, u32[]{:S(2)}, u32[]{:S(2)}) async-start(f32[8,128,128]{2,1,0:T(8,128)} %bitcast.4), calls=%async_computation.1 | async-start | bytes 1048576 | tf_op jit(solution)/shard_map/all_to_all | solution.py:41
  34.3 87.6 %all-gather.5.cloned.1.call-start = ((), (), s32[]{:S(2)}) async-start(), calls=%async_computation.5 | async-start | bytes 2621440 | tf_op jit(solution)/shard_map/all_gather | solution.py:60
  53.2 7.2 %copy-start.9 = (s32[2,3]{1,0:T(2,128)S(1)}, s32[2,3]{1,0:T(2,128)}, u32[]{:S(2)}) copy-start(s32[2,3]{1,0:T(2,128)} %param.17) | copy-start | bytes 76
  53.2 8.7 %copy-start.11 = (s32[1,128]{1,0:T(1,128)S(1)}, s32[1,128]{1,0:T(1,128)}, u32[]{:S(2)}) copy-start(s32[1,128]{1,0:T(1,128)} %param.15) | copy-start | bytes 1540
  53.2 9.0 %copy-start.10 = (s32[1,8]{1,0:T(1,128)S(1)}, s32[1,8]{1,0:T(1,128)}, u32[]{:S(2)}) copy-start(s32[1,8]{1,0:T(1,128)} %param.13) | copy-start | bytes 100
  56.9 21.2 %all-to-all-start.2 = ((f32[8,128,64]{1,2,0:T(8,128)}), f32[8,128,64]{1,2,0:T(8,128)S(1)}, u32[]{:S(2)}, u32[]{:S(2)}) async-start(f32[8,128,64]{1,2,0:T(8,128)} %copy.14), calls=%async_computation.2 | async-start | bytes 524288 | tf_op jit(solution)/shard_map/all_to_all | solution.py:40
  60.4 90.7 %all-gather.3.cloned.1.call-start = ((), (), s32[]{:S(2)}) async-start(), calls=%async_computation.4 | async-start | bytes 2621440 | tf_op jit(solution)/shard_map/all_gather | solution.py:59
  81.7 1.1 copy-start.2
  82.6 8.7 %collective-permute-start = (f32[128,64]{1,0:T(8,128)S(1)}, f32[128,64]{1,0:T(8,128)S(1)}, u32[]{:S(2)}, u32[]{:S(2)}) collective-permute-start(f32[128,64]{1,0:T(8,128)S(1)} %gather_fusion.3), channel_id=1, source_target_pairs={{0,2},{2,0},{4,6},{6,4},{8,10},{10,8},{12,14},{14,12},{1,3},{3,1},... | collective-permute-start | bytes 98312 | tf_op jit(solution)/shard_map/ppermute | solution.py:16
  82.8 4.4 %copy-start.3 = (f32[1024,64]{1,0:T(8,128)S(1)}, f32[1024,64]{1,0:T(8,128)}, u32[]{:S(2)}) copy-start(f32[1024,64]{1,0:T(8,128)} %copy-done.2) | copy-start | bytes 786436
  92.1 11.5 %copy-start.5 = (f32[1024,128]{1,0:T(8,128)S(1)}, f32[1024,128]{1,0:T(8,128)}, u32[]{:S(2)}) copy-start(f32[1024,128]{1,0:T(8,128)} %scatter_custom_fusion) | copy-start | bytes 1572868
  92.1 8.5 %collective-permute-start.2 = (f32[128,64]{1,0:T(8,128)S(1)}, f32[128,64]{1,0:T(8,128)S(1)}, u32[]{:S(2)}, u32[]{:S(2)}) collective-permute-start(f32[128,64]{1,0:T(8,128)S(1)} %gather_fusion.4), channel_id=1, source_target_pairs={{0,4},{2,6},{4,0},{6,2},{8,12},{10,14},{12,8},{14,10},{1,5},{3,7},... | collective-permute-start | bytes 98312 | tf_op jit(solution)/shard_map/ppermute | solution.py:16
  101.4 4.3 %collective-permute-start.4 = (f32[128,64]{1,0:T(8,128)S(1)}, f32[128,64]{1,0:T(8,128)S(1)}, u32[]{:S(2)}, u32[]{:S(2)}) collective-permute-start(f32[128,64]{1,0:T(8,128)S(1)} %gather_fusion.5), channel_id=1, source_target_pairs={{0,8},{2,10},{4,12},{6,14},{8,0},{10,2},{12,4},{14,6},{1,9},{3,11}... | collective-permute-start | bytes 98312 | tf_op jit(solution)/shard_map/ppermute | solution.py:16
  104.4 16.0 %copy-start.6 = (bf16[1024,128]{1,0:T(8,128)(2,1)}, bf16[1024,128]{1,0:T(8,128)(2,1)S(1)}, u32[]{:S(2)}) copy-start(bf16[1024,128]{1,0:T(8,128)(2,1)S(1)} %get-tuple-element.176) | copy-start | bytes 786436
  104.6 4.4 %collective-permute-start.1 = (f32[128,128]{1,0:T(8,128)S(1)}, f32[128,128]{1,0:T(8,128)S(1)}, u32[]{:S(2)}, u32[]{:S(2)}) collective-permute-start(f32[128,128]{1,0:T(8,128)S(1)} %fusion.75), channel_id=1, source_target_pairs={{0,2},{2,0},{4,6},{6,4},{8,10},{10,8},{12,14},{14,12},{1,3},{3,1},... | collective-permute-start | bytes 196616 | tf_op jit(solution)/shard_map/ppermute | solution.py:16
  109.3 5.8 %collective-permute-start.3 = (f32[128,128]{1,0:T(8,128)S(1)}, f32[128,128]{1,0:T(8,128)S(1)}, u32[]{:S(2)}, u32[]{:S(2)}) collective-permute-start(f32[128,128]{1,0:T(8,128)S(1)} %fusion.44), channel_id=1, source_target_pairs={{0,4},{2,6},{4,0},{6,2},{8,12},{10,14},{12,8},{14,10},{1,5},{3,7},... | collective-permute-start | bytes 196616 | tf_op jit(solution)/shard_map/ppermute | solution.py:16
  115.4 4.3 %collective-permute-start.5 = (f32[128,128]{1,0:T(8,128)S(1)}, f32[128,128]{1,0:T(8,128)S(1)}, u32[]{:S(2)}, u32[]{:S(2)}) collective-permute-start(f32[128,128]{1,0:T(8,128)S(1)} %fusion.50), channel_id=1, source_target_pairs={{0,8},{2,10},{4,12},{6,14},{8,0},{10,2},{12,4},{14,6},{1,9},{3,11}... | collective-permute-start | bytes 196616 | tf_op jit(solution)/shard_map/ppermute | solution.py:16
  154.0 0.8 copy-start.4
  161.7 0.8 copy-start.4
  167.3 2.0 copy-start.7
Sparse Core Ops, SparseCore 0:
  53.1 51.5 all-gather.4
  106.3 44.7 all-gather.2
where the time goes:
time: 312 us; the launch traced here: 310 us
  blocking collectives  127 us (41%)
  waiting for transfers between devices  81.8 us (26%)
  local copies, waits for them, and re-layouts  36.3 us (12%)
  matrix products  20.3 us (7%)
  starting transfers between devices  16.6 us (5%)
  between operations  13.8 us (4%)
  other arithmetic  11.6 us (4%)
    all_to_all x1, blocking collectives, body(): lax.all_to_all(leaving, ('leaf', 'sub'), split_axis=0, concat_axis=0, til...  127 us
    all_gather x1, waiting for transfers between devices, body(): lax.all_gather(tree_points, 'sub', axis=0, tiled=True)  27.5 us
    ppermute x6, waiting for transfers between devices, from_partner(): lax.ppermute(value, axis, [(i, i ^ 1 << stride) for i in range(lax.axis_s...  22.1 us
    all_to_all x1, waiting for transfers between devices, body(): lax.all_to_all(send_points, ('leaf', 'sub'), split_axis=0, concat_axis=0,...  15 us
    all_to_all x1, waiting for transfers between devices, body(): lax.all_to_all(send_weights, ('leaf', 'sub'), split_axis=0, concat_axis=0...  14.8 us
    dot_general x9, matrix products, kernel(): jnp.dot(targets, sources.T, precision=highest, preferred_element_type=jnp...  13.8 us
    all_to_all x1, starting transfers between devices, body(): lax.all_to_all(send_slots, ('leaf', 'sub'), split_axis=0, concat_axis=0,...  7.25 us
  transfers between devices with their start and end apart: 11, of which 10 were waited for; matrix products, arithmetic and copies ran while one was open for 10% of the time, Pallas kernels for 0%

commit v1 on v0

v1 whole, which is shorter than its diff:
```python
import functools
import math

import jax
import jax.numpy as jnp
from jax import lax
from jax.experimental import pallas as pl
from jax.experimental.pallas import tpu as pltpu
from jax.sharding import PartitionSpec as P

DIM = 64
LEAF = 512
SK = 128
LANES = 128
FEAT = 256

highest = lax.Precision.HIGHEST
point_scale = math.sqrt(2.0 * math.log2(math.e) / 32.0)
ridge = 0.5
PLACE_ROWS = 72
SLOT_ROW = 64
NORM_ROW = 65
f32 = jnp.float32
bf16 = jnp.bfloat16
VMEM = pltpu.MemorySpace.VMEM
SMEM = pltpu.MemorySpace.SMEM


def spec(space=VMEM):
    return pl.BlockSpec(memory_space=space)


def params():
    return pltpu.CompilerParams(vmem_limit_bytes=56 * 1024 * 1024)


def nt(left, right):
    return lax.dot_general(left, right, (((1,), (1,)), ((), ())), preferred_element_type=f32)


def nn(left, right):
    return jnp.dot(left, right, preferred_element_type=f32)


def column(row):
    return jnp.transpose(jnp.broadcast_to(row, (LANES, LANES)))


def iota(shape, dim):
    return lax.broadcasted_iota(jnp.int32, shape, dim)


def onehot(mask):
    return jnp.where(mask, 1.0, 0.0).astype(bf16)


def two(value):
    high = value.astype(bf16)
    return high, (value - high.astype(f32)).astype(bf16)


def three(value):
    high = value.astype(bf16)
    rest = value - high.astype(f32)
    mid = rest.astype(bf16)
    return high.astype(f32), mid.astype(f32), (rest - mid.astype(f32)).astype(bf16).astype(f32)


def sort_kernel(slot_ref, points_ref, weights_ref, light_ref, place_ref, pos_ref, perm, vals):
    chunks, split = slot_ref.shape[0], light_ref.shape[-1]
    rows = chunks * LANES
    slots = slot_ref[...]
    slot = slots.astype(f32)
    within = slots & (rows - 1)
    high, low = (within >> 5).astype(f32), (within & 31).astype(f32)
    cols = jnp.concatenate([column(slot[c : c + 1]) for c in range(chunks)], 0)
    lane = iota((rows, LANES), 1)
    for c in range(chunks):
        before = jnp.where(cols < slot[c : c + 1], 1.0, 0.0)
        rank = jnp.sum(before, axis=0, keepdims=True)
        pos_ref[c : c + 1, :] = rank
        perm[:, c * LANES : (c + 1) * LANES] = onehot(iota((rows, LANES), 0) == rank.astype(jnp.int32))
    scaled = points_ref[...] * point_scale
    ph, plo = two(scaled)
    norm = -0.5 * jnp.sum(scaled * scaled, axis=1, keepdims=True)
    nh, nm, nl = three(jnp.broadcast_to(norm, (rows, LANES)))
    high = jnp.concatenate([column(high[c : c + 1]) for c in range(chunks)], 0)
    low = jnp.concatenate([column(low[c : c + 1]) for c in range(chunks)], 0)
    extra = jnp.where(lane == 0, high, jnp.where(lane == 1, low, 0.0))
    extra = jnp.where(lane == 2, nh, jnp.where(lane == 3, nm, jnp.where(lane == 4, nl, extra)))
    vals[:, 0:128] = weights_ref[...].astype(bf16)
    vals[:, 128:192] = ph
    vals[:, 192:256] = plo
    vals[:, 256:384] = extra.astype(bf16)
    step = 256
    for s in range(rows // step):
        sorted_rows = nn(perm[s * step : (s + 1) * step, :], vals[...])
        at = (s * step) // split
        off = (s * step) % split
        width = min(step, split)
        light = jnp.transpose(sorted_rows[:, 0:128])
        both = jnp.transpose(sorted_rows[:, 128:256])
        more = jnp.transpose(sorted_rows[:, 256:384])
        light_ref[at, :, off : off + width] = light
        place_ref[at, 0:64, off : off + width] = both[0:64] + both[64:128]
        tail = iota((8, step), 0)
        slot_row = more[0:1] * 32.0 + more[1:2]
        norm_row = more[2:3] + more[3:4] + more[4:5]
        place_ref[at, 64:72, off : off + width] = jnp.where(
            tail == 0, slot_row, jnp.where(tail == 1, norm_row, 0.0)
        )


def slot_matrix(out, slot_rows):
    rows = out.shape[0]
    for c, row in enumerate(slot_rows):
        out[:, c * LANES : (c + 1) * LANES] = onehot(iota((rows, LANES), 0) == row.astype(jnp.int32))


def lanes_of(blocks):
    return blocks[0] if len(blocks) == 1 else jnp.concatenate(blocks, 1)


def exact_product(block, coefs):
    high, low = two(block)
    first = nn(high, coefs)
    return first[:, :LANES] + first[:, LANES:] + nn(low, coefs[:, :LANES])


def split_coefs(value):
    high, low = two(value)
    return jnp.concatenate([high, low], 1)


def tree_kernel(
    blocks, trees, order, my_leaf_ref, light_ref, place_ref, small_ref, upper_ref,
    a_ref, b_ref, sk_ref, coef_ref, pack_ref, perm, feats, sk_a,
):
    groups, width = light_ref.shape[0], light_ref.shape[1]
    per = light_ref.shape[2] // blocks
    rows = groups * per
    step = 256
    lane = iota((SK, LANES), 1)
    keep = lane >= LANES - width

    def block(index, carry):
        at = pl.ds(pl.multiple_of(index * per, LANES), per)
        points = lanes_of([place_ref[order[g], 0:64, at] for g in range(groups)])
        tail = [place_ref[order[g], 64:72, at] for g in range(groups)]
        slot = lanes_of([t[0:1] for t in tail])
        norm = lanes_of([t[1:2] for t in tail])
        light = lanes_of([light_ref[g, :, at] for g in range(groups)])
        high, low = two(points)
        nh, nm, nl = three(norm)
        sub = iota((64, rows), 0)
        extra_a = jnp.where(sub == 0, nh, jnp.where(sub == 1, nm, jnp.where(sub == 2, nl, 0.0)))
        extra_a = jnp.where((sub >= 3) & (sub < 6), 1.0, extra_a)
        extra_b = jnp.where(sub == 3, nh, jnp.where(sub == 4, nm, jnp.where(sub == 5, nl, 0.0)))
        extra_b = jnp.where(sub < 3, 1.0, extra_b)
        feats[0:64, :] = high
        feats[64:128, :] = low
        feats[128:192, :] = high
        feats[192:256, :] = extra_a.astype(bf16)
        feats[FEAT - width : FEAT, :] = light.astype(bf16)
        feats[256:320, :] = high
        feats[320:384, :] = high
        feats[384:448, :] = low
        feats[448:512, :] = extra_b.astype(bf16)
        slot_matrix(perm, [slot[:, c * LANES : (c + 1) * LANES] for c in range(rows // LANES)])
        for s in range(rows // step):
            placed = nt(perm[s * step : (s + 1) * step, :], feats[...])
            here = pl.ds(pl.multiple_of(index * rows + s * step, step), step)
            a_ref[here, :] = placed[:, :FEAT].astype(bf16)
            b_ref[here, :] = placed[:, FEAT:].astype(bf16)
        picks = column(small_ref[index, 0:1, :].astype(f32)).astype(jnp.int32)
        for c in range(rows // LANES):
            perm[0:SK, c * LANES : (c + 1) * LANES] = onehot(lane + c * LANES == picks)
        chosen = perm[0:SK, :]
        mine = pl.ds(pl.multiple_of(index * rows, rows), rows)
        own_a = nn(chosen, a_ref[mine, :]).astype(bf16)
        node = pl.ds(pl.multiple_of(index * SK, SK), SK)
        sk_a[node, :] = own_a
        sk_ref[node, :] = nn(chosen, b_ref[mine, :]).astype(bf16)
        tile = jnp.exp2(nt(own_a, b_ref[mine, :])).astype(bf16)
        coef = jnp.where(keep, nn(tile, a_ref[mine, 128:256]), 0.0)
        coef_ref[node, :] = split_coefs(coef)
        pack_ref[...] = coef
        return carry

    lax.fori_loop(0, blocks, block, 0)
    start, count, offset, total = 0, blocks, 0, blocks * trees
    while count > 1:
        nodes = count // 2
        for j in range(nodes):
            pair = slice((start + 2 * j) * SK, (start + 2 * j + 2) * SK)
            row = offset + my_leaf_ref[0] * nodes + j
            picks = column(upper_ref[pl.ds(row, 1), :].astype(f32)).astype(jnp.int32)
            chosen = jnp.concatenate([onehot(lane == picks), onehot(lane + LANES == picks)], 1)
            new = slice((start + count + j) * SK, (start + count + j + 1) * SK)
            own_a = nn(chosen, sk_a[pair, :]).astype(bf16)
            sk_a[new, :] = own_a
            sk_ref[new, :] = nn(chosen, sk_ref[pair, :]).astype(bf16)
            coef = exact_product(jnp.exp2(nt(own_a, sk_ref[pair, :])), coef_ref[pair, :])
            coef = jnp.where(keep, coef, 0.0)
            coef_ref[new, :] = split_coefs(coef)
            pack_ref[...] = coef
        total = total // 2
        offset = offset + total
        start, count = start + count, nodes
    top = slice(start * SK, (start + 1) * SK)
    own_a = sk_a[top, :].astype(f32)
    exact = own_a[:, :128] + pltpu.roll(own_a[:, :128], 64, 1)
    pack_ref[...] = jnp.where(lane < 64, exact, jnp.where(keep, pack_ref[...], own_a[:, 128:]))


def near_kernel(
    blocks, levels, far_levels, count_ref, list_ref, flag_ref, a_ref, b_ref, sk_ref, coef_ref, out_ref, times
):
    leaves = count_ref.shape[1]
    per_block = leaves // blocks

    def tally(leaf, carry):
        for other in range(leaves):
            times[leaf * leaves + other] = (leaf == other).astype(jnp.int32)

        def add(slot, carry):
            at = leaf * leaves + list_ref[leaf, slot]
            times[at] = times[at] + 1
            return carry

        return lax.fori_loop(0, count_ref[0, leaf], add, carry)

    lax.fori_loop(0, leaves, tally, 0)

    def target(leaf, carry):
        here = pl.ds(pl.multiple_of(leaf * LEAF, LEAF), LEAF)
        out_ref[here, :] = jnp.zeros((LEAF, LANES), f32)
        node, start, count = leaf // per_block, 0, blocks
        for level in range(levels):

            @pl.when(flag_ref[leaf // per_block, 1, (leaf % per_block) * far_levels + level] > 0)
            def _():
                other = pl.ds(pl.multiple_of((start + (node ^ 1)) * SK, SK), SK)
                tile = jnp.exp2(nt(a_ref[here, :], sk_ref[other, :]))
                out_ref[here, :] += exact_product(tile, coef_ref[other, :])

            node, start, count = node // 2, start + count, count // 2

        def source(other, carry):
            many = times[leaf * leaves + other]

            @pl.when(many > 0)
            def _():
                there = pl.ds(pl.multiple_of(other * LEAF, LEAF), LEAF)
                tile = jnp.exp2(nt(a_ref[here, :], b_ref[there, :])).astype(bf16)
                out_ref[here, :] += many.astype(f32) * nn(tile, a_ref[there, 128:256])

            return carry

        return lax.fori_loop(0, leaves, source, carry)

    lax.fori_loop(0, leaves, target, 0)


def back_kernel(
    blocks, order, first, levels, width, flag_ref, a_ref, near_ref, pack_ref, place_ref, out_ref, perm, sk, coefs
):
    groups = out_ref.shape[0]
    per = out_ref.shape[2] // blocks
    rows = groups * per
    ups = pack_ref.shape[0]
    lane = iota((SK, LANES), 1)
    for up in range(ups):
        pack = pack_ref[up]
        points = jnp.where(lane < 64, pack, 0.0)
        high, low = two(points)
        high, low = high.astype(f32), low.astype(f32)
        norms = pltpu.roll(jnp.where((lane >= 64) & (lane < 67), pack, 0.0), 3, 1)
        tail = jnp.where((lane >= 64) & (lane < 67), 1.0, low + norms)
        here = slice(up * SK, (up + 1) * SK)
        sk[here, 0:128] = (high + pltpu.roll(high, 64, 1)).astype(bf16)
        sk[here, 128:256] = tail.astype(bf16)
        coefs[here, :] = split_coefs(jnp.where(lane >= LANES - width, pack, 0.0))

    per_block = rows // LEAF

    def block(index, carry):
        at = pl.ds(pl.multiple_of(index * per, LANES), per)
        for g in range(groups):
            row = place_ref[order[g], 64:72, at][0:1]
            for c in range(per // LANES):
                lo = g * per + c * LANES
                perm[:, lo : lo + LANES] = onehot(
                    iota((rows, LANES), 0) == row[:, c * LANES : (c + 1) * LANES].astype(jnp.int32)
                )
        halves = []
        for leaf in range(per_block):
            here = pl.ds(pl.multiple_of(index * rows + leaf * LEAF, LEAF), LEAF)
            total = near_ref[here, :]
            for up in range(ups):
                flag = flag_ref[index, 1, leaf * levels + first + up].astype(f32)
                src = slice(up * SK, (up + 1) * SK)
                tile = jnp.exp2(nt(a_ref[here, :], sk[src, :]))
                total = total + flag * exact_product(tile, coefs[src, :])
            halves.append(jnp.transpose(total)[LANES - width :, :])
        total = jnp.concatenate(halves, 1)
        high, low = two(total)
        moved = nn(jnp.concatenate([high, low], 0), perm[...])
        moved = moved[:width] + moved[width:]
        for g in range(groups):
            out_ref[g, :, at] = moved[:, g * per : (g + 1) * per]
        return carry

    lax.fori_loop(0, blocks, block, 0)


def final_kernel(pos_ref, back_ref, weights_ref, out_ref, perm, vals):
    chunks = pos_ref.shape[0]
    rows = chunks * LANES
    split = back_ref.shape[2]
    cols = jnp.concatenate([column(pos_ref[c : c + 1, :]) for c in range(chunks)], 0).astype(jnp.int32)
    for c in range(chunks):
        perm[:, c * LANES : (c + 1) * LANES] = onehot(iota((rows, LANES), 1) + c * LANES == cols)
    for part in range(rows // split):
        high, low = two(back_ref[part])
        vals[0:LANES, part * split : (part + 1) * split] = high
        vals[LANES:, part * split : (part + 1) * split] = low
    step = 256
    for s in range(rows // step):
        here = slice(s * step, (s + 1) * step)
        moved = nt(perm[here, :], vals[...])
        out_ref[here, :] = ridge * weights_ref[here, :] + moved[:, :LANES] + moved[:, LANES:]


def vm(shape, dtype):
    return pltpu.VMEM(shape, dtype)


def body(points, weights, tree_slot, near_count, near_list, skeleton_base, skeleton_upper, far_use):
    blocks = lax.axis_size("sub")
    trees = lax.axis_size("leaf")
    devices = blocks * trees
    rows, columns = weights.shape
    levels = devices.bit_length() - 1
    low_levels = blocks.bit_length() - 1
    width = columns // blocks
    part = rows // trees
    leaves = blocks * rows // LEAF
    my_leaf = lax.axis_index("leaf")
    fine = part % 256 == 0 or part == rows
    split = part if fine else rows

    info = jnp.concatenate(
        [skeleton_base, jnp.pad(far_use.reshape(1, -1), ((0, 0), (0, SK - far_use.size)))], 0
    )
    small = lax.all_gather(info, "sub", axis=0, tiled=False)

    light, place, pos = pl.pallas_call(
        sort_kernel,
        out_shape=(
            jax.ShapeDtypeStruct((rows // split, columns, split), f32),
            jax.ShapeDtypeStruct((rows // split, PLACE_ROWS, split), f32),
            jax.ShapeDtypeStruct((rows // LANES, LANES), f32),
        ),
        in_specs=[spec()] * 3,
        out_specs=(spec(),) * 3,
        scratch_shapes=[vm((rows, rows), bf16), vm((rows, 384), bf16)],
        compiler_params=params(),
        name="sort_rows",
    )(tree_slot.reshape(rows // LANES, LANES), points, weights)

    def by_tree(array):
        if fine:
            return array
        return array.reshape(array.shape[1], trees, part).transpose(1, 0, 2)

    place = lax.all_to_all(by_tree(place), "leaf", split_axis=0, concat_axis=0, tiled=True)
    place = lax.all_gather(place, "sub", axis=0, tiled=False)
    light = by_tree(light).reshape(devices, width, part)
    light = lax.all_to_all(light, ("leaf", "sub"), split_axis=0, concat_axis=0, tiled=True)
    per = part // blocks
    if per % LANES == 0:
        place = place.reshape(devices, PLACE_ROWS, part)
        order = [sub * trees + leaf for leaf in range(trees) for sub in range(blocks)]
        groups = devices
    else:
        place = place.transpose(1, 0, 2, 3).reshape(devices, PLACE_ROWS, blocks, per)
        place = place.transpose(1, 2, 0, 3).reshape(1, PLACE_ROWS, blocks * rows)
        light = light.reshape(devices, width, blocks, per)
        light = light.transpose(1, 2, 0, 3).reshape(1, width, blocks * rows)
        order, groups = [0], 1

    total = blocks * rows
    nodes = 2 * blocks - 1
    where = my_leaf.astype(jnp.int32).reshape(1)
    feat_a, feat_b, sk, coefs, pack = pl.pallas_call(
        functools.partial(tree_kernel, blocks, trees, order),
        out_shape=(
            jax.ShapeDtypeStruct((total, FEAT), bf16),
            jax.ShapeDtypeStruct((total, FEAT), bf16),
            jax.ShapeDtypeStruct((nodes * SK, FEAT), bf16),
            jax.ShapeDtypeStruct((nodes * SK, FEAT), bf16),
            jax.ShapeDtypeStruct((SK, LANES), f32),
        ),
        in_specs=[spec(SMEM)] + [spec()] * 4,
        out_specs=(spec(),) * 5,
        scratch_shapes=[vm((rows, rows), bf16), vm((2 * FEAT, rows), bf16), vm((nodes * SK, FEAT), bf16)],
        compiler_params=params(),
        name="to_tree",
    )(where, light, place, small, skeleton_upper)

    packs = []
    own = pack
    offset = sum(devices >> level for level in range(1, low_levels + 1))
    lanes = jnp.arange(LANES)
    is_point, is_norm = (lanes < DIM)[None], ((lanes >= DIM) & (lanes < DIM + 3))[None]
    is_coef = (lanes >= LANES - width)[None]
    for level in range(low_levels, levels):
        stride = 1 << (level - low_levels)
        other = lax.ppermute(own, "leaf", [(i, i ^ stride) for i in range(trees)])
        packs.append(other)
        if level + 1 < levels:
            second = (my_leaf // stride) % 2 == 1
            pair = jnp.where(second, jnp.concatenate([other, own], 0), jnp.concatenate([own, other], 0))
            chosen = pair[skeleton_upper[offset + my_leaf // (2 * stride)]]
            offset += devices >> (level + 1)
            coords = jnp.where(is_point, pair, 0.0)
            norms = jnp.sum(jnp.where(is_norm, pair, 0.0), axis=1)
            inner = jnp.dot(jnp.where(is_point, chosen, 0.0), coords.T, precision=highest)
            tile = jnp.exp2(inner + norms[None] + jnp.sum(jnp.where(is_norm, chosen, 0.0), axis=1)[:, None])
            value = jnp.dot(tile, pair, precision=highest)
            own = jnp.where(is_coef, value, chosen)
    packs = jnp.stack(packs)

    near = pl.pallas_call(
        functools.partial(near_kernel, blocks, low_levels, levels),
        out_shape=jax.ShapeDtypeStruct((total, LANES), f32),
        in_specs=[spec(SMEM)] * 3 + [spec()] * 4,
        out_specs=spec(),
        scratch_shapes=[pltpu.SMEM((leaves * leaves,), jnp.int32)],
        compiler_params=params(),
        name="near_and_far",
    )(near_count, near_list[0], small, feat_a, feat_b, sk, coefs)

    ups = levels - low_levels
    back = pl.pallas_call(
        functools.partial(back_kernel, blocks, order, low_levels, levels, width),
        out_shape=jax.ShapeDtypeStruct((groups, width, total // groups), f32),
        in_specs=[spec(SMEM)] + [spec()] * 4,
        out_specs=spec(),
        scratch_shapes=[vm((rows, rows), bf16), vm((ups * SK, FEAT), bf16), vm((ups * SK, FEAT), bf16)],
        compiler_params=params(),
        name="back_order",
    )(small, feat_a, near, packs, place)

    if groups == 1:
        back = back.reshape(width, blocks, devices, per).transpose(2, 0, 1, 3).reshape(devices, width, part)
    back = lax.all_to_all(back, ("leaf", "sub"), split_axis=0, concat_axis=0, tiled=True)
    back = back.reshape(trees, columns, part)
    if not fine:
        back = back.transpose(1, 0, 2).reshape(1, columns, rows)

    return pl.pallas_call(
        final_kernel,
        out_shape=jax.ShapeDtypeStruct((rows, columns), f32),
        in_specs=[spec()] * 3,
        out_specs=spec(),
        scratch_shapes=[vm((rows, rows), bf16), vm((2 * LANES, rows), bf16)],
        compiler_params=params(),
        name="to_input_order",
    )(pos, back, weights)


def solution(mesh):
    in_specs = (
        P(("groups", "leaf", "sub"), None),
        P(("groups", "leaf", "sub"), "rep"),
        P(("groups", "leaf", "sub")),
        P(("groups", "leaf"), None),
        P(("groups", "leaf"), None, None),
        P(("groups", "leaf", "sub"), None),
        P("groups", None),
        P(("groups", "leaf", "sub"), None),
    )
    out_specs = P(("groups", "leaf", "sub"), "rep")
    return jax.shard_map(body, mesh=mesh, in_specs=in_specs, out_specs=out_specs, check_vma=False)
```

time: 312 us -> 142 us (0.46)
  blocking collectives: 127 us -> 51.1 us
  waiting for transfers between devices: 81.8 us -> 12.8 us
  Pallas kernels: 0 us -> 53.4 us
  local copies, waits for them, and re-layouts: 36.3 us -> 2.68 us
  matrix products: 20.3 us -> 0 us
  other arithmetic: 11.6 us -> 0.01 us
  starting transfers between devices: 16.6 us -> 6.62 us
    all_to_all x1 -> x2, blocking collectives: 127 us -> 30.9 us  [the longest x1 19.7 us: body(): lax.all_to_all(back, ('leaf', 'sub'), split_axis=0, concat_axis=0, tiled=...]
    pallas_call x0 -> x5, Pallas kernels: none -> 53.4 us  [the longest x1 25.3 us: body(): pl.pallas_call(functools.partial(near_kernel, blocks, low_levels, levels)...]
    all_to_all x3 -> x1, waiting for transfers between devices: 32.2 us -> 6.69 us  [body(): lax.all_to_all(light, ('leaf', 'sub'), split_axis=0, concat_axis=0, tiled...]
    ppermute x6 -> x1, waiting for transfers between devices: 22.1 us -> 0.01 us  [body(): other = lax.ppermute(own, 'leaf', [(i, i ^ stride) for i in range(trees)])]
    all_gather x2 -> x1, waiting for transfers between devices: 27.5 us -> 6.08 us  [body(): place = lax.all_gather(place, 'sub', axis=0, tiled=False)]
    gather x23 -> x0, local copies, waits for them, and re-layouts: 20.7 us -> none  [the longest x1 4.52 us: body(): tree_slot[order] % rows]
    dot_general x18 -> x0, matrix products: 20.3 us -> none  [the longest x9 13.8 us: kernel(): jnp.dot(targets, sources.T, precision=highest, preferred_element_type=jnp...]
    all_gather x0 -> x1, blocking collectives: none -> 20.2 us  [body(): small = lax.all_gather(info, 'sub', axis=0, tiled=False)]
  transfers between devices with their start and end apart: 11 -> 3, of which waited for: 10 -> 2; matrix products, arithmetic and copies ran while one was open for 10% -> 0% of each run, Pallas kernels for 0% -> 18%
where the time goes in v1:
time: 142 us; the launch traced here: 140 us
  Pallas kernels  53.4 us (38%)
  blocking collectives  51.1 us (36%)
  between operations  13.4 us (9%)
  waiting for transfers between devices  12.8 us (9%)
  starting transfers between devices  6.62 us (5%)
  local copies, waits for them, and re-layouts  2.68 us (2%)
    pallas_call x1, Pallas kernels, body(): pl.pallas_call(functools.partial(near_kernel, blocks, low_levels, levels)...  25.3 us
    all_gather x1, blocking collectives, body(): small = lax.all_gather(info, 'sub', axis=0, tiled=False)  20.2 us
    all_to_all x1, blocking collectives, body(): lax.all_to_all(back, ('leaf', 'sub'), split_axis=0, concat_axis=0, tiled=...  19.7 us
    all_to_all x1, blocking collectives, body(): lax.all_to_all(by_tree(place), 'leaf', split_axis=0, concat_axis=0, tiled...  11.2 us
    pallas_call x1, Pallas kernels, body(): pl.pallas_call(functools.partial(tree_kernel, blocks, trees, order), out_...  10.9 us
    pallas_call x1, Pallas kernels, body(): pl.pallas_call(functools.partial(back_kernel, blocks, order, low_levels,...  9.45 us
    all_to_all x1, waiting for transfers between devices, body(): lax.all_to_all(light, ('leaf', 'sub'), split_axis=0, concat_axis=0, tiled...  6.69 us
    all_gather x1, waiting for transfers between devices, body(): place = lax.all_gather(place, 'sub', axis=0, tiled=False)  6.08 us
  transfers between devices with their start and end apart: 3, of which 2 were waited for; matrix products, arithmetic and copies ran while one was open for 0% of the time, Pallas kernels for 18%

profile of v1, /device:TPU:0, one launch (start us, length us, event | category | flops | bytes accessed | tf_op | source)
XLA Modules:
  0.0 140.0 jit_solution(17495598321509975081)
XLA Ops:
  6.5 0.0 copy-start.3
  6.5 0.0 copy-start.2
  6.5 0.0 all-gather.5.cloned.1.call-start
  6.5 2.0 %copy.10.points_ref = f32[1024,64]{1,0:T(8,128)} copy(f32[1024,64]{0,1:T(8,128)} %param.8) | data formatting | bytes 524288 | tf_op args[0]
  8.5 4.5 %sort_rows.1 = (f32[2,128,512]{2,1,0:T(8,128)}, f32[2,72,512]{2,1,0:T(8,128)}, f32[8,128]{1,0:T(8,128)}) custom-call(s32[8,128]{1,0:T(8,128)} %bitcast.11, f32[1024,64]{1,0:T(8,128)} %copy.10.points_ref, f32[1024,128]{1,0:T(8,128)} %weights_ref.3), custom_call_target="tpu_custom_call" | custom-call | tf_op jit(solution)/shard_map/sort_rows/pallas_call | solution.py:358
  13.0 11.2 %all_to_all.15 = f32[2,72,512]{2,1,0:T(8,128)} all-to-all(f32[2,72,512]{2,1,0:T(8,128)} %get-tuple-element.15), channel_id=1, replica_groups=mesh['groups'=2,'leaf'=2,'sub'=4,'rep'=2] {'leaf'}, dimensions={0} | all-to-all | bytes 589824 | tf_op jit(solution)/shard_map/all_to_all | solution.py:377
  24.2 0.0 all-gather.5.cloned.1.call-update
  24.3 5.1 %all-to-all-start = ((f32[8,32,512]{2,1,0:T(8,128)}), f32[8,32,512]{2,1,0:T(8,128)S(1)}, u32[]{:S(2)}, u32[]{:S(2)}) async-start(f32[8,32,512]{2,1,0:T(8,128)} %bitcast.9), calls=%async_computation | async-start | bytes 1048576 | tf_op jit(solution)/shard_map/all_to_all | solution.py:380
  29.4 0.0 copy-done.3
  29.4 0.1 reshape.19
  29.5 0.0 copy-done.2
  29.5 20.2 %all-gather.2.small_ref.flag_ref = s32[4,2,128]{2,1,0:T(2,128)} all-gather(s32[1,2,128]{2,1,0:T(2,128)S(1)} %fusion), channel_id=2, replica_groups=mesh['groups'=2,'leaf'=2,'sub'=4,'rep'=2] {'sub'}, dimensions={0}, use_global_device_ids=true | all-gather | bytes 5120 | tf_op jit(solution)/shard_map/all_gather | solution.py:356
  49.7 6.7 %all-to-all-done.light_ref = f32[8,32,512]{2,1,0:T(8,128)S(1)} async-done(((f32[8,32,512]{2,1,0:T(8,128)}), f32[8,32,512]{2,1,0:T(8,128)S(1)}, u32[]{:S(2)}, u32[]{:S(2)}) %all-to-all-start) | async-done | bytes 524320 | tf_op jit(solution)/shard_map/all_to_all | solution.py:380
  56.4 0.0 copy-start
  56.4 6.1 %all-gather.5.cloned.1.call-done.place_ref = f32[8,72,512]{2,1,0:T(8,128)} async-done(((f32[2,72,512]{2,1,0:T(8,128)}), f32[8,72,512]{2,1,0:T(8,128)}) %all-gather.5.cloned.1.call-update) | async-done | bytes 1179664 | tf_op jit(solution)/shard_map/all_gather | solution.py:378
  62.5 0.0 copy-done
  62.5 10.9 %to_tree.1 = (bf16[4096,256]{1,0:T(8,128)(2,1)}, bf16[4096,256]{1,0:T(8,128)(2,1)}, bf16[896,256]{1,0:T(8,128)(2,1)}, bf16[896,256]{1,0:T(8,128)(2,1)}, f32[128,128]{1,0:T(8,128)}) custom-call(s32[1]{0:T(128)} %bitcast.2.my_leaf_ref, f32[8,32,512]{2,1,0:T(8,128)} %copy-done, f32[8,72,512]{2,1,0:T(8,128)} %all-gather.5.cloned.1.call-done.place_ref, ...), custom_call_target="tpu_custom_call" | custom-call | tf_op jit(solution)/shard_map/to_tree/pallas_call | solution.py:396
  73.4 1.5 %collective-permute-start = (f32[128,128]{1,0:T(8,128)}, f32[128,128]{1,0:T(8,128)S(1)}, u32[]{:S(2)}, u32[]{:S(2)}) collective-permute-start(f32[128,128]{1,0:T(8,128)} %get-tuple-element.20), channel_id=1, source_target_pairs={{0,8},{8,0},{1,9},{9,1},{2,10},{10,2},{3,11},{11,3},{4,12},{12,4},... | collective-permute-start | bytes 196616 | tf_op jit(solution)/shard_map/ppermute | solution.py:420
  74.9 25.3 %near_and_far.1.near_ref = f32[4096,128]{1,0:T(8,128)} custom-call(s32[1,8]{1,0:T(1,128)} %count_ref.1, s32[8,16]{1,0:T(8,128)} %bitcast.12, s32[4,2,128]{2,1,0:T(2,128)} %all-gather.2.small_ref.flag_ref, bf16[4096,256]{1,0:T(8,128)(2,1)} %get-tuple-element.16.a_ref, bf16[4096,256]{1,0:T(8,128)(2,1)} %get-tuple-element.17.b_ref, ...), custom_call_target="tpu_custom_call" | custom-call | tf_op jit(solution)/shard_map/near_and_far/pallas_call | solution.py:435
  100.2 0.0 collective-permute-done
  100.2 0.6 copy-done.1
  100.8 9.4 %back_order.1 = f32[8,32,512]{2,1,0:T(8,128)} custom-call(s32[4,2,128]{2,1,0:T(2,128)} %all-gather.2.small_ref.flag_ref, bf16[4096,256]{1,0:T(8,128)(2,1)} %get-tuple-element.16.a_ref, f32[4096,128]{1,0:T(8,128)} %near_and_far.1.near_ref, f32[1,128,128]{2,1,0:T(8,128)} %bitcast.10, f32[8,72,512]{2,1,0:T(8,128)} %all-gather.5.cloned.1.call-done.place_ref), custom_call_target="tpu_custom_call" | custom-call | tf_op jit(solution)/shard_map/back_order/pallas_call | solution.py:446
  110.2 19.7 %all_to_all.16 = f32[8,32,512]{2,1,0:T(8,128)} all-to-all(f32[8,32,512]{2,1,0:T(8,128)} %back_order.1), channel_id=1, replica_groups=mesh['groups'=2,'leaf'=2,'sub'=4,'rep'=2] {'leaf','sub'}, dimensions={0} | all-to-all | bytes 1048576 | tf_op jit(solution)/shard_map/all_to_all | solution.py:458
  130.0 3.2 %to_input_order.1 = f32[1024,128]{1,0:T(8,128)} custom-call(f32[8,128]{1,0:T(8,128)} %get-tuple-element.13.pos_ref, f32[2,128,512]{2,1,0:T(8,128)} %bitcast.8, f32[1024,128]{1,0:T(8,128)} %weights_ref.3), custom_call_target="tpu_custom_call" | custom-call | tf_op jit(solution)/shard_map/to_input_order/pallas_call | solution.py:463
  (2 shorter events, 0.0 us)
Async XLA Ops:
  6.5 22.9 %copy-start.3 = (s32[2,3]{1,0:T(2,128)S(1)}, s32[2,3]{1,0:T(2,128)}, u32[]{:S(2)}) copy-start(s32[2,3]{1,0:T(2,128)} %param.15) | copy-start | bytes 76
  6.5 23.0 %copy-start.2 = (s32[1,128]{1,0:T(1,128)S(1)}, s32[1,128]{1,0:T(1,128)}, u32[]{:S(2)}) copy-start(s32[1,128]{1,0:T(1,128)} %param.13) | copy-start | bytes 1540
  6.5 55.9 %all-gather.5.cloned.1.call-start = ((), (), s32[]{:S(2)}) async-start(), calls=%async_computation.3 | async-start | bytes 1474560 | tf_op jit(solution)/shard_map/all_gather | solution.py:378
  24.3 32.1 %all-to-all-start = ((f32[8,32,512]{2,1,0:T(8,128)}), f32[8,32,512]{2,1,0:T(8,128)S(1)}, u32[]{:S(2)}, u32[]{:S(2)}) async-start(f32[8,32,512]{2,1,0:T(8,128)} %bitcast.9), calls=%async_computation | async-start | bytes 1048576 | tf_op jit(solution)/shard_map/all_to_all | solution.py:380
  56.4 6.1 %copy-start = (f32[8,32,512]{2,1,0:T(8,128)}, f32[8,32,512]{2,1,0:T(8,128)S(1)}, u32[]{:S(2)}) copy-start(f32[8,32,512]{2,1,0:T(8,128)S(1)} %all-to-all-done.light_ref) | copy-start | bytes 1572868
  73.4 26.8 %collective-permute-start = (f32[128,128]{1,0:T(8,128)}, f32[128,128]{1,0:T(8,128)S(1)}, u32[]{:S(2)}, u32[]{:S(2)}) collective-permute-start(f32[128,128]{1,0:T(8,128)} %get-tuple-element.20), channel_id=1, source_target_pairs={{0,8},{8,0},{1,9},{9,1},{2,10},{10,2},{3,11},{11,3},{4,12},{12,4},... | collective-permute-start | bytes 196616 | tf_op jit(solution)/shard_map/ppermute | solution.py:420
  100.2 0.6 copy-start.1
Sparse Core Ops, SparseCore 0:
  24.4 38.0 all-gather.4

commit v2 on v0

v2 whole, which is shorter than its diff:
```python
import functools
import math

import jax
import jax.numpy as jnp
from jax import lax
from jax.experimental import pallas as pl
from jax.experimental.pallas import tpu as pltpu
from jax.sharding import PartitionSpec as P

DIM = 64
LEAF = 512
SK = 128
LANES = 128
FEAT = 256

highest = lax.Precision.HIGHEST
point_scale = math.sqrt(2.0 * math.log2(math.e) / 32.0)
ridge = 0.5
PLACE_ROWS = 72
TAIL = 64
SLOT, NORM, BASE, FLAGS = 0, 1, 2, 3
f32 = jnp.float32
bf16 = jnp.bfloat16
VMEM = pltpu.MemorySpace.VMEM
SMEM = pltpu.MemorySpace.SMEM


def spec(space=VMEM):
    return pl.BlockSpec(memory_space=space)


def params():
    return pltpu.CompilerParams(vmem_limit_bytes=48 * 1024 * 1024)


def vm(shape, dtype):
    return pltpu.VMEM(shape, dtype)


def shaped(shape, dtype):
    return jax.ShapeDtypeStruct(shape, dtype)


def nt(left, right):
    return lax.dot_general(left, right, (((1,), (1,)), ((), ())), preferred_element_type=f32)


def nn(left, right):
    return jnp.dot(left, right, preferred_element_type=f32)


def column(row):
    return jnp.transpose(jnp.broadcast_to(row, (LANES, LANES)))


def iota(shape, dim):
    return lax.broadcasted_iota(jnp.int32, shape, dim)


def onehot(mask):
    return jnp.where(mask, 1.0, 0.0).astype(bf16)


def two(value):
    high = value.astype(bf16)
    return high, (value - high.astype(f32)).astype(bf16)


def three(value):
    high = value.astype(bf16).astype(f32)
    mid = (value - high).astype(bf16).astype(f32)
    return high, mid, (value - high - mid).astype(bf16).astype(f32)


def lanes_of(blocks):
    return blocks[0] if len(blocks) == 1 else jnp.concatenate(blocks, 1)


def aligned(start, size, unit):
    return pl.ds(pl.multiple_of(start, unit), size)


def exact_product(block, coefs):
    high, low = two(block)
    first = nn(high, coefs)
    return first[:, :LANES] + first[:, LANES:] + nn(low, coefs[:, :LANES])


def split_coefs(value):
    high, low = two(value)
    return jnp.concatenate([high, low], 1)


def sort_kernel(halves, where_ref, slot_ref, points_ref, weights_ref, base_ref, flag_ref, light_ref, *refs):
    place_refs, pos_ref, perm, vals, whole = refs[:-4], refs[-4], refs[-3], refs[-2], refs[-1]
    chunks, split = slot_ref.shape[0], light_ref.shape[-1]
    rows = chunks * LANES
    slots = slot_ref[...]
    slot = slots.astype(f32)
    within = slots & (rows - 1)
    high, low = (within >> 5).astype(f32), (within & 31).astype(f32)
    cols = jnp.concatenate([column(slot[c : c + 1]) for c in range(chunks)], 0)
    before = jnp.zeros((rows, LANES), f32)
    for c in range(chunks):
        before += jnp.where(slot[c : c + 1] < cols, 1.0, 0.0)
    rank = jnp.broadcast_to(jnp.sum(before, axis=1, keepdims=True), (rows, LANES))
    place_of = rank.astype(jnp.int32)
    for c in range(chunks):
        at = slice(c * LANES, (c + 1) * LANES)
        pos_ref[c : c + 1, :] = jnp.transpose(rank[at])[0:1]
        perm[:, at] = onehot(iota((rows, LANES), 1) + c * LANES == place_of)
        vals[0:LANES, at] = jnp.transpose(weights_ref[at, :]).astype(bf16)
    scaled = points_ref[...] * point_scale
    ph, plo = two(scaled)
    nh, nm, nl = three(-0.5 * jnp.sum(scaled * scaled, axis=0, keepdims=True))
    vals[128:192, :] = ph
    vals[192:256, :] = plo
    sub = iota((16, LANES), 0)
    for c in range(chunks):
        at = slice(c * LANES, (c + 1) * LANES)
        extra = jnp.where(sub == 0, high[c : c + 1], jnp.where(sub == 1, low[c : c + 1], 0.0))
        extra = jnp.where(sub == 2, nh[:, at], jnp.where(sub == 3, nm[:, at], extra))
        vals[256:272, at] = jnp.where(sub == 4, nl[:, at], extra).astype(bf16)
    step = 256
    for s in range(rows // step):
        moved = nn(vals[...], perm[:, s * step : (s + 1) * step])
        at = slice((s * step) % split, (s * step) % split + step)
        part = (s * step) // split
        light_ref[part, :, at] = moved[0:LANES]
        whole[part, 0:TAIL, at] = moved[128:192] + moved[192:256]
        tail = iota((8, step), 0)
        slot_row = moved[256:257] * 32.0 + moved[257:258]
        norm_row = moved[258:259] + moved[259:260] + moved[260:261]
        whole[part, TAIL:, at] = jnp.where(tail == SLOT, slot_row, jnp.where(tail == NORM, norm_row, 0.0))
    if not halves:
        place_refs[0][...] = whole[...]
        return
    size = split // halves
    mine = aligned(where_ref[1] * size, size, LANES)
    for other, place in enumerate(place_refs):
        place[...] = whole[where_ref[0] ^ other, :, mine]
        place[TAIL + BASE : TAIL + BASE + 1, 0:SK] = base_ref[...].astype(f32)
        place[TAIL + FLAGS : TAIL + FLAGS + flag_ref.shape[0], 0 : flag_ref.shape[1]] = flag_ref[...].astype(f32)


class Layout:
    def __init__(self, blocks, trees, rows, halves):
        self.blocks, self.rows, self.halves = blocks, rows, halves
        self.near = [(other, sub) for other in range(trees) for sub in range(blocks)] if halves else [(0, 0)]
        self.per = rows // len(self.near)

    def place(self, refs, group, index, part):
        other, sub = self.near[group]
        if not self.halves:
            return refs[0][0, part, aligned(index * self.per, self.per, LANES)]
        each = self.blocks // self.halves
        lead = sub * self.halves + index // each
        return refs[other][lead, part, aligned((index % each) * self.per, self.per, LANES)]

    def message(self, group, leaf):
        other, sub = self.near[group]
        return (leaf ^ other) * self.blocks + sub if self.halves else 0

    def lanes(self, index):
        return aligned(index * self.per, self.per, LANES)

    def tail(self, refs, index):
        return [self.place(refs, g, index, slice(TAIL, PLACE_ROWS)) for g in range(len(self.near))]

    def info(self, refs, small_ref, index, row):
        if self.halves:
            return refs[0][index * self.halves, TAIL + row : TAIL + row + 1, 0:SK]
        return small_ref[index, row : row + 1, :]


def fill_perm(out, slot_rows):
    for c in range(out.shape[1] // LANES):
        at = slice(c * LANES, (c + 1) * LANES)
        out[:, at] = onehot(iota((out.shape[0], LANES), 0) == slot_rows[:, at].astype(jnp.int32))


def slot_row(tails):
    return lanes_of([t[SLOT : SLOT + 1] for t in tails])


def points_kernel(layout, trees, width, where_ref, upper_ref, small_ref, *refs):
    place_refs = refs[: 2 if layout.halves else 1]
    a_ref, bt_ref, skt_ref, base_ref, upper_tiles_ref, top_ref, perm, feats, sk_a = refs[len(place_refs) :]
    blocks, rows = layout.blocks, layout.rows
    groups = range(len(layout.near))
    lane = iota((SK, LANES), 1)

    def block(index, carry):
        tails = layout.tail(place_refs, index)
        points = lanes_of([layout.place(place_refs, g, index, slice(0, TAIL)) for g in groups])
        high, low = two(points)
        nh, nm, nl = three(lanes_of([t[NORM : NORM + 1] for t in tails]))
        sub = iota((64, rows), 0)
        extra_a = jnp.where(sub == 0, nh, jnp.where(sub == 1, nm, jnp.where(sub == 2, nl, 0.0)))
        extra_a = jnp.where((sub >= 3) & (sub < 6), 1.0, extra_a)
        extra_b = jnp.where(sub == 3, nh, jnp.where(sub == 4, nm, jnp.where(sub == 5, nl, 0.0)))
        extra_b = jnp.where(sub < 3, 1.0, extra_b)
        feats[0:64, :] = high
        feats[64:128, :] = low
        feats[128:192, :] = high
        feats[192:256, :] = extra_a.astype(bf16)
        feats[256:320, :] = high
        feats[320:384, :] = high
        feats[384:448, :] = low
        feats[448:512, :] = extra_b.astype(bf16)
        fill_perm(perm, slot_row(tails))
        mine = aligned(index * rows, rows, rows)
        a_ref[mine, :] = nt(perm[...], feats[0:FEAT, :]).astype(bf16)
        bt_ref[:, mine] = nt(feats[FEAT:, :], perm[...]).astype(bf16)
        picks = column(layout.info(place_refs, small_ref, index, BASE)).astype(jnp.int32)
        chosen = jnp.concatenate([onehot(lane + c * LANES == picks) for c in range(rows // LANES)], 1)
        node = aligned(index * SK, SK, SK)
        own_a = nn(chosen, a_ref[mine, :]).astype(bf16)
        sk_a[node, :] = own_a
        skt_ref[:, node] = nt(bt_ref[:, mine], chosen).astype(bf16)
        base_ref[index] = jnp.exp2(nn(own_a, bt_ref[:, mine])).astype(bf16)
        return carry

    lax.fori_loop(0, blocks, block, 0)
    start, count, offset, total = 0, blocks, 0, blocks * trees
    while count > 1:
        nodes = count // 2
        for j in range(nodes):
            pair = slice((start + 2 * j) * SK, (start + 2 * j + 2) * SK)
            row = offset + where_ref[0] * nodes + j
            picks = column(upper_ref[pl.ds(row, 1), :].astype(f32)).astype(jnp.int32)
            chosen = jnp.concatenate([onehot(lane == picks), onehot(lane + LANES == picks)], 1)
            here = start + count + j
            new = slice(here * SK, (here + 1) * SK)
            own_a = nn(chosen, sk_a[pair, :]).astype(bf16)
            sk_a[new, :] = own_a
            skt_ref[:, new] = nt(skt_ref[:, pair], chosen).astype(bf16)
            upper_tiles_ref[here - blocks] = jnp.exp2(nn(own_a, skt_ref[:, pair]))
        total = total // 2
        offset = offset + total
        start, count = start + count, nodes
    own_a = sk_a[start * SK : (start + 1) * SK, :].astype(f32)
    exact = own_a[:, :128] + pltpu.roll(own_a[:, :128], 64, 1)
    top_ref[...] = jnp.where(lane < 64, exact, own_a[:, 128:])


def weights_kernel(layout, width, where_ref, light_ref, base_ref, upper_tiles_ref, top_ref, *refs):
    place_refs = refs[: 2 if layout.halves else 1]
    w_ref, coef_ref, pack_ref, perm, feats = refs[len(place_refs) :]
    blocks, rows = layout.blocks, layout.rows
    groups = range(len(layout.near))
    feats[...] = jnp.zeros_like(feats)

    def block(index, carry):
        fill_perm(perm, slot_row(layout.tail(place_refs, index)))
        light = [light_ref[layout.message(g, where_ref[0]), :, layout.lanes(index)] for g in groups]
        feats[LANES - width :, :] = lanes_of(light).astype(bf16)
        mine = aligned(index * rows, rows, rows)
        w_ref[mine, :] = nt(perm[...], feats[...]).astype(bf16)
        coef = nn(base_ref[index], w_ref[mine, :])
        coef_ref[aligned(index * SK, SK, SK), :] = split_coefs(coef)
        pack_ref[...] = coef
        return carry

    lax.fori_loop(0, blocks, block, 0)
    start, count = 0, blocks
    while count > 1:
        for j in range(count // 2):
            pair = slice((start + 2 * j) * SK, (start + 2 * j + 2) * SK)
            here = start + count + j
            coef = exact_product(upper_tiles_ref[here - blocks], coef_ref[pair, :])
            coef_ref[here * SK : (here + 1) * SK, :] = split_coefs(coef)
            pack_ref[...] = coef
        start, count = start + count, count // 2
    pack_ref[...] = top_ref[...] + pack_ref[...]


def near_phase(first, leaves, count_ref, list_ref, a_ref, bt_ref, w_ref, acc, times, tiles, ahead):
    every = count_ref.shape[1]

    def tally(leaf, filled):
        for other in range(every):
            times[other] = (leaf == other).astype(jnp.int32)

        def add(slot, carry):
            at = list_ref[leaf, slot]
            times[at] = times[at] + 1
            return carry

        lax.fori_loop(0, count_ref[0, leaf], add, 0)
        for other in range(every):
            tiles[0, filled] = leaf
            tiles[1, filled] = other
            tiles[2, filled] = times[other]
            filled = filled + (times[other] > 0).astype(jnp.int32)
        return filled

    filled = lax.fori_loop(first, first + leaves, tally, jnp.int32(0))
    tiles[0, filled] = first
    tiles[1, filled] = 0
    half = LEAF // 2
    acc[...] = jnp.zeros_like(acc)

    def exponents(tile, part):
        target = aligned(tiles[0, tile] * LEAF, LEAF, LEAF)
        source = aligned(tiles[1, tile] * LEAF + part * half, half, half)
        return nn(a_ref[target, :], bt_ref[:, source])

    def product(tile, part, block):
        source = aligned(tiles[1, tile] * LEAF + part * half, half, half)
        return nn(block, w_ref[source, :])

    ahead[...] = exponents(0, 0)

    def step(tile, carry):
        block = jnp.exp2(ahead[...]).astype(bf16)
        second = exponents(tile, 1)
        total = product(tile, 0, block)
        ahead[...] = exponents(tile + 1, 0)
        total = total + product(tile, 1, jnp.exp2(second).astype(bf16))
        here = aligned((tiles[0, tile] - first) * LEAF, LEAF, LEAF)
        acc[here, :] += tiles[2, tile].astype(f32) * total
        return carry

    lax.fori_loop(0, filled, step, 0)


def near_kernel(first, leaves, *refs):
    near_phase(first, leaves, *refs)


def far_phase(
    layout, first, held, low_levels, where_ref, pack_ref, small_ref, place_refs, a_ref, skt_ref, coef_ref,
    acc, out_ref, perm, tops, coefs, scaled,
):
    blocks, rows = layout.blocks, layout.rows
    groups = range(len(layout.near))
    ups, width = pack_ref.shape[0], out_ref.shape[1]
    levels = low_levels + ups
    lane = iota((SK, LANES), 1)
    for up in range(ups):
        pack = pack_ref[up]
        high, low = two(jnp.where(lane < 64, pack, 0.0))
        high, low = high.astype(f32), low.astype(f32)
        is_norm = (lane >= 64) & (lane < 67)
        norms = pltpu.roll(jnp.where(is_norm, pack, 0.0), 3, 1)
        at = slice((low_levels + up) * SK, (low_levels + up + 1) * SK)
        tops[0:128, at] = jnp.transpose(high + pltpu.roll(high, 64, 1)).astype(bf16)
        tops[128:256, at] = jnp.transpose(jnp.where(is_norm, 1.0, low + norms)).astype(bf16)
        coefs[at, :] = split_coefs(jnp.where(lane >= LANES - width, pack, 0.0))

    def block(index, carry):
        node, start, count = index, 0, blocks
        for level in range(low_levels):
            at = slice(level * SK, (level + 1) * SK)
            other = aligned((start + (node ^ 1)) * SK, SK, SK)
            tops[:, at] = skt_ref[:, other]
            coefs[at, :] = coef_ref[other, :]
            node, start, count = node // 2, start + count, count // 2
        fill_perm(perm, slot_row(layout.tail(place_refs, index)))
        halves = []
        for leaf in range(rows // LEAF):
            flags = layout.info(place_refs, small_ref, index, FLAGS + leaf)
            for level in range(levels):
                at = slice(level * SK, (level + 1) * SK)
                flag = jnp.sum(jnp.where(lane[0:1] == level, flags, 0.0), axis=1, keepdims=True)
                scaled[at, :] = (coefs[at, :].astype(f32) * flag).astype(bf16)
            here = aligned(index * rows + leaf * LEAF, LEAF, LEAF)
            near = aligned((index - first) * rows + leaf * LEAF, LEAF, LEAF)
            tile = jnp.exp2(nn(a_ref[here, :], tops[...]))
            total = acc[near, :] + exact_product(tile, scaled[...])
            halves.append(jnp.transpose(total)[LANES - width :, :])
        high, low = two(jnp.concatenate(halves, 1))
        moved = nn(jnp.concatenate([high, low], 0), perm[...])
        moved = moved[:width] + moved[width:]
        for g in groups:
            out_ref[layout.message(g, where_ref[0]), :, layout.lanes(index - first)] = moved[
                :, g * layout.per : (g + 1) * layout.per
            ]
        return carry

    lax.fori_loop(first, first + held, block, 0)


def far_kernel(layout, first, held, low_levels, where_ref, pack_ref, small_ref, *refs):
    count = 2 if layout.halves else 1
    far_phase(layout, first, held, low_levels, where_ref, pack_ref, small_ref, refs[:count], *refs[count:])


def both_kernel(layout, first, held, low_levels, where_ref, pack_ref, small_ref, *refs):
    count = 2 if layout.halves else 1
    place_refs, refs = refs[:count], refs[count:]
    count_ref, list_ref, a_ref, bt_ref, w_ref, skt_ref, coef_ref, out_ref = refs[:8]
    acc, times, tiles, ahead, perm, tops, coefs, scaled = refs[8:]
    leaves = held * layout.rows // LEAF
    first_leaf = first * layout.rows // LEAF
    near_phase(first_leaf, leaves, count_ref, list_ref, a_ref, bt_ref, w_ref, acc, times, tiles, ahead)
    far_phase(
        layout, first, held, low_levels, where_ref, pack_ref, small_ref, place_refs, a_ref, skt_ref, coef_ref,
        acc, out_ref, perm, tops, coefs, scaled,
    )


def final_kernel(pos_ref, *refs):
    back_refs, (weights_ref, out_ref, perm, vals) = refs[:-4], refs[-4:]
    chunks = pos_ref.shape[0]
    rows = chunks * LANES
    split = back_refs[0].shape[2]
    cols = jnp.concatenate([column(pos_ref[c : c + 1, :]) for c in range(chunks)], 0).astype(jnp.int32)
    for c in range(chunks):
        perm[:, c * LANES : (c + 1) * LANES] = onehot(iota((rows, LANES), 1) + c * LANES == cols)
    for part in range(back_refs[0].shape[0]):
        for half, back_ref in enumerate(back_refs):
            high, low = two(back_ref[part])
            at = (part * len(back_refs) + half) * split
            vals[0:LANES, at : at + split] = high
            vals[LANES:, at : at + split] = low
    step = 256
    for s in range(rows // step):
        here = slice(s * step, (s + 1) * step)
        moved = nt(perm[here, :], vals[...])
        out_ref[here, :] = ridge * weights_ref[here, :] + moved[:, :LANES] + moved[:, LANES:]


def upper_levels(pack, skeleton_upper, my_leaf, trees, blocks, width):
    devices = trees * blocks
    level = blocks.bit_length() - 1
    offset = sum(devices >> step for step in range(1, level + 1))
    lanes = jnp.arange(LANES)[None]
    is_point, is_norm = lanes < DIM, (lanes >= DIM) & (lanes < DIM + 3)
    is_coef = lanes >= LANES - width
    packs, own, stride = [], pack, 1
    while stride < trees:
        other = lax.ppermute(own, "leaf", [(i, i ^ stride) for i in range(trees)])
        packs.append(other)
        stride *= 2
        if stride < trees:
            second = (my_leaf // (stride // 2)) % 2 == 1
            pair = jnp.where(second, jnp.concatenate([other, own], 0), jnp.concatenate([own, other], 0))
            chosen = pair[skeleton_upper[offset + my_leaf // stride]]
            level += 1
            offset += devices >> level
            norms = jnp.sum(jnp.where(is_norm, pair, 0.0), axis=1)
            chosen_norms = jnp.sum(jnp.where(is_norm, chosen, 0.0), axis=1)
            inner = jnp.dot(
                jnp.where(is_point, chosen, 0.0), jnp.where(is_point, pair, 0.0).T, precision=highest
            )
            tile = jnp.exp2(inner + norms[None] + chosen_norms[:, None])
            own = jnp.where(is_coef, jnp.dot(tile, pair, precision=highest), chosen)
    return jnp.stack(packs)


def body(points, weights, tree_slot, near_count, near_list, skeleton_base, skeleton_upper, far_use):
    blocks, trees, reps = lax.axis_size("sub"), lax.axis_size("leaf"), lax.axis_size("rep")
    devices = blocks * trees
    rows, columns = weights.shape
    low_levels = blocks.bit_length() - 1
    ups = trees.bit_length() - 1
    width = columns // blocks
    part = rows // trees
    per = part // blocks
    total = blocks * rows
    leaves = total // LEAF
    my_leaf = lax.axis_index("leaf")
    fine = trees == 2 and per % LANES == 0 and blocks % reps == 0
    halves = reps if fine else 0
    layout = Layout(blocks, trees, rows, halves)
    split = part if fine else rows
    where = jnp.stack([my_leaf, lax.axis_index("rep")]).astype(jnp.int32)

    if fine:
        place_shapes = (shaped((PLACE_ROWS, split // halves), f32),) * trees
    else:
        place_shapes = (shaped((rows // split, PLACE_ROWS, split), f32),)
    light, *place, pos = pl.pallas_call(
        functools.partial(sort_kernel, halves),
        out_shape=(shaped((rows // split, columns, split), f32),) + place_shapes + (shaped((rows // LANES, LANES), f32),),
        in_specs=[spec(SMEM)] + [spec()] * 5,
        out_specs=(spec(),) * (2 + len(place_shapes)),
        scratch_shapes=[
            vm((rows, rows), bf16),
            vm((272, rows), bf16),
            vm((rows // split, PLACE_ROWS, split), f32),
        ],
        compiler_params=params(),
        name="sort_rows",
    )(where, tree_slot.reshape(rows // LANES, LANES), points.T, weights, skeleton_base, far_use)

    if fine:
        own, sent = place
        got = lax.ppermute(sent, "leaf", [(0, 1), (1, 0)])
        place = [lax.all_gather(one, ("sub", "rep"), axis=0, tiled=False) for one in (own, got)]
        light = light.reshape(devices, width, part)
        light = lax.all_to_all(light, ("leaf", "sub"), split_axis=0, concat_axis=0, tiled=True)
        small = jnp.zeros((1, 8, SK), f32)
    else:
        info = jnp.pad(far_use.astype(f32), ((FLAGS, 5 - far_use.shape[0]), (0, SK - far_use.shape[1])))
        small = lax.all_gather(info.at[BASE].set(skeleton_base[0].astype(f32)), "sub", axis=0, tiled=False)
        place = place[0].reshape(PLACE_ROWS, trees, part).transpose(1, 0, 2)
        place = lax.all_to_all(place, "leaf", split_axis=0, concat_axis=0, tiled=True)
        place = lax.all_gather(place, "sub", axis=0, tiled=False)
        place = place.transpose(1, 0, 2, 3).reshape(devices, PLACE_ROWS, blocks, per)
        place = [place.transpose(1, 2, 0, 3).reshape(1, PLACE_ROWS, total)]
        light = light.reshape(columns, trees, part).transpose(1, 0, 2).reshape(devices, width, part)
        light = lax.all_to_all(light, ("leaf", "sub"), split_axis=0, concat_axis=0, tiled=True)
        light = light.reshape(devices, width, blocks, per)
        light = light.transpose(1, 2, 0, 3).reshape(1, width, total)

    nodes = 2 * blocks - 1
    kept = len(place)
    feat_a, feat_bt, sk, base, upper_tiles, top = pl.pallas_call(
        functools.partial(points_kernel, layout, trees, width),
        out_shape=(
            shaped((total, FEAT), bf16),
            shaped((FEAT, total), bf16),
            shaped((FEAT, nodes * SK), bf16),
            shaped((blocks, SK, rows), bf16),
            shaped((blocks - 1, SK, 2 * SK), f32),
            shaped((SK, LANES), f32),
        ),
        in_specs=[spec(SMEM)] + [spec()] * (2 + kept),
        out_specs=(spec(),) * 6,
        scratch_shapes=[vm((rows, rows), bf16), vm((2 * FEAT, rows), bf16), vm((nodes * SK, FEAT), bf16)],
        compiler_params=params(),
        name="tree_points",
    )(where, skeleton_upper, small, *place)

    tree_light, coefs, pack = pl.pallas_call(
        functools.partial(weights_kernel, layout, width),
        out_shape=(
            shaped((total, LANES), bf16),
            shaped((nodes * SK, FEAT), bf16),
            shaped((SK, LANES), f32),
        ),
        in_specs=[spec(SMEM)] + [spec()] * (4 + kept),
        out_specs=(spec(),) * 3,
        scratch_shapes=[vm((rows, rows), bf16), vm((LANES, rows), bf16)],
        compiler_params=params(),
        name="tree_weights",
    )(where, light, base, upper_tiles, top, *place)

    packs = upper_levels(pack, skeleton_upper, my_leaf, trees, blocks, width)

    held = blocks // 2
    levels = low_levels + ups
    near_scratch = [
        pltpu.SMEM((leaves,), jnp.int32),
        pltpu.SMEM((3, leaves * leaves + 1), jnp.int32),
        vm((LEAF, LEAF // 2), f32),
    ]
    far_scratch = [
        vm((rows, rows), bf16),
        vm((FEAT, levels * SK), bf16),
        vm((levels * SK, FEAT), bf16),
        vm((levels * SK, FEAT), bf16),
    ]
    if fine:
        out_shape = shaped((devices, width, part // 2), f32)
    else:
        out_shape = shaped((1, width, total // 2), f32)
    near = pl.pallas_call(
        functools.partial(near_kernel, 0, leaves // 2),
        out_shape=shaped((total // 2, LANES), f32),
        in_specs=[spec(SMEM)] * 2 + [spec()] * 3,
        out_specs=spec(),
        scratch_shapes=near_scratch,
        compiler_params=params(),
        name="near_first",
    )(near_count, near_list[0], feat_a, feat_bt, tree_light)
    first_out = pl.pallas_call(
        functools.partial(far_kernel, layout, 0, held, low_levels),
        out_shape=out_shape,
        in_specs=[spec(SMEM)] + [spec()] * (6 + kept),
        out_specs=spec(),
        scratch_shapes=far_scratch,
        compiler_params=params(),
        name="far_first",
    )(where, packs, small, *place, feat_a, sk, coefs, near)
    second_out = pl.pallas_call(
        functools.partial(both_kernel, layout, held, blocks - held, low_levels),
        out_shape=out_shape,
        in_specs=[spec(SMEM)] + [spec()] * (2 + kept) + [spec(SMEM)] * 2 + [spec()] * 5,
        out_specs=spec(),
        scratch_shapes=[vm((total // 2, LANES), f32)] + near_scratch + far_scratch,
        compiler_params=params(),
        name="near_far_second",
    )(where, packs, small, *place, near_count, near_list[0], feat_a, feat_bt, tree_light, sk, coefs)

    def give_back(out):
        if not fine:
            out = out.reshape(width, held, devices, per).transpose(2, 0, 1, 3).reshape(devices, width, part // 2)
        out = lax.all_to_all(out, ("leaf", "sub"), split_axis=0, concat_axis=0, tiled=True)
        return out.reshape(trees, columns, part // 2)

    back = [give_back(first_out), give_back(second_out)]
    if not fine:
        back = jnp.concatenate(back, 2).transpose(1, 0, 2).reshape(1, columns, rows)
        back = [back]

    return pl.pallas_call(
        final_kernel,
        out_shape=shaped((rows, columns), f32),
        in_specs=[spec()] * (2 + len(back)),
        out_specs=spec(),
        scratch_shapes=[vm((rows, rows), bf16), vm((2 * LANES, rows), bf16)],
        compiler_params=params(),
        name="to_input_order",
    )(pos, *back, weights)


def solution(mesh):
    in_specs = (
        P(("groups", "leaf", "sub"), None),
        P(("groups", "leaf", "sub"), "rep"),
        P(("groups", "leaf", "sub")),
        P(("groups", "leaf"), None),
        P(("groups", "leaf"), None, None),
        P(("groups", "leaf", "sub"), None),
        P("groups", None),
        P(("groups", "leaf", "sub"), None),
    )
    out_specs = P(("groups", "leaf", "sub"), "rep")
    return jax.shard_map(body, mesh=mesh, in_specs=in_specs, out_specs=out_specs, check_vma=False)
```

time: 312 us -> 134 us (0.43)
  waiting for transfers between devices: 81.8 us -> 0.01 us
  blocking collectives: 127 us -> 50.3 us
  Pallas kernels: 0 us -> 49.6 us
  local copies, waits for them, and re-layouts: 36.3 us -> 15.2 us
  matrix products: 20.3 us -> 0 us
  between operations: 13.8 us -> 0.11 us
  other arithmetic: 11.6 us -> 0.07 us
    all_to_all x1, blocking collectives: 127 us -> 14.7 us  [give_back(): lax.all_to_all(out, ('leaf', 'sub'), split_axis=0, concat_axis=0, tiled=T...]
    pallas_call x0 -> x7, Pallas kernels: none -> 49.6 us  [the longest x1 16.1 us: body(): pl.pallas_call(functools.partial(both_kernel, layout, held, blocks - held...]
    all_gather x0 -> x2, blocking collectives: none -> 35.7 us  [body(): lax.all_gather(one, ('sub', 'rep'), axis=0, tiled=False)]
    all_to_all x3 -> x2, waiting for transfers between devices: 32.2 us -> 0.01 us  [the longest x1 0.01 us: body(): lax.all_to_all(light, ('leaf', 'sub'), split_axis=0, concat_axis=0, tiled...]
    all_gather x2 -> x0, waiting for transfers between devices: 27.5 us -> none  [the longest x1 27.5 us: body(): lax.all_gather(tree_points, 'sub', axis=0, tiled=True)]
    ppermute x6 -> x2, waiting for transfers between devices: 22.1 us -> 0.01 us  [the longest x1 0.01 us: body(): got = lax.ppermute(sent, 'leaf', [(0, 1), (1, 0)])]
    gather x23 -> x0, local copies, waits for them, and re-layouts: 20.7 us -> none  [the longest x1 4.52 us: body(): tree_slot[order] % rows]
    dot_general x18 -> x0, matrix products: 20.3 us -> none  [the longest x9 13.8 us: kernel(): jnp.dot(targets, sources.T, precision=highest, preferred_element_type=jnp...]
  transfers between devices with their start and end apart: 11 -> 4, of which waited for: 10 -> 0; matrix products, arithmetic and copies ran while one was open for 10% -> 0% of each run, Pallas kernels for 0% -> 24%
where the time goes in v2:
time: 134 us
  blocking collectives  50.3 us (38%)
  Pallas kernels  49.6 us (37%)
  starting transfers between devices  18.3 us (14%)
  local copies, waits for them, and re-layouts  15.2 us (11%)
    all_gather x2, blocking collectives, body(): lax.all_gather(one, ('sub', 'rep'), axis=0, tiled=False)  35.7 us
    pallas_call x1, Pallas kernels, body(): pl.pallas_call(functools.partial(both_kernel, layout, held, blocks - held...  16.1 us
    unnamed x46, local copies, waits for them, and re-layouts  15.2 us
    all_to_all x1, blocking collectives, give_back(): lax.all_to_all(out, ('leaf', 'sub'), split_axis=0, concat_axis=0, tiled=T...  14.7 us
    pallas_call x1, Pallas kernels, body(): pl.pallas_call(functools.partial(points_kernel, layout, trees, width), ou...  8.86 us
    pallas_call x1, Pallas kernels, body(): pl.pallas_call(functools.partial(near_kernel, 0, leaves // 2), out_shape=...  7.73 us
    all_to_all x1, starting transfers between devices, give_back(): lax.all_to_all(out, ('leaf', 'sub'), split_axis=0, concat_axis=0, tiled=T...  7.32 us
    all_to_all x1, starting transfers between devices, body(): lax.all_to_all(light, ('leaf', 'sub'), split_axis=0, concat_axis=0, tiled...  7.25 us
  transfers between devices with their start and end apart: 4, of which 0 were waited for; matrix products, arithmetic and copies ran while one was open for 0% of the time, Pallas kernels for 24%

profile of v2, /device:TPU:0, one launch (start us, length us, event | category | flops | bytes accessed | tf_op | source)
XLA Modules:
  0.0 133.6 jit_solution(4906178397848850633)
XLA Ops:
  0.1 1.0 copy-done.2
  1.1 0.9 copy-done.15
  4.1 3.1 %sort_rows.1 = (f32[2,128,512]{2,1,0:T(8,128)}, f32[72,256]{1,0:T(8,128)S(1)}, f32[72,256]{1,0:T(8,128)S(1)}, f32[8,128]{1,0:T(8,128)S(1)}) custom-call(s32[2]{0:T(128)S(1)} %pad_add_fusion.where_ref, s32[8,128]{1,0:T(8,128)S(1)} %bitcast.25, f32[64,1024]{1,0:T(8,128)S(1)} %bitcast.22, f32[1024,128]{1,0:T(8,128)S(1)} %copy-done.2, s32[1,128]{1,0:T(1,128)S(1)} %copy-done.22, ...), custom_call_target="tpu_custom_call" | custom-call | tf_op jit(solution)/shard_map/sort_rows/pallas_call | solution.py:476
  7.1 7.3 %all-to-all-start = ((f32[8,32,512]{2,1,0:T(8,128)}), f32[8,32,512]{2,1,0:T(8,128)}, u32[]{:S(2)}, u32[]{:S(2)}) async-start(f32[8,32,512]{2,1,0:T(8,128)} %bitcast.4), calls=%async_computation | async-start | bytes 1048576 | tf_op jit(solution)/shard_map/all_to_all | solution.py:495
  14.4 2.0 %collective-permute-start = (f32[72,256]{1,0:T(8,128)S(1)}, f32[72,256]{1,0:T(8,128)S(1)}, u32[]{:S(2)}, u32[]{:S(2)}) collective-permute-start(f32[72,256]{1,0:T(8,128)S(1)} %get-tuple-element.21), channel_id=1, source_target_pairs={{0,8},{8,0},{1,9},{9,1},{2,10},{10,2},{3,11},{11,3},{4,12},{12,4},... | collective-permute-start | bytes 221192 | tf_op jit(solution)/shard_map/ppermute | solution.py:492
  16.4 20.7 %all-gather = f32[576,256]{1,0:T(8,128)S(1)} all-gather(f32[72,256]{1,0:T(8,128)S(1)} %get-tuple-element.20), channel_id=2, replica_groups=mesh['groups'=2,'leaf'=2,'sub'=4,'rep'=2] {'sub','rep'}, dimensions={0}, use_global_device_ids=true | all-gather | bytes 663552 | tf_op jit(solution)/shard_map/all_gather | solution.py:493
  37.1 15.0 %all-gather.1 = f32[576,256]{1,0:T(8,128)S(1)} all-gather(f32[72,256]{1,0:T(8,128)S(1)} %collective-permute-done), channel_id=3, replica_groups=mesh['groups'=2,'leaf'=2,'sub'=4,'rep'=2] {'sub','rep'}, dimensions={0}, use_global_device_ids=true | all-gather | bytes 663552 | tf_op jit(solution)/shard_map/all_gather | solution.py:493
  52.1 8.9 %tree_points.1 = (bf16[4096,256]{1,0:T(8,128)(2,1)S(1)}, bf16[256,4096]{1,0:T(8,128)(2,1)}, bf16[256,896]{1,0:T(8,128)(2,1)S(1)}, bf16[4,128,1024]{2,1,0:T(8,128...) custom-call(s32[2]{0:T(128)S(1)} %pad_add_fusion.where_ref, s32[6,128]{1,0:T(8,128)S(1)} %copy-done.18, ...), custom_call_target="tpu_custom_call" | custom-call | tf_op jit(solution)/shard_map/tree_points/pallas_call | solution.py:512
  61.7 1.0 copy-done.9
  63.5 1.2 copy-done.10
  64.7 1.0 copy-done.12
  65.7 5.7 %tree_weights.1 = (bf16[4096,128]{1,0:T(8,128)(2,1)S(1)}, bf16[896,256]{1,0:T(8,128)(2,1)S(1)}, f32[128,128]{1,0:T(8,128)S(1)}) custom-call(s32[2]{0:T(128)S(1)} %pad_add_fusion.where_ref, f32[8,32,512]{2,1,0:T(8,128)} %all-to-all-done.light_ref, bf16[4,128,1024]{2,1,0:T(8,128)(2,1)S(1)} %copy-done.10, f32[3,128,256]{2,1,0:T(8,128)S(1)} %copy-done.12, ...), custom_call_target="tpu_custom_call" | custom-call | tf_op jit(solution)/shard_map/tree_weights/pallas_call | solution.py:529
  71.5 1.7 %collective-permute-start.1 = (f32[128,128]{1,0:T(8,128)S(1)}, f32[128,128]{1,0:T(8,128)S(1)}, u32[]{:S(2)}, u32[]{:S(2)}) collective-permute-start(f32[128,128]{1,0:T(8,128)S(1)} %get-tuple-element.25), channel_id=1, source_target_pairs={{0,8},{8,0},{1,9},{9,1},{2,10},{10,2},{3,11},{11,3},{4,12},{12,4},... | collective-permute-start | bytes 196616 | tf_op jit(solution)/shard_map/ppermute | solution.py:435
  73.2 7.7 %near_first.1.refs_5_ = f32[2048,128]{1,0:T(8,128)S(1)} custom-call(s32[1,8]{1,0:T(1,128)S(1)} %copy-done.19, s32[8,16]{1,0:T(8,128)S(1)} %bitcast.23, bf16[4096,256]{1,0:T(8,128)(2,1)S(1)} %get-tuple-element.26.refs_2_.refs_4_, bf16[256,4096]{1,0:T(8,128)(2,1)} %get-tuple-element.29.refs_3_.refs_5_, bf16[4096,128]{1,0:T(8,128)(2,1)S(1)} %get-tuple-element.30.refs_4_.refs_6_), custom_call_target="tpu_custom_call" | custom-call | tf_op jit(solution)/shard_map/near_first/pallas_call | solution.py:562
  80.9 5.1 %far_first.1 = f32[8,32,256]{2,1,0:T(8,128)} custom-call(s32[2]{0:T(128)S(1)} %pad_add_fusion.where_ref, f32[1,128,128]{2,1,0:T(8,128)S(1)} %bitcast.20, f32[1,8,128]{2,1,0:T(8,128)S(1)} %broadcast_in_dim.3.small_ref, f32[8,72,256]{2,1,0:T(8,128)S(1)} %bitcast.13, f32[8,72,256]{2,1,0:T(8,128)S(1)} %bitcast.17, ...), custom_call_target="tpu_custom_call" | custom-call | tf_op jit(solution)/shard_map/far_first/pallas_call | solution.py:571
  86.7 7.3 %all-to-all-start.1 = ((f32[8,32,256]{2,1,0:T(8,128)}), f32[8,32,256]{2,1,0:T(8,128)}, u32[]{:S(2)}, u32[]{:S(2)}) async-start(f32[8,32,256]{2,1,0:T(8,128)} %far_first.1), calls=%async_computation.1 | async-start | bytes 524288 | tf_op jit(solution)/shard_map/all_to_all | solution.py:593
  94.0 1.2 copy-done.1
  95.2 1.0 copy-done.6
  96.2 1.0 copy-done.8
  97.2 0.8 copy-done.14
  98.7 16.1 %near_far_second.1 = f32[8,32,256]{2,1,0:T(8,128)S(1)} custom-call(s32[2]{0:T(128)S(1)} %pad_add_fusion.where_ref, f32[1,128,128]{2,1,0:T(8,128)S(1)} %bitcast.21, f32[1,8,128]{2,1,0:T(8,128)S(1)} %broadcast_in_dim.3.small_ref, f32[8,72,256]{2,1,0:T(8,128)S(1)} %bitcast.14, f32[8,72,256]{2,1,0:T(8,128)S(1)} %bitcast.18, s32[1,8]{1,0:T(1,128)S(1)} %copy-done.20, ...), custom_call_target="tpu_custom_call" | custom-call | tf_op jit(solution)/shard_map/near_far_second/pallas_call | solution.py:580
  114.9 14.7 %all_to_all.15 = f32[8,32,256]{2,1,0:T(8,128)S(1)} all-to-all(f32[8,32,256]{2,1,0:T(8,128)S(1)} %near_far_second.1), channel_id=1, replica_groups=mesh['groups'=2,'leaf'=2,'sub'=4,'rep'=2] {'leaf','sub'}, dimensions={0} | all-to-all | bytes 524288 | tf_op jit(solution)/shard_map/all_to_all | solution.py:593
  129.6 1.0 copy-done.3
  130.6 3.0 %to_input_order.1 = f32[1024,128]{1,0:T(8,128)} custom-call(f32[8,128]{1,0:T(8,128)S(1)} %get-tuple-element.18.pos_ref, f32[2,128,256]{2,1,0:T(8,128)} %bitcast.9.refs_0_, f32[2,128,256]{2,1,0:T(8,128)S(1)} %bitcast.19, f32[1024,128]{1,0:T(8,128)S(1)} %copy-done.3), custom_call_target="tpu_custom_call" | custom-call | tf_op jit(solution)/shard_map/to_input_order/pallas_call | solution.py:601
  (42 shorter events, 4.9 us)
Async XLA Ops:
  0.0 52.1 %copy-start.18 = (s32[6,128]{1,0:T(8,128)S(1)}, s32[6,128]{1,0:T(8,128)}, u32[]{:S(2)}) copy-start(s32[6,128]{1,0:T(8,128)} %upper_ref.1) | copy-start | bytes 9220
  0.1 1.0 copy-start.2
  1.1 0.9 copy-start.15
  2.1 0.7 copy-start.17
  2.8 0.7 copy-start.21
  7.1 56.3 %all-to-all-start = ((f32[8,32,512]{2,1,0:T(8,128)}), f32[8,32,512]{2,1,0:T(8,128)}, u32[]{:S(2)}, u32[]{:S(2)}) async-start(f32[8,32,512]{2,1,0:T(8,128)} %bitcast.4), calls=%async_computation | async-start | bytes 1048576 | tf_op jit(solution)/shard_map/all_to_all | solution.py:495
  14.4 22.7 %collective-permute-start = (f32[72,256]{1,0:T(8,128)S(1)}, f32[72,256]{1,0:T(8,128)S(1)}, u32[]{:S(2)}, u32[]{:S(2)}) collective-permute-start(f32[72,256]{1,0:T(8,128)S(1)} %get-tuple-element.21), channel_id=1, source_target_pairs={{0,8},{8,0},{1,9},{9,1},{2,10},{10,2},{3,11},{11,3},{4,12},{12,4},... | collective-permute-start | bytes 221192 | tf_op jit(solution)/shard_map/ppermute | solution.py:492
  52.1 21.1 %copy-start.16 = (s32[1,8,16]{2,1,0:T(8,128)S(1)}, s32[1,8,16]{2,1,0:T(8,128)}, u32[]{:S(2)}) copy-start(s32[1,8,16]{2,1,0:T(8,128)} %param.12) | copy-start | bytes 1540
  52.1 21.1 %copy-start.19 = (s32[1,8]{1,0:T(1,128)S(1)}, s32[1,8]{1,0:T(1,128)}, u32[]{:S(2)}) copy-start(s32[1,8]{1,0:T(1,128)} %refs_2_.2) | copy-start | bytes 100
  61.0 0.8 copy-start.4
  61.7 1.0 copy-start.9
  62.7 0.7 copy-start.11
  63.5 1.2 copy-start.10
  64.7 1.0 copy-start.12
  71.5 9.4 %copy-start = (bf16[4096,128]{1,0:T(8,128)(2,1)}, bf16[4096,128]{1,0:T(8,128)(2,1)S(1)}, u32[]{:S(2)}) copy-start(bf16[4096,128]{1,0:T(8,128)(2,1)S(1)} %get-tuple-element.30.refs_4_.refs_6_) | copy-start | bytes 3145732
  71.5 9.5 %copy-start.7 = (bf16[896,256]{1,0:T(8,128)(2,1)}, bf16[896,256]{1,0:T(8,128)(2,1)S(1)}, u32[]{:S(2)}) copy-start(bf16[896,256]{1,0:T(8,128)(2,1)S(1)} %get-tuple-element.28.refs_4_.refs_8_) | copy-start | bytes 1376260
  71.5 9.4 %collective-permute-start.1 = (f32[128,128]{1,0:T(8,128)S(1)}, f32[128,128]{1,0:T(8,128)S(1)}, u32[]{:S(2)}, u32[]{:S(2)}) collective-permute-start(f32[128,128]{1,0:T(8,128)S(1)} %get-tuple-element.25), channel_id=1, source_target_pairs={{0,8},{8,0},{1,9},{9,1},{2,10},{10,2},{3,11},{11,3},{4,12},{12,4},... | collective-permute-start | bytes 196616 | tf_op jit(solution)/shard_map/ppermute | solution.py:435
  73.2 7.8 %copy-start.5 = (bf16[256,896]{1,0:T(8,128)(2,1)S(1)}, bf16[256,896]{1,0:T(8,128)(2,1)}, u32[]{:S(2)}) copy-start(bf16[256,896]{1,0:T(8,128)(2,1)} %copy-done.4) | copy-start | bytes 1376260
  86.7 28.2 %all-to-all-start.1 = ((f32[8,32,256]{2,1,0:T(8,128)}), f32[8,32,256]{2,1,0:T(8,128)}, u32[]{:S(2)}, u32[]{:S(2)}) async-start(f32[8,32,256]{2,1,0:T(8,128)} %far_first.1), calls=%async_computation.1 | async-start | bytes 524288 | tf_op jit(solution)/shard_map/all_to_all | solution.py:593
  94.0 1.2 copy-start.1
  95.2 1.0 copy-start.6
  96.2 1.0 copy-start.8
  97.2 0.8 copy-start.14
  129.6 1.0 copy-start.3
  (3 other events, 1.9 us)

commit v3 on v2

v3 whole, which is shorter than its diff:
```python
import functools
import math

import jax
import jax.numpy as jnp
from jax import lax
from jax.experimental import pallas as pl
from jax.experimental.pallas import tpu as pltpu
from jax.sharding import PartitionSpec as P

DIM = 64
LEAF = 512
SK = 128
LANES = 128
FEAT = 256

highest = lax.Precision.HIGHEST
point_scale = math.sqrt(2.0 * math.log2(math.e) / 32.0)
ridge = 0.5
PLACE_ROWS = 72
TAIL = 64
SLOT, NORM, BASE, FLAGS = 0, 1, 2, 3
f32 = jnp.float32
bf16 = jnp.bfloat16
VMEM = pltpu.MemorySpace.VMEM
SMEM = pltpu.MemorySpace.SMEM


def spec(space=VMEM):
    return pl.BlockSpec(memory_space=space)


def params():
    return pltpu.CompilerParams(vmem_limit_bytes=58 * 1024 * 1024)


def vm(shape, dtype):
    return pltpu.VMEM(shape, dtype)


def shaped(shape, dtype):
    return jax.ShapeDtypeStruct(shape, dtype)


def nt(left, right):
    return lax.dot_general(left, right, (((1,), (1,)), ((), ())), preferred_element_type=f32)


def nn(left, right):
    return jnp.dot(left, right, preferred_element_type=f32)


def column(row):
    return jnp.transpose(jnp.broadcast_to(row, (LANES, LANES)))


def iota(shape, dim):
    return lax.broadcasted_iota(jnp.int32, shape, dim)


def onehot(mask):
    return jnp.where(mask, 1.0, 0.0).astype(bf16)


def two(value):
    high = value.astype(bf16)
    return high, (value - high.astype(f32)).astype(bf16)


def three(value):
    high = value.astype(bf16).astype(f32)
    mid = (value - high).astype(bf16).astype(f32)
    return high, mid, (value - high - mid).astype(bf16).astype(f32)


def lanes_of(blocks):
    return blocks[0] if len(blocks) == 1 else jnp.concatenate(blocks, 1)


def aligned(start, size, unit):
    return pl.ds(pl.multiple_of(start, unit), size)


def exact_product(block, coefs):
    high, low = two(block)
    first = nn(high, coefs)
    return first[:, :LANES] + first[:, LANES:] + nn(low, coefs[:, :LANES])


def split_coefs(value):
    high, low = two(value)
    return jnp.concatenate([high, low], 1)


def sort_kernel(blocks, where_ref, slot_ref, points_ref, weights_ref, base_ref, flag_ref, place_ref, pos_ref, *refs):
    light_refs, (perm, vals, whole, light) = refs[:-4], refs[-4:]
    chunks, split = slot_ref.shape[0], light.shape[-1]
    rows = chunks * LANES
    slots = slot_ref[...]
    slot = slots.astype(f32)
    within = slots & (rows - 1)
    high, low = (within >> 5).astype(f32), (within & 31).astype(f32)
    cols = jnp.concatenate([column(slot[c : c + 1]) for c in range(chunks)], 0)
    before = jnp.zeros((rows, LANES), f32)
    for c in range(chunks):
        before += jnp.where(slot[c : c + 1] < cols, 1.0, 0.0)
    rank = jnp.broadcast_to(jnp.sum(before, axis=1, keepdims=True), (rows, LANES))
    place_of = rank.astype(jnp.int32)
    for c in range(chunks):
        at = slice(c * LANES, (c + 1) * LANES)
        pos_ref[c : c + 1, :] = jnp.transpose(rank[at])[0:1]
        perm[:, at] = onehot(iota((rows, LANES), 1) + c * LANES == place_of)
        vals[0:LANES, at] = jnp.transpose(weights_ref[at, :]).astype(bf16)
    scaled = points_ref[...] * point_scale
    ph, plo = two(scaled)
    nh, nm, nl = three(-0.5 * jnp.sum(scaled * scaled, axis=0, keepdims=True))
    vals[128:192, :] = ph
    vals[192:256, :] = plo
    sub = iota((16, LANES), 0)
    for c in range(chunks):
        at = slice(c * LANES, (c + 1) * LANES)
        extra = jnp.where(sub == 0, high[c : c + 1], jnp.where(sub == 1, low[c : c + 1], 0.0))
        extra = jnp.where(sub == 2, nh[:, at], jnp.where(sub == 3, nm[:, at], extra))
        vals[256:272, at] = jnp.where(sub == 4, nl[:, at], extra).astype(bf16)
    step = 256
    for s in range(rows // step):
        moved = nn(vals[...], perm[:, s * step : (s + 1) * step])
        at = slice((s * step) % split, (s * step) % split + step)
        part = (s * step) // split
        light[part, :, at] = moved[0:LANES]
        whole[part, 0:TAIL, at] = moved[128:192] + moved[192:256]
        tail = iota((8, step), 0)
        slot_row = moved[256:257] * 32.0 + moved[257:258]
        norm_row = moved[258:259] + moved[259:260] + moved[260:261]
        whole[part, TAIL:, at] = jnp.where(tail == SLOT, slot_row, jnp.where(tail == NORM, norm_row, 0.0))
    if not blocks:
        place_ref[...] = whole[0]
        light_refs[0][...] = light[0]
        return
    leaf, sub, core = where_ref[0], where_ref[1], where_ref[2]
    place_ref[...] = whole[leaf ^ core]
    place_ref[TAIL + BASE : TAIL + BASE + 1, 0:SK] = base_ref[...].astype(f32)
    place_ref[TAIL + FLAGS : TAIL + FLAGS + flag_ref.shape[0], 0 : flag_ref.shape[1]] = flag_ref[...].astype(f32)
    width = LANES // blocks
    for g, light_ref in enumerate(light_refs):
        columns = aligned((sub ^ (g % blocks)) * width, width, width)
        light_ref[...] = light[leaf ^ core ^ (g // blocks), columns, :]


class Layout:
    def __init__(self, blocks, trees, rows, fine):
        self.blocks, self.rows, self.fine = blocks, rows, fine
        self.count = blocks * trees if fine else 1
        self.per = rows // self.count

    def lanes(self, index):
        return aligned(index * self.per, self.per, LANES)

    def gather(self, refs, index, part):
        return lanes_of([ref[part, self.lanes(index)] for ref in refs])

    def info(self, where_ref, refs, small_ref, index):
        if not self.fine:
            return small_ref[index]
        core = where_ref[2]
        found = jnp.zeros((PLACE_ROWS - TAIL, SK), f32)
        for step in range(self.blocks):
            mine, theirs = refs[step][TAIL:, 0:SK], refs[self.blocks + step][TAIL:, 0:SK]
            here = jnp.where(core == 0, mine, theirs)
            found = jnp.where((where_ref[1] ^ step) == index, here, found)
        return found


def fill_perm(out, slot_rows):
    for c in range(out.shape[1] // LANES):
        at = slice(c * LANES, (c + 1) * LANES)
        out[:, at] = onehot(iota((out.shape[0], LANES), 0) == slot_rows[:, at].astype(jnp.int32))


def points_kernel(layout, trees, where_ref, upper_ref, small_ref, *refs):
    place_refs, refs = refs[: layout.count], refs[layout.count :]
    a_ref, bt_ref, skt_ref, base_ref, upper_tiles_ref, top_ref, slot_ref, info_ref, perm, feats, sk_a = refs
    blocks, rows = layout.blocks, layout.rows
    lane = iota((SK, LANES), 1)

    def block(index, carry):
        tail = layout.gather(place_refs, index, slice(TAIL, PLACE_ROWS))
        slots = tail[SLOT : SLOT + 1]
        slot_ref[pl.ds(index, 1), :] = slots
        info = layout.info(where_ref, place_refs, small_ref, index)
        info_ref[index] = info
        points = layout.gather(place_refs, index, slice(0, TAIL))
        high, low = two(points)
        nh, nm, nl = three(tail[NORM : NORM + 1])
        sub = iota((64, rows), 0)
        extra_a = jnp.where(sub == 0, nh, jnp.where(sub == 1, nm, jnp.where(sub == 2, nl, 0.0)))
        extra_a = jnp.where((sub >= 3) & (sub < 6), 1.0, extra_a)
        extra_b = jnp.where(sub == 3, nh, jnp.where(sub == 4, nm, jnp.where(sub == 5, nl, 0.0)))
        extra_b = jnp.where(sub < 3, 1.0, extra_b)
        feats[0:64, :] = high
        feats[64:128, :] = low
        feats[128:192, :] = high
        feats[192:256, :] = extra_a.astype(bf16)
        feats[256:320, :] = high
        feats[320:384, :] = high
        feats[384:448, :] = low
        feats[448:512, :] = extra_b.astype(bf16)
        fill_perm(perm, slots)
        mine = aligned(index * rows, rows, rows)
        a_ref[mine, :] = nt(perm[...], feats[0:FEAT, :]).astype(bf16)
        bt_ref[:, mine] = nt(feats[FEAT:, :], perm[...]).astype(bf16)
        picks = column(info[BASE : BASE + 1]).astype(jnp.int32)
        chosen = jnp.concatenate([onehot(lane + c * LANES == picks) for c in range(rows // LANES)], 1)
        node = aligned(index * SK, SK, SK)
        own_a = nn(chosen, a_ref[mine, :]).astype(bf16)
        sk_a[node, :] = own_a
        skt_ref[:, node] = nt(bt_ref[:, mine], chosen).astype(bf16)
        base_ref[index] = jnp.exp2(nn(own_a, bt_ref[:, mine])).astype(bf16)
        return carry

    lax.fori_loop(0, blocks, block, 0)
    start, count, offset, total = 0, blocks, 0, blocks * trees
    while count > 1:
        nodes = count // 2
        for j in range(nodes):
            pair = slice((start + 2 * j) * SK, (start + 2 * j + 2) * SK)
            row = offset + where_ref[0] * nodes + j
            picks = column(upper_ref[pl.ds(row, 1), :].astype(f32)).astype(jnp.int32)
            chosen = jnp.concatenate([onehot(lane == picks), onehot(lane + LANES == picks)], 1)
            here = start + count + j
            new = slice(here * SK, (here + 1) * SK)
            own_a = nn(chosen, sk_a[pair, :]).astype(bf16)
            sk_a[new, :] = own_a
            skt_ref[:, new] = nt(skt_ref[:, pair], chosen).astype(bf16)
            upper_tiles_ref[here - blocks] = jnp.exp2(nn(own_a, skt_ref[:, pair]))
        total = total // 2
        offset = offset + total
        start, count = start + count, nodes
    own_a = sk_a[start * SK : (start + 1) * SK, :].astype(f32)
    exact = own_a[:, :128] + pltpu.roll(own_a[:, :128], 64, 1)
    top_ref[...] = jnp.where(lane < 64, exact, own_a[:, 128:])


def weights_kernel(layout, base_ref, upper_tiles_ref, top_ref, slot_ref, *refs):
    light_refs, (w_ref, coef_ref, pack_ref, perm, feats) = refs[: layout.count], refs[layout.count :]
    blocks, rows = layout.blocks, layout.rows
    width = light_refs[0].shape[0]
    feats[...] = jnp.zeros_like(feats)

    def block(index, carry):
        fill_perm(perm, slot_ref[pl.ds(index, 1), :])
        feats[LANES - width :, :] = layout.gather(light_refs, index, slice(0, width)).astype(bf16)
        mine = aligned(index * rows, rows, rows)
        w_ref[mine, :] = nt(perm[...], feats[...]).astype(bf16)
        coef = nn(base_ref[index], w_ref[mine, :])
        coef_ref[aligned(index * SK, SK, SK), :] = split_coefs(coef)
        pack_ref[...] = coef
        return carry

    lax.fori_loop(0, blocks, block, 0)
    start, count = 0, blocks
    while count > 1:
        for j in range(count // 2):
            pair = slice((start + 2 * j) * SK, (start + 2 * j + 2) * SK)
            here = start + count + j
            coef = exact_product(upper_tiles_ref[here - blocks], coef_ref[pair, :])
            coef_ref[here * SK : (here + 1) * SK, :] = split_coefs(coef)
            pack_ref[...] = coef
        start, count = start + count, count // 2
    pack_ref[...] = top_ref[...] + pack_ref[...]


def near_kernel(count_ref, list_ref, a_ref, bt_ref, w_ref, acc, times, tiles, ahead):
    every = count_ref.shape[1]

    def tally(leaf, filled):
        for other in range(every):
            times[other] = (leaf == other).astype(jnp.int32)

        def add(slot, carry):
            at = list_ref[leaf, slot]
            times[at] = times[at] + 1
            return carry

        lax.fori_loop(0, count_ref[0, leaf], add, 0)
        for other in range(every):
            tiles[0, filled] = leaf
            tiles[1, filled] = other
            tiles[2, filled] = times[other]
            filled = filled + (times[other] > 0).astype(jnp.int32)
        return filled

    filled = lax.fori_loop(0, every, tally, jnp.int32(0))
    tiles[0, filled] = 0
    tiles[1, filled] = 0
    half = LEAF // 2
    acc[...] = jnp.zeros_like(acc)

    def exponents(tile, part):
        target = aligned(tiles[0, tile] * LEAF, LEAF, LEAF)
        source = aligned(tiles[1, tile] * LEAF + part * half, half, half)
        return nn(a_ref[target, :], bt_ref[:, source])

    def product(tile, part, block):
        source = aligned(tiles[1, tile] * LEAF + part * half, half, half)
        return nn(block, w_ref[source, :])

    ahead[...] = exponents(0, 0)

    def step(tile, carry):
        block = jnp.exp2(ahead[...]).astype(bf16)
        second = exponents(tile, 1)
        total = product(tile, 0, block)
        ahead[...] = exponents(tile + 1, 0)
        total = total + product(tile, 1, jnp.exp2(second).astype(bf16))
        here = aligned(tiles[0, tile] * LEAF, LEAF, LEAF)
        acc[here, :] += tiles[2, tile].astype(f32) * total
        return carry

    lax.fori_loop(0, filled, step, 0)


def far_kernel(layout, low_levels, pack_ref, slot_ref, info_ref, a_ref, skt_ref, coef_ref, near_ref, *refs):
    out_refs, (perm, tops, coefs, scaled) = refs[: layout.count], refs[layout.count :]
    blocks, rows = layout.blocks, layout.rows
    ups, width = pack_ref.shape[0], out_refs[0].shape[0]
    levels = low_levels + ups
    lane = iota((SK, LANES), 1)
    for up in range(ups):
        pack = pack_ref[up]
        high, low = two(jnp.where(lane < 64, pack, 0.0))
        high, low = high.astype(f32), low.astype(f32)
        is_norm = (lane >= 64) & (lane < 67)
        norms = pltpu.roll(jnp.where(is_norm, pack, 0.0), 3, 1)
        at = slice((low_levels + up) * SK, (low_levels + up + 1) * SK)
        tops[0:128, at] = jnp.transpose(high + pltpu.roll(high, 64, 1)).astype(bf16)
        tops[128:256, at] = jnp.transpose(jnp.where(is_norm, 1.0, low + norms)).astype(bf16)
        coefs[at, :] = split_coefs(jnp.where(lane >= LANES - width, pack, 0.0))

    def block(index, carry):
        node, start, count = index, 0, blocks
        for level in range(low_levels):
            at = slice(level * SK, (level + 1) * SK)
            other = aligned((start + (node ^ 1)) * SK, SK, SK)
            tops[:, at] = skt_ref[:, other]
            coefs[at, :] = coef_ref[other, :]
            node, start, count = node // 2, start + count, count // 2
        fill_perm(perm, slot_ref[pl.ds(index, 1), :])
        info = info_ref[index]
        halves = []
        for leaf in range(rows // LEAF):
            flags = info[FLAGS + leaf : FLAGS + leaf + 1]
            for level in range(levels):
                at = slice(level * SK, (level + 1) * SK)
                flag = jnp.sum(jnp.where(lane[0:1] == level, flags, 0.0), axis=1, keepdims=True)
                scaled[at, :] = (coefs[at, :].astype(f32) * flag).astype(bf16)
            here = aligned(index * rows + leaf * LEAF, LEAF, LEAF)
            tile = jnp.exp2(nn(a_ref[here, :], tops[...]))
            total = near_ref[here, :] + exact_product(tile, scaled[...])
            halves.append(jnp.transpose(total)[LANES - width :, :])
        high, low = two(jnp.concatenate(halves, 1))
        moved = nn(jnp.concatenate([high, low], 0), perm[...])
        moved = moved[:width] + moved[width:]
        for g, out_ref in enumerate(out_refs):
            out_ref[:, layout.lanes(index)] = moved[:, g * layout.per : (g + 1) * layout.per]
        return carry

    lax.fori_loop(0, blocks, block, 0)


def final_kernel(blocks, where_ref, pos_ref, *refs):
    back_refs, (weights_ref, out_ref, perm, vals) = refs[:-4], refs[-4:]
    chunks = pos_ref.shape[0]
    rows = chunks * LANES
    width, split = back_refs[0].shape
    cols = jnp.concatenate([column(pos_ref[c : c + 1, :]) for c in range(chunks)], 0).astype(jnp.int32)
    for c in range(chunks):
        perm[:, c * LANES : (c + 1) * LANES] = onehot(iota((rows, LANES), 1) + c * LANES == cols)
    for g, back_ref in enumerate(back_refs):
        high, low = two(back_ref[...])
        columns, at = 0, slice(0, rows)
        if blocks:
            columns = (where_ref[1] ^ (g % blocks)) * width
            at = aligned((where_ref[0] ^ where_ref[2] ^ (g // blocks)) * split, split, split)
        vals[aligned(columns, width, width), at] = high
        vals[aligned(columns + LANES, width, width), at] = low
    step = 256
    for s in range(rows // step):
        here = slice(s * step, (s + 1) * step)
        moved = nt(perm[here, :], vals[...])
        out_ref[here, :] = ridge * weights_ref[here, :] + moved[:, :LANES] + moved[:, LANES:]


def upper_levels(pack, skeleton_upper, my_leaf, trees, blocks, width):
    devices = trees * blocks
    level = blocks.bit_length() - 1
    offset = sum(devices >> step for step in range(1, level + 1))
    lanes = jnp.arange(LANES)[None]
    is_point, is_norm = lanes < DIM, (lanes >= DIM) & (lanes < DIM + 3)
    is_coef = lanes >= LANES - width
    packs, own, stride = [], pack, 1
    while stride < trees:
        other = lax.ppermute(own, "leaf", [(i, i ^ stride) for i in range(trees)])
        packs.append(other)
        stride *= 2
        if stride < trees:
            second = (my_leaf // (stride // 2)) % 2 == 1
            pair = jnp.where(second, jnp.concatenate([other, own], 0), jnp.concatenate([own, other], 0))
            chosen = pair[skeleton_upper[offset + my_leaf // stride]]
            level += 1
            offset += devices >> level
            norms = jnp.sum(jnp.where(is_norm, pair, 0.0), axis=1)
            chosen_norms = jnp.sum(jnp.where(is_norm, chosen, 0.0), axis=1)
            inner = jnp.dot(
                jnp.where(is_point, chosen, 0.0), jnp.where(is_point, pair, 0.0).T, precision=highest
            )
            tile = jnp.exp2(inner + norms[None] + chosen_norms[:, None])
            own = jnp.where(is_coef, jnp.dot(tile, pair, precision=highest), chosen)
    return jnp.stack(packs)


def body(points, weights, tree_slot, near_count, near_list, skeleton_base, skeleton_upper, far_use):
    blocks, trees, reps = lax.axis_size("sub"), lax.axis_size("leaf"), lax.axis_size("rep")
    devices = blocks * trees
    rows, columns = weights.shape
    low_levels = blocks.bit_length() - 1
    ups = trees.bit_length() - 1
    width = columns // blocks
    part = rows // trees
    per = part // blocks
    total = blocks * rows
    leaves = total // LEAF
    my_leaf = lax.axis_index("leaf")
    fine = trees == 2 and reps == 2 and per % LANES == 0
    layout = Layout(blocks, trees, rows, fine)
    split = part if fine else rows
    where = jnp.stack([my_leaf, lax.axis_index("sub"), lax.axis_index("rep")]).astype(jnp.int32)
    message = shaped((width, part), f32) if fine else shaped((columns, rows), f32)
    arrive = shaped((width, part), f32) if fine else shaped((width, total), f32)

    place, pos, *light = pl.pallas_call(
        functools.partial(sort_kernel, blocks if fine else 0),
        out_shape=(shaped((PLACE_ROWS, split), f32), shaped((rows // LANES, LANES), f32)) + (message,) * layout.count,
        in_specs=[spec(SMEM)] + [spec()] * 5,
        out_specs=(spec(),) * (2 + layout.count),
        scratch_shapes=[
            vm((rows, rows), bf16),
            vm((272, rows), bf16),
            vm((rows // split, PLACE_ROWS, split), f32),
            vm((rows // split, columns, split), f32),
        ],
        compiler_params=params(),
        name="sort_rows",
    )(where, tree_slot.reshape(rows // LANES, LANES), points.T, weights, skeleton_base, far_use)

    axes = ("leaf", "sub", "rep")

    def swap(value, step, other=0):
        pairs = []
        for leaf in range(trees):
            for sub in range(blocks):
                for core in range(reps):
                    to = ((leaf ^ core ^ other) * blocks + (sub ^ step)) * reps + core
                    pairs.append(((leaf * blocks + sub) * reps + core, to))
        return lax.ppermute(value, axes, pairs)

    def swap_all(values):
        return [swap(value, g % blocks, g // blocks) for g, value in enumerate(values)]

    if fine:
        place = {0: swap(place, 0)}
        stride = blocks // 2
        while stride:
            for step in sorted(place):
                place[step | stride] = lax.ppermute(place[step], "sub", [(i, i ^ stride) for i in range(blocks)])
            stride //= 2
        place = [place[step] for step in range(blocks)]
        place = place + [lax.ppermute(one, "rep", [(0, 1), (1, 0)]) for one in place]
        light = swap_all(light)
        small = jnp.zeros((1, 8, SK), f32)
    else:
        info = jnp.pad(far_use.astype(f32), ((FLAGS, 5 - far_use.shape[0]), (0, SK - far_use.shape[1])))
        small = lax.all_gather(info.at[BASE].set(skeleton_base[0].astype(f32)), "sub", axis=0, tiled=False)
        place = place.reshape(PLACE_ROWS, trees, part).transpose(1, 0, 2)
        place = lax.all_to_all(place, "leaf", split_axis=0, concat_axis=0, tiled=True)
        place = lax.all_gather(place, "sub", axis=0, tiled=False)
        place = place.transpose(1, 0, 2, 3).reshape(devices, PLACE_ROWS, blocks, per)
        place = [place.transpose(1, 2, 0, 3).reshape(PLACE_ROWS, total)]
        light = light[0].reshape(columns, trees, part).transpose(1, 0, 2).reshape(devices, width, part)
        light = lax.all_to_all(light, ("leaf", "sub"), split_axis=0, concat_axis=0, tiled=True)
        light = light.reshape(devices, width, blocks, per)
        light = [light.transpose(1, 2, 0, 3).reshape(width, total)]

    nodes = 2 * blocks - 1
    feat_a, feat_bt, sk, base, upper_tiles, top, slots, info = pl.pallas_call(
        functools.partial(points_kernel, layout, trees),
        out_shape=(
            shaped((total, FEAT), bf16),
            shaped((FEAT, total), bf16),
            shaped((FEAT, nodes * SK), bf16),
            shaped((blocks, SK, rows), bf16),
            shaped((blocks - 1, SK, 2 * SK), f32),
            shaped((SK, LANES), f32),
            shaped((blocks, rows), f32),
            shaped((blocks, 8, SK), f32),
        ),
        in_specs=[spec(SMEM)] + [spec()] * (2 + layout.count),
        out_specs=(spec(),) * 8,
        scratch_shapes=[vm((rows, rows), bf16), vm((2 * FEAT, rows), bf16), vm((nodes * SK, FEAT), bf16)],
        compiler_params=params(),
        name="tree_points",
    )(where, skeleton_upper, small, *place)

    tree_light, coefs, pack = pl.pallas_call(
        functools.partial(weights_kernel, layout),
        out_shape=(
            shaped((total, LANES), bf16),
            shaped((nodes * SK, FEAT), bf16),
            shaped((SK, LANES), f32),
        ),
        in_specs=[spec()] * (4 + layout.count),
        out_specs=(spec(),) * 3,
        scratch_shapes=[vm((rows, rows), bf16), vm((LANES, rows), bf16)],
        compiler_params=params(),
        name="tree_weights",
    )(base, upper_tiles, top, slots, *light)

    packs = upper_levels(pack, skeleton_upper, my_leaf, trees, blocks, width)

    near = pl.pallas_call(
        near_kernel,
        out_shape=shaped((total, LANES), f32),
        in_specs=[spec(SMEM)] * 2 + [spec()] * 3,
        out_specs=spec(),
        scratch_shapes=[
            pltpu.SMEM((leaves,), jnp.int32),
            pltpu.SMEM((3, leaves * leaves + 1), jnp.int32),
            vm((LEAF, LEAF // 2), f32),
        ],
        compiler_params=params(),
        name="near",
    )(near_count, near_list[0], feat_a, feat_bt, tree_light)

    levels = low_levels + ups
    back = pl.pallas_call(
        functools.partial(far_kernel, layout, low_levels),
        out_shape=(arrive,) * layout.count,
        in_specs=[spec()] * 7,
        out_specs=(spec(),) * layout.count,
        scratch_shapes=[
            vm((rows, rows), bf16),
            vm((FEAT, levels * SK), bf16),
            vm((levels * SK, FEAT), bf16),
            vm((levels * SK, FEAT), bf16),
        ],
        compiler_params=params(),
        name="far",
    )(packs, slots, info, feat_a, sk, coefs, near)

    if fine:
        back = swap_all(back)
    else:
        back = back[0].reshape(width, blocks, devices, per).transpose(2, 0, 1, 3).reshape(devices, width, part)
        back = lax.all_to_all(back, ("leaf", "sub"), split_axis=0, concat_axis=0, tiled=True)
        back = [back.reshape(trees, columns, part).transpose(1, 0, 2).reshape(columns, rows)]

    return pl.pallas_call(
        functools.partial(final_kernel, blocks if fine else 0),
        out_shape=shaped((rows, columns), f32),
        in_specs=[spec(SMEM)] + [spec()] * (2 + layout.count),
        out_specs=spec(),
        scratch_shapes=[vm((rows, rows), bf16), vm((2 * LANES, rows), bf16)],
        compiler_params=params(),
        name="to_input_order",
    )(where, pos, *back, weights)


def solution(mesh):
    in_specs = (
        P(("groups", "leaf", "sub"), None),
        P(("groups", "leaf", "sub"), "rep"),
        P(("groups", "leaf", "sub")),
        P(("groups", "leaf"), None),
        P(("groups", "leaf"), None, None),
        P(("groups", "leaf", "sub"), None),
        P("groups", None),
        P(("groups", "leaf", "sub"), None),
    )
    out_specs = P(("groups", "leaf", "sub"), "rep")
    return jax.shard_map(body, mesh=mesh, in_specs=in_specs, out_specs=out_specs, check_vma=False)
```

time: 134 us -> 120 us (0.90)
  blocking collectives: 50.3 us -> 0 us
  starting transfers between devices: 18.3 us -> 47.8 us
  waiting for transfers between devices: 0.01 us -> 14 us
  local copies, waits for them, and re-layouts: 15.2 us -> 2.46 us
  Pallas kernels: 49.6 us -> 55.6 us
    ppermute x1 -> x24, starting transfers between devices: 2.02 us -> 45.8 us  [the longest x17 33.4 us: swap(): return lax.ppermute(value, axes, pairs)]
    all_gather x2 -> x0, blocking collectives: 35.7 us -> none  [body(): lax.all_gather(one, ('sub', 'rep'), axis=0, tiled=False)]
    all_to_all x1 -> x0, blocking collectives: 14.7 us -> none  [give_back(): lax.all_to_all(out, ('leaf', 'sub'), split_axis=0, concat_axis=0, tiled=T...]
    all_to_all x2 -> x0, starting transfers between devices: 14.6 us -> none  [the longest x1 7.32 us: give_back(): lax.all_to_all(out, ('leaf', 'sub'), split_axis=0, concat_axis=0, tiled=T...]
    ppermute x1 -> x24, waiting for transfers between devices: 0.01 us -> 14 us  [the longest x17 10.7 us: swap(): return lax.ppermute(value, axes, pairs)]
    unnamed x46 -> x50, local copies, waits for them, and re-layouts: 15.2 us -> 1.86 us
    pallas_call x7 -> x6, Pallas kernels: 49.6 us -> 55.6 us  [the longest x1 20.4 us: body(): pl.pallas_call(near_kernel, out_shape=shaped((total, LANES), f32), in_spe...]
  transfers between devices with their start and end apart: 4 -> 25, of which waited for: 0 -> 5; matrix products, arithmetic and copies ran while one was open for 0% -> 0% of each run, Pallas kernels for 24% -> 26%
where the time goes in v3:
time: 120 us; the launch traced here: 121 us
  Pallas kernels  55.6 us (46%)
  starting transfers between devices  47.8 us (40%)
  waiting for transfers between devices  14 us (12%)
  local copies, waits for them, and re-layouts  2.46 us (2%)
    ppermute x17, starting transfers between devices, swap(): return lax.ppermute(value, axes, pairs)  33.4 us
    pallas_call x1, Pallas kernels, body(): pl.pallas_call(near_kernel, out_shape=shaped((total, LANES), f32), in_spe...  20.4 us
    pallas_call x1, Pallas kernels, body(): pl.pallas_call(functools.partial(far_kernel, layout, low_levels), out_sha...  10.8 us
    ppermute x17, waiting for transfers between devices, swap(): return lax.ppermute(value, axes, pairs)  10.7 us
    pallas_call x1, Pallas kernels, body(): pl.pallas_call(functools.partial(points_kernel, layout, trees), out_shape...  10.4 us
    pallas_call x1, Pallas kernels, body(): pl.pallas_call(functools.partial(weights_kernel, layout), out_shape=(shap...  7.05 us
    ppermute x3, starting transfers between devices, body(): lax.ppermute(place[step], 'sub', [(i, i ^ stride) for i in range(blocks)])  6.51 us
    ppermute x4, starting transfers between devices, body(): lax.ppermute(one, 'rep', [(0, 1), (1, 0)])  5.82 us
  transfers between devices with their start and end apart: 25, of which 5 were waited for; matrix products, arithmetic and copies ran while one was open for 0% of the time, Pallas kernels for 26%

profile of v3, /device:TPU:0, one launch (start us, length us, event | category | flops | bytes accessed | tf_op | source)
XLA Modules:
  0.0 120.7 jit_solution(6070407905025378316)
XLA Ops:
  0.6 3.7 %sort_rows.1 = (f32[72,512]{1,0:T(8,128)}, f32[8,128]{1,0:T(8,128)}, f32[32,512]{1,0:T(8,128)}, f32[32,512]{1,0:T(8,128)}, f32[32,512]{1,0:T(8,128)}, /*index=5*...) custom-call(s32[3]{0:T(128)} %pad_add_fusion.where_ref, ...), custom_call_target="tpu_custom_call" | custom-call | tf_op jit(solution)/shard_map/sort_rows/pallas_call | solution.py:441
  4.3 1.6 %collective-permute-start = (f32[72,512]{1,0:T(8,128)}, f32[72,512]{1,0:T(8,128)S(1)}, u32[]{:S(2)}, u32[]{:S(2)}) collective-permute-start(f32[72,512]{1,0:T(8,128)} %get-tuple-element.35), channel_id=1, source_target_pairs={{0,0},{1,9},{2,2},{3,11},{4,4},{5,13},{6,6},{7,15},{8,8},{9,1},{10... | collective-permute-start | bytes 442376 | tf_op jit(solution)/shard_map/ppermute | solution.py:465
  5.9 4.0 %collective-permute-start.2 = (f32[72,512]{1,0:T(8,128)S(1)}, f32[72,512]{1,0:T(8,128)S(1)}, u32[]{:S(2)}, u32[]{:S(2)}) collective-permute-start(f32[72,512]{1,0:T(8,128)S(1)} %collective-permute-done.refs_0_), channel_id=1, source_target_pairs={{0,4},{2,6},{4,0},{6,2},{1,5},{3,7},{5,1},{7,3},{8,12},{10,14},{12... | collective-permute-start | bytes 442376 | tf_op jit(solution)/shard_map/ppermute | solution.py:475
  9.9 1.6 %collective-permute-start.1 = (f32[72,512]{1,0:T(8,128)S(1)}, f32[72,512]{1,0:T(8,128)S(1)}, u32[]{:S(2)}, u32[]{:S(2)}) collective-permute-start(f32[72,512]{1,0:T(8,128)S(1)} %collective-permute-done.refs_0_), channel_id=1, source_target_pairs={{0,2},{2,0},{4,6},{6,4},{1,3},{3,1},{5,7},{7,5},{8,10},{10,8},{12,... | collective-permute-start | bytes 442376 | tf_op jit(solution)/shard_map/ppermute | solution.py:475
  11.5 3.2 %collective-permute-done.2.refs_2_ = f32[72,512]{1,0:T(8,128)S(1)} collective-permute-done((f32[72,512]{1,0:T(8,128)S(1)}, f32[72,512]{1,0:T(8,128)S(1)}, u32[]{:S(2)}, u32[]{:S(2)}) %collective-permute-start.2) | collective-permute-done | bytes 147488 | tf_op jit(solution)/shard_map/ppermute | solution.py:475
  15.6 1.5 %collective-permute-start.8 = (f32[32,512]{1,0:T(8,128)}, f32[32,512]{1,0:T(8,128)S(1)}, u32[]{:S(2)}, u32[]{:S(2)}) collective-permute-start(f32[32,512]{1,0:T(8,128)} %get-tuple-element.40), channel_id=1, source_target_pairs={{0,0},{1,9},{2,2},{3,11},{4,4},{5,13},{6,6},{7,15},{8,8},{9,1},{10... | collective-permute-start | bytes 196616 | tf_op jit(solution)/shard_map/ppermute | solution.py:465
  17.1 5.2 %collective-permute-start.4 = (f32[72,512]{1,0:T(8,128)S(1)}, f32[72,512]{1,0:T(8,128)S(1)}, u32[]{:S(2)}, u32[]{:S(2)}) collective-permute-start(f32[72,512]{1,0:T(8,128)S(1)} %collective-permute-done.refs_0_), channel_id=1, source_target_pairs={{0,1},{1,0},{2,3},{3,2},{4,5},{5,4},{6,7},{7,6},{8,9},{9,8},{10,11... | collective-permute-start | bytes 442376 | tf_op jit(solution)/shard_map/ppermute | solution.py:478
  24.1 3.3 %collective-permute-done.9.refs_1_ = f32[32,512]{1,0:T(8,128)S(1)} collective-permute-done((f32[32,512]{1,0:T(8,128)}, f32[32,512]{1,0:T(8,128)S(1)}, u32[]{:S(2)}, u32[]{:S(2)}) %collective-permute-start.9) | collective-permute-done | bytes 65568 | tf_op jit(solution)/shard_map/ppermute | solution.py:465
  27.4 3.1 %collective-permute-start.10 = (f32[32,512]{1,0:T(8,128)}, f32[32,512]{1,0:T(8,128)S(1)}, u32[]{:S(2)}, u32[]{:S(2)}) collective-permute-start(f32[32,512]{1,0:T(8,128)} %get-tuple-element.42), channel_id=1, source_target_pairs={{0,4},{1,13},{2,6},{3,15},{4,0},{5,9},{6,2},{7,11},{8,12},{9,5},{1... | collective-permute-start | bytes 196616 | tf_op jit(solution)/shard_map/ppermute | solution.py:465
  30.5 4.0 %collective-permute-done.10.refs_2_ = f32[32,512]{1,0:T(8,128)S(1)} collective-permute-done((f32[32,512]{1,0:T(8,128)}, f32[32,512]{1,0:T(8,128)S(1)}, u32[]{:S(2)}, u32[]{:S(2)}) %collective-permute-start.10) | collective-permute-done | bytes 65568 | tf_op jit(solution)/shard_map/ppermute | solution.py:465
  35.8 5.5 %collective-permute-start.12 = (f32[32,512]{1,0:T(8,128)}, f32[32,512]{1,0:T(8,128)S(1)}, u32[]{:S(2)}, u32[]{:S(2)}) collective-permute-start(f32[32,512]{1,0:T(8,128)} %get-tuple-element.44), channel_id=1, source_target_pairs={{0,8},{1,1},{2,10},{3,3},{4,12},{5,5},{6,14},{7,7},{8,0},{9,9},{10... | collective-permute-start | bytes 196616 | tf_op jit(solution)/shard_map/ppermute | solution.py:465
  42.9 3.2 %collective-permute-start.15 = (f32[32,512]{1,0:T(8,128)}, f32[32,512]{1,0:T(8,128)S(1)}, u32[]{:S(2)}, u32[]{:S(2)}) collective-permute-start(f32[32,512]{1,0:T(8,128)} %get-tuple-element.47), channel_id=1, source_target_pairs={{0,14},{1,7},{2,12},{3,5},{4,10},{5,3},{6,8},{7,1},{8,6},{9,15},{1... | collective-permute-start | bytes 196616 | tf_op jit(solution)/shard_map/ppermute | solution.py:465
  46.8 10.4 %tree_points.1 = (bf16[4096,256]{1,0:T(8,128)(2,1)}, bf16[256,4096]{1,0:T(8,128)(2,1)}, bf16[256,896]{1,0:T(8,128)(2,1)}, bf16[4,128,1024]{2,1,0:T(8,128)(2,1)},...) custom-call(s32[3]{0:T(128)} %pad_add_fusion.where_ref, ...), custom_call_target="tpu_custom_call" | custom-call | tf_op jit(solution)/shard_map/tree_points/pallas_call | solution.py:495
  58.0 7.1 %tree_weights.1 = (bf16[4096,128]{1,0:T(8,128)(2,1)}, bf16[896,256]{1,0:T(8,128)(2,1)}, f32[128,128]{1,0:T(8,128)}) custom-call(bf16[4,128,1024]{2,1,0:T(8,128)(2,1)} %get-tuple-element.36.base_ref, f32[3,128,256]{2,1,0:T(8,128)} %get-tuple-element.37.upper_tiles_ref, f32[128,128]{1,0:T(8,128)} %get-tuple-element.38.top_ref, ...), custom_call_target="tpu_custom_call" | custom-call | tf_op jit(solution)/shard_map/tree_weights/pallas_call | solution.py:514
  65.0 2.0 %collective-permute-start.16 = (f32[128,128]{1,0:T(8,128)}, f32[128,128]{1,0:T(8,128)S(1)}, u32[]{:S(2)}, u32[]{:S(2)}) collective-permute-start(f32[128,128]{1,0:T(8,128)} %get-tuple-element.48), channel_id=1, source_target_pairs={{0,8},{8,0},{1,9},{9,1},{2,10},{10,2},{3,11},{11,3},{4,12},{12,4},... | collective-permute-start | bytes 196616 | tf_op jit(solution)/shard_map/ppermute | solution.py:403
  67.1 20.4 %near.1.near_ref = f32[4096,128]{1,0:T(8,128)} custom-call(s32[1,8]{1,0:T(1,128)} %count_ref.1, s32[8,16]{1,0:T(8,128)} %bitcast.9, bf16[4096,256]{1,0:T(8,128)(2,1)} %get-tuple-element.50.a_ref, bf16[256,4096]{1,0:T(8,128)(2,1)} %get-tuple-element.53.bt_ref, bf16[4096,128]{1,0:T(8,128)(2,1)} %get-tuple-element.54.w_ref), custom_call_target="tpu_custom_call" | custom-call | tf_op jit(solution)/shard_map/near/pallas_call | solution.py:530
  88.1 10.8 %far.1 = (f32[32,512]{1,0:T(8,128)}, f32[32,512]{1,0:T(8,128)}, f32[32,512]{1,0:T(8,128)}, f32[32,512]{1,0:T(8,128)}, f32[32,512]{1,0:T(8,128)}, /*index=5*/f32[...) custom-call(f32[1,128,128]{2,1,0:T(8,128)} %bitcast.8, f32[4,1024]{1,0:T(4,128)} %get-tuple-element.39.slot_ref, ...), custom_call_target="tpu_custom_call" | custom-call | tf_op jit(solution)/shard_map/far/pallas_call | solution.py:545
  98.9 1.5 %collective-permute-start.17 = (f32[32,512]{1,0:T(8,128)}, f32[32,512]{1,0:T(8,128)S(1)}, u32[]{:S(2)}, u32[]{:S(2)}) collective-permute-start(f32[32,512]{1,0:T(8,128)} %get-tuple-element.55), channel_id=1, source_target_pairs={{0,0},{1,9},{2,2},{3,11},{4,4},{5,13},{6,6},{7,15},{8,8},{9,1},{10... | collective-permute-start | bytes 196616 | tf_op jit(solution)/shard_map/ppermute | solution.py:465
  100.9 3.8 %collective-permute-start.20 = (f32[32,512]{1,0:T(8,128)}, f32[32,512]{1,0:T(8,128)S(1)}, u32[]{:S(2)}, u32[]{:S(2)}) collective-permute-start(f32[32,512]{1,0:T(8,128)} %get-tuple-element.58), channel_id=1, source_target_pairs={{0,6},{1,15},{2,4},{3,13},{4,2},{5,11},{6,0},{7,9},{8,14},{9,7},{1... | collective-permute-start | bytes 196616 | tf_op jit(solution)/shard_map/ppermute | solution.py:465
  104.7 2.4 %collective-permute-start.21 = (f32[32,512]{1,0:T(8,128)}, f32[32,512]{1,0:T(8,128)S(1)}, u32[]{:S(2)}, u32[]{:S(2)}) collective-permute-start(f32[32,512]{1,0:T(8,128)} %get-tuple-element.59), channel_id=1, source_target_pairs={{0,8},{1,1},{2,10},{3,3},{4,12},{5,5},{6,14},{7,7},{8,0},{9,9},{10... | collective-permute-start | bytes 196616 | tf_op jit(solution)/shard_map/ppermute | solution.py:465
  107.3 2.4 %collective-permute-start.23 = (f32[32,512]{1,0:T(8,128)}, f32[32,512]{1,0:T(8,128)S(1)}, u32[]{:S(2)}, u32[]{:S(2)}) collective-permute-start(f32[32,512]{1,0:T(8,128)} %get-tuple-element.61), channel_id=1, source_target_pairs={{0,12},{1,5},{2,14},{3,7},{4,8},{5,1},{6,10},{7,3},{8,4},{9,13},{1... | collective-permute-start | bytes 196616 | tf_op jit(solution)/shard_map/ppermute | solution.py:465
  109.7 3.8 %collective-permute-start.24 = (f32[32,512]{1,0:T(8,128)}, f32[32,512]{1,0:T(8,128)S(1)}, u32[]{:S(2)}, u32[]{:S(2)}) collective-permute-start(f32[32,512]{1,0:T(8,128)} %get-tuple-element.62), channel_id=1, source_target_pairs={{0,14},{1,7},{2,12},{3,5},{4,10},{5,3},{6,8},{7,1},{8,6},{9,15},{1... | collective-permute-start | bytes 196616 | tf_op jit(solution)/shard_map/ppermute | solution.py:465
  113.6 3.2 %collective-permute-done.24.refs_7_ = f32[32,512]{1,0:T(8,128)S(1)} collective-permute-done((f32[32,512]{1,0:T(8,128)}, f32[32,512]{1,0:T(8,128)S(1)}, u32[]{:S(2)}, u32[]{:S(2)}) %collective-permute-start.24) | collective-permute-done | bytes 65568 | tf_op jit(solution)/shard_map/ppermute | solution.py:465
  117.5 3.2 %to_input_order.1 = f32[1024,128]{1,0:T(8,128)} custom-call(s32[3]{0:T(128)} %pad_add_fusion.where_ref, f32[8,128]{1,0:T(8,128)} %get-tuple-element.34.pos_ref, f32[32,512]{1,0:T(8,128)} %copy-done.14, f32[32,512]{1,0:T(8,128)} %copy-done.16, f32[32,512]{1,0:T(8,128)} %copy-done.17, f32[32,512]{1,0:T(8,128)} %copy-done.19, f32[32,512]{1,0:T(8,128)} %copy-done.20, ...), custom_call_target="tpu_custom_call" | custom-call | tf_op jit(solution)/shard_map/to_input_order/pallas_call | solution.py:567
  (84 shorter events, 9.3 us)
Async XLA Ops:
  5.9 8.8 %collective-permute-start.2 = (f32[72,512]{1,0:T(8,128)S(1)}, f32[72,512]{1,0:T(8,128)S(1)}, u32[]{:S(2)}, u32[]{:S(2)}) collective-permute-start(f32[72,512]{1,0:T(8,128)S(1)} %collective-permute-done.refs_0_), channel_id=1, source_target_pairs={{0,4},{2,6},{4,0},{6,2},{1,5},{3,7},{5,1},{7,3},{8,12},{10,14},{12... | collective-permute-start | bytes 442376 | tf_op jit(solution)/shard_map/ppermute | solution.py:475
  9.9 12.4 %collective-permute-start.1 = (f32[72,512]{1,0:T(8,128)S(1)}, f32[72,512]{1,0:T(8,128)S(1)}, u32[]{:S(2)}, u32[]{:S(2)}) collective-permute-start(f32[72,512]{1,0:T(8,128)S(1)} %collective-permute-done.refs_0_), channel_id=1, source_target_pairs={{0,2},{2,0},{4,6},{6,4},{1,3},{3,1},{5,7},{7,5},{8,10},{10,8},{12,... | collective-permute-start | bytes 442376 | tf_op jit(solution)/shard_map/ppermute | solution.py:475
  14.7 8.1 %collective-permute-start.3 = (f32[72,512]{1,0:T(8,128)S(1)}, f32[72,512]{1,0:T(8,128)S(1)}, u32[]{:S(2)}, u32[]{:S(2)}) collective-permute-start(f32[72,512]{1,0:T(8,128)S(1)} %collective-permute-done.2.refs_2_), channel_id=1, source_target_pairs={{0,2},{2,0},{4,6},{6,4},{1,3},{3,1},{5,7},{7,5},{8,10},{10,8},{12,... | collective-permute-start | bytes 442376 | tf_op jit(solution)/shard_map/ppermute | solution.py:475
  15.6 7.3 %collective-permute-start.8 = (f32[32,512]{1,0:T(8,128)}, f32[32,512]{1,0:T(8,128)S(1)}, u32[]{:S(2)}, u32[]{:S(2)}) collective-permute-start(f32[32,512]{1,0:T(8,128)} %get-tuple-element.40), channel_id=1, source_target_pairs={{0,0},{1,9},{2,2},{3,11},{4,4},{5,13},{6,6},{7,15},{8,8},{9,1},{10... | collective-permute-start | bytes 196616 | tf_op jit(solution)/shard_map/ppermute | solution.py:465
  17.1 18.7 %collective-permute-start.4 = (f32[72,512]{1,0:T(8,128)S(1)}, f32[72,512]{1,0:T(8,128)S(1)}, u32[]{:S(2)}, u32[]{:S(2)}) collective-permute-start(f32[72,512]{1,0:T(8,128)S(1)} %collective-permute-done.refs_0_), channel_id=1, source_target_pairs={{0,1},{1,0},{2,3},{3,2},{4,5},{5,4},{6,7},{7,6},{8,9},{9,8},{10,11... | collective-permute-start | bytes 442376 | tf_op jit(solution)/shard_map/ppermute | solution.py:478
  22.3 19.0 %collective-permute-start.5 = (f32[72,512]{1,0:T(8,128)S(1)}, f32[72,512]{1,0:T(8,128)S(1)}, u32[]{:S(2)}, u32[]{:S(2)}) collective-permute-start(f32[72,512]{1,0:T(8,128)S(1)} %collective-permute-done.1.refs_1_), channel_id=1, source_target_pairs={{0,1},{1,0},{2,3},{3,2},{4,5},{5,4},{6,7},{7,6},{8,9},{9,8},{10,11... | collective-permute-start | bytes 442376 | tf_op jit(solution)/shard_map/ppermute | solution.py:478
  22.4 19.0 %collective-permute-start.6 = (f32[72,512]{1,0:T(8,128)S(1)}, f32[72,512]{1,0:T(8,128)S(1)}, u32[]{:S(2)}, u32[]{:S(2)}) collective-permute-start(f32[72,512]{1,0:T(8,128)S(1)} %collective-permute-done.2.refs_2_), channel_id=1, source_target_pairs={{0,1},{1,0},{2,3},{3,2},{4,5},{5,4},{6,7},{7,6},{8,9},{9,8},{10,11... | collective-permute-start | bytes 442376 | tf_op jit(solution)/shard_map/ppermute | solution.py:478
  22.9 20.1 %collective-permute-start.7 = (f32[72,512]{1,0:T(8,128)S(1)}, f32[72,512]{1,0:T(8,128)S(1)}, u32[]{:S(2)}, u32[]{:S(2)}) collective-permute-start(f32[72,512]{1,0:T(8,128)S(1)} %collective-permute-done.3.refs_3_), channel_id=1, source_target_pairs={{0,1},{1,0},{2,3},{3,2},{4,5},{5,4},{6,7},{7,6},{8,9},{9,8},{10,11... | collective-permute-start | bytes 442376 | tf_op jit(solution)/shard_map/ppermute | solution.py:478
  23.0 4.5 %collective-permute-start.9 = (f32[32,512]{1,0:T(8,128)}, f32[32,512]{1,0:T(8,128)S(1)}, u32[]{:S(2)}, u32[]{:S(2)}) collective-permute-start(f32[32,512]{1,0:T(8,128)} %get-tuple-element.41), channel_id=1, source_target_pairs={{0,2},{1,11},{2,0},{3,9},{4,6},{5,15},{6,4},{7,13},{8,10},{9,3},{1... | collective-permute-start | bytes 196616 | tf_op jit(solution)/shard_map/ppermute | solution.py:465
  27.4 7.1 %collective-permute-start.10 = (f32[32,512]{1,0:T(8,128)}, f32[32,512]{1,0:T(8,128)S(1)}, u32[]{:S(2)}, u32[]{:S(2)}) collective-permute-start(f32[32,512]{1,0:T(8,128)} %get-tuple-element.42), channel_id=1, source_target_pairs={{0,4},{1,13},{2,6},{3,15},{4,0},{5,9},{6,2},{7,11},{8,12},{9,5},{1... | collective-permute-start | bytes 196616 | tf_op jit(solution)/shard_map/ppermute | solution.py:465
  34.6 22.7 %collective-permute-start.11 = (f32[32,512]{1,0:T(8,128)}, f32[32,512]{1,0:T(8,128)S(1)}, u32[]{:S(2)}, u32[]{:S(2)}) collective-permute-start(f32[32,512]{1,0:T(8,128)} %get-tuple-element.43), channel_id=1, source_target_pairs={{0,6},{1,15},{2,4},{3,13},{4,2},{5,11},{6,0},{7,9},{8,14},{9,7},{1... | collective-permute-start | bytes 196616 | tf_op jit(solution)/shard_map/ppermute | solution.py:465
  35.8 21.5 %collective-permute-start.12 = (f32[32,512]{1,0:T(8,128)}, f32[32,512]{1,0:T(8,128)S(1)}, u32[]{:S(2)}, u32[]{:S(2)}) collective-permute-start(f32[32,512]{1,0:T(8,128)} %get-tuple-element.44), channel_id=1, source_target_pairs={{0,8},{1,1},{2,10},{3,3},{4,12},{5,5},{6,14},{7,7},{8,0},{9,9},{10... | collective-permute-start | bytes 196616 | tf_op jit(solution)/shard_map/ppermute | solution.py:465
  41.4 15.9 %collective-permute-start.13 = (f32[32,512]{1,0:T(8,128)}, f32[32,512]{1,0:T(8,128)S(1)}, u32[]{:S(2)}, u32[]{:S(2)}) collective-permute-start(f32[32,512]{1,0:T(8,128)} %get-tuple-element.45), channel_id=1, source_target_pairs={{0,10},{1,3},{2,8},{3,1},{4,14},{5,7},{6,12},{7,5},{8,2},{9,11},{1... | collective-permute-start | bytes 196616 | tf_op jit(solution)/shard_map/ppermute | solution.py:465
  41.5 15.9 %collective-permute-start.14 = (f32[32,512]{1,0:T(8,128)}, f32[32,512]{1,0:T(8,128)S(1)}, u32[]{:S(2)}, u32[]{:S(2)}) collective-permute-start(f32[32,512]{1,0:T(8,128)} %get-tuple-element.46), channel_id=1, source_target_pairs={{0,12},{1,5},{2,14},{3,7},{4,8},{5,1},{6,10},{7,3},{8,4},{9,13},{1... | collective-permute-start | bytes 196616 | tf_op jit(solution)/shard_map/ppermute | solution.py:465
  42.9 14.4 %collective-permute-start.15 = (f32[32,512]{1,0:T(8,128)}, f32[32,512]{1,0:T(8,128)S(1)}, u32[]{:S(2)}, u32[]{:S(2)}) collective-permute-start(f32[32,512]{1,0:T(8,128)} %get-tuple-element.47), channel_id=1, source_target_pairs={{0,14},{1,7},{2,12},{3,5},{4,10},{5,3},{6,8},{7,1},{8,6},{9,15},{1... | collective-permute-start | bytes 196616 | tf_op jit(solution)/shard_map/ppermute | solution.py:465
  65.0 22.4 %collective-permute-start.16 = (f32[128,128]{1,0:T(8,128)}, f32[128,128]{1,0:T(8,128)S(1)}, u32[]{:S(2)}, u32[]{:S(2)}) collective-permute-start(f32[128,128]{1,0:T(8,128)} %get-tuple-element.48), channel_id=1, source_target_pairs={{0,8},{8,0},{1,9},{9,1},{2,10},{10,2},{3,11},{11,3},{4,12},{12,4},... | collective-permute-start | bytes 196616 | tf_op jit(solution)/shard_map/ppermute | solution.py:403
  98.9 8.3 %collective-permute-start.17 = (f32[32,512]{1,0:T(8,128)}, f32[32,512]{1,0:T(8,128)S(1)}, u32[]{:S(2)}, u32[]{:S(2)}) collective-permute-start(f32[32,512]{1,0:T(8,128)} %get-tuple-element.55), channel_id=1, source_target_pairs={{0,0},{1,9},{2,2},{3,11},{4,4},{5,13},{6,6},{7,15},{8,8},{9,1},{10... | collective-permute-start | bytes 196616 | tf_op jit(solution)/shard_map/ppermute | solution.py:465
  100.4 6.9 %collective-permute-start.18 = (f32[32,512]{1,0:T(8,128)}, f32[32,512]{1,0:T(8,128)S(1)}, u32[]{:S(2)}, u32[]{:S(2)}) collective-permute-start(f32[32,512]{1,0:T(8,128)} %get-tuple-element.56), channel_id=1, source_target_pairs={{0,2},{1,11},{2,0},{3,9},{4,6},{5,15},{6,4},{7,13},{8,10},{9,3},{1... | collective-permute-start | bytes 196616 | tf_op jit(solution)/shard_map/ppermute | solution.py:465
  100.4 9.3 %collective-permute-start.19 = (f32[32,512]{1,0:T(8,128)}, f32[32,512]{1,0:T(8,128)S(1)}, u32[]{:S(2)}, u32[]{:S(2)}) collective-permute-start(f32[32,512]{1,0:T(8,128)} %get-tuple-element.57), channel_id=1, source_target_pairs={{0,4},{1,13},{2,6},{3,15},{4,0},{5,9},{6,2},{7,11},{8,12},{9,5},{1... | collective-permute-start | bytes 196616 | tf_op jit(solution)/shard_map/ppermute | solution.py:465
  100.9 12.6 %collective-permute-start.20 = (f32[32,512]{1,0:T(8,128)}, f32[32,512]{1,0:T(8,128)S(1)}, u32[]{:S(2)}, u32[]{:S(2)}) collective-permute-start(f32[32,512]{1,0:T(8,128)} %get-tuple-element.58), channel_id=1, source_target_pairs={{0,6},{1,15},{2,4},{3,13},{4,2},{5,11},{6,0},{7,9},{8,14},{9,7},{1... | collective-permute-start | bytes 196616 | tf_op jit(solution)/shard_map/ppermute | solution.py:465
  104.7 8.8 %collective-permute-start.21 = (f32[32,512]{1,0:T(8,128)}, f32[32,512]{1,0:T(8,128)S(1)}, u32[]{:S(2)}, u32[]{:S(2)}) collective-permute-start(f32[32,512]{1,0:T(8,128)} %get-tuple-element.59), channel_id=1, source_target_pairs={{0,8},{1,1},{2,10},{3,3},{4,12},{5,5},{6,14},{7,7},{8,0},{9,9},{10... | collective-permute-start | bytes 196616 | tf_op jit(solution)/shard_map/ppermute | solution.py:465
  107.2 6.3 %collective-permute-start.22 = (f32[32,512]{1,0:T(8,128)}, f32[32,512]{1,0:T(8,128)S(1)}, u32[]{:S(2)}, u32[]{:S(2)}) collective-permute-start(f32[32,512]{1,0:T(8,128)} %get-tuple-element.60), channel_id=1, source_target_pairs={{0,10},{1,3},{2,8},{3,1},{4,14},{5,7},{6,12},{7,5},{8,2},{9,11},{1... | collective-permute-start | bytes 196616 | tf_op jit(solution)/shard_map/ppermute | solution.py:465
  107.3 6.3 %collective-permute-start.23 = (f32[32,512]{1,0:T(8,128)}, f32[32,512]{1,0:T(8,128)S(1)}, u32[]{:S(2)}, u32[]{:S(2)}) collective-permute-start(f32[32,512]{1,0:T(8,128)} %get-tuple-element.61), channel_id=1, source_target_pairs={{0,12},{1,5},{2,14},{3,7},{4,8},{5,1},{6,10},{7,3},{8,4},{9,13},{1... | collective-permute-start | bytes 196616 | tf_op jit(solution)/shard_map/ppermute | solution.py:465
  109.7 7.2 %collective-permute-start.24 = (f32[32,512]{1,0:T(8,128)}, f32[32,512]{1,0:T(8,128)S(1)}, u32[]{:S(2)}, u32[]{:S(2)}) collective-permute-start(f32[32,512]{1,0:T(8,128)} %get-tuple-element.62), channel_id=1, source_target_pairs={{0,14},{1,7},{2,12},{3,5},{4,10},{5,3},{6,8},{7,1},{8,6},{9,15},{1... | collective-permute-start | bytes 196616 | tf_op jit(solution)/shard_map/ppermute | solution.py:465
  (26 other events, 279.9 us)

commit v4 on v3

--- a/solution.py
+++ b/solution.py
@@ -92,25 +92,31 @@
     return jnp.concatenate([high, low], 1)
 
 
-def sort_kernel(blocks, where_ref, slot_ref, points_ref, weights_ref, base_ref, flag_ref, place_ref, pos_ref, *refs):
-    light_refs, (perm, vals, whole, light) = refs[:-4], refs[-4:]
-    chunks, split = slot_ref.shape[0], light.shape[-1]
+def spread(perm, here, rank):
+    lane = iota((LANES, LANES), 1).astype(f32)
+    for c in range(perm.shape[1] // LANES):
+        perm[here, c * LANES : (c + 1) * LANES] = onehot(lane + float(c * LANES) == rank)
+
+
+def sort_kernel(
+    fine, where_ref, slot_ref, points_ref, weights_ref, base_ref, flag_ref, place_ref, pos_ref, light_ref, perm, vals, whole
+):
+    chunks, split = slot_ref.shape[0], light_ref.shape[-1]
     rows = chunks * LANES
     slots = slot_ref[...]
     slot = slots.astype(f32)
     within = slots & (rows - 1)
     high, low = (within >> 5).astype(f32), (within & 31).astype(f32)
-    cols = jnp.concatenate([column(slot[c : c + 1]) for c in range(chunks)], 0)
-    before = jnp.zeros((rows, LANES), f32)
-    for c in range(chunks):
-        before += jnp.where(slot[c : c + 1] < cols, 1.0, 0.0)
-    rank = jnp.broadcast_to(jnp.sum(before, axis=1, keepdims=True), (rows, LANES))
-    place_of = rank.astype(jnp.int32)
-    for c in range(chunks):
-        at = slice(c * LANES, (c + 1) * LANES)
-        pos_ref[c : c + 1, :] = jnp.transpose(rank[at])[0:1]
-        perm[:, at] = onehot(iota((rows, LANES), 1) + c * LANES == place_of)
-        vals[0:LANES, at] = jnp.transpose(weights_ref[at, :]).astype(bf16)
+    for r in range(chunks):
+        here = slice(r * LANES, (r + 1) * LANES)
+        mine = column(slot[r : r + 1])
+        before = jnp.zeros((LANES, LANES), f32)
+        for c in range(chunks):
+            before += jnp.where(slot[c : c + 1] < mine, 1.0, 0.0)
+        rank = jnp.broadcast_to(jnp.sum(before, axis=1, keepdims=True), (LANES, LANES))
+        pos_ref[r : r + 1, :] = jnp.transpose(rank)[0:1]
+        spread(perm, here, rank)
+        vals[0:LANES, here] = jnp.transpose(weights_ref[here, :]).astype(bf16)
     scaled = points_ref[...] * point_scale
     ph, plo = two(scaled)
     nh, nm, nl = three(-0.5 * jnp.sum(scaled * scaled, axis=0, keepdims=True))
@@ -127,24 +133,18 @@
         moved = nn(vals[...], perm[:, s * step : (s + 1) * step])
         at = slice((s * step) % split, (s * step) % split + step)
         part = (s * step) // split
-        light[part, :, at] = moved[0:LANES]
+        light_ref[part, :, at] = moved[0:LANES]
         whole[part, 0:TAIL, at] = moved[128:192] + moved[192:256]
         tail = iota((8, step), 0)
         slot_row = moved[256:257] * 32.0 + moved[257:258]
         norm_row = moved[258:259] + moved[259:260] + moved[260:261]
         whole[part, TAIL:, at] = jnp.where(tail == SLOT, slot_row, jnp.where(tail == NORM, norm_row, 0.0))
-    if not blocks:
+    if not fine:
         place_ref[...] = whole[0]
-        light_refs[0][...] = light[0]
         return
-    leaf, sub, core = where_ref[0], where_ref[1], where_ref[2]
-    place_ref[...] = whole[leaf ^ core]
+    place_ref[...] = whole[where_ref[0] ^ where_ref[2]]
     place_ref[TAIL + BASE : TAIL + BASE + 1, 0:SK] = base_ref[...].astype(f32)
     place_ref[TAIL + FLAGS : TAIL + FLAGS + flag_ref.shape[0], 0 : flag_ref.shape[1]] = flag_ref[...].astype(f32)
-    width = LANES // blocks
-    for g, light_ref in enumerate(light_refs):
-        columns = aligned((sub ^ (g % blocks)) * width, width, width)
-        light_ref[...] = light[leaf ^ core ^ (g // blocks), columns, :]
 
 
 class Layout:
@@ -155,6 +155,12 @@
 
     def lanes(self, index):
         return aligned(index * self.per, self.per, LANES)
+
+    def message(self, where_ref, group):
+        if not self.fine:
+            return 0
+        leaf = where_ref[0] ^ where_ref[2] ^ (group // self.blocks)
+        return leaf * self.blocks + (where_ref[1] ^ (group % self.blocks))
 
     def gather(self, refs, index, part):
         return lanes_of([ref[part, self.lanes(index)] for ref in refs])
@@ -172,14 +178,31 @@
 
 
 def fill_perm(out, slot_rows):
-    for c in range(out.shape[1] // LANES):
-        at = slice(c * LANES, (c + 1) * LANES)
-        out[:, at] = onehot(iota((out.shape[0], LANES), 0) == slot_rows[:, at].astype(jnp.int32))
+    def rows_of(r, carry):
+        tree_row = (iota((LANES, LANES), 0) + r * LANES).astype(f32)
+        for c in range(out.shape[1] // LANES):
+            at = slice(c * LANES, (c + 1) * LANES)
+            out[aligned(r * LANES, LANES, LANES), at] = onehot(tree_row == slot_rows[:, at])
+        return carry
+
+    lax.fori_loop(0, out.shape[0] // LANES, rows_of, 0)
+
+
+def round_into(out, wide, rows, columns, base=0):
+    step = max(8192 // columns, 16)
+    for r in range(0, rows, step):
+        out[pl.ds(base + r, step), :] = wide[r : r + step, 0:columns].astype(bf16)
+
+
+def exp_into(out, wide):
+    rows, columns = wide.shape
+    for r in range(0, rows, 32):
+        out[r : r + 32, :] = jnp.exp2(wide[r : r + 32, :]).astype(bf16)
 
 
 def points_kernel(layout, trees, where_ref, upper_ref, small_ref, *refs):
     place_refs, refs = refs[: layout.count], refs[layout.count :]
-    a_ref, bt_ref, skt_ref, base_ref, upper_tiles_ref, top_ref, slot_ref, info_ref, perm, feats, sk_a = refs
+    a_ref, bt_ref, skt_ref, base_ref, upper_tiles_ref, top_ref, slot_ref, info_ref, perm, feats, sk_a, wide, tall = refs
     blocks, rows = layout.blocks, layout.rows
     lane = iota((SK, LANES), 1)
 
@@ -207,15 +230,21 @@
         feats[448:512, :] = extra_b.astype(bf16)
         fill_perm(perm, slots)
         mine = aligned(index * rows, rows, rows)
-        a_ref[mine, :] = nt(perm[...], feats[0:FEAT, :]).astype(bf16)
-        bt_ref[:, mine] = nt(feats[FEAT:, :], perm[...]).astype(bf16)
+        tall[...] = nt(perm[...], feats[0:FEAT, :])
+        wide[...] = nt(feats[FEAT:, :], perm[...])
+        for r in range(0, rows, 32):
+            a_ref[aligned(index * rows + r, 32, 32), :] = tall[r : r + 32, :].astype(bf16)
+        for r in range(0, FEAT, 16):
+            bt_ref[r : r + 16, mine] = wide[r : r + 16, :].astype(bf16)
         picks = column(info[BASE : BASE + 1]).astype(jnp.int32)
         chosen = jnp.concatenate([onehot(lane + c * LANES == picks) for c in range(rows // LANES)], 1)
         node = aligned(index * SK, SK, SK)
         own_a = nn(chosen, a_ref[mine, :]).astype(bf16)
         sk_a[node, :] = own_a
         skt_ref[:, node] = nt(bt_ref[:, mine], chosen).astype(bf16)
-        base_ref[index] = jnp.exp2(nn(own_a, bt_ref[:, mine])).astype(bf16)
+        wide[0:SK, :] = nn(own_a, bt_ref[:, mine])
+        for r in range(0, SK, 16):
+            base_ref[index, r : r + 16, :] = jnp.exp2(wide[r : r + 16, :]).astype(bf16)
         return carry
 
     lax.fori_loop(0, blocks, block, 0)
@@ -241,17 +270,21 @@
     top_ref[...] = jnp.where(lane < 64, exact, own_a[:, 128:])
 
 
-def weights_kernel(layout, base_ref, upper_tiles_ref, top_ref, slot_ref, *refs):
-    light_refs, (w_ref, coef_ref, pack_ref, perm, feats) = refs[: layout.count], refs[layout.count :]
+def weights_kernel(
+    layout, where_ref, base_ref, upper_tiles_ref, top_ref, slot_ref, light_ref, w_ref, coef_ref, pack_ref, perm, feats, tall
+):
     blocks, rows = layout.blocks, layout.rows
-    width = light_refs[0].shape[0]
+    width = light_ref.shape[1]
     feats[...] = jnp.zeros_like(feats)
 
     def block(index, carry):
         fill_perm(perm, slot_ref[pl.ds(index, 1), :])
-        feats[LANES - width :, :] = layout.gather(light_refs, index, slice(0, width)).astype(bf16)
+        light = [light_ref[layout.message(where_ref, g), :, layout.lanes(index)] for g in range(layout.count)]
+        feats[LANES - width :, :] = lanes_of(light).astype(bf16)
         mine = aligned(index * rows, rows, rows)
-        w_ref[mine, :] = nt(perm[...], feats[...]).astype(bf16)
+        tall[...] = nt(perm[...], feats[...])
+        for r in range(0, rows, 64):
+            w_ref[aligned(index * rows + r, 64, 64), :] = tall[r : r + 64, :].astype(bf16)
         coef = nn(base_ref[index], w_ref[mine, :])
         coef_ref[aligned(index * SK, SK, SK), :] = split_coefs(coef)
         pack_ref[...] = coef
@@ -270,7 +303,7 @@
     pack_ref[...] = top_ref[...] + pack_ref[...]
 
 
-def near_kernel(count_ref, list_ref, a_ref, bt_ref, w_ref, acc, times, tiles, ahead):
+def near_kernel(count_ref, list_ref, a_ref, bt_ref, w_ref, acc, times, tiles, ahead, second, tile_a, tile_b):
     every = count_ref.shape[1]
 
     def tally(leaf, filled):
@@ -308,20 +341,21 @@
     ahead[...] = exponents(0, 0)
 
     def step(tile, carry):
-        block = jnp.exp2(ahead[...]).astype(bf16)
-        second = exponents(tile, 1)
-        total = product(tile, 0, block)
+        here = aligned(tiles[0, tile] * LEAF, LEAF, LEAF)
+        many = tiles[2, tile].astype(f32)
+        second[...] = exponents(tile, 1)
+        exp_into(tile_a, ahead)
+        first = product(tile, 0, tile_a[...])
         ahead[...] = exponents(tile + 1, 0)
-        total = total + product(tile, 1, jnp.exp2(second).astype(bf16))
-        here = aligned(tiles[0, tile] * LEAF, LEAF, LEAF)
-        acc[here, :] += tiles[2, tile].astype(f32) * total
+        exp_into(tile_b, second)
+        acc[here, :] += many * (first + product(tile, 1, tile_b[...]))
         return carry
 
     lax.fori_loop(0, filled, step, 0)
 
 
 def far_kernel(layout, low_levels, pack_ref, slot_ref, info_ref, a_ref, skt_ref, coef_ref, near_ref, *refs):
-    out_refs, (perm, tops, coefs, scaled) = refs[: layout.count], refs[layout.count :]
+    out_refs, (perm, tops, coefs, scaled, wide, tile, turned) = refs[: layout.count], refs[layout.count :]
     blocks, rows = layout.blocks, layout.rows
     ups, width = pack_ref.shape[0], out_refs[0].shape[0]
     levels = low_levels + ups
@@ -347,7 +381,6 @@
             node, start, count = node // 2, start + count, count // 2
         fill_perm(perm, slot_ref[pl.ds(index, 1), :])
         info = info_ref[index]
-        halves = []
         for leaf in range(rows // LEAF):
             flags = info[FLAGS + leaf : FLAGS + leaf + 1]
             for level in range(levels):
@@ -355,10 +388,14 @@
                 flag = jnp.sum(jnp.where(lane[0:1] == level, flags, 0.0), axis=1, keepdims=True)
                 scaled[at, :] = (coefs[at, :].astype(f32) * flag).astype(bf16)
             here = aligned(index * rows + leaf * LEAF, LEAF, LEAF)
-            tile = jnp.exp2(nn(a_ref[here, :], tops[...]))
-            total = near_ref[here, :] + exact_product(tile, scaled[...])
-            halves.append(jnp.transpose(total)[LANES - width :, :])
-        high, low = two(jnp.concatenate(halves, 1))
+            wide[...] = nn(a_ref[here, :], tops[...])
+            exp_into(tile, wide)
+            wide[:, 0 : 2 * LANES] = nn(tile[...], scaled[...])
+            for r in range(0, LEAF, LANES):
+                near = near_ref[aligned(index * rows + leaf * LEAF + r, LANES, LANES), :]
+                near = near + wide[r : r + LANES, 0:LANES] + wide[r : r + LANES, LANES : 2 * LANES]
+                turned[:, leaf * LEAF + r : leaf * LEAF + r + LANES] = jnp.transpose(near)[LANES - width :]
+        high, low = two(turned[...])
         moved = nn(jnp.concatenate([high, low], 0), perm[...])
         moved = moved[:width] + moved[width:]
         for g, out_ref in enumerate(out_refs):
@@ -373,9 +410,8 @@
     chunks = pos_ref.shape[0]
     rows = chunks * LANES
     width, split = back_refs[0].shape
-    cols = jnp.concatenate([column(pos_ref[c : c + 1, :]) for c in range(chunks)], 0).astype(jnp.int32)
-    for c in range(chunks):
-        perm[:, c * LANES : (c + 1) * LANES] = onehot(iota((rows, LANES), 1) + c * LANES == cols)
+    for r in range(chunks):
+        spread(perm, slice(r * LANES, (r + 1) * LANES), column(pos_ref[r : r + 1, :]))
     for g, back_ref in enumerate(back_refs):
         high, low = two(back_ref[...])
         columns, at = 0, slice(0, rows)
@@ -435,19 +471,21 @@
     layout = Layout(blocks, trees, rows, fine)
     split = part if fine else rows
     where = jnp.stack([my_leaf, lax.axis_index("sub"), lax.axis_index("rep")]).astype(jnp.int32)
-    message = shaped((width, part), f32) if fine else shaped((columns, rows), f32)
     arrive = shaped((width, part), f32) if fine else shaped((width, total), f32)
 
-    place, pos, *light = pl.pallas_call(
-        functools.partial(sort_kernel, blocks if fine else 0),
-        out_shape=(shaped((PLACE_ROWS, split), f32), shaped((rows // LANES, LANES), f32)) + (message,) * layout.count,
+    place, pos, light = pl.pallas_call(
+        functools.partial(sort_kernel, fine),
+        out_shape=(
+            shaped((PLACE_ROWS, split), f32),
+            shaped((rows // LANES, LANES), f32),
+            shaped((rows // split, columns, split), f32),
+        ),
         in_specs=[spec(SMEM)] + [spec()] * 5,
-        out_specs=(spec(),) * (2 + layout.count),
+        out_specs=(spec(),) * 3,
         scratch_shapes=[
             vm((rows, rows), bf16),
             vm((272, rows), bf16),
             vm((rows // split, PLACE_ROWS, split), f32),
-            vm((rows // split, columns, split), f32),
         ],
         compiler_params=params(),
         name="sort_rows",
@@ -465,7 +503,10 @@
         return lax.ppermute(value, axes, pairs)
 
     def swap_all(values):
-        return [swap(value, g % blocks, g // blocks) for g, value in enumerate(values)]
+        done = {}
+        for g in sorted(range(len(values)), key=lambda g: -(g % blocks)):
+            done[g] = swap(values[g], g % blocks, g // blocks)
+        return [done[g] for g in range(len(values))]
 
     if fine:
         place = {0: swap(place, 0)}
@@ -475,8 +516,10 @@
                 place[step | stride] = lax.ppermute(place[step], "sub", [(i, i ^ stride) for i in range(blocks)])
             stride //= 2
         place = [place[step] for step in range(blocks)]
+        place, light = lax.optimization_barrier((place, light))
         place = place + [lax.ppermute(one, "rep", [(0, 1), (1, 0)]) for one in place]
-        light = swap_all(light)
+        light = light.reshape(devices, width, part)
+        light = lax.all_to_all(light, ("leaf", "sub"), split_axis=0, concat_axis=0, tiled=True)
         small = jnp.zeros((1, 8, SK), f32)
     else:
         info = jnp.pad(far_use.astype(f32), ((FLAGS, 5 - far_use.shape[0]), (0, SK - far_use.shape[1])))
@@ -486,10 +529,10 @@
         place = lax.all_gather(place, "sub", axis=0, tiled=False)
         place = place.transpose(1, 0, 2, 3).reshape(devices, PLACE_ROWS, blocks, per)
         place = [place.transpose(1, 2, 0, 3).reshape(PLACE_ROWS, total)]
-        light = light[0].reshape(columns, trees, part).transpose(1, 0, 2).reshape(devices, width, part)
+        light = light.reshape(columns, trees, part).transpose(1, 0, 2).reshape(devices, width, part)
         light = lax.all_to_all(light, ("leaf", "sub"), split_axis=0, concat_axis=0, tiled=True)
         light = light.reshape(devices, width, blocks, per)
-        light = [light.transpose(1, 2, 0, 3).reshape(width, total)]
+        light = light.transpose(1, 2, 0, 3).reshape(1, width, total)
 
     nodes = 2 * blocks - 1
     feat_a, feat_bt, sk, base, upper_tiles, top, slots, info = pl.pallas_call(
@@ -506,7 +549,13 @@
         ),
         in_specs=[spec(SMEM)] + [spec()] * (2 + layout.count),
         out_specs=(spec(),) * 8,
-        scratch_shapes=[vm((rows, rows), bf16), vm((2 * FEAT, rows), bf16), vm((nodes * SK, FEAT), bf16)],
+        scratch_shapes=[
+            vm((rows, rows), bf16),
+            vm((2 * FEAT, rows), bf16),
+            vm((nodes * SK, FEAT), bf16),
+            vm((FEAT, rows), f32),
+            vm((rows, FEAT), f32),
+        ],
         compiler_params=params(),
         name="tree_points",
     )(where, skeleton_upper, small, *place)
@@ -518,12 +567,12 @@
             shaped((nodes * SK, FEAT), bf16),
             shaped((SK, LANES), f32),
         ),
-        in_specs=[spec()] * (4 + layout.count),
+        in_specs=[spec(SMEM)] + [spec()] * 5,
         out_specs=(spec(),) * 3,
-        scratch_shapes=[vm((rows, rows), bf16), vm((LANES, rows), bf16)],
+        scratch_shapes=[vm((rows, rows), bf16), vm((LANES, rows), bf16), vm((rows, LANES), f32)],
         compiler_params=params(),
         name="tree_weights",
-    )(base, upper_tiles, top, slots, *light)
+    )(where, base, upper_tiles, top, slots, light)
 
     packs = upper_levels(pack, skeleton_upper, my_leaf, trees, blocks, width)
 
@@ -536,6 +585,9 @@
             pltpu.SMEM((leaves,), jnp.int32),
             pltpu.SMEM((3, leaves * leaves + 1), jnp.int32),
             vm((LEAF, LEAF // 2), f32),
+            vm((LEAF, LEAF // 2), f32),
+            vm((LEAF, LEAF // 2), bf16),
+            vm((LEAF, LEAF // 2), bf16),
         ],
         compiler_params=params(),
         name="near",
@@ -552,6 +604,9 @@
             vm((FEAT, levels * SK), bf16),
             vm((levels * SK, FEAT), bf16),
             vm((levels * SK, FEAT), bf16),
+            vm((LEAF, levels * SK), f32),
+            vm((LEAF, levels * SK), bf16),
+            vm((width, rows), f32),
         ],
         compiler_params=params(),
         name="far",

time: 120 us -> 112 us (0.933)
  starting transfers between devices: 47.8 us -> 32.4 us
  Pallas kernels: 55.6 us -> 60.5 us
  waiting for transfers between devices: 14 us -> 15.6 us
    ppermute x17 -> x9, starting transfers between devices: 33.4 us -> 16.1 us  [swap(): return lax.ppermute(value, axes, pairs)]
    all_to_all x0 -> x1, starting transfers between devices: none -> 5.44 us  [body(): lax.all_to_all(light, ('leaf', 'sub'), split_axis=0, concat_axis=0, tiled...]
    ppermute x3, waiting for transfers between devices: 3.24 us -> 8.07 us  [body(): lax.ppermute(place[step], 'sub', [(i, i ^ stride) for i in range(blocks)])]
    ppermute x17 -> x9, waiting for transfers between devices: 10.7 us -> 6.27 us  [swap(): return lax.ppermute(value, axes, pairs)]
    ppermute x4, starting transfers between devices: 5.82 us -> 2.55 us  [body(): lax.ppermute(one, 'rep', [(0, 1), (1, 0)])]
    pallas_call x1, Pallas kernels: 10.4 us -> 13.5 us  [body(): pl.pallas_call(functools.partial(points_kernel, layout, trees), out_shape...]
    pallas_call x1, Pallas kernels: 7.05 us -> 9.47 us  [body(): pl.pallas_call(functools.partial(weights_kernel, layout), out_shape=(shap...]
    ppermute x4, waiting for transfers between devices: 0.01 us -> 1.29 us  [body(): lax.ppermute(one, 'rep', [(0, 1), (1, 0)])]
  transfers between devices with their start and end apart: 25 -> 18, of which waited for: 5 -> 9; matrix products, arithmetic and copies ran while one was open for 0% -> 1% of each run, Pallas kernels for 26% -> 29%
where the time goes in v4:
time: 112 us
  Pallas kernels  60.5 us (54%)
  starting transfers between devices  32.4 us (29%)
  waiting for transfers between devices  15.6 us (14%)
  local copies, waits for them, and re-layouts  2.66 us (2%)
    pallas_call x1, Pallas kernels, body(): pl.pallas_call(near_kernel, out_shape=shaped((total, LANES), f32), in_spe...  19.3 us
    ppermute x9, starting transfers between devices, swap(): return lax.ppermute(value, axes, pairs)  16.1 us
    pallas_call x1, Pallas kernels, body(): pl.pallas_call(functools.partial(points_kernel, layout, trees), out_shape...  13.5 us
    pallas_call x1, Pallas kernels, body(): pl.pallas_call(functools.partial(far_kernel, layout, low_levels), out_sha...  11.4 us
    pallas_call x1, Pallas kernels, body(): pl.pallas_call(functools.partial(weights_kernel, layout), out_shape=(shap...  9.47 us
    ppermute x3, waiting for transfers between devices, body(): lax.ppermute(place[step], 'sub', [(i, i ^ stride) for i in range(blocks)])  8.07 us
    ppermute x3, starting transfers between devices, body(): lax.ppermute(place[step], 'sub', [(i, i ^ stride) for i in range(blocks)])  6.51 us
    ppermute x9, waiting for transfers between devices, swap(): return lax.ppermute(value, axes, pairs)  6.27 us
  transfers between devices with their start and end apart: 18, of which 9 were waited for; matrix products, arithmetic and copies ran while one was open for 1% of the time, Pallas kernels for 29%

profile of v4, /device:TPU:0, one launch (start us, length us, event | category | flops | bytes accessed | tf_op | source)
XLA Modules:
  0.0 112.0 jit_solution(7315241325241769852)
XLA Ops:
  0.7 3.7 %sort_rows.1 = (f32[72,512]{1,0:T(8,128)}, f32[8,128]{1,0:T(8,128)}, f32[2,128,512]{2,1,0:T(8,128)}) custom-call(s32[3]{0:T(128)} %pad_add_fusion.where_ref, s32[8,128]{1,0:T(8,128)} %bitcast.12, f32[64,1024]{1,0:T(8,128)} %bitcast.9, f32[1024,128]{1,0:T(8,128)} %refs_8_.1, s32[1,128]{1,0:T(1,128)} %base_ref.1, s32[2,3]{1,0:T(2,128)} %flag_ref.1), custom_call_target="tpu_custom_call" | custom-call | tf_op jit(solution)/shard_map/sort_rows/pallas_call | solution.py:476
  4.3 1.6 %collective-permute-start = (f32[72,512]{1,0:T(8,128)}, f32[72,512]{1,0:T(8,128)S(1)}, u32[]{:S(2)}, u32[]{:S(2)}) collective-permute-start(f32[72,512]{1,0:T(8,128)} %get-tuple-element.33), channel_id=1, source_target_pairs={{0,0},{1,9},{2,2},{3,11},{4,4},{5,13},{6,6},{7,15},{8,8},{9,1},{10... | collective-permute-start | bytes 442376 | tf_op jit(solution)/shard_map/ppermute | solution.py:503
  5.9 4.0 %collective-permute-start.2 = (f32[72,512]{1,0:T(8,128)S(1)}, f32[72,512]{1,0:T(8,128)S(1)}, u32[]{:S(2)}, u32[]{:S(2)}) collective-permute-start(f32[72,512]{1,0:T(8,128)S(1)} %collective-permute-done.refs_0_), channel_id=1, source_target_pairs={{0,4},{2,6},{4,0},{6,2},{1,5},{3,7},{5,1},{7,3},{8,12},{10,14},{12... | collective-permute-start | bytes 442376 | tf_op jit(solution)/shard_map/ppermute | solution.py:516
  9.9 1.6 %collective-permute-start.1 = (f32[72,512]{1,0:T(8,128)S(1)}, f32[72,512]{1,0:T(8,128)S(1)}, u32[]{:S(2)}, u32[]{:S(2)}) collective-permute-start(f32[72,512]{1,0:T(8,128)S(1)} %collective-permute-done.refs_0_), channel_id=1, source_target_pairs={{0,2},{2,0},{4,6},{6,4},{1,3},{3,1},{5,7},{7,5},{8,10},{10,8},{12,... | collective-permute-start | bytes 442376 | tf_op jit(solution)/shard_map/ppermute | solution.py:516
  11.5 3.2 %collective-permute-done.2.refs_2_ = f32[72,512]{1,0:T(8,128)S(1)} collective-permute-done((f32[72,512]{1,0:T(8,128)S(1)}, f32[72,512]{1,0:T(8,128)S(1)}, u32[]{:S(2)}, u32[]{:S(2)}) %collective-permute-start.2) | collective-permute-done | bytes 147488 | tf_op jit(solution)/shard_map/ppermute | solution.py:516
  14.7 0.9 collective-permute-start.3
  15.6 4.8 %collective-permute-done.3.refs_3_ = f32[72,512]{1,0:T(8,128)S(1)} collective-permute-done((f32[72,512]{1,0:T(8,128)S(1)}, f32[72,512]{1,0:T(8,128)S(1)}, u32[]{:S(2)}, u32[]{:S(2)}) %collective-permute-start.3) | collective-permute-done | bytes 147488 | tf_op jit(solution)/shard_map/ppermute | solution.py:516
  20.5 5.4 %all-to-all-start = ((f32[8,32,512]{2,1,0:T(8,128)}), f32[8,32,512]{2,1,0:T(8,128)S(1)}, u32[]{:S(2)}, u32[]{:S(2)}) async-start(f32[8,32,512]{2,1,0:T(8,128)} %bitcast.8), calls=%async_computation | async-start | bytes 1048576 | tf_op jit(solution)/shard_map/all_to_all | solution.py:522
  25.9 2.0 %collective-permute-start.4 = (f32[72,512]{1,0:T(8,128)S(1)}, f32[72,512]{1,0:T(8,128)S(1)}, u32[]{:S(2)}, u32[]{:S(2)}) collective-permute-start(f32[72,512]{1,0:T(8,128)S(1)} %collective-permute-done.refs_0_), channel_id=1, source_target_pairs={{0,1},{1,0},{2,3},{3,2},{4,5},{5,4},{6,7},{7,6},{8,9},{9,8},{10,11... | collective-permute-start | bytes 442376 | tf_op jit(solution)/shard_map/ppermute | solution.py:520
  30.4 13.5 %tree_points.1 = (bf16[4096,256]{1,0:T(8,128)(2,1)}, bf16[256,4096]{1,0:T(8,128)(2,1)}, bf16[256,896]{1,0:T(8,128)(2,1)}, bf16[4,128,1024]{2,1,0:T(8,128)(2,1)},...) custom-call(s32[3]{0:T(128)} %pad_add_fusion.where_ref, ...), custom_call_target="tpu_custom_call" | custom-call | tf_op jit(solution)/shard_map/tree_points/pallas_call | solution.py:538
  44.7 9.5 %tree_weights.1 = (bf16[4096,128]{1,0:T(8,128)(2,1)}, bf16[896,256]{1,0:T(8,128)(2,1)}, f32[128,128]{1,0:T(8,128)}) custom-call(s32[3]{0:T(128)} %pad_add_fusion.where_ref, bf16[4,128,1024]{2,1,0:T(8,128)(2,1)} %get-tuple-element.39.base_ref, f32[3,128,256]{2,1,0:T(8,128)} %get-tuple-element.40.upper_tiles_ref, f32[128,128]{1,0:T(8,128)} %get-tuple-element.41.top_ref, ...), custom_call_target="tpu_custom_call" | custom-call | tf_op jit(solution)/shard_map/tree_weights/pallas_call | solution.py:563
  54.2 1.7 %collective-permute-start.8 = (f32[128,128]{1,0:T(8,128)}, f32[128,128]{1,0:T(8,128)S(1)}, u32[]{:S(2)}, u32[]{:S(2)}) collective-permute-start(f32[128,128]{1,0:T(8,128)} %get-tuple-element.44), channel_id=1, source_target_pairs={{0,8},{8,0},{1,9},{9,1},{2,10},{10,2},{3,11},{11,3},{4,12},{12,4},... | collective-permute-start | bytes 196616 | tf_op jit(solution)/shard_map/ppermute | solution.py:439
  55.9 19.3 %near.1.near_ref = f32[4096,128]{1,0:T(8,128)} custom-call(s32[1,8]{1,0:T(1,128)} %count_ref.1, s32[8,16]{1,0:T(8,128)} %bitcast.11, bf16[4096,256]{1,0:T(8,128)(2,1)} %get-tuple-element.46.a_ref, bf16[256,4096]{1,0:T(8,128)(2,1)} %get-tuple-element.49.bt_ref, bf16[4096,128]{1,0:T(8,128)(2,1)} %get-tuple-element.50.w_ref), custom_call_target="tpu_custom_call" | custom-call | tf_op jit(solution)/shard_map/near/pallas_call | solution.py:579
  75.9 11.4 %far.1 = (f32[32,512]{1,0:T(8,128)}, f32[32,512]{1,0:T(8,128)}, f32[32,512]{1,0:T(8,128)}, f32[32,512]{1,0:T(8,128)}, f32[32,512]{1,0:T(8,128)}, /*index=5*/f32[...) custom-call(f32[1,128,128]{2,1,0:T(8,128)} %bitcast.10, f32[4,1024]{1,0:T(4,128)} %get-tuple-element.42.slot_ref, ...), custom_call_target="tpu_custom_call" | custom-call | tf_op jit(solution)/shard_map/far/pallas_call | solution.py:597
  87.2 1.5 %collective-permute-start.9 = (f32[32,512]{1,0:T(8,128)}, f32[32,512]{1,0:T(8,128)S(1)}, u32[]{:S(2)}, u32[]{:S(2)}) collective-permute-start(f32[32,512]{1,0:T(8,128)} %get-tuple-element.51), channel_id=1, source_target_pairs={{0,0},{1,9},{2,2},{3,11},{4,4},{5,13},{6,6},{7,15},{8,8},{9,1},{10... | collective-permute-start | bytes 196616 | tf_op jit(solution)/shard_map/ppermute | solution.py:503
  88.7 1.5 %collective-permute-start.10 = (f32[32,512]{1,0:T(8,128)}, f32[32,512]{1,0:T(8,128)S(1)}, u32[]{:S(2)}, u32[]{:S(2)}) collective-permute-start(f32[32,512]{1,0:T(8,128)} %get-tuple-element.52), channel_id=1, source_target_pairs={{0,2},{1,11},{2,0},{3,9},{4,6},{5,15},{6,4},{7,13},{8,10},{9,3},{1... | collective-permute-start | bytes 196616 | tf_op jit(solution)/shard_map/ppermute | solution.py:503
  90.2 2.4 %collective-permute-start.11 = (f32[32,512]{1,0:T(8,128)}, f32[32,512]{1,0:T(8,128)S(1)}, u32[]{:S(2)}, u32[]{:S(2)}) collective-permute-start(f32[32,512]{1,0:T(8,128)} %get-tuple-element.53), channel_id=1, source_target_pairs={{0,4},{1,13},{2,6},{3,15},{4,0},{5,9},{6,2},{7,11},{8,12},{9,5},{1... | collective-permute-start | bytes 196616 | tf_op jit(solution)/shard_map/ppermute | solution.py:503
  93.1 2.8 %collective-permute-start.13 = (f32[32,512]{1,0:T(8,128)}, f32[32,512]{1,0:T(8,128)S(1)}, u32[]{:S(2)}, u32[]{:S(2)}) collective-permute-start(f32[32,512]{1,0:T(8,128)} %get-tuple-element.55), channel_id=1, source_target_pairs={{0,8},{1,1},{2,10},{3,3},{4,12},{5,5},{6,14},{7,7},{8,0},{9,9},{10... | collective-permute-start | bytes 196616 | tf_op jit(solution)/shard_map/ppermute | solution.py:503
  95.9 1.2 %collective-permute-start.14 = (f32[32,512]{1,0:T(8,128)}, f32[32,512]{1,0:T(8,128)S(1)}, u32[]{:S(2)}, u32[]{:S(2)}) collective-permute-start(f32[32,512]{1,0:T(8,128)} %get-tuple-element.56), channel_id=1, source_target_pairs={{0,10},{1,3},{2,8},{3,1},{4,14},{5,7},{6,12},{7,5},{8,2},{9,11},{1... | collective-permute-start | bytes 196616 | tf_op jit(solution)/shard_map/ppermute | solution.py:503
  97.1 3.8 %collective-permute-start.15 = (f32[32,512]{1,0:T(8,128)}, f32[32,512]{1,0:T(8,128)S(1)}, u32[]{:S(2)}, u32[]{:S(2)}) collective-permute-start(f32[32,512]{1,0:T(8,128)} %get-tuple-element.57), channel_id=1, source_target_pairs={{0,12},{1,5},{2,14},{3,7},{4,8},{5,1},{6,10},{7,3},{8,4},{9,13},{1... | collective-permute-start | bytes 196616 | tf_op jit(solution)/shard_map/ppermute | solution.py:503
  101.0 0.9 collective-permute-start.16
  102.3 3.5 %collective-permute-done.15.refs_6_ = f32[32,512]{1,0:T(8,128)S(1)} collective-permute-done((f32[32,512]{1,0:T(8,128)}, f32[32,512]{1,0:T(8,128)S(1)}, u32[]{:S(2)}, u32[]{:S(2)}) %collective-permute-start.15) | collective-permute-done | bytes 65568 | tf_op jit(solution)/shard_map/ppermute | solution.py:503
  105.8 2.3 %collective-permute-done.16.refs_7_ = f32[32,512]{1,0:T(8,128)S(1)} collective-permute-done((f32[32,512]{1,0:T(8,128)}, f32[32,512]{1,0:T(8,128)S(1)}, u32[]{:S(2)}, u32[]{:S(2)}) %collective-permute-start.16) | collective-permute-done | bytes 65568 | tf_op jit(solution)/shard_map/ppermute | solution.py:503
  108.8 3.2 %to_input_order.1 = f32[1024,128]{1,0:T(8,128)} custom-call(s32[3]{0:T(128)} %pad_add_fusion.where_ref, f32[8,128]{1,0:T(8,128)} %get-tuple-element.32.pos_ref, f32[32,512]{1,0:T(8,128)} %copy-done.10, f32[32,512]{1,0:T(8,128)} %copy-done.11, f32[32,512]{1,0:T(8,128)} %copy-done.12, f32[32,512]{1,0:T(8,128)} %copy-done.13, f32[32,512]{1,0:T(8,128)} %copy-done.14, ...), custom_call_target="tpu_custom_call" | custom-call | tf_op jit(solution)/shard_map/to_input_order/pallas_call | solution.py:622
  (56 shorter events, 6.2 us)
Async XLA Ops:
  4.3 1.6 %collective-permute-start = (f32[72,512]{1,0:T(8,128)}, f32[72,512]{1,0:T(8,128)S(1)}, u32[]{:S(2)}, u32[]{:S(2)}) collective-permute-start(f32[72,512]{1,0:T(8,128)} %get-tuple-element.33), channel_id=1, source_target_pairs={{0,0},{1,9},{2,2},{3,11},{4,4},{5,13},{6,6},{7,15},{8,8},{9,1},{10... | collective-permute-start | bytes 442376 | tf_op jit(solution)/shard_map/ppermute | solution.py:503
  5.9 24.5 %copy-start.1 = (f32[72,512]{1,0:T(8,128)}, f32[72,512]{1,0:T(8,128)S(1)}, u32[]{:S(2)}) copy-start(f32[72,512]{1,0:T(8,128)S(1)} %collective-permute-done.refs_0_) | copy-start | bytes 442372
  5.9 8.8 %collective-permute-start.2 = (f32[72,512]{1,0:T(8,128)S(1)}, f32[72,512]{1,0:T(8,128)S(1)}, u32[]{:S(2)}, u32[]{:S(2)}) collective-permute-start(f32[72,512]{1,0:T(8,128)S(1)} %collective-permute-done.refs_0_), channel_id=1, source_target_pairs={{0,4},{2,6},{4,0},{6,2},{1,5},{3,7},{5,1},{7,3},{8,12},{10,14},{12... | collective-permute-start | bytes 442376 | tf_op jit(solution)/shard_map/ppermute | solution.py:516
  9.9 5.7 %collective-permute-start.1 = (f32[72,512]{1,0:T(8,128)S(1)}, f32[72,512]{1,0:T(8,128)S(1)}, u32[]{:S(2)}, u32[]{:S(2)}) collective-permute-start(f32[72,512]{1,0:T(8,128)S(1)} %collective-permute-done.refs_0_), channel_id=1, source_target_pairs={{0,2},{2,0},{4,6},{6,4},{1,3},{3,1},{5,7},{7,5},{8,10},{10,8},{12,... | collective-permute-start | bytes 442376 | tf_op jit(solution)/shard_map/ppermute | solution.py:516
  14.7 15.6 %copy-start.2 = (f32[72,512]{1,0:T(8,128)}, f32[72,512]{1,0:T(8,128)S(1)}, u32[]{:S(2)}) copy-start(f32[72,512]{1,0:T(8,128)S(1)} %collective-permute-done.2.refs_2_) | copy-start | bytes 442372
  14.7 5.7 %collective-permute-start.3 = (f32[72,512]{1,0:T(8,128)S(1)}, f32[72,512]{1,0:T(8,128)S(1)}, u32[]{:S(2)}, u32[]{:S(2)}) collective-permute-start(f32[72,512]{1,0:T(8,128)S(1)} %collective-permute-done.2.refs_2_), channel_id=1, source_target_pairs={{0,2},{2,0},{4,6},{6,4},{1,3},{3,1},{5,7},{7,5},{8,10},{10,8},{12,... | collective-permute-start | bytes 442376 | tf_op jit(solution)/shard_map/ppermute | solution.py:516
  15.6 14.7 %copy-start.3 = (f32[72,512]{1,0:T(8,128)}, f32[72,512]{1,0:T(8,128)S(1)}, u32[]{:S(2)}) copy-start(f32[72,512]{1,0:T(8,128)S(1)} %collective-permute-done.1.refs_1_) | copy-start | bytes 442372
  20.5 9.9 %copy-start.4 = (f32[72,512]{1,0:T(8,128)}, f32[72,512]{1,0:T(8,128)S(1)}, u32[]{:S(2)}) copy-start(f32[72,512]{1,0:T(8,128)S(1)} %collective-permute-done.3.refs_3_) | copy-start | bytes 442372
  20.5 23.4 %all-to-all-start = ((f32[8,32,512]{2,1,0:T(8,128)}), f32[8,32,512]{2,1,0:T(8,128)S(1)}, u32[]{:S(2)}, u32[]{:S(2)}) async-start(f32[8,32,512]{2,1,0:T(8,128)} %bitcast.8), calls=%async_computation | async-start | bytes 1048576 | tf_op jit(solution)/shard_map/all_to_all | solution.py:522
  25.9 3.0 %collective-permute-start.4 = (f32[72,512]{1,0:T(8,128)S(1)}, f32[72,512]{1,0:T(8,128)S(1)}, u32[]{:S(2)}, u32[]{:S(2)}) collective-permute-start(f32[72,512]{1,0:T(8,128)S(1)} %collective-permute-done.refs_0_), channel_id=1, source_target_pairs={{0,1},{1,0},{2,3},{3,2},{4,5},{5,4},{6,7},{7,6},{8,9},{9,8},{10,11... | collective-permute-start | bytes 442376 | tf_op jit(solution)/shard_map/ppermute | solution.py:520
  27.9 1.4 %collective-permute-start.5 = (f32[72,512]{1,0:T(8,128)S(1)}, f32[72,512]{1,0:T(8,128)S(1)}, u32[]{:S(2)}, u32[]{:S(2)}) collective-permute-start(f32[72,512]{1,0:T(8,128)S(1)} %collective-permute-done.1.refs_1_), channel_id=1, source_target_pairs={{0,1},{1,0},{2,3},{3,2},{4,5},{5,4},{6,7},{7,6},{8,9},{9,8},{10,11... | collective-permute-start | bytes 442376 | tf_op jit(solution)/shard_map/ppermute | solution.py:520
  28.0 1.5 %collective-permute-start.6 = (f32[72,512]{1,0:T(8,128)S(1)}, f32[72,512]{1,0:T(8,128)S(1)}, u32[]{:S(2)}, u32[]{:S(2)}) collective-permute-start(f32[72,512]{1,0:T(8,128)S(1)} %collective-permute-done.2.refs_2_), channel_id=1, source_target_pairs={{0,1},{1,0},{2,3},{3,2},{4,5},{5,4},{6,7},{7,6},{8,9},{9,8},{10,11... | collective-permute-start | bytes 442376 | tf_op jit(solution)/shard_map/ppermute | solution.py:520
  28.4 1.4 %collective-permute-start.7 = (f32[72,512]{1,0:T(8,128)S(1)}, f32[72,512]{1,0:T(8,128)S(1)}, u32[]{:S(2)}, u32[]{:S(2)}) collective-permute-start(f32[72,512]{1,0:T(8,128)S(1)} %collective-permute-done.3.refs_3_), channel_id=1, source_target_pairs={{0,1},{1,0},{2,3},{3,2},{4,5},{5,4},{6,7},{7,6},{8,9},{9,8},{10,11... | collective-permute-start | bytes 442376 | tf_op jit(solution)/shard_map/ppermute | solution.py:520
  54.2 21.0 %collective-permute-start.8 = (f32[128,128]{1,0:T(8,128)}, f32[128,128]{1,0:T(8,128)S(1)}, u32[]{:S(2)}, u32[]{:S(2)}) collective-permute-start(f32[128,128]{1,0:T(8,128)} %get-tuple-element.44), channel_id=1, source_target_pairs={{0,8},{8,0},{1,9},{9,1},{2,10},{10,2},{3,11},{11,3},{4,12},{12,4},... | collective-permute-start | bytes 196616 | tf_op jit(solution)/shard_map/ppermute | solution.py:439
  87.2 8.6 %collective-permute-start.9 = (f32[32,512]{1,0:T(8,128)}, f32[32,512]{1,0:T(8,128)S(1)}, u32[]{:S(2)}, u32[]{:S(2)}) collective-permute-start(f32[32,512]{1,0:T(8,128)} %get-tuple-element.51), channel_id=1, source_target_pairs={{0,0},{1,9},{2,2},{3,11},{4,4},{5,13},{6,6},{7,15},{8,8},{9,1},{10... | collective-permute-start | bytes 196616 | tf_op jit(solution)/shard_map/ppermute | solution.py:503
  88.7 8.4 %collective-permute-start.10 = (f32[32,512]{1,0:T(8,128)}, f32[32,512]{1,0:T(8,128)S(1)}, u32[]{:S(2)}, u32[]{:S(2)}) collective-permute-start(f32[32,512]{1,0:T(8,128)} %get-tuple-element.52), channel_id=1, source_target_pairs={{0,2},{1,11},{2,0},{3,9},{4,6},{5,15},{6,4},{7,13},{8,10},{9,3},{1... | collective-permute-start | bytes 196616 | tf_op jit(solution)/shard_map/ppermute | solution.py:503
  90.2 10.8 %collective-permute-start.11 = (f32[32,512]{1,0:T(8,128)}, f32[32,512]{1,0:T(8,128)S(1)}, u32[]{:S(2)}, u32[]{:S(2)}) collective-permute-start(f32[32,512]{1,0:T(8,128)} %get-tuple-element.53), channel_id=1, source_target_pairs={{0,4},{1,13},{2,6},{3,15},{4,0},{5,9},{6,2},{7,11},{8,12},{9,5},{1... | collective-permute-start | bytes 196616 | tf_op jit(solution)/shard_map/ppermute | solution.py:503
  92.5 9.3 %collective-permute-start.12 = (f32[32,512]{1,0:T(8,128)}, f32[32,512]{1,0:T(8,128)S(1)}, u32[]{:S(2)}, u32[]{:S(2)}) collective-permute-start(f32[32,512]{1,0:T(8,128)} %get-tuple-element.54), channel_id=1, source_target_pairs={{0,6},{1,15},{2,4},{3,13},{4,2},{5,11},{6,0},{7,9},{8,14},{9,7},{1... | collective-permute-start | bytes 196616 | tf_op jit(solution)/shard_map/ppermute | solution.py:503
  93.1 8.8 %collective-permute-start.13 = (f32[32,512]{1,0:T(8,128)}, f32[32,512]{1,0:T(8,128)S(1)}, u32[]{:S(2)}, u32[]{:S(2)}) collective-permute-start(f32[32,512]{1,0:T(8,128)} %get-tuple-element.55), channel_id=1, source_target_pairs={{0,8},{1,1},{2,10},{3,3},{4,12},{5,5},{6,14},{7,7},{8,0},{9,9},{10... | collective-permute-start | bytes 196616 | tf_op jit(solution)/shard_map/ppermute | solution.py:503
  95.9 12.3 %copy-start.10 = (f32[32,512]{1,0:T(8,128)}, f32[32,512]{1,0:T(8,128)S(1)}, u32[]{:S(2)}) copy-start(f32[32,512]{1,0:T(8,128)S(1)} %collective-permute-done.9.refs_0_) | copy-start | bytes 196612
  95.9 6.4 %collective-permute-start.14 = (f32[32,512]{1,0:T(8,128)}, f32[32,512]{1,0:T(8,128)S(1)}, u32[]{:S(2)}, u32[]{:S(2)}) collective-permute-start(f32[32,512]{1,0:T(8,128)} %get-tuple-element.56), channel_id=1, source_target_pairs={{0,10},{1,3},{2,8},{3,1},{4,14},{5,7},{6,12},{7,5},{8,2},{9,11},{1... | collective-permute-start | bytes 196616 | tf_op jit(solution)/shard_map/ppermute | solution.py:503
  97.1 11.0 %copy-start.11 = (f32[32,512]{1,0:T(8,128)}, f32[32,512]{1,0:T(8,128)S(1)}, u32[]{:S(2)}) copy-start(f32[32,512]{1,0:T(8,128)S(1)} %collective-permute-done.10.refs_1_) | copy-start | bytes 196612
  97.1 8.7 %collective-permute-start.15 = (f32[32,512]{1,0:T(8,128)}, f32[32,512]{1,0:T(8,128)S(1)}, u32[]{:S(2)}, u32[]{:S(2)}) collective-permute-start(f32[32,512]{1,0:T(8,128)} %get-tuple-element.57), channel_id=1, source_target_pairs={{0,12},{1,5},{2,14},{3,7},{4,8},{5,1},{6,10},{7,3},{8,4},{9,13},{1... | collective-permute-start | bytes 196616 | tf_op jit(solution)/shard_map/ppermute | solution.py:503
  101.0 7.2 %collective-permute-start.16 = (f32[32,512]{1,0:T(8,128)}, f32[32,512]{1,0:T(8,128)S(1)}, u32[]{:S(2)}, u32[]{:S(2)}) collective-permute-start(f32[32,512]{1,0:T(8,128)} %get-tuple-element.58), channel_id=1, source_target_pairs={{0,14},{1,7},{2,12},{3,5},{4,10},{5,3},{6,8},{7,1},{8,6},{9,15},{1... | collective-permute-start | bytes 196616 | tf_op jit(solution)/shard_map/ppermute | solution.py:503
  (12 other events, 34.3 us)

commit v5 on v4

--- a/solution.py
+++ b/solution.py
@@ -13,6 +13,8 @@
 SK = 128
 LANES = 128
 FEAT = 256
+LOW = 256
+COORD = 144
 
 highest = lax.Precision.HIGHEST
 point_scale = math.sqrt(2.0 * math.log2(math.e) / 32.0)
@@ -81,15 +83,9 @@
     return pl.ds(pl.multiple_of(start, unit), size)
 
 
-def exact_product(block, coefs):
-    high, low = two(block)
-    first = nn(high, coefs)
-    return first[:, :LANES] + first[:, LANES:] + nn(low, coefs[:, :LANES])
-
-
-def split_coefs(value):
+def stack_two(value):
     high, low = two(value)
-    return jnp.concatenate([high, low], 1)
+    return jnp.concatenate([high, low], 0)
 
 
 def spread(perm, here, rank):
@@ -177,34 +173,40 @@
         return found
 
 
-def fill_perm(out, slot_rows):
-    def rows_of(r, carry):
-        tree_row = (iota((LANES, LANES), 0) + r * LANES).astype(f32)
-        for c in range(out.shape[1] // LANES):
-            at = slice(c * LANES, (c + 1) * LANES)
-            out[aligned(r * LANES, LANES, LANES), at] = onehot(tree_row == slot_rows[:, at])
-        return carry
-
-    lax.fori_loop(0, out.shape[0] // LANES, rows_of, 0)
-
-
-def round_into(out, wide, rows, columns, base=0):
-    step = max(8192 // columns, 16)
-    for r in range(0, rows, step):
-        out[pl.ds(base + r, step), :] = wide[r : r + step, 0:columns].astype(bf16)
-
-
-def exp_into(out, wide):
-    rows, columns = wide.shape
-    for r in range(0, rows, 32):
-        out[r : r + 32, :] = jnp.exp2(wide[r : r + 32, :]).astype(bf16)
+def low_by_column(out, low):
+    for c in range(out.shape[0] // LANES):
+        at = slice(c * LANES, (c + 1) * LANES)
+        spread(out, at, column(low[:, at]))
+
+
+def parts_of(slots):
+    slots = slots.astype(jnp.int32)
+    return slots & (LOW - 1), slots // LOW
+
+
+def feature_columns(out, at, tree):
+    out[0:64, at] = tree[0:64].astype(bf16)
+    out[64:128, at] = tree[0:64].astype(bf16)
+    out[128:192, at] = tree[64:128].astype(bf16)
+    out[192:256, at] = jnp.concatenate([tree[128:136], jnp.zeros((56, tree.shape[1]), f32)], 0).astype(bf16)
+
+
+def feature_rows(high, low, extra):
+    first = jnp.transpose(jnp.concatenate([high, low], 0))
+    second = jnp.transpose(jnp.concatenate([high, extra, jnp.zeros((56, high.shape[1]), f32)], 0))
+    return first.astype(bf16), second.astype(bf16)
 
 
 def points_kernel(layout, trees, where_ref, upper_ref, small_ref, *refs):
     place_refs, refs = refs[: layout.count], refs[layout.count :]
-    a_ref, bt_ref, skt_ref, base_ref, upper_tiles_ref, top_ref, slot_ref, info_ref, perm, feats, sk_a, wide, tall = refs
+    a_ref, bt_ref, sk_ref, base_ref, upper_tiles_ref, top_ref, slot_ref, info_ref, masked, low_hot, tree, sk_t, sk_bt = refs
     blocks, rows = layout.blocks, layout.rows
-    lane = iota((SK, LANES), 1)
+
+    def keep(node, found):
+        at = aligned(node * SK, SK, SK)
+        sk_t[:, at] = found.astype(bf16)
+        sk_ref[at, 0:128], sk_ref[at, 128:256] = feature_rows(found[0:64], found[64:128], found[136:144])
+        feature_columns(sk_bt, slice(0, SK), found)
 
     def block(index, carry):
         tail = layout.gather(place_refs, index, slice(TAIL, PLACE_ROWS))
@@ -215,36 +217,29 @@
         points = layout.gather(place_refs, index, slice(0, TAIL))
         high, low = two(points)
         nh, nm, nl = three(tail[NORM : NORM + 1])
-        sub = iota((64, rows), 0)
-        extra_a = jnp.where(sub == 0, nh, jnp.where(sub == 1, nm, jnp.where(sub == 2, nl, 0.0)))
-        extra_a = jnp.where((sub >= 3) & (sub < 6), 1.0, extra_a)
-        extra_b = jnp.where(sub == 3, nh, jnp.where(sub == 4, nm, jnp.where(sub == 5, nl, 0.0)))
-        extra_b = jnp.where(sub < 3, 1.0, extra_b)
-        feats[0:64, :] = high
-        feats[64:128, :] = low
-        feats[128:192, :] = high
-        feats[192:256, :] = extra_a.astype(bf16)
-        feats[256:320, :] = high
-        feats[320:384, :] = high
-        feats[384:448, :] = low
-        feats[448:512, :] = extra_b.astype(bf16)
-        fill_perm(perm, slots)
+        sub = iota((16, rows), 0)
+        norms = jnp.where((sub == 3) | (sub == 8), nh, jnp.where((sub == 4) | (sub == 9), nm, nl))
+        is_norm = ((sub >= 3) & (sub < 6)) | ((sub >= 8) & (sub < 11))
+        is_one = (sub < 3) | ((sub >= 11) & (sub < 14))
+        extra = jnp.where(is_norm, norms, jnp.where(is_one, 1.0, 0.0))
+        low_part, high_part = parts_of(slots)
+        low_by_column(low_hot, low_part.astype(f32))
+        for h in range(rows // LOW):
+            here = high_part == h
+            masked[h * COORD : h * COORD + 64, :] = jnp.where(here, high.astype(f32), 0.0).astype(bf16)
+            masked[h * COORD + 64 : h * COORD + 128, :] = jnp.where(here, low.astype(f32), 0.0).astype(bf16)
+            masked[h * COORD + 128 : (h + 1) * COORD, :] = jnp.where(here, extra, 0.0).astype(bf16)
+        placed = nn(masked[...], low_hot[...])
+        for h in range(rows // LOW):
+            part = placed[h * COORD : (h + 1) * COORD]
+            tree[:, h * LOW : (h + 1) * LOW] = part.astype(bf16)
+            at = aligned(index * rows + h * LOW, LOW, LOW)
+            feature_columns(bt_ref, at, part)
+            a_ref[at, 0:128], a_ref[at, 128:256] = feature_rows(part[0:64], part[64:128], part[136:144])
+        picked = onehot(iota((rows, SK), 0) == info[BASE : BASE + 1].astype(jnp.int32))
+        keep(index, nn(tree[...], picked))
         mine = aligned(index * rows, rows, rows)
-        tall[...] = nt(perm[...], feats[0:FEAT, :])
-        wide[...] = nt(feats[FEAT:, :], perm[...])
-        for r in range(0, rows, 32):
-            a_ref[aligned(index * rows + r, 32, 32), :] = tall[r : r + 32, :].astype(bf16)
-        for r in range(0, FEAT, 16):
-            bt_ref[r : r + 16, mine] = wide[r : r + 16, :].astype(bf16)
-        picks = column(info[BASE : BASE + 1]).astype(jnp.int32)
-        chosen = jnp.concatenate([onehot(lane + c * LANES == picks) for c in range(rows // LANES)], 1)
-        node = aligned(index * SK, SK, SK)
-        own_a = nn(chosen, a_ref[mine, :]).astype(bf16)
-        sk_a[node, :] = own_a
-        skt_ref[:, node] = nt(bt_ref[:, mine], chosen).astype(bf16)
-        wide[0:SK, :] = nn(own_a, bt_ref[:, mine])
-        for r in range(0, SK, 16):
-            base_ref[index, r : r + 16, :] = jnp.exp2(wide[r : r + 16, :]).astype(bf16)
+        base_ref[index] = jnp.exp2(nn(a_ref[mine, :], sk_bt[...])).astype(bf16)
         return carry
 
     lax.fori_loop(0, blocks, block, 0)
@@ -254,40 +249,42 @@
         for j in range(nodes):
             pair = slice((start + 2 * j) * SK, (start + 2 * j + 2) * SK)
             row = offset + where_ref[0] * nodes + j
-            picks = column(upper_ref[pl.ds(row, 1), :].astype(f32)).astype(jnp.int32)
-            chosen = jnp.concatenate([onehot(lane == picks), onehot(lane + LANES == picks)], 1)
+            picked = onehot(iota((2 * SK, SK), 0) == upper_ref[pl.ds(row, 1), :])
             here = start + count + j
-            new = slice(here * SK, (here + 1) * SK)
-            own_a = nn(chosen, sk_a[pair, :]).astype(bf16)
-            sk_a[new, :] = own_a
-            skt_ref[:, new] = nt(skt_ref[:, pair], chosen).astype(bf16)
-            upper_tiles_ref[here - blocks] = jnp.exp2(nn(own_a, skt_ref[:, pair]))
+            keep(here, nn(sk_t[:, pair], picked))
+            upper_tiles_ref[here - blocks] = jnp.exp2(nn(sk_ref[pair, :], sk_bt[...]))
         total = total // 2
         offset = offset + total
         start, count = start + count, nodes
-    own_a = sk_a[start * SK : (start + 1) * SK, :].astype(f32)
-    exact = own_a[:, :128] + pltpu.roll(own_a[:, :128], 64, 1)
-    top_ref[...] = jnp.where(lane < 64, exact, own_a[:, 128:])
+    found = sk_t[:, start * SK : (start + 1) * SK].astype(f32)
+    top_ref[0:64, :] = found[0:64] + found[64:128]
+    top_ref[64:72, :] = found[128:136]
+    top_ref[72:128, :] = jnp.zeros((56, SK), f32)
 
 
 def weights_kernel(
-    layout, where_ref, base_ref, upper_tiles_ref, top_ref, slot_ref, light_ref, w_ref, coef_ref, pack_ref, perm, feats, tall
+    layout, where_ref, base_ref, upper_tiles_ref, top_ref, slot_ref, light_ref, w_ref, coef_ref, pack_ref, masked, low_hot
 ):
     blocks, rows = layout.blocks, layout.rows
     width = light_ref.shape[1]
-    feats[...] = jnp.zeros_like(feats)
+    pack_ref[...] = top_ref[...]
+
+    def keep(node, coef):
+        coef_ref[:, aligned(node * SK, SK, SK)] = stack_two(coef)
+        pack_ref[LANES - width :, :] = coef
 
     def block(index, carry):
-        fill_perm(perm, slot_ref[pl.ds(index, 1), :])
+        low_part, high_part = parts_of(slot_ref[pl.ds(index, 1), :])
+        low_by_column(low_hot, low_part.astype(f32))
         light = [light_ref[layout.message(where_ref, g), :, layout.lanes(index)] for g in range(layout.count)]
-        feats[LANES - width :, :] = lanes_of(light).astype(bf16)
-        mine = aligned(index * rows, rows, rows)
-        tall[...] = nt(perm[...], feats[...])
-        for r in range(0, rows, 64):
-            w_ref[aligned(index * rows + r, 64, 64), :] = tall[r : r + 64, :].astype(bf16)
-        coef = nn(base_ref[index], w_ref[mine, :])
-        coef_ref[aligned(index * SK, SK, SK), :] = split_coefs(coef)
-        pack_ref[...] = coef
+        light = lanes_of(light)
+        for h in range(rows // LOW):
+            masked[h * width : (h + 1) * width, :] = jnp.where(high_part == h, light, 0.0).astype(bf16)
+        placed = nn(masked[...], low_hot[...])
+        parts = [placed[h * width : (h + 1) * width] for h in range(rows // LOW)]
+        own = jnp.concatenate(parts, 1).astype(bf16)
+        w_ref[:, aligned(index * rows, rows, rows)] = own
+        keep(index, nn(own, base_ref[index]))
         return carry
 
     lax.fori_loop(0, blocks, block, 0)
@@ -296,14 +293,13 @@
         for j in range(count // 2):
             pair = slice((start + 2 * j) * SK, (start + 2 * j + 2) * SK)
             here = start + count + j
-            coef = exact_product(upper_tiles_ref[here - blocks], coef_ref[pair, :])
-            coef_ref[here * SK : (here + 1) * SK, :] = split_coefs(coef)
-            pack_ref[...] = coef
+            high, low = two(upper_tiles_ref[here - blocks])
+            coef = nn(coef_ref[:, pair], high)
+            keep(here, coef[:width] + coef[width:] + nn(coef_ref[0:width, pair], low))
         start, count = start + count, count // 2
-    pack_ref[...] = top_ref[...] + pack_ref[...]
-
-
-def near_kernel(count_ref, list_ref, a_ref, bt_ref, w_ref, acc, times, tiles, ahead, second, tile_a, tile_b):
+
+
+def near_kernel(count_ref, list_ref, a_ref, bt_ref, w_ref, acc, times, tiles, ahead):
     every = count_ref.shape[1]
 
     def tally(leaf, filled):
@@ -329,77 +325,80 @@
     half = LEAF // 2
     acc[...] = jnp.zeros_like(acc)
 
+    def target(tile, part):
+        return aligned(tiles[0, tile] * LEAF + part * half, half, half)
+
     def exponents(tile, part):
-        target = aligned(tiles[0, tile] * LEAF, LEAF, LEAF)
-        source = aligned(tiles[1, tile] * LEAF + part * half, half, half)
-        return nn(a_ref[target, :], bt_ref[:, source])
-
-    def product(tile, part, block):
-        source = aligned(tiles[1, tile] * LEAF + part * half, half, half)
-        return nn(block, w_ref[source, :])
+        source = aligned(tiles[1, tile] * LEAF, LEAF, LEAF)
+        return nn(a_ref[source, :], bt_ref[:, target(tile, part)])
+
+    def add(tile, part, block):
+        source = aligned(tiles[1, tile] * LEAF, LEAF, LEAF)
+        acc[:, target(tile, part)] += tiles[2, tile].astype(f32) * nn(w_ref[:, source], block)
 
     ahead[...] = exponents(0, 0)
 
     def step(tile, carry):
-        here = aligned(tiles[0, tile] * LEAF, LEAF, LEAF)
-        many = tiles[2, tile].astype(f32)
-        second[...] = exponents(tile, 1)
-        exp_into(tile_a, ahead)
-        first = product(tile, 0, tile_a[...])
+        block = jnp.exp2(ahead[...]).astype(bf16)
+        second = exponents(tile, 1)
+        add(tile, 0, block)
         ahead[...] = exponents(tile + 1, 0)
-        exp_into(tile_b, second)
-        acc[here, :] += many * (first + product(tile, 1, tile_b[...]))
+        add(tile, 1, jnp.exp2(second).astype(bf16))
         return carry
 
     lax.fori_loop(0, filled, step, 0)
 
 
-def far_kernel(layout, low_levels, pack_ref, slot_ref, info_ref, a_ref, skt_ref, coef_ref, near_ref, *refs):
-    out_refs, (perm, tops, coefs, scaled, wide, tile, turned) = refs[: layout.count], refs[layout.count :]
+def far_kernel(layout, low_levels, pack_ref, slot_ref, info_ref, bt_ref, sk_ref, coef_ref, near_ref, *refs):
+    out_refs, (tops, coefs, low_hot) = refs[: layout.count], refs[layout.count :]
     blocks, rows = layout.blocks, layout.rows
     ups, width = pack_ref.shape[0], out_refs[0].shape[0]
     levels = low_levels + ups
-    lane = iota((SK, LANES), 1)
+    lane = iota((1, SK), 1)
     for up in range(ups):
         pack = pack_ref[up]
-        high, low = two(jnp.where(lane < 64, pack, 0.0))
-        high, low = high.astype(f32), low.astype(f32)
-        is_norm = (lane >= 64) & (lane < 67)
-        norms = pltpu.roll(jnp.where(is_norm, pack, 0.0), 3, 1)
+        high, low = two(pack[0:64])
+        sub = iota((8, SK), 0)
+        extra = jnp.where(sub == 0, pack[67:68], jnp.where(sub == 1, pack[68:69], pack[69:70]))
+        extra = jnp.where(sub < 3, extra, jnp.where(sub < 6, 1.0, 0.0))
         at = slice((low_levels + up) * SK, (low_levels + up + 1) * SK)
-        tops[0:128, at] = jnp.transpose(high + pltpu.roll(high, 64, 1)).astype(bf16)
-        tops[128:256, at] = jnp.transpose(jnp.where(is_norm, 1.0, low + norms)).astype(bf16)
-        coefs[at, :] = split_coefs(jnp.where(lane >= LANES - width, pack, 0.0))
+        tops[at, 0:128], tops[at, 128:256] = feature_rows(high.astype(f32), low.astype(f32), extra)
+        coefs[:, at] = stack_two(pack[LANES - width :])
 
     def block(index, carry):
         node, start, count = index, 0, blocks
         for level in range(low_levels):
             at = slice(level * SK, (level + 1) * SK)
             other = aligned((start + (node ^ 1)) * SK, SK, SK)
-            tops[:, at] = skt_ref[:, other]
-            coefs[at, :] = coef_ref[other, :]
+            tops[at, :] = sk_ref[other, :]
+            coefs[:, at] = coef_ref[:, other]
             node, start, count = node // 2, start + count, count // 2
-        fill_perm(perm, slot_ref[pl.ds(index, 1), :])
+        low_part, high_part = parts_of(slot_ref[pl.ds(index, 1), :])
+        for c in range(rows // LANES):
+            at = slice(c * LANES, (c + 1) * LANES)
+            low_hot[:, at] = onehot(iota((LOW, LANES), 0) == low_part[:, at])
         info = info_ref[index]
+        totals = []
         for leaf in range(rows // LEAF):
             flags = info[FLAGS + leaf : FLAGS + leaf + 1]
+            used = []
             for level in range(levels):
-                at = slice(level * SK, (level + 1) * SK)
-                flag = jnp.sum(jnp.where(lane[0:1] == level, flags, 0.0), axis=1, keepdims=True)
-                scaled[at, :] = (coefs[at, :].astype(f32) * flag).astype(bf16)
+                flag = jnp.sum(jnp.where(lane == level, flags, 0.0), axis=1, keepdims=True)
+                used.append(jnp.broadcast_to(flag, (1, SK)))
             here = aligned(index * rows + leaf * LEAF, LEAF, LEAF)
-            wide[...] = nn(a_ref[here, :], tops[...])
-            exp_into(tile, wide)
-            wide[:, 0 : 2 * LANES] = nn(tile[...], scaled[...])
-            for r in range(0, LEAF, LANES):
-                near = near_ref[aligned(index * rows + leaf * LEAF + r, LANES, LANES), :]
-                near = near + wide[r : r + LANES, 0:LANES] + wide[r : r + LANES, LANES : 2 * LANES]
-                turned[:, leaf * LEAF + r : leaf * LEAF + r + LANES] = jnp.transpose(near)[LANES - width :]
-        high, low = two(turned[...])
-        moved = nn(jnp.concatenate([high, low], 0), perm[...])
-        moved = moved[:width] + moved[width:]
+            tile = jnp.exp2(nn(tops[...], bt_ref[:, here])).astype(bf16)
+            scaled = (coefs[...].astype(f32) * jnp.concatenate(used, 1)).astype(bf16)
+            far = nn(scaled, tile)
+            totals.append(near_ref[:, here] + far[:width] + far[width:])
+        both = stack_two(jnp.concatenate(totals, 1))
+        parts = [both[:, h * LOW : (h + 1) * LOW] for h in range(rows // LOW)]
+        moved = nn(jnp.concatenate(parts, 0), low_hot[...])
+        result = jnp.zeros((2 * width, rows), f32)
+        for h in range(rows // LOW):
+            result = jnp.where(high_part == h, moved[h * 2 * width : (h + 1) * 2 * width], result)
+        result = result[:width] + result[width:]
         for g, out_ref in enumerate(out_refs):
-            out_ref[:, layout.lanes(index)] = moved[:, g * layout.per : (g + 1) * layout.per]
+            out_ref[:, layout.lanes(index)] = result[:, g * layout.per : (g + 1) * layout.per]
         return carry
 
     lax.fori_loop(0, blocks, block, 0)
@@ -431,9 +430,9 @@
     devices = trees * blocks
     level = blocks.bit_length() - 1
     offset = sum(devices >> step for step in range(1, level + 1))
-    lanes = jnp.arange(LANES)[None]
-    is_point, is_norm = lanes < DIM, (lanes >= DIM) & (lanes < DIM + 3)
-    is_coef = lanes >= LANES - width
+    line = jnp.arange(LANES)[:, None]
+    is_point, is_norm = line < DIM, (line >= DIM + 3) & (line < DIM + 6)
+    is_coef = line >= LANES - width
     packs, own, stride = [], pack, 1
     while stride < trees:
         other = lax.ppermute(own, "leaf", [(i, i ^ stride) for i in range(trees)])
@@ -441,17 +440,17 @@
         stride *= 2
         if stride < trees:
             second = (my_leaf // (stride // 2)) % 2 == 1
-            pair = jnp.where(second, jnp.concatenate([other, own], 0), jnp.concatenate([own, other], 0))
-            chosen = pair[skeleton_upper[offset + my_leaf // stride]]
+            pair = jnp.where(second, jnp.concatenate([other, own], 1), jnp.concatenate([own, other], 1))
+            chosen = pair[:, skeleton_upper[offset + my_leaf // stride]]
             level += 1
             offset += devices >> level
-            norms = jnp.sum(jnp.where(is_norm, pair, 0.0), axis=1)
-            chosen_norms = jnp.sum(jnp.where(is_norm, chosen, 0.0), axis=1)
+            norms = jnp.sum(jnp.where(is_norm, pair, 0.0), axis=0)
+            chosen_norms = jnp.sum(jnp.where(is_norm, chosen, 0.0), axis=0)
             inner = jnp.dot(
-                jnp.where(is_point, chosen, 0.0), jnp.where(is_point, pair, 0.0).T, precision=highest
+                jnp.where(is_point, pair, 0.0).T, jnp.where(is_point, chosen, 0.0), precision=highest
             )
-            tile = jnp.exp2(inner + norms[None] + chosen_norms[:, None])
-            own = jnp.where(is_coef, jnp.dot(tile, pair, precision=highest), chosen)
+            tile = jnp.exp2(inner + norms[:, None] + chosen_norms[None])
+            own = jnp.where(is_coef, jnp.dot(pair, tile, precision=highest), chosen)
     return jnp.stack(packs)
 
 
@@ -540,9 +539,9 @@
         out_shape=(
             shaped((total, FEAT), bf16),
             shaped((FEAT, total), bf16),
-            shaped((FEAT, nodes * SK), bf16),
-            shaped((blocks, SK, rows), bf16),
-            shaped((blocks - 1, SK, 2 * SK), f32),
+            shaped((nodes * SK, FEAT), bf16),
+            shaped((blocks, rows, SK), bf16),
+            shaped((blocks - 1, 2 * SK, SK), f32),
             shaped((SK, LANES), f32),
             shaped((blocks, rows), f32),
             shaped((blocks, 8, SK), f32),
@@ -550,11 +549,11 @@
         in_specs=[spec(SMEM)] + [spec()] * (2 + layout.count),
         out_specs=(spec(),) * 8,
         scratch_shapes=[
-            vm((rows, rows), bf16),
-            vm((2 * FEAT, rows), bf16),
-            vm((nodes * SK, FEAT), bf16),
-            vm((FEAT, rows), f32),
-            vm((rows, FEAT), f32),
+            vm((rows // LOW * COORD, rows), bf16),
+            vm((rows, LOW), bf16),
+            vm((COORD, rows), bf16),
+            vm((COORD, nodes * SK), bf16),
+            vm((FEAT, SK), bf16),
         ],
         compiler_params=params(),
         name="tree_points",
@@ -563,13 +562,13 @@
     tree_light, coefs, pack = pl.pallas_call(
         functools.partial(weights_kernel, layout),
         out_shape=(
-            shaped((total, LANES), bf16),
-            shaped((nodes * SK, FEAT), bf16),
-            shaped((SK, LANES), f32),
+            shaped((width, total), bf16),
+            shaped((2 * width, nodes * SK), bf16),
+            shaped((LANES, SK), f32),
         ),
         in_specs=[spec(SMEM)] + [spec()] * 5,
         out_specs=(spec(),) * 3,
-        scratch_shapes=[vm((rows, rows), bf16), vm((LANES, rows), bf16), vm((rows, LANES), f32)],
+        scratch_shapes=[vm((rows // LOW * width, rows), bf16), vm((rows, LOW), bf16)],
         compiler_params=params(),
         name="tree_weights",
     )(where, base, upper_tiles, top, slots, light)
@@ -578,16 +577,13 @@
 
     near = pl.pallas_call(
         near_kernel,
-        out_shape=shaped((total, LANES), f32),
+        out_shape=shaped((width, total), f32),
         in_specs=[spec(SMEM)] * 2 + [spec()] * 3,
         out_specs=spec(),
         scratch_shapes=[
             pltpu.SMEM((leaves,), jnp.int32),
             pltpu.SMEM((3, leaves * leaves + 1), jnp.int32),
             vm((LEAF, LEAF // 2), f32),
-            vm((LEAF, LEAF // 2), f32),
-            vm((LEAF, LEAF // 2), bf16),
-            vm((LEAF, LEAF // 2), bf16),
         ],
         compiler_params=params(),
         name="near",
@@ -599,18 +595,10 @@
         out_shape=(arrive,) * layout.count,
         in_specs=[spec()] * 7,
         out_specs=(spec(),) * layout.count,
-        scratch_shapes=[
-            vm((rows, rows), bf16),
-            vm((FEAT, levels * SK), bf16),
-            vm((levels * SK, FEAT), bf16),
-            vm((levels * SK, FEAT), bf16),
-            vm((LEAF, levels * SK), f32),
-            vm((LEAF, levels * SK), bf16),
-            vm((width, rows), f32),
-        ],
+        scratch_shapes=[vm((levels * SK, FEAT), bf16), vm((2 * width, levels * SK), bf16), vm((LOW, rows), bf16)],
         compiler_params=params(),
         name="far",
-    )(packs, slots, info, feat_a, sk, coefs, near)
+    )(packs, slots, info, feat_bt, sk, coefs, near)
 
     if fine:
         back = swap_all(back)

time: 112 us -> 94.5 us (0.84)
  Pallas kernels: 60.5 us -> 43.5 us
  starting transfers between devices: 32.4 us -> 31.2 us
    pallas_call x1, Pallas kernels: 9.47 us -> 4.78 us  [body(): pl.pallas_call(functools.partial(weights_kernel, layout), out_shape=(shap...]
    pallas_call x1, Pallas kernels: 11.4 us -> 6.67 us  [body(): pl.pallas_call(functools.partial(far_kernel, layout, low_levels), out_sha...]
    pallas_call x1, Pallas kernels: 13.5 us -> 8.88 us  [body(): pl.pallas_call(functools.partial(points_kernel, layout, trees), out_shape...]
    pallas_call x1, Pallas kernels: 19.3 us -> 16.3 us  [body(): pl.pallas_call(near_kernel, out_shape=shaped((width, total), f32), in_spe...]
    all_to_all x1, waiting for transfers between devices: 0.01 us -> 2.4 us  [body(): lax.all_to_all(light, ('leaf', 'sub'), split_axis=0, concat_axis=0, tiled...]
    ppermute x9, waiting for transfers between devices: 6.27 us -> 3.93 us  [swap(): return lax.ppermute(value, axes, pairs)]
    ppermute x1, starting transfers between devices: 1.74 us -> 0.56 us  [upper_levels(): other = lax.ppermute(own, 'leaf', [(i, i ^ stride) for i in range(trees)])]
  transfers between devices with their start and end apart: 18 -> 18, of which waited for: 9 -> 9; matrix products, arithmetic and copies ran while one was open for 1% -> 1% of each run, Pallas kernels for 29% -> 27%
where the time goes in v5:
time: 94.5 us; the launch traced here: 93.9 us
  Pallas kernels  43.5 us (46%)
  starting transfers between devices  31.2 us (33%)
  waiting for transfers between devices  15.7 us (17%)
  local copies, waits for them, and re-layouts  2.67 us (3%)
    pallas_call x1, Pallas kernels, body(): pl.pallas_call(near_kernel, out_shape=shaped((width, total), f32), in_spe...  16.3 us
    ppermute x9, starting transfers between devices, swap(): return lax.ppermute(value, axes, pairs)  16.1 us
    pallas_call x1, Pallas kernels, body(): pl.pallas_call(functools.partial(points_kernel, layout, trees), out_shape...  8.88 us
    ppermute x3, waiting for transfers between devices, body(): lax.ppermute(place[step], 'sub', [(i, i ^ stride) for i in range(blocks)])  8.06 us
    pallas_call x1, Pallas kernels, body(): pl.pallas_call(functools.partial(far_kernel, layout, low_levels), out_sha...  6.67 us
    ppermute x3, starting transfers between devices, body(): lax.ppermute(place[step], 'sub', [(i, i ^ stride) for i in range(blocks)])  6.51 us
    all_to_all x1, starting transfers between devices, body(): lax.all_to_all(light, ('leaf', 'sub'), split_axis=0, concat_axis=0, tiled...  5.45 us
    pallas_call x1, Pallas kernels, body(): pl.pallas_call(functools.partial(weights_kernel, layout), out_shape=(shap...  4.78 us
  transfers between devices with their start and end apart: 18, of which 9 were waited for; matrix products, arithmetic and copies ran while one was open for 1% of the time, Pallas kernels for 27%

profile of v5, /device:TPU:0, one launch (start us, length us, event | category | flops | bytes accessed | tf_op | source)
XLA Modules:
  0.0 93.9 jit_solution(6133457039833434860)
XLA Ops:
  0.7 3.7 %sort_rows.1 = (f32[72,512]{1,0:T(8,128)}, f32[8,128]{1,0:T(8,128)}, f32[2,128,512]{2,1,0:T(8,128)}) custom-call(s32[3]{0:T(128)} %pad_add_fusion.where_ref, s32[8,128]{1,0:T(8,128)} %bitcast.11, f32[64,1024]{1,0:T(8,128)} %bitcast.9, f32[1024,128]{1,0:T(8,128)} %refs_8_.1, s32[1,128]{1,0:T(1,128)} %base_ref.1, s32[2,3]{1,0:T(2,128)} %flag_ref.1), custom_call_target="tpu_custom_call" | custom-call | tf_op jit(solution)/shard_map/sort_rows/pallas_call | solution.py:475
  4.3 1.6 %collective-permute-start = (f32[72,512]{1,0:T(8,128)}, f32[72,512]{1,0:T(8,128)S(1)}, u32[]{:S(2)}, u32[]{:S(2)}) collective-permute-start(f32[72,512]{1,0:T(8,128)} %get-tuple-element.33), channel_id=1, source_target_pairs={{0,0},{1,9},{2,2},{3,11},{4,4},{5,13},{6,6},{7,15},{8,8},{9,1},{10... | collective-permute-start | bytes 442376 | tf_op jit(solution)/shard_map/ppermute | solution.py:502
  5.9 4.0 %collective-permute-start.2 = (f32[72,512]{1,0:T(8,128)S(1)}, f32[72,512]{1,0:T(8,128)S(1)}, u32[]{:S(2)}, u32[]{:S(2)}) collective-permute-start(f32[72,512]{1,0:T(8,128)S(1)} %collective-permute-done.refs_0_), channel_id=1, source_target_pairs={{0,4},{2,6},{4,0},{6,2},{1,5},{3,7},{5,1},{7,3},{8,12},{10,14},{12... | collective-permute-start | bytes 442376 | tf_op jit(solution)/shard_map/ppermute | solution.py:515
  9.9 1.6 %collective-permute-start.1 = (f32[72,512]{1,0:T(8,128)S(1)}, f32[72,512]{1,0:T(8,128)S(1)}, u32[]{:S(2)}, u32[]{:S(2)}) collective-permute-start(f32[72,512]{1,0:T(8,128)S(1)} %collective-permute-done.refs_0_), channel_id=1, source_target_pairs={{0,2},{2,0},{4,6},{6,4},{1,3},{3,1},{5,7},{7,5},{8,10},{10,8},{12,... | collective-permute-start | bytes 442376 | tf_op jit(solution)/shard_map/ppermute | solution.py:515
  11.5 3.2 %collective-permute-done.2.refs_2_ = f32[72,512]{1,0:T(8,128)S(1)} collective-permute-done((f32[72,512]{1,0:T(8,128)S(1)}, f32[72,512]{1,0:T(8,128)S(1)}, u32[]{:S(2)}, u32[]{:S(2)}) %collective-permute-start.2) | collective-permute-done | bytes 147488 | tf_op jit(solution)/shard_map/ppermute | solution.py:515
  14.8 0.9 collective-permute-start.3
  15.7 4.8 %collective-permute-done.3.refs_3_ = f32[72,512]{1,0:T(8,128)S(1)} collective-permute-done((f32[72,512]{1,0:T(8,128)S(1)}, f32[72,512]{1,0:T(8,128)S(1)}, u32[]{:S(2)}, u32[]{:S(2)}) %collective-permute-start.3) | collective-permute-done | bytes 147488 | tf_op jit(solution)/shard_map/ppermute | solution.py:515
  20.5 5.5 %all-to-all-start = ((f32[8,32,512]{2,1,0:T(8,128)}), f32[8,32,512]{2,1,0:T(8,128)S(1)}, u32[]{:S(2)}, u32[]{:S(2)}) async-start(f32[8,32,512]{2,1,0:T(8,128)} %bitcast.8), calls=%async_computation | async-start | bytes 1048576 | tf_op jit(solution)/shard_map/all_to_all | solution.py:521
  25.9 2.0 %collective-permute-start.4 = (f32[72,512]{1,0:T(8,128)S(1)}, f32[72,512]{1,0:T(8,128)S(1)}, u32[]{:S(2)}, u32[]{:S(2)}) collective-permute-start(f32[72,512]{1,0:T(8,128)S(1)} %collective-permute-done.refs_0_), channel_id=1, source_target_pairs={{0,1},{1,0},{2,3},{3,2},{4,5},{5,4},{6,7},{7,6},{8,9},{9,8},{10,11... | collective-permute-start | bytes 442376 | tf_op jit(solution)/shard_map/ppermute | solution.py:519
  30.5 8.9 %tree_points.1 = (bf16[4096,256]{1,0:T(8,128)(2,1)}, bf16[256,4096]{1,0:T(8,128)(2,1)}, bf16[896,256]{1,0:T(8,128)(2,1)}, bf16[4,1024,128]{2,1,0:T(8,128)(2,1)},...) custom-call(s32[3]{0:T(128)} %pad_add_fusion.where_ref, ...), custom_call_target="tpu_custom_call" | custom-call | tf_op jit(solution)/shard_map/tree_points/pallas_call | solution.py:537
  39.3 2.4 %all-to-all-done.light_ref = f32[8,32,512]{2,1,0:T(8,128)S(1)} async-done(((f32[8,32,512]{2,1,0:T(8,128)}), f32[8,32,512]{2,1,0:T(8,128)S(1)}, u32[]{:S(2)}, u32[]{:S(2)}) %all-to-all-start) | async-done | bytes 524320 | tf_op jit(solution)/shard_map/all_to_all | solution.py:521
  41.8 0.8 copy-done
  42.5 4.8 %tree_weights.1 = (bf16[32,4096]{1,0:T(8,128)(2,1)}, bf16[64,896]{1,0:T(8,128)(2,1)}, f32[128,128]{1,0:T(8,128)}) custom-call(s32[3]{0:T(128)} %pad_add_fusion.where_ref, bf16[4,1024,128]{2,1,0:T(8,128)(2,1)} %get-tuple-element.39.base_ref, f32[3,256,128]{2,1,0:T(8,128)} %get-tuple-element.40.upper_tiles_ref, f32[128,128]{1,0:T(8,128)} %get-tuple-element.41.top_ref, ...), custom_call_target="tpu_custom_call" | custom-call | tf_op jit(solution)/shard_map/tree_weights/pallas_call | solution.py:562
  47.9 16.3 %near.1.near_ref = f32[32,4096]{1,0:T(8,128)} custom-call(s32[1,8]{1,0:T(1,128)} %count_ref.1, s32[8,16]{1,0:T(8,128)} %bitcast.12, bf16[4096,256]{1,0:T(8,128)(2,1)} %get-tuple-element.49.a_ref, bf16[256,4096]{1,0:T(8,128)(2,1)} %get-tuple-element.46.bt_ref, bf16[32,4096]{1,0:T(8,128)(2,1)} %get-tuple-element.50.w_ref), custom_call_target="tpu_custom_call" | custom-call | tf_op jit(solution)/shard_map/near/pallas_call | solution.py:578
  64.8 6.7 %far.1 = (f32[32,512]{1,0:T(8,128)}, f32[32,512]{1,0:T(8,128)}, f32[32,512]{1,0:T(8,128)}, f32[32,512]{1,0:T(8,128)}, f32[32,512]{1,0:T(8,128)}, /*index=5*/f32[...) custom-call(f32[1,128,128]{2,1,0:T(8,128)} %bitcast.10, f32[4,1024]{1,0:T(4,128)} %get-tuple-element.42.slot_ref, ...), custom_call_target="tpu_custom_call" | custom-call | tf_op jit(solution)/shard_map/far/pallas_call | solution.py:593
  71.5 1.5 %collective-permute-start.9 = (f32[32,512]{1,0:T(8,128)}, f32[32,512]{1,0:T(8,128)S(1)}, u32[]{:S(2)}, u32[]{:S(2)}) collective-permute-start(f32[32,512]{1,0:T(8,128)} %get-tuple-element.51), channel_id=1, source_target_pairs={{0,0},{1,9},{2,2},{3,11},{4,4},{5,13},{6,6},{7,15},{8,8},{9,1},{10... | collective-permute-start | bytes 196616 | tf_op jit(solution)/shard_map/ppermute | solution.py:502
  73.2 2.4 %collective-permute-start.11 = (f32[32,512]{1,0:T(8,128)}, f32[32,512]{1,0:T(8,128)S(1)}, u32[]{:S(2)}, u32[]{:S(2)}) collective-permute-start(f32[32,512]{1,0:T(8,128)} %get-tuple-element.53), channel_id=1, source_target_pairs={{0,4},{1,13},{2,6},{3,15},{4,0},{5,9},{6,2},{7,11},{8,12},{9,5},{1... | collective-permute-start | bytes 196616 | tf_op jit(solution)/shard_map/ppermute | solution.py:502
  75.6 1.8 %collective-permute-start.12 = (f32[32,512]{1,0:T(8,128)}, f32[32,512]{1,0:T(8,128)S(1)}, u32[]{:S(2)}, u32[]{:S(2)}) collective-permute-start(f32[32,512]{1,0:T(8,128)} %get-tuple-element.54), channel_id=1, source_target_pairs={{0,6},{1,15},{2,4},{3,13},{4,2},{5,11},{6,0},{7,9},{8,14},{9,7},{1... | collective-permute-start | bytes 196616 | tf_op jit(solution)/shard_map/ppermute | solution.py:502
  77.4 2.1 %collective-permute-start.13 = (f32[32,512]{1,0:T(8,128)}, f32[32,512]{1,0:T(8,128)S(1)}, u32[]{:S(2)}, u32[]{:S(2)}) collective-permute-start(f32[32,512]{1,0:T(8,128)} %get-tuple-element.55), channel_id=1, source_target_pairs={{0,8},{1,1},{2,10},{3,3},{4,12},{5,5},{6,14},{7,7},{8,0},{9,9},{10... | collective-permute-start | bytes 196616 | tf_op jit(solution)/shard_map/ppermute | solution.py:502
  80.2 2.7 %collective-permute-start.15 = (f32[32,512]{1,0:T(8,128)}, f32[32,512]{1,0:T(8,128)S(1)}, u32[]{:S(2)}, u32[]{:S(2)}) collective-permute-start(f32[32,512]{1,0:T(8,128)} %get-tuple-element.57), channel_id=1, source_target_pairs={{0,12},{1,5},{2,14},{3,7},{4,8},{5,1},{6,10},{7,3},{8,4},{9,13},{1... | collective-permute-start | bytes 196616 | tf_op jit(solution)/shard_map/ppermute | solution.py:502
  82.9 3.2 %collective-permute-start.16 = (f32[32,512]{1,0:T(8,128)}, f32[32,512]{1,0:T(8,128)S(1)}, u32[]{:S(2)}, u32[]{:S(2)}) collective-permute-start(f32[32,512]{1,0:T(8,128)} %get-tuple-element.58), channel_id=1, source_target_pairs={{0,14},{1,7},{2,12},{3,5},{4,10},{5,3},{6,8},{7,1},{8,6},{9,15},{1... | collective-permute-start | bytes 196616 | tf_op jit(solution)/shard_map/ppermute | solution.py:502
  86.2 1.3 %collective-permute-done.15.refs_6_ = f32[32,512]{1,0:T(8,128)S(1)} collective-permute-done((f32[32,512]{1,0:T(8,128)}, f32[32,512]{1,0:T(8,128)S(1)}, u32[]{:S(2)}, u32[]{:S(2)}) %collective-permute-start.15) | collective-permute-done | bytes 65568 | tf_op jit(solution)/shard_map/ppermute | solution.py:502
  87.4 2.6 %collective-permute-done.16.refs_7_ = f32[32,512]{1,0:T(8,128)S(1)} collective-permute-done((f32[32,512]{1,0:T(8,128)}, f32[32,512]{1,0:T(8,128)S(1)}, u32[]{:S(2)}, u32[]{:S(2)}) %collective-permute-start.16) | collective-permute-done | bytes 65568 | tf_op jit(solution)/shard_map/ppermute | solution.py:502
  90.7 3.2 %to_input_order.1 = f32[1024,128]{1,0:T(8,128)} custom-call(s32[3]{0:T(128)} %pad_add_fusion.where_ref, f32[8,128]{1,0:T(8,128)} %get-tuple-element.32.pos_ref, f32[32,512]{1,0:T(8,128)} %copy-done.9, f32[32,512]{1,0:T(8,128)} %copy-done.10, f32[32,512]{1,0:T(8,128)} %copy-done.11, f32[32,512]{1,0:T(8,128)} %copy-done.12, f32[32,512]{1,0:T(8,128)} %copy-done.13, ...), custom_call_target="tpu_custom_call" | custom-call | tf_op jit(solution)/shard_map/to_input_order/pallas_call | solution.py:610
  (56 shorter events, 6.0 us)
Async XLA Ops:
  4.3 1.6 %collective-permute-start = (f32[72,512]{1,0:T(8,128)}, f32[72,512]{1,0:T(8,128)S(1)}, u32[]{:S(2)}, u32[]{:S(2)}) collective-permute-start(f32[72,512]{1,0:T(8,128)} %get-tuple-element.33), channel_id=1, source_target_pairs={{0,0},{1,9},{2,2},{3,11},{4,4},{5,13},{6,6},{7,15},{8,8},{9,1},{10... | collective-permute-start | bytes 442376 | tf_op jit(solution)/shard_map/ppermute | solution.py:502
  5.9 24.5 %copy-start.1 = (f32[72,512]{1,0:T(8,128)}, f32[72,512]{1,0:T(8,128)S(1)}, u32[]{:S(2)}) copy-start(f32[72,512]{1,0:T(8,128)S(1)} %collective-permute-done.refs_0_) | copy-start | bytes 442372
  5.9 8.8 %collective-permute-start.2 = (f32[72,512]{1,0:T(8,128)S(1)}, f32[72,512]{1,0:T(8,128)S(1)}, u32[]{:S(2)}, u32[]{:S(2)}) collective-permute-start(f32[72,512]{1,0:T(8,128)S(1)} %collective-permute-done.refs_0_), channel_id=1, source_target_pairs={{0,4},{2,6},{4,0},{6,2},{1,5},{3,7},{5,1},{7,3},{8,12},{10,14},{12... | collective-permute-start | bytes 442376 | tf_op jit(solution)/shard_map/ppermute | solution.py:515
  9.9 5.7 %collective-permute-start.1 = (f32[72,512]{1,0:T(8,128)S(1)}, f32[72,512]{1,0:T(8,128)S(1)}, u32[]{:S(2)}, u32[]{:S(2)}) collective-permute-start(f32[72,512]{1,0:T(8,128)S(1)} %collective-permute-done.refs_0_), channel_id=1, source_target_pairs={{0,2},{2,0},{4,6},{6,4},{1,3},{3,1},{5,7},{7,5},{8,10},{10,8},{12,... | collective-permute-start | bytes 442376 | tf_op jit(solution)/shard_map/ppermute | solution.py:515
  14.8 15.7 %copy-start.2 = (f32[72,512]{1,0:T(8,128)}, f32[72,512]{1,0:T(8,128)S(1)}, u32[]{:S(2)}) copy-start(f32[72,512]{1,0:T(8,128)S(1)} %collective-permute-done.2.refs_2_) | copy-start | bytes 442372
  14.8 5.7 %collective-permute-start.3 = (f32[72,512]{1,0:T(8,128)S(1)}, f32[72,512]{1,0:T(8,128)S(1)}, u32[]{:S(2)}, u32[]{:S(2)}) collective-permute-start(f32[72,512]{1,0:T(8,128)S(1)} %collective-permute-done.2.refs_2_), channel_id=1, source_target_pairs={{0,2},{2,0},{4,6},{6,4},{1,3},{3,1},{5,7},{7,5},{8,10},{10,8},{12,... | collective-permute-start | bytes 442376 | tf_op jit(solution)/shard_map/ppermute | solution.py:515
  15.7 14.8 %copy-start.3 = (f32[72,512]{1,0:T(8,128)}, f32[72,512]{1,0:T(8,128)S(1)}, u32[]{:S(2)}) copy-start(f32[72,512]{1,0:T(8,128)S(1)} %collective-permute-done.1.refs_1_) | copy-start | bytes 442372
  20.5 9.9 %copy-start.4 = (f32[72,512]{1,0:T(8,128)}, f32[72,512]{1,0:T(8,128)S(1)}, u32[]{:S(2)}) copy-start(f32[72,512]{1,0:T(8,128)S(1)} %collective-permute-done.3.refs_3_) | copy-start | bytes 442372
  20.5 21.3 %all-to-all-start = ((f32[8,32,512]{2,1,0:T(8,128)}), f32[8,32,512]{2,1,0:T(8,128)S(1)}, u32[]{:S(2)}, u32[]{:S(2)}) async-start(f32[8,32,512]{2,1,0:T(8,128)} %bitcast.8), calls=%async_computation | async-start | bytes 1048576 | tf_op jit(solution)/shard_map/all_to_all | solution.py:521
  25.9 3.0 %collective-permute-start.4 = (f32[72,512]{1,0:T(8,128)S(1)}, f32[72,512]{1,0:T(8,128)S(1)}, u32[]{:S(2)}, u32[]{:S(2)}) collective-permute-start(f32[72,512]{1,0:T(8,128)S(1)} %collective-permute-done.refs_0_), channel_id=1, source_target_pairs={{0,1},{1,0},{2,3},{3,2},{4,5},{5,4},{6,7},{7,6},{8,9},{9,8},{10,11... | collective-permute-start | bytes 442376 | tf_op jit(solution)/shard_map/ppermute | solution.py:519
  27.9 1.4 %collective-permute-start.5 = (f32[72,512]{1,0:T(8,128)S(1)}, f32[72,512]{1,0:T(8,128)S(1)}, u32[]{:S(2)}, u32[]{:S(2)}) collective-permute-start(f32[72,512]{1,0:T(8,128)S(1)} %collective-permute-done.1.refs_1_), channel_id=1, source_target_pairs={{0,1},{1,0},{2,3},{3,2},{4,5},{5,4},{6,7},{7,6},{8,9},{9,8},{10,11... | collective-permute-start | bytes 442376 | tf_op jit(solution)/shard_map/ppermute | solution.py:519
  28.0 1.5 %collective-permute-start.6 = (f32[72,512]{1,0:T(8,128)S(1)}, f32[72,512]{1,0:T(8,128)S(1)}, u32[]{:S(2)}, u32[]{:S(2)}) collective-permute-start(f32[72,512]{1,0:T(8,128)S(1)} %collective-permute-done.2.refs_2_), channel_id=1, source_target_pairs={{0,1},{1,0},{2,3},{3,2},{4,5},{5,4},{6,7},{7,6},{8,9},{9,8},{10,11... | collective-permute-start | bytes 442376 | tf_op jit(solution)/shard_map/ppermute | solution.py:519
  28.4 1.4 %collective-permute-start.7 = (f32[72,512]{1,0:T(8,128)S(1)}, f32[72,512]{1,0:T(8,128)S(1)}, u32[]{:S(2)}, u32[]{:S(2)}) collective-permute-start(f32[72,512]{1,0:T(8,128)S(1)} %collective-permute-done.3.refs_3_), channel_id=1, source_target_pairs={{0,1},{1,0},{2,3},{3,2},{4,5},{5,4},{6,7},{7,6},{8,9},{9,8},{10,11... | collective-permute-start | bytes 442376 | tf_op jit(solution)/shard_map/ppermute | solution.py:519
  47.3 16.9 %collective-permute-start.8 = (f32[128,128]{1,0:T(8,128)}, f32[128,128]{1,0:T(8,128)S(1)}, u32[]{:S(2)}, u32[]{:S(2)}) collective-permute-start(f32[128,128]{1,0:T(8,128)} %get-tuple-element.44), channel_id=1, source_target_pairs={{0,8},{8,0},{1,9},{9,1},{2,10},{10,2},{3,11},{11,3},{4,12},{12,4},... | collective-permute-start | bytes 196616 | tf_op jit(solution)/shard_map/ppermute | solution.py:438
  71.5 8.0 %collective-permute-start.9 = (f32[32,512]{1,0:T(8,128)}, f32[32,512]{1,0:T(8,128)S(1)}, u32[]{:S(2)}, u32[]{:S(2)}) collective-permute-start(f32[32,512]{1,0:T(8,128)} %get-tuple-element.51), channel_id=1, source_target_pairs={{0,0},{1,9},{2,2},{3,11},{4,4},{5,13},{6,6},{7,15},{8,8},{9,1},{10... | collective-permute-start | bytes 196616 | tf_op jit(solution)/shard_map/ppermute | solution.py:502
  73.0 7.2 %collective-permute-start.10 = (f32[32,512]{1,0:T(8,128)}, f32[32,512]{1,0:T(8,128)S(1)}, u32[]{:S(2)}, u32[]{:S(2)}) collective-permute-start(f32[32,512]{1,0:T(8,128)} %get-tuple-element.52), channel_id=1, source_target_pairs={{0,2},{1,11},{2,0},{3,9},{4,6},{5,15},{6,4},{7,13},{8,10},{9,3},{1... | collective-permute-start | bytes 196616 | tf_op jit(solution)/shard_map/ppermute | solution.py:502
  73.2 9.7 %collective-permute-start.11 = (f32[32,512]{1,0:T(8,128)}, f32[32,512]{1,0:T(8,128)S(1)}, u32[]{:S(2)}, u32[]{:S(2)}) collective-permute-start(f32[32,512]{1,0:T(8,128)} %get-tuple-element.53), channel_id=1, source_target_pairs={{0,4},{1,13},{2,6},{3,15},{4,0},{5,9},{6,2},{7,11},{8,12},{9,5},{1... | collective-permute-start | bytes 196616 | tf_op jit(solution)/shard_map/ppermute | solution.py:502
  75.6 10.5 %collective-permute-start.12 = (f32[32,512]{1,0:T(8,128)}, f32[32,512]{1,0:T(8,128)S(1)}, u32[]{:S(2)}, u32[]{:S(2)}) collective-permute-start(f32[32,512]{1,0:T(8,128)} %get-tuple-element.54), channel_id=1, source_target_pairs={{0,6},{1,15},{2,4},{3,13},{4,2},{5,11},{6,0},{7,9},{8,14},{9,7},{1... | collective-permute-start | bytes 196616 | tf_op jit(solution)/shard_map/ppermute | solution.py:502
  77.4 8.8 %collective-permute-start.13 = (f32[32,512]{1,0:T(8,128)}, f32[32,512]{1,0:T(8,128)S(1)}, u32[]{:S(2)}, u32[]{:S(2)}) collective-permute-start(f32[32,512]{1,0:T(8,128)} %get-tuple-element.55), channel_id=1, source_target_pairs={{0,8},{1,1},{2,10},{3,3},{4,12},{5,5},{6,14},{7,7},{8,0},{9,9},{10... | collective-permute-start | bytes 196616 | tf_op jit(solution)/shard_map/ppermute | solution.py:502
  79.4 10.6 %copy-start.9 = (f32[32,512]{1,0:T(8,128)}, f32[32,512]{1,0:T(8,128)S(1)}, u32[]{:S(2)}) copy-start(f32[32,512]{1,0:T(8,128)S(1)} %collective-permute-done.9.refs_0_) | copy-start | bytes 196612
  79.5 6.7 %collective-permute-start.14 = (f32[32,512]{1,0:T(8,128)}, f32[32,512]{1,0:T(8,128)S(1)}, u32[]{:S(2)}, u32[]{:S(2)}) collective-permute-start(f32[32,512]{1,0:T(8,128)} %get-tuple-element.56), channel_id=1, source_target_pairs={{0,10},{1,3},{2,8},{3,1},{4,14},{5,7},{6,12},{7,5},{8,2},{9,11},{1... | collective-permute-start | bytes 196616 | tf_op jit(solution)/shard_map/ppermute | solution.py:502
  80.2 9.9 %copy-start.10 = (f32[32,512]{1,0:T(8,128)}, f32[32,512]{1,0:T(8,128)S(1)}, u32[]{:S(2)}) copy-start(f32[32,512]{1,0:T(8,128)S(1)} %collective-permute-done.10.refs_1_) | copy-start | bytes 196612
  80.2 7.3 %collective-permute-start.15 = (f32[32,512]{1,0:T(8,128)}, f32[32,512]{1,0:T(8,128)S(1)}, u32[]{:S(2)}, u32[]{:S(2)}) collective-permute-start(f32[32,512]{1,0:T(8,128)} %get-tuple-element.57), channel_id=1, source_target_pairs={{0,12},{1,5},{2,14},{3,7},{4,8},{5,1},{6,10},{7,3},{8,4},{9,13},{1... | collective-permute-start | bytes 196616 | tf_op jit(solution)/shard_map/ppermute | solution.py:502
  82.9 7.2 %collective-permute-start.16 = (f32[32,512]{1,0:T(8,128)}, f32[32,512]{1,0:T(8,128)S(1)}, u32[]{:S(2)}, u32[]{:S(2)}) collective-permute-start(f32[32,512]{1,0:T(8,128)} %get-tuple-element.58), channel_id=1, source_target_pairs={{0,14},{1,7},{2,12},{3,5},{4,10},{5,3},{6,8},{7,1},{8,6},{9,15},{1... | collective-permute-start | bytes 196616 | tf_op jit(solution)/shard_map/ppermute | solution.py:502
  (12 other events, 28.1 us)

commit v6 on v5

--- a/solution.py
+++ b/solution.py
@@ -1,5 +1,4 @@
 import functools
-import math
 
 import jax
 import jax.numpy as jnp
@@ -17,7 +16,7 @@
 COORD = 144
 
 highest = lax.Precision.HIGHEST
-point_scale = math.sqrt(2.0 * math.log2(math.e) / 32.0)
+point_scale = 0.25
 ridge = 0.5
 PLACE_ROWS = 72
 TAIL = 64
@@ -32,8 +31,12 @@
     return pl.BlockSpec(memory_space=space)
 
 
-def params():
-    return pltpu.CompilerParams(vmem_limit_bytes=58 * 1024 * 1024)
+def params(mib=58):
+    return pltpu.CompilerParams(vmem_limit_bytes=mib * 1024 * 1024)
+
+
+def held(array):
+    return pltpu.with_memory_space_constraint(array, VMEM)
 
 
 def vm(shape, dtype):
@@ -95,7 +98,7 @@
 
 
 def sort_kernel(
-    fine, where_ref, slot_ref, points_ref, weights_ref, base_ref, flag_ref, place_ref, pos_ref, light_ref, perm, vals, whole
+    fine, slot_ref, points_ref, weights_ref, base_ref, flag_ref, place_ref, pos_ref, light_ref, perm, vals, whole
 ):
     chunks, split = slot_ref.shape[0], light_ref.shape[-1]
     rows = chunks * LANES
@@ -138,7 +141,7 @@
     if not fine:
         place_ref[...] = whole[0]
         return
-    place_ref[...] = whole[where_ref[0] ^ where_ref[2]]
+    place_ref[...] = whole[lax.axis_index("leaf") ^ lax.axis_index("rep")]
     place_ref[TAIL + BASE : TAIL + BASE + 1, 0:SK] = base_ref[...].astype(f32)
     place_ref[TAIL + FLAGS : TAIL + FLAGS + flag_ref.shape[0], 0 : flag_ref.shape[1]] = flag_ref[...].astype(f32)
 
@@ -152,24 +155,24 @@
     def lanes(self, index):
         return aligned(index * self.per, self.per, LANES)
 
-    def message(self, where_ref, group):
+    def message(self, group):
         if not self.fine:
             return 0
-        leaf = where_ref[0] ^ where_ref[2] ^ (group // self.blocks)
-        return leaf * self.blocks + (where_ref[1] ^ (group % self.blocks))
+        leaf = lax.axis_index("leaf") ^ lax.axis_index("rep") ^ (group // self.blocks)
+        return leaf * self.blocks + (lax.axis_index("sub") ^ (group % self.blocks))
 
     def gather(self, refs, index, part):
         return lanes_of([ref[part, self.lanes(index)] for ref in refs])
 
-    def info(self, where_ref, refs, small_ref, index):
+    def info(self, refs, small_ref, index):
         if not self.fine:
             return small_ref[index]
-        core = where_ref[2]
+        core = lax.axis_index("rep")
         found = jnp.zeros((PLACE_ROWS - TAIL, SK), f32)
         for step in range(self.blocks):
             mine, theirs = refs[step][TAIL:, 0:SK], refs[self.blocks + step][TAIL:, 0:SK]
             here = jnp.where(core == 0, mine, theirs)
-            found = jnp.where((where_ref[1] ^ step) == index, here, found)
+            found = jnp.where((lax.axis_index("sub") ^ step) == index, here, found)
         return found
 
 
@@ -197,7 +200,7 @@
     return first.astype(bf16), second.astype(bf16)
 
 
-def points_kernel(layout, trees, where_ref, upper_ref, small_ref, *refs):
+def points_kernel(layout, trees, upper_ref, small_ref, *refs):
     place_refs, refs = refs[: layout.count], refs[layout.count :]
     a_ref, bt_ref, sk_ref, base_ref, upper_tiles_ref, top_ref, slot_ref, info_ref, masked, low_hot, tree, sk_t, sk_bt = refs
     blocks, rows = layout.blocks, layout.rows
@@ -212,7 +215,7 @@
         tail = layout.gather(place_refs, index, slice(TAIL, PLACE_ROWS))
         slots = tail[SLOT : SLOT + 1]
         slot_ref[pl.ds(index, 1), :] = slots
-        info = layout.info(where_ref, place_refs, small_ref, index)
+        info = layout.info(place_refs, small_ref, index)
         info_ref[index] = info
         points = layout.gather(place_refs, index, slice(0, TAIL))
         high, low = two(points)
@@ -239,7 +242,7 @@
         picked = onehot(iota((rows, SK), 0) == info[BASE : BASE + 1].astype(jnp.int32))
         keep(index, nn(tree[...], picked))
         mine = aligned(index * rows, rows, rows)
-        base_ref[index] = jnp.exp2(nn(a_ref[mine, :], sk_bt[...])).astype(bf16)
+        base_ref[index] = jnp.exp(nn(a_ref[mine, :], sk_bt[...])).astype(bf16)
         return carry
 
     lax.fori_loop(0, blocks, block, 0)
@@ -248,11 +251,11 @@
         nodes = count // 2
         for j in range(nodes):
             pair = slice((start + 2 * j) * SK, (start + 2 * j + 2) * SK)
-            row = offset + where_ref[0] * nodes + j
+            row = offset + lax.axis_index("leaf") * nodes + j
             picked = onehot(iota((2 * SK, SK), 0) == upper_ref[pl.ds(row, 1), :])
             here = start + count + j
             keep(here, nn(sk_t[:, pair], picked))
-            upper_tiles_ref[here - blocks] = jnp.exp2(nn(sk_ref[pair, :], sk_bt[...]))
+            upper_tiles_ref[here - blocks] = jnp.exp(nn(sk_ref[pair, :], sk_bt[...]))
         total = total // 2
         offset = offset + total
         start, count = start + count, nodes
@@ -263,7 +266,7 @@
 
 
 def weights_kernel(
-    layout, where_ref, base_ref, upper_tiles_ref, top_ref, slot_ref, light_ref, w_ref, coef_ref, pack_ref, masked, low_hot
+    layout, base_ref, upper_tiles_ref, top_ref, slot_ref, light_ref, w_ref, coef_ref, pack_ref, masked, low_hot
 ):
     blocks, rows = layout.blocks, layout.rows
     width = light_ref.shape[1]
@@ -276,7 +279,7 @@
     def block(index, carry):
         low_part, high_part = parts_of(slot_ref[pl.ds(index, 1), :])
         low_by_column(low_hot, low_part.astype(f32))
-        light = [light_ref[layout.message(where_ref, g), :, layout.lanes(index)] for g in range(layout.count)]
+        light = [light_ref[layout.message(g), :, layout.lanes(index)] for g in range(layout.count)]
         light = lanes_of(light)
         for h in range(rows // LOW):
             masked[h * width : (h + 1) * width, :] = jnp.where(high_part == h, light, 0.0).astype(bf16)
@@ -339,11 +342,11 @@
     ahead[...] = exponents(0, 0)
 
     def step(tile, carry):
-        block = jnp.exp2(ahead[...]).astype(bf16)
+        block = jnp.exp(ahead[...]).astype(bf16)
         second = exponents(tile, 1)
         add(tile, 0, block)
         ahead[...] = exponents(tile + 1, 0)
-        add(tile, 1, jnp.exp2(second).astype(bf16))
+        add(tile, 1, jnp.exp(second).astype(bf16))
         return carry
 
     lax.fori_loop(0, filled, step, 0)
@@ -386,7 +389,7 @@
                 flag = jnp.sum(jnp.where(lane == level, flags, 0.0), axis=1, keepdims=True)
                 used.append(jnp.broadcast_to(flag, (1, SK)))
             here = aligned(index * rows + leaf * LEAF, LEAF, LEAF)
-            tile = jnp.exp2(nn(tops[...], bt_ref[:, here])).astype(bf16)
+            tile = jnp.exp(nn(tops[...], bt_ref[:, here])).astype(bf16)
             scaled = (coefs[...].astype(f32) * jnp.concatenate(used, 1)).astype(bf16)
             far = nn(scaled, tile)
             totals.append(near_ref[:, here] + far[:width] + far[width:])
@@ -404,7 +407,7 @@
     lax.fori_loop(0, blocks, block, 0)
 
 
-def final_kernel(blocks, where_ref, pos_ref, *refs):
+def final_kernel(blocks, pos_ref, *refs):
     back_refs, (weights_ref, out_ref, perm, vals) = refs[:-4], refs[-4:]
     chunks = pos_ref.shape[0]
     rows = chunks * LANES
@@ -415,8 +418,8 @@
         high, low = two(back_ref[...])
         columns, at = 0, slice(0, rows)
         if blocks:
-            columns = (where_ref[1] ^ (g % blocks)) * width
-            at = aligned((where_ref[0] ^ where_ref[2] ^ (g // blocks)) * split, split, split)
+            columns = (lax.axis_index("sub") ^ (g % blocks)) * width
+            at = aligned((lax.axis_index("leaf") ^ lax.axis_index("rep") ^ (g // blocks)) * split, split, split)
         vals[aligned(columns, width, width), at] = high
         vals[aligned(columns + LANES, width, width), at] = low
     step = 256
@@ -449,7 +452,7 @@
             inner = jnp.dot(
                 jnp.where(is_point, pair, 0.0).T, jnp.where(is_point, chosen, 0.0), precision=highest
             )
-            tile = jnp.exp2(inner + norms[:, None] + chosen_norms[None])
+            tile = jnp.exp(inner + norms[:, None] + chosen_norms[None])
             own = jnp.where(is_coef, jnp.dot(pair, tile, precision=highest), chosen)
     return jnp.stack(packs)
 
@@ -469,7 +472,6 @@
     fine = trees == 2 and reps == 2 and per % LANES == 0
     layout = Layout(blocks, trees, rows, fine)
     split = part if fine else rows
-    where = jnp.stack([my_leaf, lax.axis_index("sub"), lax.axis_index("rep")]).astype(jnp.int32)
     arrive = shaped((width, part), f32) if fine else shaped((width, total), f32)
 
     place, pos, light = pl.pallas_call(
@@ -479,7 +481,7 @@
             shaped((rows // LANES, LANES), f32),
             shaped((rows // split, columns, split), f32),
         ),
-        in_specs=[spec(SMEM)] + [spec()] * 5,
+        in_specs=[spec()] * 5,
         out_specs=(spec(),) * 3,
         scratch_shapes=[
             vm((rows, rows), bf16),
@@ -488,7 +490,7 @@
         ],
         compiler_params=params(),
         name="sort_rows",
-    )(where, tree_slot.reshape(rows // LANES, LANES), points.T, weights, skeleton_base, far_use)
+    )(tree_slot.reshape(rows // LANES, LANES), points.T, weights, skeleton_base, far_use)
 
     axes = ("leaf", "sub", "rep")
 
@@ -515,11 +517,11 @@
                 place[step | stride] = lax.ppermute(place[step], "sub", [(i, i ^ stride) for i in range(blocks)])
             stride //= 2
         place = [place[step] for step in range(blocks)]
-        place, light = lax.optimization_barrier((place, light))
+        place[1], light = lax.optimization_barrier((place[1], light))
         place = place + [lax.ppermute(one, "rep", [(0, 1), (1, 0)]) for one in place]
         light = light.reshape(devices, width, part)
         light = lax.all_to_all(light, ("leaf", "sub"), split_axis=0, concat_axis=0, tiled=True)
-        small = jnp.zeros((1, 8, SK), f32)
+        small = pos
     else:
         info = jnp.pad(far_use.astype(f32), ((FLAGS, 5 - far_use.shape[0]), (0, SK - far_use.shape[1])))
         small = lax.all_gather(info.at[BASE].set(skeleton_base[0].astype(f32)), "sub", axis=0, tiled=False)
@@ -537,16 +539,16 @@
     feat_a, feat_bt, sk, base, upper_tiles, top, slots, info = pl.pallas_call(
         functools.partial(points_kernel, layout, trees),
         out_shape=(
-            shaped((total, FEAT), bf16),
-            shaped((FEAT, total), bf16),
-            shaped((nodes * SK, FEAT), bf16),
-            shaped((blocks, rows, SK), bf16),
-            shaped((blocks - 1, 2 * SK, SK), f32),
-            shaped((SK, LANES), f32),
-            shaped((blocks, rows), f32),
-            shaped((blocks, 8, SK), f32),
+            vm((total, FEAT), bf16),
+            vm((FEAT, total), bf16),
+            vm((nodes * SK, FEAT), bf16),
+            vm((blocks, rows, SK), bf16),
+            vm((blocks - 1, 2 * SK, SK), f32),
+            vm((SK, LANES), f32),
+            vm((blocks, rows), f32),
+            vm((blocks, 8, SK), f32),
         ),
-        in_specs=[spec(SMEM)] + [spec()] * (2 + layout.count),
+        in_specs=[spec()] * (2 + layout.count),
         out_specs=(spec(),) * 8,
         scratch_shapes=[
             vm((rows // LOW * COORD, rows), bf16),
@@ -555,29 +557,29 @@
             vm((COORD, nodes * SK), bf16),
             vm((FEAT, SK), bf16),
         ],
-        compiler_params=params(),
+        compiler_params=params(40),
         name="tree_points",
-    )(where, skeleton_upper, small, *place)
+    )(skeleton_upper, small, *place)
 
     tree_light, coefs, pack = pl.pallas_call(
         functools.partial(weights_kernel, layout),
         out_shape=(
-            shaped((width, total), bf16),
-            shaped((2 * width, nodes * SK), bf16),
+            vm((width, total), bf16),
+            vm((2 * width, nodes * SK), bf16),
             shaped((LANES, SK), f32),
         ),
-        in_specs=[spec(SMEM)] + [spec()] * 5,
+        in_specs=[spec()] * 5,
         out_specs=(spec(),) * 3,
         scratch_shapes=[vm((rows // LOW * width, rows), bf16), vm((rows, LOW), bf16)],
-        compiler_params=params(),
+        compiler_params=params(40),
         name="tree_weights",
-    )(where, base, upper_tiles, top, slots, light)
+    )(held(base), held(upper_tiles), held(top), held(slots), light)
 
     packs = upper_levels(pack, skeleton_upper, my_leaf, trees, blocks, width)
 
     near = pl.pallas_call(
         near_kernel,
-        out_shape=shaped((width, total), f32),
+        out_shape=vm((width, total), f32),
         in_specs=[spec(SMEM)] * 2 + [spec()] * 3,
         out_specs=spec(),
         scratch_shapes=[
@@ -585,9 +587,9 @@
             pltpu.SMEM((3, leaves * leaves + 1), jnp.int32),
             vm((LEAF, LEAF // 2), f32),
         ],
-        compiler_params=params(),
+        compiler_params=params(40),
         name="near",
-    )(near_count, near_list[0], feat_a, feat_bt, tree_light)
+    )(near_count, near_list[0], held(feat_a), held(feat_bt), held(tree_light))
 
     levels = low_levels + ups
     back = pl.pallas_call(
@@ -596,9 +598,9 @@
         in_specs=[spec()] * 7,
         out_specs=(spec(),) * layout.count,
         scratch_shapes=[vm((levels * SK, FEAT), bf16), vm((2 * width, levels * SK), bf16), vm((LOW, rows), bf16)],
-        compiler_params=params(),
+        compiler_params=params(40),
         name="far",
-    )(packs, slots, info, feat_bt, sk, coefs, near)
+    )(packs, *[held(one) for one in (slots, info, feat_bt, sk, coefs, near)])
 
     if fine:
         back = swap_all(back)
@@ -610,12 +612,12 @@
     return pl.pallas_call(
         functools.partial(final_kernel, blocks if fine else 0),
         out_shape=shaped((rows, columns), f32),
-        in_specs=[spec(SMEM)] + [spec()] * (2 + layout.count),
+        in_specs=[spec()] * (2 + layout.count),
         out_specs=spec(),
         scratch_shapes=[vm((rows, rows), bf16), vm((2 * LANES, rows), bf16)],
-        compiler_params=params(),
+        compiler_params=params(40),
         name="to_input_order",
-    )(where, pos, *back, weights)
+    )(pos, *back, weights)
 
 
 def solution(mesh):

time: 94.5 us -> 106 us (1.12)
  waiting for transfers between devices: 15.7 us -> 30.5 us
  Pallas kernels: 43.5 us -> 30.5 us
  local copies, waits for them, and re-layouts: 2.67 us -> 10.3 us
  starting transfers between devices: 31.2 us -> 33.1 us
    ppermute x3, waiting for transfers between devices: 8.06 us -> 23 us  [body(): lax.ppermute(place[step], 'sub', [(i, i ^ stride) for i in range(blocks)])]
    unnamed x36 -> x32, local copies, waits for them, and re-layouts: 2.04 us -> 10.3 us
    pallas_call x2, Pallas kernels: 21.1 us -> 14.8 us  [the longest x1 12.2 us: body(): pl.pallas_call(near_kernel, out_shape=vm((width, total), f32), in_specs=[...]
    pallas_call x1, Pallas kernels: 8.88 us -> 6 us  [body(): pl.pallas_call(functools.partial(points_kernel, layout, trees), out_shape...]
    ppermute x9, waiting for transfers between devices: 3.93 us -> 6.56 us  [swap(): return lax.ppermute(value, axes, pairs)]
    pallas_call x1, Pallas kernels: 6.67 us -> 4.17 us  [body(): pl.pallas_call(functools.partial(far_kernel, layout, low_levels), out_sha...]
    all_to_all x1, waiting for transfers between devices: 2.4 us -> 0.01 us  [body(): lax.all_to_all(light, ('leaf', 'sub'), split_axis=0, concat_axis=0, tiled...]
    pallas_call x1, Pallas kernels: 3.25 us -> 1.91 us  [body(): pl.pallas_call(functools.partial(final_kernel, blocks if fine else 0), ou...]
  transfers between devices with their start and end apart: 18 -> 18, of which waited for: 9 -> 7; matrix products, arithmetic and copies ran while one was open for 1% -> 0% of each run, Pallas kernels for 27% -> 17%
where the time goes in v6:
time: 106 us; the launch traced here: 105 us
  starting transfers between devices  33.1 us (31%)
  Pallas kernels  30.5 us (29%)
  waiting for transfers between devices  30.5 us (29%)
  local copies, waits for them, and re-layouts  10.3 us (10%)
    ppermute x3, waiting for transfers between devices, body(): lax.ppermute(place[step], 'sub', [(i, i ^ stride) for i in range(blocks)])  23 us
    ppermute x9, starting transfers between devices, swap(): return lax.ppermute(value, axes, pairs)  15.7 us
    pallas_call x1, Pallas kernels, body(): pl.pallas_call(near_kernel, out_shape=vm((width, total), f32), in_specs=[...  12.2 us
    unnamed x32, local copies, waits for them, and re-layouts  10.3 us
    ppermute x9, waiting for transfers between devices, swap(): return lax.ppermute(value, axes, pairs)  6.56 us
    ppermute x3, starting transfers between devices, body(): lax.ppermute(place[step], 'sub', [(i, i ^ stride) for i in range(blocks)])  6.3 us
    all_to_all x1, starting transfers between devices, body(): lax.all_to_all(light, ('leaf', 'sub'), split_axis=0, concat_axis=0, tiled...  6.25 us
    pallas_call x1, Pallas kernels, body(): pl.pallas_call(functools.partial(points_kernel, layout, trees), out_shape...  6 us
  transfers between devices with their start and end apart: 18, of which 7 were waited for; matrix products, arithmetic and copies ran while one was open for 0% of the time, Pallas kernels for 17%

profile of v6, /device:TPU:0, one launch (start us, length us, event | category | flops | bytes accessed | tf_op | source)
XLA Modules:
  0.0 104.6 jit_solution(14758574322251275398)
XLA Ops:
  0.0 3.7 %sort_rows.1 = (f32[72,512]{1,0:T(8,128)}, f32[8,128]{1,0:T(8,128)}, f32[2,128,512]{2,1,0:T(8,128)}) custom-call(s32[8,128]{1,0:T(8,128)} %bitcast.9, f32[64,1024]{1,0:T(8,128)} %bitcast.8, f32[1024,128]{1,0:T(8,128)} %refs_8_.1, s32[1,128]{1,0:T(1,128)} %base_ref.1, s32[2,3]{1,0:T(2,128)} %flag_ref.1), custom_call_target="tpu_custom_call" | custom-call | tf_op jit(solution)/shard_map/sort_rows/pallas_call | solution.py:477
  3.7 1.6 %collective-permute-start = (f32[72,512]{1,0:T(8,128)}, f32[72,512]{1,0:T(8,128)S(1)}, u32[]{:S(2)}, u32[]{:S(2)}) collective-permute-start(f32[72,512]{1,0:T(8,128)} %get-tuple-element.30), channel_id=1, source_target_pairs={{0,0},{1,9},{2,2},{3,11},{4,4},{5,13},{6,6},{7,15},{8,8},{9,1},{10... | collective-permute-start | bytes 442376 | tf_op jit(solution)/shard_map/ppermute | solution.py:504
  5.2 3.0 %collective-permute-start.1 = (f32[72,512]{1,0:T(8,128)S(1)}, f32[72,512]{1,0:T(8,128)S(1)}, u32[]{:S(2)}, u32[]{:S(2)}) collective-permute-start(f32[72,512]{1,0:T(8,128)S(1)} %collective-permute-done.refs_0_), channel_id=1, source_target_pairs={{0,2},{2,0},{4,6},{6,4},{1,3},{3,1},{5,7},{7,5},{8,10},{10,8},{12,... | collective-permute-start | bytes 442376 | tf_op jit(solution)/shard_map/ppermute | solution.py:517
  8.2 3.1 %collective-permute-done.1.refs_1_ = f32[72,512]{1,0:T(8,128)S(1)} collective-permute-done((f32[72,512]{1,0:T(8,128)S(1)}, f32[72,512]{1,0:T(8,128)S(1)}, u32[]{:S(2)}, u32[]{:S(2)}) %collective-permute-start.1) | collective-permute-done | bytes 147488 | tf_op jit(solution)/shard_map/ppermute | solution.py:517
  11.4 6.3 %all-to-all-start = ((f32[8,32,512]{2,1,0:T(8,128)}), f32[8,32,512]{2,1,0:T(8,128)S(1)}, u32[]{:S(2)}, u32[]{:S(2)}) async-start(f32[8,32,512]{2,1,0:T(8,128)} %bitcast.7), calls=%async_computation | async-start | bytes 1048576 | tf_op jit(solution)/shard_map/all_to_all | solution.py:523
  17.6 2.9 %collective-permute-start.2 = (f32[72,512]{1,0:T(8,128)S(1)}, f32[72,512]{1,0:T(8,128)S(1)}, u32[]{:S(2)}, u32[]{:S(2)}) collective-permute-start(f32[72,512]{1,0:T(8,128)S(1)} %collective-permute-done.refs_0_), channel_id=1, source_target_pairs={{0,4},{2,6},{4,0},{6,2},{1,5},{3,7},{5,1},{7,3},{8,12},{10,14},{12... | collective-permute-start | bytes 442376 | tf_op jit(solution)/shard_map/ppermute | solution.py:517
  20.5 17.0 %collective-permute-done.2.refs_2_ = f32[72,512]{1,0:T(8,128)S(1)} collective-permute-done((f32[72,512]{1,0:T(8,128)S(1)}, f32[72,512]{1,0:T(8,128)S(1)}, u32[]{:S(2)}, u32[]{:S(2)}) %collective-permute-start.2) | collective-permute-done | bytes 147488 | tf_op jit(solution)/shard_map/ppermute | solution.py:517
  37.9 1.8 %collective-permute-start.4 = (f32[72,512]{1,0:T(8,128)S(1)}, f32[72,512]{1,0:T(8,128)S(1)}, u32[]{:S(2)}, u32[]{:S(2)}) collective-permute-start(f32[72,512]{1,0:T(8,128)S(1)} %collective-permute-done.refs_0_), channel_id=1, source_target_pairs={{0,1},{1,0},{2,3},{3,2},{4,5},{5,4},{6,7},{7,6},{8,9},{9,8},{10,11... | collective-permute-start | bytes 442376 | tf_op jit(solution)/shard_map/ppermute | solution.py:521
  40.2 2.9 %collective-permute-done.3.refs_3_ = f32[72,512]{1,0:T(8,128)S(1)} collective-permute-done((f32[72,512]{1,0:T(8,128)S(1)}, f32[72,512]{1,0:T(8,128)S(1)}, u32[]{:S(2)}, u32[]{:S(2)}) %collective-permute-start.3) | collective-permute-done | bytes 147488 | tf_op jit(solution)/shard_map/ppermute | solution.py:517
  48.3 6.0 %tree_points.1 = (bf16[4096,256]{1,0:T(8,128)(2,1)S(1)}, bf16[256,4096]{1,0:T(8,128)(2,1)S(1)}, bf16[896,256]{1,0:T(8,128)(2,1)S(1)}, bf16[4,1024,128]{2,1,0:T(8...) custom-call(s32[6,128]{1,0:T(8,128)S(1)} %copy-done.13, ...), custom_call_target="tpu_custom_call" | custom-call | tf_op jit(solution)/shard_map/tree_points/pallas_call | solution.py:539
  54.3 1.4 %copy-done.1 = bf16[4096,256]{1,0:T(8,128)(2,1)} copy-done((bf16[4096,256]{1,0:T(8,128)(2,1)}, bf16[4096,256]{1,0:T(8,128)(2,1)S(1)}, u32[]{:S(2)}) %copy-start.1) | copy-done | bytes 2097176
  57.2 1.2 %copy-done.4 = bf16[4,1024,128]{2,1,0:T(8,128)(2,1)S(1)} copy-done((bf16[4,1024,128]{2,1,0:T(8,128)(2,1)S(1)}, bf16[4,1024,128]{2,1,0:T(8,128)(2,1)}, u32[]{:S(2)}) %copy-start.4) | copy-done | bytes 1048600
  58.4 2.6 %tree_weights.1 = (bf16[32,4096]{1,0:T(8,128)(2,1)S(1)}, bf16[64,896]{1,0:T(8,128)(2,1)S(1)}, f32[128,128]{1,0:T(8,128)S(1)}) custom-call(bf16[4,1024,128]{2,1,0:T(8,128)(2,1)S(1)} %copy-done.4, f32[3,256,128]{2,1,0:T(8,128)S(1)} %get-tuple-element.34.upper_tiles_ref, f32[128,128]{1,0:T(8,128)S(1)} %get-tuple-element.35.top_ref, ...), custom_call_target="tpu_custom_call" | custom-call | tf_op jit(solution)/shard_map/tree_weights/pallas_call | solution.py:564
  61.0 1.5 %collective-permute-start.8 = (f32[128,128]{1,0:T(8,128)S(1)}, f32[128,128]{1,0:T(8,128)S(1)}, u32[]{:S(2)}, u32[]{:S(2)}) collective-permute-start(f32[128,128]{1,0:T(8,128)S(1)} %get-tuple-element.38), channel_id=1, source_target_pairs={{0,8},{8,0},{1,9},{9,1},{2,10},{10,2},{3,11},{11,3},{4,12},{12,4},... | collective-permute-start | bytes 196616 | tf_op jit(solution)/shard_map/ppermute | solution.py:441
  62.6 1.6 %copy-done.2 = bf16[4096,256]{1,0:T(8,128)(2,1)S(1)} copy-done((bf16[4096,256]{1,0:T(8,128)(2,1)S(1)}, bf16[4096,256]{1,0:T(8,128)(2,1)}, u32[]{:S(2)}) %copy-start.2) | copy-done | bytes 2097176
  65.5 12.2 %near.1.near_ref = f32[32,4096]{1,0:T(8,128)S(1)} custom-call(s32[1,8]{1,0:T(1,128)S(1)} %copy-done.15, s32[8,16]{1,0:T(8,128)S(1)} %bitcast.6, bf16[4096,256]{1,0:T(8,128)(2,1)S(1)} %copy-done.2, bf16[256,4096]{1,0:T(8,128)(2,1)S(1)} %get-tuple-element.40.bt_ref, bf16[32,4096]{1,0:T(8,128)(2,1)S(1)} %get-tuple-element.44.w_ref), custom_call_target="tpu_custom_call" | custom-call | tf_op jit(solution)/shard_map/near/pallas_call | solution.py:580
  77.8 4.2 %far.1 = (f32[32,512]{1,0:T(8,128)S(1)}, f32[32,512]{1,0:T(8,128)S(1)}, f32[32,512]{1,0:T(8,128)S(1)}, f32[32,512]{1,0:T(8,128)S(1)}, f32[32,512]{1,0:T(8,128)S(...) custom-call(f32[1,128,128]{2,1,0:T(8,128)S(1)} %bitcast.5, ...), custom_call_target="tpu_custom_call" | custom-call | tf_op jit(solution)/shard_map/far/pallas_call | solution.py:595
  83.6 3.0 %collective-permute-start.11 = (f32[32,512]{1,0:T(8,128)S(1)}, f32[32,512]{1,0:T(8,128)S(1)}, u32[]{:S(2)}, u32[]{:S(2)}) collective-permute-start(f32[32,512]{1,0:T(8,128)S(1)} %get-tuple-element.47), channel_id=1, source_target_pairs={{0,4},{1,13},{2,6},{3,15},{4,0},{5,9},{6,2},{7,11},{8,12},{9,5},{1... | collective-permute-start | bytes 196616 | tf_op jit(solution)/shard_map/ppermute | solution.py:504
  87.1 4.2 %collective-permute-start.13 = (f32[32,512]{1,0:T(8,128)S(1)}, f32[32,512]{1,0:T(8,128)S(1)}, u32[]{:S(2)}, u32[]{:S(2)}) collective-permute-start(f32[32,512]{1,0:T(8,128)S(1)} %get-tuple-element.49), channel_id=1, source_target_pairs={{0,8},{1,1},{2,10},{3,3},{4,12},{5,5},{6,14},{7,7},{8,0},{9,9},{10... | collective-permute-start | bytes 196616 | tf_op jit(solution)/shard_map/ppermute | solution.py:504
  91.4 4.3 %collective-permute-start.15 = (f32[32,512]{1,0:T(8,128)S(1)}, f32[32,512]{1,0:T(8,128)S(1)}, u32[]{:S(2)}, u32[]{:S(2)}) collective-permute-start(f32[32,512]{1,0:T(8,128)S(1)} %get-tuple-element.51), channel_id=1, source_target_pairs={{0,12},{1,5},{2,14},{3,7},{4,8},{5,1},{6,10},{7,3},{8,4},{9,13},{1... | collective-permute-start | bytes 196616 | tf_op jit(solution)/shard_map/ppermute | solution.py:504
  96.1 1.6 %collective-permute-done.14.refs_5_ = f32[32,512]{1,0:T(8,128)S(1)} collective-permute-done((f32[32,512]{1,0:T(8,128)S(1)}, f32[32,512]{1,0:T(8,128)S(1)}, u32[]{:S(2)}, u32[]{:S(2)}) %collective-permute-start.14) | collective-permute-done | bytes 65568 | tf_op jit(solution)/shard_map/ppermute | solution.py:504
  97.7 2.9 %collective-permute-done.15.refs_6_ = f32[32,512]{1,0:T(8,128)S(1)} collective-permute-done((f32[32,512]{1,0:T(8,128)S(1)}, f32[32,512]{1,0:T(8,128)S(1)}, u32[]{:S(2)}, u32[]{:S(2)}) %collective-permute-start.15) | collective-permute-done | bytes 65568 | tf_op jit(solution)/shard_map/ppermute | solution.py:504
  100.6 2.1 %collective-permute-done.16.refs_7_ = f32[32,512]{1,0:T(8,128)S(1)} collective-permute-done((f32[32,512]{1,0:T(8,128)S(1)}, f32[32,512]{1,0:T(8,128)S(1)}, u32[]{:S(2)}, u32[]{:S(2)}) %collective-permute-start.16) | collective-permute-done | bytes 65568 | tf_op jit(solution)/shard_map/ppermute | solution.py:504
  102.7 1.9 %to_input_order.1 = f32[1024,128]{1,0:T(8,128)} custom-call(f32[8,128]{1,0:T(8,128)S(1)} %copy-done.12, f32[32,512]{1,0:T(8,128)S(1)} %collective-permute-done.9.refs_0_, f32[32,512]{1,0:T(8,128)S(1)} %collective-permute-done.10.refs_1_, f32[32,512]{1,0:T(8,128)S(1)} %collective-permute-done.11.refs_2_, f32[32,512]{1,0:T(8,128)S(1)} %collective-permute-done.12.refs_3_, ...), custom_call_target="tpu_custom_call" | custom-call | tf_op jit(solution)/shard_map/to_input_order/pallas_call | solution.py:612
  (50 shorter events, 11.6 us)
Async XLA Ops:
  3.7 1.6 %collective-permute-start = (f32[72,512]{1,0:T(8,128)}, f32[72,512]{1,0:T(8,128)S(1)}, u32[]{:S(2)}, u32[]{:S(2)}) collective-permute-start(f32[72,512]{1,0:T(8,128)} %get-tuple-element.30), channel_id=1, source_target_pairs={{0,0},{1,9},{2,2},{3,11},{4,4},{5,13},{6,6},{7,15},{8,8},{9,1},{10... | collective-permute-start | bytes 442376 | tf_op jit(solution)/shard_map/ppermute | solution.py:504
  5.2 39.9 %copy-start.5 = (f32[72,512]{1,0:T(8,128)}, f32[72,512]{1,0:T(8,128)S(1)}, u32[]{:S(2)}) copy-start(f32[72,512]{1,0:T(8,128)S(1)} %collective-permute-done.refs_0_) | copy-start | bytes 442372
  5.2 6.1 %collective-permute-start.1 = (f32[72,512]{1,0:T(8,128)S(1)}, f32[72,512]{1,0:T(8,128)S(1)}, u32[]{:S(2)}, u32[]{:S(2)}) collective-permute-start(f32[72,512]{1,0:T(8,128)S(1)} %collective-permute-done.refs_0_), channel_id=1, source_target_pairs={{0,2},{2,0},{4,6},{6,4},{1,3},{3,1},{5,7},{7,5},{8,10},{10,8},{12,... | collective-permute-start | bytes 442376 | tf_op jit(solution)/shard_map/ppermute | solution.py:517
  11.4 33.7 %copy-start.7 = (f32[72,512]{1,0:T(8,128)}, f32[72,512]{1,0:T(8,128)S(1)}, u32[]{:S(2)}) copy-start(f32[72,512]{1,0:T(8,128)S(1)} %collective-permute-done.1.refs_1_) | copy-start | bytes 442372
  11.4 45.9 %all-to-all-start = ((f32[8,32,512]{2,1,0:T(8,128)}), f32[8,32,512]{2,1,0:T(8,128)S(1)}, u32[]{:S(2)}, u32[]{:S(2)}) async-start(f32[8,32,512]{2,1,0:T(8,128)} %bitcast.7), calls=%async_computation | async-start | bytes 1048576 | tf_op jit(solution)/shard_map/all_to_all | solution.py:523
  17.6 19.9 %collective-permute-start.2 = (f32[72,512]{1,0:T(8,128)S(1)}, f32[72,512]{1,0:T(8,128)S(1)}, u32[]{:S(2)}, u32[]{:S(2)}) collective-permute-start(f32[72,512]{1,0:T(8,128)S(1)} %collective-permute-done.refs_0_), channel_id=1, source_target_pairs={{0,4},{2,6},{4,0},{6,2},{1,5},{3,7},{5,1},{7,3},{8,12},{10,14},{12... | collective-permute-start | bytes 442376 | tf_op jit(solution)/shard_map/ppermute | solution.py:517
  37.5 5.5 %collective-permute-start.3 = (f32[72,512]{1,0:T(8,128)S(1)}, f32[72,512]{1,0:T(8,128)S(1)}, u32[]{:S(2)}, u32[]{:S(2)}) collective-permute-start(f32[72,512]{1,0:T(8,128)S(1)} %collective-permute-done.2.refs_2_), channel_id=1, source_target_pairs={{0,2},{2,0},{4,6},{6,4},{1,3},{3,1},{5,7},{7,5},{8,10},{10,8},{12,... | collective-permute-start | bytes 442376 | tf_op jit(solution)/shard_map/ppermute | solution.py:517
  37.9 6.2 %collective-permute-start.4 = (f32[72,512]{1,0:T(8,128)S(1)}, f32[72,512]{1,0:T(8,128)S(1)}, u32[]{:S(2)}, u32[]{:S(2)}) collective-permute-start(f32[72,512]{1,0:T(8,128)S(1)} %collective-permute-done.refs_0_), channel_id=1, source_target_pairs={{0,1},{1,0},{2,3},{3,2},{4,5},{5,4},{6,7},{7,6},{8,9},{9,8},{10,11... | collective-permute-start | bytes 442376 | tf_op jit(solution)/shard_map/ppermute | solution.py:521
  39.7 4.4 %collective-permute-start.5 = (f32[72,512]{1,0:T(8,128)S(1)}, f32[72,512]{1,0:T(8,128)S(1)}, u32[]{:S(2)}, u32[]{:S(2)}) collective-permute-start(f32[72,512]{1,0:T(8,128)S(1)} %collective-permute-done.1.refs_1_), channel_id=1, source_target_pairs={{0,1},{1,0},{2,3},{3,2},{4,5},{5,4},{6,7},{7,6},{8,9},{9,8},{10,11... | collective-permute-start | bytes 442376 | tf_op jit(solution)/shard_map/ppermute | solution.py:521
  39.7 4.4 %collective-permute-start.6 = (f32[72,512]{1,0:T(8,128)S(1)}, f32[72,512]{1,0:T(8,128)S(1)}, u32[]{:S(2)}, u32[]{:S(2)}) collective-permute-start(f32[72,512]{1,0:T(8,128)S(1)} %collective-permute-done.2.refs_2_), channel_id=1, source_target_pairs={{0,1},{1,0},{2,3},{3,2},{4,5},{5,4},{6,7},{7,6},{8,9},{9,8},{10,11... | collective-permute-start | bytes 442376 | tf_op jit(solution)/shard_map/ppermute | solution.py:521
  43.0 2.0 %collective-permute-start.7 = (f32[72,512]{1,0:T(8,128)S(1)}, f32[72,512]{1,0:T(8,128)S(1)}, u32[]{:S(2)}, u32[]{:S(2)}) collective-permute-start(f32[72,512]{1,0:T(8,128)S(1)} %collective-permute-done.3.refs_3_), channel_id=1, source_target_pairs={{0,1},{1,0},{2,3},{3,2},{4,5},{5,4},{6,7},{7,6},{8,9},{9,8},{10,11... | collective-permute-start | bytes 442376 | tf_op jit(solution)/shard_map/ppermute | solution.py:521
  61.0 16.7 %collective-permute-start.8 = (f32[128,128]{1,0:T(8,128)S(1)}, f32[128,128]{1,0:T(8,128)S(1)}, u32[]{:S(2)}, u32[]{:S(2)}) collective-permute-start(f32[128,128]{1,0:T(8,128)S(1)} %get-tuple-element.38), channel_id=1, source_target_pairs={{0,8},{8,0},{1,9},{9,1},{2,10},{10,2},{3,11},{11,3},{4,12},{12,4},... | collective-permute-start | bytes 196616 | tf_op jit(solution)/shard_map/ppermute | solution.py:441
  62.6 1.6 %copy-start.2 = (bf16[4096,256]{1,0:T(8,128)(2,1)S(1)}, bf16[4096,256]{1,0:T(8,128)(2,1)}, u32[]{:S(2)}) copy-start(bf16[4096,256]{1,0:T(8,128)(2,1)} %copy-done.1) | copy-start | bytes 6291460
  65.5 12.2 %copy-start.10 = (f32[4,8,128]{2,1,0:T(8,128)S(1)}, f32[4,8,128]{2,1,0:T(8,128)}, u32[]{:S(2)}) copy-start(f32[4,8,128]{2,1,0:T(8,128)} %copy-done.9) | copy-start | bytes 49156
  77.7 25.0 %copy-start = (f32[1024,128]{1,0:T(8,128)S(1)}, f32[1024,128]{1,0:T(8,128)}, u32[]{:S(2)}) copy-start(f32[1024,128]{1,0:T(8,128)} %refs_8_.1) | copy-start | bytes 1572868
  77.7 24.9 %copy-start.12 = (f32[8,128]{1,0:T(8,128)S(1)}, f32[8,128]{1,0:T(8,128)}, u32[]{:S(2)}) copy-start(f32[8,128]{1,0:T(8,128)} %get-tuple-element.29.small_ref.pos_ref) | copy-start | bytes 12292
  81.9 9.4 %collective-permute-start.9 = (f32[32,512]{1,0:T(8,128)S(1)}, f32[32,512]{1,0:T(8,128)S(1)}, u32[]{:S(2)}, u32[]{:S(2)}) collective-permute-start(f32[32,512]{1,0:T(8,128)S(1)} %get-tuple-element.45), channel_id=1, source_target_pairs={{0,0},{1,9},{2,2},{3,11},{4,4},{5,13},{6,6},{7,15},{8,8},{9,1},{10... | collective-permute-start | bytes 196616 | tf_op jit(solution)/shard_map/ppermute | solution.py:504
  82.6 8.8 %collective-permute-start.10 = (f32[32,512]{1,0:T(8,128)S(1)}, f32[32,512]{1,0:T(8,128)S(1)}, u32[]{:S(2)}, u32[]{:S(2)}) collective-permute-start(f32[32,512]{1,0:T(8,128)S(1)} %get-tuple-element.46), channel_id=1, source_target_pairs={{0,2},{1,11},{2,0},{3,9},{4,6},{5,15},{6,4},{7,13},{8,10},{9,3},{1... | collective-permute-start | bytes 196616 | tf_op jit(solution)/shard_map/ppermute | solution.py:504
  83.6 12.1 %collective-permute-start.11 = (f32[32,512]{1,0:T(8,128)S(1)}, f32[32,512]{1,0:T(8,128)S(1)}, u32[]{:S(2)}, u32[]{:S(2)}) collective-permute-start(f32[32,512]{1,0:T(8,128)S(1)} %get-tuple-element.47), channel_id=1, source_target_pairs={{0,4},{1,13},{2,6},{3,15},{4,0},{5,9},{6,2},{7,11},{8,12},{9,5},{1... | collective-permute-start | bytes 196616 | tf_op jit(solution)/shard_map/ppermute | solution.py:504
  86.7 9.5 %collective-permute-start.12 = (f32[32,512]{1,0:T(8,128)S(1)}, f32[32,512]{1,0:T(8,128)S(1)}, u32[]{:S(2)}, u32[]{:S(2)}) collective-permute-start(f32[32,512]{1,0:T(8,128)S(1)} %get-tuple-element.48), channel_id=1, source_target_pairs={{0,6},{1,15},{2,4},{3,13},{4,2},{5,11},{6,0},{7,9},{8,14},{9,7},{1... | collective-permute-start | bytes 196616 | tf_op jit(solution)/shard_map/ppermute | solution.py:504
  87.1 9.1 %collective-permute-start.13 = (f32[32,512]{1,0:T(8,128)S(1)}, f32[32,512]{1,0:T(8,128)S(1)}, u32[]{:S(2)}, u32[]{:S(2)}) collective-permute-start(f32[32,512]{1,0:T(8,128)S(1)} %get-tuple-element.49), channel_id=1, source_target_pairs={{0,8},{1,1},{2,10},{3,3},{4,12},{5,5},{6,14},{7,7},{8,0},{9,9},{10... | collective-permute-start | bytes 196616 | tf_op jit(solution)/shard_map/ppermute | solution.py:504
  91.3 6.4 %collective-permute-start.14 = (f32[32,512]{1,0:T(8,128)S(1)}, f32[32,512]{1,0:T(8,128)S(1)}, u32[]{:S(2)}, u32[]{:S(2)}) collective-permute-start(f32[32,512]{1,0:T(8,128)S(1)} %get-tuple-element.50), channel_id=1, source_target_pairs={{0,10},{1,3},{2,8},{3,1},{4,14},{5,7},{6,12},{7,5},{8,2},{9,11},{1... | collective-permute-start | bytes 196616 | tf_op jit(solution)/shard_map/ppermute | solution.py:504
  91.4 9.2 %collective-permute-start.15 = (f32[32,512]{1,0:T(8,128)S(1)}, f32[32,512]{1,0:T(8,128)S(1)}, u32[]{:S(2)}, u32[]{:S(2)}) collective-permute-start(f32[32,512]{1,0:T(8,128)S(1)} %get-tuple-element.51), channel_id=1, source_target_pairs={{0,12},{1,5},{2,14},{3,7},{4,8},{5,1},{6,10},{7,3},{8,4},{9,13},{1... | collective-permute-start | bytes 196616 | tf_op jit(solution)/shard_map/ppermute | solution.py:504
  95.7 7.0 %collective-permute-start.16 = (f32[32,512]{1,0:T(8,128)S(1)}, f32[32,512]{1,0:T(8,128)S(1)}, u32[]{:S(2)}, u32[]{:S(2)}) collective-permute-start(f32[32,512]{1,0:T(8,128)S(1)} %get-tuple-element.52), channel_id=1, source_target_pairs={{0,14},{1,7},{2,12},{3,5},{4,10},{5,3},{6,8},{7,1},{8,6},{9,15},{1... | collective-permute-start | bytes 196616 | tf_op jit(solution)/shard_map/ppermute | solution.py:504
  (10 other events, 8.7 us)

commit v7 on v6

--- a/solution.py
+++ b/solution.py
@@ -33,6 +33,10 @@
 
 def params(mib=58):
     return pltpu.CompilerParams(vmem_limit_bytes=mib * 1024 * 1024)
+
+
+def in_hbm(array):
+    return pltpu.with_memory_space_constraint(array, pltpu.MemorySpace.HBM)
 
 
 def held(array):
@@ -191,7 +195,8 @@
     out[0:64, at] = tree[0:64].astype(bf16)
     out[64:128, at] = tree[0:64].astype(bf16)
     out[128:192, at] = tree[64:128].astype(bf16)
-    out[192:256, at] = jnp.concatenate([tree[128:136], jnp.zeros((56, tree.shape[1]), f32)], 0).astype(bf16)
+    out[192:208, at] = jnp.where(iota((16, tree.shape[1]), 0) < 8, tree[128:144].astype(f32), 0.0).astype(bf16)
+    out[208:256, at] = jnp.zeros((48, tree.shape[1]), bf16)
 
 
 def feature_rows(high, low, extra):
@@ -200,9 +205,14 @@
     return first.astype(bf16), second.astype(bf16)
 
 
-def points_kernel(layout, trees, upper_ref, small_ref, *refs):
+def points_kernel(layout, trees, upper_ref, *refs):
+    if not layout.fine:
+        small_ref, refs = refs[0], refs[1:]
+    else:
+        small_ref = None
     place_refs, refs = refs[: layout.count], refs[layout.count :]
-    a_ref, bt_ref, sk_ref, base_ref, upper_tiles_ref, top_ref, slot_ref, info_ref, masked, low_hot, tree, sk_t, sk_bt = refs
+    tree_ref, a_hbm, base_hbm, sk_ref, upper_tiles_ref, top_ref, slot_ref, info_ref = refs[:8]
+    masked, low_hot, a_ref, base_ref, sk_t, sk_bt, sems = refs[8:]
     blocks, rows = layout.blocks, layout.rows
 
     def keep(node, found):
@@ -235,14 +245,15 @@
         placed = nn(masked[...], low_hot[...])
         for h in range(rows // LOW):
             part = placed[h * COORD : (h + 1) * COORD]
-            tree[:, h * LOW : (h + 1) * LOW] = part.astype(bf16)
             at = aligned(index * rows + h * LOW, LOW, LOW)
-            feature_columns(bt_ref, at, part)
+            tree_ref[:, at] = part.astype(bf16)
             a_ref[at, 0:128], a_ref[at, 128:256] = feature_rows(part[0:64], part[64:128], part[136:144])
         picked = onehot(iota((rows, SK), 0) == info[BASE : BASE + 1].astype(jnp.int32))
-        keep(index, nn(tree[...], picked))
         mine = aligned(index * rows, rows, rows)
+        pltpu.make_async_copy(a_ref.at[mine], a_hbm.at[mine], sems.at[0, index]).start()
+        keep(index, nn(tree_ref[:, mine], picked))
         base_ref[index] = jnp.exp(nn(a_ref[mine, :], sk_bt[...])).astype(bf16)
+        pltpu.make_async_copy(base_ref.at[index], base_hbm.at[index], sems.at[1, index]).start()
         return carry
 
     lax.fori_loop(0, blocks, block, 0)
@@ -263,14 +274,20 @@
     top_ref[0:64, :] = found[0:64] + found[64:128]
     top_ref[64:72, :] = found[128:136]
     top_ref[72:128, :] = jnp.zeros((56, SK), f32)
+    for index in range(blocks):
+        mine = slice(index * rows, (index + 1) * rows)
+        pltpu.make_async_copy(a_ref.at[mine], a_hbm.at[mine], sems.at[0, index]).wait()
+        pltpu.make_async_copy(base_ref.at[index], base_hbm.at[index], sems.at[1, index]).wait()
 
 
 def weights_kernel(
-    layout, base_ref, upper_tiles_ref, top_ref, slot_ref, light_ref, w_ref, coef_ref, pack_ref, masked, low_hot
+    layout, base_hbm, upper_tiles_ref, top_ref, slot_ref, light_ref, w_ref, coef_ref, pack_ref, masked, low_hot, base_ref, sems
 ):
     blocks, rows = layout.blocks, layout.rows
     width = light_ref.shape[1]
     pack_ref[...] = top_ref[...]
+    for index in range(blocks):
+        pltpu.make_async_copy(base_hbm.at[index], base_ref.at[index], sems.at[index]).start()
 
     def keep(node, coef):
         coef_ref[:, aligned(node * SK, SK, SK)] = stack_two(coef)
@@ -287,6 +304,7 @@
         parts = [placed[h * width : (h + 1) * width] for h in range(rows // LOW)]
         own = jnp.concatenate(parts, 1).astype(bf16)
         w_ref[:, aligned(index * rows, rows, rows)] = own
+        pltpu.make_async_copy(base_hbm.at[index], base_ref.at[index], sems.at[index]).wait()
         keep(index, nn(own, base_ref[index]))
         return carry
 
@@ -302,8 +320,13 @@
         start, count = start + count, count // 2
 
 
-def near_kernel(count_ref, list_ref, a_ref, bt_ref, w_ref, acc, times, tiles, ahead):
+def near_kernel(count_ref, list_ref, a_hbm, tree_ref, w_ref, acc, times, tiles, a_ref, bt_ref, sem):
     every = count_ref.shape[1]
+    copy = pltpu.make_async_copy(a_hbm, a_ref, sem)
+    copy.start()
+    for leaf in range(every):
+        here = slice(leaf * LEAF, (leaf + 1) * LEAF)
+        feature_columns(bt_ref, here, tree_ref[:, here])
 
     def tally(leaf, filled):
         for other in range(every):
@@ -325,6 +348,7 @@
     filled = lax.fori_loop(0, every, tally, jnp.int32(0))
     tiles[0, filled] = 0
     tiles[1, filled] = 0
+    tiles[2, filled] = 0
     half = LEAF // 2
     acc[...] = jnp.zeros_like(acc)
 
@@ -339,21 +363,19 @@
         source = aligned(tiles[1, tile] * LEAF, LEAF, LEAF)
         acc[:, target(tile, part)] += tiles[2, tile].astype(f32) * nn(w_ref[:, source], block)
 
-    ahead[...] = exponents(0, 0)
-
-    def step(tile, carry):
-        block = jnp.exp(ahead[...]).astype(bf16)
-        second = exponents(tile, 1)
-        add(tile, 0, block)
-        ahead[...] = exponents(tile + 1, 0)
-        add(tile, 1, jnp.exp(second).astype(bf16))
+    copy.wait()
+
+    def step(pair, carry):
+        for tile in (2 * pair, 2 * pair + 1):
+            for part in range(2):
+                add(tile, part, jnp.exp(exponents(tile, part)).astype(bf16))
         return carry
 
-    lax.fori_loop(0, filled, step, 0)
-
-
-def far_kernel(layout, low_levels, pack_ref, slot_ref, info_ref, bt_ref, sk_ref, coef_ref, near_ref, *refs):
-    out_refs, (tops, coefs, low_hot) = refs[: layout.count], refs[layout.count :]
+    lax.fori_loop(0, (filled + 1) // 2, step, 0)
+
+
+def far_kernel(layout, low_levels, pack_ref, slot_ref, info_ref, tree_ref, sk_ref, coef_ref, near_ref, *refs):
+    out_refs, (tops, coefs, low_hot, bt_ref) = refs[: layout.count], refs[layout.count :]
     blocks, rows = layout.blocks, layout.rows
     ups, width = pack_ref.shape[0], out_refs[0].shape[0]
     levels = low_levels + ups
@@ -389,7 +411,8 @@
                 flag = jnp.sum(jnp.where(lane == level, flags, 0.0), axis=1, keepdims=True)
                 used.append(jnp.broadcast_to(flag, (1, SK)))
             here = aligned(index * rows + leaf * LEAF, LEAF, LEAF)
-            tile = jnp.exp(nn(tops[...], bt_ref[:, here])).astype(bf16)
+            feature_columns(bt_ref, slice(0, LEAF), tree_ref[:, here])
+            tile = jnp.exp(nn(tops[...], bt_ref[...])).astype(bf16)
             scaled = (coefs[...].astype(f32) * jnp.concatenate(used, 1)).astype(bf16)
             far = nn(scaled, tile)
             totals.append(near_ref[:, here] + far[:width] + far[width:])
@@ -510,21 +533,26 @@
         return [done[g] for g in range(len(values))]
 
     if fine:
-        place = {0: swap(place, 0)}
-        stride = blocks // 2
-        while stride:
-            for step in sorted(place):
-                place[step | stride] = lax.ppermute(place[step], "sub", [(i, i ^ stride) for i in range(blocks)])
-            stride //= 2
+        sent, far_off = place, blocks // 2
+        place = {far_off: swap(sent, far_off)}
+        step = 1
+        while step < far_off:
+            place[step] = swap(sent, step)
+            step *= 2
+        place[0] = swap(sent, 0)
+        for step in range(1, blocks):
+            if step not in place:
+                last = step & -step
+                place[step] = lax.ppermute(place[step ^ last], "sub", [(i, i ^ last) for i in range(blocks)])
+        place[1], tied, light = lax.optimization_barrier((place[1], place[far_off], light))
         place = [place[step] for step in range(blocks)]
-        place[1], light = lax.optimization_barrier((place[1], light))
         place = place + [lax.ppermute(one, "rep", [(0, 1), (1, 0)]) for one in place]
         light = light.reshape(devices, width, part)
         light = lax.all_to_all(light, ("leaf", "sub"), split_axis=0, concat_axis=0, tiled=True)
-        small = pos
+        small = []
     else:
         info = jnp.pad(far_use.astype(f32), ((FLAGS, 5 - far_use.shape[0]), (0, SK - far_use.shape[1])))
-        small = lax.all_gather(info.at[BASE].set(skeleton_base[0].astype(f32)), "sub", axis=0, tiled=False)
+        small = [lax.all_gather(info.at[BASE].set(skeleton_base[0].astype(f32)), "sub", axis=0, tiled=False)]
         place = place.reshape(PLACE_ROWS, trees, part).transpose(1, 0, 2)
         place = lax.all_to_all(place, "leaf", split_axis=0, concat_axis=0, tiled=True)
         place = lax.all_gather(place, "sub", axis=0, tiled=False)
@@ -536,30 +564,32 @@
         light = light.transpose(1, 2, 0, 3).reshape(1, width, total)
 
     nodes = 2 * blocks - 1
-    feat_a, feat_bt, sk, base, upper_tiles, top, slots, info = pl.pallas_call(
+    tree, feat_a, base, sk, upper_tiles, top, slots, info = pl.pallas_call(
         functools.partial(points_kernel, layout, trees),
         out_shape=(
-            vm((total, FEAT), bf16),
-            vm((FEAT, total), bf16),
+            vm((COORD, total), bf16),
+            pltpu.MemorySpace.HBM((total, FEAT), bf16),
+            pltpu.MemorySpace.HBM((blocks, rows, SK), bf16),
             vm((nodes * SK, FEAT), bf16),
-            vm((blocks, rows, SK), bf16),
             vm((blocks - 1, 2 * SK, SK), f32),
             vm((SK, LANES), f32),
             vm((blocks, rows), f32),
             vm((blocks, 8, SK), f32),
         ),
-        in_specs=[spec()] * (2 + layout.count),
-        out_specs=(spec(),) * 8,
+        in_specs=[spec()] * (1 + len(small) + layout.count),
+        out_specs=(spec(), spec(pl.ANY), spec(pl.ANY)) + (spec(),) * 5,
         scratch_shapes=[
             vm((rows // LOW * COORD, rows), bf16),
             vm((rows, LOW), bf16),
-            vm((COORD, rows), bf16),
+            vm((total, FEAT), bf16),
+            vm((blocks, rows, SK), bf16),
             vm((COORD, nodes * SK), bf16),
             vm((FEAT, SK), bf16),
+            pltpu.SemaphoreType.DMA((2, blocks)),
         ],
         compiler_params=params(40),
         name="tree_points",
-    )(skeleton_upper, small, *place)
+    )(in_hbm(skeleton_upper), *small, *place)
 
     tree_light, coefs, pack = pl.pallas_call(
         functools.partial(weights_kernel, layout),
@@ -568,28 +598,35 @@
             vm((2 * width, nodes * SK), bf16),
             shaped((LANES, SK), f32),
         ),
-        in_specs=[spec()] * 5,
+        in_specs=[spec(pl.ANY)] + [spec()] * 4,
         out_specs=(spec(),) * 3,
-        scratch_shapes=[vm((rows // LOW * width, rows), bf16), vm((rows, LOW), bf16)],
+        scratch_shapes=[
+            vm((rows // LOW * width, rows), bf16),
+            vm((rows, LOW), bf16),
+            vm((blocks, rows, SK), bf16),
+            pltpu.SemaphoreType.DMA((blocks,)),
+        ],
         compiler_params=params(40),
         name="tree_weights",
-    )(held(base), held(upper_tiles), held(top), held(slots), light)
+    )(in_hbm(base), held(upper_tiles), held(top), held(slots), light)
 
     packs = upper_levels(pack, skeleton_upper, my_leaf, trees, blocks, width)
 
     near = pl.pallas_call(
         near_kernel,
         out_shape=vm((width, total), f32),
-        in_specs=[spec(SMEM)] * 2 + [spec()] * 3,
+        in_specs=[spec(SMEM)] * 2 + [spec(pl.ANY)] + [spec()] * 2,
         out_specs=spec(),
         scratch_shapes=[
             pltpu.SMEM((leaves,), jnp.int32),
             pltpu.SMEM((3, leaves * leaves + 1), jnp.int32),
-            vm((LEAF, LEAF // 2), f32),
+            vm((total, FEAT), bf16),
+            vm((FEAT, total), bf16),
+            pltpu.SemaphoreType.DMA(()),
         ],
         compiler_params=params(40),
         name="near",
-    )(near_count, near_list[0], held(feat_a), held(feat_bt), held(tree_light))
+    )(in_hbm(near_count), in_hbm(near_list[0]), in_hbm(feat_a), held(tree), held(tree_light))
 
     levels = low_levels + ups
     back = pl.pallas_call(
@@ -597,10 +634,10 @@
         out_shape=(arrive,) * layout.count,
         in_specs=[spec()] * 7,
         out_specs=(spec(),) * layout.count,
-        scratch_shapes=[vm((levels * SK, FEAT), bf16), vm((2 * width, levels * SK), bf16), vm((LOW, rows), bf16)],
+        scratch_shapes=[vm((levels * SK, FEAT), bf16), vm((2 * width, levels * SK), bf16), vm((LOW, rows), bf16), vm((FEAT, LEAF), bf16)],
         compiler_params=params(40),
         name="far",
-    )(packs, *[held(one) for one in (slots, info, feat_bt, sk, coefs, near)])
+    )(packs, *[held(one) for one in (slots, info, tree, sk, coefs, near)])
 
     if fine:
         back = swap_all(back)

time: 106 us -> 94.5 us (0.89)
  waiting for transfers between devices: 30.5 us -> 17.3 us
  local copies, waits for them, and re-layouts: 10.3 us -> 0.01 us
  Pallas kernels: 30.5 us -> 39.9 us
  starting transfers between devices: 33.1 us -> 35.3 us
    ppermute x3 -> x1, waiting for transfers between devices: 23 us -> 4.62 us  [body(): lax.ppermute(place[step ^ last], 'sub', [(i, i ^ last) for i in range(blo...]
    unnamed x32 -> x4, local copies, waits for them, and re-layouts: 10.3 us -> 0.01 us
    pallas_call x1, Pallas kernels: 12.2 us -> 19.2 us  [body(): pl.pallas_call(near_kernel, out_shape=vm((width, total), f32), in_specs=[...]
    ppermute x9 -> x11, starting transfers between devices: 15.7 us -> 22.3 us  [swap(): return lax.ppermute(value, axes, pairs)]
    ppermute x9 -> x11, waiting for transfers between devices: 6.56 us -> 11.3 us  [swap(): return lax.ppermute(value, axes, pairs)]
    ppermute x3 -> x1, starting transfers between devices: 6.3 us -> 2.02 us  [body(): lax.ppermute(place[step ^ last], 'sub', [(i, i ^ last) for i in range(blo...]
    pallas_call x1, Pallas kernels: 6 us -> 7.54 us  [body(): pl.pallas_call(functools.partial(points_kernel, layout, trees), out_shape...]
    all_to_all x1, starting transfers between devices: 6.25 us -> 4.78 us  [body(): lax.all_to_all(light, ('leaf', 'sub'), split_axis=0, concat_axis=0, tiled...]
  transfers between devices with their start and end apart: 18 -> 18, of which waited for: 7 -> 6; matrix products, arithmetic and copies ran while one was open for 0% -> 0% of each run, Pallas kernels for 17% -> 29%
where the time goes in v7:
time: 94.5 us; the launch traced here: 92.6 us
  Pallas kernels  39.9 us (42%)
  starting transfers between devices  35.3 us (37%)
  waiting for transfers between devices  17.3 us (18%)
    ppermute x11, starting transfers between devices, swap(): return lax.ppermute(value, axes, pairs)  22.3 us
    pallas_call x1, Pallas kernels, body(): pl.pallas_call(near_kernel, out_shape=vm((width, total), f32), in_specs=[...  19.2 us
    ppermute x11, waiting for transfers between devices, swap(): return lax.ppermute(value, axes, pairs)  11.3 us
    pallas_call x1, Pallas kernels, body(): pl.pallas_call(functools.partial(points_kernel, layout, trees), out_shape...  7.54 us
    all_to_all x1, starting transfers between devices, body(): lax.all_to_all(light, ('leaf', 'sub'), split_axis=0, concat_axis=0, tiled...  4.78 us
    ppermute x1, waiting for transfers between devices, body(): lax.ppermute(place[step ^ last], 'sub', [(i, i ^ last) for i in range(blo...  4.62 us
    ppermute x4, starting transfers between devices, body(): lax.ppermute(one, 'rep', [(0, 1), (1, 0)])  4.34 us
    pallas_call x1, Pallas kernels, body(): pl.pallas_call(functools.partial(far_kernel, layout, low_levels), out_sha...  4.24 us
  transfers between devices with their start and end apart: 18, of which 6 were waited for; matrix products, arithmetic and copies ran while one was open for 0% of the time, Pallas kernels for 29%

profile of v7, /device:TPU:0, one launch (start us, length us, event | category | flops | bytes accessed | tf_op | source)
XLA Modules:
  0.0 92.6 jit_solution(9259742945087761143)
XLA Ops:
  0.0 3.7 %sort_rows.1 = (f32[72,512]{1,0:T(8,128)}, f32[8,128]{1,0:T(8,128)}, f32[2,128,512]{2,1,0:T(8,128)}) custom-call(s32[8,128]{1,0:T(8,128)} %bitcast.8, f32[64,1024]{1,0:T(8,128)} %bitcast.7, f32[1024,128]{1,0:T(8,128)} %refs_8_.1, s32[1,128]{1,0:T(1,128)} %base_ref.1, s32[2,3]{1,0:T(2,128)} %flag_ref.1), custom_call_target="tpu_custom_call" | custom-call | tf_op jit(solution)/shard_map/sort_rows/pallas_call | solution.py:500
  3.7 4.0 %collective-permute-start.2 = (f32[72,512]{1,0:T(8,128)}, f32[72,512]{1,0:T(8,128)S(1)}, u32[]{:S(2)}, u32[]{:S(2)}) collective-permute-start(f32[72,512]{1,0:T(8,128)} %get-tuple-element.30), channel_id=1, source_target_pairs={{0,4},{1,13},{2,6},{3,15},{4,0},{5,9},{6,2},{7,11},{8,12},{9,5},{1... | collective-permute-start | bytes 442376 | tf_op jit(solution)/shard_map/ppermute | solution.py:527
  7.7 1.6 %collective-permute-start.1 = (f32[72,512]{1,0:T(8,128)}, f32[72,512]{1,0:T(8,128)S(1)}, u32[]{:S(2)}, u32[]{:S(2)}) collective-permute-start(f32[72,512]{1,0:T(8,128)} %get-tuple-element.30), channel_id=1, source_target_pairs={{0,2},{1,11},{2,0},{3,9},{4,6},{5,15},{6,4},{7,13},{8,10},{9,3},{1... | collective-permute-start | bytes 442376 | tf_op jit(solution)/shard_map/ppermute | solution.py:527
  9.3 6.5 %collective-permute-done.2.refs_2_ = f32[72,512]{1,0:T(8,128)S(1)} collective-permute-done((f32[72,512]{1,0:T(8,128)}, f32[72,512]{1,0:T(8,128)S(1)}, u32[]{:S(2)}, u32[]{:S(2)}) %collective-permute-start.2) | collective-permute-done | bytes 147488 | tf_op jit(solution)/shard_map/ppermute | solution.py:527
  16.0 4.8 %all-to-all-start = ((f32[8,32,512]{2,1,0:T(8,128)}), f32[8,32,512]{2,1,0:T(8,128)S(1)}, u32[]{:S(2)}, u32[]{:S(2)}) async-start(f32[8,32,512]{2,1,0:T(8,128)} %bitcast.6), calls=%async_computation | async-start | bytes 1048576 | tf_op jit(solution)/shard_map/all_to_all | solution.py:551
  20.8 1.6 %collective-permute-start = (f32[72,512]{1,0:T(8,128)}, f32[72,512]{1,0:T(8,128)S(1)}, u32[]{:S(2)}, u32[]{:S(2)}) collective-permute-start(f32[72,512]{1,0:T(8,128)} %get-tuple-element.30), channel_id=1, source_target_pairs={{0,0},{1,9},{2,2},{3,11},{4,4},{5,13},{6,6},{7,15},{8,8},{9,1},{10... | collective-permute-start | bytes 442376 | tf_op jit(solution)/shard_map/ppermute | solution.py:527
  22.4 2.0 %collective-permute-start.3 = (f32[72,512]{1,0:T(8,128)S(1)}, f32[72,512]{1,0:T(8,128)S(1)}, u32[]{:S(2)}, u32[]{:S(2)}) collective-permute-start(f32[72,512]{1,0:T(8,128)S(1)} %collective-permute-done.2.refs_2_), channel_id=1, source_target_pairs={{0,2},{2,0},{4,6},{6,4},{1,3},{3,1},{5,7},{7,5},{8,10},{10,8},{12,... | collective-permute-start | bytes 442376 | tf_op jit(solution)/shard_map/ppermute | solution.py:546
  25.7 3.0 %collective-permute-start.4 = (f32[72,512]{1,0:T(8,128)S(1)}, f32[72,512]{1,0:T(8,128)S(1)}, u32[]{:S(2)}, u32[]{:S(2)}) collective-permute-start(f32[72,512]{1,0:T(8,128)S(1)} %collective-permute-done.refs_0_), channel_id=1, source_target_pairs={{0,1},{1,0},{2,3},{3,2},{4,5},{5,4},{6,7},{7,6},{8,9},{9,8},{10,11... | collective-permute-start | bytes 442376 | tf_op jit(solution)/shard_map/ppermute | solution.py:549
  28.7 4.6 %collective-permute-done.3.refs_3_ = f32[72,512]{1,0:T(8,128)S(1)} collective-permute-done((f32[72,512]{1,0:T(8,128)S(1)}, f32[72,512]{1,0:T(8,128)S(1)}, u32[]{:S(2)}, u32[]{:S(2)}) %collective-permute-start.3) | collective-permute-done | bytes 147488 | tf_op jit(solution)/shard_map/ppermute | solution.py:546
  33.4 1.3 %collective-permute-done.7.refs_7_ = f32[72,512]{1,0:T(8,128)S(1)} collective-permute-done((f32[72,512]{1,0:T(8,128)S(1)}, f32[72,512]{1,0:T(8,128)S(1)}, u32[]{:S(2)}, u32[]{:S(2)}) %collective-permute-start.7) | collective-permute-done | bytes 147488 | tf_op jit(solution)/shard_map/ppermute | solution.py:549
  34.7 7.5 %tree_points.1 = (bf16[144,4096]{1,0:T(8,128)(2,1)S(1)}, bf16[4096,256]{1,0:T(8,128)(2,1)}, bf16[4,1024,128]{2,1,0:T(8,128)(2,1)}, bf16[896,256]{1,0:T(8,128)(2,...) custom-call(s32[6,128]{1,0:T(8,128)} %upper_ref.1, ...), custom_call_target="tpu_custom_call" | custom-call | tf_op jit(solution)/shard_map/tree_points/pallas_call | solution.py:567
  42.3 3.3 %tree_weights.1 = (bf16[32,4096]{1,0:T(8,128)(2,1)S(1)}, bf16[64,896]{1,0:T(8,128)(2,1)S(1)}, f32[128,128]{1,0:T(8,128)S(1)}) custom-call(bf16[4,1024,128]{2,1,0:T(8,128)(2,1)} %get-tuple-element.33.base_hbm, f32[3,256,128]{2,1,0:T(8,128)S(1)} %get-tuple-element.34.upper_tiles_ref, f32[128,128]{1,0:T(8,128)S(1)} %get-tuple-element.35.top_ref, ...), custom_call_target="tpu_custom_call" | custom-call | tf_op jit(solution)/shard_map/tree_weights/pallas_call | solution.py:594
  45.6 1.8 %collective-permute-start.8 = (f32[128,128]{1,0:T(8,128)S(1)}, f32[128,128]{1,0:T(8,128)S(1)}, u32[]{:S(2)}, u32[]{:S(2)}) collective-permute-start(f32[128,128]{1,0:T(8,128)S(1)} %get-tuple-element.38), channel_id=1, source_target_pairs={{0,8},{8,0},{1,9},{9,1},{2,10},{10,2},{3,11},{11,3},{4,12},{12,4},... | collective-permute-start | bytes 196616 | tf_op jit(solution)/shard_map/ppermute | solution.py:464
  47.4 19.2 %near.1.near_ref = f32[32,4096]{1,0:T(8,128)S(1)} custom-call(s32[1,8]{1,0:T(1,128)} %count_ref.1, s32[8,16]{1,0:T(8,128)} %bitcast.9, bf16[4096,256]{1,0:T(8,128)(2,1)} %get-tuple-element.43.a_hbm, bf16[144,4096]{1,0:T(8,128)(2,1)S(1)} %get-tuple-element.40.tree_ref, bf16[32,4096]{1,0:T(8,128)(2,1)S(1)} %get-tuple-element.44.w_ref), custom_call_target="tpu_custom_call" | custom-call | tf_op jit(solution)/shard_map/near/pallas_call | solution.py:615
  66.7 4.2 %far.1 = (f32[32,512]{1,0:T(8,128)S(1)}, f32[32,512]{1,0:T(8,128)S(1)}, f32[32,512]{1,0:T(8,128)S(1)}, f32[32,512]{1,0:T(8,128)S(1)}, f32[32,512]{1,0:T(8,128)S(...) custom-call(f32[1,128,128]{2,1,0:T(8,128)S(1)} %bitcast.5, ...), custom_call_target="tpu_custom_call" | custom-call | tf_op jit(solution)/shard_map/far/pallas_call | solution.py:632
  71.6 2.6 %collective-permute-start.10 = (f32[32,512]{1,0:T(8,128)S(1)}, f32[32,512]{1,0:T(8,128)S(1)}, u32[]{:S(2)}, u32[]{:S(2)}) collective-permute-start(f32[32,512]{1,0:T(8,128)S(1)} %get-tuple-element.46), channel_id=1, source_target_pairs={{0,2},{1,11},{2,0},{3,9},{4,6},{5,15},{6,4},{7,13},{8,10},{9,3},{1... | collective-permute-start | bytes 196616 | tf_op jit(solution)/shard_map/ppermute | solution.py:527
  74.1 2.3 %collective-permute-start.11 = (f32[32,512]{1,0:T(8,128)S(1)}, f32[32,512]{1,0:T(8,128)S(1)}, u32[]{:S(2)}, u32[]{:S(2)}) collective-permute-start(f32[32,512]{1,0:T(8,128)S(1)} %get-tuple-element.47), channel_id=1, source_target_pairs={{0,4},{1,13},{2,6},{3,15},{4,0},{5,9},{6,2},{7,11},{8,12},{9,5},{1... | collective-permute-start | bytes 196616 | tf_op jit(solution)/shard_map/ppermute | solution.py:527
  77.4 1.9 %collective-permute-start.13 = (f32[32,512]{1,0:T(8,128)S(1)}, f32[32,512]{1,0:T(8,128)S(1)}, u32[]{:S(2)}, u32[]{:S(2)}) collective-permute-start(f32[32,512]{1,0:T(8,128)S(1)} %get-tuple-element.49), channel_id=1, source_target_pairs={{0,8},{1,1},{2,10},{3,3},{4,12},{5,5},{6,14},{7,7},{8,0},{9,9},{10... | collective-permute-start | bytes 196616 | tf_op jit(solution)/shard_map/ppermute | solution.py:527
  79.3 2.1 %collective-permute-start.14 = (f32[32,512]{1,0:T(8,128)S(1)}, f32[32,512]{1,0:T(8,128)S(1)}, u32[]{:S(2)}, u32[]{:S(2)}) collective-permute-start(f32[32,512]{1,0:T(8,128)S(1)} %get-tuple-element.50), channel_id=1, source_target_pairs={{0,10},{1,3},{2,8},{3,1},{4,14},{5,7},{6,12},{7,5},{8,2},{9,11},{1... | collective-permute-start | bytes 196616 | tf_op jit(solution)/shard_map/ppermute | solution.py:527
  81.4 2.3 %collective-permute-start.15 = (f32[32,512]{1,0:T(8,128)S(1)}, f32[32,512]{1,0:T(8,128)S(1)}, u32[]{:S(2)}, u32[]{:S(2)}) collective-permute-start(f32[32,512]{1,0:T(8,128)S(1)} %get-tuple-element.51), channel_id=1, source_target_pairs={{0,12},{1,5},{2,14},{3,7},{4,8},{5,1},{6,10},{7,3},{8,4},{9,13},{1... | collective-permute-start | bytes 196616 | tf_op jit(solution)/shard_map/ppermute | solution.py:527
  83.7 2.4 %collective-permute-start.16 = (f32[32,512]{1,0:T(8,128)S(1)}, f32[32,512]{1,0:T(8,128)S(1)}, u32[]{:S(2)}, u32[]{:S(2)}) collective-permute-start(f32[32,512]{1,0:T(8,128)S(1)} %get-tuple-element.52), channel_id=1, source_target_pairs={{0,14},{1,7},{2,12},{3,5},{4,10},{5,3},{6,8},{7,1},{8,6},{9,15},{1... | collective-permute-start | bytes 196616 | tf_op jit(solution)/shard_map/ppermute | solution.py:527
  86.1 1.6 %collective-permute-done.15.refs_6_ = f32[32,512]{1,0:T(8,128)S(1)} collective-permute-done((f32[32,512]{1,0:T(8,128)S(1)}, f32[32,512]{1,0:T(8,128)S(1)}, u32[]{:S(2)}, u32[]{:S(2)}) %collective-permute-start.15) | collective-permute-done | bytes 65568 | tf_op jit(solution)/shard_map/ppermute | solution.py:527
  87.7 3.0 %collective-permute-done.16.refs_7_ = f32[32,512]{1,0:T(8,128)S(1)} collective-permute-done((f32[32,512]{1,0:T(8,128)S(1)}, f32[32,512]{1,0:T(8,128)S(1)}, u32[]{:S(2)}, u32[]{:S(2)}) %collective-permute-start.16) | collective-permute-done | bytes 65568 | tf_op jit(solution)/shard_map/ppermute | solution.py:527
  90.7 1.9 %to_input_order.1 = f32[1024,128]{1,0:T(8,128)} custom-call(f32[8,128]{1,0:T(8,128)S(1)} %copy-done.1, f32[32,512]{1,0:T(8,128)S(1)} %collective-permute-done.9.refs_0_, f32[32,512]{1,0:T(8,128)S(1)} %collective-permute-done.10.refs_1_, f32[32,512]{1,0:T(8,128)S(1)} %collective-permute-done.11.refs_2_, f32[32,512]{1,0:T(8,128)S(1)} %collective-permute-done.12.refs_3_, ...), custom_call_target="tpu_custom_call" | custom-call | tf_op jit(solution)/shard_map/to_input_order/pallas_call | solution.py:649
  (22 shorter events, 3.3 us)
Async XLA Ops:
  3.7 12.1 %collective-permute-start.2 = (f32[72,512]{1,0:T(8,128)}, f32[72,512]{1,0:T(8,128)S(1)}, u32[]{:S(2)}, u32[]{:S(2)}) collective-permute-start(f32[72,512]{1,0:T(8,128)} %get-tuple-element.30), channel_id=1, source_target_pairs={{0,4},{1,13},{2,6},{3,15},{4,0},{5,9},{6,2},{7,11},{8,12},{9,5},{1... | collective-permute-start | bytes 442376 | tf_op jit(solution)/shard_map/ppermute | solution.py:527
  7.7 8.3 %collective-permute-start.1 = (f32[72,512]{1,0:T(8,128)}, f32[72,512]{1,0:T(8,128)S(1)}, u32[]{:S(2)}, u32[]{:S(2)}) collective-permute-start(f32[72,512]{1,0:T(8,128)} %get-tuple-element.30), channel_id=1, source_target_pairs={{0,2},{1,11},{2,0},{3,9},{4,6},{5,15},{6,4},{7,13},{8,10},{9,3},{1... | collective-permute-start | bytes 442376 | tf_op jit(solution)/shard_map/ppermute | solution.py:527
  16.0 26.2 %all-to-all-start = ((f32[8,32,512]{2,1,0:T(8,128)}), f32[8,32,512]{2,1,0:T(8,128)S(1)}, u32[]{:S(2)}, u32[]{:S(2)}) async-start(f32[8,32,512]{2,1,0:T(8,128)} %bitcast.6), calls=%async_computation | async-start | bytes 1048576 | tf_op jit(solution)/shard_map/all_to_all | solution.py:551
  20.8 4.9 %collective-permute-start = (f32[72,512]{1,0:T(8,128)}, f32[72,512]{1,0:T(8,128)S(1)}, u32[]{:S(2)}, u32[]{:S(2)}) collective-permute-start(f32[72,512]{1,0:T(8,128)} %get-tuple-element.30), channel_id=1, source_target_pairs={{0,0},{1,9},{2,2},{3,11},{4,4},{5,13},{6,6},{7,15},{8,8},{9,1},{10... | collective-permute-start | bytes 442376 | tf_op jit(solution)/shard_map/ppermute | solution.py:527
  22.4 11.0 %collective-permute-start.3 = (f32[72,512]{1,0:T(8,128)S(1)}, f32[72,512]{1,0:T(8,128)S(1)}, u32[]{:S(2)}, u32[]{:S(2)}) collective-permute-start(f32[72,512]{1,0:T(8,128)S(1)} %collective-permute-done.2.refs_2_), channel_id=1, source_target_pairs={{0,2},{2,0},{4,6},{6,4},{1,3},{3,1},{5,7},{7,5},{8,10},{10,8},{12,... | collective-permute-start | bytes 442376 | tf_op jit(solution)/shard_map/ppermute | solution.py:546
  24.4 9.0 %collective-permute-start.5 = (f32[72,512]{1,0:T(8,128)S(1)}, f32[72,512]{1,0:T(8,128)S(1)}, u32[]{:S(2)}, u32[]{:S(2)}) collective-permute-start(f32[72,512]{1,0:T(8,128)S(1)} %collective-permute-done.1.refs_1_), channel_id=1, source_target_pairs={{0,1},{1,0},{2,3},{3,2},{4,5},{5,4},{6,7},{7,6},{8,9},{9,8},{10,11... | collective-permute-start | bytes 442376 | tf_op jit(solution)/shard_map/ppermute | solution.py:549
  25.7 7.7 %collective-permute-start.6 = (f32[72,512]{1,0:T(8,128)S(1)}, f32[72,512]{1,0:T(8,128)S(1)}, u32[]{:S(2)}, u32[]{:S(2)}) collective-permute-start(f32[72,512]{1,0:T(8,128)S(1)} %collective-permute-done.2.refs_2_), channel_id=1, source_target_pairs={{0,1},{1,0},{2,3},{3,2},{4,5},{5,4},{6,7},{7,6},{8,9},{9,8},{10,11... | collective-permute-start | bytes 442376 | tf_op jit(solution)/shard_map/ppermute | solution.py:549
  25.7 7.7 %collective-permute-start.4 = (f32[72,512]{1,0:T(8,128)S(1)}, f32[72,512]{1,0:T(8,128)S(1)}, u32[]{:S(2)}, u32[]{:S(2)}) collective-permute-start(f32[72,512]{1,0:T(8,128)S(1)} %collective-permute-done.refs_0_), channel_id=1, source_target_pairs={{0,1},{1,0},{2,3},{3,2},{4,5},{5,4},{6,7},{7,6},{8,9},{9,8},{10,11... | collective-permute-start | bytes 442376 | tf_op jit(solution)/shard_map/ppermute | solution.py:549
  33.4 1.4 %collective-permute-start.7 = (f32[72,512]{1,0:T(8,128)S(1)}, f32[72,512]{1,0:T(8,128)S(1)}, u32[]{:S(2)}, u32[]{:S(2)}) collective-permute-start(f32[72,512]{1,0:T(8,128)S(1)} %collective-permute-done.3.refs_3_), channel_id=1, source_target_pairs={{0,1},{1,0},{2,3},{3,2},{4,5},{5,4},{6,7},{7,6},{8,9},{9,8},{10,11... | collective-permute-start | bytes 442376 | tf_op jit(solution)/shard_map/ppermute | solution.py:549
  45.6 21.0 %collective-permute-start.8 = (f32[128,128]{1,0:T(8,128)S(1)}, f32[128,128]{1,0:T(8,128)S(1)}, u32[]{:S(2)}, u32[]{:S(2)}) collective-permute-start(f32[128,128]{1,0:T(8,128)S(1)} %get-tuple-element.38), channel_id=1, source_target_pairs={{0,8},{8,0},{1,9},{9,1},{2,10},{10,2},{3,11},{11,3},{4,12},{12,4},... | collective-permute-start | bytes 196616 | tf_op jit(solution)/shard_map/ppermute | solution.py:464
  66.6 24.0 %copy-start = (f32[1024,128]{1,0:T(8,128)S(1)}, f32[1024,128]{1,0:T(8,128)}, u32[]{:S(2)}) copy-start(f32[1024,128]{1,0:T(8,128)} %refs_8_.1) | copy-start | bytes 1572868
  66.6 24.0 %copy-start.1 = (f32[8,128]{1,0:T(8,128)S(1)}, f32[8,128]{1,0:T(8,128)}, u32[]{:S(2)}) copy-start(f32[8,128]{1,0:T(8,128)} %get-tuple-element.29.pos_ref) | copy-start | bytes 12292
  70.9 8.4 %collective-permute-start.9 = (f32[32,512]{1,0:T(8,128)S(1)}, f32[32,512]{1,0:T(8,128)S(1)}, u32[]{:S(2)}, u32[]{:S(2)}) collective-permute-start(f32[32,512]{1,0:T(8,128)S(1)} %get-tuple-element.45), channel_id=1, source_target_pairs={{0,0},{1,9},{2,2},{3,11},{4,4},{5,13},{6,6},{7,15},{8,8},{9,1},{10... | collective-permute-start | bytes 196616 | tf_op jit(solution)/shard_map/ppermute | solution.py:527
  71.6 9.8 %collective-permute-start.10 = (f32[32,512]{1,0:T(8,128)S(1)}, f32[32,512]{1,0:T(8,128)S(1)}, u32[]{:S(2)}, u32[]{:S(2)}) collective-permute-start(f32[32,512]{1,0:T(8,128)S(1)} %get-tuple-element.46), channel_id=1, source_target_pairs={{0,2},{1,11},{2,0},{3,9},{4,6},{5,15},{6,4},{7,13},{8,10},{9,3},{1... | collective-permute-start | bytes 196616 | tf_op jit(solution)/shard_map/ppermute | solution.py:527
  74.1 9.6 %collective-permute-start.11 = (f32[32,512]{1,0:T(8,128)S(1)}, f32[32,512]{1,0:T(8,128)S(1)}, u32[]{:S(2)}, u32[]{:S(2)}) collective-permute-start(f32[32,512]{1,0:T(8,128)S(1)} %get-tuple-element.47), channel_id=1, source_target_pairs={{0,4},{1,13},{2,6},{3,15},{4,0},{5,9},{6,2},{7,11},{8,12},{9,5},{1... | collective-permute-start | bytes 196616 | tf_op jit(solution)/shard_map/ppermute | solution.py:527
  76.4 9.7 %collective-permute-start.12 = (f32[32,512]{1,0:T(8,128)S(1)}, f32[32,512]{1,0:T(8,128)S(1)}, u32[]{:S(2)}, u32[]{:S(2)}) collective-permute-start(f32[32,512]{1,0:T(8,128)S(1)} %get-tuple-element.48), channel_id=1, source_target_pairs={{0,6},{1,15},{2,4},{3,13},{4,2},{5,11},{6,0},{7,9},{8,14},{9,7},{1... | collective-permute-start | bytes 196616 | tf_op jit(solution)/shard_map/ppermute | solution.py:527
  77.4 8.7 %collective-permute-start.13 = (f32[32,512]{1,0:T(8,128)S(1)}, f32[32,512]{1,0:T(8,128)S(1)}, u32[]{:S(2)}, u32[]{:S(2)}) collective-permute-start(f32[32,512]{1,0:T(8,128)S(1)} %get-tuple-element.49), channel_id=1, source_target_pairs={{0,8},{1,1},{2,10},{3,3},{4,12},{5,5},{6,14},{7,7},{8,0},{9,9},{10... | collective-permute-start | bytes 196616 | tf_op jit(solution)/shard_map/ppermute | solution.py:527
  79.3 6.8 %collective-permute-start.14 = (f32[32,512]{1,0:T(8,128)S(1)}, f32[32,512]{1,0:T(8,128)S(1)}, u32[]{:S(2)}, u32[]{:S(2)}) collective-permute-start(f32[32,512]{1,0:T(8,128)S(1)} %get-tuple-element.50), channel_id=1, source_target_pairs={{0,10},{1,3},{2,8},{3,1},{4,14},{5,7},{6,12},{7,5},{8,2},{9,11},{1... | collective-permute-start | bytes 196616 | tf_op jit(solution)/shard_map/ppermute | solution.py:527
  81.4 6.3 %collective-permute-start.15 = (f32[32,512]{1,0:T(8,128)S(1)}, f32[32,512]{1,0:T(8,128)S(1)}, u32[]{:S(2)}, u32[]{:S(2)}) collective-permute-start(f32[32,512]{1,0:T(8,128)S(1)} %get-tuple-element.51), channel_id=1, source_target_pairs={{0,12},{1,5},{2,14},{3,7},{4,8},{5,1},{6,10},{7,3},{8,4},{9,13},{1... | collective-permute-start | bytes 196616 | tf_op jit(solution)/shard_map/ppermute | solution.py:527
  83.7 7.0 %collective-permute-start.16 = (f32[32,512]{1,0:T(8,128)S(1)}, f32[32,512]{1,0:T(8,128)S(1)}, u32[]{:S(2)}, u32[]{:S(2)}) collective-permute-start(f32[32,512]{1,0:T(8,128)S(1)} %get-tuple-element.52), channel_id=1, source_target_pairs={{0,14},{1,7},{2,12},{3,5},{4,10},{5,3},{6,8},{7,1},{8,6},{9,15},{1... | collective-permute-start | bytes 196616 | tf_op jit(solution)/shard_map/ppermute | solution.py:527

commit v8 on v7

--- a/solution.py
+++ b/solution.py
@@ -320,7 +320,7 @@
         start, count = start + count, count // 2
 
 
-def near_kernel(count_ref, list_ref, a_hbm, tree_ref, w_ref, acc, times, tiles, a_ref, bt_ref, sem):
+def near_kernel(count_ref, list_ref, a_hbm, tree_ref, w_ref, acc, times, tiles, a_ref, bt_ref, sem, *halves):
     every = count_ref.shape[1]
     copy = pltpu.make_async_copy(a_hbm, a_ref, sem)
     copy.start()
@@ -346,14 +346,17 @@
         return filled
 
     filled = lax.fori_loop(0, every, tally, jnp.int32(0))
-    tiles[0, filled] = 0
-    tiles[1, filled] = 0
-    tiles[2, filled] = 0
+    for more in range(2):
+        tiles[0, filled + more] = 0
+        tiles[1, filled + more] = 0
     half = LEAF // 2
     acc[...] = jnp.zeros_like(acc)
 
     def target(tile, part):
         return aligned(tiles[0, tile] * LEAF + part * half, half, half)
+
+    even, odd = halves[0:2], halves[2:4]
+    even_tile, odd_tile = halves[4:6], halves[6:8]
 
     def exponents(tile, part):
         source = aligned(tiles[1, tile] * LEAF, LEAF, LEAF)
@@ -361,17 +364,35 @@
 
     def add(tile, part, block):
         source = aligned(tiles[1, tile] * LEAF, LEAF, LEAF)
-        acc[:, target(tile, part)] += tiles[2, tile].astype(f32) * nn(w_ref[:, source], block)
+        acc[:, target(tile, part)] += tiles[2, tile].astype(f32) * nn(w_ref[:, source], block[part][...])
+
+    def phase(tile, upcoming, ready, made, previous):
+        for part in range(2):
+            upcoming[part][...] = exponents(tile + 1, part)
+            made[part][...] = jnp.exp(ready[part][...]).astype(bf16)
+            add(tile - 1, part, previous)
 
     copy.wait()
+    for part in range(2):
+        even[part][...] = exponents(0, part)
+        even_tile[part][...] = jnp.exp(even[part][...]).astype(bf16)
+        odd[part][...] = exponents(1, part)
 
     def step(pair, carry):
-        for tile in (2 * pair, 2 * pair + 1):
-            for part in range(2):
-                add(tile, part, jnp.exp(exponents(tile, part)).astype(bf16))
+        phase(2 * pair + 1, even, odd, odd_tile, even_tile)
+        phase(2 * pair + 2, odd, even, even_tile, odd_tile)
         return carry
 
-    lax.fori_loop(0, (filled + 1) // 2, step, 0)
+    lax.fori_loop(0, (filled - 1) // 2, step, 0)
+    done = 2 * ((filled - 1) // 2)
+    for part in range(2):
+        add(done, part, even_tile)
+
+    @pl.when(done + 1 < filled)
+    def _():
+        for part in range(2):
+            odd_tile[part][...] = jnp.exp(odd[part][...]).astype(bf16)
+            add(done + 1, part, odd_tile)
 
 
 def far_kernel(layout, low_levels, pack_ref, slot_ref, info_ref, tree_ref, sk_ref, coef_ref, near_ref, *refs):
@@ -533,20 +554,15 @@
         return [done[g] for g in range(len(values))]
 
     if fine:
-        sent, far_off = place, blocks // 2
-        place = {far_off: swap(sent, far_off)}
-        step = 1
-        while step < far_off:
-            place[step] = swap(sent, step)
-            step *= 2
-        place[0] = swap(sent, 0)
-        for step in range(1, blocks):
-            if step not in place:
-                last = step & -step
-                place[step] = lax.ppermute(place[step ^ last], "sub", [(i, i ^ last) for i in range(blocks)])
-        place[1], tied, light = lax.optimization_barrier((place[1], place[far_off], light))
-        place = [place[step] for step in range(blocks)]
-        place = place + [lax.ppermute(one, "rep", [(0, 1), (1, 0)]) for one in place]
+        place = {0: swap(place, 0)}
+        stride = blocks // 2
+        while stride:
+            for step in sorted(place):
+                place[step | stride] = lax.ppermute(place[step], "sub", [(i, i ^ stride) for i in range(blocks)])
+            stride //= 2
+        theirs = {step: lax.ppermute(one, "rep", [(0, 1), (1, 0)]) for step, one in place.items()}
+        theirs[blocks // 2], light = lax.optimization_barrier((theirs[blocks // 2], light))
+        place = [place[step] for step in range(blocks)] + [theirs[step] for step in range(blocks)]
         light = light.reshape(devices, width, part)
         light = lax.all_to_all(light, ("leaf", "sub"), split_axis=0, concat_axis=0, tiled=True)
         small = []
@@ -619,11 +635,13 @@
         out_specs=spec(),
         scratch_shapes=[
             pltpu.SMEM((leaves,), jnp.int32),
-            pltpu.SMEM((3, leaves * leaves + 1), jnp.int32),
+            pltpu.SMEM((3, leaves * leaves + 2), jnp.int32),
             vm((total, FEAT), bf16),
             vm((FEAT, total), bf16),
             pltpu.SemaphoreType.DMA(()),
-        ],
+        ]
+        + [vm((LEAF, LEAF // 2), f32)] * 4
+        + [vm((LEAF, LEAF // 2), bf16)] * 4,
         compiler_params=params(40),
         name="near",
     )(in_hbm(near_count), in_hbm(near_list[0]), in_hbm(feat_a), held(tree), held(tree_light))

time: 94.5 us -> 91.5 us (0.968); the launches traced: 92.6 us -> 91.3 us
  waiting for transfers between devices: 17.3 us -> 27.2 us
  Pallas kernels: 39.9 us -> 31.4 us
  starting transfers between devices: 35.3 us -> 32.6 us
    ppermute x1 -> x3, waiting for transfers between devices: 4.62 us -> 20.2 us  [body(): lax.ppermute(place[step], 'sub', [(i, i ^ stride) for i in range(blocks)])]
    pallas_call x1, Pallas kernels: 19.2 us -> 10.7 us  [body(): pl.pallas_call(near_kernel, out_shape=vm((width, total), f32), in_specs=[...]
    ppermute x11 -> x9, starting transfers between devices: 22.3 us -> 15.4 us  [swap(): return lax.ppermute(value, axes, pairs)]
    ppermute x11 -> x9, waiting for transfers between devices: 11.3 us -> 4.56 us  [swap(): return lax.ppermute(value, axes, pairs)]
    ppermute x1 -> x3, starting transfers between devices: 2.02 us -> 6.1 us  [body(): lax.ppermute(place[step], 'sub', [(i, i ^ stride) for i in range(blocks)])]
    ppermute x4, waiting for transfers between devices: 1.36 us -> 2.37 us  [body(): lax.ppermute(one, 'rep', [(0, 1), (1, 0)])]
    all_to_all x1, starting transfers between devices: 4.78 us -> 5.76 us  [body(): lax.all_to_all(light, ('leaf', 'sub'), split_axis=0, concat_axis=0, tiled...]
  transfers between devices with their start and end apart: 18 -> 18, of which waited for: 6 -> 7; matrix products, arithmetic and copies ran while one was open for 0% -> 0% of each run, Pallas kernels for 29% -> 20%
where the time goes in v8:
time: 91.5 us; the launch traced here: 91.3 us
  starting transfers between devices  32.6 us (36%)
  Pallas kernels  31.4 us (34%)
  waiting for transfers between devices  27.2 us (30%)
    ppermute x3, waiting for transfers between devices, body(): lax.ppermute(place[step], 'sub', [(i, i ^ stride) for i in range(blocks)])  20.2 us
    ppermute x9, starting transfers between devices, swap(): return lax.ppermute(value, axes, pairs)  15.4 us
    pallas_call x1, Pallas kernels, body(): pl.pallas_call(near_kernel, out_shape=vm((width, total), f32), in_specs=[...  10.7 us
    pallas_call x1, Pallas kernels, body(): pl.pallas_call(functools.partial(points_kernel, layout, trees), out_shape...  7.54 us
    ppermute x3, starting transfers between devices, body(): lax.ppermute(place[step], 'sub', [(i, i ^ stride) for i in range(blocks)])  6.1 us
    all_to_all x1, starting transfers between devices, body(): lax.all_to_all(light, ('leaf', 'sub'), split_axis=0, concat_axis=0, tiled...  5.76 us
    ppermute x9, waiting for transfers between devices, swap(): return lax.ppermute(value, axes, pairs)  4.56 us
    pallas_call x1, Pallas kernels, body(): pl.pallas_call(functools.partial(far_kernel, layout, low_levels), out_sha...  4.23 us
  transfers between devices with their start and end apart: 18, of which 7 were waited for; matrix products, arithmetic and copies ran while one was open for 0% of the time, Pallas kernels for 20%

profile of v8, /device:TPU:0, one launch (start us, length us, event | category | flops | bytes accessed | tf_op | source)
XLA Modules:
  0.0 91.3 jit_solution(6205538147521497283)
XLA Ops:
  0.0 3.7 %sort_rows.1 = (f32[72,512]{1,0:T(8,128)}, f32[8,128]{1,0:T(8,128)}, f32[2,128,512]{2,1,0:T(8,128)}) custom-call(s32[8,128]{1,0:T(8,128)} %bitcast.8, f32[64,1024]{1,0:T(8,128)} %bitcast.7, f32[1024,128]{1,0:T(8,128)} %refs_8_.1, s32[1,128]{1,0:T(1,128)} %base_ref.1, s32[2,3]{1,0:T(2,128)} %flag_ref.1), custom_call_target="tpu_custom_call" | custom-call | tf_op jit(solution)/shard_map/sort_rows/pallas_call | solution.py:521
  3.7 1.6 %collective-permute-start = (f32[72,512]{1,0:T(8,128)}, f32[72,512]{1,0:T(8,128)S(1)}, u32[]{:S(2)}, u32[]{:S(2)}) collective-permute-start(f32[72,512]{1,0:T(8,128)} %get-tuple-element.30), channel_id=1, source_target_pairs={{0,0},{1,9},{2,2},{3,11},{4,4},{5,13},{6,6},{7,15},{8,8},{9,1},{10... | collective-permute-start | bytes 442376 | tf_op jit(solution)/shard_map/ppermute | solution.py:548
  5.2 4.0 %collective-permute-start.2 = (f32[72,512]{1,0:T(8,128)S(1)}, f32[72,512]{1,0:T(8,128)S(1)}, u32[]{:S(2)}, u32[]{:S(2)}) collective-permute-start(f32[72,512]{1,0:T(8,128)S(1)} %collective-permute-done.refs_0_), channel_id=1, source_target_pairs={{0,4},{2,6},{4,0},{6,2},{1,5},{3,7},{5,1},{7,3},{8,12},{10,14},{12... | collective-permute-start | bytes 442376 | tf_op jit(solution)/shard_map/ppermute | solution.py:561
  9.3 4.7 %collective-permute-done.2.refs_2_ = f32[72,512]{1,0:T(8,128)S(1)} collective-permute-done((f32[72,512]{1,0:T(8,128)S(1)}, f32[72,512]{1,0:T(8,128)S(1)}, u32[]{:S(2)}, u32[]{:S(2)}) %collective-permute-start.2) | collective-permute-done | bytes 147488 | tf_op jit(solution)/shard_map/ppermute | solution.py:561
  14.0 3.8 %collective-permute-start.6 = (f32[72,512]{1,0:T(8,128)S(1)}, f32[72,512]{1,0:T(8,128)S(1)}, u32[]{:S(2)}, u32[]{:S(2)}) collective-permute-start(f32[72,512]{1,0:T(8,128)S(1)} %collective-permute-done.2.refs_2_), channel_id=1, source_target_pairs={{0,1},{1,0},{2,3},{3,2},{4,5},{5,4},{6,7},{7,6},{8,9},{9,8},{10,11... | collective-permute-start | bytes 442376 | tf_op jit(solution)/shard_map/ppermute | solution.py:563
  17.7 1.0 %collective-permute-done.6.refs_6_ = f32[72,512]{1,0:T(8,128)S(1)} collective-permute-done((f32[72,512]{1,0:T(8,128)S(1)}, f32[72,512]{1,0:T(8,128)S(1)}, u32[]{:S(2)}, u32[]{:S(2)}) %collective-permute-start.6) | collective-permute-done | bytes 147488 | tf_op jit(solution)/shard_map/ppermute | solution.py:563
  18.7 5.8 %all-to-all-start = ((f32[8,32,512]{2,1,0:T(8,128)}), f32[8,32,512]{2,1,0:T(8,128)S(1)}, u32[]{:S(2)}, u32[]{:S(2)}) async-start(f32[8,32,512]{2,1,0:T(8,128)} %bitcast.6), calls=%async_computation | async-start | bytes 1048576 | tf_op jit(solution)/shard_map/all_to_all | solution.py:567
  24.5 2.0 %collective-permute-start.1 = (f32[72,512]{1,0:T(8,128)S(1)}, f32[72,512]{1,0:T(8,128)S(1)}, u32[]{:S(2)}, u32[]{:S(2)}) collective-permute-start(f32[72,512]{1,0:T(8,128)S(1)} %collective-permute-done.refs_0_), channel_id=1, source_target_pairs={{0,2},{2,0},{4,6},{6,4},{1,3},{3,1},{5,7},{7,5},{8,10},{10,8},{12,... | collective-permute-start | bytes 442376 | tf_op jit(solution)/shard_map/ppermute | solution.py:561
  26.6 13.3 %collective-permute-done.1.refs_1_ = f32[72,512]{1,0:T(8,128)S(1)} collective-permute-done((f32[72,512]{1,0:T(8,128)S(1)}, f32[72,512]{1,0:T(8,128)S(1)}, u32[]{:S(2)}, u32[]{:S(2)}) %collective-permute-start.1) | collective-permute-done | bytes 147488 | tf_op jit(solution)/shard_map/ppermute | solution.py:561
  39.8 2.3 %collective-permute-done.3.refs_3_ = f32[72,512]{1,0:T(8,128)S(1)} collective-permute-done((f32[72,512]{1,0:T(8,128)S(1)}, f32[72,512]{1,0:T(8,128)S(1)}, u32[]{:S(2)}, u32[]{:S(2)}) %collective-permute-start.3) | collective-permute-done | bytes 147488 | tf_op jit(solution)/shard_map/ppermute | solution.py:561
  42.1 1.4 %collective-permute-done.7.refs_7_ = f32[72,512]{1,0:T(8,128)S(1)} collective-permute-done((f32[72,512]{1,0:T(8,128)S(1)}, f32[72,512]{1,0:T(8,128)S(1)}, u32[]{:S(2)}, u32[]{:S(2)}) %collective-permute-start.7) | collective-permute-done | bytes 147488 | tf_op jit(solution)/shard_map/ppermute | solution.py:563
  43.5 7.5 %tree_points.1 = (bf16[144,4096]{1,0:T(8,128)(2,1)S(1)}, bf16[4096,256]{1,0:T(8,128)(2,1)}, bf16[4,1024,128]{2,1,0:T(8,128)(2,1)}, bf16[896,256]{1,0:T(8,128)(2,...) custom-call(s32[6,128]{1,0:T(8,128)} %upper_ref.1, ...), custom_call_target="tpu_custom_call" | custom-call | tf_op jit(solution)/shard_map/tree_points/pallas_call | solution.py:583
  51.1 3.3 %tree_weights.1 = (bf16[32,4096]{1,0:T(8,128)(2,1)S(1)}, bf16[64,896]{1,0:T(8,128)(2,1)S(1)}, f32[128,128]{1,0:T(8,128)S(1)}) custom-call(bf16[4,1024,128]{2,1,0:T(8,128)(2,1)} %get-tuple-element.33.base_hbm, f32[3,256,128]{2,1,0:T(8,128)S(1)} %get-tuple-element.34.upper_tiles_ref, f32[128,128]{1,0:T(8,128)S(1)} %get-tuple-element.35.top_ref, ...), custom_call_target="tpu_custom_call" | custom-call | tf_op jit(solution)/shard_map/tree_weights/pallas_call | solution.py:610
  54.4 1.5 %collective-permute-start.8 = (f32[128,128]{1,0:T(8,128)S(1)}, f32[128,128]{1,0:T(8,128)S(1)}, u32[]{:S(2)}, u32[]{:S(2)}) collective-permute-start(f32[128,128]{1,0:T(8,128)S(1)} %get-tuple-element.38), channel_id=1, source_target_pairs={{0,8},{8,0},{1,9},{9,1},{2,10},{10,2},{3,11},{11,3},{4,12},{12,4},... | collective-permute-start | bytes 196616 | tf_op jit(solution)/shard_map/ppermute | solution.py:485
  55.9 10.7 %near.1.near_ref = f32[32,4096]{1,0:T(8,128)S(1)} custom-call(s32[1,8]{1,0:T(1,128)} %count_ref.1, s32[8,16]{1,0:T(8,128)} %bitcast.9, bf16[4096,256]{1,0:T(8,128)(2,1)} %get-tuple-element.43.a_hbm, bf16[144,4096]{1,0:T(8,128)(2,1)S(1)} %get-tuple-element.40.tree_ref, bf16[32,4096]{1,0:T(8,128)(2,1)S(1)} %get-tuple-element.44.w_ref), custom_call_target="tpu_custom_call" | custom-call | tf_op jit(solution)/shard_map/near/pallas_call | solution.py:631
  66.7 4.2 %far.1 = (f32[32,512]{1,0:T(8,128)S(1)}, f32[32,512]{1,0:T(8,128)S(1)}, f32[32,512]{1,0:T(8,128)S(1)}, f32[32,512]{1,0:T(8,128)S(1)}, f32[32,512]{1,0:T(8,128)S(...) custom-call(f32[1,128,128]{2,1,0:T(8,128)S(1)} %bitcast.5, ...), custom_call_target="tpu_custom_call" | custom-call | tf_op jit(solution)/shard_map/far/pallas_call | solution.py:650
  72.3 2.3 %collective-permute-start.11 = (f32[32,512]{1,0:T(8,128)S(1)}, f32[32,512]{1,0:T(8,128)S(1)}, u32[]{:S(2)}, u32[]{:S(2)}) collective-permute-start(f32[32,512]{1,0:T(8,128)S(1)} %get-tuple-element.47), channel_id=1, source_target_pairs={{0,4},{1,13},{2,6},{3,15},{4,0},{5,9},{6,2},{7,11},{8,12},{9,5},{1... | collective-permute-start | bytes 196616 | tf_op jit(solution)/shard_map/ppermute | solution.py:548
  74.6 1.5 %collective-permute-start.12 = (f32[32,512]{1,0:T(8,128)S(1)}, f32[32,512]{1,0:T(8,128)S(1)}, u32[]{:S(2)}, u32[]{:S(2)}) collective-permute-start(f32[32,512]{1,0:T(8,128)S(1)} %get-tuple-element.48), channel_id=1, source_target_pairs={{0,6},{1,15},{2,4},{3,13},{4,2},{5,11},{6,0},{7,9},{8,14},{9,7},{1... | collective-permute-start | bytes 196616 | tf_op jit(solution)/shard_map/ppermute | solution.py:548
  76.0 2.7 %collective-permute-start.13 = (f32[32,512]{1,0:T(8,128)S(1)}, f32[32,512]{1,0:T(8,128)S(1)}, u32[]{:S(2)}, u32[]{:S(2)}) collective-permute-start(f32[32,512]{1,0:T(8,128)S(1)} %get-tuple-element.49), channel_id=1, source_target_pairs={{0,8},{1,1},{2,10},{3,3},{4,12},{5,5},{6,14},{7,7},{8,0},{9,9},{10... | collective-permute-start | bytes 196616 | tf_op jit(solution)/shard_map/ppermute | solution.py:548
  79.5 2.8 %collective-permute-start.15 = (f32[32,512]{1,0:T(8,128)S(1)}, f32[32,512]{1,0:T(8,128)S(1)}, u32[]{:S(2)}, u32[]{:S(2)}) collective-permute-start(f32[32,512]{1,0:T(8,128)S(1)} %get-tuple-element.51), channel_id=1, source_target_pairs={{0,12},{1,5},{2,14},{3,7},{4,8},{5,1},{6,10},{7,3},{8,4},{9,13},{1... | collective-permute-start | bytes 196616 | tf_op jit(solution)/shard_map/ppermute | solution.py:548
  82.4 2.4 %collective-permute-start.16 = (f32[32,512]{1,0:T(8,128)S(1)}, f32[32,512]{1,0:T(8,128)S(1)}, u32[]{:S(2)}, u32[]{:S(2)}) collective-permute-start(f32[32,512]{1,0:T(8,128)S(1)} %get-tuple-element.52), channel_id=1, source_target_pairs={{0,14},{1,7},{2,12},{3,5},{4,10},{5,3},{6,8},{7,1},{8,6},{9,15},{1... | collective-permute-start | bytes 196616 | tf_op jit(solution)/shard_map/ppermute | solution.py:548
  84.8 2.8 %collective-permute-done.15.refs_6_ = f32[32,512]{1,0:T(8,128)S(1)} collective-permute-done((f32[32,512]{1,0:T(8,128)S(1)}, f32[32,512]{1,0:T(8,128)S(1)}, u32[]{:S(2)}, u32[]{:S(2)}) %collective-permute-start.15) | collective-permute-done | bytes 65568 | tf_op jit(solution)/shard_map/ppermute | solution.py:548
  87.6 1.7 %collective-permute-done.16.refs_7_ = f32[32,512]{1,0:T(8,128)S(1)} collective-permute-done((f32[32,512]{1,0:T(8,128)S(1)}, f32[32,512]{1,0:T(8,128)S(1)}, u32[]{:S(2)}, u32[]{:S(2)}) %collective-permute-start.16) | collective-permute-done | bytes 65568 | tf_op jit(solution)/shard_map/ppermute | solution.py:548
  89.3 1.9 %to_input_order.1 = f32[1024,128]{1,0:T(8,128)} custom-call(f32[8,128]{1,0:T(8,128)S(1)} %copy-done.1, f32[32,512]{1,0:T(8,128)S(1)} %collective-permute-done.9.refs_0_, f32[32,512]{1,0:T(8,128)S(1)} %collective-permute-done.10.refs_1_, f32[32,512]{1,0:T(8,128)S(1)} %collective-permute-done.11.refs_2_, f32[32,512]{1,0:T(8,128)S(1)} %collective-permute-done.12.refs_3_, ...), custom_call_target="tpu_custom_call" | custom-call | tf_op jit(solution)/shard_map/to_input_order/pallas_call | solution.py:667
  (22 shorter events, 2.3 us)
Async XLA Ops:
  3.7 1.6 %collective-permute-start = (f32[72,512]{1,0:T(8,128)}, f32[72,512]{1,0:T(8,128)S(1)}, u32[]{:S(2)}, u32[]{:S(2)}) collective-permute-start(f32[72,512]{1,0:T(8,128)} %get-tuple-element.30), channel_id=1, source_target_pairs={{0,0},{1,9},{2,2},{3,11},{4,4},{5,13},{6,6},{7,15},{8,8},{9,1},{10... | collective-permute-start | bytes 442376 | tf_op jit(solution)/shard_map/ppermute | solution.py:548
  5.2 8.7 %collective-permute-start.2 = (f32[72,512]{1,0:T(8,128)S(1)}, f32[72,512]{1,0:T(8,128)S(1)}, u32[]{:S(2)}, u32[]{:S(2)}) collective-permute-start(f32[72,512]{1,0:T(8,128)S(1)} %collective-permute-done.refs_0_), channel_id=1, source_target_pairs={{0,4},{2,6},{4,0},{6,2},{1,5},{3,7},{5,1},{7,3},{8,12},{10,14},{12... | collective-permute-start | bytes 442376 | tf_op jit(solution)/shard_map/ppermute | solution.py:561
  14.0 4.8 %collective-permute-start.6 = (f32[72,512]{1,0:T(8,128)S(1)}, f32[72,512]{1,0:T(8,128)S(1)}, u32[]{:S(2)}, u32[]{:S(2)}) collective-permute-start(f32[72,512]{1,0:T(8,128)S(1)} %collective-permute-done.2.refs_2_), channel_id=1, source_target_pairs={{0,1},{1,0},{2,3},{3,2},{4,5},{5,4},{6,7},{7,6},{8,9},{9,8},{10,11... | collective-permute-start | bytes 442376 | tf_op jit(solution)/shard_map/ppermute | solution.py:563
  18.7 32.3 %all-to-all-start = ((f32[8,32,512]{2,1,0:T(8,128)}), f32[8,32,512]{2,1,0:T(8,128)S(1)}, u32[]{:S(2)}, u32[]{:S(2)}) async-start(f32[8,32,512]{2,1,0:T(8,128)} %bitcast.6), calls=%async_computation | async-start | bytes 1048576 | tf_op jit(solution)/shard_map/all_to_all | solution.py:567
  24.5 15.3 %collective-permute-start.1 = (f32[72,512]{1,0:T(8,128)S(1)}, f32[72,512]{1,0:T(8,128)S(1)}, u32[]{:S(2)}, u32[]{:S(2)}) collective-permute-start(f32[72,512]{1,0:T(8,128)S(1)} %collective-permute-done.refs_0_), channel_id=1, source_target_pairs={{0,2},{2,0},{4,6},{6,4},{1,3},{3,1},{5,7},{7,5},{8,10},{10,8},{12,... | collective-permute-start | bytes 442376 | tf_op jit(solution)/shard_map/ppermute | solution.py:561
  26.5 15.6 %collective-permute-start.3 = (f32[72,512]{1,0:T(8,128)S(1)}, f32[72,512]{1,0:T(8,128)S(1)}, u32[]{:S(2)}, u32[]{:S(2)}) collective-permute-start(f32[72,512]{1,0:T(8,128)S(1)} %collective-permute-done.2.refs_2_), channel_id=1, source_target_pairs={{0,2},{2,0},{4,6},{6,4},{1,3},{3,1},{5,7},{7,5},{8,10},{10,8},{12,... | collective-permute-start | bytes 442376 | tf_op jit(solution)/shard_map/ppermute | solution.py:561
  26.6 15.6 %collective-permute-start.4 = (f32[72,512]{1,0:T(8,128)S(1)}, f32[72,512]{1,0:T(8,128)S(1)}, u32[]{:S(2)}, u32[]{:S(2)}) collective-permute-start(f32[72,512]{1,0:T(8,128)S(1)} %collective-permute-done.refs_0_), channel_id=1, source_target_pairs={{0,1},{1,0},{2,3},{3,2},{4,5},{5,4},{6,7},{7,6},{8,9},{9,8},{10,11... | collective-permute-start | bytes 442376 | tf_op jit(solution)/shard_map/ppermute | solution.py:563
  39.8 2.3 %collective-permute-start.5 = (f32[72,512]{1,0:T(8,128)S(1)}, f32[72,512]{1,0:T(8,128)S(1)}, u32[]{:S(2)}, u32[]{:S(2)}) collective-permute-start(f32[72,512]{1,0:T(8,128)S(1)} %collective-permute-done.1.refs_1_), channel_id=1, source_target_pairs={{0,1},{1,0},{2,3},{3,2},{4,5},{5,4},{6,7},{7,6},{8,9},{9,8},{10,11... | collective-permute-start | bytes 442376 | tf_op jit(solution)/shard_map/ppermute | solution.py:563
  42.1 1.4 %collective-permute-start.7 = (f32[72,512]{1,0:T(8,128)S(1)}, f32[72,512]{1,0:T(8,128)S(1)}, u32[]{:S(2)}, u32[]{:S(2)}) collective-permute-start(f32[72,512]{1,0:T(8,128)S(1)} %collective-permute-done.3.refs_3_), channel_id=1, source_target_pairs={{0,1},{1,0},{2,3},{3,2},{4,5},{5,4},{6,7},{7,6},{8,9},{9,8},{10,11... | collective-permute-start | bytes 442376 | tf_op jit(solution)/shard_map/ppermute | solution.py:563
  54.4 12.3 %collective-permute-start.8 = (f32[128,128]{1,0:T(8,128)S(1)}, f32[128,128]{1,0:T(8,128)S(1)}, u32[]{:S(2)}, u32[]{:S(2)}) collective-permute-start(f32[128,128]{1,0:T(8,128)S(1)} %get-tuple-element.38), channel_id=1, source_target_pairs={{0,8},{8,0},{1,9},{9,1},{2,10},{10,2},{3,11},{11,3},{4,12},{12,4},... | collective-permute-start | bytes 196616 | tf_op jit(solution)/shard_map/ppermute | solution.py:485
  66.6 22.7 %copy-start = (f32[1024,128]{1,0:T(8,128)S(1)}, f32[1024,128]{1,0:T(8,128)}, u32[]{:S(2)}) copy-start(f32[1024,128]{1,0:T(8,128)} %refs_8_.1) | copy-start | bytes 1572868
  66.6 22.7 %copy-start.1 = (f32[8,128]{1,0:T(8,128)S(1)}, f32[8,128]{1,0:T(8,128)}, u32[]{:S(2)}) copy-start(f32[8,128]{1,0:T(8,128)} %get-tuple-element.29.pos_ref) | copy-start | bytes 12292
  70.9 7.8 %collective-permute-start.9 = (f32[32,512]{1,0:T(8,128)S(1)}, f32[32,512]{1,0:T(8,128)S(1)}, u32[]{:S(2)}, u32[]{:S(2)}) collective-permute-start(f32[32,512]{1,0:T(8,128)S(1)} %get-tuple-element.45), channel_id=1, source_target_pairs={{0,0},{1,9},{2,2},{3,11},{4,4},{5,13},{6,6},{7,15},{8,8},{9,1},{10... | collective-permute-start | bytes 196616 | tf_op jit(solution)/shard_map/ppermute | solution.py:548
  71.6 7.9 %collective-permute-start.10 = (f32[32,512]{1,0:T(8,128)S(1)}, f32[32,512]{1,0:T(8,128)S(1)}, u32[]{:S(2)}, u32[]{:S(2)}) collective-permute-start(f32[32,512]{1,0:T(8,128)S(1)} %get-tuple-element.46), channel_id=1, source_target_pairs={{0,2},{1,11},{2,0},{3,9},{4,6},{5,15},{6,4},{7,13},{8,10},{9,3},{1... | collective-permute-start | bytes 196616 | tf_op jit(solution)/shard_map/ppermute | solution.py:548
  72.3 10.1 %collective-permute-start.11 = (f32[32,512]{1,0:T(8,128)S(1)}, f32[32,512]{1,0:T(8,128)S(1)}, u32[]{:S(2)}, u32[]{:S(2)}) collective-permute-start(f32[32,512]{1,0:T(8,128)S(1)} %get-tuple-element.47), channel_id=1, source_target_pairs={{0,4},{1,13},{2,6},{3,15},{4,0},{5,9},{6,2},{7,11},{8,12},{9,5},{1... | collective-permute-start | bytes 196616 | tf_op jit(solution)/shard_map/ppermute | solution.py:548
  74.6 10.2 %collective-permute-start.12 = (f32[32,512]{1,0:T(8,128)S(1)}, f32[32,512]{1,0:T(8,128)S(1)}, u32[]{:S(2)}, u32[]{:S(2)}) collective-permute-start(f32[32,512]{1,0:T(8,128)S(1)} %get-tuple-element.48), channel_id=1, source_target_pairs={{0,6},{1,15},{2,4},{3,13},{4,2},{5,11},{6,0},{7,9},{8,14},{9,7},{1... | collective-permute-start | bytes 196616 | tf_op jit(solution)/shard_map/ppermute | solution.py:548
  76.0 8.7 %collective-permute-start.13 = (f32[32,512]{1,0:T(8,128)S(1)}, f32[32,512]{1,0:T(8,128)S(1)}, u32[]{:S(2)}, u32[]{:S(2)}) collective-permute-start(f32[32,512]{1,0:T(8,128)S(1)} %get-tuple-element.49), channel_id=1, source_target_pairs={{0,8},{1,1},{2,10},{3,3},{4,12},{5,5},{6,14},{7,7},{8,0},{9,9},{10... | collective-permute-start | bytes 196616 | tf_op jit(solution)/shard_map/ppermute | solution.py:548
  78.7 6.0 %collective-permute-start.14 = (f32[32,512]{1,0:T(8,128)S(1)}, f32[32,512]{1,0:T(8,128)S(1)}, u32[]{:S(2)}, u32[]{:S(2)}) collective-permute-start(f32[32,512]{1,0:T(8,128)S(1)} %get-tuple-element.50), channel_id=1, source_target_pairs={{0,10},{1,3},{2,8},{3,1},{4,14},{5,7},{6,12},{7,5},{8,2},{9,11},{1... | collective-permute-start | bytes 196616 | tf_op jit(solution)/shard_map/ppermute | solution.py:548
  79.5 8.1 %collective-permute-start.15 = (f32[32,512]{1,0:T(8,128)S(1)}, f32[32,512]{1,0:T(8,128)S(1)}, u32[]{:S(2)}, u32[]{:S(2)}) collective-permute-start(f32[32,512]{1,0:T(8,128)S(1)} %get-tuple-element.51), channel_id=1, source_target_pairs={{0,12},{1,5},{2,14},{3,7},{4,8},{5,1},{6,10},{7,3},{8,4},{9,13},{1... | collective-permute-start | bytes 196616 | tf_op jit(solution)/shard_map/ppermute | solution.py:548
  82.4 7.0 %collective-permute-start.16 = (f32[32,512]{1,0:T(8,128)S(1)}, f32[32,512]{1,0:T(8,128)S(1)}, u32[]{:S(2)}, u32[]{:S(2)}) collective-permute-start(f32[32,512]{1,0:T(8,128)S(1)} %get-tuple-element.52), channel_id=1, source_target_pairs={{0,14},{1,7},{2,12},{3,5},{4,10},{5,3},{6,8},{7,1},{8,6},{9,15},{1... | collective-permute-start | bytes 196616 | tf_op jit(solution)/shard_map/ppermute | solution.py:548

commit v9 on v8

--- a/solution.py
+++ b/solution.py
@@ -561,7 +561,6 @@
                 place[step | stride] = lax.ppermute(place[step], "sub", [(i, i ^ stride) for i in range(blocks)])
             stride //= 2
         theirs = {step: lax.ppermute(one, "rep", [(0, 1), (1, 0)]) for step, one in place.items()}
-        theirs[blocks // 2], light = lax.optimization_barrier((theirs[blocks // 2], light))
         place = [place[step] for step in range(blocks)] + [theirs[step] for step in range(blocks)]
         light = light.reshape(devices, width, part)
         light = lax.all_to_all(light, ("leaf", "sub"), split_axis=0, concat_axis=0, tiled=True)

time: 91.5 us -> 85.7 us (0.937)
  starting transfers between devices: 32.6 us -> 29.1 us
  waiting for transfers between devices: 27.2 us -> 25 us
    ppermute x4, starting transfers between devices: 3.8 us -> 0.52 us  [body(): lax.ppermute(one, 'rep', [(0, 1), (1, 0)])]
    ppermute x3, starting transfers between devices: 6.1 us -> 4.39 us  [body(): lax.ppermute(place[step], 'sub', [(i, i ^ stride) for i in range(blocks)])]
    all_to_all x1, starting transfers between devices: 5.76 us -> 7.25 us  [body(): lax.all_to_all(light, ('leaf', 'sub'), split_axis=0, concat_axis=0, tiled...]
    ppermute x4, waiting for transfers between devices: 2.37 us -> 1.36 us  [body(): lax.ppermute(one, 'rep', [(0, 1), (1, 0)])]
  transfers between devices with their start and end apart: 18 -> 18, of which waited for: 7 -> 5; matrix products, arithmetic and copies ran while one was open for 0% -> 0% of each run, Pallas kernels for 20% -> 21%
where the time goes in v9:
time: 85.7 us; the launch traced here: 84.9 us
  Pallas kernels  30.8 us (36%)
  starting transfers between devices  29.1 us (34%)
  waiting for transfers between devices  25 us (29%)
    ppermute x3, waiting for transfers between devices, body(): lax.ppermute(place[step], 'sub', [(i, i ^ stride) for i in range(blocks)])  19.5 us
    ppermute x9, starting transfers between devices, swap(): return lax.ppermute(value, axes, pairs)  15.4 us
    pallas_call x1, Pallas kernels, body(): pl.pallas_call(near_kernel, out_shape=vm((width, total), f32), in_specs=[...  10.1 us
    pallas_call x1, Pallas kernels, body(): pl.pallas_call(functools.partial(points_kernel, layout, trees), out_shape...  7.55 us
    all_to_all x1, starting transfers between devices, body(): lax.all_to_all(light, ('leaf', 'sub'), split_axis=0, concat_axis=0, tiled...  7.25 us
    ppermute x3, starting transfers between devices, body(): lax.ppermute(place[step], 'sub', [(i, i ^ stride) for i in range(blocks)])  4.39 us
    pallas_call x1, Pallas kernels, body(): pl.pallas_call(functools.partial(far_kernel, layout, low_levels), out_sha...  4.23 us
    ppermute x9, waiting for transfers between devices, swap(): return lax.ppermute(value, axes, pairs)  4.11 us
  transfers between devices with their start and end apart: 18, of which 5 were waited for; matrix products, arithmetic and copies ran while one was open for 0% of the time, Pallas kernels for 21%

profile of v9, /device:TPU:0, one launch (start us, length us, event | category | flops | bytes accessed | tf_op | source)
XLA Modules:
  0.0 84.9 jit_solution(5860455085236724743)
XLA Ops:
  0.0 3.7 %sort_rows.1 = (f32[72,512]{1,0:T(8,128)}, f32[8,128]{1,0:T(8,128)}, f32[2,128,512]{2,1,0:T(8,128)}) custom-call(s32[8,128]{1,0:T(8,128)} %bitcast.8, f32[64,1024]{1,0:T(8,128)} %bitcast.7, f32[1024,128]{1,0:T(8,128)} %refs_8_.1, s32[1,128]{1,0:T(1,128)} %base_ref.1, s32[2,3]{1,0:T(2,128)} %flag_ref.1), custom_call_target="tpu_custom_call" | custom-call | tf_op jit(solution)/shard_map/sort_rows/pallas_call | solution.py:521
  3.7 7.3 %all-to-all-start = ((f32[8,32,512]{2,1,0:T(8,128)}), f32[8,32,512]{2,1,0:T(8,128)S(1)}, u32[]{:S(2)}, u32[]{:S(2)}) async-start(f32[8,32,512]{2,1,0:T(8,128)} %bitcast.6), calls=%async_computation | async-start | bytes 1048576 | tf_op jit(solution)/shard_map/all_to_all | solution.py:566
  10.9 1.6 %collective-permute-start = (f32[72,512]{1,0:T(8,128)}, f32[72,512]{1,0:T(8,128)S(1)}, u32[]{:S(2)}, u32[]{:S(2)}) collective-permute-start(f32[72,512]{1,0:T(8,128)} %get-tuple-element.28), channel_id=1, source_target_pairs={{0,0},{1,9},{2,2},{3,11},{4,4},{5,13},{6,6},{7,15},{8,8},{9,1},{10... | collective-permute-start | bytes 442376 | tf_op jit(solution)/shard_map/ppermute | solution.py:548
  12.5 2.9 %collective-permute-start.2 = (f32[72,512]{1,0:T(8,128)S(1)}, f32[72,512]{1,0:T(8,128)S(1)}, u32[]{:S(2)}, u32[]{:S(2)}) collective-permute-start(f32[72,512]{1,0:T(8,128)S(1)} %collective-permute-done.refs_0_), channel_id=1, source_target_pairs={{0,4},{2,6},{4,0},{6,2},{1,5},{3,7},{5,1},{7,3},{8,12},{10,14},{12... | collective-permute-start | bytes 442376 | tf_op jit(solution)/shard_map/ppermute | solution.py:561
  15.4 1.5 %collective-permute-start.1 = (f32[72,512]{1,0:T(8,128)S(1)}, f32[72,512]{1,0:T(8,128)S(1)}, u32[]{:S(2)}, u32[]{:S(2)}) collective-permute-start(f32[72,512]{1,0:T(8,128)S(1)} %collective-permute-done.refs_0_), channel_id=1, source_target_pairs={{0,2},{2,0},{4,6},{6,4},{1,3},{3,1},{5,7},{7,5},{8,10},{10,8},{12,... | collective-permute-start | bytes 442376 | tf_op jit(solution)/shard_map/ppermute | solution.py:561
  16.9 14.9 %collective-permute-done.2.refs_2_ = f32[72,512]{1,0:T(8,128)S(1)} collective-permute-done((f32[72,512]{1,0:T(8,128)S(1)}, f32[72,512]{1,0:T(8,128)S(1)}, u32[]{:S(2)}, u32[]{:S(2)}) %collective-permute-start.2) | collective-permute-done | bytes 147488 | tf_op jit(solution)/shard_map/ppermute | solution.py:561
  31.7 0.5 collective-permute-start.6
  32.2 4.6 %collective-permute-done.3.refs_3_ = f32[72,512]{1,0:T(8,128)S(1)} collective-permute-done((f32[72,512]{1,0:T(8,128)S(1)}, f32[72,512]{1,0:T(8,128)S(1)}, u32[]{:S(2)}, u32[]{:S(2)}) %collective-permute-start.3) | collective-permute-done | bytes 147488 | tf_op jit(solution)/shard_map/ppermute | solution.py:561
  36.9 1.3 %collective-permute-done.7.refs_7_ = f32[72,512]{1,0:T(8,128)S(1)} collective-permute-done((f32[72,512]{1,0:T(8,128)S(1)}, f32[72,512]{1,0:T(8,128)S(1)}, u32[]{:S(2)}, u32[]{:S(2)}) %collective-permute-start.7) | collective-permute-done | bytes 147488 | tf_op jit(solution)/shard_map/ppermute | solution.py:563
  38.2 7.5 %tree_points.1 = (bf16[144,4096]{1,0:T(8,128)(2,1)S(1)}, bf16[4096,256]{1,0:T(8,128)(2,1)}, bf16[4,1024,128]{2,1,0:T(8,128)(2,1)}, bf16[896,256]{1,0:T(8,128)(2,...) custom-call(s32[6,128]{1,0:T(8,128)} %upper_ref.1, ...), custom_call_target="tpu_custom_call" | custom-call | tf_op jit(solution)/shard_map/tree_points/pallas_call | solution.py:582
  45.8 3.3 %tree_weights.1 = (bf16[32,4096]{1,0:T(8,128)(2,1)S(1)}, bf16[64,896]{1,0:T(8,128)(2,1)S(1)}, f32[128,128]{1,0:T(8,128)S(1)}) custom-call(bf16[4,1024,128]{2,1,0:T(8,128)(2,1)} %get-tuple-element.29.base_hbm, f32[3,256,128]{2,1,0:T(8,128)S(1)} %get-tuple-element.30.upper_tiles_ref, f32[128,128]{1,0:T(8,128)S(1)} %get-tuple-element.31.top_ref, ...), custom_call_target="tpu_custom_call" | custom-call | tf_op jit(solution)/shard_map/tree_weights/pallas_call | solution.py:609
  49.1 1.5 %collective-permute-start.8 = (f32[128,128]{1,0:T(8,128)S(1)}, f32[128,128]{1,0:T(8,128)S(1)}, u32[]{:S(2)}, u32[]{:S(2)}) collective-permute-start(f32[128,128]{1,0:T(8,128)S(1)} %get-tuple-element.34), channel_id=1, source_target_pairs={{0,8},{8,0},{1,9},{9,1},{2,10},{10,2},{3,11},{11,3},{4,12},{12,4},... | collective-permute-start | bytes 196616 | tf_op jit(solution)/shard_map/ppermute | solution.py:485
  50.7 10.1 %near.1.near_ref = f32[32,4096]{1,0:T(8,128)S(1)} custom-call(s32[1,8]{1,0:T(1,128)} %count_ref.1, s32[8,16]{1,0:T(8,128)} %bitcast.9, bf16[4096,256]{1,0:T(8,128)(2,1)} %get-tuple-element.39.a_hbm, bf16[144,4096]{1,0:T(8,128)(2,1)S(1)} %get-tuple-element.36.tree_ref, bf16[32,4096]{1,0:T(8,128)(2,1)S(1)} %get-tuple-element.40.w_ref), custom_call_target="tpu_custom_call" | custom-call | tf_op jit(solution)/shard_map/near/pallas_call | solution.py:630
  60.8 4.2 %far.1 = (f32[32,512]{1,0:T(8,128)S(1)}, f32[32,512]{1,0:T(8,128)S(1)}, f32[32,512]{1,0:T(8,128)S(1)}, f32[32,512]{1,0:T(8,128)S(1)}, f32[32,512]{1,0:T(8,128)S(...) custom-call(f32[1,128,128]{2,1,0:T(8,128)S(1)} %bitcast.5, ...), custom_call_target="tpu_custom_call" | custom-call | tf_op jit(solution)/shard_map/far/pallas_call | solution.py:649
  65.0 0.7 collective-permute-start.9
  65.8 2.6 %collective-permute-start.11 = (f32[32,512]{1,0:T(8,128)S(1)}, f32[32,512]{1,0:T(8,128)S(1)}, u32[]{:S(2)}, u32[]{:S(2)}) collective-permute-start(f32[32,512]{1,0:T(8,128)S(1)} %get-tuple-element.43), channel_id=1, source_target_pairs={{0,4},{1,13},{2,6},{3,15},{4,0},{5,9},{6,2},{7,11},{8,12},{9,5},{1... | collective-permute-start | bytes 196616 | tf_op jit(solution)/shard_map/ppermute | solution.py:548
  68.4 1.7 %collective-permute-start.12 = (f32[32,512]{1,0:T(8,128)S(1)}, f32[32,512]{1,0:T(8,128)S(1)}, u32[]{:S(2)}, u32[]{:S(2)}) collective-permute-start(f32[32,512]{1,0:T(8,128)S(1)} %get-tuple-element.44), channel_id=1, source_target_pairs={{0,6},{1,15},{2,4},{3,13},{4,2},{5,11},{6,0},{7,9},{8,14},{9,7},{1... | collective-permute-start | bytes 196616 | tf_op jit(solution)/shard_map/ppermute | solution.py:548
  70.2 2.4 %collective-permute-start.13 = (f32[32,512]{1,0:T(8,128)S(1)}, f32[32,512]{1,0:T(8,128)S(1)}, u32[]{:S(2)}, u32[]{:S(2)}) collective-permute-start(f32[32,512]{1,0:T(8,128)S(1)} %get-tuple-element.45), channel_id=1, source_target_pairs={{0,8},{1,1},{2,10},{3,3},{4,12},{5,5},{6,14},{7,7},{8,0},{9,9},{10... | collective-permute-start | bytes 196616 | tf_op jit(solution)/shard_map/ppermute | solution.py:548
  72.6 0.2 collective-permute-start.14
  72.8 3.2 %collective-permute-start.15 = (f32[32,512]{1,0:T(8,128)S(1)}, f32[32,512]{1,0:T(8,128)S(1)}, u32[]{:S(2)}, u32[]{:S(2)}) collective-permute-start(f32[32,512]{1,0:T(8,128)S(1)} %get-tuple-element.47), channel_id=1, source_target_pairs={{0,12},{1,5},{2,14},{3,7},{4,8},{5,1},{6,10},{7,3},{8,4},{9,13},{1... | collective-permute-start | bytes 196616 | tf_op jit(solution)/shard_map/ppermute | solution.py:548
  76.0 2.9 %collective-permute-start.16 = (f32[32,512]{1,0:T(8,128)S(1)}, f32[32,512]{1,0:T(8,128)S(1)}, u32[]{:S(2)}, u32[]{:S(2)}) collective-permute-start(f32[32,512]{1,0:T(8,128)S(1)} %get-tuple-element.48), channel_id=1, source_target_pairs={{0,14},{1,7},{2,12},{3,5},{4,10},{5,3},{6,8},{7,1},{8,6},{9,15},{1... | collective-permute-start | bytes 196616 | tf_op jit(solution)/shard_map/ppermute | solution.py:548
  78.9 0.7 collective-permute-done.15.refs_6_
  79.6 3.4 %collective-permute-done.16.refs_7_ = f32[32,512]{1,0:T(8,128)S(1)} collective-permute-done((f32[32,512]{1,0:T(8,128)S(1)}, f32[32,512]{1,0:T(8,128)S(1)}, u32[]{:S(2)}, u32[]{:S(2)}) %collective-permute-start.16) | collective-permute-done | bytes 65568 | tf_op jit(solution)/shard_map/ppermute | solution.py:548
  83.0 1.9 %to_input_order.1 = f32[1024,128]{1,0:T(8,128)} custom-call(f32[8,128]{1,0:T(8,128)S(1)} %copy-done.1, f32[32,512]{1,0:T(8,128)S(1)} %collective-permute-done.9.refs_0_, f32[32,512]{1,0:T(8,128)S(1)} %collective-permute-done.10.refs_1_, f32[32,512]{1,0:T(8,128)S(1)} %collective-permute-done.11.refs_2_, f32[32,512]{1,0:T(8,128)S(1)} %collective-permute-done.12.refs_3_, ...), custom_call_target="tpu_custom_call" | custom-call | tf_op jit(solution)/shard_map/to_input_order/pallas_call | solution.py:666
  (22 shorter events, 0.1 us)
Async XLA Ops:
  3.7 42.1 %all-to-all-start = ((f32[8,32,512]{2,1,0:T(8,128)}), f32[8,32,512]{2,1,0:T(8,128)S(1)}, u32[]{:S(2)}, u32[]{:S(2)}) async-start(f32[8,32,512]{2,1,0:T(8,128)} %bitcast.6), calls=%async_computation | async-start | bytes 1048576 | tf_op jit(solution)/shard_map/all_to_all | solution.py:566
  10.9 1.6 %collective-permute-start = (f32[72,512]{1,0:T(8,128)}, f32[72,512]{1,0:T(8,128)S(1)}, u32[]{:S(2)}, u32[]{:S(2)}) collective-permute-start(f32[72,512]{1,0:T(8,128)} %get-tuple-element.28), channel_id=1, source_target_pairs={{0,0},{1,9},{2,2},{3,11},{4,4},{5,13},{6,6},{7,15},{8,8},{9,1},{10... | collective-permute-start | bytes 442376 | tf_op jit(solution)/shard_map/ppermute | solution.py:548
  12.5 19.2 %collective-permute-start.2 = (f32[72,512]{1,0:T(8,128)S(1)}, f32[72,512]{1,0:T(8,128)S(1)}, u32[]{:S(2)}, u32[]{:S(2)}) collective-permute-start(f32[72,512]{1,0:T(8,128)S(1)} %collective-permute-done.refs_0_), channel_id=1, source_target_pairs={{0,4},{2,6},{4,0},{6,2},{1,5},{3,7},{5,1},{7,3},{8,12},{10,14},{12... | collective-permute-start | bytes 442376 | tf_op jit(solution)/shard_map/ppermute | solution.py:561
  15.4 16.8 %collective-permute-start.1 = (f32[72,512]{1,0:T(8,128)S(1)}, f32[72,512]{1,0:T(8,128)S(1)}, u32[]{:S(2)}, u32[]{:S(2)}) collective-permute-start(f32[72,512]{1,0:T(8,128)S(1)} %collective-permute-done.refs_0_), channel_id=1, source_target_pairs={{0,2},{2,0},{4,6},{6,4},{1,3},{3,1},{5,7},{7,5},{8,10},{10,8},{12,... | collective-permute-start | bytes 442376 | tf_op jit(solution)/shard_map/ppermute | solution.py:561
  31.7 5.1 %collective-permute-start.3 = (f32[72,512]{1,0:T(8,128)S(1)}, f32[72,512]{1,0:T(8,128)S(1)}, u32[]{:S(2)}, u32[]{:S(2)}) collective-permute-start(f32[72,512]{1,0:T(8,128)S(1)} %collective-permute-done.2.refs_2_), channel_id=1, source_target_pairs={{0,2},{2,0},{4,6},{6,4},{1,3},{3,1},{5,7},{7,5},{8,10},{10,8},{12,... | collective-permute-start | bytes 442376 | tf_op jit(solution)/shard_map/ppermute | solution.py:561
  31.7 5.1 %collective-permute-start.4 = (f32[72,512]{1,0:T(8,128)S(1)}, f32[72,512]{1,0:T(8,128)S(1)}, u32[]{:S(2)}, u32[]{:S(2)}) collective-permute-start(f32[72,512]{1,0:T(8,128)S(1)} %collective-permute-done.refs_0_), channel_id=1, source_target_pairs={{0,1},{1,0},{2,3},{3,2},{4,5},{5,4},{6,7},{7,6},{8,9},{9,8},{10,11... | collective-permute-start | bytes 442376 | tf_op jit(solution)/shard_map/ppermute | solution.py:563
  31.7 5.1 %collective-permute-start.6 = (f32[72,512]{1,0:T(8,128)S(1)}, f32[72,512]{1,0:T(8,128)S(1)}, u32[]{:S(2)}, u32[]{:S(2)}) collective-permute-start(f32[72,512]{1,0:T(8,128)S(1)} %collective-permute-done.2.refs_2_), channel_id=1, source_target_pairs={{0,1},{1,0},{2,3},{3,2},{4,5},{5,4},{6,7},{7,6},{8,9},{9,8},{10,11... | collective-permute-start | bytes 442376 | tf_op jit(solution)/shard_map/ppermute | solution.py:563
  32.2 4.6 %collective-permute-start.5 = (f32[72,512]{1,0:T(8,128)S(1)}, f32[72,512]{1,0:T(8,128)S(1)}, u32[]{:S(2)}, u32[]{:S(2)}) collective-permute-start(f32[72,512]{1,0:T(8,128)S(1)} %collective-permute-done.1.refs_1_), channel_id=1, source_target_pairs={{0,1},{1,0},{2,3},{3,2},{4,5},{5,4},{6,7},{7,6},{8,9},{9,8},{10,11... | collective-permute-start | bytes 442376 | tf_op jit(solution)/shard_map/ppermute | solution.py:563
  36.9 1.4 %collective-permute-start.7 = (f32[72,512]{1,0:T(8,128)S(1)}, f32[72,512]{1,0:T(8,128)S(1)}, u32[]{:S(2)}, u32[]{:S(2)}) collective-permute-start(f32[72,512]{1,0:T(8,128)S(1)} %collective-permute-done.3.refs_3_), channel_id=1, source_target_pairs={{0,1},{1,0},{2,3},{3,2},{4,5},{5,4},{6,7},{7,6},{8,9},{9,8},{10,11... | collective-permute-start | bytes 442376 | tf_op jit(solution)/shard_map/ppermute | solution.py:563
  49.1 11.6 %collective-permute-start.8 = (f32[128,128]{1,0:T(8,128)S(1)}, f32[128,128]{1,0:T(8,128)S(1)}, u32[]{:S(2)}, u32[]{:S(2)}) collective-permute-start(f32[128,128]{1,0:T(8,128)S(1)} %get-tuple-element.34), channel_id=1, source_target_pairs={{0,8},{8,0},{1,9},{9,1},{2,10},{10,2},{3,11},{11,3},{4,12},{12,4},... | collective-permute-start | bytes 196616 | tf_op jit(solution)/shard_map/ppermute | solution.py:485
  60.8 22.2 %copy-start = (f32[1024,128]{1,0:T(8,128)S(1)}, f32[1024,128]{1,0:T(8,128)}, u32[]{:S(2)}) copy-start(f32[1024,128]{1,0:T(8,128)} %refs_8_.1) | copy-start | bytes 1572868
  60.8 22.2 %copy-start.1 = (f32[8,128]{1,0:T(8,128)S(1)}, f32[8,128]{1,0:T(8,128)}, u32[]{:S(2)}) copy-start(f32[8,128]{1,0:T(8,128)} %get-tuple-element.27.pos_ref) | copy-start | bytes 12292
  65.0 7.6 %collective-permute-start.9 = (f32[32,512]{1,0:T(8,128)S(1)}, f32[32,512]{1,0:T(8,128)S(1)}, u32[]{:S(2)}, u32[]{:S(2)}) collective-permute-start(f32[32,512]{1,0:T(8,128)S(1)} %get-tuple-element.41), channel_id=1, source_target_pairs={{0,0},{1,9},{2,2},{3,11},{4,4},{5,13},{6,6},{7,15},{8,8},{9,1},{10... | collective-permute-start | bytes 196616 | tf_op jit(solution)/shard_map/ppermute | solution.py:548
  65.7 7.1 %collective-permute-start.10 = (f32[32,512]{1,0:T(8,128)S(1)}, f32[32,512]{1,0:T(8,128)S(1)}, u32[]{:S(2)}, u32[]{:S(2)}) collective-permute-start(f32[32,512]{1,0:T(8,128)S(1)} %get-tuple-element.42), channel_id=1, source_target_pairs={{0,2},{1,11},{2,0},{3,9},{4,6},{5,15},{6,4},{7,13},{8,10},{9,3},{1... | collective-permute-start | bytes 196616 | tf_op jit(solution)/shard_map/ppermute | solution.py:548
  65.8 10.2 %collective-permute-start.11 = (f32[32,512]{1,0:T(8,128)S(1)}, f32[32,512]{1,0:T(8,128)S(1)}, u32[]{:S(2)}, u32[]{:S(2)}) collective-permute-start(f32[32,512]{1,0:T(8,128)S(1)} %get-tuple-element.43), channel_id=1, source_target_pairs={{0,4},{1,13},{2,6},{3,15},{4,0},{5,9},{6,2},{7,11},{8,12},{9,5},{1... | collective-permute-start | bytes 196616 | tf_op jit(solution)/shard_map/ppermute | solution.py:548
  68.4 10.5 %collective-permute-start.12 = (f32[32,512]{1,0:T(8,128)S(1)}, f32[32,512]{1,0:T(8,128)S(1)}, u32[]{:S(2)}, u32[]{:S(2)}) collective-permute-start(f32[32,512]{1,0:T(8,128)S(1)} %get-tuple-element.44), channel_id=1, source_target_pairs={{0,6},{1,15},{2,4},{3,13},{4,2},{5,11},{6,0},{7,9},{8,14},{9,7},{1... | collective-permute-start | bytes 196616 | tf_op jit(solution)/shard_map/ppermute | solution.py:548
  70.2 8.7 %collective-permute-start.13 = (f32[32,512]{1,0:T(8,128)S(1)}, f32[32,512]{1,0:T(8,128)S(1)}, u32[]{:S(2)}, u32[]{:S(2)}) collective-permute-start(f32[32,512]{1,0:T(8,128)S(1)} %get-tuple-element.45), channel_id=1, source_target_pairs={{0,8},{1,1},{2,10},{3,3},{4,12},{5,5},{6,14},{7,7},{8,0},{9,9},{10... | collective-permute-start | bytes 196616 | tf_op jit(solution)/shard_map/ppermute | solution.py:548
  72.6 6.3 %collective-permute-start.14 = (f32[32,512]{1,0:T(8,128)S(1)}, f32[32,512]{1,0:T(8,128)S(1)}, u32[]{:S(2)}, u32[]{:S(2)}) collective-permute-start(f32[32,512]{1,0:T(8,128)S(1)} %get-tuple-element.46), channel_id=1, source_target_pairs={{0,10},{1,3},{2,8},{3,1},{4,14},{5,7},{6,12},{7,5},{8,2},{9,11},{1... | collective-permute-start | bytes 196616 | tf_op jit(solution)/shard_map/ppermute | solution.py:548
  72.8 6.8 %collective-permute-start.15 = (f32[32,512]{1,0:T(8,128)S(1)}, f32[32,512]{1,0:T(8,128)S(1)}, u32[]{:S(2)}, u32[]{:S(2)}) collective-permute-start(f32[32,512]{1,0:T(8,128)S(1)} %get-tuple-element.47), channel_id=1, source_target_pairs={{0,12},{1,5},{2,14},{3,7},{4,8},{5,1},{6,10},{7,3},{8,4},{9,13},{1... | collective-permute-start | bytes 196616 | tf_op jit(solution)/shard_map/ppermute | solution.py:548
  76.0 7.0 %collective-permute-start.16 = (f32[32,512]{1,0:T(8,128)S(1)}, f32[32,512]{1,0:T(8,128)S(1)}, u32[]{:S(2)}, u32[]{:S(2)}) collective-permute-start(f32[32,512]{1,0:T(8,128)S(1)} %get-tuple-element.48), channel_id=1, source_target_pairs={{0,14},{1,7},{2,12},{3,5},{4,10},{5,3},{6,8},{7,1},{8,6},{9,15},{1... | collective-permute-start | bytes 196616 | tf_op jit(solution)/shard_map/ppermute | solution.py:548

commit v10 on v9

--- a/solution.py
+++ b/solution.py
@@ -101,15 +101,13 @@
         perm[here, c * LANES : (c + 1) * LANES] = onehot(lane + float(c * LANES) == rank)
 
 
-def sort_kernel(
-    fine, slot_ref, points_ref, weights_ref, base_ref, flag_ref, place_ref, pos_ref, light_ref, perm, vals, whole
-):
-    chunks, split = slot_ref.shape[0], light_ref.shape[-1]
-    rows = chunks * LANES
+def place_kernel(fine, slot_ref, points_ref, base_ref, flag_ref, place_ref, pos_ref, masked, low_hot):
+    chunks = slot_ref.shape[0]
     slots = slot_ref[...]
     slot = slots.astype(f32)
-    within = slots & (rows - 1)
+    within = slots & (chunks * LANES - 1)
     high, low = (within >> 5).astype(f32), (within & 31).astype(f32)
+    ranks = []
     for r in range(chunks):
         here = slice(r * LANES, (r + 1) * LANES)
         mine = column(slot[r : r + 1])
@@ -117,37 +115,51 @@
         for c in range(chunks):
             before += jnp.where(slot[c : c + 1] < mine, 1.0, 0.0)
         rank = jnp.broadcast_to(jnp.sum(before, axis=1, keepdims=True), (LANES, LANES))
-        pos_ref[r : r + 1, :] = jnp.transpose(rank)[0:1]
-        spread(perm, here, rank)
-        vals[0:LANES, here] = jnp.transpose(weights_ref[here, :]).astype(bf16)
+        ranks.append(jnp.transpose(rank)[0:1])
+        pos_ref[r : r + 1, :] = ranks[-1]
+        spread(low_hot, here, (rank.astype(jnp.int32) & (LOW - 1)).astype(f32))
     scaled = points_ref[...] * point_scale
     ph, plo = two(scaled)
     nh, nm, nl = three(-0.5 * jnp.sum(scaled * scaled, axis=0, keepdims=True))
-    vals[128:192, :] = ph
-    vals[192:256, :] = plo
-    sub = iota((16, LANES), 0)
+    high, low = lanes_of([high[c : c + 1] for c in range(chunks)]), lanes_of([low[c : c + 1] for c in range(chunks)])
+    sub = iota((16, chunks * LANES), 0)
+    extra = jnp.where(sub == 0, high, jnp.where(sub == 1, low, 0.0))
+    extra = jnp.where(sub == 2, nh, jnp.where(sub == 3, nm, jnp.where(sub == 4, nl, extra)))
+    high_part = lanes_of(ranks).astype(jnp.int32) // LOW
+    parts = place_ref.shape[1] // LOW
+    first = (lax.axis_index("leaf") ^ lax.axis_index("rep")) * parts if fine else 0
+    for h in range(parts):
+        here = high_part == first + h
+        masked[h * COORD : h * COORD + 64, :] = jnp.where(here, ph.astype(f32), 0.0).astype(bf16)
+        masked[h * COORD + 64 : h * COORD + 128, :] = jnp.where(here, plo.astype(f32), 0.0).astype(bf16)
+        masked[h * COORD + 128 : (h + 1) * COORD, :] = jnp.where(here, extra, 0.0).astype(bf16)
+    placed = nn(masked[...], low_hot[...])
+    tail = iota((PLACE_ROWS - TAIL, LOW), 0)
+    for h in range(parts):
+        at = slice(h * LOW, (h + 1) * LOW)
+        moved = placed[h * COORD : (h + 1) * COORD]
+        place_ref[0:TAIL, at] = moved[0:64] + moved[64:128]
+        slot_row = moved[128:129] * 32.0 + moved[129:130]
+        norm_row = moved[130:131] + moved[131:132] + moved[132:133]
+        place_ref[TAIL:, at] = jnp.where(tail == SLOT, slot_row, jnp.where(tail == NORM, norm_row, 0.0))
+    if fine:
+        place_ref[TAIL + BASE : TAIL + BASE + 1, 0:SK] = base_ref[...].astype(f32)
+        place_ref[TAIL + FLAGS : TAIL + FLAGS + flag_ref.shape[0], 0 : flag_ref.shape[1]] = flag_ref[...].astype(f32)
+
+
+def light_kernel(pos_ref, weights_ref, light_ref, masked, low_hot):
+    chunks, split = pos_ref.shape[0], light_ref.shape[2]
+    low_part, high_part = parts_of(lanes_of([pos_ref[c : c + 1, :] for c in range(chunks)]))
+    low_by_column(low_hot, low_part.astype(f32))
     for c in range(chunks):
         at = slice(c * LANES, (c + 1) * LANES)
-        extra = jnp.where(sub == 0, high[c : c + 1], jnp.where(sub == 1, low[c : c + 1], 0.0))
-        extra = jnp.where(sub == 2, nh[:, at], jnp.where(sub == 3, nm[:, at], extra))
-        vals[256:272, at] = jnp.where(sub == 4, nl[:, at], extra).astype(bf16)
-    step = 256
-    for s in range(rows // step):
-        moved = nn(vals[...], perm[:, s * step : (s + 1) * step])
-        at = slice((s * step) % split, (s * step) % split + step)
-        part = (s * step) // split
-        light_ref[part, :, at] = moved[0:LANES]
-        whole[part, 0:TAIL, at] = moved[128:192] + moved[192:256]
-        tail = iota((8, step), 0)
-        slot_row = moved[256:257] * 32.0 + moved[257:258]
-        norm_row = moved[258:259] + moved[259:260] + moved[260:261]
-        whole[part, TAIL:, at] = jnp.where(tail == SLOT, slot_row, jnp.where(tail == NORM, norm_row, 0.0))
-    if not fine:
-        place_ref[...] = whole[0]
-        return
-    place_ref[...] = whole[lax.axis_index("leaf") ^ lax.axis_index("rep")]
-    place_ref[TAIL + BASE : TAIL + BASE + 1, 0:SK] = base_ref[...].astype(f32)
-    place_ref[TAIL + FLAGS : TAIL + FLAGS + flag_ref.shape[0], 0 : flag_ref.shape[1]] = flag_ref[...].astype(f32)
+        turned = jnp.transpose(weights_ref[at, :])
+        for h in range(chunks * LANES // LOW):
+            masked[h * LANES : (h + 1) * LANES, at] = jnp.where(high_part[:, at] == h, turned, 0.0).astype(bf16)
+    placed = nn(masked[...], low_hot[...])
+    for h in range(chunks * LANES // LOW):
+        at = h * LOW
+        light_ref[at // split, :, at % split : at % split + LOW] = placed[h * LANES : (h + 1) * LANES]
 
 
 class Layout:
@@ -205,14 +217,41 @@
     return first.astype(bf16), second.astype(bf16)
 
 
-def points_kernel(layout, trees, upper_ref, *refs):
+def list_tiles(count_ref, list_ref, tiles, times):
+    every = count_ref.shape[1]
+
+    def tally(leaf, filled):
+        for other in range(every):
+            times[other] = (leaf == other).astype(jnp.int32)
+
+        def add(slot, carry):
+            at = list_ref[leaf, slot]
+            times[at] = times[at] + 1
+            return carry
+
+        lax.fori_loop(0, count_ref[0, leaf], add, 0)
+        for other in range(every):
+            tiles[0, filled] = leaf
+            tiles[1, filled] = other
+            tiles[2, filled] = times[other]
+            filled = filled + (times[other] > 0).astype(jnp.int32)
+        return filled
+
+    filled = lax.fori_loop(0, every, tally, jnp.int32(0))
+    for more in range(2):
+        tiles[0, filled + more] = 0
+        tiles[1, filled + more] = 0
+    tiles[0, tiles.shape[1] - 1] = filled
+
+
+def points_kernel(layout, trees, count_ref, list_ref, upper_ref, *refs):
     if not layout.fine:
         small_ref, refs = refs[0], refs[1:]
     else:
         small_ref = None
     place_refs, refs = refs[: layout.count], refs[layout.count :]
-    tree_ref, a_hbm, base_hbm, sk_ref, upper_tiles_ref, top_ref, slot_ref, info_ref = refs[:8]
-    masked, low_hot, a_ref, base_ref, sk_t, sk_bt, sems = refs[8:]
+    tree_ref, a_hbm, base_hbm, sk_ref, upper_tiles_ref, top_ref, slot_ref, info_ref, tiles = refs[:9]
+    masked, low_hot, a_ref, base_ref, sk_t, sk_bt, sems, times = refs[9:]
     blocks, rows = layout.blocks, layout.rows
 
     def keep(node, found):
@@ -274,6 +313,7 @@
     top_ref[0:64, :] = found[0:64] + found[64:128]
     top_ref[64:72, :] = found[128:136]
     top_ref[72:128, :] = jnp.zeros((56, SK), f32)
+    list_tiles(count_ref, list_ref, tiles, times)
     for index in range(blocks):
         mine = slice(index * rows, (index + 1) * rows)
         pltpu.make_async_copy(a_ref.at[mine], a_hbm.at[mine], sems.at[0, index]).wait()
@@ -320,35 +360,14 @@
         start, count = start + count, count // 2
 
 
-def near_kernel(count_ref, list_ref, a_hbm, tree_ref, w_ref, acc, times, tiles, a_ref, bt_ref, sem, *halves):
-    every = count_ref.shape[1]
+def near_kernel(tiles, a_hbm, tree_ref, w_ref, acc, a_ref, bt_ref, sem, *halves):
     copy = pltpu.make_async_copy(a_hbm, a_ref, sem)
     copy.start()
-    for leaf in range(every):
+    for leaf in range(bt_ref.shape[1] // LEAF):
         here = slice(leaf * LEAF, (leaf + 1) * LEAF)
         feature_columns(bt_ref, here, tree_ref[:, here])
 
-    def tally(leaf, filled):
-        for other in range(every):
-            times[other] = (leaf == other).astype(jnp.int32)
-
-        def add(slot, carry):
-            at = list_ref[leaf, slot]
-            times[at] = times[at] + 1
-            return carry
-
-        lax.fori_loop(0, count_ref[0, leaf], add, 0)
-        for other in range(every):
-            tiles[0, filled] = leaf
-            tiles[1, filled] = other
-            tiles[2, filled] = times[other]
-            filled = filled + (times[other] > 0).astype(jnp.int32)
-        return filled
-
-    filled = lax.fori_loop(0, every, tally, jnp.int32(0))
-    for more in range(2):
-        tiles[0, filled + more] = 0
-        tiles[1, filled + more] = 0
+    filled = tiles[0, tiles.shape[1] - 1]
     half = LEAF // 2
     acc[...] = jnp.zeros_like(acc)
 
@@ -451,6 +470,10 @@
     lax.fori_loop(0, blocks, block, 0)
 
 
+def far_first(blocks, count):
+    return sorted(range(count), key=lambda g: -((g % blocks) * 2 // blocks) if blocks else 0)
+
+
 def final_kernel(blocks, pos_ref, *refs):
     back_refs, (weights_ref, out_ref, perm, vals) = refs[:-4], refs[-4:]
     chunks = pos_ref.shape[0]
@@ -458,7 +481,7 @@
     width, split = back_refs[0].shape
     for r in range(chunks):
         spread(perm, slice(r * LANES, (r + 1) * LANES), column(pos_ref[r : r + 1, :]))
-    for g, back_ref in enumerate(back_refs):
+    for g, back_ref in zip(far_first(blocks, len(back_refs)), back_refs):
         high, low = two(back_ref[...])
         columns, at = 0, slice(0, rows)
         if blocks:
@@ -518,23 +541,24 @@
     split = part if fine else rows
     arrive = shaped((width, part), f32) if fine else shaped((width, total), f32)
 
-    place, pos, light = pl.pallas_call(
-        functools.partial(sort_kernel, fine),
-        out_shape=(
-            shaped((PLACE_ROWS, split), f32),
-            shaped((rows // LANES, LANES), f32),
-            shaped((rows // split, columns, split), f32),
-        ),
-        in_specs=[spec()] * 5,
-        out_specs=(spec(),) * 3,
-        scratch_shapes=[
-            vm((rows, rows), bf16),
-            vm((272, rows), bf16),
-            vm((rows // split, PLACE_ROWS, split), f32),
-        ],
+    place, pos = pl.pallas_call(
+        functools.partial(place_kernel, fine),
+        out_shape=(shaped((PLACE_ROWS, split), f32), shaped((rows // LANES, LANES), f32)),
+        in_specs=[spec()] * 4,
+        out_specs=(spec(),) * 2,
+        scratch_shapes=[vm((split // LOW * COORD, rows), bf16), vm((rows, LOW), bf16)],
         compiler_params=params(),
-        name="sort_rows",
-    )(tree_slot.reshape(rows // LANES, LANES), points.T, weights, skeleton_base, far_use)
+        name="sort_points",
+    )(tree_slot.reshape(rows // LANES, LANES), points.T, skeleton_base, far_use)
+    light = pl.pallas_call(
+        light_kernel,
+        out_shape=shaped((rows // split, columns, split), f32),
+        in_specs=[spec()] * 2,
+        out_specs=spec(),
+        scratch_shapes=[vm((rows // LOW * LANES, rows), bf16), vm((rows, LOW), bf16)],
+        compiler_params=params(),
+        name="sort_weights",
+    )(pos, weights)
 
     axes = ("leaf", "sub", "rep")
 
@@ -548,10 +572,7 @@
         return lax.ppermute(value, axes, pairs)
 
     def swap_all(values):
-        done = {}
-        for g in sorted(range(len(values)), key=lambda g: -(g % blocks)):
-            done[g] = swap(values[g], g % blocks, g // blocks)
-        return [done[g] for g in range(len(values))]
+        return [swap(values[g], g % blocks, g // blocks) for g in far_first(blocks, len(values))]
 
     if fine:
         place = {0: swap(place, 0)}
@@ -560,6 +581,7 @@
             for step in sorted(place):
                 place[step | stride] = lax.ppermute(place[step], "sub", [(i, i ^ stride) for i in range(blocks)])
             stride //= 2
+        place, light = lax.optimization_barrier((place, light))
         theirs = {step: lax.ppermute(one, "rep", [(0, 1), (1, 0)]) for step, one in place.items()}
         place = [place[step] for step in range(blocks)] + [theirs[step] for step in range(blocks)]
         light = light.reshape(devices, width, part)
@@ -579,7 +601,7 @@
         light = light.transpose(1, 2, 0, 3).reshape(1, width, total)
 
     nodes = 2 * blocks - 1
-    tree, feat_a, base, sk, upper_tiles, top, slots, info = pl.pallas_call(
+    tree, feat_a, base, sk, upper_tiles, top, slots, info, tiles = pl.pallas_call(
         functools.partial(points_kernel, layout, trees),
         out_shape=(
             vm((COORD, total), bf16),
@@ -590,9 +612,10 @@
             vm((SK, LANES), f32),
             vm((blocks, rows), f32),
             vm((blocks, 8, SK), f32),
+            shaped((3, leaves * leaves + 3), jnp.int32),
         ),
-        in_specs=[spec()] * (1 + len(small) + layout.count),
-        out_specs=(spec(), spec(pl.ANY), spec(pl.ANY)) + (spec(),) * 5,
+        in_specs=[spec(SMEM)] * 2 + [spec()] * (1 + len(small) + layout.count),
+        out_specs=(spec(), spec(pl.ANY), spec(pl.ANY)) + (spec(),) * 5 + (spec(SMEM),),
         scratch_shapes=[
             vm((rows // LOW * COORD, rows), bf16),
             vm((rows, LOW), bf16),
@@ -601,10 +624,11 @@
             vm((COORD, nodes * SK), bf16),
             vm((FEAT, SK), bf16),
             pltpu.SemaphoreType.DMA((2, blocks)),
+            pltpu.SMEM((leaves,), jnp.int32),
         ],
         compiler_params=params(40),
         name="tree_points",
-    )(in_hbm(skeleton_upper), *small, *place)
+    )(in_hbm(near_count), in_hbm(near_list[0]), in_hbm(skeleton_upper), *small, *place)
 
     tree_light, coefs, pack = pl.pallas_call(
         functools.partial(weights_kernel, layout),
@@ -630,11 +654,9 @@
     near = pl.pallas_call(
         near_kernel,
         out_shape=vm((width, total), f32),
-        in_specs=[spec(SMEM)] * 2 + [spec(pl.ANY)] + [spec()] * 2,
+        in_specs=[spec(SMEM), spec(pl.ANY)] + [spec()] * 2,
         out_specs=spec(),
         scratch_shapes=[
-            pltpu.SMEM((leaves,), jnp.int32),
-            pltpu.SMEM((3, leaves * leaves + 2), jnp.int32),
             vm((total, FEAT), bf16),
             vm((FEAT, total), bf16),
             pltpu.SemaphoreType.DMA(()),
@@ -643,7 +665,7 @@
         + [vm((LEAF, LEAF // 2), bf16)] * 4,
         compiler_params=params(40),
         name="near",
-    )(in_hbm(near_count), in_hbm(near_list[0]), in_hbm(feat_a), held(tree), held(tree_light))
+    )(in_hbm(tiles), in_hbm(feat_a), held(tree), held(tree_light))
 
     levels = low_levels + ups
     back = pl.pallas_call(

time: 85.7 us -> 81.1 us (0.946)
  waiting for transfers between devices: 25 us -> 13.8 us
  starting transfers between devices: 29.1 us -> 32.2 us
  Pallas kernels: 30.8 us -> 33.6 us
    ppermute x3, waiting for transfers between devices: 19.5 us -> 5.51 us  [body(): lax.ppermute(place[step], 'sub', [(i, i ^ stride) for i in range(blocks)])]
    all_to_all x1, waiting for transfers between devices: 0.01 us -> 2.57 us  [body(): lax.all_to_all(light, ('leaf', 'sub'), split_axis=0, concat_axis=0, tiled...]
    ppermute x3, starting transfers between devices: 4.39 us -> 6.51 us  [body(): lax.ppermute(place[step], 'sub', [(i, i ^ stride) for i in range(blocks)])]
    ppermute x4, starting transfers between devices: 0.52 us -> 2.54 us  [body(): lax.ppermute(one, 'rep', [(0, 1), (1, 0)])]
    all_to_all x1, starting transfers between devices: 7.25 us -> 5.45 us  [body(): lax.all_to_all(light, ('leaf', 'sub'), split_axis=0, concat_axis=0, tiled...]
    ppermute x9, starting transfers between devices: 15.4 us -> 17 us  [swap(): return lax.ppermute(value, axes, pairs)]
    pallas_call x1 -> x2, Pallas kernels: 3.65 us -> 5.3 us  [the longest x1 2.74 us: body(): pl.pallas_call(functools.partial(place_kernel, fine), out_shape=(shaped((...]
    pallas_call x1, Pallas kernels: 7.55 us -> 8.8 us  [body(): pl.pallas_call(functools.partial(points_kernel, layout, trees), out_shape...]
  transfers between devices with their start and end apart: 18 -> 18, of which waited for: 5 -> 10; matrix products, arithmetic and copies ran while one was open for 0% -> 0% of each run, Pallas kernels for 21% -> 27%
where the time goes in v10:
time: 81.1 us; the launch traced here: 80.3 us
  Pallas kernels  33.6 us (41%)
  starting transfers between devices  32.2 us (40%)
  waiting for transfers between devices  13.8 us (17%)
    ppermute x9, starting transfers between devices, swap(): return lax.ppermute(value, axes, pairs)  17 us
    pallas_call x1, Pallas kernels, body(): pl.pallas_call(near_kernel, out_shape=vm((width, total), f32), in_specs=[...  10 us
    pallas_call x1, Pallas kernels, body(): pl.pallas_call(functools.partial(points_kernel, layout, trees), out_shape...  8.8 us
    ppermute x3, starting transfers between devices, body(): lax.ppermute(place[step], 'sub', [(i, i ^ stride) for i in range(blocks)])  6.51 us
    ppermute x3, waiting for transfers between devices, body(): lax.ppermute(place[step], 'sub', [(i, i ^ stride) for i in range(blocks)])  5.51 us
    all_to_all x1, starting transfers between devices, body(): lax.all_to_all(light, ('leaf', 'sub'), split_axis=0, concat_axis=0, tiled...  5.45 us
    ppermute x9, waiting for transfers between devices, swap(): return lax.ppermute(value, axes, pairs)  4.46 us
    pallas_call x1, Pallas kernels, body(): pl.pallas_call(functools.partial(far_kernel, layout, low_levels), out_sha...  4.23 us
  transfers between devices with their start and end apart: 18, of which 10 were waited for; matrix products, arithmetic and copies ran while one was open for 0% of the time, Pallas kernels for 27%

profile of v10, /device:TPU:0, one launch (start us, length us, event | category | flops | bytes accessed | tf_op | source)
XLA Modules:
  0.0 80.3 jit_solution(6494567612234897469)
XLA Ops:
  0.0 2.7 %sort_points.1 = (f32[72,512]{1,0:T(8,128)}, f32[8,128]{1,0:T(8,128)}) custom-call(s32[8,128]{1,0:T(8,128)} %bitcast.8, f32[64,1024]{1,0:T(8,128)} %bitcast.7, s32[1,128]{1,0:T(1,128)} %base_ref.1, s32[2,3]{1,0:T(2,128)} %flag_ref.1), custom_call_target="tpu_custom_call" | custom-call | tf_op jit(solution)/shard_map/sort_points/pallas_call | solution.py:544
  2.7 1.6 %collective-permute-start = (f32[72,512]{1,0:T(8,128)}, f32[72,512]{1,0:T(8,128)S(1)}, u32[]{:S(2)}, u32[]{:S(2)}) collective-permute-start(f32[72,512]{1,0:T(8,128)} %get-tuple-element.33), channel_id=1, source_target_pairs={{0,0},{1,9},{2,2},{3,11},{4,4},{5,13},{6,6},{7,15},{8,8},{9,1},{10... | collective-permute-start | bytes 442376 | tf_op jit(solution)/shard_map/ppermute | solution.py:572
  4.3 4.0 %collective-permute-start.2 = (f32[72,512]{1,0:T(8,128)S(1)}, f32[72,512]{1,0:T(8,128)S(1)}, u32[]{:S(2)}, u32[]{:S(2)}) collective-permute-start(f32[72,512]{1,0:T(8,128)S(1)} %collective-permute-done.refs_0_), channel_id=1, source_target_pairs={{0,4},{2,6},{4,0},{6,2},{1,5},{3,7},{5,1},{7,3},{8,12},{10,14},{12... | collective-permute-start | bytes 442376 | tf_op jit(solution)/shard_map/ppermute | solution.py:582
  8.3 1.6 %collective-permute-start.1 = (f32[72,512]{1,0:T(8,128)S(1)}, f32[72,512]{1,0:T(8,128)S(1)}, u32[]{:S(2)}, u32[]{:S(2)}) collective-permute-start(f32[72,512]{1,0:T(8,128)S(1)} %collective-permute-done.refs_0_), channel_id=1, source_target_pairs={{0,2},{2,0},{4,6},{6,4},{1,3},{3,1},{5,7},{7,5},{8,10},{10,8},{12,... | collective-permute-start | bytes 442376 | tf_op jit(solution)/shard_map/ppermute | solution.py:582
  9.9 3.2 %collective-permute-done.2.refs_2_ = f32[72,512]{1,0:T(8,128)S(1)} collective-permute-done((f32[72,512]{1,0:T(8,128)S(1)}, f32[72,512]{1,0:T(8,128)S(1)}, u32[]{:S(2)}, u32[]{:S(2)}) %collective-permute-start.2) | collective-permute-done | bytes 147488 | tf_op jit(solution)/shard_map/ppermute | solution.py:582
  13.2 0.9 %collective-permute-start.3 = (f32[72,512]{1,0:T(8,128)S(1)}, f32[72,512]{1,0:T(8,128)S(1)}, u32[]{:S(2)}, u32[]{:S(2)}) collective-permute-start(f32[72,512]{1,0:T(8,128)S(1)} %collective-permute-done.2.refs_2_), channel_id=1, source_target_pairs={{0,2},{2,0},{4,6},{6,4},{1,3},{3,1},{5,7},{7,5},{8,10},{10,8},{12,... | collective-permute-start | bytes 442376 | tf_op jit(solution)/shard_map/ppermute | solution.py:582
  14.1 2.6 %sort_weights.1 = f32[2,128,512]{2,1,0:T(8,128)} custom-call(f32[8,128]{1,0:T(8,128)} %get-tuple-element.32.pos_ref, f32[1024,128]{1,0:T(8,128)} %refs_8_.1), custom_call_target="tpu_custom_call" | custom-call | tf_op jit(solution)/shard_map/sort_weights/pallas_call | solution.py:553
  16.6 2.3 %collective-permute-done.3.refs_3_ = f32[72,512]{1,0:T(8,128)S(1)} collective-permute-done((f32[72,512]{1,0:T(8,128)S(1)}, f32[72,512]{1,0:T(8,128)S(1)}, u32[]{:S(2)}, u32[]{:S(2)}) %collective-permute-start.3) | collective-permute-done | bytes 147488 | tf_op jit(solution)/shard_map/ppermute | solution.py:582
  18.9 5.5 %all-to-all-start = ((f32[8,32,512]{2,1,0:T(8,128)}), f32[8,32,512]{2,1,0:T(8,128)S(1)}, u32[]{:S(2)}, u32[]{:S(2)}) async-start(f32[8,32,512]{2,1,0:T(8,128)} %bitcast.6), calls=%async_computation | async-start | bytes 1048576 | tf_op jit(solution)/shard_map/all_to_all | solution.py:588
  24.3 2.0 %collective-permute-start.4 = (f32[72,512]{1,0:T(8,128)S(1)}, f32[72,512]{1,0:T(8,128)S(1)}, u32[]{:S(2)}, u32[]{:S(2)}) collective-permute-start(f32[72,512]{1,0:T(8,128)S(1)} %collective-permute-done.refs_0_), channel_id=1, source_target_pairs={{0,1},{1,0},{2,3},{3,2},{4,5},{5,4},{6,7},{7,6},{8,9},{9,8},{10,11... | collective-permute-start | bytes 442376 | tf_op jit(solution)/shard_map/ppermute | solution.py:585
  28.2 8.8 %tree_points.1 = (bf16[144,4096]{1,0:T(8,128)(2,1)S(1)}, bf16[4096,256]{1,0:T(8,128)(2,1)}, bf16[4,1024,128]{2,1,0:T(8,128)(2,1)}, bf16[896,256]{1,0:T(8,128)(2,...) custom-call(s32[1,8]{1,0:T(1,128)} %count_ref.1, ...), custom_call_target="tpu_custom_call" | custom-call | tf_op jit(solution)/shard_map/tree_points/pallas_call | solution.py:604
  37.6 2.6 %all-to-all-done.light_ref = f32[8,32,512]{2,1,0:T(8,128)S(1)} async-done(((f32[8,32,512]{2,1,0:T(8,128)}), f32[8,32,512]{2,1,0:T(8,128)S(1)}, u32[]{:S(2)}, u32[]{:S(2)}) %all-to-all-start) | async-done | bytes 524320 | tf_op jit(solution)/shard_map/all_to_all | solution.py:588
  40.1 3.3 %tree_weights.1 = (bf16[32,4096]{1,0:T(8,128)(2,1)S(1)}, bf16[64,896]{1,0:T(8,128)(2,1)S(1)}, f32[128,128]{1,0:T(8,128)S(1)}) custom-call(bf16[4,1024,128]{2,1,0:T(8,128)(2,1)} %get-tuple-element.38.base_hbm, f32[3,256,128]{2,1,0:T(8,128)S(1)} %get-tuple-element.39.upper_tiles_ref, f32[128,128]{1,0:T(8,128)S(1)} %get-tuple-element.40.top_ref, ...), custom_call_target="tpu_custom_call" | custom-call | tf_op jit(solution)/shard_map/tree_weights/pallas_call | solution.py:633
  44.1 10.0 %near.1.near_ref = f32[32,4096]{1,0:T(8,128)S(1)} custom-call(s32[3,67]{1,0:T(4,128)} %copy-done.2, bf16[4096,256]{1,0:T(8,128)(2,1)} %get-tuple-element.49.a_hbm, bf16[144,4096]{1,0:T(8,128)(2,1)S(1)} %get-tuple-element.45.tree_ref, bf16[32,4096]{1,0:T(8,128)(2,1)S(1)} %get-tuple-element.50.w_ref), custom_call_target="tpu_custom_call" | custom-call | tf_op jit(solution)/shard_map/near/pallas_call | solution.py:654
  54.2 4.2 %far.1 = (f32[32,512]{1,0:T(8,128)S(1)}, f32[32,512]{1,0:T(8,128)S(1)}, f32[32,512]{1,0:T(8,128)S(1)}, f32[32,512]{1,0:T(8,128)S(1)}, f32[32,512]{1,0:T(8,128)S(...) custom-call(f32[1,128,128]{2,1,0:T(8,128)S(1)} %bitcast.5, ...), custom_call_target="tpu_custom_call" | custom-call | tf_op jit(solution)/shard_map/far/pallas_call | solution.py:671
  58.4 1.6 %collective-permute-start.9 = (f32[32,512]{1,0:T(8,128)S(1)}, f32[32,512]{1,0:T(8,128)S(1)}, u32[]{:S(2)}, u32[]{:S(2)}) collective-permute-start(f32[32,512]{1,0:T(8,128)S(1)} %get-tuple-element.51), channel_id=1, source_target_pairs={{0,4},{1,13},{2,6},{3,15},{4,0},{5,9},{6,2},{7,11},{8,12},{9,5},{1... | collective-permute-start | bytes 196616 | tf_op jit(solution)/shard_map/ppermute | solution.py:572
  60.0 0.9 %collective-permute-start.10 = (f32[32,512]{1,0:T(8,128)S(1)}, f32[32,512]{1,0:T(8,128)S(1)}, u32[]{:S(2)}, u32[]{:S(2)}) collective-permute-start(f32[32,512]{1,0:T(8,128)S(1)} %get-tuple-element.52), channel_id=1, source_target_pairs={{0,6},{1,15},{2,4},{3,13},{4,2},{5,11},{6,0},{7,9},{8,14},{9,7},{1... | collective-permute-start | bytes 196616 | tf_op jit(solution)/shard_map/ppermute | solution.py:572
  60.9 2.3 %collective-permute-start.11 = (f32[32,512]{1,0:T(8,128)S(1)}, f32[32,512]{1,0:T(8,128)S(1)}, u32[]{:S(2)}, u32[]{:S(2)}) collective-permute-start(f32[32,512]{1,0:T(8,128)S(1)} %get-tuple-element.53), channel_id=1, source_target_pairs={{0,12},{1,5},{2,14},{3,7},{4,8},{5,1},{6,10},{7,3},{8,4},{9,13},{1... | collective-permute-start | bytes 196616 | tf_op jit(solution)/shard_map/ppermute | solution.py:572
  63.2 2.0 %collective-permute-start.12 = (f32[32,512]{1,0:T(8,128)S(1)}, f32[32,512]{1,0:T(8,128)S(1)}, u32[]{:S(2)}, u32[]{:S(2)}) collective-permute-start(f32[32,512]{1,0:T(8,128)S(1)} %get-tuple-element.54), channel_id=1, source_target_pairs={{0,14},{1,7},{2,12},{3,5},{4,10},{5,3},{6,8},{7,1},{8,6},{9,15},{1... | collective-permute-start | bytes 196616 | tf_op jit(solution)/shard_map/ppermute | solution.py:572
  65.9 3.0 %collective-permute-start.14 = (f32[32,512]{1,0:T(8,128)S(1)}, f32[32,512]{1,0:T(8,128)S(1)}, u32[]{:S(2)}, u32[]{:S(2)}) collective-permute-start(f32[32,512]{1,0:T(8,128)S(1)} %get-tuple-element.56), channel_id=1, source_target_pairs={{0,2},{1,11},{2,0},{3,9},{4,6},{5,15},{6,4},{7,13},{8,10},{9,3},{1... | collective-permute-start | bytes 196616 | tf_op jit(solution)/shard_map/ppermute | solution.py:572
  68.9 3.9 %collective-permute-start.15 = (f32[32,512]{1,0:T(8,128)S(1)}, f32[32,512]{1,0:T(8,128)S(1)}, u32[]{:S(2)}, u32[]{:S(2)}) collective-permute-start(f32[32,512]{1,0:T(8,128)S(1)} %get-tuple-element.57), channel_id=1, source_target_pairs={{0,8},{1,1},{2,10},{3,3},{4,12},{5,5},{6,14},{7,7},{8,0},{9,9},{10... | collective-permute-start | bytes 196616 | tf_op jit(solution)/shard_map/ppermute | solution.py:572
  73.2 1.1 %collective-permute-start.16 = (f32[32,512]{1,0:T(8,128)S(1)}, f32[32,512]{1,0:T(8,128)S(1)}, u32[]{:S(2)}, u32[]{:S(2)}) collective-permute-start(f32[32,512]{1,0:T(8,128)S(1)} %get-tuple-element.58), channel_id=1, source_target_pairs={{0,10},{1,3},{2,8},{3,1},{4,14},{5,7},{6,12},{7,5},{8,2},{9,11},{1... | collective-permute-start | bytes 196616 | tf_op jit(solution)/shard_map/ppermute | solution.py:572
  75.1 3.4 %collective-permute-done.16.refs_7_ = f32[32,512]{1,0:T(8,128)S(1)} collective-permute-done((f32[32,512]{1,0:T(8,128)S(1)}, f32[32,512]{1,0:T(8,128)S(1)}, u32[]{:S(2)}, u32[]{:S(2)}) %collective-permute-start.16) | collective-permute-done | bytes 65568 | tf_op jit(solution)/shard_map/ppermute | solution.py:572
  78.4 1.9 %to_input_order.1 = f32[1024,128]{1,0:T(8,128)} custom-call(f32[8,128]{1,0:T(8,128)S(1)} %copy-done.1, f32[32,512]{1,0:T(8,128)S(1)} %collective-permute-done.9.refs_0_, f32[32,512]{1,0:T(8,128)S(1)} %collective-permute-done.10.refs_1_, f32[32,512]{1,0:T(8,128)S(1)} %collective-permute-done.11.refs_2_, f32[32,512]{1,0:T(8,128)S(1)} %collective-permute-done.12.refs_3_, ...), custom_call_target="tpu_custom_call" | custom-call | tf_op jit(solution)/shard_map/to_input_order/pallas_call | solution.py:688
  (25 shorter events, 4.9 us)
Async XLA Ops:
  2.7 1.6 %collective-permute-start = (f32[72,512]{1,0:T(8,128)}, f32[72,512]{1,0:T(8,128)S(1)}, u32[]{:S(2)}, u32[]{:S(2)}) collective-permute-start(f32[72,512]{1,0:T(8,128)} %get-tuple-element.33), channel_id=1, source_target_pairs={{0,0},{1,9},{2,2},{3,11},{4,4},{5,13},{6,6},{7,15},{8,8},{9,1},{10... | collective-permute-start | bytes 442376 | tf_op jit(solution)/shard_map/ppermute | solution.py:572
  4.3 8.8 %collective-permute-start.2 = (f32[72,512]{1,0:T(8,128)S(1)}, f32[72,512]{1,0:T(8,128)S(1)}, u32[]{:S(2)}, u32[]{:S(2)}) collective-permute-start(f32[72,512]{1,0:T(8,128)S(1)} %collective-permute-done.refs_0_), channel_id=1, source_target_pairs={{0,4},{2,6},{4,0},{6,2},{1,5},{3,7},{5,1},{7,3},{8,12},{10,14},{12... | collective-permute-start | bytes 442376 | tf_op jit(solution)/shard_map/ppermute | solution.py:582
  8.3 8.3 %collective-permute-start.1 = (f32[72,512]{1,0:T(8,128)S(1)}, f32[72,512]{1,0:T(8,128)S(1)}, u32[]{:S(2)}, u32[]{:S(2)}) collective-permute-start(f32[72,512]{1,0:T(8,128)S(1)} %collective-permute-done.refs_0_), channel_id=1, source_target_pairs={{0,2},{2,0},{4,6},{6,4},{1,3},{3,1},{5,7},{7,5},{8,10},{10,8},{12,... | collective-permute-start | bytes 442376 | tf_op jit(solution)/shard_map/ppermute | solution.py:582
  13.2 5.7 %collective-permute-start.3 = (f32[72,512]{1,0:T(8,128)S(1)}, f32[72,512]{1,0:T(8,128)S(1)}, u32[]{:S(2)}, u32[]{:S(2)}) collective-permute-start(f32[72,512]{1,0:T(8,128)S(1)} %collective-permute-done.2.refs_2_), channel_id=1, source_target_pairs={{0,2},{2,0},{4,6},{6,4},{1,3},{3,1},{5,7},{7,5},{8,10},{10,8},{12,... | collective-permute-start | bytes 442376 | tf_op jit(solution)/shard_map/ppermute | solution.py:582
  18.9 21.3 %all-to-all-start = ((f32[8,32,512]{2,1,0:T(8,128)}), f32[8,32,512]{2,1,0:T(8,128)S(1)}, u32[]{:S(2)}, u32[]{:S(2)}) async-start(f32[8,32,512]{2,1,0:T(8,128)} %bitcast.6), calls=%async_computation | async-start | bytes 1048576 | tf_op jit(solution)/shard_map/all_to_all | solution.py:588
  24.3 3.0 %collective-permute-start.4 = (f32[72,512]{1,0:T(8,128)S(1)}, f32[72,512]{1,0:T(8,128)S(1)}, u32[]{:S(2)}, u32[]{:S(2)}) collective-permute-start(f32[72,512]{1,0:T(8,128)S(1)} %collective-permute-done.refs_0_), channel_id=1, source_target_pairs={{0,1},{1,0},{2,3},{3,2},{4,5},{5,4},{6,7},{7,6},{8,9},{9,8},{10,11... | collective-permute-start | bytes 442376 | tf_op jit(solution)/shard_map/ppermute | solution.py:585
  26.3 1.4 %collective-permute-start.5 = (f32[72,512]{1,0:T(8,128)S(1)}, f32[72,512]{1,0:T(8,128)S(1)}, u32[]{:S(2)}, u32[]{:S(2)}) collective-permute-start(f32[72,512]{1,0:T(8,128)S(1)} %collective-permute-done.1.refs_1_), channel_id=1, source_target_pairs={{0,1},{1,0},{2,3},{3,2},{4,5},{5,4},{6,7},{7,6},{8,9},{9,8},{10,11... | collective-permute-start | bytes 442376 | tf_op jit(solution)/shard_map/ppermute | solution.py:585
  26.4 1.5 %collective-permute-start.6 = (f32[72,512]{1,0:T(8,128)S(1)}, f32[72,512]{1,0:T(8,128)S(1)}, u32[]{:S(2)}, u32[]{:S(2)}) collective-permute-start(f32[72,512]{1,0:T(8,128)S(1)} %collective-permute-done.2.refs_2_), channel_id=1, source_target_pairs={{0,1},{1,0},{2,3},{3,2},{4,5},{5,4},{6,7},{7,6},{8,9},{9,8},{10,11... | collective-permute-start | bytes 442376 | tf_op jit(solution)/shard_map/ppermute | solution.py:585
  26.8 1.4 %collective-permute-start.7 = (f32[72,512]{1,0:T(8,128)S(1)}, f32[72,512]{1,0:T(8,128)S(1)}, u32[]{:S(2)}, u32[]{:S(2)}) collective-permute-start(f32[72,512]{1,0:T(8,128)S(1)} %collective-permute-done.3.refs_3_), channel_id=1, source_target_pairs={{0,1},{1,0},{2,3},{3,2},{4,5},{5,4},{6,7},{7,6},{8,9},{9,8},{10,11... | collective-permute-start | bytes 442376 | tf_op jit(solution)/shard_map/ppermute | solution.py:585
  37.0 0.6 copy-start.2
  43.5 10.7 %collective-permute-start.8 = (f32[128,128]{1,0:T(8,128)S(1)}, f32[128,128]{1,0:T(8,128)S(1)}, u32[]{:S(2)}, u32[]{:S(2)}) collective-permute-start(f32[128,128]{1,0:T(8,128)S(1)} %get-tuple-element.43), channel_id=1, source_target_pairs={{0,8},{8,0},{1,9},{9,1},{2,10},{10,2},{3,11},{11,3},{4,12},{12,4},... | collective-permute-start | bytes 196616 | tf_op jit(solution)/shard_map/ppermute | solution.py:508
  54.2 24.3 %copy-start = (f32[1024,128]{1,0:T(8,128)S(1)}, f32[1024,128]{1,0:T(8,128)}, u32[]{:S(2)}) copy-start(f32[1024,128]{1,0:T(8,128)} %refs_8_.1) | copy-start | bytes 1572868
  54.2 24.2 %copy-start.1 = (f32[8,128]{1,0:T(8,128)S(1)}, f32[8,128]{1,0:T(8,128)}, u32[]{:S(2)}) copy-start(f32[8,128]{1,0:T(8,128)} %get-tuple-element.32.pos_ref) | copy-start | bytes 12292
  58.4 7.5 %collective-permute-start.9 = (f32[32,512]{1,0:T(8,128)S(1)}, f32[32,512]{1,0:T(8,128)S(1)}, u32[]{:S(2)}, u32[]{:S(2)}) collective-permute-start(f32[32,512]{1,0:T(8,128)S(1)} %get-tuple-element.51), channel_id=1, source_target_pairs={{0,4},{1,13},{2,6},{3,15},{4,0},{5,9},{6,2},{7,11},{8,12},{9,5},{1... | collective-permute-start | bytes 196616 | tf_op jit(solution)/shard_map/ppermute | solution.py:572
  60.0 8.9 %collective-permute-start.10 = (f32[32,512]{1,0:T(8,128)S(1)}, f32[32,512]{1,0:T(8,128)S(1)}, u32[]{:S(2)}, u32[]{:S(2)}) collective-permute-start(f32[32,512]{1,0:T(8,128)S(1)} %get-tuple-element.52), channel_id=1, source_target_pairs={{0,6},{1,15},{2,4},{3,13},{4,2},{5,11},{6,0},{7,9},{8,14},{9,7},{1... | collective-permute-start | bytes 196616 | tf_op jit(solution)/shard_map/ppermute | solution.py:572
  60.9 12.3 %collective-permute-start.11 = (f32[32,512]{1,0:T(8,128)S(1)}, f32[32,512]{1,0:T(8,128)S(1)}, u32[]{:S(2)}, u32[]{:S(2)}) collective-permute-start(f32[32,512]{1,0:T(8,128)S(1)} %get-tuple-element.53), channel_id=1, source_target_pairs={{0,12},{1,5},{2,14},{3,7},{4,8},{5,1},{6,10},{7,3},{8,4},{9,13},{1... | collective-permute-start | bytes 196616 | tf_op jit(solution)/shard_map/ppermute | solution.py:572
  63.2 11.1 %collective-permute-start.12 = (f32[32,512]{1,0:T(8,128)S(1)}, f32[32,512]{1,0:T(8,128)S(1)}, u32[]{:S(2)}, u32[]{:S(2)}) collective-permute-start(f32[32,512]{1,0:T(8,128)S(1)} %get-tuple-element.54), channel_id=1, source_target_pairs={{0,14},{1,7},{2,12},{3,5},{4,10},{5,3},{6,8},{7,1},{8,6},{9,15},{1... | collective-permute-start | bytes 196616 | tf_op jit(solution)/shard_map/ppermute | solution.py:572
  65.2 9.1 %collective-permute-start.13 = (f32[32,512]{1,0:T(8,128)S(1)}, f32[32,512]{1,0:T(8,128)S(1)}, u32[]{:S(2)}, u32[]{:S(2)}) collective-permute-start(f32[32,512]{1,0:T(8,128)S(1)} %get-tuple-element.55), channel_id=1, source_target_pairs={{0,0},{1,9},{2,2},{3,11},{4,4},{5,13},{6,6},{7,15},{8,8},{9,1},{10... | collective-permute-start | bytes 196616 | tf_op jit(solution)/shard_map/ppermute | solution.py:572
  65.9 8.5 %collective-permute-start.14 = (f32[32,512]{1,0:T(8,128)S(1)}, f32[32,512]{1,0:T(8,128)S(1)}, u32[]{:S(2)}, u32[]{:S(2)}) collective-permute-start(f32[32,512]{1,0:T(8,128)S(1)} %get-tuple-element.56), channel_id=1, source_target_pairs={{0,2},{1,11},{2,0},{3,9},{4,6},{5,15},{6,4},{7,13},{8,10},{9,3},{1... | collective-permute-start | bytes 196616 | tf_op jit(solution)/shard_map/ppermute | solution.py:572
  68.9 6.2 %collective-permute-start.15 = (f32[32,512]{1,0:T(8,128)S(1)}, f32[32,512]{1,0:T(8,128)S(1)}, u32[]{:S(2)}, u32[]{:S(2)}) collective-permute-start(f32[32,512]{1,0:T(8,128)S(1)} %get-tuple-element.57), channel_id=1, source_target_pairs={{0,8},{1,1},{2,10},{3,3},{4,12},{5,5},{6,14},{7,7},{8,0},{9,9},{10... | collective-permute-start | bytes 196616 | tf_op jit(solution)/shard_map/ppermute | solution.py:572
  73.2 5.2 %collective-permute-start.16 = (f32[32,512]{1,0:T(8,128)S(1)}, f32[32,512]{1,0:T(8,128)S(1)}, u32[]{:S(2)}, u32[]{:S(2)}) collective-permute-start(f32[32,512]{1,0:T(8,128)S(1)} %get-tuple-element.58), channel_id=1, source_target_pairs={{0,10},{1,3},{2,8},{3,1},{4,14},{5,7},{6,12},{7,5},{8,2},{9,11},{1... | collective-permute-start | bytes 196616 | tf_op jit(solution)/shard_map/ppermute | solution.py:572

commit v11 on v10

--- a/solution.py
+++ b/solution.py
@@ -169,7 +169,7 @@
         self.per = rows // self.count
 
     def lanes(self, index):
-        return aligned(index * self.per, self.per, LANES)
+        return slice(index * self.per, (index + 1) * self.per)
 
     def message(self, group):
         if not self.fine:
@@ -255,17 +255,21 @@
     blocks, rows = layout.blocks, layout.rows
 
     def keep(node, found):
-        at = aligned(node * SK, SK, SK)
+        at = slice(node * SK, (node + 1) * SK)
         sk_t[:, at] = found.astype(bf16)
         sk_ref[at, 0:128], sk_ref[at, 128:256] = feature_rows(found[0:64], found[64:128], found[136:144])
-        feature_columns(sk_bt, slice(0, SK), found)
-
-    def block(index, carry):
+        feature_columns(sk_bt, at, found)
+
+    high_parts = rows // LOW
+    infos = []
+    for index in range(blocks):
         tail = layout.gather(place_refs, index, slice(TAIL, PLACE_ROWS))
         slots = tail[SLOT : SLOT + 1]
-        slot_ref[pl.ds(index, 1), :] = slots
-        info = layout.info(place_refs, small_ref, index)
-        info_ref[index] = info
+        slot_ref[index : index + 1, :] = slots
+        infos.append(layout.info(place_refs, small_ref, index))
+        info_ref[index] = infos[-1]
+        low_part, high_part = parts_of(slots)
+        low_by_column(low_hot.at[index], low_part.astype(f32))
         points = layout.gather(place_refs, index, slice(0, TAIL))
         high, low = two(points)
         nh, nm, nl = three(tail[NORM : NORM + 1])
@@ -274,28 +278,32 @@
         is_norm = ((sub >= 3) & (sub < 6)) | ((sub >= 8) & (sub < 11))
         is_one = (sub < 3) | ((sub >= 11) & (sub < 14))
         extra = jnp.where(is_norm, norms, jnp.where(is_one, 1.0, 0.0))
-        low_part, high_part = parts_of(slots)
-        low_by_column(low_hot, low_part.astype(f32))
-        for h in range(rows // LOW):
+        for h in range(high_parts):
             here = high_part == h
-            masked[h * COORD : h * COORD + 64, :] = jnp.where(here, high.astype(f32), 0.0).astype(bf16)
-            masked[h * COORD + 64 : h * COORD + 128, :] = jnp.where(here, low.astype(f32), 0.0).astype(bf16)
-            masked[h * COORD + 128 : (h + 1) * COORD, :] = jnp.where(here, extra, 0.0).astype(bf16)
-        placed = nn(masked[...], low_hot[...])
-        for h in range(rows // LOW):
+            at = h * COORD
+            masked[index, at : at + 64, :] = jnp.where(here, high.astype(f32), 0.0).astype(bf16)
+            masked[index, at + 64 : at + 128, :] = jnp.where(here, low.astype(f32), 0.0).astype(bf16)
+            masked[index, at + 128 : at + COORD, :] = jnp.where(here, extra, 0.0).astype(bf16)
+    copies = []
+    for index in range(blocks):
+        placed = nn(masked[index], low_hot[index])
+        for h in range(high_parts):
             part = placed[h * COORD : (h + 1) * COORD]
-            at = aligned(index * rows + h * LOW, LOW, LOW)
+            at = slice(index * rows + h * LOW, index * rows + (h + 1) * LOW)
             tree_ref[:, at] = part.astype(bf16)
             a_ref[at, 0:128], a_ref[at, 128:256] = feature_rows(part[0:64], part[64:128], part[136:144])
-        picked = onehot(iota((rows, SK), 0) == info[BASE : BASE + 1].astype(jnp.int32))
-        mine = aligned(index * rows, rows, rows)
-        pltpu.make_async_copy(a_ref.at[mine], a_hbm.at[mine], sems.at[0, index]).start()
+        mine = slice(index * rows, (index + 1) * rows)
+        copies.append(pltpu.make_async_copy(a_ref.at[mine], a_hbm.at[mine], sems.at[0, index]))
+        copies[-1].start()
+    for index in range(blocks):
+        mine = slice(index * rows, (index + 1) * rows)
+        picked = onehot(iota((rows, SK), 0) == infos[index][BASE : BASE + 1].astype(jnp.int32))
         keep(index, nn(tree_ref[:, mine], picked))
-        base_ref[index] = jnp.exp(nn(a_ref[mine, :], sk_bt[...])).astype(bf16)
-        pltpu.make_async_copy(base_ref.at[index], base_hbm.at[index], sems.at[1, index]).start()
-        return carry
-
-    lax.fori_loop(0, blocks, block, 0)
+    for index in range(blocks):
+        mine = slice(index * rows, (index + 1) * rows)
+        base_ref[index] = jnp.exp(nn(a_ref[mine, :], sk_bt[:, index * SK : (index + 1) * SK])).astype(bf16)
+        copies.append(pltpu.make_async_copy(base_ref.at[index], base_hbm.at[index], sems.at[1, index]))
+        copies[-1].start()
     start, count, offset, total = 0, blocks, 0, blocks * trees
     while count > 1:
         nodes = count // 2
@@ -305,7 +313,7 @@
             picked = onehot(iota((2 * SK, SK), 0) == upper_ref[pl.ds(row, 1), :])
             here = start + count + j
             keep(here, nn(sk_t[:, pair], picked))
-            upper_tiles_ref[here - blocks] = jnp.exp(nn(sk_ref[pair, :], sk_bt[...]))
+            upper_tiles_ref[here - blocks] = jnp.exp(nn(sk_ref[pair, :], sk_bt[:, here * SK : (here + 1) * SK]))
         total = total // 2
         offset = offset + total
         start, count = start + count, nodes
@@ -314,10 +322,8 @@
     top_ref[64:72, :] = found[128:136]
     top_ref[72:128, :] = jnp.zeros((56, SK), f32)
     list_tiles(count_ref, list_ref, tiles, times)
-    for index in range(blocks):
-        mine = slice(index * rows, (index + 1) * rows)
-        pltpu.make_async_copy(a_ref.at[mine], a_hbm.at[mine], sems.at[0, index]).wait()
-        pltpu.make_async_copy(base_ref.at[index], base_hbm.at[index], sems.at[1, index]).wait()
+    for copy in copies:
+        copy.wait()
 
 
 def weights_kernel(
@@ -330,25 +336,24 @@
         pltpu.make_async_copy(base_hbm.at[index], base_ref.at[index], sems.at[index]).start()
 
     def keep(node, coef):
-        coef_ref[:, aligned(node * SK, SK, SK)] = stack_two(coef)
+        coef_ref[:, node * SK : (node + 1) * SK] = stack_two(coef)
         pack_ref[LANES - width :, :] = coef
 
-    def block(index, carry):
-        low_part, high_part = parts_of(slot_ref[pl.ds(index, 1), :])
-        low_by_column(low_hot, low_part.astype(f32))
+    for index in range(blocks):
+        low_part, high_part = parts_of(slot_ref[index : index + 1, :])
+        low_by_column(low_hot.at[index], low_part.astype(f32))
         light = [light_ref[layout.message(g), :, layout.lanes(index)] for g in range(layout.count)]
         light = lanes_of(light)
         for h in range(rows // LOW):
-            masked[h * width : (h + 1) * width, :] = jnp.where(high_part == h, light, 0.0).astype(bf16)
-        placed = nn(masked[...], low_hot[...])
-        parts = [placed[h * width : (h + 1) * width] for h in range(rows // LOW)]
-        own = jnp.concatenate(parts, 1).astype(bf16)
-        w_ref[:, aligned(index * rows, rows, rows)] = own
+            masked[index, h * width : (h + 1) * width, :] = jnp.where(high_part == h, light, 0.0).astype(bf16)
+    for index in range(blocks):
+        placed = nn(masked[index], low_hot[index])
+        for h in range(rows // LOW):
+            at = index * rows + h * LOW
+            w_ref[:, at : at + LOW] = placed[h * width : (h + 1) * width].astype(bf16)
+    for index in range(blocks):
         pltpu.make_async_copy(base_hbm.at[index], base_ref.at[index], sems.at[index]).wait()
-        keep(index, nn(own, base_ref[index]))
-        return carry
-
-    lax.fori_loop(0, blocks, block, 0)
+        keep(index, nn(w_ref[:, index * rows : (index + 1) * rows], base_ref[index]))
     start, count = 0, blocks
     while count > 1:
         for j in range(count // 2):
@@ -415,10 +420,13 @@
 
 
 def far_kernel(layout, low_levels, pack_ref, slot_ref, info_ref, tree_ref, sk_ref, coef_ref, near_ref, *refs):
-    out_refs, (tops, coefs, low_hot, bt_ref) = refs[: layout.count], refs[layout.count :]
+    out_refs, refs = refs[: layout.count], refs[layout.count :]
+    tops, coefs, scaled, low_hot, bt_ref, sums, masked = refs[:7]
+    powers, tiles = refs[7:9], refs[9:11]
     blocks, rows = layout.blocks, layout.rows
     ups, width = pack_ref.shape[0], out_refs[0].shape[0]
     levels = low_levels + ups
+    per_block = rows // LEAF
     lane = iota((1, SK), 1)
     for up in range(ups):
         pack = pack_ref[up]
@@ -427,47 +435,66 @@
         extra = jnp.where(sub == 0, pack[67:68], jnp.where(sub == 1, pack[68:69], pack[69:70]))
         extra = jnp.where(sub < 3, extra, jnp.where(sub < 6, 1.0, 0.0))
         at = slice((low_levels + up) * SK, (low_levels + up + 1) * SK)
-        tops[at, 0:128], tops[at, 128:256] = feature_rows(high.astype(f32), low.astype(f32), extra)
-        coefs[:, at] = stack_two(pack[LANES - width :])
-
-    def block(index, carry):
+        rows_of = feature_rows(high.astype(f32), low.astype(f32), extra)
+        coef = stack_two(pack[LANES - width :])
+        for index in range(blocks):
+            tops[index, at, 0:128], tops[index, at, 128:256] = rows_of
+            coefs[index, :, at] = coef
+    for index in range(blocks):
         node, start, count = index, 0, blocks
         for level in range(low_levels):
             at = slice(level * SK, (level + 1) * SK)
-            other = aligned((start + (node ^ 1)) * SK, SK, SK)
-            tops[at, :] = sk_ref[other, :]
-            coefs[:, at] = coef_ref[:, other]
+            other = slice((start + (node ^ 1)) * SK, (start + (node ^ 1) + 1) * SK)
+            tops[index, at, :] = sk_ref[other, :]
+            coefs[index, :, at] = coef_ref[:, other]
             node, start, count = node // 2, start + count, count // 2
-        low_part, high_part = parts_of(slot_ref[pl.ds(index, 1), :])
-        for c in range(rows // LANES):
-            at = slice(c * LANES, (c + 1) * LANES)
-            low_hot[:, at] = onehot(iota((LOW, LANES), 0) == low_part[:, at])
-        info = info_ref[index]
-        totals = []
-        for leaf in range(rows // LEAF):
-            flags = info[FLAGS + leaf : FLAGS + leaf + 1]
+        for leaf in range(per_block):
+            here = (index * per_block + leaf) * LEAF
+            feature_columns(bt_ref, slice(here, here + LEAF), tree_ref[:, here : here + LEAF])
+            flags = info_ref[index, FLAGS + leaf : FLAGS + leaf + 1, :]
             used = []
             for level in range(levels):
                 flag = jnp.sum(jnp.where(lane == level, flags, 0.0), axis=1, keepdims=True)
                 used.append(jnp.broadcast_to(flag, (1, SK)))
-            here = aligned(index * rows + leaf * LEAF, LEAF, LEAF)
-            feature_columns(bt_ref, slice(0, LEAF), tree_ref[:, here])
-            tile = jnp.exp(nn(tops[...], bt_ref[...])).astype(bf16)
-            scaled = (coefs[...].astype(f32) * jnp.concatenate(used, 1)).astype(bf16)
-            far = nn(scaled, tile)
-            totals.append(near_ref[:, here] + far[:width] + far[width:])
-        both = stack_two(jnp.concatenate(totals, 1))
-        parts = [both[:, h * LOW : (h + 1) * LOW] for h in range(rows // LOW)]
-        moved = nn(jnp.concatenate(parts, 0), low_hot[...])
+            used = jnp.concatenate(used, 1)
+            scaled[index * per_block + leaf] = (coefs[index].astype(f32) * used).astype(bf16)
+
+    def exponents(leaf):
+        powers[leaf % 2][...] = nn(tops[leaf // per_block], bt_ref[:, leaf * LEAF : (leaf + 1) * LEAF])
+
+    def product(leaf):
+        here = slice(leaf * LEAF, (leaf + 1) * LEAF)
+        far = nn(scaled[leaf], tiles[leaf % 2][...])
+        sums[:, here] = near_ref[:, here] + far[:width] + far[width:]
+
+    leaves = blocks * per_block
+    exponents(0)
+    for leaf in range(leaves):
+        if leaf + 1 < leaves:
+            exponents(leaf + 1)
+        tiles[leaf % 2][...] = jnp.exp(powers[leaf % 2][...]).astype(bf16)
+        if leaf:
+            product(leaf - 1)
+    product(leaves - 1)
+
+    high_parts = []
+    for index in range(blocks):
+        low_part, high_part = parts_of(slot_ref[index : index + 1, :])
+        high_parts.append(high_part)
+        for c in range(rows // LANES):
+            at = slice(c * LANES, (c + 1) * LANES)
+            low_hot[index, :, at] = onehot(iota((LOW, LANES), 0) == low_part[:, at])
+        for h in range(rows // LOW):
+            at = index * rows + h * LOW
+            masked[index, h * 2 * width : (h + 1) * 2 * width, :] = stack_two(sums[:, at : at + LOW])
+    for index in range(blocks):
+        moved = nn(masked[index], low_hot[index])
         result = jnp.zeros((2 * width, rows), f32)
         for h in range(rows // LOW):
-            result = jnp.where(high_part == h, moved[h * 2 * width : (h + 1) * 2 * width], result)
+            result = jnp.where(high_parts[index] == h, moved[h * 2 * width : (h + 1) * 2 * width], result)
         result = result[:width] + result[width:]
         for g, out_ref in enumerate(out_refs):
             out_ref[:, layout.lanes(index)] = result[:, g * layout.per : (g + 1) * layout.per]
-        return carry
-
-    lax.fori_loop(0, blocks, block, 0)
 
 
 def far_first(blocks, count):
@@ -550,16 +577,6 @@
         compiler_params=params(),
         name="sort_points",
     )(tree_slot.reshape(rows // LANES, LANES), points.T, skeleton_base, far_use)
-    light = pl.pallas_call(
-        light_kernel,
-        out_shape=shaped((rows // split, columns, split), f32),
-        in_specs=[spec()] * 2,
-        out_specs=spec(),
-        scratch_shapes=[vm((rows // LOW * LANES, rows), bf16), vm((rows, LOW), bf16)],
-        compiler_params=params(),
-        name="sort_weights",
-    )(pos, weights)
-
     axes = ("leaf", "sub", "rep")
 
     def swap(value, step, other=0):
@@ -574,6 +591,17 @@
     def swap_all(values):
         return [swap(values[g], g % blocks, g // blocks) for g in far_first(blocks, len(values))]
 
+    def sorted_light():
+        return pl.pallas_call(
+            light_kernel,
+            out_shape=shaped((rows // split, columns, split), f32),
+            in_specs=[spec()] * 2,
+            out_specs=spec(),
+            scratch_shapes=[vm((rows // LOW * LANES, rows), bf16), vm((rows, LOW), bf16)],
+            compiler_params=params(),
+            name="sort_weights",
+        )(pos, weights)
+
     if fine:
         place = {0: swap(place, 0)}
         stride = blocks // 2
@@ -581,10 +609,10 @@
             for step in sorted(place):
                 place[step | stride] = lax.ppermute(place[step], "sub", [(i, i ^ stride) for i in range(blocks)])
             stride //= 2
-        place, light = lax.optimization_barrier((place, light))
+        place[blocks // 2], pos = lax.optimization_barrier((place[blocks // 2], pos))
         theirs = {step: lax.ppermute(one, "rep", [(0, 1), (1, 0)]) for step, one in place.items()}
         place = [place[step] for step in range(blocks)] + [theirs[step] for step in range(blocks)]
-        light = light.reshape(devices, width, part)
+        light = sorted_light().reshape(devices, width, part)
         light = lax.all_to_all(light, ("leaf", "sub"), split_axis=0, concat_axis=0, tiled=True)
         small = []
     else:
@@ -595,7 +623,7 @@
         place = lax.all_gather(place, "sub", axis=0, tiled=False)
         place = place.transpose(1, 0, 2, 3).reshape(devices, PLACE_ROWS, blocks, per)
         place = [place.transpose(1, 2, 0, 3).reshape(PLACE_ROWS, total)]
-        light = light.reshape(columns, trees, part).transpose(1, 0, 2).reshape(devices, width, part)
+        light = sorted_light().reshape(columns, trees, part).transpose(1, 0, 2).reshape(devices, width, part)
         light = lax.all_to_all(light, ("leaf", "sub"), split_axis=0, concat_axis=0, tiled=True)
         light = light.reshape(devices, width, blocks, per)
         light = light.transpose(1, 2, 0, 3).reshape(1, width, total)
@@ -612,17 +640,17 @@
             vm((SK, LANES), f32),
             vm((blocks, rows), f32),
             vm((blocks, 8, SK), f32),
-            shaped((3, leaves * leaves + 3), jnp.int32),
+            pltpu.MemorySpace.HBM((3, leaves * leaves + 3), jnp.int32),
         ),
         in_specs=[spec(SMEM)] * 2 + [spec()] * (1 + len(small) + layout.count),
         out_specs=(spec(), spec(pl.ANY), spec(pl.ANY)) + (spec(),) * 5 + (spec(SMEM),),
         scratch_shapes=[
-            vm((rows // LOW * COORD, rows), bf16),
-            vm((rows, LOW), bf16),
+            vm((blocks, rows // LOW * COORD, rows), bf16),
+            vm((blocks, rows, LOW), bf16),
             vm((total, FEAT), bf16),
             vm((blocks, rows, SK), bf16),
             vm((COORD, nodes * SK), bf16),
-            vm((FEAT, SK), bf16),
+            vm((FEAT, nodes * SK), bf16),
             pltpu.SemaphoreType.DMA((2, blocks)),
             pltpu.SMEM((leaves,), jnp.int32),
         ],
@@ -640,8 +668,8 @@
         in_specs=[spec(pl.ANY)] + [spec()] * 4,
         out_specs=(spec(),) * 3,
         scratch_shapes=[
-            vm((rows // LOW * width, rows), bf16),
-            vm((rows, LOW), bf16),
+            vm((blocks, rows // LOW * width, rows), bf16),
+            vm((blocks, rows, LOW), bf16),
             vm((blocks, rows, SK), bf16),
             pltpu.SemaphoreType.DMA((blocks,)),
         ],
@@ -673,7 +701,17 @@
         out_shape=(arrive,) * layout.count,
         in_specs=[spec()] * 7,
         out_specs=(spec(),) * layout.count,
-        scratch_shapes=[vm((levels * SK, FEAT), bf16), vm((2 * width, levels * SK), bf16), vm((LOW, rows), bf16), vm((FEAT, LEAF), bf16)],
+        scratch_shapes=[
+            vm((blocks, levels * SK, FEAT), bf16),
+            vm((blocks, 2 * width, levels * SK), bf16),
+            vm((leaves, 2 * width, levels * SK), bf16),
+            vm((blocks, LOW, rows), bf16),
+            vm((FEAT, total), bf16),
+            vm((width, total), f32),
+            vm((blocks, rows // LOW * 2 * width, LOW), bf16),
+        ]
+        + [vm((levels * SK, LEAF), f32)] * 2
+        + [vm((levels * SK, LEAF), bf16)] * 2,
         compiler_params=params(40),
         name="far",
     )(packs, *[held(one) for one in (slots, info, tree, sk, coefs, near)])

time: 81.1 us -> 85.6 us (1.055)
  starting transfers between devices: 32.2 us -> 41.1 us
  Pallas kernels: 33.6 us -> 29 us
  waiting for transfers between devices: 13.8 us -> 14.9 us
    ppermute x4, starting transfers between devices: 2.54 us -> 10.6 us  [body(): lax.ppermute(one, 'rep', [(0, 1), (1, 0)])]
    ppermute x3, waiting for transfers between devices: 5.51 us -> 10.3 us  [body(): lax.ppermute(place[step], 'sub', [(i, i ^ stride) for i in range(blocks)])]
    pallas_call x1, Pallas kernels: 8.8 us -> 5.36 us  [body(): pl.pallas_call(functools.partial(points_kernel, layout, trees), out_shape...]
    all_to_all x1, waiting for transfers between devices: 2.57 us -> 0.01 us  [body(): lax.all_to_all(light, ('leaf', 'sub'), split_axis=0, concat_axis=0, tiled...]
    pallas_call x1, Pallas kernels: 4.23 us -> 2.77 us  [body(): pl.pallas_call(functools.partial(far_kernel, layout, low_levels), out_sha...]
    ppermute x9, waiting for transfers between devices: 4.46 us -> 3.52 us  [swap(): return lax.ppermute(value, axes, pairs)]
    ppermute x1, starting transfers between devices: 0.63 us -> 1.54 us  [upper_levels(): other = lax.ppermute(own, 'leaf', [(i, i ^ stride) for i in range(trees)])]
    pallas_call x1, Pallas kernels: 10 us -> 10.9 us  [body(): pl.pallas_call(near_kernel, out_shape=vm((width, total), f32), in_specs=[...]
  transfers between devices with their start and end apart: 18 -> 18, of which waited for: 10 -> 6; matrix products, arithmetic and copies ran while one was open for 0% -> 0% of each run, Pallas kernels for 27% -> 19%
where the time goes in v11:
time: 85.6 us; the launch traced here: 85 us
  starting transfers between devices  41.1 us (48%)
  Pallas kernels  29 us (34%)
  waiting for transfers between devices  14.9 us (17%)
    ppermute x9, starting transfers between devices, swap(): return lax.ppermute(value, axes, pairs)  16.7 us
    pallas_call x1, Pallas kernels, body(): pl.pallas_call(near_kernel, out_shape=vm((width, total), f32), in_specs=[...  10.9 us
    ppermute x4, starting transfers between devices, body(): lax.ppermute(one, 'rep', [(0, 1), (1, 0)])  10.6 us
    ppermute x3, waiting for transfers between devices, body(): lax.ppermute(place[step], 'sub', [(i, i ^ stride) for i in range(blocks)])  10.3 us
    ppermute x3, starting transfers between devices, body(): lax.ppermute(place[step], 'sub', [(i, i ^ stride) for i in range(blocks)])  6.1 us
    all_to_all x1, starting transfers between devices, body(): lax.all_to_all(light, ('leaf', 'sub'), split_axis=0, concat_axis=0, tiled...  6.02 us
    pallas_call x1, Pallas kernels, body(): pl.pallas_call(functools.partial(points_kernel, layout, trees), out_shape...  5.36 us
    ppermute x9, waiting for transfers between devices, swap(): return lax.ppermute(value, axes, pairs)  3.52 us
  transfers between devices with their start and end apart: 18, of which 6 were waited for; matrix products, arithmetic and copies ran while one was open for 0% of the time, Pallas kernels for 19%

profile of v11, /device:TPU:0, one launch (start us, length us, event | category | flops | bytes accessed | tf_op | source)
XLA Modules:
  0.0 85.0 jit_solution(10677471773239019892)
XLA Ops:
  0.0 2.7 %sort_points.1 = (f32[72,512]{1,0:T(8,128)}, f32[8,128]{1,0:T(8,128)}) custom-call(s32[8,128]{1,0:T(8,128)} %bitcast.8, f32[64,1024]{1,0:T(8,128)} %bitcast.7, s32[1,128]{1,0:T(1,128)} %base_ref.1, s32[2,3]{1,0:T(2,128)} %flag_ref.1), custom_call_target="tpu_custom_call" | custom-call | tf_op jit(solution)/shard_map/sort_points/pallas_call | solution.py:571
  2.7 1.6 %collective-permute-start = (f32[72,512]{1,0:T(8,128)}, f32[72,512]{1,0:T(8,128)S(1)}, u32[]{:S(2)}, u32[]{:S(2)}) collective-permute-start(f32[72,512]{1,0:T(8,128)} %get-tuple-element.29), channel_id=1, source_target_pairs={{0,0},{1,9},{2,2},{3,11},{4,4},{5,13},{6,6},{7,15},{8,8},{9,1},{10... | collective-permute-start | bytes 442376 | tf_op jit(solution)/shard_map/ppermute | solution.py:589
  4.3 4.0 %collective-permute-start.1 = (f32[72,512]{1,0:T(8,128)S(1)}, f32[72,512]{1,0:T(8,128)S(1)}, u32[]{:S(2)}, u32[]{:S(2)}) collective-permute-start(f32[72,512]{1,0:T(8,128)S(1)} %collective-permute-done.refs_0_), channel_id=1, source_target_pairs={{0,4},{2,6},{4,0},{6,2},{1,5},{3,7},{5,1},{7,3},{8,12},{10,14},{12... | collective-permute-start | bytes 442376 | tf_op jit(solution)/shard_map/ppermute | solution.py:610
  8.3 4.7 %collective-permute-done.1.refs_2_ = f32[72,512]{1,0:T(8,128)S(1)} collective-permute-done((f32[72,512]{1,0:T(8,128)S(1)}, f32[72,512]{1,0:T(8,128)S(1)}, u32[]{:S(2)}, u32[]{:S(2)}) %collective-permute-start.1) | collective-permute-done | bytes 147488 | tf_op jit(solution)/shard_map/ppermute | solution.py:610
  13.0 2.6 %sort_weights.1 = f32[2,128,512]{2,1,0:T(8,128)} custom-call(f32[8,128]{1,0:T(8,128)} %get-tuple-element.31.pos_ref, f32[1024,128]{1,0:T(8,128)} %refs_8_.1), custom_call_target="tpu_custom_call" | custom-call | tf_op jit(solution)/shard_map/sort_weights/pallas_call | solution.py:595
  15.6 6.0 %all-to-all-start = ((f32[8,32,512]{2,1,0:T(8,128)}), f32[8,32,512]{2,1,0:T(8,128)S(1)}, u32[]{:S(2)}, u32[]{:S(2)}) async-start(f32[8,32,512]{2,1,0:T(8,128)} %bitcast.6), calls=%async_computation | async-start | bytes 1048576 | tf_op jit(solution)/shard_map/all_to_all | solution.py:616
  21.6 2.0 %collective-permute-start.2 = (f32[72,512]{1,0:T(8,128)S(1)}, f32[72,512]{1,0:T(8,128)S(1)}, u32[]{:S(2)}, u32[]{:S(2)}) collective-permute-start(f32[72,512]{1,0:T(8,128)S(1)} %collective-permute-done.refs_0_), channel_id=1, source_target_pairs={{0,2},{2,0},{4,6},{6,4},{1,3},{3,1},{5,7},{7,5},{8,10},{10,8},{12,... | collective-permute-start | bytes 442376 | tf_op jit(solution)/shard_map/ppermute | solution.py:610
  23.7 2.7 %collective-permute-start.4 = (f32[72,512]{1,0:T(8,128)S(1)}, f32[72,512]{1,0:T(8,128)S(1)}, u32[]{:S(2)}, u32[]{:S(2)}) collective-permute-start(f32[72,512]{1,0:T(8,128)S(1)} %collective-permute-done.refs_0_), channel_id=1, source_target_pairs={{0,1},{1,0},{2,3},{3,2},{4,5},{5,4},{6,7},{7,6},{8,9},{9,8},{10,11... | collective-permute-start | bytes 442376 | tf_op jit(solution)/shard_map/ppermute | solution.py:613
  26.4 5.6 %collective-permute-done.2.refs_1_ = f32[72,512]{1,0:T(8,128)S(1)} collective-permute-done((f32[72,512]{1,0:T(8,128)S(1)}, f32[72,512]{1,0:T(8,128)S(1)}, u32[]{:S(2)}, u32[]{:S(2)}) %collective-permute-start.2) | collective-permute-done | bytes 147488 | tf_op jit(solution)/shard_map/ppermute | solution.py:610
  32.0 6.4 %collective-permute-start.5 = (f32[72,512]{1,0:T(8,128)S(1)}, f32[72,512]{1,0:T(8,128)S(1)}, u32[]{:S(2)}, u32[]{:S(2)}) collective-permute-start(f32[72,512]{1,0:T(8,128)S(1)} %collective-permute-done.2.refs_1_), channel_id=1, source_target_pairs={{0,1},{1,0},{2,3},{3,2},{4,5},{5,4},{6,7},{7,6},{8,9},{9,8},{10,11... | collective-permute-start | bytes 442376 | tf_op jit(solution)/shard_map/ppermute | solution.py:613
  38.4 1.6 %collective-permute-start.7 = (f32[72,512]{1,0:T(8,128)S(1)}, f32[72,512]{1,0:T(8,128)S(1)}, u32[]{:S(2)}, u32[]{:S(2)}) collective-permute-start(f32[72,512]{1,0:T(8,128)S(1)} %collective-permute-done.3.refs_3_), channel_id=1, source_target_pairs={{0,1},{1,0},{2,3},{3,2},{4,5},{5,4},{6,7},{7,6},{8,9},{9,8},{10,11... | collective-permute-start | bytes 442376 | tf_op jit(solution)/shard_map/ppermute | solution.py:613
  41.0 5.4 %tree_points.1 = (bf16[144,4096]{1,0:T(8,128)(2,1)S(1)}, bf16[4096,256]{1,0:T(8,128)(2,1)}, bf16[4,1024,128]{2,1,0:T(8,128)(2,1)}, bf16[896,256]{1,0:T(8,128)(2,...) custom-call(s32[1,8]{1,0:T(1,128)} %count_ref.1, ...), custom_call_target="tpu_custom_call" | custom-call | tf_op jit(solution)/shard_map/tree_points/pallas_call | solution.py:632
  46.3 2.7 %tree_weights.1 = (bf16[32,4096]{1,0:T(8,128)(2,1)S(1)}, bf16[64,896]{1,0:T(8,128)(2,1)S(1)}, f32[128,128]{1,0:T(8,128)S(1)}) custom-call(bf16[4,1024,128]{2,1,0:T(8,128)(2,1)} %get-tuple-element.33.base_hbm, f32[3,256,128]{2,1,0:T(8,128)S(1)} %get-tuple-element.34.upper_tiles_ref, f32[128,128]{1,0:T(8,128)S(1)} %get-tuple-element.35.top_ref, ...), custom_call_target="tpu_custom_call" | custom-call | tf_op jit(solution)/shard_map/tree_weights/pallas_call | solution.py:661
  49.1 1.5 %collective-permute-start.8 = (f32[128,128]{1,0:T(8,128)S(1)}, f32[128,128]{1,0:T(8,128)S(1)}, u32[]{:S(2)}, u32[]{:S(2)}) collective-permute-start(f32[128,128]{1,0:T(8,128)S(1)} %get-tuple-element.37), channel_id=1, source_target_pairs={{0,8},{8,0},{1,9},{9,1},{2,10},{10,2},{3,11},{11,3},{4,12},{12,4},... | collective-permute-start | bytes 196616 | tf_op jit(solution)/shard_map/ppermute | solution.py:535
  50.6 10.9 %near.1.near_ref = f32[32,4096]{1,0:T(8,128)S(1)} custom-call(s32[3,67]{1,0:T(4,128)} %get-tuple-element.42.tiles, bf16[4096,256]{1,0:T(8,128)(2,1)} %get-tuple-element.43.a_hbm, bf16[144,4096]{1,0:T(8,128)(2,1)S(1)} %get-tuple-element.39.tree_ref, bf16[32,4096]{1,0:T(8,128)(2,1)S(1)} %get-tuple-element.44.w_ref), custom_call_target="tpu_custom_call" | custom-call | tf_op jit(solution)/shard_map/near/pallas_call | solution.py:682
  61.6 2.8 %far.1 = (f32[32,512]{1,0:T(8,128)S(1)}, f32[32,512]{1,0:T(8,128)S(1)}, f32[32,512]{1,0:T(8,128)S(1)}, f32[32,512]{1,0:T(8,128)S(1)}, f32[32,512]{1,0:T(8,128)S(...) custom-call(f32[1,128,128]{2,1,0:T(8,128)S(1)} %bitcast.5, ...), custom_call_target="tpu_custom_call" | custom-call | tf_op jit(solution)/shard_map/far/pallas_call | solution.py:699
  64.3 2.4 %collective-permute-start.9 = (f32[32,512]{1,0:T(8,128)S(1)}, f32[32,512]{1,0:T(8,128)S(1)}, u32[]{:S(2)}, u32[]{:S(2)}) collective-permute-start(f32[32,512]{1,0:T(8,128)S(1)} %get-tuple-element.45), channel_id=1, source_target_pairs={{0,4},{1,13},{2,6},{3,15},{4,0},{5,9},{6,2},{7,11},{8,12},{9,5},{1... | collective-permute-start | bytes 196616 | tf_op jit(solution)/shard_map/ppermute | solution.py:589
  68.0 3.2 %collective-permute-start.12 = (f32[32,512]{1,0:T(8,128)S(1)}, f32[32,512]{1,0:T(8,128)S(1)}, u32[]{:S(2)}, u32[]{:S(2)}) collective-permute-start(f32[32,512]{1,0:T(8,128)S(1)} %get-tuple-element.48), channel_id=1, source_target_pairs={{0,14},{1,7},{2,12},{3,5},{4,10},{5,3},{6,8},{7,1},{8,6},{9,15},{1... | collective-permute-start | bytes 196616 | tf_op jit(solution)/shard_map/ppermute | solution.py:589
  71.8 3.2 %collective-permute-start.14 = (f32[32,512]{1,0:T(8,128)S(1)}, f32[32,512]{1,0:T(8,128)S(1)}, u32[]{:S(2)}, u32[]{:S(2)}) collective-permute-start(f32[32,512]{1,0:T(8,128)S(1)} %get-tuple-element.50), channel_id=1, source_target_pairs={{0,2},{1,11},{2,0},{3,9},{4,6},{5,15},{6,4},{7,13},{8,10},{9,3},{1... | collective-permute-start | bytes 196616 | tf_op jit(solution)/shard_map/ppermute | solution.py:589
  75.0 1.9 %collective-permute-start.15 = (f32[32,512]{1,0:T(8,128)S(1)}, f32[32,512]{1,0:T(8,128)S(1)}, u32[]{:S(2)}, u32[]{:S(2)}) collective-permute-start(f32[32,512]{1,0:T(8,128)S(1)} %get-tuple-element.51), channel_id=1, source_target_pairs={{0,8},{1,1},{2,10},{3,3},{4,12},{5,5},{6,14},{7,7},{8,0},{9,9},{10... | collective-permute-start | bytes 196616 | tf_op jit(solution)/shard_map/ppermute | solution.py:589
  76.9 1.0 %collective-permute-done.11.refs_2_ = f32[32,512]{1,0:T(8,128)S(1)} collective-permute-done((f32[32,512]{1,0:T(8,128)S(1)}, f32[32,512]{1,0:T(8,128)S(1)}, u32[]{:S(2)}, u32[]{:S(2)}) %collective-permute-start.11) | collective-permute-done | bytes 65568 | tf_op jit(solution)/shard_map/ppermute | solution.py:589
  77.9 2.7 %collective-permute-start.16 = (f32[32,512]{1,0:T(8,128)S(1)}, f32[32,512]{1,0:T(8,128)S(1)}, u32[]{:S(2)}, u32[]{:S(2)}) collective-permute-start(f32[32,512]{1,0:T(8,128)S(1)} %get-tuple-element.52), channel_id=1, source_target_pairs={{0,10},{1,3},{2,8},{3,1},{4,14},{5,7},{6,12},{7,5},{8,2},{9,11},{1... | collective-permute-start | bytes 196616 | tf_op jit(solution)/shard_map/ppermute | solution.py:589
  81.1 1.9 %collective-permute-done.16.refs_7_ = f32[32,512]{1,0:T(8,128)S(1)} collective-permute-done((f32[32,512]{1,0:T(8,128)S(1)}, f32[32,512]{1,0:T(8,128)S(1)}, u32[]{:S(2)}, u32[]{:S(2)}) %collective-permute-start.16) | collective-permute-done | bytes 65568 | tf_op jit(solution)/shard_map/ppermute | solution.py:589
  83.1 1.9 %to_input_order.1 = f32[1024,128]{1,0:T(8,128)} custom-call(f32[8,128]{1,0:T(8,128)S(1)} %copy-done.1, f32[32,512]{1,0:T(8,128)S(1)} %collective-permute-done.9.refs_0_, f32[32,512]{1,0:T(8,128)S(1)} %collective-permute-done.10.refs_1_, f32[32,512]{1,0:T(8,128)S(1)} %collective-permute-done.11.refs_2_, f32[32,512]{1,0:T(8,128)S(1)} %collective-permute-done.12.refs_3_, ...), custom_call_target="tpu_custom_call" | custom-call | tf_op jit(solution)/shard_map/to_input_order/pallas_call | solution.py:726
  (23 shorter events, 3.5 us)
Async XLA Ops:
  2.7 1.6 %collective-permute-start = (f32[72,512]{1,0:T(8,128)}, f32[72,512]{1,0:T(8,128)S(1)}, u32[]{:S(2)}, u32[]{:S(2)}) collective-permute-start(f32[72,512]{1,0:T(8,128)} %get-tuple-element.29), channel_id=1, source_target_pairs={{0,0},{1,9},{2,2},{3,11},{4,4},{5,13},{6,6},{7,15},{8,8},{9,1},{10... | collective-permute-start | bytes 442376 | tf_op jit(solution)/shard_map/ppermute | solution.py:589
  4.3 8.7 %collective-permute-start.1 = (f32[72,512]{1,0:T(8,128)S(1)}, f32[72,512]{1,0:T(8,128)S(1)}, u32[]{:S(2)}, u32[]{:S(2)}) collective-permute-start(f32[72,512]{1,0:T(8,128)S(1)} %collective-permute-done.refs_0_), channel_id=1, source_target_pairs={{0,4},{2,6},{4,0},{6,2},{1,5},{3,7},{5,1},{7,3},{8,12},{10,14},{12... | collective-permute-start | bytes 442376 | tf_op jit(solution)/shard_map/ppermute | solution.py:610
  15.6 30.7 %all-to-all-start = ((f32[8,32,512]{2,1,0:T(8,128)}), f32[8,32,512]{2,1,0:T(8,128)S(1)}, u32[]{:S(2)}, u32[]{:S(2)}) async-start(f32[8,32,512]{2,1,0:T(8,128)} %bitcast.6), calls=%async_computation | async-start | bytes 1048576 | tf_op jit(solution)/shard_map/all_to_all | solution.py:616
  21.6 10.4 %collective-permute-start.2 = (f32[72,512]{1,0:T(8,128)S(1)}, f32[72,512]{1,0:T(8,128)S(1)}, u32[]{:S(2)}, u32[]{:S(2)}) collective-permute-start(f32[72,512]{1,0:T(8,128)S(1)} %collective-permute-done.refs_0_), channel_id=1, source_target_pairs={{0,2},{2,0},{4,6},{6,4},{1,3},{3,1},{5,7},{7,5},{8,10},{10,8},{12,... | collective-permute-start | bytes 442376 | tf_op jit(solution)/shard_map/ppermute | solution.py:610
  23.6 14.7 %collective-permute-start.3 = (f32[72,512]{1,0:T(8,128)S(1)}, f32[72,512]{1,0:T(8,128)S(1)}, u32[]{:S(2)}, u32[]{:S(2)}) collective-permute-start(f32[72,512]{1,0:T(8,128)S(1)} %collective-permute-done.1.refs_2_), channel_id=1, source_target_pairs={{0,2},{2,0},{4,6},{6,4},{1,3},{3,1},{5,7},{7,5},{8,10},{10,8},{12,... | collective-permute-start | bytes 442376 | tf_op jit(solution)/shard_map/ppermute | solution.py:610
  23.7 16.3 %collective-permute-start.4 = (f32[72,512]{1,0:T(8,128)S(1)}, f32[72,512]{1,0:T(8,128)S(1)}, u32[]{:S(2)}, u32[]{:S(2)}) collective-permute-start(f32[72,512]{1,0:T(8,128)S(1)} %collective-permute-done.refs_0_), channel_id=1, source_target_pairs={{0,1},{1,0},{2,3},{3,2},{4,5},{5,4},{6,7},{7,6},{8,9},{9,8},{10,11... | collective-permute-start | bytes 442376 | tf_op jit(solution)/shard_map/ppermute | solution.py:613
  26.4 13.6 %collective-permute-start.6 = (f32[72,512]{1,0:T(8,128)S(1)}, f32[72,512]{1,0:T(8,128)S(1)}, u32[]{:S(2)}, u32[]{:S(2)}) collective-permute-start(f32[72,512]{1,0:T(8,128)S(1)} %collective-permute-done.1.refs_2_), channel_id=1, source_target_pairs={{0,1},{1,0},{2,3},{3,2},{4,5},{5,4},{6,7},{7,6},{8,9},{9,8},{10,11... | collective-permute-start | bytes 442376 | tf_op jit(solution)/shard_map/ppermute | solution.py:613
  32.0 8.0 %collective-permute-start.5 = (f32[72,512]{1,0:T(8,128)S(1)}, f32[72,512]{1,0:T(8,128)S(1)}, u32[]{:S(2)}, u32[]{:S(2)}) collective-permute-start(f32[72,512]{1,0:T(8,128)S(1)} %collective-permute-done.2.refs_1_), channel_id=1, source_target_pairs={{0,1},{1,0},{2,3},{3,2},{4,5},{5,4},{6,7},{7,6},{8,9},{9,8},{10,11... | collective-permute-start | bytes 442376 | tf_op jit(solution)/shard_map/ppermute | solution.py:613
  38.4 2.6 %collective-permute-start.7 = (f32[72,512]{1,0:T(8,128)S(1)}, f32[72,512]{1,0:T(8,128)S(1)}, u32[]{:S(2)}, u32[]{:S(2)}) collective-permute-start(f32[72,512]{1,0:T(8,128)S(1)} %collective-permute-done.3.refs_3_), channel_id=1, source_target_pairs={{0,1},{1,0},{2,3},{3,2},{4,5},{5,4},{6,7},{7,6},{8,9},{9,8},{10,11... | collective-permute-start | bytes 442376 | tf_op jit(solution)/shard_map/ppermute | solution.py:613
  49.1 12.5 %collective-permute-start.8 = (f32[128,128]{1,0:T(8,128)S(1)}, f32[128,128]{1,0:T(8,128)S(1)}, u32[]{:S(2)}, u32[]{:S(2)}) collective-permute-start(f32[128,128]{1,0:T(8,128)S(1)} %get-tuple-element.37), channel_id=1, source_target_pairs={{0,8},{8,0},{1,9},{9,1},{2,10},{10,2},{3,11},{11,3},{4,12},{12,4},... | collective-permute-start | bytes 196616 | tf_op jit(solution)/shard_map/ppermute | solution.py:535
  61.5 21.5 %copy-start = (f32[1024,128]{1,0:T(8,128)S(1)}, f32[1024,128]{1,0:T(8,128)}, u32[]{:S(2)}) copy-start(f32[1024,128]{1,0:T(8,128)} %refs_8_.1) | copy-start | bytes 1572868
  61.5 21.5 %copy-start.1 = (f32[8,128]{1,0:T(8,128)S(1)}, f32[8,128]{1,0:T(8,128)}, u32[]{:S(2)}) copy-start(f32[8,128]{1,0:T(8,128)} %get-tuple-element.31.pos_ref) | copy-start | bytes 12292
  64.3 7.5 %collective-permute-start.9 = (f32[32,512]{1,0:T(8,128)S(1)}, f32[32,512]{1,0:T(8,128)S(1)}, u32[]{:S(2)}, u32[]{:S(2)}) collective-permute-start(f32[32,512]{1,0:T(8,128)S(1)} %get-tuple-element.45), channel_id=1, source_target_pairs={{0,4},{1,13},{2,6},{3,15},{4,0},{5,9},{6,2},{7,11},{8,12},{9,5},{1... | collective-permute-start | bytes 196616 | tf_op jit(solution)/shard_map/ppermute | solution.py:589
  66.8 8.2 %collective-permute-start.10 = (f32[32,512]{1,0:T(8,128)S(1)}, f32[32,512]{1,0:T(8,128)S(1)}, u32[]{:S(2)}, u32[]{:S(2)}) collective-permute-start(f32[32,512]{1,0:T(8,128)S(1)} %get-tuple-element.46), channel_id=1, source_target_pairs={{0,6},{1,15},{2,4},{3,13},{4,2},{5,11},{6,0},{7,9},{8,14},{9,7},{1... | collective-permute-start | bytes 196616 | tf_op jit(solution)/shard_map/ppermute | solution.py:589
  67.4 10.5 %collective-permute-start.11 = (f32[32,512]{1,0:T(8,128)S(1)}, f32[32,512]{1,0:T(8,128)S(1)}, u32[]{:S(2)}, u32[]{:S(2)}) collective-permute-start(f32[32,512]{1,0:T(8,128)S(1)} %get-tuple-element.47), channel_id=1, source_target_pairs={{0,12},{1,5},{2,14},{3,7},{4,8},{5,1},{6,10},{7,3},{8,4},{9,13},{1... | collective-permute-start | bytes 196616 | tf_op jit(solution)/shard_map/ppermute | solution.py:589
  68.0 12.6 %collective-permute-start.12 = (f32[32,512]{1,0:T(8,128)S(1)}, f32[32,512]{1,0:T(8,128)S(1)}, u32[]{:S(2)}, u32[]{:S(2)}) collective-permute-start(f32[32,512]{1,0:T(8,128)S(1)} %get-tuple-element.48), channel_id=1, source_target_pairs={{0,14},{1,7},{2,12},{3,5},{4,10},{5,3},{6,8},{7,1},{8,6},{9,15},{1... | collective-permute-start | bytes 196616 | tf_op jit(solution)/shard_map/ppermute | solution.py:589
  71.2 9.4 %collective-permute-start.13 = (f32[32,512]{1,0:T(8,128)S(1)}, f32[32,512]{1,0:T(8,128)S(1)}, u32[]{:S(2)}, u32[]{:S(2)}) collective-permute-start(f32[32,512]{1,0:T(8,128)S(1)} %get-tuple-element.49), channel_id=1, source_target_pairs={{0,0},{1,9},{2,2},{3,11},{4,4},{5,13},{6,6},{7,15},{8,8},{9,1},{10... | collective-permute-start | bytes 196616 | tf_op jit(solution)/shard_map/ppermute | solution.py:589
  71.8 8.8 %collective-permute-start.14 = (f32[32,512]{1,0:T(8,128)S(1)}, f32[32,512]{1,0:T(8,128)S(1)}, u32[]{:S(2)}, u32[]{:S(2)}) collective-permute-start(f32[32,512]{1,0:T(8,128)S(1)} %get-tuple-element.50), channel_id=1, source_target_pairs={{0,2},{1,11},{2,0},{3,9},{4,6},{5,15},{6,4},{7,13},{8,10},{9,3},{1... | collective-permute-start | bytes 196616 | tf_op jit(solution)/shard_map/ppermute | solution.py:589
  75.0 6.1 %collective-permute-start.15 = (f32[32,512]{1,0:T(8,128)S(1)}, f32[32,512]{1,0:T(8,128)S(1)}, u32[]{:S(2)}, u32[]{:S(2)}) collective-permute-start(f32[32,512]{1,0:T(8,128)S(1)} %get-tuple-element.51), channel_id=1, source_target_pairs={{0,8},{1,1},{2,10},{3,3},{4,12},{5,5},{6,14},{7,7},{8,0},{9,9},{10... | collective-permute-start | bytes 196616 | tf_op jit(solution)/shard_map/ppermute | solution.py:589
  77.9 5.2 %collective-permute-start.16 = (f32[32,512]{1,0:T(8,128)S(1)}, f32[32,512]{1,0:T(8,128)S(1)}, u32[]{:S(2)}, u32[]{:S(2)}) collective-permute-start(f32[32,512]{1,0:T(8,128)S(1)} %get-tuple-element.52), channel_id=1, source_target_pairs={{0,10},{1,3},{2,8},{3,1},{4,14},{5,7},{6,12},{7,5},{8,2},{9,11},{1... | collective-permute-start | bytes 196616 | tf_op jit(solution)/shard_map/ppermute | solution.py:589

commit v12 on v11

--- a/solution.py
+++ b/solution.py
@@ -609,10 +609,11 @@
             for step in sorted(place):
                 place[step | stride] = lax.ppermute(place[step], "sub", [(i, i ^ stride) for i in range(blocks)])
             stride //= 2
-        place[blocks // 2], pos = lax.optimization_barrier((place[blocks // 2], pos))
+        light = sorted_light()
+        place, light = lax.optimization_barrier((place, light))
         theirs = {step: lax.ppermute(one, "rep", [(0, 1), (1, 0)]) for step, one in place.items()}
         place = [place[step] for step in range(blocks)] + [theirs[step] for step in range(blocks)]
-        light = sorted_light().reshape(devices, width, part)
+        light = light.reshape(devices, width, part)
         light = lax.all_to_all(light, ("leaf", "sub"), split_axis=0, concat_axis=0, tiled=True)
         small = []
     else:

time: 85.6 us -> 77.6 us (0.907)
  starting transfers between devices: 41.1 us -> 29.6 us
  waiting for transfers between devices: 14.9 us -> 18.3 us
    ppermute x4, starting transfers between devices: 10.6 us -> 2.54 us  [body(): lax.ppermute(one, 'rep', [(0, 1), (1, 0)])]
    all_to_all x1, waiting for transfers between devices: 0.01 us -> 6.6 us  [body(): lax.all_to_all(light, ('leaf', 'sub'), split_axis=0, concat_axis=0, tiled...]
    ppermute x3, waiting for transfers between devices: 10.3 us -> 5.51 us  [body(): lax.ppermute(place[step], 'sub', [(i, i ^ stride) for i in range(blocks)])]
    ppermute x9, starting transfers between devices: 16.7 us -> 14.5 us  [swap(): return lax.ppermute(value, axes, pairs)]
    ppermute x9, waiting for transfers between devices: 3.52 us -> 4.85 us  [swap(): return lax.ppermute(value, axes, pairs)]
    ppermute x1, starting transfers between devices: 1.54 us -> 0.63 us  [upper_levels(): other = lax.ppermute(own, 'leaf', [(i, i ^ stride) for i in range(trees)])]
  transfers between devices with their start and end apart: 18 -> 18, of which waited for: 6 -> 10; matrix products, arithmetic and copies ran while one was open for 0% -> 0% of each run, Pallas kernels for 19% -> 24%
where the time goes in v12:
time: 77.6 us; the launch traced here: 76.9 us
  starting transfers between devices  29.6 us (38%)
  Pallas kernels  28.9 us (37%)
  waiting for transfers between devices  18.3 us (24%)
    ppermute x9, starting transfers between devices, swap(): return lax.ppermute(value, axes, pairs)  14.5 us
    pallas_call x1, Pallas kernels, body(): pl.pallas_call(near_kernel, out_shape=vm((width, total), f32), in_specs=[...  10.9 us
    all_to_all x1, waiting for transfers between devices, body(): lax.all_to_all(light, ('leaf', 'sub'), split_axis=0, concat_axis=0, tiled...  6.6 us
    ppermute x3, starting transfers between devices, body(): lax.ppermute(place[step], 'sub', [(i, i ^ stride) for i in range(blocks)])  6.51 us
    ppermute x3, waiting for transfers between devices, body(): lax.ppermute(place[step], 'sub', [(i, i ^ stride) for i in range(blocks)])  5.51 us
    all_to_all x1, starting transfers between devices, body(): lax.all_to_all(light, ('leaf', 'sub'), split_axis=0, concat_axis=0, tiled...  5.45 us
    pallas_call x1, Pallas kernels, body(): pl.pallas_call(functools.partial(points_kernel, layout, trees), out_shape...  5.36 us
    ppermute x9, waiting for transfers between devices, swap(): return lax.ppermute(value, axes, pairs)  4.85 us
  transfers between devices with their start and end apart: 18, of which 10 were waited for; matrix products, arithmetic and copies ran while one was open for 0% of the time, Pallas kernels for 24%

profile of v12, /device:TPU:0, one launch (start us, length us, event | category | flops | bytes accessed | tf_op | source)
XLA Modules:
  0.0 76.9 jit_solution(16338486224568832782)
XLA Ops:
  0.0 2.7 %sort_points.1 = (f32[72,512]{1,0:T(8,128)}, f32[8,128]{1,0:T(8,128)}) custom-call(s32[8,128]{1,0:T(8,128)} %bitcast.8, f32[64,1024]{1,0:T(8,128)} %bitcast.7, s32[1,128]{1,0:T(1,128)} %base_ref.1, s32[2,3]{1,0:T(2,128)} %flag_ref.1), custom_call_target="tpu_custom_call" | custom-call | tf_op jit(solution)/shard_map/sort_points/pallas_call | solution.py:571
  2.7 1.6 %collective-permute-start = (f32[72,512]{1,0:T(8,128)}, f32[72,512]{1,0:T(8,128)S(1)}, u32[]{:S(2)}, u32[]{:S(2)}) collective-permute-start(f32[72,512]{1,0:T(8,128)} %get-tuple-element.33), channel_id=1, source_target_pairs={{0,0},{1,9},{2,2},{3,11},{4,4},{5,13},{6,6},{7,15},{8,8},{9,1},{10... | collective-permute-start | bytes 442376 | tf_op jit(solution)/shard_map/ppermute | solution.py:589
  4.3 4.0 %collective-permute-start.2 = (f32[72,512]{1,0:T(8,128)S(1)}, f32[72,512]{1,0:T(8,128)S(1)}, u32[]{:S(2)}, u32[]{:S(2)}) collective-permute-start(f32[72,512]{1,0:T(8,128)S(1)} %collective-permute-done.refs_0_), channel_id=1, source_target_pairs={{0,4},{2,6},{4,0},{6,2},{1,5},{3,7},{5,1},{7,3},{8,12},{10,14},{12... | collective-permute-start | bytes 442376 | tf_op jit(solution)/shard_map/ppermute | solution.py:610
  8.3 1.6 %collective-permute-start.1 = (f32[72,512]{1,0:T(8,128)S(1)}, f32[72,512]{1,0:T(8,128)S(1)}, u32[]{:S(2)}, u32[]{:S(2)}) collective-permute-start(f32[72,512]{1,0:T(8,128)S(1)} %collective-permute-done.refs_0_), channel_id=1, source_target_pairs={{0,2},{2,0},{4,6},{6,4},{1,3},{3,1},{5,7},{7,5},{8,10},{10,8},{12,... | collective-permute-start | bytes 442376 | tf_op jit(solution)/shard_map/ppermute | solution.py:610
  9.9 3.2 %collective-permute-done.2.refs_2_ = f32[72,512]{1,0:T(8,128)S(1)} collective-permute-done((f32[72,512]{1,0:T(8,128)S(1)}, f32[72,512]{1,0:T(8,128)S(1)}, u32[]{:S(2)}, u32[]{:S(2)}) %collective-permute-start.2) | collective-permute-done | bytes 147488 | tf_op jit(solution)/shard_map/ppermute | solution.py:610
  13.2 0.9 %collective-permute-start.3 = (f32[72,512]{1,0:T(8,128)S(1)}, f32[72,512]{1,0:T(8,128)S(1)}, u32[]{:S(2)}, u32[]{:S(2)}) collective-permute-start(f32[72,512]{1,0:T(8,128)S(1)} %collective-permute-done.2.refs_2_), channel_id=1, source_target_pairs={{0,2},{2,0},{4,6},{6,4},{1,3},{3,1},{5,7},{7,5},{8,10},{10,8},{12,... | collective-permute-start | bytes 442376 | tf_op jit(solution)/shard_map/ppermute | solution.py:610
  14.1 2.6 %sort_weights.1 = f32[2,128,512]{2,1,0:T(8,128)} custom-call(f32[8,128]{1,0:T(8,128)} %get-tuple-element.32.pos_ref, f32[1024,128]{1,0:T(8,128)} %refs_8_.1), custom_call_target="tpu_custom_call" | custom-call | tf_op jit(solution)/shard_map/sort_weights/pallas_call | solution.py:595
  16.6 2.3 %collective-permute-done.3.refs_3_ = f32[72,512]{1,0:T(8,128)S(1)} collective-permute-done((f32[72,512]{1,0:T(8,128)S(1)}, f32[72,512]{1,0:T(8,128)S(1)}, u32[]{:S(2)}, u32[]{:S(2)}) %collective-permute-start.3) | collective-permute-done | bytes 147488 | tf_op jit(solution)/shard_map/ppermute | solution.py:610
  18.9 5.5 %all-to-all-start = ((f32[8,32,512]{2,1,0:T(8,128)}), f32[8,32,512]{2,1,0:T(8,128)S(1)}, u32[]{:S(2)}, u32[]{:S(2)}) async-start(f32[8,32,512]{2,1,0:T(8,128)} %bitcast.6), calls=%async_computation | async-start | bytes 1048576 | tf_op jit(solution)/shard_map/all_to_all | solution.py:617
  24.3 2.0 %collective-permute-start.4 = (f32[72,512]{1,0:T(8,128)S(1)}, f32[72,512]{1,0:T(8,128)S(1)}, u32[]{:S(2)}, u32[]{:S(2)}) collective-permute-start(f32[72,512]{1,0:T(8,128)S(1)} %collective-permute-done.refs_0_), channel_id=1, source_target_pairs={{0,1},{1,0},{2,3},{3,2},{4,5},{5,4},{6,7},{7,6},{8,9},{9,8},{10,11... | collective-permute-start | bytes 442376 | tf_op jit(solution)/shard_map/ppermute | solution.py:614
  28.2 5.4 %tree_points.1 = (bf16[144,4096]{1,0:T(8,128)(2,1)S(1)}, bf16[4096,256]{1,0:T(8,128)(2,1)}, bf16[4,1024,128]{2,1,0:T(8,128)(2,1)}, bf16[896,256]{1,0:T(8,128)(2,...) custom-call(s32[1,8]{1,0:T(1,128)} %count_ref.1, ...), custom_call_target="tpu_custom_call" | custom-call | tf_op jit(solution)/shard_map/tree_points/pallas_call | solution.py:633
  33.6 6.6 %all-to-all-done.light_ref = f32[8,32,512]{2,1,0:T(8,128)S(1)} async-done(((f32[8,32,512]{2,1,0:T(8,128)}), f32[8,32,512]{2,1,0:T(8,128)S(1)}, u32[]{:S(2)}, u32[]{:S(2)}) %all-to-all-start) | async-done | bytes 524320 | tf_op jit(solution)/shard_map/all_to_all | solution.py:617
  40.1 2.7 %tree_weights.1 = (bf16[32,4096]{1,0:T(8,128)(2,1)S(1)}, bf16[64,896]{1,0:T(8,128)(2,1)S(1)}, f32[128,128]{1,0:T(8,128)S(1)}) custom-call(bf16[4,1024,128]{2,1,0:T(8,128)(2,1)} %get-tuple-element.38.base_hbm, f32[3,256,128]{2,1,0:T(8,128)S(1)} %get-tuple-element.39.upper_tiles_ref, f32[128,128]{1,0:T(8,128)S(1)} %get-tuple-element.40.top_ref, ...), custom_call_target="tpu_custom_call" | custom-call | tf_op jit(solution)/shard_map/tree_weights/pallas_call | solution.py:662
  43.5 10.9 %near.1.near_ref = f32[32,4096]{1,0:T(8,128)S(1)} custom-call(s32[3,67]{1,0:T(4,128)} %get-tuple-element.48.tiles, bf16[4096,256]{1,0:T(8,128)(2,1)} %get-tuple-element.49.a_hbm, bf16[144,4096]{1,0:T(8,128)(2,1)S(1)} %get-tuple-element.45.tree_ref, bf16[32,4096]{1,0:T(8,128)(2,1)S(1)} %get-tuple-element.50.w_ref), custom_call_target="tpu_custom_call" | custom-call | tf_op jit(solution)/shard_map/near/pallas_call | solution.py:683
  54.4 2.8 %far.1 = (f32[32,512]{1,0:T(8,128)S(1)}, f32[32,512]{1,0:T(8,128)S(1)}, f32[32,512]{1,0:T(8,128)S(1)}, f32[32,512]{1,0:T(8,128)S(1)}, f32[32,512]{1,0:T(8,128)S(...) custom-call(f32[1,128,128]{2,1,0:T(8,128)S(1)} %bitcast.5, ...), custom_call_target="tpu_custom_call" | custom-call | tf_op jit(solution)/shard_map/far/pallas_call | solution.py:700
  57.2 1.6 %collective-permute-start.9 = (f32[32,512]{1,0:T(8,128)S(1)}, f32[32,512]{1,0:T(8,128)S(1)}, u32[]{:S(2)}, u32[]{:S(2)}) collective-permute-start(f32[32,512]{1,0:T(8,128)S(1)} %get-tuple-element.51), channel_id=1, source_target_pairs={{0,4},{1,13},{2,6},{3,15},{4,0},{5,9},{6,2},{7,11},{8,12},{9,5},{1... | collective-permute-start | bytes 196616 | tf_op jit(solution)/shard_map/ppermute | solution.py:589
  59.9 4.1 %collective-permute-start.12 = (f32[32,512]{1,0:T(8,128)S(1)}, f32[32,512]{1,0:T(8,128)S(1)}, u32[]{:S(2)}, u32[]{:S(2)}) collective-permute-start(f32[32,512]{1,0:T(8,128)S(1)} %get-tuple-element.54), channel_id=1, source_target_pairs={{0,14},{1,7},{2,12},{3,5},{4,10},{5,3},{6,8},{7,1},{8,6},{9,15},{1... | collective-permute-start | bytes 196616 | tf_op jit(solution)/shard_map/ppermute | solution.py:589
  64.0 0.7 collective-permute-start.13
  64.8 0.8 %collective-permute-done.10.refs_1_ = f32[32,512]{1,0:T(8,128)S(1)} collective-permute-done((f32[32,512]{1,0:T(8,128)S(1)}, f32[32,512]{1,0:T(8,128)S(1)}, u32[]{:S(2)}, u32[]{:S(2)}) %collective-permute-start.10) | collective-permute-done | bytes 65568 | tf_op jit(solution)/shard_map/ppermute | solution.py:589
  65.6 1.9 %collective-permute-start.15 = (f32[32,512]{1,0:T(8,128)S(1)}, f32[32,512]{1,0:T(8,128)S(1)}, u32[]{:S(2)}, u32[]{:S(2)}) collective-permute-start(f32[32,512]{1,0:T(8,128)S(1)} %get-tuple-element.57), channel_id=1, source_target_pairs={{0,8},{1,1},{2,10},{3,3},{4,12},{5,5},{6,14},{7,7},{8,0},{9,9},{10... | collective-permute-start | bytes 196616 | tf_op jit(solution)/shard_map/ppermute | solution.py:589
  67.5 1.8 %collective-permute-done.11.refs_2_ = f32[32,512]{1,0:T(8,128)S(1)} collective-permute-done((f32[32,512]{1,0:T(8,128)S(1)}, f32[32,512]{1,0:T(8,128)S(1)}, u32[]{:S(2)}, u32[]{:S(2)}) %collective-permute-start.11) | collective-permute-done | bytes 65568 | tf_op jit(solution)/shard_map/ppermute | solution.py:589
  69.3 3.5 %collective-permute-start.16 = (f32[32,512]{1,0:T(8,128)S(1)}, f32[32,512]{1,0:T(8,128)S(1)}, u32[]{:S(2)}, u32[]{:S(2)}) collective-permute-start(f32[32,512]{1,0:T(8,128)S(1)} %get-tuple-element.58), channel_id=1, source_target_pairs={{0,10},{1,3},{2,8},{3,1},{4,14},{5,7},{6,12},{7,5},{8,2},{9,11},{1... | collective-permute-start | bytes 196616 | tf_op jit(solution)/shard_map/ppermute | solution.py:589
  72.8 2.2 %collective-permute-done.16.refs_7_ = f32[32,512]{1,0:T(8,128)S(1)} collective-permute-done((f32[32,512]{1,0:T(8,128)S(1)}, f32[32,512]{1,0:T(8,128)S(1)}, u32[]{:S(2)}, u32[]{:S(2)}) %collective-permute-start.16) | collective-permute-done | bytes 65568 | tf_op jit(solution)/shard_map/ppermute | solution.py:589
  75.0 1.9 %to_input_order.1 = f32[1024,128]{1,0:T(8,128)} custom-call(f32[8,128]{1,0:T(8,128)S(1)} %copy-done.1, f32[32,512]{1,0:T(8,128)S(1)} %collective-permute-done.9.refs_0_, f32[32,512]{1,0:T(8,128)S(1)} %collective-permute-done.10.refs_1_, f32[32,512]{1,0:T(8,128)S(1)} %collective-permute-done.11.refs_2_, f32[32,512]{1,0:T(8,128)S(1)} %collective-permute-done.12.refs_3_, ...), custom_call_target="tpu_custom_call" | custom-call | tf_op jit(solution)/shard_map/to_input_order/pallas_call | solution.py:727
  (23 shorter events, 3.8 us)
Async XLA Ops:
  2.7 1.6 %collective-permute-start = (f32[72,512]{1,0:T(8,128)}, f32[72,512]{1,0:T(8,128)S(1)}, u32[]{:S(2)}, u32[]{:S(2)}) collective-permute-start(f32[72,512]{1,0:T(8,128)} %get-tuple-element.33), channel_id=1, source_target_pairs={{0,0},{1,9},{2,2},{3,11},{4,4},{5,13},{6,6},{7,15},{8,8},{9,1},{10... | collective-permute-start | bytes 442376 | tf_op jit(solution)/shard_map/ppermute | solution.py:589
  4.3 8.8 %collective-permute-start.2 = (f32[72,512]{1,0:T(8,128)S(1)}, f32[72,512]{1,0:T(8,128)S(1)}, u32[]{:S(2)}, u32[]{:S(2)}) collective-permute-start(f32[72,512]{1,0:T(8,128)S(1)} %collective-permute-done.refs_0_), channel_id=1, source_target_pairs={{0,4},{2,6},{4,0},{6,2},{1,5},{3,7},{5,1},{7,3},{8,12},{10,14},{12... | collective-permute-start | bytes 442376 | tf_op jit(solution)/shard_map/ppermute | solution.py:610
  8.3 8.3 %collective-permute-start.1 = (f32[72,512]{1,0:T(8,128)S(1)}, f32[72,512]{1,0:T(8,128)S(1)}, u32[]{:S(2)}, u32[]{:S(2)}) collective-permute-start(f32[72,512]{1,0:T(8,128)S(1)} %collective-permute-done.refs_0_), channel_id=1, source_target_pairs={{0,2},{2,0},{4,6},{6,4},{1,3},{3,1},{5,7},{7,5},{8,10},{10,8},{12,... | collective-permute-start | bytes 442376 | tf_op jit(solution)/shard_map/ppermute | solution.py:610
  13.2 5.7 %collective-permute-start.3 = (f32[72,512]{1,0:T(8,128)S(1)}, f32[72,512]{1,0:T(8,128)S(1)}, u32[]{:S(2)}, u32[]{:S(2)}) collective-permute-start(f32[72,512]{1,0:T(8,128)S(1)} %collective-permute-done.2.refs_2_), channel_id=1, source_target_pairs={{0,2},{2,0},{4,6},{6,4},{1,3},{3,1},{5,7},{7,5},{8,10},{10,8},{12,... | collective-permute-start | bytes 442376 | tf_op jit(solution)/shard_map/ppermute | solution.py:610
  18.9 21.3 %all-to-all-start = ((f32[8,32,512]{2,1,0:T(8,128)}), f32[8,32,512]{2,1,0:T(8,128)S(1)}, u32[]{:S(2)}, u32[]{:S(2)}) async-start(f32[8,32,512]{2,1,0:T(8,128)} %bitcast.6), calls=%async_computation | async-start | bytes 1048576 | tf_op jit(solution)/shard_map/all_to_all | solution.py:617
  24.3 3.0 %collective-permute-start.4 = (f32[72,512]{1,0:T(8,128)S(1)}, f32[72,512]{1,0:T(8,128)S(1)}, u32[]{:S(2)}, u32[]{:S(2)}) collective-permute-start(f32[72,512]{1,0:T(8,128)S(1)} %collective-permute-done.refs_0_), channel_id=1, source_target_pairs={{0,1},{1,0},{2,3},{3,2},{4,5},{5,4},{6,7},{7,6},{8,9},{9,8},{10,11... | collective-permute-start | bytes 442376 | tf_op jit(solution)/shard_map/ppermute | solution.py:614
  26.3 1.4 %collective-permute-start.5 = (f32[72,512]{1,0:T(8,128)S(1)}, f32[72,512]{1,0:T(8,128)S(1)}, u32[]{:S(2)}, u32[]{:S(2)}) collective-permute-start(f32[72,512]{1,0:T(8,128)S(1)} %collective-permute-done.1.refs_1_), channel_id=1, source_target_pairs={{0,1},{1,0},{2,3},{3,2},{4,5},{5,4},{6,7},{7,6},{8,9},{9,8},{10,11... | collective-permute-start | bytes 442376 | tf_op jit(solution)/shard_map/ppermute | solution.py:614
  26.4 1.5 %collective-permute-start.6 = (f32[72,512]{1,0:T(8,128)S(1)}, f32[72,512]{1,0:T(8,128)S(1)}, u32[]{:S(2)}, u32[]{:S(2)}) collective-permute-start(f32[72,512]{1,0:T(8,128)S(1)} %collective-permute-done.2.refs_2_), channel_id=1, source_target_pairs={{0,1},{1,0},{2,3},{3,2},{4,5},{5,4},{6,7},{7,6},{8,9},{9,8},{10,11... | collective-permute-start | bytes 442376 | tf_op jit(solution)/shard_map/ppermute | solution.py:614
  26.8 1.4 %collective-permute-start.7 = (f32[72,512]{1,0:T(8,128)S(1)}, f32[72,512]{1,0:T(8,128)S(1)}, u32[]{:S(2)}, u32[]{:S(2)}) collective-permute-start(f32[72,512]{1,0:T(8,128)S(1)} %collective-permute-done.3.refs_3_), channel_id=1, source_target_pairs={{0,1},{1,0},{2,3},{3,2},{4,5},{5,4},{6,7},{7,6},{8,9},{9,8},{10,11... | collective-permute-start | bytes 442376 | tf_op jit(solution)/shard_map/ppermute | solution.py:614
  42.9 11.5 %collective-permute-start.8 = (f32[128,128]{1,0:T(8,128)S(1)}, f32[128,128]{1,0:T(8,128)S(1)}, u32[]{:S(2)}, u32[]{:S(2)}) collective-permute-start(f32[128,128]{1,0:T(8,128)S(1)} %get-tuple-element.43), channel_id=1, source_target_pairs={{0,8},{8,0},{1,9},{9,1},{2,10},{10,2},{3,11},{11,3},{4,12},{12,4},... | collective-permute-start | bytes 196616 | tf_op jit(solution)/shard_map/ppermute | solution.py:535
  54.4 20.6 %copy-start = (f32[1024,128]{1,0:T(8,128)S(1)}, f32[1024,128]{1,0:T(8,128)}, u32[]{:S(2)}) copy-start(f32[1024,128]{1,0:T(8,128)} %refs_8_.1) | copy-start | bytes 1572868
  54.4 20.6 %copy-start.1 = (f32[8,128]{1,0:T(8,128)S(1)}, f32[8,128]{1,0:T(8,128)}, u32[]{:S(2)}) copy-start(f32[8,128]{1,0:T(8,128)} %get-tuple-element.32.pos_ref) | copy-start | bytes 12292
  57.2 7.5 %collective-permute-start.9 = (f32[32,512]{1,0:T(8,128)S(1)}, f32[32,512]{1,0:T(8,128)S(1)}, u32[]{:S(2)}, u32[]{:S(2)}) collective-permute-start(f32[32,512]{1,0:T(8,128)S(1)} %get-tuple-element.51), channel_id=1, source_target_pairs={{0,4},{1,13},{2,6},{3,15},{4,0},{5,9},{6,2},{7,11},{8,12},{9,5},{1... | collective-permute-start | bytes 196616 | tf_op jit(solution)/shard_map/ppermute | solution.py:589
  58.8 6.8 %collective-permute-start.10 = (f32[32,512]{1,0:T(8,128)S(1)}, f32[32,512]{1,0:T(8,128)S(1)}, u32[]{:S(2)}, u32[]{:S(2)}) collective-permute-start(f32[32,512]{1,0:T(8,128)S(1)} %get-tuple-element.52), channel_id=1, source_target_pairs={{0,6},{1,15},{2,4},{3,13},{4,2},{5,11},{6,0},{7,9},{8,14},{9,7},{1... | collective-permute-start | bytes 196616 | tf_op jit(solution)/shard_map/ppermute | solution.py:589
  59.3 10.0 %collective-permute-start.11 = (f32[32,512]{1,0:T(8,128)S(1)}, f32[32,512]{1,0:T(8,128)S(1)}, u32[]{:S(2)}, u32[]{:S(2)}) collective-permute-start(f32[32,512]{1,0:T(8,128)S(1)} %get-tuple-element.53), channel_id=1, source_target_pairs={{0,12},{1,5},{2,14},{3,7},{4,8},{5,1},{6,10},{7,3},{8,4},{9,13},{1... | collective-permute-start | bytes 196616 | tf_op jit(solution)/shard_map/ppermute | solution.py:589
  59.9 12.8 %collective-permute-start.12 = (f32[32,512]{1,0:T(8,128)S(1)}, f32[32,512]{1,0:T(8,128)S(1)}, u32[]{:S(2)}, u32[]{:S(2)}) collective-permute-start(f32[32,512]{1,0:T(8,128)S(1)} %get-tuple-element.54), channel_id=1, source_target_pairs={{0,14},{1,7},{2,12},{3,5},{4,10},{5,3},{6,8},{7,1},{8,6},{9,15},{1... | collective-permute-start | bytes 196616 | tf_op jit(solution)/shard_map/ppermute | solution.py:589
  64.0 8.7 %collective-permute-start.13 = (f32[32,512]{1,0:T(8,128)S(1)}, f32[32,512]{1,0:T(8,128)S(1)}, u32[]{:S(2)}, u32[]{:S(2)}) collective-permute-start(f32[32,512]{1,0:T(8,128)S(1)} %get-tuple-element.55), channel_id=1, source_target_pairs={{0,0},{1,9},{2,2},{3,11},{4,4},{5,13},{6,6},{7,15},{8,8},{9,1},{10... | collective-permute-start | bytes 196616 | tf_op jit(solution)/shard_map/ppermute | solution.py:589
  64.7 8.1 %collective-permute-start.14 = (f32[32,512]{1,0:T(8,128)S(1)}, f32[32,512]{1,0:T(8,128)S(1)}, u32[]{:S(2)}, u32[]{:S(2)}) collective-permute-start(f32[32,512]{1,0:T(8,128)S(1)} %get-tuple-element.56), channel_id=1, source_target_pairs={{0,2},{1,11},{2,0},{3,9},{4,6},{5,15},{6,4},{7,13},{8,10},{9,3},{1... | collective-permute-start | bytes 196616 | tf_op jit(solution)/shard_map/ppermute | solution.py:589
  65.6 7.2 %collective-permute-start.15 = (f32[32,512]{1,0:T(8,128)S(1)}, f32[32,512]{1,0:T(8,128)S(1)}, u32[]{:S(2)}, u32[]{:S(2)}) collective-permute-start(f32[32,512]{1,0:T(8,128)S(1)} %get-tuple-element.57), channel_id=1, source_target_pairs={{0,8},{1,1},{2,10},{3,3},{4,12},{5,5},{6,14},{7,7},{8,0},{9,9},{10... | collective-permute-start | bytes 196616 | tf_op jit(solution)/shard_map/ppermute | solution.py:589
  69.3 5.7 %collective-permute-start.16 = (f32[32,512]{1,0:T(8,128)S(1)}, f32[32,512]{1,0:T(8,128)S(1)}, u32[]{:S(2)}, u32[]{:S(2)}) collective-permute-start(f32[32,512]{1,0:T(8,128)S(1)} %get-tuple-element.58), channel_id=1, source_target_pairs={{0,10},{1,3},{2,8},{3,1},{4,14},{5,7},{6,12},{7,5},{8,2},{9,11},{1... | collective-permute-start | bytes 196616 | tf_op jit(solution)/shard_map/ppermute | solution.py:589

commit v13 on v12

--- a/solution.py
+++ b/solution.py
@@ -167,6 +167,11 @@
         self.blocks, self.rows, self.fine = blocks, rows, fine
         self.count = blocks * trees if fine else 1
         self.per = rows // self.count
+        self.halves = 2 if fine else 1
+        self.span = LEAF // self.halves
+
+    def core(self):
+        return lax.axis_index("rep") if self.fine else 0
 
     def lanes(self, index):
         return slice(index * self.per, (index + 1) * self.per)
@@ -320,32 +325,33 @@
     found = sk_t[:, start * SK : (start + 1) * SK].astype(f32)
     top_ref[0:64, :] = found[0:64] + found[64:128]
     top_ref[64:72, :] = found[128:136]
-    top_ref[72:128, :] = jnp.zeros((56, SK), f32)
     list_tiles(count_ref, list_ref, tiles, times)
     for copy in copies:
         copy.wait()
 
 
-def weights_kernel(
-    layout, base_hbm, upper_tiles_ref, top_ref, slot_ref, light_ref, w_ref, coef_ref, pack_ref, masked, low_hot, base_ref, sems
-):
+def weights_kernel(layout, base_hbm, upper_tiles_ref, top_ref, slot_ref, *refs):
+    light_refs, refs = refs[: layout.halves], refs[layout.halves :]
+    w_ref, coef_ref, pack_ref, masked, low_hot, base_ref, sems = refs
     blocks, rows = layout.blocks, layout.rows
-    width = light_ref.shape[1]
-    pack_ref[...] = top_ref[...]
+    each = light_refs[0].shape[1]
+    width = each * layout.halves
+    pack_ref[0:PLACE_ROWS, :] = top_ref[...]
     for index in range(blocks):
         pltpu.make_async_copy(base_hbm.at[index], base_ref.at[index], sems.at[index]).start()
 
     def keep(node, coef):
         coef_ref[:, node * SK : (node + 1) * SK] = stack_two(coef)
-        pack_ref[LANES - width :, :] = coef
+        pack_ref[PLACE_ROWS:, :] = coef
 
     for index in range(blocks):
         low_part, high_part = parts_of(slot_ref[index : index + 1, :])
         low_by_column(low_hot.at[index], low_part.astype(f32))
-        light = [light_ref[layout.message(g), :, layout.lanes(index)] for g in range(layout.count)]
-        light = lanes_of(light)
-        for h in range(rows // LOW):
-            masked[index, h * width : (h + 1) * width, :] = jnp.where(high_part == h, light, 0.0).astype(bf16)
+        for half, light_ref in enumerate(light_refs):
+            light = lanes_of([light_ref[layout.message(g), :, layout.lanes(index)] for g in range(layout.count)])
+            for h in range(rows // LOW):
+                at = h * width + half * each
+                masked[index, at : at + each, :] = jnp.where(high_part == h, light, 0.0).astype(bf16)
     for index in range(blocks):
         placed = nn(masked[index], low_hot[index])
         for h in range(rows // LOW):
@@ -365,19 +371,19 @@
         start, count = start + count, count // 2
 
 
-def near_kernel(tiles, a_hbm, tree_ref, w_ref, acc, a_ref, bt_ref, sem, *halves):
+def near_kernel(layout, tiles, a_hbm, tree_ref, w_ref, acc, a_ref, bt_ref, sem, *halves):
     copy = pltpu.make_async_copy(a_hbm, a_ref, sem)
     copy.start()
-    for leaf in range(bt_ref.shape[1] // LEAF):
-        here = slice(leaf * LEAF, (leaf + 1) * LEAF)
-        feature_columns(bt_ref, here, tree_ref[:, here])
-
+    span, half = layout.span, LEAF // 2
+    parts = range(span // half)
+    for leaf in range(bt_ref.shape[1] // span):
+        here = aligned(leaf * LEAF + layout.core() * span, span, span)
+        feature_columns(bt_ref, slice(leaf * span, (leaf + 1) * span), tree_ref[:, here])
     filled = tiles[0, tiles.shape[1] - 1]
-    half = LEAF // 2
     acc[...] = jnp.zeros_like(acc)
 
     def target(tile, part):
-        return aligned(tiles[0, tile] * LEAF + part * half, half, half)
+        return aligned(tiles[0, tile] * span + part * half, half, half)
 
     even, odd = halves[0:2], halves[2:4]
     even_tile, odd_tile = halves[4:6], halves[6:8]
@@ -391,13 +397,13 @@
         acc[:, target(tile, part)] += tiles[2, tile].astype(f32) * nn(w_ref[:, source], block[part][...])
 
     def phase(tile, upcoming, ready, made, previous):
-        for part in range(2):
+        for part in parts:
             upcoming[part][...] = exponents(tile + 1, part)
             made[part][...] = jnp.exp(ready[part][...]).astype(bf16)
             add(tile - 1, part, previous)
 
     copy.wait()
-    for part in range(2):
+    for part in parts:
         even[part][...] = exponents(0, part)
         even_tile[part][...] = jnp.exp(even[part][...]).astype(bf16)
         odd[part][...] = exponents(1, part)
@@ -409,23 +415,24 @@
 
     lax.fori_loop(0, (filled - 1) // 2, step, 0)
     done = 2 * ((filled - 1) // 2)
-    for part in range(2):
+    for part in parts:
         add(done, part, even_tile)
 
     @pl.when(done + 1 < filled)
     def _():
-        for part in range(2):
+        for part in parts:
             odd_tile[part][...] = jnp.exp(odd[part][...]).astype(bf16)
             add(done + 1, part, odd_tile)
 
 
 def far_kernel(layout, low_levels, pack_ref, slot_ref, info_ref, tree_ref, sk_ref, coef_ref, near_ref, *refs):
-    out_refs, refs = refs[: layout.count], refs[layout.count :]
+    out_refs, refs = refs[: layout.halves], refs[layout.halves :]
     tops, coefs, scaled, low_hot, bt_ref, sums, masked = refs[:7]
     powers, tiles = refs[7:9], refs[9:11]
     blocks, rows = layout.blocks, layout.rows
-    ups, width = pack_ref.shape[0], out_refs[0].shape[0]
+    ups, width = pack_ref.shape[0], near_ref.shape[0]
     levels = low_levels + ups
+    span, core = layout.span, layout.core()
     per_block = rows // LEAF
     lane = iota((1, SK), 1)
     for up in range(ups):
@@ -436,7 +443,7 @@
         extra = jnp.where(sub < 3, extra, jnp.where(sub < 6, 1.0, 0.0))
         at = slice((low_levels + up) * SK, (low_levels + up + 1) * SK)
         rows_of = feature_rows(high.astype(f32), low.astype(f32), extra)
-        coef = stack_two(pack[LANES - width :])
+        coef = stack_two(pack[PLACE_ROWS:])
         for index in range(blocks):
             tops[index, at, 0:128], tops[index, at, 128:256] = rows_of
             coefs[index, :, at] = coef
@@ -450,7 +457,8 @@
             node, start, count = node // 2, start + count, count // 2
         for leaf in range(per_block):
             here = (index * per_block + leaf) * LEAF
-            feature_columns(bt_ref, slice(here, here + LEAF), tree_ref[:, here : here + LEAF])
+            at = slice(here // layout.halves, here // layout.halves + span)
+            feature_columns(bt_ref, at, tree_ref[:, aligned(here + core * span, span, span)])
             flags = info_ref[index, FLAGS + leaf : FLAGS + leaf + 1, :]
             used = []
             for level in range(levels):
@@ -460,10 +468,10 @@
             scaled[index * per_block + leaf] = (coefs[index].astype(f32) * used).astype(bf16)
 
     def exponents(leaf):
-        powers[leaf % 2][...] = nn(tops[leaf // per_block], bt_ref[:, leaf * LEAF : (leaf + 1) * LEAF])
+        powers[leaf % 2][...] = nn(tops[leaf // per_block], bt_ref[:, leaf * span : (leaf + 1) * span])
 
     def product(leaf):
-        here = slice(leaf * LEAF, (leaf + 1) * LEAF)
+        here = slice(leaf * span, (leaf + 1) * span)
         far = nn(scaled[leaf], tiles[leaf % 2][...])
         sums[:, here] = near_ref[:, here] + far[:width] + far[width:]
 
@@ -478,27 +486,36 @@
     product(leaves - 1)
 
     high_parts = []
+    pieces = rows // LOW // layout.halves
     for index in range(blocks):
         low_part, high_part = parts_of(slot_ref[index : index + 1, :])
         high_parts.append(high_part)
         for c in range(rows // LANES):
             at = slice(c * LANES, (c + 1) * LANES)
             low_hot[index, :, at] = onehot(iota((LOW, LANES), 0) == low_part[:, at])
-        for h in range(rows // LOW):
-            at = index * rows + h * LOW
-            masked[index, h * 2 * width : (h + 1) * 2 * width, :] = stack_two(sums[:, at : at + LOW])
+        for k in range(pieces):
+            at = (index * pieces + k) * LOW
+            masked[index, k * 2 * width : (k + 1) * 2 * width, :] = stack_two(sums[:, at : at + LOW])
     for index in range(blocks):
         moved = nn(masked[index], low_hot[index])
         result = jnp.zeros((2 * width, rows), f32)
-        for h in range(rows // LOW):
-            result = jnp.where(high_parts[index] == h, moved[h * 2 * width : (h + 1) * 2 * width], result)
+        for k in range(pieces):
+            here = high_parts[index] == k * layout.halves + core
+            result = jnp.where(here, moved[k * 2 * width : (k + 1) * 2 * width], result)
         result = result[:width] + result[width:]
-        for g, out_ref in enumerate(out_refs):
-            out_ref[:, layout.lanes(index)] = result[:, g * layout.per : (g + 1) * layout.per]
-
-
-def far_first(blocks, count):
-    return sorted(range(count), key=lambda g: -((g % blocks) * 2 // blocks) if blocks else 0)
+        if not layout.fine:
+            out_refs[0][0, :, layout.lanes(index)] = result
+            continue
+        for g in range(layout.count):
+            out_ref = out_refs[g // blocks]
+            out_ref[g % blocks, :, layout.lanes(index)] = result[:, g * layout.per : (g + 1) * layout.per]
+
+
+def add_kernel(kept_ref, got_ref, *out_refs):
+    half = kept_ref.shape[1] // 2
+    for step, out_ref in enumerate(out_refs):
+        out_ref[0:half, :] = kept_ref[step, 0:half, :] + got_ref[step, half:, :]
+        out_ref[half:, :] = kept_ref[step, half:, :] + got_ref[step, 0:half, :]
 
 
 def final_kernel(blocks, pos_ref, *refs):
@@ -506,14 +523,17 @@
     chunks = pos_ref.shape[0]
     rows = chunks * LANES
     width, split = back_refs[0].shape
+    width = LANES // blocks if blocks else width
     for r in range(chunks):
         spread(perm, slice(r * LANES, (r + 1) * LANES), column(pos_ref[r : r + 1, :]))
-    for g, back_ref in zip(far_first(blocks, len(back_refs)), back_refs):
-        high, low = two(back_ref[...])
+    for g, back_ref in enumerate(back_refs):
         columns, at = 0, slice(0, rows)
+        value = back_ref[...]
         if blocks:
             columns = (lax.axis_index("sub") ^ (g % blocks)) * width
             at = aligned((lax.axis_index("leaf") ^ lax.axis_index("rep") ^ (g // blocks)) * split, split, split)
+            value = value[0:width] if g < blocks else value[width:]
+        high, low = two(value)
         vals[aligned(columns, width, width), at] = high
         vals[aligned(columns + LANES, width, width), at] = low
     step = 256
@@ -523,13 +543,13 @@
         out_ref[here, :] = ridge * weights_ref[here, :] + moved[:, :LANES] + moved[:, LANES:]
 
 
-def upper_levels(pack, skeleton_upper, my_leaf, trees, blocks, width):
+def upper_levels(pack, skeleton_upper, my_leaf, trees, blocks):
     devices = trees * blocks
     level = blocks.bit_length() - 1
     offset = sum(devices >> step for step in range(1, level + 1))
-    line = jnp.arange(LANES)[:, None]
+    line = jnp.arange(pack.shape[0])[:, None]
     is_point, is_norm = line < DIM, (line >= DIM + 3) & (line < DIM + 6)
-    is_coef = line >= LANES - width
+    is_coef = line >= PLACE_ROWS
     packs, own, stride = [], pack, 1
     while stride < trees:
         other = lax.ppermute(own, "leaf", [(i, i ^ stride) for i in range(trees)])
@@ -566,7 +586,7 @@
     fine = trees == 2 and reps == 2 and per % LANES == 0
     layout = Layout(blocks, trees, rows, fine)
     split = part if fine else rows
-    arrive = shaped((width, part), f32) if fine else shaped((width, total), f32)
+    cols = width * layout.halves
 
     place, pos = pl.pallas_call(
         functools.partial(place_kernel, fine),
@@ -588,8 +608,8 @@
                     pairs.append(((leaf * blocks + sub) * reps + core, to))
         return lax.ppermute(value, axes, pairs)
 
-    def swap_all(values):
-        return [swap(values[g], g % blocks, g // blocks) for g in far_first(blocks, len(values))]
+    def other_core(value):
+        return lax.ppermute(value, "rep", [(0, 1), (1, 0)])
 
     def sorted_light():
         return pl.pallas_call(
@@ -611,10 +631,11 @@
             stride //= 2
         light = sorted_light()
         place, light = lax.optimization_barrier((place, light))
-        theirs = {step: lax.ppermute(one, "rep", [(0, 1), (1, 0)]) for step, one in place.items()}
+        theirs = {step: other_core(one) for step, one in place.items()}
         place = [place[step] for step in range(blocks)] + [theirs[step] for step in range(blocks)]
         light = light.reshape(devices, width, part)
         light = lax.all_to_all(light, ("leaf", "sub"), split_axis=0, concat_axis=0, tiled=True)
+        light = [light, other_core(light)]
         small = []
     else:
         info = jnp.pad(far_use.astype(f32), ((FLAGS, 5 - far_use.shape[0]), (0, SK - far_use.shape[1])))
@@ -627,7 +648,7 @@
         light = sorted_light().reshape(columns, trees, part).transpose(1, 0, 2).reshape(devices, width, part)
         light = lax.all_to_all(light, ("leaf", "sub"), split_axis=0, concat_axis=0, tiled=True)
         light = light.reshape(devices, width, blocks, per)
-        light = light.transpose(1, 2, 0, 3).reshape(1, width, total)
+        light = [light.transpose(1, 2, 0, 3).reshape(1, width, total)]
 
     nodes = 2 * blocks - 1
     tree, feat_a, base, sk, upper_tiles, top, slots, info, tiles = pl.pallas_call(
@@ -638,7 +659,7 @@
             pltpu.MemorySpace.HBM((blocks, rows, SK), bf16),
             vm((nodes * SK, FEAT), bf16),
             vm((blocks - 1, 2 * SK, SK), f32),
-            vm((SK, LANES), f32),
+            vm((PLACE_ROWS, SK), f32),
             vm((blocks, rows), f32),
             vm((blocks, 8, SK), f32),
             pltpu.MemorySpace.HBM((3, leaves * leaves + 3), jnp.int32),
@@ -662,32 +683,32 @@
     tree_light, coefs, pack = pl.pallas_call(
         functools.partial(weights_kernel, layout),
         out_shape=(
-            vm((width, total), bf16),
-            vm((2 * width, nodes * SK), bf16),
-            shaped((LANES, SK), f32),
+            vm((cols, total), bf16),
+            vm((2 * cols, nodes * SK), bf16),
+            shaped((PLACE_ROWS + cols, SK), f32),
         ),
-        in_specs=[spec(pl.ANY)] + [spec()] * 4,
+        in_specs=[spec(pl.ANY)] + [spec()] * (3 + layout.halves),
         out_specs=(spec(),) * 3,
         scratch_shapes=[
-            vm((blocks, rows // LOW * width, rows), bf16),
+            vm((blocks, rows // LOW * cols, rows), bf16),
             vm((blocks, rows, LOW), bf16),
             vm((blocks, rows, SK), bf16),
             pltpu.SemaphoreType.DMA((blocks,)),
         ],
         compiler_params=params(40),
         name="tree_weights",
-    )(in_hbm(base), held(upper_tiles), held(top), held(slots), light)
-
-    packs = upper_levels(pack, skeleton_upper, my_leaf, trees, blocks, width)
+    )(in_hbm(base), held(upper_tiles), held(top), held(slots), *light)
+
+    packs = upper_levels(pack, skeleton_upper, my_leaf, trees, blocks)
 
     near = pl.pallas_call(
-        near_kernel,
-        out_shape=vm((width, total), f32),
+        functools.partial(near_kernel, layout),
+        out_shape=vm((cols, total // layout.halves), f32),
         in_specs=[spec(SMEM), spec(pl.ANY)] + [spec()] * 2,
         out_specs=spec(),
         scratch_shapes=[
             vm((total, FEAT), bf16),
-            vm((FEAT, total), bf16),
+            vm((FEAT, total // layout.halves), bf16),
             pltpu.SemaphoreType.DMA(()),
         ]
         + [vm((LEAF, LEAF // 2), f32)] * 4
@@ -699,28 +720,39 @@
     levels = low_levels + ups
     back = pl.pallas_call(
         functools.partial(far_kernel, layout, low_levels),
-        out_shape=(arrive,) * layout.count,
+        out_shape=(shaped((layout.count // layout.halves, cols, total // layout.count), f32),) * layout.halves,
         in_specs=[spec()] * 7,
-        out_specs=(spec(),) * layout.count,
+        out_specs=(spec(),) * layout.halves,
         scratch_shapes=[
             vm((blocks, levels * SK, FEAT), bf16),
-            vm((blocks, 2 * width, levels * SK), bf16),
-            vm((leaves, 2 * width, levels * SK), bf16),
+            vm((blocks, 2 * cols, levels * SK), bf16),
+            vm((leaves, 2 * cols, levels * SK), bf16),
             vm((blocks, LOW, rows), bf16),
-            vm((FEAT, total), bf16),
-            vm((width, total), f32),
-            vm((blocks, rows // LOW * 2 * width, LOW), bf16),
+            vm((FEAT, total // layout.halves), bf16),
+            vm((cols, total // layout.halves), f32),
+            vm((blocks, rows // LOW // layout.halves * 2 * cols, LOW), bf16),
         ]
-        + [vm((levels * SK, LEAF), f32)] * 2
-        + [vm((levels * SK, LEAF), bf16)] * 2,
+        + [vm((levels * SK, layout.span), f32)] * 2
+        + [vm((levels * SK, layout.span), bf16)] * 2,
         compiler_params=params(40),
         name="far",
     )(packs, *[held(one) for one in (slots, info, tree, sk, coefs, near)])
 
     if fine:
-        back = swap_all(back)
+        kept, sent = back
+        sums = pl.pallas_call(
+            add_kernel,
+            out_shape=(shaped((cols, part), f32),) * blocks,
+            in_specs=[spec()] * 2,
+            out_specs=(spec(),) * blocks,
+            compiler_params=params(40),
+            name="add_cores",
+        )(kept, other_core(sent))
+        back = {step: swap(sums[step], step) for step in reversed(range(blocks))}
+        back = [back[step] for step in range(blocks)]
+        back = back + [other_core(one) for one in back]
     else:
-        back = back[0].reshape(width, blocks, devices, per).transpose(2, 0, 1, 3).reshape(devices, width, part)
+        back = back[0].reshape(cols, blocks, devices, per).transpose(2, 0, 1, 3).reshape(devices, width, part)
         back = lax.all_to_all(back, ("leaf", "sub"), split_axis=0, concat_axis=0, tiled=True)
         back = [back.reshape(trees, columns, part).transpose(1, 0, 2).reshape(columns, rows)]
 

time: 77.6 us -> 84 us (1.082)
  blocking collectives: 0 us -> 21.3 us
  waiting for transfers between devices: 18.3 us -> 10 us
  Pallas kernels: 28.9 us -> 25.6 us
  starting transfers between devices: 29.6 us -> 26.7 us
    all_to_all x0 -> x1, blocking collectives: none -> 21.3 us  [body(): lax.all_to_all(light, ('leaf', 'sub'), split_axis=0, concat_axis=0, tiled...]
    ppermute x4 -> x10, starting transfers between devices: 2.54 us -> 12.9 us  [other_core(): return lax.ppermute(value, 'rep', [(0, 1), (1, 0)])]
    ppermute x9 -> x5, starting transfers between devices: 14.5 us -> 6.67 us  [swap(): return lax.ppermute(value, axes, pairs)]
    all_to_all x1 -> x0, waiting for transfers between devices: 6.6 us -> none  [body(): lax.all_to_all(light, ('leaf', 'sub'), split_axis=0, concat_axis=0, tiled...]
    all_to_all x1 -> x0, starting transfers between devices: 5.45 us -> none  [body(): lax.all_to_all(light, ('leaf', 'sub'), split_axis=0, concat_axis=0, tiled...]
    ppermute x9 -> x5, waiting for transfers between devices: 4.85 us -> 0.01 us  [swap(): return lax.ppermute(value, axes, pairs)]
    ppermute x4 -> x10, waiting for transfers between devices: 1.3 us -> 4.53 us  [other_core(): return lax.ppermute(value, 'rep', [(0, 1), (1, 0)])]
    pallas_call x1 -> x2, Pallas kernels: 10.9 us -> 8.01 us  [the longest x1 7.96 us: body(): pl.pallas_call(functools.partial(near_kernel, layout), out_shape=vm((cols...]
  transfers between devices with their start and end apart: 18 -> 19, of which waited for: 10 -> 9; matrix products, arithmetic and copies ran while one was open for 0% -> 0% of each run, Pallas kernels for 24% -> 19%
where the time goes in v13:
time: 84 us; the launch traced here: 83.7 us
  starting transfers between devices  26.7 us (32%)
  Pallas kernels  25.6 us (30%)
  blocking collectives  21.3 us (25%)
  waiting for transfers between devices  10 us (12%)
    all_to_all x1, blocking collectives, body(): lax.all_to_all(light, ('leaf', 'sub'), split_axis=0, concat_axis=0, tiled...  21.3 us
    ppermute x10, starting transfers between devices, other_core(): return lax.ppermute(value, 'rep', [(0, 1), (1, 0)])  12.9 us
    pallas_call x1, Pallas kernels, body(): pl.pallas_call(functools.partial(near_kernel, layout), out_shape=vm((cols...  7.96 us
    ppermute x5, starting transfers between devices, swap(): return lax.ppermute(value, axes, pairs)  6.67 us
    ppermute x3, starting transfers between devices, body(): lax.ppermute(place[step], 'sub', [(i, i ^ stride) for i in range(blocks)])  6.51 us
    ppermute x3, waiting for transfers between devices, body(): lax.ppermute(place[step], 'sub', [(i, i ^ stride) for i in range(blocks)])  5.51 us
    pallas_call x1, Pallas kernels, body(): pl.pallas_call(functools.partial(points_kernel, layout, trees), out_shape...  5.37 us
    ppermute x10, waiting for transfers between devices, other_core(): return lax.ppermute(value, 'rep', [(0, 1), (1, 0)])  4.53 us
  transfers between devices with their start and end apart: 19, of which 9 were waited for; matrix products, arithmetic and copies ran while one was open for 0% of the time, Pallas kernels for 19%

profile of v13, /device:TPU:0, one launch (start us, length us, event | category | flops | bytes accessed | tf_op | source)
XLA Modules:
  0.0 83.7 jit_solution(3437480844083710726)
XLA Ops:
  0.0 2.7 %sort_points.1 = (f32[72,512]{1,0:T(8,128)}, f32[8,128]{1,0:T(8,128)}) custom-call(s32[8,128]{1,0:T(8,128)} %bitcast.8, f32[64,1024]{1,0:T(8,128)} %bitcast.7, s32[1,128]{1,0:T(1,128)} %base_ref.1, s32[2,3]{1,0:T(2,128)} %flag_ref.1), custom_call_target="tpu_custom_call" | custom-call | tf_op jit(solution)/shard_map/sort_points/pallas_call | solution.py:591
  2.7 1.6 %collective-permute-start = (f32[72,512]{1,0:T(8,128)}, f32[72,512]{1,0:T(8,128)S(1)}, u32[]{:S(2)}, u32[]{:S(2)}) collective-permute-start(f32[72,512]{1,0:T(8,128)} %get-tuple-element.31), channel_id=1, source_target_pairs={{0,0},{1,9},{2,2},{3,11},{4,4},{5,13},{6,6},{7,15},{8,8},{9,1},{10... | collective-permute-start | bytes 442376 | tf_op jit(solution)/shard_map/ppermute | solution.py:609
  4.3 4.0 %collective-permute-start.2 = (f32[72,512]{1,0:T(8,128)S(1)}, f32[72,512]{1,0:T(8,128)S(1)}, u32[]{:S(2)}, u32[]{:S(2)}) collective-permute-start(f32[72,512]{1,0:T(8,128)S(1)} %collective-permute-done.refs_0_), channel_id=1, source_target_pairs={{0,4},{2,6},{4,0},{6,2},{1,5},{3,7},{5,1},{7,3},{8,12},{10,14},{12... | collective-permute-start | bytes 442376 | tf_op jit(solution)/shard_map/ppermute | solution.py:630
  8.3 1.6 %collective-permute-start.1 = (f32[72,512]{1,0:T(8,128)S(1)}, f32[72,512]{1,0:T(8,128)S(1)}, u32[]{:S(2)}, u32[]{:S(2)}) collective-permute-start(f32[72,512]{1,0:T(8,128)S(1)} %collective-permute-done.refs_0_), channel_id=1, source_target_pairs={{0,2},{2,0},{4,6},{6,4},{1,3},{3,1},{5,7},{7,5},{8,10},{10,8},{12,... | collective-permute-start | bytes 442376 | tf_op jit(solution)/shard_map/ppermute | solution.py:630
  9.9 3.2 %collective-permute-done.2.refs_2_ = f32[72,512]{1,0:T(8,128)S(1)} collective-permute-done((f32[72,512]{1,0:T(8,128)S(1)}, f32[72,512]{1,0:T(8,128)S(1)}, u32[]{:S(2)}, u32[]{:S(2)}) %collective-permute-start.2) | collective-permute-done | bytes 147488 | tf_op jit(solution)/shard_map/ppermute | solution.py:630
  13.2 0.9 %collective-permute-start.3 = (f32[72,512]{1,0:T(8,128)S(1)}, f32[72,512]{1,0:T(8,128)S(1)}, u32[]{:S(2)}, u32[]{:S(2)}) collective-permute-start(f32[72,512]{1,0:T(8,128)S(1)} %collective-permute-done.2.refs_2_), channel_id=1, source_target_pairs={{0,2},{2,0},{4,6},{6,4},{1,3},{3,1},{5,7},{7,5},{8,10},{10,8},{12,... | collective-permute-start | bytes 442376 | tf_op jit(solution)/shard_map/ppermute | solution.py:630
  14.1 2.6 %sort_weights.1 = f32[2,128,512]{2,1,0:T(8,128)} custom-call(f32[8,128]{1,0:T(8,128)} %get-tuple-element.30.pos_ref, f32[1024,128]{1,0:T(8,128)} %refs_8_.1), custom_call_target="tpu_custom_call" | custom-call | tf_op jit(solution)/shard_map/sort_weights/pallas_call | solution.py:615
  16.6 2.3 %collective-permute-done.3.refs_3_ = f32[72,512]{1,0:T(8,128)S(1)} collective-permute-done((f32[72,512]{1,0:T(8,128)S(1)}, f32[72,512]{1,0:T(8,128)S(1)}, u32[]{:S(2)}, u32[]{:S(2)}) %collective-permute-start.3) | collective-permute-done | bytes 147488 | tf_op jit(solution)/shard_map/ppermute | solution.py:630
  18.9 21.3 %all_to_all.5.refs_0_ = f32[8,32,512]{2,1,0:T(8,128)S(1)} all-to-all(f32[8,32,512]{2,1,0:T(8,128)} %bitcast.6), channel_id=1, replica_groups=mesh['groups'=2,'leaf'=2,'sub'=4,'rep'=2] {'leaf','sub'}, dimensions={0} | all-to-all | bytes 1048576 | tf_op jit(solution)/shard_map/all_to_all | solution.py:637
  40.1 0.8 collective-permute-start.8
  42.0 0.7 collective-permute-done.4.refs_4_
  43.3 5.4 %tree_points.1 = (bf16[144,4096]{1,0:T(8,128)(2,1)S(1)}, bf16[4096,256]{1,0:T(8,128)(2,1)}, bf16[4,1024,128]{2,1,0:T(8,128)(2,1)}, bf16[896,256]{1,0:T(8,128)(2,...) custom-call(s32[1,8]{1,0:T(1,128)} %count_ref.1, ...), custom_call_target="tpu_custom_call" | custom-call | tf_op jit(solution)/shard_map/tree_points/pallas_call | solution.py:654
  48.7 2.8 %tree_weights.1 = (bf16[64,4096]{1,0:T(8,128)(2,1)S(1)}, bf16[128,896]{1,0:T(8,128)(2,1)S(1)}, f32[136,128]{1,0:T(8,128)S(1)}) custom-call(bf16[4,1024,128]{2,1,0:T(8,128)(2,1)} %get-tuple-element.36.base_hbm, f32[3,256,128]{2,1,0:T(8,128)S(1)} %get-tuple-element.37.upper_tiles_ref, f32[72,128]{1,0:T(8,128)S(1)} %get-tuple-element.38.top_ref, ...), custom_call_target="tpu_custom_call" | custom-call | tf_op jit(solution)/shard_map/tree_weights/pallas_call | solution.py:683
  52.2 8.0 %near.1.near_ref = f32[64,2048]{1,0:T(8,128)S(1)} custom-call(s32[3,67]{1,0:T(4,128)} %get-tuple-element.46.tiles, bf16[4096,256]{1,0:T(8,128)(2,1)} %get-tuple-element.47.a_hbm, bf16[144,4096]{1,0:T(8,128)(2,1)S(1)} %get-tuple-element.43.tree_ref, bf16[64,4096]{1,0:T(8,128)(2,1)S(1)} %get-tuple-element.48.w_ref), custom_call_target="tpu_custom_call" | custom-call | tf_op jit(solution)/shard_map/near/pallas_call | solution.py:704
  60.2 2.2 %far.1 = (f32[4,64,512]{2,1,0:T(8,128)S(1)}, f32[4,64,512]{2,1,0:T(8,128)S(1)}) custom-call(f32[1,136,128]{2,1,0:T(8,128)S(1)} %bitcast.5, f32[4,1024]{1,0:T(4,128)S(1)} %get-tuple-element.39.slot_ref, f32[4,8,128]{2,1,0:T(8,128)S(1)} %get-tuple-element.42.info_ref, bf16[144,4096]{1,0:T(8,128)(2,1)S(1)} %get-tuple-element.43.tree_ref, ...), custom_call_target="tpu_custom_call" | custom-call | tf_op jit(solution)/shard_map/far/pallas_call | solution.py:721
  62.5 1.8 %collective-permute-done.10.got_ref = f32[4,64,512]{2,1,0:T(8,128)S(1)} collective-permute-done((f32[4,64,512]{2,1,0:T(8,128)S(1)}, f32[4,64,512]{2,1,0:T(8,128)S(1)}, u32[]{:S(2)}, u32[]{:S(2)}) %collective-permute-start.10) | collective-permute-done | bytes 524320 | tf_op jit(solution)/shard_map/ppermute | solution.py:612
  64.4 0.7 collective-permute-start.11
  65.1 1.1 %collective-permute-start.13 = (f32[64,512]{1,0:T(8,128)S(1)}, f32[64,512]{1,0:T(8,128)S(1)}, u32[]{:S(2)}, u32[]{:S(2)}) collective-permute-start(f32[64,512]{1,0:T(8,128)S(1)} %get-tuple-element.53), channel_id=1, source_target_pairs={{0,4},{1,13},{2,6},{3,15},{4,0},{5,9},{6,2},{7,11},{8,12},{9,5},{1... | collective-permute-start | bytes 393224 | tf_op jit(solution)/shard_map/ppermute | solution.py:609
  66.2 3.3 %collective-permute-start.14 = (f32[64,512]{1,0:T(8,128)S(1)}, f32[64,512]{1,0:T(8,128)S(1)}, u32[]{:S(2)}, u32[]{:S(2)}) collective-permute-start(f32[64,512]{1,0:T(8,128)S(1)} %get-tuple-element.54), channel_id=1, source_target_pairs={{0,6},{1,15},{2,4},{3,13},{4,2},{5,11},{6,0},{7,9},{8,14},{9,7},{1... | collective-permute-start | bytes 393224 | tf_op jit(solution)/shard_map/ppermute | solution.py:609
  69.5 2.6 %collective-permute-start.15 = (f32[64,512]{1,0:T(8,128)S(1)}, f32[64,512]{1,0:T(8,128)S(1)}, u32[]{:S(2)}, u32[]{:S(2)}) collective-permute-start(f32[64,512]{1,0:T(8,128)S(1)} %collective-permute-done.11.refs_0_), channel_id=1, source_target_pairs={{0,1},{1,0},{2,3},{3,2},{4,5},{5,4},{6,7},{7,6},{8,9},{9,8},{10,11... | collective-permute-start | bytes 393224 | tf_op jit(solution)/shard_map/ppermute | solution.py:612
  72.1 2.1 %collective-permute-start.16 = (f32[64,512]{1,0:T(8,128)S(1)}, f32[64,512]{1,0:T(8,128)S(1)}, u32[]{:S(2)}, u32[]{:S(2)}) collective-permute-start(f32[64,512]{1,0:T(8,128)S(1)} %collective-permute-done.12.refs_1_), channel_id=1, source_target_pairs={{0,1},{1,0},{2,3},{3,2},{4,5},{5,4},{6,7},{7,6},{8,9},{9,8},{10,11... | collective-permute-start | bytes 393224 | tf_op jit(solution)/shard_map/ppermute | solution.py:612
  74.2 6.2 %collective-permute-start.17 = (f32[64,512]{1,0:T(8,128)S(1)}, f32[64,512]{1,0:T(8,128)S(1)}, u32[]{:S(2)}, u32[]{:S(2)}) collective-permute-start(f32[64,512]{1,0:T(8,128)S(1)} %collective-permute-done.13.refs_2_), channel_id=1, source_target_pairs={{0,1},{1,0},{2,3},{3,2},{4,5},{5,4},{6,7},{7,6},{8,9},{9,8},{10,11... | collective-permute-start | bytes 393224 | tf_op jit(solution)/shard_map/ppermute | solution.py:612
  80.4 1.0 %collective-permute-done.17.refs_6_ = f32[64,512]{1,0:T(8,128)S(1)} collective-permute-done((f32[64,512]{1,0:T(8,128)S(1)}, f32[64,512]{1,0:T(8,128)S(1)}, u32[]{:S(2)}, u32[]{:S(2)}) %collective-permute-start.17) | collective-permute-done | bytes 131104 | tf_op jit(solution)/shard_map/ppermute | solution.py:612
  81.8 1.9 %to_input_order.1 = f32[1024,128]{1,0:T(8,128)} custom-call(f32[8,128]{1,0:T(8,128)S(1)} %copy-done.1, f32[64,512]{1,0:T(8,128)S(1)} %collective-permute-done.11.refs_0_, f32[64,512]{1,0:T(8,128)S(1)} %collective-permute-done.12.refs_1_, f32[64,512]{1,0:T(8,128)S(1)} %collective-permute-done.13.refs_2_, f32[64,512]{1,0:T(8,128)S(1)} %collective-permute-done.14.refs_3_, ...), custom_call_target="tpu_custom_call" | custom-call | tf_op jit(solution)/shard_map/to_input_order/pallas_call | solution.py:759
  (27 shorter events, 3.0 us)
Async XLA Ops:
  2.7 1.6 %collective-permute-start = (f32[72,512]{1,0:T(8,128)}, f32[72,512]{1,0:T(8,128)S(1)}, u32[]{:S(2)}, u32[]{:S(2)}) collective-permute-start(f32[72,512]{1,0:T(8,128)} %get-tuple-element.31), channel_id=1, source_target_pairs={{0,0},{1,9},{2,2},{3,11},{4,4},{5,13},{6,6},{7,15},{8,8},{9,1},{10... | collective-permute-start | bytes 442376 | tf_op jit(solution)/shard_map/ppermute | solution.py:609
  4.3 8.8 %collective-permute-start.2 = (f32[72,512]{1,0:T(8,128)S(1)}, f32[72,512]{1,0:T(8,128)S(1)}, u32[]{:S(2)}, u32[]{:S(2)}) collective-permute-start(f32[72,512]{1,0:T(8,128)S(1)} %collective-permute-done.refs_0_), channel_id=1, source_target_pairs={{0,4},{2,6},{4,0},{6,2},{1,5},{3,7},{5,1},{7,3},{8,12},{10,14},{12... | collective-permute-start | bytes 442376 | tf_op jit(solution)/shard_map/ppermute | solution.py:630
  8.3 8.3 %collective-permute-start.1 = (f32[72,512]{1,0:T(8,128)S(1)}, f32[72,512]{1,0:T(8,128)S(1)}, u32[]{:S(2)}, u32[]{:S(2)}) collective-permute-start(f32[72,512]{1,0:T(8,128)S(1)} %collective-permute-done.refs_0_), channel_id=1, source_target_pairs={{0,2},{2,0},{4,6},{6,4},{1,3},{3,1},{5,7},{7,5},{8,10},{10,8},{12,... | collective-permute-start | bytes 442376 | tf_op jit(solution)/shard_map/ppermute | solution.py:630
  13.2 5.7 %collective-permute-start.3 = (f32[72,512]{1,0:T(8,128)S(1)}, f32[72,512]{1,0:T(8,128)S(1)}, u32[]{:S(2)}, u32[]{:S(2)}) collective-permute-start(f32[72,512]{1,0:T(8,128)S(1)} %collective-permute-done.2.refs_2_), channel_id=1, source_target_pairs={{0,2},{2,0},{4,6},{6,4},{1,3},{3,1},{5,7},{7,5},{8,10},{10,8},{12,... | collective-permute-start | bytes 442376 | tf_op jit(solution)/shard_map/ppermute | solution.py:630
  40.1 8.6 %collective-permute-start.8 = (f32[8,32,512]{2,1,0:T(8,128)S(1)}, f32[8,32,512]{2,1,0:T(8,128)S(1)}, u32[]{:S(2)}, u32[]{:S(2)}) collective-permute-start(f32[8,32,512]{2,1,0:T(8,128)S(1)} %all_to_all.5.refs_0_), channel_id=1, source_target_pairs={{0,1},{1,0},{2,3},{3,2},{4,5},{5,4},{6,7},{7,6},{8,9},{9,8},{10,11... | collective-permute-start | bytes 1572872 | tf_op jit(solution)/shard_map/ppermute | solution.py:612
  41.0 1.7 %collective-permute-start.4 = (f32[72,512]{1,0:T(8,128)S(1)}, f32[72,512]{1,0:T(8,128)S(1)}, u32[]{:S(2)}, u32[]{:S(2)}) collective-permute-start(f32[72,512]{1,0:T(8,128)S(1)} %collective-permute-done.refs_0_), channel_id=1, source_target_pairs={{0,1},{1,0},{2,3},{3,2},{4,5},{5,4},{6,7},{7,6},{8,9},{9,8},{10,11... | collective-permute-start | bytes 442376 | tf_op jit(solution)/shard_map/ppermute | solution.py:612
  41.0 2.0 %collective-permute-start.5 = (f32[72,512]{1,0:T(8,128)S(1)}, f32[72,512]{1,0:T(8,128)S(1)}, u32[]{:S(2)}, u32[]{:S(2)}) collective-permute-start(f32[72,512]{1,0:T(8,128)S(1)} %collective-permute-done.1.refs_1_), channel_id=1, source_target_pairs={{0,1},{1,0},{2,3},{3,2},{4,5},{5,4},{6,7},{7,6},{8,9},{9,8},{10,11... | collective-permute-start | bytes 442376 | tf_op jit(solution)/shard_map/ppermute | solution.py:612
  41.5 1.7 %collective-permute-start.6 = (f32[72,512]{1,0:T(8,128)S(1)}, f32[72,512]{1,0:T(8,128)S(1)}, u32[]{:S(2)}, u32[]{:S(2)}) collective-permute-start(f32[72,512]{1,0:T(8,128)S(1)} %collective-permute-done.2.refs_2_), channel_id=1, source_target_pairs={{0,1},{1,0},{2,3},{3,2},{4,5},{5,4},{6,7},{7,6},{8,9},{9,8},{10,11... | collective-permute-start | bytes 442376 | tf_op jit(solution)/shard_map/ppermute | solution.py:612
  41.5 1.9 %collective-permute-start.7 = (f32[72,512]{1,0:T(8,128)S(1)}, f32[72,512]{1,0:T(8,128)S(1)}, u32[]{:S(2)}, u32[]{:S(2)}) collective-permute-start(f32[72,512]{1,0:T(8,128)S(1)} %collective-permute-done.3.refs_3_), channel_id=1, source_target_pairs={{0,1},{1,0},{2,3},{3,2},{4,5},{5,4},{6,7},{7,6},{8,9},{9,8},{10,11... | collective-permute-start | bytes 442376 | tf_op jit(solution)/shard_map/ppermute | solution.py:612
  51.5 8.6 %collective-permute-start.9 = (f32[136,128]{1,0:T(8,128)S(1)}, f32[136,128]{1,0:T(8,128)S(1)}, u32[]{:S(2)}, u32[]{:S(2)}) collective-permute-start(f32[136,128]{1,0:T(8,128)S(1)} %get-tuple-element.41), channel_id=1, source_target_pairs={{0,8},{8,0},{1,9},{9,1},{2,10},{10,2},{3,11},{11,3},{4,12},{12,4},... | collective-permute-start | bytes 208904 | tf_op jit(solution)/shard_map/ppermute | solution.py:555
  60.1 21.6 %copy-start = (f32[1024,128]{1,0:T(8,128)S(1)}, f32[1024,128]{1,0:T(8,128)}, u32[]{:S(2)}) copy-start(f32[1024,128]{1,0:T(8,128)} %refs_8_.1) | copy-start | bytes 1572868
  60.1 21.6 %copy-start.1 = (f32[8,128]{1,0:T(8,128)S(1)}, f32[8,128]{1,0:T(8,128)}, u32[]{:S(2)}) copy-start(f32[8,128]{1,0:T(8,128)} %get-tuple-element.30.pos_ref) | copy-start | bytes 12292
  62.3 2.0 %collective-permute-start.10 = (f32[4,64,512]{2,1,0:T(8,128)S(1)}, f32[4,64,512]{2,1,0:T(8,128)S(1)}, u32[]{:S(2)}, u32[]{:S(2)}) collective-permute-start(f32[4,64,512]{2,1,0:T(8,128)S(1)} %get-tuple-element.50), channel_id=1, source_target_pairs={{0,1},{1,0},{2,3},{3,2},{4,5},{5,4},{6,7},{7,6},{8,9},{9,8},{10,11... | collective-permute-start | bytes 1572872 | tf_op jit(solution)/shard_map/ppermute | solution.py:612
  64.4 5.1 %collective-permute-start.11 = (f32[64,512]{1,0:T(8,128)S(1)}, f32[64,512]{1,0:T(8,128)S(1)}, u32[]{:S(2)}, u32[]{:S(2)}) collective-permute-start(f32[64,512]{1,0:T(8,128)S(1)} %get-tuple-element.51), channel_id=1, source_target_pairs={{0,0},{1,9},{2,2},{3,11},{4,4},{5,13},{6,6},{7,15},{8,8},{9,1},{10... | collective-permute-start | bytes 393224 | tf_op jit(solution)/shard_map/ppermute | solution.py:609
  65.0 7.1 %collective-permute-start.12 = (f32[64,512]{1,0:T(8,128)S(1)}, f32[64,512]{1,0:T(8,128)S(1)}, u32[]{:S(2)}, u32[]{:S(2)}) collective-permute-start(f32[64,512]{1,0:T(8,128)S(1)} %get-tuple-element.52), channel_id=1, source_target_pairs={{0,2},{1,11},{2,0},{3,9},{4,6},{5,15},{6,4},{7,13},{8,10},{9,3},{1... | collective-permute-start | bytes 393224 | tf_op jit(solution)/shard_map/ppermute | solution.py:609
  65.1 9.1 %collective-permute-start.13 = (f32[64,512]{1,0:T(8,128)S(1)}, f32[64,512]{1,0:T(8,128)S(1)}, u32[]{:S(2)}, u32[]{:S(2)}) collective-permute-start(f32[64,512]{1,0:T(8,128)S(1)} %get-tuple-element.53), channel_id=1, source_target_pairs={{0,4},{1,13},{2,6},{3,15},{4,0},{5,9},{6,2},{7,11},{8,12},{9,5},{1... | collective-permute-start | bytes 393224 | tf_op jit(solution)/shard_map/ppermute | solution.py:609
  66.2 14.2 %collective-permute-start.14 = (f32[64,512]{1,0:T(8,128)S(1)}, f32[64,512]{1,0:T(8,128)S(1)}, u32[]{:S(2)}, u32[]{:S(2)}) collective-permute-start(f32[64,512]{1,0:T(8,128)S(1)} %get-tuple-element.54), channel_id=1, source_target_pairs={{0,6},{1,15},{2,4},{3,13},{4,2},{5,11},{6,0},{7,9},{8,14},{9,7},{1... | collective-permute-start | bytes 393224 | tf_op jit(solution)/shard_map/ppermute | solution.py:609
  69.5 10.9 %collective-permute-start.15 = (f32[64,512]{1,0:T(8,128)S(1)}, f32[64,512]{1,0:T(8,128)S(1)}, u32[]{:S(2)}, u32[]{:S(2)}) collective-permute-start(f32[64,512]{1,0:T(8,128)S(1)} %collective-permute-done.11.refs_0_), channel_id=1, source_target_pairs={{0,1},{1,0},{2,3},{3,2},{4,5},{5,4},{6,7},{7,6},{8,9},{9,8},{10,11... | collective-permute-start | bytes 393224 | tf_op jit(solution)/shard_map/ppermute | solution.py:612
  72.1 8.3 %collective-permute-start.16 = (f32[64,512]{1,0:T(8,128)S(1)}, f32[64,512]{1,0:T(8,128)S(1)}, u32[]{:S(2)}, u32[]{:S(2)}) collective-permute-start(f32[64,512]{1,0:T(8,128)S(1)} %collective-permute-done.12.refs_1_), channel_id=1, source_target_pairs={{0,1},{1,0},{2,3},{3,2},{4,5},{5,4},{6,7},{7,6},{8,9},{9,8},{10,11... | collective-permute-start | bytes 393224 | tf_op jit(solution)/shard_map/ppermute | solution.py:612
  74.2 7.2 %collective-permute-start.17 = (f32[64,512]{1,0:T(8,128)S(1)}, f32[64,512]{1,0:T(8,128)S(1)}, u32[]{:S(2)}, u32[]{:S(2)}) collective-permute-start(f32[64,512]{1,0:T(8,128)S(1)} %collective-permute-done.13.refs_2_), channel_id=1, source_target_pairs={{0,1},{1,0},{2,3},{3,2},{4,5},{5,4},{6,7},{7,6},{8,9},{9,8},{10,11... | collective-permute-start | bytes 393224 | tf_op jit(solution)/shard_map/ppermute | solution.py:612
  80.4 1.3 %collective-permute-start.18 = (f32[64,512]{1,0:T(8,128)S(1)}, f32[64,512]{1,0:T(8,128)S(1)}, u32[]{:S(2)}, u32[]{:S(2)}) collective-permute-start(f32[64,512]{1,0:T(8,128)S(1)} %collective-permute-done.14.refs_3_), channel_id=1, source_target_pairs={{0,1},{1,0},{2,3},{3,2},{4,5},{5,4},{6,7},{7,6},{8,9},{9,8},{10,11... | collective-permute-start | bytes 393224 | tf_op jit(solution)/shard_map/ppermute | solution.py:612

commit v14 on v13

--- a/solution.py
+++ b/solution.py
@@ -13,6 +13,7 @@
 LANES = 128
 FEAT = 256
 LOW = 256
+AHEAD = 24
 COORD = 144
 
 highest = lax.Precision.HIGHEST
@@ -169,6 +170,7 @@
         self.per = rows // self.count
         self.halves = 2 if fine else 1
         self.span = LEAF // self.halves
+        self.ahead = AHEAD // 4 * 4 if fine else 4
 
     def core(self):
         return lax.axis_index("rep") if self.fine else 0
@@ -222,6 +224,36 @@
     return first.astype(bf16), second.astype(bf16)
 
 
+def target_columns(layout, out, tree_ref):
+    span = layout.span
+    for leaf in range(out.shape[1] // span):
+        here = aligned(leaf * LEAF + layout.core() * span, span, span)
+        feature_columns(out, slice(leaf * span, (leaf + 1) * span), tree_ref[:, here])
+
+
+def tile_exponents(layout, tiles, tile, a_ref, bt_ref):
+    source = aligned(tiles[1, tile] * LEAF, LEAF, LEAF)
+    target = aligned(tiles[0, tile] * layout.span, layout.span, layout.span)
+    return nn(a_ref[source, :], bt_ref[:, target])
+
+
+def tiles_ahead(layout, tiles, a_ref, bt_ref, even, odd, made, made_hbm, sems):
+    def send(tile):
+        return pltpu.make_async_copy(made.at[tile], made_hbm.at[tile], sems.at[tile])
+
+    even[...] = tile_exponents(layout, tiles, 0, a_ref, bt_ref)
+
+    def step(pair, carry):
+        for tile, ready, upcoming in ((2 * pair, even, odd), (2 * pair + 1, odd, even)):
+            upcoming[...] = tile_exponents(layout, tiles, tile + 1, a_ref, bt_ref)
+            made[tile] = jnp.exp(ready[...]).astype(bf16)
+            send(tile).start()
+        return carry
+
+    lax.fori_loop(0, layout.ahead // 2, step, 0)
+    return [send(tile) for tile in range(layout.ahead)]
+
+
 def list_tiles(count_ref, list_ref, tiles, times):
     every = count_ref.shape[1]
 
@@ -243,9 +275,13 @@
         return filled
 
     filled = lax.fori_loop(0, every, tally, jnp.int32(0))
-    for more in range(2):
-        tiles[0, filled + more] = 0
-        tiles[1, filled + more] = 0
+
+    def pad(more, carry):
+        tiles[0, more] = 0
+        tiles[1, more] = 0
+        return carry
+
+    lax.fori_loop(filled, tiles.shape[1] - 1, pad, 0)
     tiles[0, tiles.shape[1] - 1] = filled
 
 
@@ -255,8 +291,8 @@
     else:
         small_ref = None
     place_refs, refs = refs[: layout.count], refs[layout.count :]
-    tree_ref, a_hbm, base_hbm, sk_ref, upper_tiles_ref, top_ref, slot_ref, info_ref, tiles = refs[:9]
-    masked, low_hot, a_ref, base_ref, sk_t, sk_bt, sems, times = refs[9:]
+    tree_ref, a_hbm, base_hbm, sk_ref, upper_tiles_ref, top_ref, slot_ref, info_ref, tiles, made_hbm = refs[:10]
+    masked, low_hot, a_ref, base_ref, sk_t, sk_bt, sems, times, bt_ref, even, odd, made, made_sems = refs[10:]
     blocks, rows = layout.blocks, layout.rows
 
     def keep(node, found):
@@ -326,6 +362,8 @@
     top_ref[0:64, :] = found[0:64] + found[64:128]
     top_ref[64:72, :] = found[128:136]
     list_tiles(count_ref, list_ref, tiles, times)
+    target_columns(layout, bt_ref, tree_ref)
+    copies += tiles_ahead(layout, tiles, a_ref, bt_ref, even, odd, made, made_hbm, made_sems)
     for copy in copies:
         copy.wait()
 
@@ -371,58 +409,66 @@
         start, count = start + count, count // 2
 
 
-def near_kernel(layout, tiles, a_hbm, tree_ref, w_ref, acc, a_ref, bt_ref, sem, *halves):
-    copy = pltpu.make_async_copy(a_hbm, a_ref, sem)
+def near_kernel(layout, tiles, a_hbm, made_hbm, tree_ref, w_ref, acc, a_ref, bt_ref, made, sems, even, odd, even_tile, odd_tile):
+    ahead, span = layout.ahead, layout.span
+
+    def fetch(tile):
+        return pltpu.make_async_copy(made_hbm.at[tile], made.at[tile], sems.at[tile])
+
+    copy = pltpu.make_async_copy(a_hbm, a_ref, sems.at[ahead])
+    for tile in range(ahead):
+        fetch(tile).start()
     copy.start()
-    span, half = layout.span, LEAF // 2
-    parts = range(span // half)
-    for leaf in range(bt_ref.shape[1] // span):
-        here = aligned(leaf * LEAF + layout.core() * span, span, span)
-        feature_columns(bt_ref, slice(leaf * span, (leaf + 1) * span), tree_ref[:, here])
     filled = tiles[0, tiles.shape[1] - 1]
     acc[...] = jnp.zeros_like(acc)
-
-    def target(tile, part):
-        return aligned(tiles[0, tile] * span + part * half, half, half)
-
-    even, odd = halves[0:2], halves[2:4]
-    even_tile, odd_tile = halves[4:6], halves[6:8]
-
-    def exponents(tile, part):
+    target_columns(layout, bt_ref, tree_ref)
+
+    def exponents(tile):
+        return tile_exponents(layout, tiles, tile, a_ref, bt_ref)
+
+    def add(tile, block):
         source = aligned(tiles[1, tile] * LEAF, LEAF, LEAF)
-        return nn(a_ref[source, :], bt_ref[:, target(tile, part)])
-
-    def add(tile, part, block):
-        source = aligned(tiles[1, tile] * LEAF, LEAF, LEAF)
-        acc[:, target(tile, part)] += tiles[2, tile].astype(f32) * nn(w_ref[:, source], block[part][...])
-
-    def phase(tile, upcoming, ready, made, previous):
-        for part in parts:
-            upcoming[part][...] = exponents(tile + 1, part)
-            made[part][...] = jnp.exp(ready[part][...]).astype(bf16)
-            add(tile - 1, part, previous)
-
+        target = aligned(tiles[0, tile] * span, span, span)
+        acc[:, target] += tiles[2, tile].astype(f32) * nn(w_ref[:, source], block)
+
+    def arrived(quad, carry):
+        for more in range(4):
+            fetch(4 * quad + more).wait()
+            tile = 4 * quad + more
+
+            @pl.when(tile < filled)
+            def _():
+                add(tile, made[tile])
+
+        return carry
+
+    lax.fori_loop(0, ahead // 4, arrived, 0)
     copy.wait()
-    for part in parts:
-        even[part][...] = exponents(0, part)
-        even_tile[part][...] = jnp.exp(even[part][...]).astype(bf16)
-        odd[part][...] = exponents(1, part)
-
-    def step(pair, carry):
-        phase(2 * pair + 1, even, odd, odd_tile, even_tile)
-        phase(2 * pair + 2, odd, even, even_tile, odd_tile)
-        return carry
-
-    lax.fori_loop(0, (filled - 1) // 2, step, 0)
-    done = 2 * ((filled - 1) // 2)
-    for part in parts:
-        add(done, part, even_tile)
-
-    @pl.when(done + 1 < filled)
+
+    @pl.when(filled > ahead)
     def _():
-        for part in parts:
-            odd_tile[part][...] = jnp.exp(odd[part][...]).astype(bf16)
-            add(done + 1, part, odd_tile)
+        even[...] = exponents(ahead)
+        even_tile[...] = jnp.exp(even[...]).astype(bf16)
+        odd[...] = exponents(ahead + 1)
+
+        def phase(tile, upcoming, ready, finished, previous):
+            upcoming[...] = exponents(tile + 1)
+            finished[...] = jnp.exp(ready[...]).astype(bf16)
+            add(tile - 1, previous[...])
+
+        def step(pair, carry):
+            phase(ahead + 2 * pair + 1, even, odd, odd_tile, even_tile)
+            phase(ahead + 2 * pair + 2, odd, even, even_tile, odd_tile)
+            return carry
+
+        pairs = (filled - ahead - 1) // 2
+        lax.fori_loop(0, pairs, step, 0)
+        add(ahead + 2 * pairs, even_tile[...])
+
+        @pl.when(ahead + 2 * pairs + 1 < filled)
+        def _():
+            odd_tile[...] = jnp.exp(odd[...]).astype(bf16)
+            add(ahead + 2 * pairs + 1, odd_tile[...])
 
 
 def far_kernel(layout, low_levels, pack_ref, slot_ref, info_ref, tree_ref, sk_ref, coef_ref, near_ref, *refs):
@@ -456,9 +502,6 @@
             coefs[index, :, at] = coef_ref[:, other]
             node, start, count = node // 2, start + count, count // 2
         for leaf in range(per_block):
-            here = (index * per_block + leaf) * LEAF
-            at = slice(here // layout.halves, here // layout.halves + span)
-            feature_columns(bt_ref, at, tree_ref[:, aligned(here + core * span, span, span)])
             flags = info_ref[index, FLAGS + leaf : FLAGS + leaf + 1, :]
             used = []
             for level in range(levels):
@@ -466,6 +509,8 @@
                 used.append(jnp.broadcast_to(flag, (1, SK)))
             used = jnp.concatenate(used, 1)
             scaled[index * per_block + leaf] = (coefs[index].astype(f32) * used).astype(bf16)
+
+    target_columns(layout, bt_ref, tree_ref)
 
     def exponents(leaf):
         powers[leaf % 2][...] = nn(tops[leaf // per_block], bt_ref[:, leaf * span : (leaf + 1) * span])
@@ -518,6 +563,10 @@
         out_ref[half:, :] = kept_ref[step, half:, :] + got_ref[step, 0:half, :]
 
 
+def far_first(blocks):
+    return sorted(range(blocks), key=lambda step: -(step * 2 // blocks))
+
+
 def final_kernel(blocks, pos_ref, *refs):
     back_refs, (weights_ref, out_ref, perm, vals) = refs[:-4], refs[-4:]
     chunks = pos_ref.shape[0]
@@ -530,7 +579,7 @@
         columns, at = 0, slice(0, rows)
         value = back_ref[...]
         if blocks:
-            columns = (lax.axis_index("sub") ^ (g % blocks)) * width
+            columns = (lax.axis_index("sub") ^ far_first(blocks)[g % blocks]) * width
             at = aligned((lax.axis_index("leaf") ^ lax.axis_index("rep") ^ (g // blocks)) * split, split, split)
             value = value[0:width] if g < blocks else value[width:]
         high, low = two(value)
@@ -635,7 +684,6 @@
         place = [place[step] for step in range(blocks)] + [theirs[step] for step in range(blocks)]
         light = light.reshape(devices, width, part)
         light = lax.all_to_all(light, ("leaf", "sub"), split_axis=0, concat_axis=0, tiled=True)
-        light = [light, other_core(light)]
         small = []
     else:
         info = jnp.pad(far_use.astype(f32), ((FLAGS, 5 - far_use.shape[0]), (0, SK - far_use.shape[1])))
@@ -651,7 +699,7 @@
         light = [light.transpose(1, 2, 0, 3).reshape(1, width, total)]
 
     nodes = 2 * blocks - 1
-    tree, feat_a, base, sk, upper_tiles, top, slots, info, tiles = pl.pallas_call(
+    tree, feat_a, base, sk, upper_tiles, top, slots, info, tiles, made = pl.pallas_call(
         functools.partial(points_kernel, layout, trees),
         out_shape=(
             vm((COORD, total), bf16),
@@ -663,9 +711,10 @@
             vm((blocks, rows), f32),
             vm((blocks, 8, SK), f32),
             pltpu.MemorySpace.HBM((3, leaves * leaves + 3), jnp.int32),
+            pltpu.MemorySpace.HBM((layout.ahead, LEAF, layout.span), bf16),
         ),
         in_specs=[spec(SMEM)] * 2 + [spec()] * (1 + len(small) + layout.count),
-        out_specs=(spec(), spec(pl.ANY), spec(pl.ANY)) + (spec(),) * 5 + (spec(SMEM),),
+        out_specs=(spec(), spec(pl.ANY), spec(pl.ANY)) + (spec(),) * 5 + (spec(SMEM), spec(pl.ANY)),
         scratch_shapes=[
             vm((blocks, rows // LOW * COORD, rows), bf16),
             vm((blocks, rows, LOW), bf16),
@@ -675,11 +724,19 @@
             vm((FEAT, nodes * SK), bf16),
             pltpu.SemaphoreType.DMA((2, blocks)),
             pltpu.SMEM((leaves,), jnp.int32),
+            vm((FEAT, total // layout.halves), bf16),
+            vm((LEAF, layout.span), f32),
+            vm((LEAF, layout.span), f32),
+            vm((layout.ahead, LEAF, layout.span), bf16),
+            pltpu.SemaphoreType.DMA((layout.ahead,)),
         ],
         compiler_params=params(40),
         name="tree_points",
     )(in_hbm(near_count), in_hbm(near_list[0]), in_hbm(skeleton_upper), *small, *place)
 
+    if fine:
+        light, slots = lax.optimization_barrier((light, slots))
+        light = [light, other_core(light)]
     tree_light, coefs, pack = pl.pallas_call(
         functools.partial(weights_kernel, layout),
         out_shape=(
@@ -704,18 +761,19 @@
     near = pl.pallas_call(
         functools.partial(near_kernel, layout),
         out_shape=vm((cols, total // layout.halves), f32),
-        in_specs=[spec(SMEM), spec(pl.ANY)] + [spec()] * 2,
+        in_specs=[spec(SMEM), spec(pl.ANY), spec(pl.ANY)] + [spec()] * 2,
         out_specs=spec(),
         scratch_shapes=[
             vm((total, FEAT), bf16),
             vm((FEAT, total // layout.halves), bf16),
-            pltpu.SemaphoreType.DMA(()),
+            vm((layout.ahead, LEAF, layout.span), bf16),
+            pltpu.SemaphoreType.DMA((layout.ahead + 1,)),
         ]
-        + [vm((LEAF, LEAF // 2), f32)] * 4
-        + [vm((LEAF, LEAF // 2), bf16)] * 4,
+        + [vm((LEAF, layout.span), f32)] * 2
+        + [vm((LEAF, layout.span), bf16)] * 2,
         compiler_params=params(40),
         name="near",
-    )(in_hbm(tiles), in_hbm(feat_a), held(tree), held(tree_light))
+    )(in_hbm(tiles), in_hbm(feat_a), in_hbm(made), held(tree), held(tree_light))
 
     levels = low_levels + ups
     back = pl.pallas_call(
@@ -748,8 +806,7 @@
             compiler_params=params(40),
             name="add_cores",
         )(kept, other_core(sent))
-        back = {step: swap(sums[step], step) for step in reversed(range(blocks))}
-        back = [back[step] for step in range(blocks)]
+        back = [swap(sums[step], step) for step in far_first(blocks)]
         back = back + [other_core(one) for one in back]
     else:
         back = back[0].reshape(cols, blocks, devices, per).transpose(2, 0, 1, 3).reshape(devices, width, part)

time: 84 us -> 76.1 us (0.906)
  blocking collectives: 21.3 us -> 0 us
  waiting for transfers between devices: 10 us -> 23.3 us
  Pallas kernels: 25.6 us -> 29.8 us
  starting transfers between devices: 26.7 us -> 22.7 us
    all_to_all x1 -> x0, blocking collectives: 21.3 us -> none  [body(): lax.all_to_all(light, ('leaf', 'sub'), split_axis=0, concat_axis=0, tiled...]
    ppermute x5, waiting for transfers between devices: 0.01 us -> 10.6 us  [swap(): return lax.ppermute(value, axes, pairs)]
    ppermute x10, starting transfers between devices: 12.9 us -> 4.22 us  [other_core(): return lax.ppermute(value, 'rep', [(0, 1), (1, 0)])]
    all_to_all x0 -> x1, starting transfers between devices: none -> 5.45 us  [body(): lax.all_to_all(light, ('leaf', 'sub'), split_axis=0, concat_axis=0, tiled...]
    pallas_call x1, Pallas kernels: 5.37 us -> 10.7 us  [body(): pl.pallas_call(functools.partial(points_kernel, layout, trees), out_shape...]
    ppermute x10, waiting for transfers between devices: 4.53 us -> 5.86 us  [other_core(): return lax.ppermute(value, 'rep', [(0, 1), (1, 0)])]
    all_to_all x0 -> x1, waiting for transfers between devices: none -> 1.3 us  [body(): lax.all_to_all(light, ('leaf', 'sub'), split_axis=0, concat_axis=0, tiled...]
    pallas_call x1, Pallas kernels: 7.96 us -> 6.85 us  [body(): pl.pallas_call(functools.partial(near_kernel, layout), out_shape=vm((cols...]
  transfers between devices with their start and end apart: 19 -> 20, of which waited for: 9 -> 12; matrix products, arithmetic and copies ran while one was open for 0% -> 0% of each run, Pallas kernels for 19% -> 26%
where the time goes in v14:
time: 76.1 us; the launch traced here: 75.8 us
  Pallas kernels  29.8 us (39%)
  waiting for transfers between devices  23.3 us (31%)
  starting transfers between devices  22.7 us (30%)
    pallas_call x1, Pallas kernels, body(): pl.pallas_call(functools.partial(points_kernel, layout, trees), out_shape...  10.7 us
    ppermute x5, waiting for transfers between devices, swap(): return lax.ppermute(value, axes, pairs)  10.6 us
    pallas_call x1, Pallas kernels, body(): pl.pallas_call(functools.partial(near_kernel, layout), out_shape=vm((cols...  6.85 us
    ppermute x3, starting transfers between devices, body(): lax.ppermute(place[step], 'sub', [(i, i ^ stride) for i in range(blocks)])  6.51 us
    ppermute x10, waiting for transfers between devices, other_core(): return lax.ppermute(value, 'rep', [(0, 1), (1, 0)])  5.86 us
    ppermute x5, starting transfers between devices, swap(): return lax.ppermute(value, axes, pairs)  5.83 us
    ppermute x3, waiting for transfers between devices, body(): lax.ppermute(place[step], 'sub', [(i, i ^ stride) for i in range(blocks)])  5.51 us
    all_to_all x1, starting transfers between devices, body(): lax.all_to_all(light, ('leaf', 'sub'), split_axis=0, concat_axis=0, tiled...  5.45 us
  transfers between devices with their start and end apart: 20, of which 12 were waited for; matrix products, arithmetic and copies ran while one was open for 0% of the time, Pallas kernels for 26%

profile of v14, /device:TPU:0, one launch (start us, length us, event | category | flops | bytes accessed | tf_op | source)
XLA Modules:
  0.0 75.8 jit_solution(728540561420616271)
XLA Ops:
  0.0 2.7 %sort_points.1 = (f32[72,512]{1,0:T(8,128)}, f32[8,128]{1,0:T(8,128)}) custom-call(s32[8,128]{1,0:T(8,128)} %bitcast.8, f32[64,1024]{1,0:T(8,128)} %bitcast.7, s32[1,128]{1,0:T(1,128)} %base_ref.1, s32[2,3]{1,0:T(2,128)} %flag_ref.1), custom_call_target="tpu_custom_call" | custom-call | tf_op jit(solution)/shard_map/sort_points/pallas_call | solution.py:640
  2.7 1.6 %collective-permute-start = (f32[72,512]{1,0:T(8,128)}, f32[72,512]{1,0:T(8,128)S(1)}, u32[]{:S(2)}, u32[]{:S(2)}) collective-permute-start(f32[72,512]{1,0:T(8,128)} %get-tuple-element.34), channel_id=1, source_target_pairs={{0,0},{1,9},{2,2},{3,11},{4,4},{5,13},{6,6},{7,15},{8,8},{9,1},{10... | collective-permute-start | bytes 442376 | tf_op jit(solution)/shard_map/ppermute | solution.py:658
  4.3 4.0 %collective-permute-start.2 = (f32[72,512]{1,0:T(8,128)S(1)}, f32[72,512]{1,0:T(8,128)S(1)}, u32[]{:S(2)}, u32[]{:S(2)}) collective-permute-start(f32[72,512]{1,0:T(8,128)S(1)} %collective-permute-done.refs_0_), channel_id=1, source_target_pairs={{0,4},{2,6},{4,0},{6,2},{1,5},{3,7},{5,1},{7,3},{8,12},{10,14},{12... | collective-permute-start | bytes 442376 | tf_op jit(solution)/shard_map/ppermute | solution.py:679
  8.3 1.6 %collective-permute-start.1 = (f32[72,512]{1,0:T(8,128)S(1)}, f32[72,512]{1,0:T(8,128)S(1)}, u32[]{:S(2)}, u32[]{:S(2)}) collective-permute-start(f32[72,512]{1,0:T(8,128)S(1)} %collective-permute-done.refs_0_), channel_id=1, source_target_pairs={{0,2},{2,0},{4,6},{6,4},{1,3},{3,1},{5,7},{7,5},{8,10},{10,8},{12,... | collective-permute-start | bytes 442376 | tf_op jit(solution)/shard_map/ppermute | solution.py:679
  9.9 3.2 %collective-permute-done.2.refs_2_ = f32[72,512]{1,0:T(8,128)S(1)} collective-permute-done((f32[72,512]{1,0:T(8,128)S(1)}, f32[72,512]{1,0:T(8,128)S(1)}, u32[]{:S(2)}, u32[]{:S(2)}) %collective-permute-start.2) | collective-permute-done | bytes 147488 | tf_op jit(solution)/shard_map/ppermute | solution.py:679
  13.2 0.9 %collective-permute-start.3 = (f32[72,512]{1,0:T(8,128)S(1)}, f32[72,512]{1,0:T(8,128)S(1)}, u32[]{:S(2)}, u32[]{:S(2)}) collective-permute-start(f32[72,512]{1,0:T(8,128)S(1)} %collective-permute-done.2.refs_2_), channel_id=1, source_target_pairs={{0,2},{2,0},{4,6},{6,4},{1,3},{3,1},{5,7},{7,5},{8,10},{10,8},{12,... | collective-permute-start | bytes 442376 | tf_op jit(solution)/shard_map/ppermute | solution.py:679
  14.1 2.6 %sort_weights.1 = f32[2,128,512]{2,1,0:T(8,128)} custom-call(f32[8,128]{1,0:T(8,128)} %get-tuple-element.33.pos_ref, f32[1024,128]{1,0:T(8,128)} %refs_8_.1), custom_call_target="tpu_custom_call" | custom-call | tf_op jit(solution)/shard_map/sort_weights/pallas_call | solution.py:664
  16.6 2.3 %collective-permute-done.3.refs_3_ = f32[72,512]{1,0:T(8,128)S(1)} collective-permute-done((f32[72,512]{1,0:T(8,128)S(1)}, f32[72,512]{1,0:T(8,128)S(1)}, u32[]{:S(2)}, u32[]{:S(2)}) %collective-permute-start.3) | collective-permute-done | bytes 147488 | tf_op jit(solution)/shard_map/ppermute | solution.py:679
  18.9 5.5 %all-to-all-start = ((f32[8,32,512]{2,1,0:T(8,128)}), f32[8,32,512]{2,1,0:T(8,128)S(1)}, u32[]{:S(2)}, u32[]{:S(2)}) async-start(f32[8,32,512]{2,1,0:T(8,128)} %bitcast.6), calls=%async_computation | async-start | bytes 1048576 | tf_op jit(solution)/shard_map/all_to_all | solution.py:686
  24.3 2.0 %collective-permute-start.4 = (f32[72,512]{1,0:T(8,128)S(1)}, f32[72,512]{1,0:T(8,128)S(1)}, u32[]{:S(2)}, u32[]{:S(2)}) collective-permute-start(f32[72,512]{1,0:T(8,128)S(1)} %collective-permute-done.refs_0_), channel_id=1, source_target_pairs={{0,1},{1,0},{2,3},{3,2},{4,5},{5,4},{6,7},{7,6},{8,9},{9,8},{10,11... | collective-permute-start | bytes 442376 | tf_op jit(solution)/shard_map/ppermute | solution.py:661
  28.2 10.7 %tree_points.1 = (bf16[144,4096]{1,0:T(8,128)(2,1)S(1)}, bf16[4096,256]{1,0:T(8,128)(2,1)}, bf16[4,1024,128]{2,1,0:T(8,128)(2,1)}, bf16[896,256]{1,0:T(8,128)(2,...) custom-call(s32[1,8]{1,0:T(1,128)} %count_ref.1, ...), custom_call_target="tpu_custom_call" | custom-call | tf_op jit(solution)/shard_map/tree_points/pallas_call | solution.py:702
  38.9 1.3 %all-to-all-done.refs_0_ = f32[8,32,512]{2,1,0:T(8,128)S(1)} async-done(((f32[8,32,512]{2,1,0:T(8,128)}), f32[8,32,512]{2,1,0:T(8,128)S(1)}, u32[]{:S(2)}, u32[]{:S(2)}) %all-to-all-start) | async-done | bytes 524320 | tf_op jit(solution)/shard_map/all_to_all | solution.py:686
  40.1 0.8 %collective-permute-start.8 = (f32[8,32,512]{2,1,0:T(8,128)S(1)}, f32[8,32,512]{2,1,0:T(8,128)S(1)}, u32[]{:S(2)}, u32[]{:S(2)}) collective-permute-start(f32[8,32,512]{2,1,0:T(8,128)S(1)} %all-to-all-done.refs_0_), channel_id=1, source_target_pairs={{0,1},{1,0},{2,3},{3,2},{4,5},{5,4},{6,7},{7,6},{8,9},{9,8},{10,11... | collective-permute-start | bytes 1572872 | tf_op jit(solution)/shard_map/ppermute | solution.py:661
  41.0 1.5 %collective-permute-done.8.refs_1_ = f32[8,32,512]{2,1,0:T(8,128)S(1)} collective-permute-done((f32[8,32,512]{2,1,0:T(8,128)S(1)}, f32[8,32,512]{2,1,0:T(8,128)S(1)}, u32[]{:S(2)}, u32[]{:S(2)}) %collective-permute-start.8) | collective-permute-done | bytes 524320 | tf_op jit(solution)/shard_map/ppermute | solution.py:661
  42.5 2.8 %tree_weights.1 = (bf16[64,4096]{1,0:T(8,128)(2,1)S(1)}, bf16[128,896]{1,0:T(8,128)(2,1)S(1)}, f32[136,128]{1,0:T(8,128)S(1)}) custom-call(bf16[4,1024,128]{2,1,0:T(8,128)(2,1)} %get-tuple-element.39.base_hbm, f32[3,256,128]{2,1,0:T(8,128)S(1)} %get-tuple-element.40.upper_tiles_ref, f32[72,128]{1,0:T(8,128)S(1)} %get-tuple-element.41.top_ref, ...), custom_call_target="tpu_custom_call" | custom-call | tf_op jit(solution)/shard_map/tree_weights/pallas_call | solution.py:740
  45.9 6.8 %near.1.near_ref = f32[64,2048]{1,0:T(8,128)S(1)} custom-call(s32[3,67]{1,0:T(4,128)} %get-tuple-element.51.tiles, bf16[4096,256]{1,0:T(8,128)(2,1)} %get-tuple-element.52.a_hbm, bf16[24,512,256]{2,1,0:T(8,128)(2,1)} %get-tuple-element.53.made_hbm, bf16[144,4096]{1,0:T(8,128)(2,1)S(1)} %get-tuple-element.48.tree_ref, ...), custom_call_target="tpu_custom_call" | custom-call | tf_op jit(solution)/shard_map/near/pallas_call | solution.py:761
  52.8 2.2 %far.1 = (f32[4,64,512]{2,1,0:T(8,128)S(1)}, f32[4,64,512]{2,1,0:T(8,128)S(1)}) custom-call(f32[1,136,128]{2,1,0:T(8,128)S(1)} %bitcast.5, f32[4,1024]{1,0:T(4,128)S(1)} %get-tuple-element.44.slot_ref, f32[4,8,128]{2,1,0:T(8,128)S(1)} %get-tuple-element.47.info_ref, bf16[144,4096]{1,0:T(8,128)(2,1)S(1)} %get-tuple-element.48.tree_ref, ...), custom_call_target="tpu_custom_call" | custom-call | tf_op jit(solution)/shard_map/far/pallas_call | solution.py:779
  55.1 1.8 %collective-permute-done.10.got_ref = f32[4,64,512]{2,1,0:T(8,128)S(1)} collective-permute-done((f32[4,64,512]{2,1,0:T(8,128)S(1)}, f32[4,64,512]{2,1,0:T(8,128)S(1)}, u32[]{:S(2)}, u32[]{:S(2)}) %collective-permute-start.10) | collective-permute-done | bytes 524320 | tf_op jit(solution)/shard_map/ppermute | solution.py:661
  57.0 1.9 %collective-permute-start.11 = (f32[64,512]{1,0:T(8,128)S(1)}, f32[64,512]{1,0:T(8,128)S(1)}, u32[]{:S(2)}, u32[]{:S(2)}) collective-permute-start(f32[64,512]{1,0:T(8,128)S(1)} %get-tuple-element.57), channel_id=1, source_target_pairs={{0,4},{1,13},{2,6},{3,15},{4,0},{5,9},{6,2},{7,11},{8,12},{9,5},{1... | collective-permute-start | bytes 393224 | tf_op jit(solution)/shard_map/ppermute | solution.py:658
  58.9 1.5 %collective-permute-start.12 = (f32[64,512]{1,0:T(8,128)S(1)}, f32[64,512]{1,0:T(8,128)S(1)}, u32[]{:S(2)}, u32[]{:S(2)}) collective-permute-start(f32[64,512]{1,0:T(8,128)S(1)} %get-tuple-element.58), channel_id=1, source_target_pairs={{0,6},{1,15},{2,4},{3,13},{4,2},{5,11},{6,0},{7,9},{8,14},{9,7},{1... | collective-permute-start | bytes 393224 | tf_op jit(solution)/shard_map/ppermute | solution.py:658
  61.3 8.5 %collective-permute-done.11.refs_0_ = f32[64,512]{1,0:T(8,128)S(1)} collective-permute-done((f32[64,512]{1,0:T(8,128)S(1)}, f32[64,512]{1,0:T(8,128)S(1)}, u32[]{:S(2)}, u32[]{:S(2)}) %collective-permute-start.11) | collective-permute-done | bytes 131104 | tf_op jit(solution)/shard_map/ppermute | solution.py:658
  70.4 2.1 %collective-permute-done.14.refs_3_ = f32[64,512]{1,0:T(8,128)S(1)} collective-permute-done((f32[64,512]{1,0:T(8,128)S(1)}, f32[64,512]{1,0:T(8,128)S(1)}, u32[]{:S(2)}, u32[]{:S(2)}) %collective-permute-start.14) | collective-permute-done | bytes 131104 | tf_op jit(solution)/shard_map/ppermute | solution.py:658
  72.7 1.2 %collective-permute-done.18.refs_7_ = f32[64,512]{1,0:T(8,128)S(1)} collective-permute-done((f32[64,512]{1,0:T(8,128)S(1)}, f32[64,512]{1,0:T(8,128)S(1)}, u32[]{:S(2)}, u32[]{:S(2)}) %collective-permute-start.18) | collective-permute-done | bytes 131104 | tf_op jit(solution)/shard_map/ppermute | solution.py:661
  73.9 1.9 %to_input_order.1 = f32[1024,128]{1,0:T(8,128)} custom-call(f32[8,128]{1,0:T(8,128)S(1)} %copy-done.1, f32[64,512]{1,0:T(8,128)S(1)} %collective-permute-done.11.refs_0_, f32[64,512]{1,0:T(8,128)S(1)} %collective-permute-done.12.refs_1_, f32[64,512]{1,0:T(8,128)S(1)} %collective-permute-done.13.refs_2_, f32[64,512]{1,0:T(8,128)S(1)} %collective-permute-done.14.refs_3_, ...), custom_call_target="tpu_custom_call" | custom-call | tf_op jit(solution)/shard_map/to_input_order/pallas_call | solution.py:816
  (28 shorter events, 4.4 us)
Async XLA Ops:
  2.7 1.6 %collective-permute-start = (f32[72,512]{1,0:T(8,128)}, f32[72,512]{1,0:T(8,128)S(1)}, u32[]{:S(2)}, u32[]{:S(2)}) collective-permute-start(f32[72,512]{1,0:T(8,128)} %get-tuple-element.34), channel_id=1, source_target_pairs={{0,0},{1,9},{2,2},{3,11},{4,4},{5,13},{6,6},{7,15},{8,8},{9,1},{10... | collective-permute-start | bytes 442376 | tf_op jit(solution)/shard_map/ppermute | solution.py:658
  4.3 8.8 %collective-permute-start.2 = (f32[72,512]{1,0:T(8,128)S(1)}, f32[72,512]{1,0:T(8,128)S(1)}, u32[]{:S(2)}, u32[]{:S(2)}) collective-permute-start(f32[72,512]{1,0:T(8,128)S(1)} %collective-permute-done.refs_0_), channel_id=1, source_target_pairs={{0,4},{2,6},{4,0},{6,2},{1,5},{3,7},{5,1},{7,3},{8,12},{10,14},{12... | collective-permute-start | bytes 442376 | tf_op jit(solution)/shard_map/ppermute | solution.py:679
  8.3 8.3 %collective-permute-start.1 = (f32[72,512]{1,0:T(8,128)S(1)}, f32[72,512]{1,0:T(8,128)S(1)}, u32[]{:S(2)}, u32[]{:S(2)}) collective-permute-start(f32[72,512]{1,0:T(8,128)S(1)} %collective-permute-done.refs_0_), channel_id=1, source_target_pairs={{0,2},{2,0},{4,6},{6,4},{1,3},{3,1},{5,7},{7,5},{8,10},{10,8},{12,... | collective-permute-start | bytes 442376 | tf_op jit(solution)/shard_map/ppermute | solution.py:679
  13.2 5.7 %collective-permute-start.3 = (f32[72,512]{1,0:T(8,128)S(1)}, f32[72,512]{1,0:T(8,128)S(1)}, u32[]{:S(2)}, u32[]{:S(2)}) collective-permute-start(f32[72,512]{1,0:T(8,128)S(1)} %collective-permute-done.2.refs_2_), channel_id=1, source_target_pairs={{0,2},{2,0},{4,6},{6,4},{1,3},{3,1},{5,7},{7,5},{8,10},{10,8},{12,... | collective-permute-start | bytes 442376 | tf_op jit(solution)/shard_map/ppermute | solution.py:679
  18.9 21.3 %all-to-all-start = ((f32[8,32,512]{2,1,0:T(8,128)}), f32[8,32,512]{2,1,0:T(8,128)S(1)}, u32[]{:S(2)}, u32[]{:S(2)}) async-start(f32[8,32,512]{2,1,0:T(8,128)} %bitcast.6), calls=%async_computation | async-start | bytes 1048576 | tf_op jit(solution)/shard_map/all_to_all | solution.py:686
  24.3 3.0 %collective-permute-start.4 = (f32[72,512]{1,0:T(8,128)S(1)}, f32[72,512]{1,0:T(8,128)S(1)}, u32[]{:S(2)}, u32[]{:S(2)}) collective-permute-start(f32[72,512]{1,0:T(8,128)S(1)} %collective-permute-done.refs_0_), channel_id=1, source_target_pairs={{0,1},{1,0},{2,3},{3,2},{4,5},{5,4},{6,7},{7,6},{8,9},{9,8},{10,11... | collective-permute-start | bytes 442376 | tf_op jit(solution)/shard_map/ppermute | solution.py:661
  26.3 1.4 %collective-permute-start.5 = (f32[72,512]{1,0:T(8,128)S(1)}, f32[72,512]{1,0:T(8,128)S(1)}, u32[]{:S(2)}, u32[]{:S(2)}) collective-permute-start(f32[72,512]{1,0:T(8,128)S(1)} %collective-permute-done.1.refs_1_), channel_id=1, source_target_pairs={{0,1},{1,0},{2,3},{3,2},{4,5},{5,4},{6,7},{7,6},{8,9},{9,8},{10,11... | collective-permute-start | bytes 442376 | tf_op jit(solution)/shard_map/ppermute | solution.py:661
  26.4 1.5 %collective-permute-start.6 = (f32[72,512]{1,0:T(8,128)S(1)}, f32[72,512]{1,0:T(8,128)S(1)}, u32[]{:S(2)}, u32[]{:S(2)}) collective-permute-start(f32[72,512]{1,0:T(8,128)S(1)} %collective-permute-done.2.refs_2_), channel_id=1, source_target_pairs={{0,1},{1,0},{2,3},{3,2},{4,5},{5,4},{6,7},{7,6},{8,9},{9,8},{10,11... | collective-permute-start | bytes 442376 | tf_op jit(solution)/shard_map/ppermute | solution.py:661
  26.8 1.4 %collective-permute-start.7 = (f32[72,512]{1,0:T(8,128)S(1)}, f32[72,512]{1,0:T(8,128)S(1)}, u32[]{:S(2)}, u32[]{:S(2)}) collective-permute-start(f32[72,512]{1,0:T(8,128)S(1)} %collective-permute-done.3.refs_3_), channel_id=1, source_target_pairs={{0,1},{1,0},{2,3},{3,2},{4,5},{5,4},{6,7},{7,6},{8,9},{9,8},{10,11... | collective-permute-start | bytes 442376 | tf_op jit(solution)/shard_map/ppermute | solution.py:661
  40.1 2.3 %collective-permute-start.8 = (f32[8,32,512]{2,1,0:T(8,128)S(1)}, f32[8,32,512]{2,1,0:T(8,128)S(1)}, u32[]{:S(2)}, u32[]{:S(2)}) collective-permute-start(f32[8,32,512]{2,1,0:T(8,128)S(1)} %all-to-all-done.refs_0_), channel_id=1, source_target_pairs={{0,1},{1,0},{2,3},{3,2},{4,5},{5,4},{6,7},{7,6},{8,9},{9,8},{10,11... | collective-permute-start | bytes 1572872 | tf_op jit(solution)/shard_map/ppermute | solution.py:661
  45.3 7.5 %collective-permute-start.9 = (f32[136,128]{1,0:T(8,128)S(1)}, f32[136,128]{1,0:T(8,128)S(1)}, u32[]{:S(2)}, u32[]{:S(2)}) collective-permute-start(f32[136,128]{1,0:T(8,128)S(1)} %get-tuple-element.46), channel_id=1, source_target_pairs={{0,8},{8,0},{1,9},{9,1},{2,10},{10,2},{3,11},{11,3},{4,12},{12,4},... | collective-permute-start | bytes 208904 | tf_op jit(solution)/shard_map/ppermute | solution.py:604
  52.8 21.1 %copy-start = (f32[1024,128]{1,0:T(8,128)S(1)}, f32[1024,128]{1,0:T(8,128)}, u32[]{:S(2)}) copy-start(f32[1024,128]{1,0:T(8,128)} %refs_8_.1) | copy-start | bytes 1572868
  52.8 21.1 %copy-start.1 = (f32[8,128]{1,0:T(8,128)S(1)}, f32[8,128]{1,0:T(8,128)}, u32[]{:S(2)}) copy-start(f32[8,128]{1,0:T(8,128)} %get-tuple-element.33.pos_ref) | copy-start | bytes 12292
  55.0 2.0 %collective-permute-start.10 = (f32[4,64,512]{2,1,0:T(8,128)S(1)}, f32[4,64,512]{2,1,0:T(8,128)S(1)}, u32[]{:S(2)}, u32[]{:S(2)}) collective-permute-start(f32[4,64,512]{2,1,0:T(8,128)S(1)} %get-tuple-element.56), channel_id=1, source_target_pairs={{0,1},{1,0},{2,3},{3,2},{4,5},{5,4},{6,7},{7,6},{8,9},{9,8},{10,11... | collective-permute-start | bytes 1572872 | tf_op jit(solution)/shard_map/ppermute | solution.py:661
  57.0 12.8 %collective-permute-start.11 = (f32[64,512]{1,0:T(8,128)S(1)}, f32[64,512]{1,0:T(8,128)S(1)}, u32[]{:S(2)}, u32[]{:S(2)}) collective-permute-start(f32[64,512]{1,0:T(8,128)S(1)} %get-tuple-element.57), channel_id=1, source_target_pairs={{0,4},{1,13},{2,6},{3,15},{4,0},{5,9},{6,2},{7,11},{8,12},{9,5},{1... | collective-permute-start | bytes 393224 | tf_op jit(solution)/shard_map/ppermute | solution.py:658
  58.9 10.9 %collective-permute-start.12 = (f32[64,512]{1,0:T(8,128)S(1)}, f32[64,512]{1,0:T(8,128)S(1)}, u32[]{:S(2)}, u32[]{:S(2)}) collective-permute-start(f32[64,512]{1,0:T(8,128)S(1)} %get-tuple-element.58), channel_id=1, source_target_pairs={{0,6},{1,15},{2,4},{3,13},{4,2},{5,11},{6,0},{7,9},{8,14},{9,7},{1... | collective-permute-start | bytes 393224 | tf_op jit(solution)/shard_map/ppermute | solution.py:658
  60.4 10.0 %collective-permute-start.13 = (f32[64,512]{1,0:T(8,128)S(1)}, f32[64,512]{1,0:T(8,128)S(1)}, u32[]{:S(2)}, u32[]{:S(2)}) collective-permute-start(f32[64,512]{1,0:T(8,128)S(1)} %get-tuple-element.59), channel_id=1, source_target_pairs={{0,0},{1,9},{2,2},{3,11},{4,4},{5,13},{6,6},{7,15},{8,8},{9,1},{10... | collective-permute-start | bytes 393224 | tf_op jit(solution)/shard_map/ppermute | solution.py:658
  61.1 11.5 %collective-permute-start.14 = (f32[64,512]{1,0:T(8,128)S(1)}, f32[64,512]{1,0:T(8,128)S(1)}, u32[]{:S(2)}, u32[]{:S(2)}) collective-permute-start(f32[64,512]{1,0:T(8,128)S(1)} %get-tuple-element.60), channel_id=1, source_target_pairs={{0,2},{1,11},{2,0},{3,9},{4,6},{5,15},{6,4},{7,13},{8,10},{9,3},{1... | collective-permute-start | bytes 393224 | tf_op jit(solution)/shard_map/ppermute | solution.py:658
  69.8 2.8 %collective-permute-start.15 = (f32[64,512]{1,0:T(8,128)S(1)}, f32[64,512]{1,0:T(8,128)S(1)}, u32[]{:S(2)}, u32[]{:S(2)}) collective-permute-start(f32[64,512]{1,0:T(8,128)S(1)} %collective-permute-done.11.refs_0_), channel_id=1, source_target_pairs={{0,1},{1,0},{2,3},{3,2},{4,5},{5,4},{6,7},{7,6},{8,9},{9,8},{10,11... | collective-permute-start | bytes 393224 | tf_op jit(solution)/shard_map/ppermute | solution.py:661
  69.9 2.8 %collective-permute-start.16 = (f32[64,512]{1,0:T(8,128)S(1)}, f32[64,512]{1,0:T(8,128)S(1)}, u32[]{:S(2)}, u32[]{:S(2)}) collective-permute-start(f32[64,512]{1,0:T(8,128)S(1)} %collective-permute-done.12.refs_1_), channel_id=1, source_target_pairs={{0,1},{1,0},{2,3},{3,2},{4,5},{5,4},{6,7},{7,6},{8,9},{9,8},{10,11... | collective-permute-start | bytes 393224 | tf_op jit(solution)/shard_map/ppermute | solution.py:661
  70.4 2.3 %collective-permute-start.17 = (f32[64,512]{1,0:T(8,128)S(1)}, f32[64,512]{1,0:T(8,128)S(1)}, u32[]{:S(2)}, u32[]{:S(2)}) collective-permute-start(f32[64,512]{1,0:T(8,128)S(1)} %collective-permute-done.13.refs_2_), channel_id=1, source_target_pairs={{0,1},{1,0},{2,3},{3,2},{4,5},{5,4},{6,7},{7,6},{8,9},{9,8},{10,11... | collective-permute-start | bytes 393224 | tf_op jit(solution)/shard_map/ppermute | solution.py:661
  72.5 1.3 %collective-permute-start.18 = (f32[64,512]{1,0:T(8,128)S(1)}, f32[64,512]{1,0:T(8,128)S(1)}, u32[]{:S(2)}, u32[]{:S(2)}) collective-permute-start(f32[64,512]{1,0:T(8,128)S(1)} %collective-permute-done.14.refs_3_), channel_id=1, source_target_pairs={{0,1},{1,0},{2,3},{3,2},{4,5},{5,4},{6,7},{7,6},{8,9},{9,8},{10,11... | collective-permute-start | bytes 393224 | tf_op jit(solution)/shard_map/ppermute | solution.py:661

commit v15 on v14

--- a/solution.py
+++ b/solution.py
@@ -13,7 +13,7 @@
 LANES = 128
 FEAT = 256
 LOW = 256
-AHEAD = 24
+AHEAD = 8
 COORD = 144
 
 highest = lax.Precision.HIGHEST
@@ -148,19 +148,38 @@
         place_ref[TAIL + FLAGS : TAIL + FLAGS + flag_ref.shape[0], 0 : flag_ref.shape[1]] = flag_ref[...].astype(f32)
 
 
-def light_kernel(pos_ref, weights_ref, light_ref, masked, low_hot):
-    chunks, split = pos_ref.shape[0], light_ref.shape[2]
+def light_kernel(blocks, pos_ref, weights_ref, *refs):
+    light_refs, (masked, low_hot, placed) = refs[:-3], refs[-3:]
+    chunks = pos_ref.shape[0]
+    high_count = chunks * LANES // LOW
     low_part, high_part = parts_of(lanes_of([pos_ref[c : c + 1, :] for c in range(chunks)]))
     low_by_column(low_hot, low_part.astype(f32))
     for c in range(chunks):
         at = slice(c * LANES, (c + 1) * LANES)
         turned = jnp.transpose(weights_ref[at, :])
-        for h in range(chunks * LANES // LOW):
+        for h in range(high_count):
             masked[h * LANES : (h + 1) * LANES, at] = jnp.where(high_part[:, at] == h, turned, 0.0).astype(bf16)
-    placed = nn(masked[...], low_hot[...])
-    for h in range(chunks * LANES // LOW):
-        at = h * LOW
-        light_ref[at // split, :, at % split : at % split + LOW] = placed[h * LANES : (h + 1) * LANES]
+    moved = nn(masked[...], low_hot[...])
+    for h in range(high_count):
+        if not blocks:
+            light_refs[0][:, h * LOW : (h + 1) * LOW] = moved[h * LANES : (h + 1) * LANES]
+        placed[h] = moved[h * LANES : (h + 1) * LANES]
+    if not blocks:
+        return
+    width, parts = LANES // blocks, high_count // 2
+    for other, light_ref in enumerate(light_refs):
+        first = (lax.axis_index("leaf") ^ lax.axis_index("rep") ^ other) * parts
+        for step in range(blocks):
+            columns = aligned((lax.axis_index("sub") ^ step) * width, width, width)
+            for h in range(parts):
+                light_ref[step, :, h * LOW : (h + 1) * LOW] = placed[first + h, columns, :]
+
+
+def join_kernel(kept_ref, got_ref, *out_refs):
+    half = kept_ref.shape[1]
+    for step, out_ref in enumerate(out_refs):
+        out_ref[0:half, :] = kept_ref[step]
+        out_ref[half:, :] = got_ref[step]
 
 
 class Layout:
@@ -178,11 +197,10 @@
     def lanes(self, index):
         return slice(index * self.per, (index + 1) * self.per)
 
-    def message(self, group):
-        if not self.fine:
-            return 0
-        leaf = lax.axis_index("leaf") ^ lax.axis_index("rep") ^ (group // self.blocks)
-        return leaf * self.blocks + (lax.axis_index("sub") ^ (group % self.blocks))
+    def columns(self, group, half, each):
+        if self.fine and group >= self.blocks:
+            half = 1 - half
+        return slice(half * each, (half + 1) * each)
 
     def gather(self, refs, index, part):
         return lanes_of([ref[part, self.lanes(index)] for ref in refs])
@@ -369,11 +387,15 @@
 
 
 def weights_kernel(layout, base_hbm, upper_tiles_ref, top_ref, slot_ref, *refs):
-    light_refs, refs = refs[: layout.halves], refs[layout.halves :]
+    light_refs, refs = refs[: layout.count], refs[layout.count :]
+    if layout.fine:
+        order = far_first(layout.blocks)
+        order = order + [layout.blocks + step for step in order]
+        light_refs = [light_refs[order.index(g)] for g in range(layout.count)]
     w_ref, coef_ref, pack_ref, masked, low_hot, base_ref, sems = refs
     blocks, rows = layout.blocks, layout.rows
-    each = light_refs[0].shape[1]
-    width = each * layout.halves
+    width = light_refs[0].shape[0]
+    each = width // layout.halves
     pack_ref[0:PLACE_ROWS, :] = top_ref[...]
     for index in range(blocks):
         pltpu.make_async_copy(base_hbm.at[index], base_ref.at[index], sems.at[index]).start()
@@ -385,8 +407,9 @@
     for index in range(blocks):
         low_part, high_part = parts_of(slot_ref[index : index + 1, :])
         low_by_column(low_hot.at[index], low_part.astype(f32))
-        for half, light_ref in enumerate(light_refs):
-            light = lanes_of([light_ref[layout.message(g), :, layout.lanes(index)] for g in range(layout.count)])
+        for half in range(layout.halves):
+            light = [ref[layout.columns(g, half, each), layout.lanes(index)] for g, ref in enumerate(light_refs)]
+            light = lanes_of(light)
             for h in range(rows // LOW):
                 at = h * width + half * each
                 masked[index, at : at + each, :] = jnp.where(high_part == h, light, 0.0).astype(bf16)
@@ -416,9 +439,9 @@
         return pltpu.make_async_copy(made_hbm.at[tile], made.at[tile], sems.at[tile])
 
     copy = pltpu.make_async_copy(a_hbm, a_ref, sems.at[ahead])
+    copy.start()
     for tile in range(ahead):
         fetch(tile).start()
-    copy.start()
     filled = tiles[0, tiles.shape[1] - 1]
     acc[...] = jnp.zeros_like(acc)
     target_columns(layout, bt_ref, tree_ref)
@@ -431,18 +454,6 @@
         target = aligned(tiles[0, tile] * span, span, span)
         acc[:, target] += tiles[2, tile].astype(f32) * nn(w_ref[:, source], block)
 
-    def arrived(quad, carry):
-        for more in range(4):
-            fetch(4 * quad + more).wait()
-            tile = 4 * quad + more
-
-            @pl.when(tile < filled)
-            def _():
-                add(tile, made[tile])
-
-        return carry
-
-    lax.fori_loop(0, ahead // 4, arrived, 0)
     copy.wait()
 
     @pl.when(filled > ahead)
@@ -469,6 +480,19 @@
         def _():
             odd_tile[...] = jnp.exp(odd[...]).astype(bf16)
             add(ahead + 2 * pairs + 1, odd_tile[...])
+
+    def arrived(quad, carry):
+        for more in range(4):
+            fetch(4 * quad + more).wait()
+            tile = 4 * quad + more
+
+            @pl.when(tile < filled)
+            def _():
+                add(tile, made[tile])
+
+        return carry
+
+    lax.fori_loop(0, ahead // 4, arrived, 0)
 
 
 def far_kernel(layout, low_levels, pack_ref, slot_ref, info_ref, tree_ref, sk_ref, coef_ref, near_ref, *refs):
@@ -661,15 +685,23 @@
         return lax.ppermute(value, "rep", [(0, 1), (1, 0)])
 
     def sorted_light():
+        if fine:
+            shapes = (shaped((blocks, width, part), f32),) * 2
+        else:
+            shapes = (shaped((columns, rows), f32),)
         return pl.pallas_call(
-            light_kernel,
-            out_shape=shaped((rows // split, columns, split), f32),
+            functools.partial(light_kernel, blocks if fine else 0),
+            out_shape=shapes,
             in_specs=[spec()] * 2,
-            out_specs=spec(),
-            scratch_shapes=[vm((rows // LOW * LANES, rows), bf16), vm((rows, LOW), bf16)],
-            compiler_params=params(),
+            out_specs=(spec(),) * len(shapes),
+            scratch_shapes=[
+                vm((rows // LOW * LANES, rows), bf16),
+                vm((rows, LOW), bf16),
+                vm((rows // LOW, LANES, LOW), f32),
+            ],
+            compiler_params=params(40),
             name="sort_weights",
-        )(pos, weights)
+        )(in_hbm(pos), in_hbm(weights))
 
     if fine:
         place = {0: swap(place, 0)}
@@ -678,12 +710,19 @@
             for step in sorted(place):
                 place[step | stride] = lax.ppermute(place[step], "sub", [(i, i ^ stride) for i in range(blocks)])
             stride //= 2
-        light = sorted_light()
+        kept, sent = sorted_light()
+        light = pl.pallas_call(
+            join_kernel,
+            out_shape=(shaped((cols, part), f32),) * blocks,
+            in_specs=[spec()] * 2,
+            out_specs=(spec(),) * blocks,
+            compiler_params=params(40),
+            name="join_cores",
+        )(kept, other_core(sent))
         place, light = lax.optimization_barrier((place, light))
         theirs = {step: other_core(one) for step, one in place.items()}
         place = [place[step] for step in range(blocks)] + [theirs[step] for step in range(blocks)]
-        light = light.reshape(devices, width, part)
-        light = lax.all_to_all(light, ("leaf", "sub"), split_axis=0, concat_axis=0, tiled=True)
+        light = [swap(light[step], step) for step in far_first(blocks)]
         small = []
     else:
         info = jnp.pad(far_use.astype(f32), ((FLAGS, 5 - far_use.shape[0]), (0, SK - far_use.shape[1])))
@@ -693,10 +732,10 @@
         place = lax.all_gather(place, "sub", axis=0, tiled=False)
         place = place.transpose(1, 0, 2, 3).reshape(devices, PLACE_ROWS, blocks, per)
         place = [place.transpose(1, 2, 0, 3).reshape(PLACE_ROWS, total)]
-        light = sorted_light().reshape(columns, trees, part).transpose(1, 0, 2).reshape(devices, width, part)
+        light = sorted_light()[0].reshape(columns, trees, part).transpose(1, 0, 2).reshape(devices, width, part)
         light = lax.all_to_all(light, ("leaf", "sub"), split_axis=0, concat_axis=0, tiled=True)
         light = light.reshape(devices, width, blocks, per)
-        light = [light.transpose(1, 2, 0, 3).reshape(1, width, total)]
+        light = [light.transpose(1, 2, 0, 3).reshape(width, total)]
 
     nodes = 2 * blocks - 1
     tree, feat_a, base, sk, upper_tiles, top, slots, info, tiles, made = pl.pallas_call(
@@ -736,7 +775,7 @@
 
     if fine:
         light, slots = lax.optimization_barrier((light, slots))
-        light = [light, other_core(light)]
+        light = light + [other_core(one) for one in light]
     tree_light, coefs, pack = pl.pallas_call(
         functools.partial(weights_kernel, layout),
         out_shape=(
@@ -744,7 +783,7 @@
             vm((2 * cols, nodes * SK), bf16),
             shaped((PLACE_ROWS + cols, SK), f32),
         ),
-        in_specs=[spec(pl.ANY)] + [spec()] * (3 + layout.halves),
+        in_specs=[spec(pl.ANY)] + [spec()] * (3 + layout.count),
         out_specs=(spec(),) * 3,
         scratch_shapes=[
             vm((blocks, rows // LOW * cols, rows), bf16),

time: 76.1 us -> 76.9 us (1.011)
  starting transfers between devices: 22.7 us -> 25.9 us
  Pallas kernels: 29.8 us -> 27.2 us
    ppermute x5 -> x9, starting transfers between devices: 5.83 us -> 11.4 us  [swap(): return lax.ppermute(value, axes, pairs)]
    all_to_all x1 -> x0, starting transfers between devices: 5.45 us -> none  [body(): lax.all_to_all(light, ('leaf', 'sub'), split_axis=0, concat_axis=0, tiled...]
    ppermute x10 -> x14, starting transfers between devices: 4.22 us -> 7.28 us  [other_core(): return lax.ppermute(value, 'rep', [(0, 1), (1, 0)])]
    pallas_call x1, Pallas kernels: 10.7 us -> 8.06 us  [body(): pl.pallas_call(functools.partial(points_kernel, layout, trees), out_shape...]
    ppermute x5 -> x9, waiting for transfers between devices: 10.6 us -> 12.3 us  [swap(): return lax.ppermute(value, axes, pairs)]
    ppermute x10 -> x14, waiting for transfers between devices: 5.86 us -> 4.25 us  [other_core(): return lax.ppermute(value, 'rep', [(0, 1), (1, 0)])]
    ppermute x3, waiting for transfers between devices: 5.51 us -> 6.92 us  [body(): lax.ppermute(place[step], 'sub', [(i, i ^ stride) for i in range(blocks)])]
    all_to_all x1 -> x0, waiting for transfers between devices: 1.3 us -> none  [body(): lax.all_to_all(light, ('leaf', 'sub'), split_axis=0, concat_axis=0, tiled...]
  transfers between devices with their start and end apart: 20 -> 27, of which waited for: 12 -> 12; matrix products, arithmetic and copies ran while one was open for 0% -> 0% of each run, Pallas kernels for 26% -> 23%
where the time goes in v15:
time: 76.9 us; the launch traced here: 76.8 us
  Pallas kernels  27.2 us (35%)
  starting transfers between devices  25.9 us (34%)
  waiting for transfers between devices  23.4 us (30%)
    ppermute x9, waiting for transfers between devices, swap(): return lax.ppermute(value, axes, pairs)  12.3 us
    ppermute x9, starting transfers between devices, swap(): return lax.ppermute(value, axes, pairs)  11.4 us
    pallas_call x1, Pallas kernels, body(): pl.pallas_call(functools.partial(points_kernel, layout, trees), out_shape...  8.06 us
    pallas_call x1, Pallas kernels, body(): pl.pallas_call(functools.partial(near_kernel, layout), out_shape=vm((cols...  7.54 us
    ppermute x14, starting transfers between devices, other_core(): return lax.ppermute(value, 'rep', [(0, 1), (1, 0)])  7.28 us
    ppermute x3, waiting for transfers between devices, body(): lax.ppermute(place[step], 'sub', [(i, i ^ stride) for i in range(blocks)])  6.92 us
    ppermute x3, starting transfers between devices, body(): lax.ppermute(place[step], 'sub', [(i, i ^ stride) for i in range(blocks)])  6.06 us
    ppermute x14, waiting for transfers between devices, other_core(): return lax.ppermute(value, 'rep', [(0, 1), (1, 0)])  4.25 us
  transfers between devices with their start and end apart: 27, of which 12 were waited for; matrix products, arithmetic and copies ran while one was open for 0% of the time, Pallas kernels for 23%

profile of v15, /device:TPU:0, one launch (start us, length us, event | category | flops | bytes accessed | tf_op | source)
XLA Modules:
  0.0 76.8 jit_solution(4241139755368405523)
XLA Ops:
  0.0 2.7 %sort_points.1 = (f32[72,512]{1,0:T(8,128)}, f32[8,128]{1,0:T(8,128)}) custom-call(s32[8,128]{1,0:T(8,128)} %bitcast.6, f32[64,1024]{1,0:T(8,128)} %bitcast.5, s32[1,128]{1,0:T(1,128)} %base_ref.1, s32[2,3]{1,0:T(2,128)} %flag_ref.1), custom_call_target="tpu_custom_call" | custom-call | tf_op jit(solution)/shard_map/sort_points/pallas_call | solution.py:664
  2.7 1.6 %collective-permute-start = (f32[72,512]{1,0:T(8,128)}, f32[72,512]{1,0:T(8,128)S(1)}, u32[]{:S(2)}, u32[]{:S(2)}) collective-permute-start(f32[72,512]{1,0:T(8,128)} %get-tuple-element.46), channel_id=1, source_target_pairs={{0,0},{1,9},{2,2},{3,11},{4,4},{5,13},{6,6},{7,15},{8,8},{9,1},{10... | collective-permute-start | bytes 442376 | tf_op jit(solution)/shard_map/ppermute | solution.py:682
  4.3 4.0 %collective-permute-start.2 = (f32[72,512]{1,0:T(8,128)S(1)}, f32[72,512]{1,0:T(8,128)S(1)}, u32[]{:S(2)}, u32[]{:S(2)}) collective-permute-start(f32[72,512]{1,0:T(8,128)S(1)} %collective-permute-done.refs_0_), channel_id=1, source_target_pairs={{0,4},{2,6},{4,0},{6,2},{1,5},{3,7},{5,1},{7,3},{8,12},{10,14},{12... | collective-permute-start | bytes 442376 | tf_op jit(solution)/shard_map/ppermute | solution.py:711
  8.3 1.8 %sort_weights.1 = (f32[4,32,512]{2,1,0:T(8,128)S(1)}, f32[4,32,512]{2,1,0:T(8,128)S(1)}) custom-call(f32[8,128]{1,0:T(8,128)} %get-tuple-element.45.pos_ref, f32[1024,128]{1,0:T(8,128)} %refs_8_.1), custom_call_target="tpu_custom_call" | custom-call | tf_op jit(solution)/shard_map/sort_weights/pallas_call | solution.py:692
  10.1 4.4 %collective-permute-start.4 = (f32[4,32,512]{2,1,0:T(8,128)S(1)}, f32[4,32,512]{2,1,0:T(8,128)S(1)}, u32[]{:S(2)}, u32[]{:S(2)}) collective-permute-start(f32[4,32,512]{2,1,0:T(8,128)S(1)} %get-tuple-element.48), channel_id=1, source_target_pairs={{0,1},{1,0},{2,3},{3,2},{4,5},{5,4},{6,7},{7,6},{8,9},{9,8},{10,11... | collective-permute-start | bytes 786440 | tf_op jit(solution)/shard_map/ppermute | solution.py:685
  14.6 1.6 %collective-permute-start.1 = (f32[72,512]{1,0:T(8,128)S(1)}, f32[72,512]{1,0:T(8,128)S(1)}, u32[]{:S(2)}, u32[]{:S(2)}) collective-permute-start(f32[72,512]{1,0:T(8,128)S(1)} %collective-permute-done.refs_0_), channel_id=1, source_target_pairs={{0,2},{2,0},{4,6},{6,4},{1,3},{3,1},{5,7},{7,5},{8,10},{10,8},{12,... | collective-permute-start | bytes 442376 | tf_op jit(solution)/shard_map/ppermute | solution.py:711
  16.7 4.6 %collective-permute-done.1.refs_1_ = f32[72,512]{1,0:T(8,128)S(1)} collective-permute-done((f32[72,512]{1,0:T(8,128)S(1)}, f32[72,512]{1,0:T(8,128)S(1)}, u32[]{:S(2)}, u32[]{:S(2)}) %collective-permute-start.1) | collective-permute-done | bytes 147488 | tf_op jit(solution)/shard_map/ppermute | solution.py:711
  21.3 2.3 %collective-permute-done.3.refs_3_ = f32[72,512]{1,0:T(8,128)S(1)} collective-permute-done((f32[72,512]{1,0:T(8,128)S(1)}, f32[72,512]{1,0:T(8,128)S(1)}, u32[]{:S(2)}, u32[]{:S(2)}) %collective-permute-start.3) | collective-permute-done | bytes 147488 | tf_op jit(solution)/shard_map/ppermute | solution.py:711
  24.6 0.9 %collective-permute-start.9 = (f32[64,512]{1,0:T(8,128)S(1)}, f32[64,512]{1,0:T(8,128)S(1)}, u32[]{:S(2)}, u32[]{:S(2)}) collective-permute-start(f32[64,512]{1,0:T(8,128)S(1)} %get-tuple-element.60), channel_id=1, source_target_pairs={{0,4},{1,13},{2,6},{3,15},{4,0},{5,9},{6,2},{7,11},{8,12},{9,5},{1... | collective-permute-start | bytes 393224 | tf_op jit(solution)/shard_map/ppermute | solution.py:682
  25.5 3.0 %collective-permute-start.10 = (f32[64,512]{1,0:T(8,128)S(1)}, f32[64,512]{1,0:T(8,128)S(1)}, u32[]{:S(2)}, u32[]{:S(2)}) collective-permute-start(f32[64,512]{1,0:T(8,128)S(1)} %get-tuple-element.61), channel_id=1, source_target_pairs={{0,6},{1,15},{2,4},{3,13},{4,2},{5,11},{6,0},{7,9},{8,14},{9,7},{1... | collective-permute-start | bytes 393224 | tf_op jit(solution)/shard_map/ppermute | solution.py:682
  28.5 0.7 collective-permute-start.11
  29.3 8.1 %tree_points.1 = (bf16[144,4096]{1,0:T(8,128)(2,1)S(1)}, bf16[4096,256]{1,0:T(8,128)(2,1)}, bf16[4,1024,128]{2,1,0:T(8,128)(2,1)}, bf16[896,256]{1,0:T(8,128)(2,...) custom-call(s32[1,8]{1,0:T(1,128)} %count_ref.1, ...), custom_call_target="tpu_custom_call" | custom-call | tf_op jit(solution)/shard_map/tree_points/pallas_call | solution.py:741
  37.6 2.4 %collective-permute-done.12.refs_3_ = f32[64,512]{1,0:T(8,128)S(1)} collective-permute-done((f32[64,512]{1,0:T(8,128)S(1)}, f32[64,512]{1,0:T(8,128)S(1)}, u32[]{:S(2)}, u32[]{:S(2)}) %collective-permute-start.12) | collective-permute-done | bytes 131104 | tf_op jit(solution)/shard_map/ppermute | solution.py:682
  42.1 2.9 %tree_weights.1 = (bf16[64,4096]{1,0:T(8,128)(2,1)S(1)}, bf16[128,896]{1,0:T(8,128)(2,1)S(1)}, f32[136,128]{1,0:T(8,128)S(1)}) custom-call(bf16[4,1024,128]{2,1,0:T(8,128)(2,1)} %get-tuple-element.57.base_hbm, f32[3,256,128]{2,1,0:T(8,128)S(1)} %get-tuple-element.58.upper_tiles_ref, f32[72,128]{1,0:T(8,128)S(1)} %get-tuple-element.59.top_ref, ...), custom_call_target="tpu_custom_call" | custom-call | tf_op jit(solution)/shard_map/tree_weights/pallas_call | solution.py:779
  45.0 1.2 %collective-permute-start.17 = (f32[136,128]{1,0:T(8,128)S(1)}, f32[136,128]{1,0:T(8,128)S(1)}, u32[]{:S(2)}, u32[]{:S(2)}) collective-permute-start(f32[136,128]{1,0:T(8,128)S(1)} %get-tuple-element.70), channel_id=1, source_target_pairs={{0,8},{8,0},{1,9},{9,1},{2,10},{10,2},{3,11},{11,3},{4,12},{12,4},... | collective-permute-start | bytes 208904 | tf_op jit(solution)/shard_map/ppermute | solution.py:628
  46.3 7.5 %near.1.near_ref = f32[64,2048]{1,0:T(8,128)S(1)} custom-call(s32[3,67]{1,0:T(4,128)} %get-tuple-element.75.tiles, bf16[4096,256]{1,0:T(8,128)(2,1)} %get-tuple-element.76.a_hbm, bf16[8,512,256]{2,1,0:T(8,128)(2,1)} %get-tuple-element.77.made_hbm, bf16[144,4096]{1,0:T(8,128)(2,1)S(1)} %get-tuple-element.72.tree_ref, bf16[64,4096]{1,0:T(8,128)(2,1)S(1)} %get-tuple-element.78.w_ref), custom_call_target="tpu_custom_call" | custom-call | tf_op jit(solution)/shard_map/near/pallas_call | solution.py:800
  53.8 2.2 %far.1 = (f32[4,64,512]{2,1,0:T(8,128)S(1)}, f32[4,64,512]{2,1,0:T(8,128)S(1)}) custom-call(f32[1,136,128]{2,1,0:T(8,128)S(1)} %bitcast.4, f32[4,1024]{1,0:T(4,128)S(1)} %get-tuple-element.65.slot_ref, f32[4,8,128]{2,1,0:T(8,128)S(1)} %get-tuple-element.71.info_ref, bf16[144,4096]{1,0:T(8,128)(2,1)S(1)} %get-tuple-element.72.tree_ref, ...), custom_call_target="tpu_custom_call" | custom-call | tf_op jit(solution)/shard_map/far/pallas_call | solution.py:818
  56.1 1.9 %collective-permute-done.18.got_ref = f32[4,64,512]{2,1,0:T(8,128)S(1)} collective-permute-done((f32[4,64,512]{2,1,0:T(8,128)S(1)}, f32[4,64,512]{2,1,0:T(8,128)S(1)}, u32[]{:S(2)}, u32[]{:S(2)}) %collective-permute-start.18) | collective-permute-done | bytes 524320 | tf_op jit(solution)/shard_map/ppermute | solution.py:685
  58.1 1.4 %collective-permute-start.19 = (f32[64,512]{1,0:T(8,128)S(1)}, f32[64,512]{1,0:T(8,128)S(1)}, u32[]{:S(2)}, u32[]{:S(2)}) collective-permute-start(f32[64,512]{1,0:T(8,128)S(1)} %get-tuple-element.81), channel_id=1, source_target_pairs={{0,4},{1,13},{2,6},{3,15},{4,0},{5,9},{6,2},{7,11},{8,12},{9,5},{1... | collective-permute-start | bytes 393224 | tf_op jit(solution)/shard_map/ppermute | solution.py:682
  59.5 3.0 %collective-permute-start.20 = (f32[64,512]{1,0:T(8,128)S(1)}, f32[64,512]{1,0:T(8,128)S(1)}, u32[]{:S(2)}, u32[]{:S(2)}) collective-permute-start(f32[64,512]{1,0:T(8,128)S(1)} %get-tuple-element.82), channel_id=1, source_target_pairs={{0,6},{1,15},{2,4},{3,13},{4,2},{5,11},{6,0},{7,9},{8,14},{9,7},{1... | collective-permute-start | bytes 393224 | tf_op jit(solution)/shard_map/ppermute | solution.py:682
  63.2 7.8 %collective-permute-done.19.refs_0_ = f32[64,512]{1,0:T(8,128)S(1)} collective-permute-done((f32[64,512]{1,0:T(8,128)S(1)}, f32[64,512]{1,0:T(8,128)S(1)}, u32[]{:S(2)}, u32[]{:S(2)}) %collective-permute-start.19) | collective-permute-done | bytes 131104 | tf_op jit(solution)/shard_map/ppermute | solution.py:682
  71.6 1.8 %collective-permute-done.22.refs_3_ = f32[64,512]{1,0:T(8,128)S(1)} collective-permute-done((f32[64,512]{1,0:T(8,128)S(1)}, f32[64,512]{1,0:T(8,128)S(1)}, u32[]{:S(2)}, u32[]{:S(2)}) %collective-permute-start.22) | collective-permute-done | bytes 131104 | tf_op jit(solution)/shard_map/ppermute | solution.py:682
  73.6 1.2 %collective-permute-done.26.refs_7_ = f32[64,512]{1,0:T(8,128)S(1)} collective-permute-done((f32[64,512]{1,0:T(8,128)S(1)}, f32[64,512]{1,0:T(8,128)S(1)}, u32[]{:S(2)}, u32[]{:S(2)}) %collective-permute-start.26) | collective-permute-done | bytes 131104 | tf_op jit(solution)/shard_map/ppermute | solution.py:685
  74.8 1.9 %to_input_order.1 = f32[1024,128]{1,0:T(8,128)} custom-call(f32[8,128]{1,0:T(8,128)S(1)} %copy-done.1, f32[64,512]{1,0:T(8,128)S(1)} %collective-permute-done.19.refs_0_, f32[64,512]{1,0:T(8,128)S(1)} %collective-permute-done.20.refs_1_, f32[64,512]{1,0:T(8,128)S(1)} %collective-permute-done.21.refs_2_, f32[64,512]{1,0:T(8,128)S(1)} %collective-permute-done.22.refs_3_, ...), custom_call_target="tpu_custom_call" | custom-call | tf_op jit(solution)/shard_map/to_input_order/pallas_call | solution.py:855
  (43 shorter events, 5.6 us)
Async XLA Ops:
  2.7 1.6 %collective-permute-start = (f32[72,512]{1,0:T(8,128)}, f32[72,512]{1,0:T(8,128)S(1)}, u32[]{:S(2)}, u32[]{:S(2)}) collective-permute-start(f32[72,512]{1,0:T(8,128)} %get-tuple-element.46), channel_id=1, source_target_pairs={{0,0},{1,9},{2,2},{3,11},{4,4},{5,13},{6,6},{7,15},{8,8},{9,1},{10... | collective-permute-start | bytes 442376 | tf_op jit(solution)/shard_map/ppermute | solution.py:682
  4.3 11.9 %collective-permute-start.2 = (f32[72,512]{1,0:T(8,128)S(1)}, f32[72,512]{1,0:T(8,128)S(1)}, u32[]{:S(2)}, u32[]{:S(2)}) collective-permute-start(f32[72,512]{1,0:T(8,128)S(1)} %collective-permute-done.refs_0_), channel_id=1, source_target_pairs={{0,4},{2,6},{4,0},{6,2},{1,5},{3,7},{5,1},{7,3},{8,12},{10,14},{12... | collective-permute-start | bytes 442376 | tf_op jit(solution)/shard_map/ppermute | solution.py:711
  10.1 6.5 %collective-permute-start.4 = (f32[4,32,512]{2,1,0:T(8,128)S(1)}, f32[4,32,512]{2,1,0:T(8,128)S(1)}, u32[]{:S(2)}, u32[]{:S(2)}) collective-permute-start(f32[4,32,512]{2,1,0:T(8,128)S(1)} %get-tuple-element.48), channel_id=1, source_target_pairs={{0,1},{1,0},{2,3},{3,2},{4,5},{5,4},{6,7},{7,6},{8,9},{9,8},{10,11... | collective-permute-start | bytes 786440 | tf_op jit(solution)/shard_map/ppermute | solution.py:685
  14.6 6.7 %collective-permute-start.1 = (f32[72,512]{1,0:T(8,128)S(1)}, f32[72,512]{1,0:T(8,128)S(1)}, u32[]{:S(2)}, u32[]{:S(2)}) collective-permute-start(f32[72,512]{1,0:T(8,128)S(1)} %collective-permute-done.refs_0_), channel_id=1, source_target_pairs={{0,2},{2,0},{4,6},{6,4},{1,3},{3,1},{5,7},{7,5},{8,10},{10,8},{12,... | collective-permute-start | bytes 442376 | tf_op jit(solution)/shard_map/ppermute | solution.py:711
  16.2 7.4 %collective-permute-start.3 = (f32[72,512]{1,0:T(8,128)S(1)}, f32[72,512]{1,0:T(8,128)S(1)}, u32[]{:S(2)}, u32[]{:S(2)}) collective-permute-start(f32[72,512]{1,0:T(8,128)S(1)} %collective-permute-done.2.refs_2_), channel_id=1, source_target_pairs={{0,2},{2,0},{4,6},{6,4},{1,3},{3,1},{5,7},{7,5},{8,10},{10,8},{12,... | collective-permute-start | bytes 442376 | tf_op jit(solution)/shard_map/ppermute | solution.py:711
  23.6 1.9 %collective-permute-start.5 = (f32[72,512]{1,0:T(8,128)S(1)}, f32[72,512]{1,0:T(8,128)S(1)}, u32[]{:S(2)}, u32[]{:S(2)}) collective-permute-start(f32[72,512]{1,0:T(8,128)S(1)} %collective-permute-done.refs_0_), channel_id=1, source_target_pairs={{0,1},{1,0},{2,3},{3,2},{4,5},{5,4},{6,7},{7,6},{8,9},{9,8},{10,11... | collective-permute-start | bytes 442376 | tf_op jit(solution)/shard_map/ppermute | solution.py:685
  23.6 5.0 %collective-permute-start.6 = (f32[72,512]{1,0:T(8,128)S(1)}, f32[72,512]{1,0:T(8,128)S(1)}, u32[]{:S(2)}, u32[]{:S(2)}) collective-permute-start(f32[72,512]{1,0:T(8,128)S(1)} %collective-permute-done.1.refs_1_), channel_id=1, source_target_pairs={{0,1},{1,0},{2,3},{3,2},{4,5},{5,4},{6,7},{7,6},{8,9},{9,8},{10,11... | collective-permute-start | bytes 442376 | tf_op jit(solution)/shard_map/ppermute | solution.py:685
  24.1 5.1 %collective-permute-start.7 = (f32[72,512]{1,0:T(8,128)S(1)}, f32[72,512]{1,0:T(8,128)S(1)}, u32[]{:S(2)}, u32[]{:S(2)}) collective-permute-start(f32[72,512]{1,0:T(8,128)S(1)} %collective-permute-done.2.refs_2_), channel_id=1, source_target_pairs={{0,1},{1,0},{2,3},{3,2},{4,5},{5,4},{6,7},{7,6},{8,9},{9,8},{10,11... | collective-permute-start | bytes 442376 | tf_op jit(solution)/shard_map/ppermute | solution.py:685
  24.1 5.2 %collective-permute-start.8 = (f32[72,512]{1,0:T(8,128)S(1)}, f32[72,512]{1,0:T(8,128)S(1)}, u32[]{:S(2)}, u32[]{:S(2)}) collective-permute-start(f32[72,512]{1,0:T(8,128)S(1)} %collective-permute-done.3.refs_3_), channel_id=1, source_target_pairs={{0,1},{1,0},{2,3},{3,2},{4,5},{5,4},{6,7},{7,6},{8,9},{9,8},{10,11... | collective-permute-start | bytes 442376 | tf_op jit(solution)/shard_map/ppermute | solution.py:685
  24.6 13.0 %collective-permute-start.9 = (f32[64,512]{1,0:T(8,128)S(1)}, f32[64,512]{1,0:T(8,128)S(1)}, u32[]{:S(2)}, u32[]{:S(2)}) collective-permute-start(f32[64,512]{1,0:T(8,128)S(1)} %get-tuple-element.60), channel_id=1, source_target_pairs={{0,4},{1,13},{2,6},{3,15},{4,0},{5,9},{6,2},{7,11},{8,12},{9,5},{1... | collective-permute-start | bytes 393224 | tf_op jit(solution)/shard_map/ppermute | solution.py:682
  25.5 12.0 %collective-permute-start.10 = (f32[64,512]{1,0:T(8,128)S(1)}, f32[64,512]{1,0:T(8,128)S(1)}, u32[]{:S(2)}, u32[]{:S(2)}) collective-permute-start(f32[64,512]{1,0:T(8,128)S(1)} %get-tuple-element.61), channel_id=1, source_target_pairs={{0,6},{1,15},{2,4},{3,13},{4,2},{5,11},{6,0},{7,9},{8,14},{9,7},{1... | collective-permute-start | bytes 393224 | tf_op jit(solution)/shard_map/ppermute | solution.py:682
  28.5 9.0 %collective-permute-start.11 = (f32[64,512]{1,0:T(8,128)S(1)}, f32[64,512]{1,0:T(8,128)S(1)}, u32[]{:S(2)}, u32[]{:S(2)}) collective-permute-start(f32[64,512]{1,0:T(8,128)S(1)} %get-tuple-element.62), channel_id=1, source_target_pairs={{0,0},{1,9},{2,2},{3,11},{4,4},{5,13},{6,6},{7,15},{8,8},{9,1},{10... | collective-permute-start | bytes 393224 | tf_op jit(solution)/shard_map/ppermute | solution.py:682
  29.2 10.7 %collective-permute-start.12 = (f32[64,512]{1,0:T(8,128)S(1)}, f32[64,512]{1,0:T(8,128)S(1)}, u32[]{:S(2)}, u32[]{:S(2)}) collective-permute-start(f32[64,512]{1,0:T(8,128)S(1)} %get-tuple-element.63), channel_id=1, source_target_pairs={{0,2},{1,11},{2,0},{3,9},{4,6},{5,15},{6,4},{7,13},{8,10},{9,3},{1... | collective-permute-start | bytes 393224 | tf_op jit(solution)/shard_map/ppermute | solution.py:682
  40.0 1.3 %collective-permute-start.13 = (f32[64,512]{1,0:T(8,128)S(1)}, f32[64,512]{1,0:T(8,128)S(1)}, u32[]{:S(2)}, u32[]{:S(2)}) collective-permute-start(f32[64,512]{1,0:T(8,128)S(1)} %collective-permute-done.9.refs_0_), channel_id=1, source_target_pairs={{0,1},{1,0},{2,3},{3,2},{4,5},{5,4},{6,7},{7,6},{8,9},{9,8},{10,11... | collective-permute-start | bytes 393224 | tf_op jit(solution)/shard_map/ppermute | solution.py:685
  40.3 1.3 %collective-permute-start.14 = (f32[64,512]{1,0:T(8,128)S(1)}, f32[64,512]{1,0:T(8,128)S(1)}, u32[]{:S(2)}, u32[]{:S(2)}) collective-permute-start(f32[64,512]{1,0:T(8,128)S(1)} %collective-permute-done.10.refs_1_), channel_id=1, source_target_pairs={{0,1},{1,0},{2,3},{3,2},{4,5},{5,4},{6,7},{7,6},{8,9},{9,8},{10,11... | collective-permute-start | bytes 393224 | tf_op jit(solution)/shard_map/ppermute | solution.py:685
  45.0 8.8 %collective-permute-start.17 = (f32[136,128]{1,0:T(8,128)S(1)}, f32[136,128]{1,0:T(8,128)S(1)}, u32[]{:S(2)}, u32[]{:S(2)}) collective-permute-start(f32[136,128]{1,0:T(8,128)S(1)} %get-tuple-element.70), channel_id=1, source_target_pairs={{0,8},{8,0},{1,9},{9,1},{2,10},{10,2},{3,11},{11,3},{4,12},{12,4},... | collective-permute-start | bytes 208904 | tf_op jit(solution)/shard_map/ppermute | solution.py:628
  56.0 2.0 %collective-permute-start.18 = (f32[4,64,512]{2,1,0:T(8,128)S(1)}, f32[4,64,512]{2,1,0:T(8,128)S(1)}, u32[]{:S(2)}, u32[]{:S(2)}) collective-permute-start(f32[4,64,512]{2,1,0:T(8,128)S(1)} %get-tuple-element.80), channel_id=1, source_target_pairs={{0,1},{1,0},{2,3},{3,2},{4,5},{5,4},{6,7},{7,6},{8,9},{9,8},{10,11... | collective-permute-start | bytes 1572872 | tf_op jit(solution)/shard_map/ppermute | solution.py:685
  58.1 13.0 %collective-permute-start.19 = (f32[64,512]{1,0:T(8,128)S(1)}, f32[64,512]{1,0:T(8,128)S(1)}, u32[]{:S(2)}, u32[]{:S(2)}) collective-permute-start(f32[64,512]{1,0:T(8,128)S(1)} %get-tuple-element.81), channel_id=1, source_target_pairs={{0,4},{1,13},{2,6},{3,15},{4,0},{5,9},{6,2},{7,11},{8,12},{9,5},{1... | collective-permute-start | bytes 393224 | tf_op jit(solution)/shard_map/ppermute | solution.py:682
  59.5 11.6 %collective-permute-start.20 = (f32[64,512]{1,0:T(8,128)S(1)}, f32[64,512]{1,0:T(8,128)S(1)}, u32[]{:S(2)}, u32[]{:S(2)}) collective-permute-start(f32[64,512]{1,0:T(8,128)S(1)} %get-tuple-element.82), channel_id=1, source_target_pairs={{0,6},{1,15},{2,4},{3,13},{4,2},{5,11},{6,0},{7,9},{8,14},{9,7},{1... | collective-permute-start | bytes 393224 | tf_op jit(solution)/shard_map/ppermute | solution.py:682
  62.5 9.1 %collective-permute-start.21 = (f32[64,512]{1,0:T(8,128)S(1)}, f32[64,512]{1,0:T(8,128)S(1)}, u32[]{:S(2)}, u32[]{:S(2)}) collective-permute-start(f32[64,512]{1,0:T(8,128)S(1)} %get-tuple-element.83), channel_id=1, source_target_pairs={{0,0},{1,9},{2,2},{3,11},{4,4},{5,13},{6,6},{7,15},{8,8},{9,1},{10... | collective-permute-start | bytes 393224 | tf_op jit(solution)/shard_map/ppermute | solution.py:682
  63.1 10.3 %collective-permute-start.22 = (f32[64,512]{1,0:T(8,128)S(1)}, f32[64,512]{1,0:T(8,128)S(1)}, u32[]{:S(2)}, u32[]{:S(2)}) collective-permute-start(f32[64,512]{1,0:T(8,128)S(1)} %get-tuple-element.84), channel_id=1, source_target_pairs={{0,2},{1,11},{2,0},{3,9},{4,6},{5,15},{6,4},{7,13},{8,10},{9,3},{1... | collective-permute-start | bytes 393224 | tf_op jit(solution)/shard_map/ppermute | solution.py:682
  71.1 2.6 %collective-permute-start.23 = (f32[64,512]{1,0:T(8,128)S(1)}, f32[64,512]{1,0:T(8,128)S(1)}, u32[]{:S(2)}, u32[]{:S(2)}) collective-permute-start(f32[64,512]{1,0:T(8,128)S(1)} %collective-permute-done.19.refs_0_), channel_id=1, source_target_pairs={{0,1},{1,0},{2,3},{3,2},{4,5},{5,4},{6,7},{7,6},{8,9},{9,8},{10,11... | collective-permute-start | bytes 393224 | tf_op jit(solution)/shard_map/ppermute | solution.py:685
  71.1 2.6 %collective-permute-start.24 = (f32[64,512]{1,0:T(8,128)S(1)}, f32[64,512]{1,0:T(8,128)S(1)}, u32[]{:S(2)}, u32[]{:S(2)}) collective-permute-start(f32[64,512]{1,0:T(8,128)S(1)} %collective-permute-done.20.refs_1_), channel_id=1, source_target_pairs={{0,1},{1,0},{2,3},{3,2},{4,5},{5,4},{6,7},{7,6},{8,9},{9,8},{10,11... | collective-permute-start | bytes 393224 | tf_op jit(solution)/shard_map/ppermute | solution.py:685
  71.6 2.1 %collective-permute-start.25 = (f32[64,512]{1,0:T(8,128)S(1)}, f32[64,512]{1,0:T(8,128)S(1)}, u32[]{:S(2)}, u32[]{:S(2)}) collective-permute-start(f32[64,512]{1,0:T(8,128)S(1)} %collective-permute-done.21.refs_2_), channel_id=1, source_target_pairs={{0,1},{1,0},{2,3},{3,2},{4,5},{5,4},{6,7},{7,6},{8,9},{9,8},{10,11... | collective-permute-start | bytes 393224 | tf_op jit(solution)/shard_map/ppermute | solution.py:685
  (5 other events, 46.1 us)

commit v16 on v15

--- a/solution.py
+++ b/solution.py
@@ -259,16 +259,19 @@
     def send(tile):
         return pltpu.make_async_copy(made.at[tile], made_hbm.at[tile], sems.at[tile])
 
-    even[...] = tile_exponents(layout, tiles, 0, a_ref, bt_ref)
+    for k in range(2):
+        even[k] = tile_exponents(layout, tiles, k, a_ref, bt_ref)
 
     def step(pair, carry):
-        for tile, ready, upcoming in ((2 * pair, even, odd), (2 * pair + 1, odd, even)):
-            upcoming[...] = tile_exponents(layout, tiles, tile + 1, a_ref, bt_ref)
-            made[tile] = jnp.exp(ready[...]).astype(bf16)
-            send(tile).start()
+        for unit, ready, upcoming in ((2 * pair, even, odd), (2 * pair + 1, odd, even)):
+            for k in range(2):
+                tile = 2 * unit + k
+                upcoming[k] = tile_exponents(layout, tiles, tile + 2, a_ref, bt_ref)
+                made[tile] = jnp.exp(ready[k]).astype(bf16)
+                send(tile).start()
         return carry
 
-    lax.fori_loop(0, layout.ahead // 2, step, 0)
+    lax.fori_loop(0, layout.ahead // 4, step, 0)
     return [send(tile) for tile in range(layout.ahead)]
 
 
@@ -297,6 +300,7 @@
     def pad(more, carry):
         tiles[0, more] = 0
         tiles[1, more] = 0
+        tiles[2, more] = 0
         return carry
 
     lax.fori_loop(filled, tiles.shape[1] - 1, pad, 0)
@@ -446,8 +450,9 @@
     acc[...] = jnp.zeros_like(acc)
     target_columns(layout, bt_ref, tree_ref)
 
-    def exponents(tile):
-        return tile_exponents(layout, tiles, tile, a_ref, bt_ref)
+    def exponents(unit, out):
+        for k in range(2):
+            out[k] = tile_exponents(layout, tiles, ahead + 2 * unit + k, a_ref, bt_ref)
 
     def add(tile, block):
         source = aligned(tiles[1, tile] * LEAF, LEAF, LEAF)
@@ -458,28 +463,33 @@
 
     @pl.when(filled > ahead)
     def _():
-        even[...] = exponents(ahead)
-        even_tile[...] = jnp.exp(even[...]).astype(bf16)
-        odd[...] = exponents(ahead + 1)
-
-        def phase(tile, upcoming, ready, finished, previous):
-            upcoming[...] = exponents(tile + 1)
-            finished[...] = jnp.exp(ready[...]).astype(bf16)
-            add(tile - 1, previous[...])
+        exponents(0, even)
+        for k in range(2):
+            even_tile[k] = jnp.exp(even[k]).astype(bf16)
+        exponents(1, odd)
+
+        def phase(unit, upcoming, ready, finished, previous):
+            for k in range(2):
+                upcoming[k] = tile_exponents(layout, tiles, ahead + 2 * (unit + 1) + k, a_ref, bt_ref)
+                finished[k] = jnp.exp(ready[k]).astype(bf16)
+                add(ahead + 2 * (unit - 1) + k, previous[k])
 
         def step(pair, carry):
-            phase(ahead + 2 * pair + 1, even, odd, odd_tile, even_tile)
-            phase(ahead + 2 * pair + 2, odd, even, even_tile, odd_tile)
+            phase(2 * pair + 1, even, odd, odd_tile, even_tile)
+            phase(2 * pair + 2, odd, even, even_tile, odd_tile)
             return carry
 
-        pairs = (filled - ahead - 1) // 2
+        units = (filled - ahead + 1) // 2
+        pairs = (units - 1) // 2
         lax.fori_loop(0, pairs, step, 0)
-        add(ahead + 2 * pairs, even_tile[...])
-
-        @pl.when(ahead + 2 * pairs + 1 < filled)
+        for k in range(2):
+            add(ahead + 4 * pairs + k, even_tile[k])
+
+        @pl.when(2 * pairs + 1 < units)
         def _():
-            odd_tile[...] = jnp.exp(odd[...]).astype(bf16)
-            add(ahead + 2 * pairs + 1, odd_tile[...])
+            for k in range(2):
+                odd_tile[k] = jnp.exp(odd[k]).astype(bf16)
+                add(ahead + 4 * pairs + 2 + k, odd_tile[k])
 
     def arrived(quad, carry):
         for more in range(4):
@@ -684,7 +694,7 @@
     def other_core(value):
         return lax.ppermute(value, "rep", [(0, 1), (1, 0)])
 
-    def sorted_light():
+    def sorted_light(pos):
         if fine:
             shapes = (shaped((blocks, width, part), f32),) * 2
         else:
@@ -704,13 +714,14 @@
         )(in_hbm(pos), in_hbm(weights))
 
     if fine:
-        place = {0: swap(place, 0)}
+        kept, sent = sorted_light(pos)
+        place, kept, sent = lax.optimization_barrier((swap(place, 0), kept, sent))
+        place = {0: place}
         stride = blocks // 2
         while stride:
             for step in sorted(place):
                 place[step | stride] = lax.ppermute(place[step], "sub", [(i, i ^ stride) for i in range(blocks)])
             stride //= 2
-        kept, sent = sorted_light()
         light = pl.pallas_call(
             join_kernel,
             out_shape=(shaped((cols, part), f32),) * blocks,
@@ -732,7 +743,7 @@
         place = lax.all_gather(place, "sub", axis=0, tiled=False)
         place = place.transpose(1, 0, 2, 3).reshape(devices, PLACE_ROWS, blocks, per)
         place = [place.transpose(1, 2, 0, 3).reshape(PLACE_ROWS, total)]
-        light = sorted_light()[0].reshape(columns, trees, part).transpose(1, 0, 2).reshape(devices, width, part)
+        light = sorted_light(pos)[0].reshape(columns, trees, part).transpose(1, 0, 2).reshape(devices, width, part)
         light = lax.all_to_all(light, ("leaf", "sub"), split_axis=0, concat_axis=0, tiled=True)
         light = light.reshape(devices, width, blocks, per)
         light = [light.transpose(1, 2, 0, 3).reshape(width, total)]
@@ -749,7 +760,7 @@
             vm((PLACE_ROWS, SK), f32),
             vm((blocks, rows), f32),
             vm((blocks, 8, SK), f32),
-            pltpu.MemorySpace.HBM((3, leaves * leaves + 3), jnp.int32),
+            pltpu.MemorySpace.HBM((3, leaves * leaves + 8), jnp.int32),
             pltpu.MemorySpace.HBM((layout.ahead, LEAF, layout.span), bf16),
         ),
         in_specs=[spec(SMEM)] * 2 + [spec()] * (1 + len(small) + layout.count),
@@ -764,8 +775,8 @@
             pltpu.SemaphoreType.DMA((2, blocks)),
             pltpu.SMEM((leaves,), jnp.int32),
             vm((FEAT, total // layout.halves), bf16),
-            vm((LEAF, layout.span), f32),
-            vm((LEAF, layout.span), f32),
+            vm((2, LEAF, layout.span), f32),
+            vm((2, LEAF, layout.span), f32),
             vm((layout.ahead, LEAF, layout.span), bf16),
             pltpu.SemaphoreType.DMA((layout.ahead,)),
         ],
@@ -808,8 +819,8 @@
             vm((layout.ahead, LEAF, layout.span), bf16),
             pltpu.SemaphoreType.DMA((layout.ahead + 1,)),
         ]
-        + [vm((LEAF, layout.span), f32)] * 2
-        + [vm((LEAF, layout.span), bf16)] * 2,
+        + [vm((2, LEAF, layout.span), f32)] * 2
+        + [vm((2, LEAF, layout.span), bf16)] * 2,
         compiler_params=params(40),
         name="near",
     )(in_hbm(tiles), in_hbm(feat_a), in_hbm(made), held(tree), held(tree_light))

time: 76.9 us -> 77.1 us (level)
  starting transfers between devices: 25.9 us -> 26.8 us
    ppermute x3, starting transfers between devices: 6.06 us -> 8.46 us  [body(): lax.ppermute(place[step], 'sub', [(i, i ^ stride) for i in range(blocks)])]
    ppermute x14, starting transfers between devices: 7.28 us -> 5.54 us  [other_core(): return lax.ppermute(value, 'rep', [(0, 1), (1, 0)])]
  transfers between devices with their start and end apart: 27 -> 27, of which waited for: 12 -> 12; matrix products, arithmetic and copies ran while one was open for 0% -> 0% of each run, Pallas kernels for 23% -> 22%
where the time goes in v16:
time: 77.1 us; the launch traced here: 76.8 us
  Pallas kernels  26.9 us (35%)
  starting transfers between devices  26.8 us (35%)
  waiting for transfers between devices  22.9 us (30%)
    ppermute x9, waiting for transfers between devices, swap(): return lax.ppermute(value, axes, pairs)  11.9 us
    ppermute x9, starting transfers between devices, swap(): return lax.ppermute(value, axes, pairs)  11.8 us
    ppermute x3, starting transfers between devices, body(): lax.ppermute(place[step], 'sub', [(i, i ^ stride) for i in range(blocks)])  8.46 us
    pallas_call x1, Pallas kernels, body(): pl.pallas_call(functools.partial(points_kernel, layout, trees), out_shape...  7.85 us
    pallas_call x1, Pallas kernels, body(): pl.pallas_call(functools.partial(near_kernel, layout), out_shape=vm((cols...  7.44 us
    ppermute x3, waiting for transfers between devices, body(): lax.ppermute(place[step], 'sub', [(i, i ^ stride) for i in range(blocks)])  6.86 us
    ppermute x14, starting transfers between devices, other_core(): return lax.ppermute(value, 'rep', [(0, 1), (1, 0)])  5.54 us
    ppermute x14, waiting for transfers between devices, other_core(): return lax.ppermute(value, 'rep', [(0, 1), (1, 0)])  4.16 us
  transfers between devices with their start and end apart: 27, of which 12 were waited for; matrix products, arithmetic and copies ran while one was open for 0% of the time, Pallas kernels for 22%

profile of v16, /device:TPU:0, one launch (start us, length us, event | category | flops | bytes accessed | tf_op | source)
XLA Modules:
  0.0 76.8 jit_solution(160099477072472151)
XLA Ops:
  0.0 2.7 %sort_points.1 = (f32[72,512]{1,0:T(8,128)}, f32[8,128]{1,0:T(8,128)}) custom-call(s32[8,128]{1,0:T(8,128)} %bitcast.6, f32[64,1024]{1,0:T(8,128)} %bitcast.5, s32[1,128]{1,0:T(1,128)} %base_ref.1, s32[2,3]{1,0:T(2,128)} %flag_ref.1), custom_call_target="tpu_custom_call" | custom-call | tf_op jit(solution)/shard_map/sort_points/pallas_call | solution.py:674
  2.7 1.6 %collective-permute-start = (f32[72,512]{1,0:T(8,128)}, f32[72,512]{1,0:T(8,128)S(1)}, u32[]{:S(2)}, u32[]{:S(2)}) collective-permute-start(f32[72,512]{1,0:T(8,128)} %get-tuple-element.49), channel_id=1, source_target_pairs={{0,0},{1,9},{2,2},{3,11},{4,4},{5,13},{6,6},{7,15},{8,8},{9,1},{10... | collective-permute-start | bytes 442376 | tf_op jit(solution)/shard_map/ppermute | solution.py:692
  4.3 1.8 %sort_weights.1 = (f32[4,32,512]{2,1,0:T(8,128)S(1)}, f32[4,32,512]{2,1,0:T(8,128)S(1)}) custom-call(f32[8,128]{1,0:T(8,128)} %get-tuple-element.48.pos_ref, f32[1024,128]{1,0:T(8,128)} %refs_8_.1), custom_call_target="tpu_custom_call" | custom-call | tf_op jit(solution)/shard_map/sort_weights/pallas_call | solution.py:702
  6.1 4.1 %collective-permute-start.2 = (f32[72,512]{1,0:T(8,128)S(1)}, f32[72,512]{1,0:T(8,128)S(1)}, u32[]{:S(2)}, u32[]{:S(2)}) collective-permute-start(f32[72,512]{1,0:T(8,128)S(1)} %collective-permute-done.refs_0_), channel_id=1, source_target_pairs={{0,4},{2,6},{4,0},{6,2},{1,5},{3,7},{5,1},{7,3},{8,12},{10,14},{12... | collective-permute-start | bytes 442376 | tf_op jit(solution)/shard_map/ppermute | solution.py:723
  10.2 2.2 %collective-permute-start.4 = (f32[4,32,512]{2,1,0:T(8,128)S(1)}, f32[4,32,512]{2,1,0:T(8,128)S(1)}, u32[]{:S(2)}, u32[]{:S(2)}) collective-permute-start(f32[4,32,512]{2,1,0:T(8,128)S(1)} %get-tuple-element.54), channel_id=1, source_target_pairs={{0,1},{1,0},{2,3},{3,2},{4,5},{5,4},{6,7},{7,6},{8,9},{9,8},{10,11... | collective-permute-start | bytes 786440 | tf_op jit(solution)/shard_map/ppermute | solution.py:695
  12.4 1.6 %collective-permute-start.1 = (f32[72,512]{1,0:T(8,128)S(1)}, f32[72,512]{1,0:T(8,128)S(1)}, u32[]{:S(2)}, u32[]{:S(2)}) collective-permute-start(f32[72,512]{1,0:T(8,128)S(1)} %collective-permute-done.refs_0_), channel_id=1, source_target_pairs={{0,2},{2,0},{4,6},{6,4},{1,3},{3,1},{5,7},{7,5},{8,10},{10,8},{12,... | collective-permute-start | bytes 442376 | tf_op jit(solution)/shard_map/ppermute | solution.py:723
  14.0 2.2 %collective-permute-done.2.refs_2_ = f32[72,512]{1,0:T(8,128)S(1)} collective-permute-done((f32[72,512]{1,0:T(8,128)S(1)}, f32[72,512]{1,0:T(8,128)S(1)}, u32[]{:S(2)}, u32[]{:S(2)}) %collective-permute-start.2) | collective-permute-done | bytes 147488 | tf_op jit(solution)/shard_map/ppermute | solution.py:723
  16.2 2.8 %collective-permute-start.3 = (f32[72,512]{1,0:T(8,128)S(1)}, f32[72,512]{1,0:T(8,128)S(1)}, u32[]{:S(2)}, u32[]{:S(2)}) collective-permute-start(f32[72,512]{1,0:T(8,128)S(1)} %collective-permute-done.2.refs_2_), channel_id=1, source_target_pairs={{0,2},{2,0},{4,6},{6,4},{1,3},{3,1},{5,7},{7,5},{8,10},{10,8},{12,... | collective-permute-start | bytes 442376 | tf_op jit(solution)/shard_map/ppermute | solution.py:723
  19.9 3.8 %collective-permute-done.3.refs_3_ = f32[72,512]{1,0:T(8,128)S(1)} collective-permute-done((f32[72,512]{1,0:T(8,128)S(1)}, f32[72,512]{1,0:T(8,128)S(1)}, u32[]{:S(2)}, u32[]{:S(2)}) %collective-permute-start.3) | collective-permute-done | bytes 147488 | tf_op jit(solution)/shard_map/ppermute | solution.py:723
  24.7 2.8 %collective-permute-start.9 = (f32[64,512]{1,0:T(8,128)S(1)}, f32[64,512]{1,0:T(8,128)S(1)}, u32[]{:S(2)}, u32[]{:S(2)}) collective-permute-start(f32[64,512]{1,0:T(8,128)S(1)} %get-tuple-element.66), channel_id=1, source_target_pairs={{0,4},{1,13},{2,6},{3,15},{4,0},{5,9},{6,2},{7,11},{8,12},{9,5},{1... | collective-permute-start | bytes 393224 | tf_op jit(solution)/shard_map/ppermute | solution.py:692
  27.6 1.5 %collective-permute-start.10 = (f32[64,512]{1,0:T(8,128)S(1)}, f32[64,512]{1,0:T(8,128)S(1)}, u32[]{:S(2)}, u32[]{:S(2)}) collective-permute-start(f32[64,512]{1,0:T(8,128)S(1)} %get-tuple-element.67), channel_id=1, source_target_pairs={{0,6},{1,15},{2,4},{3,13},{4,2},{5,11},{6,0},{7,9},{8,14},{9,7},{1... | collective-permute-start | bytes 393224 | tf_op jit(solution)/shard_map/ppermute | solution.py:692
  30.1 7.9 %tree_points.1 = (bf16[144,4096]{1,0:T(8,128)(2,1)S(1)}, bf16[4096,256]{1,0:T(8,128)(2,1)}, bf16[4,1024,128]{2,1,0:T(8,128)(2,1)}, bf16[896,256]{1,0:T(8,128)(2,...) custom-call(s32[1,8]{1,0:T(1,128)} %count_ref.1, ...), custom_call_target="tpu_custom_call" | custom-call | tf_op jit(solution)/shard_map/tree_points/pallas_call | solution.py:752
  38.0 2.4 %collective-permute-done.12.refs_3_ = f32[64,512]{1,0:T(8,128)S(1)} collective-permute-done((f32[64,512]{1,0:T(8,128)S(1)}, f32[64,512]{1,0:T(8,128)S(1)}, u32[]{:S(2)}, u32[]{:S(2)}) %collective-permute-start.12) | collective-permute-done | bytes 131104 | tf_op jit(solution)/shard_map/ppermute | solution.py:692
  42.7 2.9 %tree_weights.1 = (bf16[64,4096]{1,0:T(8,128)(2,1)S(1)}, bf16[128,896]{1,0:T(8,128)(2,1)S(1)}, f32[136,128]{1,0:T(8,128)S(1)}) custom-call(bf16[4,1024,128]{2,1,0:T(8,128)(2,1)} %get-tuple-element.63.base_hbm, f32[3,256,128]{2,1,0:T(8,128)S(1)} %get-tuple-element.64.upper_tiles_ref, f32[72,128]{1,0:T(8,128)S(1)} %get-tuple-element.65.top_ref, ...), custom_call_target="tpu_custom_call" | custom-call | tf_op jit(solution)/shard_map/tree_weights/pallas_call | solution.py:790
  45.6 0.9 %collective-permute-start.17 = (f32[136,128]{1,0:T(8,128)S(1)}, f32[136,128]{1,0:T(8,128)S(1)}, u32[]{:S(2)}, u32[]{:S(2)}) collective-permute-start(f32[136,128]{1,0:T(8,128)S(1)} %get-tuple-element.76), channel_id=1, source_target_pairs={{0,8},{8,0},{1,9},{9,1},{2,10},{10,2},{3,11},{11,3},{4,12},{12,4},... | collective-permute-start | bytes 208904 | tf_op jit(solution)/shard_map/ppermute | solution.py:638
  46.5 7.4 %near.1.near_ref = f32[64,2048]{1,0:T(8,128)S(1)} custom-call(s32[3,72]{1,0:T(4,128)} %get-tuple-element.81.tiles, bf16[4096,256]{1,0:T(8,128)(2,1)} %get-tuple-element.82.a_hbm, bf16[8,512,256]{2,1,0:T(8,128)(2,1)} %get-tuple-element.83.made_hbm, bf16[144,4096]{1,0:T(8,128)(2,1)S(1)} %get-tuple-element.78.tree_ref, bf16[64,4096]{1,0:T(8,128)(2,1)S(1)} %get-tuple-element.84.w_ref), custom_call_target="tpu_custom_call" | custom-call | tf_op jit(solution)/shard_map/near/pallas_call | solution.py:811
  54.0 2.2 %far.1 = (f32[4,64,512]{2,1,0:T(8,128)S(1)}, f32[4,64,512]{2,1,0:T(8,128)S(1)}) custom-call(f32[1,136,128]{2,1,0:T(8,128)S(1)} %bitcast.4, f32[4,1024]{1,0:T(4,128)S(1)} %get-tuple-element.71.slot_ref, f32[4,8,128]{2,1,0:T(8,128)S(1)} %get-tuple-element.77.info_ref, bf16[144,4096]{1,0:T(8,128)(2,1)S(1)} %get-tuple-element.78.tree_ref, ...), custom_call_target="tpu_custom_call" | custom-call | tf_op jit(solution)/shard_map/far/pallas_call | solution.py:829
  56.2 1.9 %collective-permute-done.18.got_ref = f32[4,64,512]{2,1,0:T(8,128)S(1)} collective-permute-done((f32[4,64,512]{2,1,0:T(8,128)S(1)}, f32[4,64,512]{2,1,0:T(8,128)S(1)}, u32[]{:S(2)}, u32[]{:S(2)}) %collective-permute-start.18) | collective-permute-done | bytes 524320 | tf_op jit(solution)/shard_map/ppermute | solution.py:695
  58.2 3.0 %collective-permute-start.19 = (f32[64,512]{1,0:T(8,128)S(1)}, f32[64,512]{1,0:T(8,128)S(1)}, u32[]{:S(2)}, u32[]{:S(2)}) collective-permute-start(f32[64,512]{1,0:T(8,128)S(1)} %get-tuple-element.87), channel_id=1, source_target_pairs={{0,4},{1,13},{2,6},{3,15},{4,0},{5,9},{6,2},{7,11},{8,12},{9,5},{1... | collective-permute-start | bytes 393224 | tf_op jit(solution)/shard_map/ppermute | solution.py:692
  61.2 1.0 %collective-permute-start.20 = (f32[64,512]{1,0:T(8,128)S(1)}, f32[64,512]{1,0:T(8,128)S(1)}, u32[]{:S(2)}, u32[]{:S(2)}) collective-permute-start(f32[64,512]{1,0:T(8,128)S(1)} %get-tuple-element.88), channel_id=1, source_target_pairs={{0,6},{1,15},{2,4},{3,13},{4,2},{5,11},{6,0},{7,9},{8,14},{9,7},{1... | collective-permute-start | bytes 393224 | tf_op jit(solution)/shard_map/ppermute | solution.py:692
  63.2 8.1 %collective-permute-done.19.refs_0_ = f32[64,512]{1,0:T(8,128)S(1)} collective-permute-done((f32[64,512]{1,0:T(8,128)S(1)}, f32[64,512]{1,0:T(8,128)S(1)}, u32[]{:S(2)}, u32[]{:S(2)}) %collective-permute-start.19) | collective-permute-done | bytes 131104 | tf_op jit(solution)/shard_map/ppermute | solution.py:692
  71.8 1.5 %collective-permute-done.22.refs_3_ = f32[64,512]{1,0:T(8,128)S(1)} collective-permute-done((f32[64,512]{1,0:T(8,128)S(1)}, f32[64,512]{1,0:T(8,128)S(1)}, u32[]{:S(2)}, u32[]{:S(2)}) %collective-permute-start.22) | collective-permute-done | bytes 131104 | tf_op jit(solution)/shard_map/ppermute | solution.py:692
  73.9 1.0 %collective-permute-done.26.refs_7_ = f32[64,512]{1,0:T(8,128)S(1)} collective-permute-done((f32[64,512]{1,0:T(8,128)S(1)}, f32[64,512]{1,0:T(8,128)S(1)}, u32[]{:S(2)}, u32[]{:S(2)}) %collective-permute-start.26) | collective-permute-done | bytes 131104 | tf_op jit(solution)/shard_map/ppermute | solution.py:695
  74.8 1.9 %to_input_order.1 = f32[1024,128]{1,0:T(8,128)} custom-call(f32[8,128]{1,0:T(8,128)S(1)} %copy-done.1, f32[64,512]{1,0:T(8,128)S(1)} %collective-permute-done.19.refs_0_, f32[64,512]{1,0:T(8,128)S(1)} %collective-permute-done.20.refs_1_, f32[64,512]{1,0:T(8,128)S(1)} %collective-permute-done.21.refs_2_, f32[64,512]{1,0:T(8,128)S(1)} %collective-permute-done.22.refs_3_, ...), custom_call_target="tpu_custom_call" | custom-call | tf_op jit(solution)/shard_map/to_input_order/pallas_call | solution.py:866
  (43 shorter events, 7.4 us)
Async XLA Ops:
  2.7 3.4 %collective-permute-start = (f32[72,512]{1,0:T(8,128)}, f32[72,512]{1,0:T(8,128)S(1)}, u32[]{:S(2)}, u32[]{:S(2)}) collective-permute-start(f32[72,512]{1,0:T(8,128)} %get-tuple-element.49), channel_id=1, source_target_pairs={{0,0},{1,9},{2,2},{3,11},{4,4},{5,13},{6,6},{7,15},{8,8},{9,1},{10... | collective-permute-start | bytes 442376 | tf_op jit(solution)/shard_map/ppermute | solution.py:692
  6.1 10.1 %collective-permute-start.2 = (f32[72,512]{1,0:T(8,128)S(1)}, f32[72,512]{1,0:T(8,128)S(1)}, u32[]{:S(2)}, u32[]{:S(2)}) collective-permute-start(f32[72,512]{1,0:T(8,128)S(1)} %collective-permute-done.refs_0_), channel_id=1, source_target_pairs={{0,4},{2,6},{4,0},{6,2},{1,5},{3,7},{5,1},{7,3},{8,12},{10,14},{12... | collective-permute-start | bytes 442376 | tf_op jit(solution)/shard_map/ppermute | solution.py:723
  10.2 8.8 %collective-permute-start.4 = (f32[4,32,512]{2,1,0:T(8,128)S(1)}, f32[4,32,512]{2,1,0:T(8,128)S(1)}, u32[]{:S(2)}, u32[]{:S(2)}) collective-permute-start(f32[4,32,512]{2,1,0:T(8,128)S(1)} %get-tuple-element.54), channel_id=1, source_target_pairs={{0,1},{1,0},{2,3},{3,2},{4,5},{5,4},{6,7},{7,6},{8,9},{9,8},{10,11... | collective-permute-start | bytes 786440 | tf_op jit(solution)/shard_map/ppermute | solution.py:695
  12.4 7.5 %collective-permute-start.1 = (f32[72,512]{1,0:T(8,128)S(1)}, f32[72,512]{1,0:T(8,128)S(1)}, u32[]{:S(2)}, u32[]{:S(2)}) collective-permute-start(f32[72,512]{1,0:T(8,128)S(1)} %collective-permute-done.refs_0_), channel_id=1, source_target_pairs={{0,2},{2,0},{4,6},{6,4},{1,3},{3,1},{5,7},{7,5},{8,10},{10,8},{12,... | collective-permute-start | bytes 442376 | tf_op jit(solution)/shard_map/ppermute | solution.py:723
  16.2 7.4 %collective-permute-start.3 = (f32[72,512]{1,0:T(8,128)S(1)}, f32[72,512]{1,0:T(8,128)S(1)}, u32[]{:S(2)}, u32[]{:S(2)}) collective-permute-start(f32[72,512]{1,0:T(8,128)S(1)} %collective-permute-done.2.refs_2_), channel_id=1, source_target_pairs={{0,2},{2,0},{4,6},{6,4},{1,3},{3,1},{5,7},{7,5},{8,10},{10,8},{12,... | collective-permute-start | bytes 442376 | tf_op jit(solution)/shard_map/ppermute | solution.py:723
  23.7 3.9 %collective-permute-start.5 = (f32[72,512]{1,0:T(8,128)S(1)}, f32[72,512]{1,0:T(8,128)S(1)}, u32[]{:S(2)}, u32[]{:S(2)}) collective-permute-start(f32[72,512]{1,0:T(8,128)S(1)} %collective-permute-done.refs_0_), channel_id=1, source_target_pairs={{0,1},{1,0},{2,3},{3,2},{4,5},{5,4},{6,7},{7,6},{8,9},{9,8},{10,11... | collective-permute-start | bytes 442376 | tf_op jit(solution)/shard_map/ppermute | solution.py:695
  23.8 5.3 %collective-permute-start.6 = (f32[72,512]{1,0:T(8,128)S(1)}, f32[72,512]{1,0:T(8,128)S(1)}, u32[]{:S(2)}, u32[]{:S(2)}) collective-permute-start(f32[72,512]{1,0:T(8,128)S(1)} %collective-permute-done.1.refs_1_), channel_id=1, source_target_pairs={{0,1},{1,0},{2,3},{3,2},{4,5},{5,4},{6,7},{7,6},{8,9},{9,8},{10,11... | collective-permute-start | bytes 442376 | tf_op jit(solution)/shard_map/ppermute | solution.py:695
  24.2 5.6 %collective-permute-start.7 = (f32[72,512]{1,0:T(8,128)S(1)}, f32[72,512]{1,0:T(8,128)S(1)}, u32[]{:S(2)}, u32[]{:S(2)}) collective-permute-start(f32[72,512]{1,0:T(8,128)S(1)} %collective-permute-done.2.refs_2_), channel_id=1, source_target_pairs={{0,1},{1,0},{2,3},{3,2},{4,5},{5,4},{6,7},{7,6},{8,9},{9,8},{10,11... | collective-permute-start | bytes 442376 | tf_op jit(solution)/shard_map/ppermute | solution.py:695
  24.3 5.7 %collective-permute-start.8 = (f32[72,512]{1,0:T(8,128)S(1)}, f32[72,512]{1,0:T(8,128)S(1)}, u32[]{:S(2)}, u32[]{:S(2)}) collective-permute-start(f32[72,512]{1,0:T(8,128)S(1)} %collective-permute-done.3.refs_3_), channel_id=1, source_target_pairs={{0,1},{1,0},{2,3},{3,2},{4,5},{5,4},{6,7},{7,6},{8,9},{9,8},{10,11... | collective-permute-start | bytes 442376 | tf_op jit(solution)/shard_map/ppermute | solution.py:695
  24.7 13.2 %collective-permute-start.9 = (f32[64,512]{1,0:T(8,128)S(1)}, f32[64,512]{1,0:T(8,128)S(1)}, u32[]{:S(2)}, u32[]{:S(2)}) collective-permute-start(f32[64,512]{1,0:T(8,128)S(1)} %get-tuple-element.66), channel_id=1, source_target_pairs={{0,4},{1,13},{2,6},{3,15},{4,0},{5,9},{6,2},{7,11},{8,12},{9,5},{1... | collective-permute-start | bytes 393224 | tf_op jit(solution)/shard_map/ppermute | solution.py:692
  27.6 10.4 %collective-permute-start.10 = (f32[64,512]{1,0:T(8,128)S(1)}, f32[64,512]{1,0:T(8,128)S(1)}, u32[]{:S(2)}, u32[]{:S(2)}) collective-permute-start(f32[64,512]{1,0:T(8,128)S(1)} %get-tuple-element.67), channel_id=1, source_target_pairs={{0,6},{1,15},{2,4},{3,13},{4,2},{5,11},{6,0},{7,9},{8,14},{9,7},{1... | collective-permute-start | bytes 393224 | tf_op jit(solution)/shard_map/ppermute | solution.py:692
  29.1 8.9 %collective-permute-start.11 = (f32[64,512]{1,0:T(8,128)S(1)}, f32[64,512]{1,0:T(8,128)S(1)}, u32[]{:S(2)}, u32[]{:S(2)}) collective-permute-start(f32[64,512]{1,0:T(8,128)S(1)} %get-tuple-element.68), channel_id=1, source_target_pairs={{0,0},{1,9},{2,2},{3,11},{4,4},{5,13},{6,6},{7,15},{8,8},{9,1},{10... | collective-permute-start | bytes 393224 | tf_op jit(solution)/shard_map/ppermute | solution.py:692
  29.8 10.5 %collective-permute-start.12 = (f32[64,512]{1,0:T(8,128)S(1)}, f32[64,512]{1,0:T(8,128)S(1)}, u32[]{:S(2)}, u32[]{:S(2)}) collective-permute-start(f32[64,512]{1,0:T(8,128)S(1)} %get-tuple-element.69), channel_id=1, source_target_pairs={{0,2},{1,11},{2,0},{3,9},{4,6},{5,15},{6,4},{7,13},{8,10},{9,3},{1... | collective-permute-start | bytes 393224 | tf_op jit(solution)/shard_map/ppermute | solution.py:692
  40.3 1.5 %collective-permute-start.13 = (f32[64,512]{1,0:T(8,128)S(1)}, f32[64,512]{1,0:T(8,128)S(1)}, u32[]{:S(2)}, u32[]{:S(2)}) collective-permute-start(f32[64,512]{1,0:T(8,128)S(1)} %collective-permute-done.9.refs_0_), channel_id=1, source_target_pairs={{0,1},{1,0},{2,3},{3,2},{4,5},{5,4},{6,7},{7,6},{8,9},{9,8},{10,11... | collective-permute-start | bytes 393224 | tf_op jit(solution)/shard_map/ppermute | solution.py:695
  45.6 8.4 %collective-permute-start.17 = (f32[136,128]{1,0:T(8,128)S(1)}, f32[136,128]{1,0:T(8,128)S(1)}, u32[]{:S(2)}, u32[]{:S(2)}) collective-permute-start(f32[136,128]{1,0:T(8,128)S(1)} %get-tuple-element.76), channel_id=1, source_target_pairs={{0,8},{8,0},{1,9},{9,1},{2,10},{10,2},{3,11},{11,3},{4,12},{12,4},... | collective-permute-start | bytes 208904 | tf_op jit(solution)/shard_map/ppermute | solution.py:638
  56.2 2.0 %collective-permute-start.18 = (f32[4,64,512]{2,1,0:T(8,128)S(1)}, f32[4,64,512]{2,1,0:T(8,128)S(1)}, u32[]{:S(2)}, u32[]{:S(2)}) collective-permute-start(f32[4,64,512]{2,1,0:T(8,128)S(1)} %get-tuple-element.86), channel_id=1, source_target_pairs={{0,1},{1,0},{2,3},{3,2},{4,5},{5,4},{6,7},{7,6},{8,9},{9,8},{10,11... | collective-permute-start | bytes 1572872 | tf_op jit(solution)/shard_map/ppermute | solution.py:695
  58.2 13.0 %collective-permute-start.19 = (f32[64,512]{1,0:T(8,128)S(1)}, f32[64,512]{1,0:T(8,128)S(1)}, u32[]{:S(2)}, u32[]{:S(2)}) collective-permute-start(f32[64,512]{1,0:T(8,128)S(1)} %get-tuple-element.87), channel_id=1, source_target_pairs={{0,4},{1,13},{2,6},{3,15},{4,0},{5,9},{6,2},{7,11},{8,12},{9,5},{1... | collective-permute-start | bytes 393224 | tf_op jit(solution)/shard_map/ppermute | solution.py:692
  61.2 10.0 %collective-permute-start.20 = (f32[64,512]{1,0:T(8,128)S(1)}, f32[64,512]{1,0:T(8,128)S(1)}, u32[]{:S(2)}, u32[]{:S(2)}) collective-permute-start(f32[64,512]{1,0:T(8,128)S(1)} %get-tuple-element.88), channel_id=1, source_target_pairs={{0,6},{1,15},{2,4},{3,13},{4,2},{5,11},{6,0},{7,9},{8,14},{9,7},{1... | collective-permute-start | bytes 393224 | tf_op jit(solution)/shard_map/ppermute | solution.py:692
  62.2 9.5 %collective-permute-start.21 = (f32[64,512]{1,0:T(8,128)S(1)}, f32[64,512]{1,0:T(8,128)S(1)}, u32[]{:S(2)}, u32[]{:S(2)}) collective-permute-start(f32[64,512]{1,0:T(8,128)S(1)} %get-tuple-element.89), channel_id=1, source_target_pairs={{0,0},{1,9},{2,2},{3,11},{4,4},{5,13},{6,6},{7,15},{8,8},{9,1},{10... | collective-permute-start | bytes 393224 | tf_op jit(solution)/shard_map/ppermute | solution.py:692
  62.9 10.4 %collective-permute-start.22 = (f32[64,512]{1,0:T(8,128)S(1)}, f32[64,512]{1,0:T(8,128)S(1)}, u32[]{:S(2)}, u32[]{:S(2)}) collective-permute-start(f32[64,512]{1,0:T(8,128)S(1)} %get-tuple-element.90), channel_id=1, source_target_pairs={{0,2},{1,11},{2,0},{3,9},{4,6},{5,15},{6,4},{7,13},{8,10},{9,3},{1... | collective-permute-start | bytes 393224 | tf_op jit(solution)/shard_map/ppermute | solution.py:692
  71.2 2.6 %collective-permute-start.23 = (f32[64,512]{1,0:T(8,128)S(1)}, f32[64,512]{1,0:T(8,128)S(1)}, u32[]{:S(2)}, u32[]{:S(2)}) collective-permute-start(f32[64,512]{1,0:T(8,128)S(1)} %collective-permute-done.19.refs_0_), channel_id=1, source_target_pairs={{0,1},{1,0},{2,3},{3,2},{4,5},{5,4},{6,7},{7,6},{8,9},{9,8},{10,11... | collective-permute-start | bytes 393224 | tf_op jit(solution)/shard_map/ppermute | solution.py:695
  71.2 2.6 %collective-permute-start.24 = (f32[64,512]{1,0:T(8,128)S(1)}, f32[64,512]{1,0:T(8,128)S(1)}, u32[]{:S(2)}, u32[]{:S(2)}) collective-permute-start(f32[64,512]{1,0:T(8,128)S(1)} %collective-permute-done.20.refs_1_), channel_id=1, source_target_pairs={{0,1},{1,0},{2,3},{3,2},{4,5},{5,4},{6,7},{7,6},{8,9},{9,8},{10,11... | collective-permute-start | bytes 393224 | tf_op jit(solution)/shard_map/ppermute | solution.py:695
  71.7 2.1 %collective-permute-start.25 = (f32[64,512]{1,0:T(8,128)S(1)}, f32[64,512]{1,0:T(8,128)S(1)}, u32[]{:S(2)}, u32[]{:S(2)}) collective-permute-start(f32[64,512]{1,0:T(8,128)S(1)} %collective-permute-done.21.refs_2_), channel_id=1, source_target_pairs={{0,1},{1,0},{2,3},{3,2},{4,5},{5,4},{6,7},{7,6},{8,9},{9,8},{10,11... | collective-permute-start | bytes 393224 | tf_op jit(solution)/shard_map/ppermute | solution.py:695
  73.3 1.5 %collective-permute-start.26 = (f32[64,512]{1,0:T(8,128)S(1)}, f32[64,512]{1,0:T(8,128)S(1)}, u32[]{:S(2)}, u32[]{:S(2)}) collective-permute-start(f32[64,512]{1,0:T(8,128)S(1)} %collective-permute-done.22.refs_3_), channel_id=1, source_target_pairs={{0,1},{1,0},{2,3},{3,2},{4,5},{5,4},{6,7},{7,6},{8,9},{9,8},{10,11... | collective-permute-start | bytes 393224 | tf_op jit(solution)/shard_map/ppermute | solution.py:695
  (5 other events, 45.9 us)

commit v17 on v16

--- a/solution.py
+++ b/solution.py
@@ -13,7 +13,7 @@
 LANES = 128
 FEAT = 256
 LOW = 256
-AHEAD = 8
+AHEAD = 4
 COORD = 144
 
 highest = lax.Precision.HIGHEST
@@ -714,14 +714,14 @@
         )(in_hbm(pos), in_hbm(weights))
 
     if fine:
-        kept, sent = sorted_light(pos)
-        place, kept, sent = lax.optimization_barrier((swap(place, 0), kept, sent))
-        place = {0: place}
+        place = {0: swap(place, 0)}
         stride = blocks // 2
         while stride:
             for step in sorted(place):
                 place[step | stride] = lax.ppermute(place[step], "sub", [(i, i ^ stride) for i in range(blocks)])
             stride //= 2
+        kept, sent = sorted_light(pos)
+        place, kept, sent = lax.optimization_barrier((place, kept, sent))
         light = pl.pallas_call(
             join_kernel,
             out_shape=(shaped((cols, part), f32),) * blocks,
@@ -730,7 +730,6 @@
             compiler_params=params(40),
             name="join_cores",
         )(kept, other_core(sent))
-        place, light = lax.optimization_barrier((place, light))
         theirs = {step: other_core(one) for step, one in place.items()}
         place = [place[step] for step in range(blocks)] + [theirs[step] for step in range(blocks)]
         light = [swap(light[step], step) for step in far_first(blocks)]

time: 77.1 us -> 74 us (0.960)
  starting transfers between devices: 26.8 us -> 23.5 us
  waiting for transfers between devices: 22.9 us -> 24.3 us
  Pallas kernels: 26.9 us -> 25.9 us
    ppermute x3, starting transfers between devices: 8.46 us -> 6.51 us  [body(): lax.ppermute(place[step], 'sub', [(i, i ^ stride) for i in range(blocks)])]
    ppermute x9, waiting for transfers between devices: 11.9 us -> 13.8 us  [swap(): return lax.ppermute(value, axes, pairs)]
    ppermute x9, starting transfers between devices: 11.8 us -> 10.7 us  [swap(): return lax.ppermute(value, axes, pairs)]
  transfers between devices with their start and end apart: 27 -> 27, of which waited for: 12 -> 13; matrix products, arithmetic and copies ran while one was open for 0% -> 0% of each run, Pallas kernels for 22% -> 22%
where the time goes in v17:
time: 74 us; the launch traced here: 73.9 us
  Pallas kernels  25.9 us (35%)
  waiting for transfers between devices  24.3 us (33%)
  starting transfers between devices  23.5 us (32%)
    ppermute x9, waiting for transfers between devices, swap(): return lax.ppermute(value, axes, pairs)  13.8 us
    ppermute x9, starting transfers between devices, swap(): return lax.ppermute(value, axes, pairs)  10.7 us
    pallas_call x1, Pallas kernels, body(): pl.pallas_call(functools.partial(near_kernel, layout), out_shape=vm((cols...  7.14 us
    pallas_call x1, Pallas kernels, body(): pl.pallas_call(functools.partial(points_kernel, layout, trees), out_shape...  7.11 us
    ppermute x3, starting transfers between devices, body(): lax.ppermute(place[step], 'sub', [(i, i ^ stride) for i in range(blocks)])  6.51 us
    ppermute x3, waiting for transfers between devices, body(): lax.ppermute(place[step], 'sub', [(i, i ^ stride) for i in range(blocks)])  6.25 us
    ppermute x14, starting transfers between devices, other_core(): return lax.ppermute(value, 'rep', [(0, 1), (1, 0)])  5.15 us
    ppermute x14, waiting for transfers between devices, other_core(): return lax.ppermute(value, 'rep', [(0, 1), (1, 0)])  4.29 us
  transfers between devices with their start and end apart: 27, of which 13 were waited for; matrix products, arithmetic and copies ran while one was open for 0% of the time, Pallas kernels for 22%

profile of v17, /device:TPU:0, one launch (start us, length us, event | category | flops | bytes accessed | tf_op | source)
XLA Modules:
  0.0 73.9 jit_solution(9738930404379292839)
XLA Ops:
  0.0 2.7 %sort_points.1 = (f32[72,512]{1,0:T(8,128)}, f32[8,128]{1,0:T(8,128)}) custom-call(s32[8,128]{1,0:T(8,128)} %bitcast.6, f32[64,1024]{1,0:T(8,128)} %bitcast.5, s32[1,128]{1,0:T(1,128)} %base_ref.1, s32[2,3]{1,0:T(2,128)} %flag_ref.1), custom_call_target="tpu_custom_call" | custom-call | tf_op jit(solution)/shard_map/sort_points/pallas_call | solution.py:674
  2.7 1.6 %collective-permute-start = (f32[72,512]{1,0:T(8,128)}, f32[72,512]{1,0:T(8,128)S(1)}, u32[]{:S(2)}, u32[]{:S(2)}) collective-permute-start(f32[72,512]{1,0:T(8,128)} %get-tuple-element.44), channel_id=1, source_target_pairs={{0,0},{1,9},{2,2},{3,11},{4,4},{5,13},{6,6},{7,15},{8,8},{9,1},{10... | collective-permute-start | bytes 442376 | tf_op jit(solution)/shard_map/ppermute | solution.py:692
  4.3 4.0 %collective-permute-start.2 = (f32[72,512]{1,0:T(8,128)S(1)}, f32[72,512]{1,0:T(8,128)S(1)}, u32[]{:S(2)}, u32[]{:S(2)}) collective-permute-start(f32[72,512]{1,0:T(8,128)S(1)} %collective-permute-done.refs_0_), channel_id=1, source_target_pairs={{0,4},{2,6},{4,0},{6,2},{1,5},{3,7},{5,1},{7,3},{8,12},{10,14},{12... | collective-permute-start | bytes 442376 | tf_op jit(solution)/shard_map/ppermute | solution.py:721
  8.3 1.6 %collective-permute-start.1 = (f32[72,512]{1,0:T(8,128)S(1)}, f32[72,512]{1,0:T(8,128)S(1)}, u32[]{:S(2)}, u32[]{:S(2)}) collective-permute-start(f32[72,512]{1,0:T(8,128)S(1)} %collective-permute-done.refs_0_), channel_id=1, source_target_pairs={{0,2},{2,0},{4,6},{6,4},{1,3},{3,1},{5,7},{7,5},{8,10},{10,8},{12,... | collective-permute-start | bytes 442376 | tf_op jit(solution)/shard_map/ppermute | solution.py:721
  9.9 3.2 %collective-permute-done.2.refs_2_ = f32[72,512]{1,0:T(8,128)S(1)} collective-permute-done((f32[72,512]{1,0:T(8,128)S(1)}, f32[72,512]{1,0:T(8,128)S(1)}, u32[]{:S(2)}, u32[]{:S(2)}) %collective-permute-start.2) | collective-permute-done | bytes 147488 | tf_op jit(solution)/shard_map/ppermute | solution.py:721
  13.2 0.9 %collective-permute-start.3 = (f32[72,512]{1,0:T(8,128)S(1)}, f32[72,512]{1,0:T(8,128)S(1)}, u32[]{:S(2)}, u32[]{:S(2)}) collective-permute-start(f32[72,512]{1,0:T(8,128)S(1)} %collective-permute-done.2.refs_2_), channel_id=1, source_target_pairs={{0,2},{2,0},{4,6},{6,4},{1,3},{3,1},{5,7},{7,5},{8,10},{10,8},{12,... | collective-permute-start | bytes 442376 | tf_op jit(solution)/shard_map/ppermute | solution.py:721
  14.1 1.8 %sort_weights.1 = (f32[4,32,512]{2,1,0:T(8,128)S(1)}, f32[4,32,512]{2,1,0:T(8,128)S(1)}) custom-call(f32[8,128]{1,0:T(8,128)} %get-tuple-element.43.pos_ref, f32[1024,128]{1,0:T(8,128)} %refs_8_.1), custom_call_target="tpu_custom_call" | custom-call | tf_op jit(solution)/shard_map/sort_weights/pallas_call | solution.py:702
  15.9 3.0 %collective-permute-done.3.refs_3_ = f32[72,512]{1,0:T(8,128)S(1)} collective-permute-done((f32[72,512]{1,0:T(8,128)S(1)}, f32[72,512]{1,0:T(8,128)S(1)}, u32[]{:S(2)}, u32[]{:S(2)}) %collective-permute-start.3) | collective-permute-done | bytes 147488 | tf_op jit(solution)/shard_map/ppermute | solution.py:721
  18.9 2.0 %collective-permute-start.8 = (f32[4,32,512]{2,1,0:T(8,128)S(1)}, f32[4,32,512]{2,1,0:T(8,128)S(1)}, u32[]{:S(2)}, u32[]{:S(2)}) collective-permute-start(f32[4,32,512]{2,1,0:T(8,128)S(1)} %get-tuple-element.55), channel_id=1, source_target_pairs={{0,1},{1,0},{2,3},{3,2},{4,5},{5,4},{6,7},{7,6},{8,9},{9,8},{10,11... | collective-permute-start | bytes 786440 | tf_op jit(solution)/shard_map/ppermute | solution.py:695
  22.1 2.3 %collective-permute-start.9 = (f32[64,512]{1,0:T(8,128)S(1)}, f32[64,512]{1,0:T(8,128)S(1)}, u32[]{:S(2)}, u32[]{:S(2)}) collective-permute-start(f32[64,512]{1,0:T(8,128)S(1)} %get-tuple-element.56), channel_id=1, source_target_pairs={{0,4},{1,13},{2,6},{3,15},{4,0},{5,9},{6,2},{7,11},{8,12},{9,5},{1... | collective-permute-start | bytes 393224 | tf_op jit(solution)/shard_map/ppermute | solution.py:692
  24.5 1.3 %collective-permute-start.10 = (f32[64,512]{1,0:T(8,128)S(1)}, f32[64,512]{1,0:T(8,128)S(1)}, u32[]{:S(2)}, u32[]{:S(2)}) collective-permute-start(f32[64,512]{1,0:T(8,128)S(1)} %get-tuple-element.57), channel_id=1, source_target_pairs={{0,6},{1,15},{2,4},{3,13},{4,2},{5,11},{6,0},{7,9},{8,14},{9,7},{1... | collective-permute-start | bytes 393224 | tf_op jit(solution)/shard_map/ppermute | solution.py:692
  27.0 7.1 %tree_points.1 = (bf16[144,4096]{1,0:T(8,128)(2,1)S(1)}, bf16[4096,256]{1,0:T(8,128)(2,1)}, bf16[4,1024,128]{2,1,0:T(8,128)(2,1)}, bf16[896,256]{1,0:T(8,128)(2,...) custom-call(s32[1,8]{1,0:T(1,128)} %count_ref.1, ...), custom_call_target="tpu_custom_call" | custom-call | tf_op jit(solution)/shard_map/tree_points/pallas_call | solution.py:751
  34.1 0.8 %collective-permute-done.9.refs_0_ = f32[64,512]{1,0:T(8,128)S(1)} collective-permute-done((f32[64,512]{1,0:T(8,128)S(1)}, f32[64,512]{1,0:T(8,128)S(1)}, u32[]{:S(2)}, u32[]{:S(2)}) %collective-permute-start.9) | collective-permute-done | bytes 131104 | tf_op jit(solution)/shard_map/ppermute | solution.py:692
  34.9 2.7 %collective-permute-done.12.refs_3_ = f32[64,512]{1,0:T(8,128)S(1)} collective-permute-done((f32[64,512]{1,0:T(8,128)S(1)}, f32[64,512]{1,0:T(8,128)S(1)}, u32[]{:S(2)}, u32[]{:S(2)}) %collective-permute-start.12) | collective-permute-done | bytes 131104 | tf_op jit(solution)/shard_map/ppermute | solution.py:692
  39.9 2.9 %tree_weights.1 = (bf16[64,4096]{1,0:T(8,128)(2,1)S(1)}, bf16[128,896]{1,0:T(8,128)(2,1)S(1)}, f32[136,128]{1,0:T(8,128)S(1)}) custom-call(bf16[4,1024,128]{2,1,0:T(8,128)(2,1)} %get-tuple-element.51.base_hbm, f32[3,256,128]{2,1,0:T(8,128)S(1)} %get-tuple-element.52.upper_tiles_ref, f32[72,128]{1,0:T(8,128)S(1)} %get-tuple-element.53.top_ref, ...), custom_call_target="tpu_custom_call" | custom-call | tf_op jit(solution)/shard_map/tree_weights/pallas_call | solution.py:789
  42.8 1.1 %collective-permute-start.17 = (f32[136,128]{1,0:T(8,128)S(1)}, f32[136,128]{1,0:T(8,128)S(1)}, u32[]{:S(2)}, u32[]{:S(2)}) collective-permute-start(f32[136,128]{1,0:T(8,128)S(1)} %get-tuple-element.66), channel_id=1, source_target_pairs={{0,8},{8,0},{1,9},{9,1},{2,10},{10,2},{3,11},{11,3},{4,12},{12,4},... | collective-permute-start | bytes 208904 | tf_op jit(solution)/shard_map/ppermute | solution.py:638
  43.9 7.1 %near.1.near_ref = f32[64,2048]{1,0:T(8,128)S(1)} custom-call(s32[3,72]{1,0:T(4,128)} %get-tuple-element.71.tiles, bf16[4096,256]{1,0:T(8,128)(2,1)} %get-tuple-element.72.a_hbm, bf16[4,512,256]{2,1,0:T(8,128)(2,1)} %get-tuple-element.73.made_hbm, bf16[144,4096]{1,0:T(8,128)(2,1)S(1)} %get-tuple-element.68.tree_ref, bf16[64,4096]{1,0:T(8,128)(2,1)S(1)} %get-tuple-element.74.w_ref), custom_call_target="tpu_custom_call" | custom-call | tf_op jit(solution)/shard_map/near/pallas_call | solution.py:810
  51.1 2.2 %far.1 = (f32[4,64,512]{2,1,0:T(8,128)S(1)}, f32[4,64,512]{2,1,0:T(8,128)S(1)}) custom-call(f32[1,136,128]{2,1,0:T(8,128)S(1)} %bitcast.4, f32[4,1024]{1,0:T(4,128)S(1)} %get-tuple-element.61.slot_ref, f32[4,8,128]{2,1,0:T(8,128)S(1)} %get-tuple-element.67.info_ref, bf16[144,4096]{1,0:T(8,128)(2,1)S(1)} %get-tuple-element.68.tree_ref, ...), custom_call_target="tpu_custom_call" | custom-call | tf_op jit(solution)/shard_map/far/pallas_call | solution.py:828
  53.3 1.9 %collective-permute-done.18.got_ref = f32[4,64,512]{2,1,0:T(8,128)S(1)} collective-permute-done((f32[4,64,512]{2,1,0:T(8,128)S(1)}, f32[4,64,512]{2,1,0:T(8,128)S(1)}, u32[]{:S(2)}, u32[]{:S(2)}) %collective-permute-start.18) | collective-permute-done | bytes 524320 | tf_op jit(solution)/shard_map/ppermute | solution.py:695
  55.3 2.5 %collective-permute-start.19 = (f32[64,512]{1,0:T(8,128)S(1)}, f32[64,512]{1,0:T(8,128)S(1)}, u32[]{:S(2)}, u32[]{:S(2)}) collective-permute-start(f32[64,512]{1,0:T(8,128)S(1)} %get-tuple-element.77), channel_id=1, source_target_pairs={{0,4},{1,13},{2,6},{3,15},{4,0},{5,9},{6,2},{7,11},{8,12},{9,5},{1... | collective-permute-start | bytes 393224 | tf_op jit(solution)/shard_map/ppermute | solution.py:692
  59.7 8.6 %collective-permute-done.19.refs_0_ = f32[64,512]{1,0:T(8,128)S(1)} collective-permute-done((f32[64,512]{1,0:T(8,128)S(1)}, f32[64,512]{1,0:T(8,128)S(1)}, u32[]{:S(2)}, u32[]{:S(2)}) %collective-permute-start.19) | collective-permute-done | bytes 131104 | tf_op jit(solution)/shard_map/ppermute | solution.py:692
  68.9 1.7 %collective-permute-done.22.refs_3_ = f32[64,512]{1,0:T(8,128)S(1)} collective-permute-done((f32[64,512]{1,0:T(8,128)S(1)}, f32[64,512]{1,0:T(8,128)S(1)}, u32[]{:S(2)}, u32[]{:S(2)}) %collective-permute-start.22) | collective-permute-done | bytes 131104 | tf_op jit(solution)/shard_map/ppermute | solution.py:692
  70.9 1.0 %collective-permute-done.26.refs_7_ = f32[64,512]{1,0:T(8,128)S(1)} collective-permute-done((f32[64,512]{1,0:T(8,128)S(1)}, f32[64,512]{1,0:T(8,128)S(1)}, u32[]{:S(2)}, u32[]{:S(2)}) %collective-permute-start.26) | collective-permute-done | bytes 131104 | tf_op jit(solution)/shard_map/ppermute | solution.py:695
  71.9 1.9 %to_input_order.1 = f32[1024,128]{1,0:T(8,128)} custom-call(f32[8,128]{1,0:T(8,128)S(1)} %copy-done.1, f32[64,512]{1,0:T(8,128)S(1)} %collective-permute-done.19.refs_0_, f32[64,512]{1,0:T(8,128)S(1)} %collective-permute-done.20.refs_1_, f32[64,512]{1,0:T(8,128)S(1)} %collective-permute-done.21.refs_2_, f32[64,512]{1,0:T(8,128)S(1)} %collective-permute-done.22.refs_3_, ...), custom_call_target="tpu_custom_call" | custom-call | tf_op jit(solution)/shard_map/to_input_order/pallas_call | solution.py:865
  (43 shorter events, 7.7 us)
Async XLA Ops:
  2.7 1.6 %collective-permute-start = (f32[72,512]{1,0:T(8,128)}, f32[72,512]{1,0:T(8,128)S(1)}, u32[]{:S(2)}, u32[]{:S(2)}) collective-permute-start(f32[72,512]{1,0:T(8,128)} %get-tuple-element.44), channel_id=1, source_target_pairs={{0,0},{1,9},{2,2},{3,11},{4,4},{5,13},{6,6},{7,15},{8,8},{9,1},{10... | collective-permute-start | bytes 442376 | tf_op jit(solution)/shard_map/ppermute | solution.py:692
  4.3 8.8 %collective-permute-start.2 = (f32[72,512]{1,0:T(8,128)S(1)}, f32[72,512]{1,0:T(8,128)S(1)}, u32[]{:S(2)}, u32[]{:S(2)}) collective-permute-start(f32[72,512]{1,0:T(8,128)S(1)} %collective-permute-done.refs_0_), channel_id=1, source_target_pairs={{0,4},{2,6},{4,0},{6,2},{1,5},{3,7},{5,1},{7,3},{8,12},{10,14},{12... | collective-permute-start | bytes 442376 | tf_op jit(solution)/shard_map/ppermute | solution.py:721
  8.3 7.5 %collective-permute-start.1 = (f32[72,512]{1,0:T(8,128)S(1)}, f32[72,512]{1,0:T(8,128)S(1)}, u32[]{:S(2)}, u32[]{:S(2)}) collective-permute-start(f32[72,512]{1,0:T(8,128)S(1)} %collective-permute-done.refs_0_), channel_id=1, source_target_pairs={{0,2},{2,0},{4,6},{6,4},{1,3},{3,1},{5,7},{7,5},{8,10},{10,8},{12,... | collective-permute-start | bytes 442376 | tf_op jit(solution)/shard_map/ppermute | solution.py:721
  13.2 5.7 %collective-permute-start.3 = (f32[72,512]{1,0:T(8,128)S(1)}, f32[72,512]{1,0:T(8,128)S(1)}, u32[]{:S(2)}, u32[]{:S(2)}) collective-permute-start(f32[72,512]{1,0:T(8,128)S(1)} %collective-permute-done.2.refs_2_), channel_id=1, source_target_pairs={{0,2},{2,0},{4,6},{6,4},{1,3},{3,1},{5,7},{7,5},{8,10},{10,8},{12,... | collective-permute-start | bytes 442376 | tf_op jit(solution)/shard_map/ppermute | solution.py:721
  18.9 3.2 %collective-permute-start.8 = (f32[4,32,512]{2,1,0:T(8,128)S(1)}, f32[4,32,512]{2,1,0:T(8,128)S(1)}, u32[]{:S(2)}, u32[]{:S(2)}) collective-permute-start(f32[4,32,512]{2,1,0:T(8,128)S(1)} %get-tuple-element.55), channel_id=1, source_target_pairs={{0,1},{1,0},{2,3},{3,2},{4,5},{5,4},{6,7},{7,6},{8,9},{9,8},{10,11... | collective-permute-start | bytes 786440 | tf_op jit(solution)/shard_map/ppermute | solution.py:695
  20.9 3.5 %collective-permute-start.4 = (f32[72,512]{1,0:T(8,128)S(1)}, f32[72,512]{1,0:T(8,128)S(1)}, u32[]{:S(2)}, u32[]{:S(2)}) collective-permute-start(f32[72,512]{1,0:T(8,128)S(1)} %collective-permute-done.refs_0_), channel_id=1, source_target_pairs={{0,1},{1,0},{2,3},{3,2},{4,5},{5,4},{6,7},{7,6},{8,9},{9,8},{10,11... | collective-permute-start | bytes 442376 | tf_op jit(solution)/shard_map/ppermute | solution.py:695
  20.9 4.8 %collective-permute-start.5 = (f32[72,512]{1,0:T(8,128)S(1)}, f32[72,512]{1,0:T(8,128)S(1)}, u32[]{:S(2)}, u32[]{:S(2)}) collective-permute-start(f32[72,512]{1,0:T(8,128)S(1)} %collective-permute-done.1.refs_1_), channel_id=1, source_target_pairs={{0,1},{1,0},{2,3},{3,2},{4,5},{5,4},{6,7},{7,6},{8,9},{9,8},{10,11... | collective-permute-start | bytes 442376 | tf_op jit(solution)/shard_map/ppermute | solution.py:695
  21.4 5.0 %collective-permute-start.6 = (f32[72,512]{1,0:T(8,128)S(1)}, f32[72,512]{1,0:T(8,128)S(1)}, u32[]{:S(2)}, u32[]{:S(2)}) collective-permute-start(f32[72,512]{1,0:T(8,128)S(1)} %collective-permute-done.2.refs_2_), channel_id=1, source_target_pairs={{0,1},{1,0},{2,3},{3,2},{4,5},{5,4},{6,7},{7,6},{8,9},{9,8},{10,11... | collective-permute-start | bytes 442376 | tf_op jit(solution)/shard_map/ppermute | solution.py:695
  21.4 5.5 %collective-permute-start.7 = (f32[72,512]{1,0:T(8,128)S(1)}, f32[72,512]{1,0:T(8,128)S(1)}, u32[]{:S(2)}, u32[]{:S(2)}) collective-permute-start(f32[72,512]{1,0:T(8,128)S(1)} %collective-permute-done.3.refs_3_), channel_id=1, source_target_pairs={{0,1},{1,0},{2,3},{3,2},{4,5},{5,4},{6,7},{7,6},{8,9},{9,8},{10,11... | collective-permute-start | bytes 442376 | tf_op jit(solution)/shard_map/ppermute | solution.py:695
  22.1 12.8 %collective-permute-start.9 = (f32[64,512]{1,0:T(8,128)S(1)}, f32[64,512]{1,0:T(8,128)S(1)}, u32[]{:S(2)}, u32[]{:S(2)}) collective-permute-start(f32[64,512]{1,0:T(8,128)S(1)} %get-tuple-element.56), channel_id=1, source_target_pairs={{0,4},{1,13},{2,6},{3,15},{4,0},{5,9},{6,2},{7,11},{8,12},{9,5},{1... | collective-permute-start | bytes 393224 | tf_op jit(solution)/shard_map/ppermute | solution.py:692
  24.5 10.4 %collective-permute-start.10 = (f32[64,512]{1,0:T(8,128)S(1)}, f32[64,512]{1,0:T(8,128)S(1)}, u32[]{:S(2)}, u32[]{:S(2)}) collective-permute-start(f32[64,512]{1,0:T(8,128)S(1)} %get-tuple-element.57), channel_id=1, source_target_pairs={{0,6},{1,15},{2,4},{3,13},{4,2},{5,11},{6,0},{7,9},{8,14},{9,7},{1... | collective-permute-start | bytes 393224 | tf_op jit(solution)/shard_map/ppermute | solution.py:692
  25.7 9.1 %collective-permute-start.11 = (f32[64,512]{1,0:T(8,128)S(1)}, f32[64,512]{1,0:T(8,128)S(1)}, u32[]{:S(2)}, u32[]{:S(2)}) collective-permute-start(f32[64,512]{1,0:T(8,128)S(1)} %get-tuple-element.58), channel_id=1, source_target_pairs={{0,0},{1,9},{2,2},{3,11},{4,4},{5,13},{6,6},{7,15},{8,8},{9,1},{10... | collective-permute-start | bytes 393224 | tf_op jit(solution)/shard_map/ppermute | solution.py:692
  26.4 11.2 %collective-permute-start.12 = (f32[64,512]{1,0:T(8,128)S(1)}, f32[64,512]{1,0:T(8,128)S(1)}, u32[]{:S(2)}, u32[]{:S(2)}) collective-permute-start(f32[64,512]{1,0:T(8,128)S(1)} %get-tuple-element.59), channel_id=1, source_target_pairs={{0,2},{1,11},{2,0},{3,9},{4,6},{5,15},{6,4},{7,13},{8,10},{9,3},{1... | collective-permute-start | bytes 393224 | tf_op jit(solution)/shard_map/ppermute | solution.py:692
  37.6 1.4 %collective-permute-start.13 = (f32[64,512]{1,0:T(8,128)S(1)}, f32[64,512]{1,0:T(8,128)S(1)}, u32[]{:S(2)}, u32[]{:S(2)}) collective-permute-start(f32[64,512]{1,0:T(8,128)S(1)} %collective-permute-done.9.refs_0_), channel_id=1, source_target_pairs={{0,1},{1,0},{2,3},{3,2},{4,5},{5,4},{6,7},{7,6},{8,9},{9,8},{10,11... | collective-permute-start | bytes 393224 | tf_op jit(solution)/shard_map/ppermute | solution.py:695
  38.1 1.4 %collective-permute-start.15 = (f32[64,512]{1,0:T(8,128)S(1)}, f32[64,512]{1,0:T(8,128)S(1)}, u32[]{:S(2)}, u32[]{:S(2)}) collective-permute-start(f32[64,512]{1,0:T(8,128)S(1)} %collective-permute-done.11.refs_2_), channel_id=1, source_target_pairs={{0,1},{1,0},{2,3},{3,2},{4,5},{5,4},{6,7},{7,6},{8,9},{9,8},{10,11... | collective-permute-start | bytes 393224 | tf_op jit(solution)/shard_map/ppermute | solution.py:695
  42.8 8.3 %collective-permute-start.17 = (f32[136,128]{1,0:T(8,128)S(1)}, f32[136,128]{1,0:T(8,128)S(1)}, u32[]{:S(2)}, u32[]{:S(2)}) collective-permute-start(f32[136,128]{1,0:T(8,128)S(1)} %get-tuple-element.66), channel_id=1, source_target_pairs={{0,8},{8,0},{1,9},{9,1},{2,10},{10,2},{3,11},{11,3},{4,12},{12,4},... | collective-permute-start | bytes 208904 | tf_op jit(solution)/shard_map/ppermute | solution.py:638
  53.3 2.0 %collective-permute-start.18 = (f32[4,64,512]{2,1,0:T(8,128)S(1)}, f32[4,64,512]{2,1,0:T(8,128)S(1)}, u32[]{:S(2)}, u32[]{:S(2)}) collective-permute-start(f32[4,64,512]{2,1,0:T(8,128)S(1)} %get-tuple-element.76), channel_id=1, source_target_pairs={{0,1},{1,0},{2,3},{3,2},{4,5},{5,4},{6,7},{7,6},{8,9},{9,8},{10,11... | collective-permute-start | bytes 1572872 | tf_op jit(solution)/shard_map/ppermute | solution.py:695
  55.3 13.0 %collective-permute-start.19 = (f32[64,512]{1,0:T(8,128)S(1)}, f32[64,512]{1,0:T(8,128)S(1)}, u32[]{:S(2)}, u32[]{:S(2)}) collective-permute-start(f32[64,512]{1,0:T(8,128)S(1)} %get-tuple-element.77), channel_id=1, source_target_pairs={{0,4},{1,13},{2,6},{3,15},{4,0},{5,9},{6,2},{7,11},{8,12},{9,5},{1... | collective-permute-start | bytes 393224 | tf_op jit(solution)/shard_map/ppermute | solution.py:692
  57.8 10.5 %collective-permute-start.20 = (f32[64,512]{1,0:T(8,128)S(1)}, f32[64,512]{1,0:T(8,128)S(1)}, u32[]{:S(2)}, u32[]{:S(2)}) collective-permute-start(f32[64,512]{1,0:T(8,128)S(1)} %get-tuple-element.78), channel_id=1, source_target_pairs={{0,6},{1,15},{2,4},{3,13},{4,2},{5,11},{6,0},{7,9},{8,14},{9,7},{1... | collective-permute-start | bytes 393224 | tf_op jit(solution)/shard_map/ppermute | solution.py:692
  58.5 10.3 %collective-permute-start.21 = (f32[64,512]{1,0:T(8,128)S(1)}, f32[64,512]{1,0:T(8,128)S(1)}, u32[]{:S(2)}, u32[]{:S(2)}) collective-permute-start(f32[64,512]{1,0:T(8,128)S(1)} %get-tuple-element.79), channel_id=1, source_target_pairs={{0,0},{1,9},{2,2},{3,11},{4,4},{5,13},{6,6},{7,15},{8,8},{9,1},{10... | collective-permute-start | bytes 393224 | tf_op jit(solution)/shard_map/ppermute | solution.py:692
  59.1 11.4 %collective-permute-start.22 = (f32[64,512]{1,0:T(8,128)S(1)}, f32[64,512]{1,0:T(8,128)S(1)}, u32[]{:S(2)}, u32[]{:S(2)}) collective-permute-start(f32[64,512]{1,0:T(8,128)S(1)} %get-tuple-element.80), channel_id=1, source_target_pairs={{0,2},{1,11},{2,0},{3,9},{4,6},{5,15},{6,4},{7,13},{8,10},{9,3},{1... | collective-permute-start | bytes 393224 | tf_op jit(solution)/shard_map/ppermute | solution.py:692
  68.3 2.7 %collective-permute-start.23 = (f32[64,512]{1,0:T(8,128)S(1)}, f32[64,512]{1,0:T(8,128)S(1)}, u32[]{:S(2)}, u32[]{:S(2)}) collective-permute-start(f32[64,512]{1,0:T(8,128)S(1)} %collective-permute-done.19.refs_0_), channel_id=1, source_target_pairs={{0,1},{1,0},{2,3},{3,2},{4,5},{5,4},{6,7},{7,6},{8,9},{9,8},{10,11... | collective-permute-start | bytes 393224 | tf_op jit(solution)/shard_map/ppermute | solution.py:695
  68.3 2.6 %collective-permute-start.24 = (f32[64,512]{1,0:T(8,128)S(1)}, f32[64,512]{1,0:T(8,128)S(1)}, u32[]{:S(2)}, u32[]{:S(2)}) collective-permute-start(f32[64,512]{1,0:T(8,128)S(1)} %collective-permute-done.20.refs_1_), channel_id=1, source_target_pairs={{0,1},{1,0},{2,3},{3,2},{4,5},{5,4},{6,7},{7,6},{8,9},{9,8},{10,11... | collective-permute-start | bytes 393224 | tf_op jit(solution)/shard_map/ppermute | solution.py:695
  68.8 2.1 %collective-permute-start.25 = (f32[64,512]{1,0:T(8,128)S(1)}, f32[64,512]{1,0:T(8,128)S(1)}, u32[]{:S(2)}, u32[]{:S(2)}) collective-permute-start(f32[64,512]{1,0:T(8,128)S(1)} %collective-permute-done.21.refs_2_), channel_id=1, source_target_pairs={{0,1},{1,0},{2,3},{3,2},{4,5},{5,4},{6,7},{7,6},{8,9},{9,8},{10,11... | collective-permute-start | bytes 393224 | tf_op jit(solution)/shard_map/ppermute | solution.py:695
  (5 other events, 45.8 us)

commit v18 on v17

--- a/solution.py
+++ b/solution.py
@@ -13,7 +13,7 @@
 LANES = 128
 FEAT = 256
 LOW = 256
-AHEAD = 4
+AHEAD = 8
 COORD = 144
 
 highest = lax.Precision.HIGHEST
@@ -784,8 +784,11 @@
     )(in_hbm(near_count), in_hbm(near_list[0]), in_hbm(skeleton_upper), *small, *place)
 
     if fine:
-        light, slots = lax.optimization_barrier((light, slots))
-        light = light + [other_core(one) for one in light]
+        theirs = []
+        for step in range(blocks):
+            light[step], slots = lax.optimization_barrier((light[step], slots))
+            theirs.append(other_core(light[step]))
+        light = light + theirs
     tree_light, coefs, pack = pl.pallas_call(
         functools.partial(weights_kernel, layout),
         out_shape=(

time: 74 us -> 74.2 us (level)
  waiting for transfers between devices: 24.3 us -> 23.4 us
    ppermute x9, waiting for transfers between devices: 13.8 us -> 12.8 us  [swap(): return lax.ppermute(value, axes, pairs)]
    pallas_call x1, Pallas kernels: 7.11 us -> 7.87 us  [body(): pl.pallas_call(functools.partial(points_kernel, layout, trees), out_shape...]
  transfers between devices with their start and end apart: 27 -> 27, of which waited for: 13 -> 12; matrix products, arithmetic and copies ran while one was open for 0% -> 0% of each run, Pallas kernels for 22% -> 23%
where the time goes in v18:
time: 74.2 us; the launch traced here: 73.9 us
  Pallas kernels  26.6 us (36%)
  starting transfers between devices  23.7 us (32%)
  waiting for transfers between devices  23.4 us (32%)
    ppermute x9, waiting for transfers between devices, swap(): return lax.ppermute(value, axes, pairs)  12.8 us
    ppermute x9, starting transfers between devices, swap(): return lax.ppermute(value, axes, pairs)  11 us
    pallas_call x1, Pallas kernels, body(): pl.pallas_call(functools.partial(points_kernel, layout, trees), out_shape...  7.87 us
    pallas_call x1, Pallas kernels, body(): pl.pallas_call(functools.partial(near_kernel, layout), out_shape=vm((cols...  7.15 us
    ppermute x3, starting transfers between devices, body(): lax.ppermute(place[step], 'sub', [(i, i ^ stride) for i in range(blocks)])  6.51 us
    ppermute x3, waiting for transfers between devices, body(): lax.ppermute(place[step], 'sub', [(i, i ^ stride) for i in range(blocks)])  6.26 us
    ppermute x14, starting transfers between devices, other_core(): return lax.ppermute(value, 'rep', [(0, 1), (1, 0)])  5.16 us
    ppermute x14, waiting for transfers between devices, other_core(): return lax.ppermute(value, 'rep', [(0, 1), (1, 0)])  4.33 us
  transfers between devices with their start and end apart: 27, of which 12 were waited for; matrix products, arithmetic and copies ran while one was open for 0% of the time, Pallas kernels for 23%

profile of v18, /device:TPU:0, one launch (start us, length us, event | category | flops | bytes accessed | tf_op | source)
XLA Modules:
  0.0 73.9 jit_solution(11576681850565833590)
XLA Ops:
  0.0 2.7 %sort_points.1 = (f32[72,512]{1,0:T(8,128)}, f32[8,128]{1,0:T(8,128)}) custom-call(s32[8,128]{1,0:T(8,128)} %bitcast.6, f32[64,1024]{1,0:T(8,128)} %bitcast.5, s32[1,128]{1,0:T(1,128)} %base_ref.1, s32[2,3]{1,0:T(2,128)} %flag_ref.1), custom_call_target="tpu_custom_call" | custom-call | tf_op jit(solution)/shard_map/sort_points/pallas_call | solution.py:674
  2.7 1.6 %collective-permute-start = (f32[72,512]{1,0:T(8,128)}, f32[72,512]{1,0:T(8,128)S(1)}, u32[]{:S(2)}, u32[]{:S(2)}) collective-permute-start(f32[72,512]{1,0:T(8,128)} %get-tuple-element.47), channel_id=1, source_target_pairs={{0,0},{1,9},{2,2},{3,11},{4,4},{5,13},{6,6},{7,15},{8,8},{9,1},{10... | collective-permute-start | bytes 442376 | tf_op jit(solution)/shard_map/ppermute | solution.py:692
  4.3 4.0 %collective-permute-start.2 = (f32[72,512]{1,0:T(8,128)S(1)}, f32[72,512]{1,0:T(8,128)S(1)}, u32[]{:S(2)}, u32[]{:S(2)}) collective-permute-start(f32[72,512]{1,0:T(8,128)S(1)} %collective-permute-done.refs_0_), channel_id=1, source_target_pairs={{0,4},{2,6},{4,0},{6,2},{1,5},{3,7},{5,1},{7,3},{8,12},{10,14},{12... | collective-permute-start | bytes 442376 | tf_op jit(solution)/shard_map/ppermute | solution.py:721
  8.3 1.6 %collective-permute-start.1 = (f32[72,512]{1,0:T(8,128)S(1)}, f32[72,512]{1,0:T(8,128)S(1)}, u32[]{:S(2)}, u32[]{:S(2)}) collective-permute-start(f32[72,512]{1,0:T(8,128)S(1)} %collective-permute-done.refs_0_), channel_id=1, source_target_pairs={{0,2},{2,0},{4,6},{6,4},{1,3},{3,1},{5,7},{7,5},{8,10},{10,8},{12,... | collective-permute-start | bytes 442376 | tf_op jit(solution)/shard_map/ppermute | solution.py:721
  9.9 3.2 %collective-permute-done.2.refs_2_ = f32[72,512]{1,0:T(8,128)S(1)} collective-permute-done((f32[72,512]{1,0:T(8,128)S(1)}, f32[72,512]{1,0:T(8,128)S(1)}, u32[]{:S(2)}, u32[]{:S(2)}) %collective-permute-start.2) | collective-permute-done | bytes 147488 | tf_op jit(solution)/shard_map/ppermute | solution.py:721
  13.2 0.9 %collective-permute-start.3 = (f32[72,512]{1,0:T(8,128)S(1)}, f32[72,512]{1,0:T(8,128)S(1)}, u32[]{:S(2)}, u32[]{:S(2)}) collective-permute-start(f32[72,512]{1,0:T(8,128)S(1)} %collective-permute-done.2.refs_2_), channel_id=1, source_target_pairs={{0,2},{2,0},{4,6},{6,4},{1,3},{3,1},{5,7},{7,5},{8,10},{10,8},{12,... | collective-permute-start | bytes 442376 | tf_op jit(solution)/shard_map/ppermute | solution.py:721
  14.1 1.8 %sort_weights.1 = (f32[4,32,512]{2,1,0:T(8,128)S(1)}, f32[4,32,512]{2,1,0:T(8,128)S(1)}) custom-call(f32[8,128]{1,0:T(8,128)} %get-tuple-element.46.pos_ref, f32[1024,128]{1,0:T(8,128)} %refs_8_.1), custom_call_target="tpu_custom_call" | custom-call | tf_op jit(solution)/shard_map/sort_weights/pallas_call | solution.py:702
  15.9 3.0 %collective-permute-done.3.refs_3_ = f32[72,512]{1,0:T(8,128)S(1)} collective-permute-done((f32[72,512]{1,0:T(8,128)S(1)}, f32[72,512]{1,0:T(8,128)S(1)}, u32[]{:S(2)}, u32[]{:S(2)}) %collective-permute-start.3) | collective-permute-done | bytes 147488 | tf_op jit(solution)/shard_map/ppermute | solution.py:721
  18.9 2.0 %collective-permute-start.8 = (f32[4,32,512]{2,1,0:T(8,128)S(1)}, f32[4,32,512]{2,1,0:T(8,128)S(1)}, u32[]{:S(2)}, u32[]{:S(2)}) collective-permute-start(f32[4,32,512]{2,1,0:T(8,128)S(1)} %get-tuple-element.58), channel_id=1, source_target_pairs={{0,1},{1,0},{2,3},{3,2},{4,5},{5,4},{6,7},{7,6},{8,9},{9,8},{10,11... | collective-permute-start | bytes 786440 | tf_op jit(solution)/shard_map/ppermute | solution.py:695
  22.1 2.3 %collective-permute-start.12 = (f32[64,512]{1,0:T(8,128)S(1)}, f32[64,512]{1,0:T(8,128)S(1)}, u32[]{:S(2)}, u32[]{:S(2)}) collective-permute-start(f32[64,512]{1,0:T(8,128)S(1)} %get-tuple-element.62), channel_id=1, source_target_pairs={{0,4},{1,13},{2,6},{3,15},{4,0},{5,9},{6,2},{7,11},{8,12},{9,5},{1... | collective-permute-start | bytes 393224 | tf_op jit(solution)/shard_map/ppermute | solution.py:692
  24.5 1.3 %collective-permute-start.11 = (f32[64,512]{1,0:T(8,128)S(1)}, f32[64,512]{1,0:T(8,128)S(1)}, u32[]{:S(2)}, u32[]{:S(2)}) collective-permute-start(f32[64,512]{1,0:T(8,128)S(1)} %get-tuple-element.61), channel_id=1, source_target_pairs={{0,6},{1,15},{2,4},{3,13},{4,2},{5,11},{6,0},{7,9},{8,14},{9,7},{1... | collective-permute-start | bytes 393224 | tf_op jit(solution)/shard_map/ppermute | solution.py:692
  27.0 7.9 %tree_points.1 = (bf16[144,4096]{1,0:T(8,128)(2,1)S(1)}, bf16[4096,256]{1,0:T(8,128)(2,1)}, bf16[4,1024,128]{2,1,0:T(8,128)(2,1)}, bf16[896,256]{1,0:T(8,128)(2,...) custom-call(s32[1,8]{1,0:T(1,128)} %count_ref.1, ...), custom_call_target="tpu_custom_call" | custom-call | tf_op jit(solution)/shard_map/tree_points/pallas_call | solution.py:751
  34.9 2.7 %collective-permute-done.9.refs_3_ = f32[64,512]{1,0:T(8,128)S(1)} collective-permute-done((f32[64,512]{1,0:T(8,128)S(1)}, f32[64,512]{1,0:T(8,128)S(1)}, u32[]{:S(2)}, u32[]{:S(2)}) %collective-permute-start.9) | collective-permute-done | bytes 131104 | tf_op jit(solution)/shard_map/ppermute | solution.py:692
  40.0 2.9 %tree_weights.1 = (bf16[64,4096]{1,0:T(8,128)(2,1)S(1)}, bf16[128,896]{1,0:T(8,128)(2,1)S(1)}, f32[136,128]{1,0:T(8,128)S(1)}) custom-call(bf16[4,1024,128]{2,1,0:T(8,128)(2,1)} %get-tuple-element.54.base_hbm, f32[3,256,128]{2,1,0:T(8,128)S(1)} %get-tuple-element.55.upper_tiles_ref, f32[72,128]{1,0:T(8,128)S(1)} %get-tuple-element.56.top_ref, ...), custom_call_target="tpu_custom_call" | custom-call | tf_op jit(solution)/shard_map/tree_weights/pallas_call | solution.py:792
  42.9 1.0 %collective-permute-start.17 = (f32[136,128]{1,0:T(8,128)S(1)}, f32[136,128]{1,0:T(8,128)S(1)}, u32[]{:S(2)}, u32[]{:S(2)}) collective-permute-start(f32[136,128]{1,0:T(8,128)S(1)} %get-tuple-element.72), channel_id=1, source_target_pairs={{0,8},{8,0},{1,9},{9,1},{2,10},{10,2},{3,11},{11,3},{4,12},{12,4},... | collective-permute-start | bytes 208904 | tf_op jit(solution)/shard_map/ppermute | solution.py:638
  43.9 7.2 %near.1.near_ref = f32[64,2048]{1,0:T(8,128)S(1)} custom-call(s32[3,72]{1,0:T(4,128)} %get-tuple-element.77.tiles, bf16[4096,256]{1,0:T(8,128)(2,1)} %get-tuple-element.78.a_hbm, bf16[8,512,256]{2,1,0:T(8,128)(2,1)} %get-tuple-element.79.made_hbm, bf16[144,4096]{1,0:T(8,128)(2,1)S(1)} %get-tuple-element.74.tree_ref, bf16[64,4096]{1,0:T(8,128)(2,1)S(1)} %get-tuple-element.80.w_ref), custom_call_target="tpu_custom_call" | custom-call | tf_op jit(solution)/shard_map/near/pallas_call | solution.py:813
  51.1 2.2 %far.1 = (f32[4,64,512]{2,1,0:T(8,128)S(1)}, f32[4,64,512]{2,1,0:T(8,128)S(1)}) custom-call(f32[1,136,128]{2,1,0:T(8,128)S(1)} %bitcast.4, f32[4,1024]{1,0:T(4,128)S(1)} %get-tuple-element.67.slot_ref, f32[4,8,128]{2,1,0:T(8,128)S(1)} %get-tuple-element.73.info_ref, bf16[144,4096]{1,0:T(8,128)(2,1)S(1)} %get-tuple-element.74.tree_ref, ...), custom_call_target="tpu_custom_call" | custom-call | tf_op jit(solution)/shard_map/far/pallas_call | solution.py:831
  53.3 1.9 %collective-permute-done.18.got_ref = f32[4,64,512]{2,1,0:T(8,128)S(1)} collective-permute-done((f32[4,64,512]{2,1,0:T(8,128)S(1)}, f32[4,64,512]{2,1,0:T(8,128)S(1)}, u32[]{:S(2)}, u32[]{:S(2)}) %collective-permute-start.18) | collective-permute-done | bytes 524320 | tf_op jit(solution)/shard_map/ppermute | solution.py:695
  55.3 2.9 %collective-permute-start.19 = (f32[64,512]{1,0:T(8,128)S(1)}, f32[64,512]{1,0:T(8,128)S(1)}, u32[]{:S(2)}, u32[]{:S(2)}) collective-permute-start(f32[64,512]{1,0:T(8,128)S(1)} %get-tuple-element.83), channel_id=1, source_target_pairs={{0,4},{1,13},{2,6},{3,15},{4,0},{5,9},{6,2},{7,11},{8,12},{9,5},{1... | collective-permute-start | bytes 393224 | tf_op jit(solution)/shard_map/ppermute | solution.py:692
  58.2 1.0 %collective-permute-start.20 = (f32[64,512]{1,0:T(8,128)S(1)}, f32[64,512]{1,0:T(8,128)S(1)}, u32[]{:S(2)}, u32[]{:S(2)}) collective-permute-start(f32[64,512]{1,0:T(8,128)S(1)} %get-tuple-element.84), channel_id=1, source_target_pairs={{0,6},{1,15},{2,4},{3,13},{4,2},{5,11},{6,0},{7,9},{8,14},{9,7},{1... | collective-permute-start | bytes 393224 | tf_op jit(solution)/shard_map/ppermute | solution.py:692
  59.9 8.4 %collective-permute-done.19.refs_0_ = f32[64,512]{1,0:T(8,128)S(1)} collective-permute-done((f32[64,512]{1,0:T(8,128)S(1)}, f32[64,512]{1,0:T(8,128)S(1)}, u32[]{:S(2)}, u32[]{:S(2)}) %collective-permute-start.19) | collective-permute-done | bytes 131104 | tf_op jit(solution)/shard_map/ppermute | solution.py:692
  68.9 1.7 %collective-permute-done.22.refs_3_ = f32[64,512]{1,0:T(8,128)S(1)} collective-permute-done((f32[64,512]{1,0:T(8,128)S(1)}, f32[64,512]{1,0:T(8,128)S(1)}, u32[]{:S(2)}, u32[]{:S(2)}) %collective-permute-start.22) | collective-permute-done | bytes 131104 | tf_op jit(solution)/shard_map/ppermute | solution.py:692
  71.0 1.0 %collective-permute-done.26.refs_7_ = f32[64,512]{1,0:T(8,128)S(1)} collective-permute-done((f32[64,512]{1,0:T(8,128)S(1)}, f32[64,512]{1,0:T(8,128)S(1)}, u32[]{:S(2)}, u32[]{:S(2)}) %collective-permute-start.26) | collective-permute-done | bytes 131104 | tf_op jit(solution)/shard_map/ppermute | solution.py:695
  72.0 1.9 %to_input_order.1 = f32[1024,128]{1,0:T(8,128)} custom-call(f32[8,128]{1,0:T(8,128)S(1)} %copy-done.1, f32[64,512]{1,0:T(8,128)S(1)} %collective-permute-done.19.refs_0_, f32[64,512]{1,0:T(8,128)S(1)} %collective-permute-done.20.refs_1_, f32[64,512]{1,0:T(8,128)S(1)} %collective-permute-done.21.refs_2_, f32[64,512]{1,0:T(8,128)S(1)} %collective-permute-done.22.refs_3_, ...), custom_call_target="tpu_custom_call" | custom-call | tf_op jit(solution)/shard_map/to_input_order/pallas_call | solution.py:868
  (43 shorter events, 6.6 us)
Async XLA Ops:
  2.7 1.6 %collective-permute-start = (f32[72,512]{1,0:T(8,128)}, f32[72,512]{1,0:T(8,128)S(1)}, u32[]{:S(2)}, u32[]{:S(2)}) collective-permute-start(f32[72,512]{1,0:T(8,128)} %get-tuple-element.47), channel_id=1, source_target_pairs={{0,0},{1,9},{2,2},{3,11},{4,4},{5,13},{6,6},{7,15},{8,8},{9,1},{10... | collective-permute-start | bytes 442376 | tf_op jit(solution)/shard_map/ppermute | solution.py:692
  4.3 8.8 %collective-permute-start.2 = (f32[72,512]{1,0:T(8,128)S(1)}, f32[72,512]{1,0:T(8,128)S(1)}, u32[]{:S(2)}, u32[]{:S(2)}) collective-permute-start(f32[72,512]{1,0:T(8,128)S(1)} %collective-permute-done.refs_0_), channel_id=1, source_target_pairs={{0,4},{2,6},{4,0},{6,2},{1,5},{3,7},{5,1},{7,3},{8,12},{10,14},{12... | collective-permute-start | bytes 442376 | tf_op jit(solution)/shard_map/ppermute | solution.py:721
  8.3 7.5 %collective-permute-start.1 = (f32[72,512]{1,0:T(8,128)S(1)}, f32[72,512]{1,0:T(8,128)S(1)}, u32[]{:S(2)}, u32[]{:S(2)}) collective-permute-start(f32[72,512]{1,0:T(8,128)S(1)} %collective-permute-done.refs_0_), channel_id=1, source_target_pairs={{0,2},{2,0},{4,6},{6,4},{1,3},{3,1},{5,7},{7,5},{8,10},{10,8},{12,... | collective-permute-start | bytes 442376 | tf_op jit(solution)/shard_map/ppermute | solution.py:721
  13.2 5.7 %collective-permute-start.3 = (f32[72,512]{1,0:T(8,128)S(1)}, f32[72,512]{1,0:T(8,128)S(1)}, u32[]{:S(2)}, u32[]{:S(2)}) collective-permute-start(f32[72,512]{1,0:T(8,128)S(1)} %collective-permute-done.2.refs_2_), channel_id=1, source_target_pairs={{0,2},{2,0},{4,6},{6,4},{1,3},{3,1},{5,7},{7,5},{8,10},{10,8},{12,... | collective-permute-start | bytes 442376 | tf_op jit(solution)/shard_map/ppermute | solution.py:721
  18.9 3.2 %collective-permute-start.8 = (f32[4,32,512]{2,1,0:T(8,128)S(1)}, f32[4,32,512]{2,1,0:T(8,128)S(1)}, u32[]{:S(2)}, u32[]{:S(2)}) collective-permute-start(f32[4,32,512]{2,1,0:T(8,128)S(1)} %get-tuple-element.58), channel_id=1, source_target_pairs={{0,1},{1,0},{2,3},{3,2},{4,5},{5,4},{6,7},{7,6},{8,9},{9,8},{10,11... | collective-permute-start | bytes 786440 | tf_op jit(solution)/shard_map/ppermute | solution.py:695
  20.9 3.5 %collective-permute-start.4 = (f32[72,512]{1,0:T(8,128)S(1)}, f32[72,512]{1,0:T(8,128)S(1)}, u32[]{:S(2)}, u32[]{:S(2)}) collective-permute-start(f32[72,512]{1,0:T(8,128)S(1)} %collective-permute-done.refs_0_), channel_id=1, source_target_pairs={{0,1},{1,0},{2,3},{3,2},{4,5},{5,4},{6,7},{7,6},{8,9},{9,8},{10,11... | collective-permute-start | bytes 442376 | tf_op jit(solution)/shard_map/ppermute | solution.py:695
  20.9 4.8 %collective-permute-start.5 = (f32[72,512]{1,0:T(8,128)S(1)}, f32[72,512]{1,0:T(8,128)S(1)}, u32[]{:S(2)}, u32[]{:S(2)}) collective-permute-start(f32[72,512]{1,0:T(8,128)S(1)} %collective-permute-done.1.refs_1_), channel_id=1, source_target_pairs={{0,1},{1,0},{2,3},{3,2},{4,5},{5,4},{6,7},{7,6},{8,9},{9,8},{10,11... | collective-permute-start | bytes 442376 | tf_op jit(solution)/shard_map/ppermute | solution.py:695
  21.4 5.0 %collective-permute-start.6 = (f32[72,512]{1,0:T(8,128)S(1)}, f32[72,512]{1,0:T(8,128)S(1)}, u32[]{:S(2)}, u32[]{:S(2)}) collective-permute-start(f32[72,512]{1,0:T(8,128)S(1)} %collective-permute-done.2.refs_2_), channel_id=1, source_target_pairs={{0,1},{1,0},{2,3},{3,2},{4,5},{5,4},{6,7},{7,6},{8,9},{9,8},{10,11... | collective-permute-start | bytes 442376 | tf_op jit(solution)/shard_map/ppermute | solution.py:695
  21.4 5.5 %collective-permute-start.7 = (f32[72,512]{1,0:T(8,128)S(1)}, f32[72,512]{1,0:T(8,128)S(1)}, u32[]{:S(2)}, u32[]{:S(2)}) collective-permute-start(f32[72,512]{1,0:T(8,128)S(1)} %collective-permute-done.3.refs_3_), channel_id=1, source_target_pairs={{0,1},{1,0},{2,3},{3,2},{4,5},{5,4},{6,7},{7,6},{8,9},{9,8},{10,11... | collective-permute-start | bytes 442376 | tf_op jit(solution)/shard_map/ppermute | solution.py:695
  22.1 12.8 %collective-permute-start.12 = (f32[64,512]{1,0:T(8,128)S(1)}, f32[64,512]{1,0:T(8,128)S(1)}, u32[]{:S(2)}, u32[]{:S(2)}) collective-permute-start(f32[64,512]{1,0:T(8,128)S(1)} %get-tuple-element.62), channel_id=1, source_target_pairs={{0,4},{1,13},{2,6},{3,15},{4,0},{5,9},{6,2},{7,11},{8,12},{9,5},{1... | collective-permute-start | bytes 393224 | tf_op jit(solution)/shard_map/ppermute | solution.py:692
  24.5 10.4 %collective-permute-start.11 = (f32[64,512]{1,0:T(8,128)S(1)}, f32[64,512]{1,0:T(8,128)S(1)}, u32[]{:S(2)}, u32[]{:S(2)}) collective-permute-start(f32[64,512]{1,0:T(8,128)S(1)} %get-tuple-element.61), channel_id=1, source_target_pairs={{0,6},{1,15},{2,4},{3,13},{4,2},{5,11},{6,0},{7,9},{8,14},{9,7},{1... | collective-permute-start | bytes 393224 | tf_op jit(solution)/shard_map/ppermute | solution.py:692
  25.7 9.1 %collective-permute-start.10 = (f32[64,512]{1,0:T(8,128)S(1)}, f32[64,512]{1,0:T(8,128)S(1)}, u32[]{:S(2)}, u32[]{:S(2)}) collective-permute-start(f32[64,512]{1,0:T(8,128)S(1)} %get-tuple-element.60), channel_id=1, source_target_pairs={{0,0},{1,9},{2,2},{3,11},{4,4},{5,13},{6,6},{7,15},{8,8},{9,1},{10... | collective-permute-start | bytes 393224 | tf_op jit(solution)/shard_map/ppermute | solution.py:692
  26.4 11.2 %collective-permute-start.9 = (f32[64,512]{1,0:T(8,128)S(1)}, f32[64,512]{1,0:T(8,128)S(1)}, u32[]{:S(2)}, u32[]{:S(2)}) collective-permute-start(f32[64,512]{1,0:T(8,128)S(1)} %get-tuple-element.59), channel_id=1, source_target_pairs={{0,2},{1,11},{2,0},{3,9},{4,6},{5,15},{6,4},{7,13},{8,10},{9,3},{1... | collective-permute-start | bytes 393224 | tf_op jit(solution)/shard_map/ppermute | solution.py:692
  37.6 1.5 %collective-permute-start.16 = (f32[64,512]{1,0:T(8,128)S(1)}, f32[64,512]{1,0:T(8,128)S(1)}, u32[]{:S(2)}, u32[]{:S(2)}) collective-permute-start(f32[64,512]{1,0:T(8,128)S(1)} %collective-permute-done.9.refs_3_), channel_id=1, source_target_pairs={{0,1},{1,0},{2,3},{3,2},{4,5},{5,4},{6,7},{7,6},{8,9},{9,8},{10,11... | collective-permute-start | bytes 393224 | tf_op jit(solution)/shard_map/ppermute | solution.py:695
  38.2 1.5 %collective-permute-start.14 = (f32[64,512]{1,0:T(8,128)S(1)}, f32[64,512]{1,0:T(8,128)S(1)}, u32[]{:S(2)}, u32[]{:S(2)}) collective-permute-start(f32[64,512]{1,0:T(8,128)S(1)} %collective-permute-done.11.refs_1_), channel_id=1, source_target_pairs={{0,1},{1,0},{2,3},{3,2},{4,5},{5,4},{6,7},{7,6},{8,9},{9,8},{10,11... | collective-permute-start | bytes 393224 | tf_op jit(solution)/shard_map/ppermute | solution.py:695
  42.9 8.2 %collective-permute-start.17 = (f32[136,128]{1,0:T(8,128)S(1)}, f32[136,128]{1,0:T(8,128)S(1)}, u32[]{:S(2)}, u32[]{:S(2)}) collective-permute-start(f32[136,128]{1,0:T(8,128)S(1)} %get-tuple-element.72), channel_id=1, source_target_pairs={{0,8},{8,0},{1,9},{9,1},{2,10},{10,2},{3,11},{11,3},{4,12},{12,4},... | collective-permute-start | bytes 208904 | tf_op jit(solution)/shard_map/ppermute | solution.py:638
  53.3 2.0 %collective-permute-start.18 = (f32[4,64,512]{2,1,0:T(8,128)S(1)}, f32[4,64,512]{2,1,0:T(8,128)S(1)}, u32[]{:S(2)}, u32[]{:S(2)}) collective-permute-start(f32[4,64,512]{2,1,0:T(8,128)S(1)} %get-tuple-element.82), channel_id=1, source_target_pairs={{0,1},{1,0},{2,3},{3,2},{4,5},{5,4},{6,7},{7,6},{8,9},{9,8},{10,11... | collective-permute-start | bytes 1572872 | tf_op jit(solution)/shard_map/ppermute | solution.py:695
  55.3 13.0 %collective-permute-start.19 = (f32[64,512]{1,0:T(8,128)S(1)}, f32[64,512]{1,0:T(8,128)S(1)}, u32[]{:S(2)}, u32[]{:S(2)}) collective-permute-start(f32[64,512]{1,0:T(8,128)S(1)} %get-tuple-element.83), channel_id=1, source_target_pairs={{0,4},{1,13},{2,6},{3,15},{4,0},{5,9},{6,2},{7,11},{8,12},{9,5},{1... | collective-permute-start | bytes 393224 | tf_op jit(solution)/shard_map/ppermute | solution.py:692
  58.2 10.1 %collective-permute-start.20 = (f32[64,512]{1,0:T(8,128)S(1)}, f32[64,512]{1,0:T(8,128)S(1)}, u32[]{:S(2)}, u32[]{:S(2)}) collective-permute-start(f32[64,512]{1,0:T(8,128)S(1)} %get-tuple-element.84), channel_id=1, source_target_pairs={{0,6},{1,15},{2,4},{3,13},{4,2},{5,11},{6,0},{7,9},{8,14},{9,7},{1... | collective-permute-start | bytes 393224 | tf_op jit(solution)/shard_map/ppermute | solution.py:692
  59.2 9.6 %collective-permute-start.21 = (f32[64,512]{1,0:T(8,128)S(1)}, f32[64,512]{1,0:T(8,128)S(1)}, u32[]{:S(2)}, u32[]{:S(2)}) collective-permute-start(f32[64,512]{1,0:T(8,128)S(1)} %get-tuple-element.85), channel_id=1, source_target_pairs={{0,0},{1,9},{2,2},{3,11},{4,4},{5,13},{6,6},{7,15},{8,8},{9,1},{10... | collective-permute-start | bytes 393224 | tf_op jit(solution)/shard_map/ppermute | solution.py:692
  59.9 10.7 %collective-permute-start.22 = (f32[64,512]{1,0:T(8,128)S(1)}, f32[64,512]{1,0:T(8,128)S(1)}, u32[]{:S(2)}, u32[]{:S(2)}) collective-permute-start(f32[64,512]{1,0:T(8,128)S(1)} %get-tuple-element.86), channel_id=1, source_target_pairs={{0,2},{1,11},{2,0},{3,9},{4,6},{5,15},{6,4},{7,13},{8,10},{9,3},{1... | collective-permute-start | bytes 393224 | tf_op jit(solution)/shard_map/ppermute | solution.py:692
  68.3 2.6 %collective-permute-start.23 = (f32[64,512]{1,0:T(8,128)S(1)}, f32[64,512]{1,0:T(8,128)S(1)}, u32[]{:S(2)}, u32[]{:S(2)}) collective-permute-start(f32[64,512]{1,0:T(8,128)S(1)} %collective-permute-done.19.refs_0_), channel_id=1, source_target_pairs={{0,1},{1,0},{2,3},{3,2},{4,5},{5,4},{6,7},{7,6},{8,9},{9,8},{10,11... | collective-permute-start | bytes 393224 | tf_op jit(solution)/shard_map/ppermute | solution.py:695
  68.3 2.6 %collective-permute-start.24 = (f32[64,512]{1,0:T(8,128)S(1)}, f32[64,512]{1,0:T(8,128)S(1)}, u32[]{:S(2)}, u32[]{:S(2)}) collective-permute-start(f32[64,512]{1,0:T(8,128)S(1)} %collective-permute-done.20.refs_1_), channel_id=1, source_target_pairs={{0,1},{1,0},{2,3},{3,2},{4,5},{5,4},{6,7},{7,6},{8,9},{9,8},{10,11... | collective-permute-start | bytes 393224 | tf_op jit(solution)/shard_map/ppermute | solution.py:695
  68.8 2.1 %collective-permute-start.25 = (f32[64,512]{1,0:T(8,128)S(1)}, f32[64,512]{1,0:T(8,128)S(1)}, u32[]{:S(2)}, u32[]{:S(2)}) collective-permute-start(f32[64,512]{1,0:T(8,128)S(1)} %collective-permute-done.21.refs_2_), channel_id=1, source_target_pairs={{0,1},{1,0},{2,3},{3,2},{4,5},{5,4},{6,7},{7,6},{8,9},{9,8},{10,11... | collective-permute-start | bytes 393224 | tf_op jit(solution)/shard_map/ppermute | solution.py:695
  (5 other events, 45.8 us)

commit v19 on v17

--- a/solution.py
+++ b/solution.py
@@ -13,7 +13,6 @@
 LANES = 128
 FEAT = 256
 LOW = 256
-AHEAD = 4
 COORD = 144
 
 highest = lax.Precision.HIGHEST
@@ -189,7 +188,6 @@
         self.per = rows // self.count
         self.halves = 2 if fine else 1
         self.span = LEAF // self.halves
-        self.ahead = AHEAD // 4 * 4 if fine else 4
 
     def core(self):
         return lax.axis_index("rep") if self.fine else 0
@@ -255,26 +253,6 @@
     return nn(a_ref[source, :], bt_ref[:, target])
 
 
-def tiles_ahead(layout, tiles, a_ref, bt_ref, even, odd, made, made_hbm, sems):
-    def send(tile):
-        return pltpu.make_async_copy(made.at[tile], made_hbm.at[tile], sems.at[tile])
-
-    for k in range(2):
-        even[k] = tile_exponents(layout, tiles, k, a_ref, bt_ref)
-
-    def step(pair, carry):
-        for unit, ready, upcoming in ((2 * pair, even, odd), (2 * pair + 1, odd, even)):
-            for k in range(2):
-                tile = 2 * unit + k
-                upcoming[k] = tile_exponents(layout, tiles, tile + 2, a_ref, bt_ref)
-                made[tile] = jnp.exp(ready[k]).astype(bf16)
-                send(tile).start()
-        return carry
-
-    lax.fori_loop(0, layout.ahead // 4, step, 0)
-    return [send(tile) for tile in range(layout.ahead)]
-
-
 def list_tiles(count_ref, list_ref, tiles, times):
     every = count_ref.shape[1]
 
@@ -313,8 +291,8 @@
     else:
         small_ref = None
     place_refs, refs = refs[: layout.count], refs[layout.count :]
-    tree_ref, a_hbm, base_hbm, sk_ref, upper_tiles_ref, top_ref, slot_ref, info_ref, tiles, made_hbm = refs[:10]
-    masked, low_hot, a_ref, base_ref, sk_t, sk_bt, sems, times, bt_ref, even, odd, made, made_sems = refs[10:]
+    tree_ref, a_hbm, base_hbm, sk_ref, upper_tiles_ref, top_ref, slot_ref, info_ref, tiles = refs[:9]
+    masked, low_hot, a_ref, base_ref, sk_t, sk_bt, sems, times = refs[9:]
     blocks, rows = layout.blocks, layout.rows
 
     def keep(node, found):
@@ -384,8 +362,6 @@
     top_ref[0:64, :] = found[0:64] + found[64:128]
     top_ref[64:72, :] = found[128:136]
     list_tiles(count_ref, list_ref, tiles, times)
-    target_columns(layout, bt_ref, tree_ref)
-    copies += tiles_ahead(layout, tiles, a_ref, bt_ref, even, odd, made, made_hbm, made_sems)
     for copy in copies:
         copy.wait()
 
@@ -436,23 +412,17 @@
         start, count = start + count, count // 2
 
 
-def near_kernel(layout, tiles, a_hbm, made_hbm, tree_ref, w_ref, acc, a_ref, bt_ref, made, sems, even, odd, even_tile, odd_tile):
-    ahead, span = layout.ahead, layout.span
-
-    def fetch(tile):
-        return pltpu.make_async_copy(made_hbm.at[tile], made.at[tile], sems.at[tile])
-
-    copy = pltpu.make_async_copy(a_hbm, a_ref, sems.at[ahead])
+def near_kernel(layout, tiles, a_hbm, tree_ref, w_ref, acc, a_ref, bt_ref, sem, even, odd, even_tile, odd_tile):
+    span = layout.span
+    copy = pltpu.make_async_copy(a_hbm, a_ref, sem)
     copy.start()
-    for tile in range(ahead):
-        fetch(tile).start()
     filled = tiles[0, tiles.shape[1] - 1]
     acc[...] = jnp.zeros_like(acc)
     target_columns(layout, bt_ref, tree_ref)
 
     def exponents(unit, out):
         for k in range(2):
-            out[k] = tile_exponents(layout, tiles, ahead + 2 * unit + k, a_ref, bt_ref)
+            out[k] = tile_exponents(layout, tiles, 2 * unit + k, a_ref, bt_ref)
 
     def add(tile, block):
         source = aligned(tiles[1, tile] * LEAF, LEAF, LEAF)
@@ -460,49 +430,33 @@
         acc[:, target] += tiles[2, tile].astype(f32) * nn(w_ref[:, source], block)
 
     copy.wait()
-
-    @pl.when(filled > ahead)
+    exponents(0, even)
+    for k in range(2):
+        even_tile[k] = jnp.exp(even[k]).astype(bf16)
+    exponents(1, odd)
+
+    def phase(unit, upcoming, ready, finished, previous):
+        for k in range(2):
+            upcoming[k] = tile_exponents(layout, tiles, 2 * (unit + 1) + k, a_ref, bt_ref)
+            finished[k] = jnp.exp(ready[k]).astype(bf16)
+            add(2 * (unit - 1) + k, previous[k])
+
+    def step(pair, carry):
+        phase(2 * pair + 1, even, odd, odd_tile, even_tile)
+        phase(2 * pair + 2, odd, even, even_tile, odd_tile)
+        return carry
+
+    units = (filled + 1) // 2
+    pairs = (units - 1) // 2
+    lax.fori_loop(0, pairs, step, 0)
+    for k in range(2):
+        add(4 * pairs + k, even_tile[k])
+
+    @pl.when(2 * pairs + 1 < units)
     def _():
-        exponents(0, even)
         for k in range(2):
-            even_tile[k] = jnp.exp(even[k]).astype(bf16)
-        exponents(1, odd)
-
-        def phase(unit, upcoming, ready, finished, previous):
-            for k in range(2):
-                upcoming[k] = tile_exponents(layout, tiles, ahead + 2 * (unit + 1) + k, a_ref, bt_ref)
-                finished[k] = jnp.exp(ready[k]).astype(bf16)
-                add(ahead + 2 * (unit - 1) + k, previous[k])
-
-        def step(pair, carry):
-            phase(2 * pair + 1, even, odd, odd_tile, even_tile)
-            phase(2 * pair + 2, odd, even, even_tile, odd_tile)
-            return carry
-
-        units = (filled - ahead + 1) // 2
-        pairs = (units - 1) // 2
-        lax.fori_loop(0, pairs, step, 0)
-        for k in range(2):
-            add(ahead + 4 * pairs + k, even_tile[k])
-
-        @pl.when(2 * pairs + 1 < units)
-        def _():
-            for k in range(2):
-                odd_tile[k] = jnp.exp(odd[k]).astype(bf16)
-                add(ahead + 4 * pairs + 2 + k, odd_tile[k])
-
-    def arrived(quad, carry):
-        for more in range(4):
-            fetch(4 * quad + more).wait()
-            tile = 4 * quad + more
-
-            @pl.when(tile < filled)
-            def _():
-                add(tile, made[tile])
-
-        return carry
-
-    lax.fori_loop(0, ahead // 4, arrived, 0)
+            odd_tile[k] = jnp.exp(odd[k]).astype(bf16)
+            add(4 * pairs + 2 + k, odd_tile[k])
 
 
 def far_kernel(layout, low_levels, pack_ref, slot_ref, info_ref, tree_ref, sk_ref, coef_ref, near_ref, *refs):
@@ -748,7 +702,7 @@
         light = [light.transpose(1, 2, 0, 3).reshape(width, total)]
 
     nodes = 2 * blocks - 1
-    tree, feat_a, base, sk, upper_tiles, top, slots, info, tiles, made = pl.pallas_call(
+    tree, feat_a, base, sk, upper_tiles, top, slots, info, tiles = pl.pallas_call(
         functools.partial(points_kernel, layout, trees),
         out_shape=(
             vm((COORD, total), bf16),
@@ -760,10 +714,9 @@
             vm((blocks, rows), f32),
             vm((blocks, 8, SK), f32),
             pltpu.MemorySpace.HBM((3, leaves * leaves + 8), jnp.int32),
-            pltpu.MemorySpace.HBM((layout.ahead, LEAF, layout.span), bf16),
         ),
         in_specs=[spec(SMEM)] * 2 + [spec()] * (1 + len(small) + layout.count),
-        out_specs=(spec(), spec(pl.ANY), spec(pl.ANY)) + (spec(),) * 5 + (spec(SMEM), spec(pl.ANY)),
+        out_specs=(spec(), spec(pl.ANY), spec(pl.ANY)) + (spec(),) * 5 + (spec(SMEM),),
         scratch_shapes=[
             vm((blocks, rows // LOW * COORD, rows), bf16),
             vm((blocks, rows, LOW), bf16),
@@ -773,11 +726,6 @@
             vm((FEAT, nodes * SK), bf16),
             pltpu.SemaphoreType.DMA((2, blocks)),
             pltpu.SMEM((leaves,), jnp.int32),
-            vm((FEAT, total // layout.halves), bf16),
-            vm((2, LEAF, layout.span), f32),
-            vm((2, LEAF, layout.span), f32),
-            vm((layout.ahead, LEAF, layout.span), bf16),
-            pltpu.SemaphoreType.DMA((layout.ahead,)),
         ],
         compiler_params=params(40),
         name="tree_points",
@@ -810,19 +758,18 @@
     near = pl.pallas_call(
         functools.partial(near_kernel, layout),
         out_shape=vm((cols, total // layout.halves), f32),
-        in_specs=[spec(SMEM), spec(pl.ANY), spec(pl.ANY)] + [spec()] * 2,
+        in_specs=[spec(SMEM), spec(pl.ANY)] + [spec()] * 2,
         out_specs=spec(),
         scratch_shapes=[
             vm((total, FEAT), bf16),
             vm((FEAT, total // layout.halves), bf16),
-            vm((layout.ahead, LEAF, layout.span), bf16),
-            pltpu.SemaphoreType.DMA((layout.ahead + 1,)),
+            pltpu.SemaphoreType.DMA(()),
         ]
         + [vm((2, LEAF, layout.span), f32)] * 2
         + [vm((2, LEAF, layout.span), bf16)] * 2,
         compiler_params=params(40),
         name="near",
-    )(in_hbm(tiles), in_hbm(feat_a), in_hbm(made), held(tree), held(tree_light))
+    )(in_hbm(tiles), in_hbm(feat_a), held(tree), held(tree_light))
 
     levels = low_levels + ups
     back = pl.pallas_call(

time: 74 us -> 74.1 us (level)
  Pallas kernels: 25.9 us -> 24.6 us
    pallas_call x1, Pallas kernels: 7.11 us -> 5.65 us  [body(): pl.pallas_call(functools.partial(points_kernel, layout, trees), out_shape...]
  transfers between devices with their start and end apart: 27 -> 27, of which waited for: 13 -> 13; matrix products, arithmetic and copies ran while one was open for 0% -> 0% of each run, Pallas kernels for 22% -> 20%
where the time goes in v19:
time: 74.1 us; the launch traced here: 73.7 us
  waiting for transfers between devices  25 us (34%)
  Pallas kernels  24.6 us (33%)
  starting transfers between devices  23.9 us (32%)
    ppermute x9, waiting for transfers between devices, swap(): return lax.ppermute(value, axes, pairs)  14.5 us
    ppermute x9, starting transfers between devices, swap(): return lax.ppermute(value, axes, pairs)  10.7 us
    pallas_call x1, Pallas kernels, body(): pl.pallas_call(functools.partial(near_kernel, layout), out_shape=vm((cols...  7.32 us
    ppermute x3, starting transfers between devices, body(): lax.ppermute(place[step], 'sub', [(i, i ^ stride) for i in range(blocks)])  6.51 us
    ppermute x3, waiting for transfers between devices, body(): lax.ppermute(place[step], 'sub', [(i, i ^ stride) for i in range(blocks)])  6.25 us
    pallas_call x1, Pallas kernels, body(): pl.pallas_call(functools.partial(points_kernel, layout, trees), out_shape...  5.65 us
    ppermute x14, starting transfers between devices, other_core(): return lax.ppermute(value, 'rep', [(0, 1), (1, 0)])  5.56 us
    ppermute x14, waiting for transfers between devices, other_core(): return lax.ppermute(value, 'rep', [(0, 1), (1, 0)])  4.29 us
  transfers between devices with their start and end apart: 27, of which 13 were waited for; matrix products, arithmetic and copies ran while one was open for 0% of the time, Pallas kernels for 20%

profile of v19, /device:TPU:0, one launch (start us, length us, event | category | flops | bytes accessed | tf_op | source)
XLA Modules:
  0.0 73.7 jit_solution(12979824955341799591)
XLA Ops:
  0.0 2.7 %sort_points.1 = (f32[72,512]{1,0:T(8,128)}, f32[8,128]{1,0:T(8,128)}) custom-call(s32[8,128]{1,0:T(8,128)} %bitcast.6, f32[64,1024]{1,0:T(8,128)} %bitcast.5, s32[1,128]{1,0:T(1,128)} %base_ref.1, s32[2,3]{1,0:T(2,128)} %flag_ref.1), custom_call_target="tpu_custom_call" | custom-call | tf_op jit(solution)/shard_map/sort_points/pallas_call | solution.py:628
  2.7 1.6 %collective-permute-start = (f32[72,512]{1,0:T(8,128)}, f32[72,512]{1,0:T(8,128)S(1)}, u32[]{:S(2)}, u32[]{:S(2)}) collective-permute-start(f32[72,512]{1,0:T(8,128)} %get-tuple-element.43), channel_id=1, source_target_pairs={{0,0},{1,9},{2,2},{3,11},{4,4},{5,13},{6,6},{7,15},{8,8},{9,1},{10... | collective-permute-start | bytes 442376 | tf_op jit(solution)/shard_map/ppermute | solution.py:646
  4.3 4.0 %collective-permute-start.2 = (f32[72,512]{1,0:T(8,128)S(1)}, f32[72,512]{1,0:T(8,128)S(1)}, u32[]{:S(2)}, u32[]{:S(2)}) collective-permute-start(f32[72,512]{1,0:T(8,128)S(1)} %collective-permute-done.refs_0_), channel_id=1, source_target_pairs={{0,4},{2,6},{4,0},{6,2},{1,5},{3,7},{5,1},{7,3},{8,12},{10,14},{12... | collective-permute-start | bytes 442376 | tf_op jit(solution)/shard_map/ppermute | solution.py:675
  8.3 1.6 %collective-permute-start.1 = (f32[72,512]{1,0:T(8,128)S(1)}, f32[72,512]{1,0:T(8,128)S(1)}, u32[]{:S(2)}, u32[]{:S(2)}) collective-permute-start(f32[72,512]{1,0:T(8,128)S(1)} %collective-permute-done.refs_0_), channel_id=1, source_target_pairs={{0,2},{2,0},{4,6},{6,4},{1,3},{3,1},{5,7},{7,5},{8,10},{10,8},{12,... | collective-permute-start | bytes 442376 | tf_op jit(solution)/shard_map/ppermute | solution.py:675
  9.9 3.2 %collective-permute-done.2.refs_2_ = f32[72,512]{1,0:T(8,128)S(1)} collective-permute-done((f32[72,512]{1,0:T(8,128)S(1)}, f32[72,512]{1,0:T(8,128)S(1)}, u32[]{:S(2)}, u32[]{:S(2)}) %collective-permute-start.2) | collective-permute-done | bytes 147488 | tf_op jit(solution)/shard_map/ppermute | solution.py:675
  13.2 0.9 %collective-permute-start.3 = (f32[72,512]{1,0:T(8,128)S(1)}, f32[72,512]{1,0:T(8,128)S(1)}, u32[]{:S(2)}, u32[]{:S(2)}) collective-permute-start(f32[72,512]{1,0:T(8,128)S(1)} %collective-permute-done.2.refs_2_), channel_id=1, source_target_pairs={{0,2},{2,0},{4,6},{6,4},{1,3},{3,1},{5,7},{7,5},{8,10},{10,8},{12,... | collective-permute-start | bytes 442376 | tf_op jit(solution)/shard_map/ppermute | solution.py:675
  14.1 1.8 %sort_weights.1 = (f32[4,32,512]{2,1,0:T(8,128)S(1)}, f32[4,32,512]{2,1,0:T(8,128)S(1)}) custom-call(f32[8,128]{1,0:T(8,128)} %get-tuple-element.42.pos_ref, f32[1024,128]{1,0:T(8,128)} %refs_8_.1), custom_call_target="tpu_custom_call" | custom-call | tf_op jit(solution)/shard_map/sort_weights/pallas_call | solution.py:656
  15.9 3.0 %collective-permute-done.3.refs_3_ = f32[72,512]{1,0:T(8,128)S(1)} collective-permute-done((f32[72,512]{1,0:T(8,128)S(1)}, f32[72,512]{1,0:T(8,128)S(1)}, u32[]{:S(2)}, u32[]{:S(2)}) %collective-permute-start.3) | collective-permute-done | bytes 147488 | tf_op jit(solution)/shard_map/ppermute | solution.py:675
  18.9 2.0 %collective-permute-start.8 = (f32[4,32,512]{2,1,0:T(8,128)S(1)}, f32[4,32,512]{2,1,0:T(8,128)S(1)}, u32[]{:S(2)}, u32[]{:S(2)}) collective-permute-start(f32[4,32,512]{2,1,0:T(8,128)S(1)} %get-tuple-element.54), channel_id=1, source_target_pairs={{0,1},{1,0},{2,3},{3,2},{4,5},{5,4},{6,7},{7,6},{8,9},{9,8},{10,11... | collective-permute-start | bytes 786440 | tf_op jit(solution)/shard_map/ppermute | solution.py:649
  22.1 2.3 %collective-permute-start.9 = (f32[64,512]{1,0:T(8,128)S(1)}, f32[64,512]{1,0:T(8,128)S(1)}, u32[]{:S(2)}, u32[]{:S(2)}) collective-permute-start(f32[64,512]{1,0:T(8,128)S(1)} %get-tuple-element.55), channel_id=1, source_target_pairs={{0,4},{1,13},{2,6},{3,15},{4,0},{5,9},{6,2},{7,11},{8,12},{9,5},{1... | collective-permute-start | bytes 393224 | tf_op jit(solution)/shard_map/ppermute | solution.py:646
  24.5 1.3 %collective-permute-start.10 = (f32[64,512]{1,0:T(8,128)S(1)}, f32[64,512]{1,0:T(8,128)S(1)}, u32[]{:S(2)}, u32[]{:S(2)}) collective-permute-start(f32[64,512]{1,0:T(8,128)S(1)} %get-tuple-element.56), channel_id=1, source_target_pairs={{0,6},{1,15},{2,4},{3,13},{4,2},{5,11},{6,0},{7,9},{8,14},{9,7},{1... | collective-permute-start | bytes 393224 | tf_op jit(solution)/shard_map/ppermute | solution.py:646
  27.0 5.6 %tree_points.1 = (bf16[144,4096]{1,0:T(8,128)(2,1)S(1)}, bf16[4096,256]{1,0:T(8,128)(2,1)}, bf16[4,1024,128]{2,1,0:T(8,128)(2,1)}, bf16[896,256]{1,0:T(8,128)(2,...) custom-call(s32[1,8]{1,0:T(1,128)} %count_ref.1, ...), custom_call_target="tpu_custom_call" | custom-call | tf_op jit(solution)/shard_map/tree_points/pallas_call | solution.py:705
  32.6 2.3 %collective-permute-done.9.refs_0_ = f32[64,512]{1,0:T(8,128)S(1)} collective-permute-done((f32[64,512]{1,0:T(8,128)S(1)}, f32[64,512]{1,0:T(8,128)S(1)}, u32[]{:S(2)}, u32[]{:S(2)}) %collective-permute-start.9) | collective-permute-done | bytes 131104 | tf_op jit(solution)/shard_map/ppermute | solution.py:646
  34.9 2.7 %collective-permute-done.12.refs_3_ = f32[64,512]{1,0:T(8,128)S(1)} collective-permute-done((f32[64,512]{1,0:T(8,128)S(1)}, f32[64,512]{1,0:T(8,128)S(1)}, u32[]{:S(2)}, u32[]{:S(2)}) %collective-permute-start.12) | collective-permute-done | bytes 131104 | tf_op jit(solution)/shard_map/ppermute | solution.py:646
  39.9 2.9 %tree_weights.1 = (bf16[64,4096]{1,0:T(8,128)(2,1)S(1)}, bf16[128,896]{1,0:T(8,128)(2,1)S(1)}, f32[136,128]{1,0:T(8,128)S(1)}) custom-call(bf16[4,1024,128]{2,1,0:T(8,128)(2,1)} %get-tuple-element.50.base_hbm, f32[3,256,128]{2,1,0:T(8,128)S(1)} %get-tuple-element.51.upper_tiles_ref, f32[72,128]{1,0:T(8,128)S(1)} %get-tuple-element.52.top_ref, ...), custom_call_target="tpu_custom_call" | custom-call | tf_op jit(solution)/shard_map/tree_weights/pallas_call | solution.py:737
  42.8 1.1 %collective-permute-start.17 = (f32[136,128]{1,0:T(8,128)S(1)}, f32[136,128]{1,0:T(8,128)S(1)}, u32[]{:S(2)}, u32[]{:S(2)}) collective-permute-start(f32[136,128]{1,0:T(8,128)S(1)} %get-tuple-element.65), channel_id=1, source_target_pairs={{0,8},{8,0},{1,9},{9,1},{2,10},{10,2},{3,11},{11,3},{4,12},{12,4},... | collective-permute-start | bytes 208904 | tf_op jit(solution)/shard_map/ppermute | solution.py:592
  43.9 7.3 %near.1.near_ref = f32[64,2048]{1,0:T(8,128)S(1)} custom-call(s32[3,72]{1,0:T(4,128)} %get-tuple-element.70.tiles, bf16[4096,256]{1,0:T(8,128)(2,1)} %get-tuple-element.71.a_hbm, bf16[144,4096]{1,0:T(8,128)(2,1)S(1)} %get-tuple-element.67.tree_ref, bf16[64,4096]{1,0:T(8,128)(2,1)S(1)} %get-tuple-element.72.w_ref), custom_call_target="tpu_custom_call" | custom-call | tf_op jit(solution)/shard_map/near/pallas_call | solution.py:758
  51.3 2.2 %far.1 = (f32[4,64,512]{2,1,0:T(8,128)S(1)}, f32[4,64,512]{2,1,0:T(8,128)S(1)}) custom-call(f32[1,136,128]{2,1,0:T(8,128)S(1)} %bitcast.4, f32[4,1024]{1,0:T(4,128)S(1)} %get-tuple-element.60.slot_ref, f32[4,8,128]{2,1,0:T(8,128)S(1)} %get-tuple-element.66.info_ref, bf16[144,4096]{1,0:T(8,128)(2,1)S(1)} %get-tuple-element.67.tree_ref, ...), custom_call_target="tpu_custom_call" | custom-call | tf_op jit(solution)/shard_map/far/pallas_call | solution.py:775
  53.5 1.9 %collective-permute-done.18.got_ref = f32[4,64,512]{2,1,0:T(8,128)S(1)} collective-permute-done((f32[4,64,512]{2,1,0:T(8,128)S(1)}, f32[4,64,512]{2,1,0:T(8,128)S(1)}, u32[]{:S(2)}, u32[]{:S(2)}) %collective-permute-start.18) | collective-permute-done | bytes 524320 | tf_op jit(solution)/shard_map/ppermute | solution.py:649
  55.5 2.5 %collective-permute-start.19 = (f32[64,512]{1,0:T(8,128)S(1)}, f32[64,512]{1,0:T(8,128)S(1)}, u32[]{:S(2)}, u32[]{:S(2)}) collective-permute-start(f32[64,512]{1,0:T(8,128)S(1)} %get-tuple-element.75), channel_id=1, source_target_pairs={{0,4},{1,13},{2,6},{3,15},{4,0},{5,9},{6,2},{7,11},{8,12},{9,5},{1... | collective-permute-start | bytes 393224 | tf_op jit(solution)/shard_map/ppermute | solution.py:646
  59.9 8.3 %collective-permute-done.19.refs_0_ = f32[64,512]{1,0:T(8,128)S(1)} collective-permute-done((f32[64,512]{1,0:T(8,128)S(1)}, f32[64,512]{1,0:T(8,128)S(1)}, u32[]{:S(2)}, u32[]{:S(2)}) %collective-permute-start.19) | collective-permute-done | bytes 131104 | tf_op jit(solution)/shard_map/ppermute | solution.py:646
  68.9 1.2 %collective-permute-done.22.refs_3_ = f32[64,512]{1,0:T(8,128)S(1)} collective-permute-done((f32[64,512]{1,0:T(8,128)S(1)}, f32[64,512]{1,0:T(8,128)S(1)}, u32[]{:S(2)}, u32[]{:S(2)}) %collective-permute-start.22) | collective-permute-done | bytes 131104 | tf_op jit(solution)/shard_map/ppermute | solution.py:646
  70.8 1.0 %collective-permute-done.26.refs_7_ = f32[64,512]{1,0:T(8,128)S(1)} collective-permute-done((f32[64,512]{1,0:T(8,128)S(1)}, f32[64,512]{1,0:T(8,128)S(1)}, u32[]{:S(2)}, u32[]{:S(2)}) %collective-permute-start.26) | collective-permute-done | bytes 131104 | tf_op jit(solution)/shard_map/ppermute | solution.py:649
  71.7 1.9 %to_input_order.1 = f32[1024,128]{1,0:T(8,128)} custom-call(f32[8,128]{1,0:T(8,128)S(1)} %copy-done.1, f32[64,512]{1,0:T(8,128)S(1)} %collective-permute-done.19.refs_0_, f32[64,512]{1,0:T(8,128)S(1)} %collective-permute-done.20.refs_1_, f32[64,512]{1,0:T(8,128)S(1)} %collective-permute-done.21.refs_2_, f32[64,512]{1,0:T(8,128)S(1)} %collective-permute-done.22.refs_3_, ...), custom_call_target="tpu_custom_call" | custom-call | tf_op jit(solution)/shard_map/to_input_order/pallas_call | solution.py:812
  (43 shorter events, 8.1 us)
Async XLA Ops:
  2.7 1.6 %collective-permute-start = (f32[72,512]{1,0:T(8,128)}, f32[72,512]{1,0:T(8,128)S(1)}, u32[]{:S(2)}, u32[]{:S(2)}) collective-permute-start(f32[72,512]{1,0:T(8,128)} %get-tuple-element.43), channel_id=1, source_target_pairs={{0,0},{1,9},{2,2},{3,11},{4,4},{5,13},{6,6},{7,15},{8,8},{9,1},{10... | collective-permute-start | bytes 442376 | tf_op jit(solution)/shard_map/ppermute | solution.py:646
  4.3 8.8 %collective-permute-start.2 = (f32[72,512]{1,0:T(8,128)S(1)}, f32[72,512]{1,0:T(8,128)S(1)}, u32[]{:S(2)}, u32[]{:S(2)}) collective-permute-start(f32[72,512]{1,0:T(8,128)S(1)} %collective-permute-done.refs_0_), channel_id=1, source_target_pairs={{0,4},{2,6},{4,0},{6,2},{1,5},{3,7},{5,1},{7,3},{8,12},{10,14},{12... | collective-permute-start | bytes 442376 | tf_op jit(solution)/shard_map/ppermute | solution.py:675
  8.3 7.5 %collective-permute-start.1 = (f32[72,512]{1,0:T(8,128)S(1)}, f32[72,512]{1,0:T(8,128)S(1)}, u32[]{:S(2)}, u32[]{:S(2)}) collective-permute-start(f32[72,512]{1,0:T(8,128)S(1)} %collective-permute-done.refs_0_), channel_id=1, source_target_pairs={{0,2},{2,0},{4,6},{6,4},{1,3},{3,1},{5,7},{7,5},{8,10},{10,8},{12,... | collective-permute-start | bytes 442376 | tf_op jit(solution)/shard_map/ppermute | solution.py:675
  13.2 5.7 %collective-permute-start.3 = (f32[72,512]{1,0:T(8,128)S(1)}, f32[72,512]{1,0:T(8,128)S(1)}, u32[]{:S(2)}, u32[]{:S(2)}) collective-permute-start(f32[72,512]{1,0:T(8,128)S(1)} %collective-permute-done.2.refs_2_), channel_id=1, source_target_pairs={{0,2},{2,0},{4,6},{6,4},{1,3},{3,1},{5,7},{7,5},{8,10},{10,8},{12,... | collective-permute-start | bytes 442376 | tf_op jit(solution)/shard_map/ppermute | solution.py:675
  18.9 3.2 %collective-permute-start.8 = (f32[4,32,512]{2,1,0:T(8,128)S(1)}, f32[4,32,512]{2,1,0:T(8,128)S(1)}, u32[]{:S(2)}, u32[]{:S(2)}) collective-permute-start(f32[4,32,512]{2,1,0:T(8,128)S(1)} %get-tuple-element.54), channel_id=1, source_target_pairs={{0,1},{1,0},{2,3},{3,2},{4,5},{5,4},{6,7},{7,6},{8,9},{9,8},{10,11... | collective-permute-start | bytes 786440 | tf_op jit(solution)/shard_map/ppermute | solution.py:649
  20.9 3.5 %collective-permute-start.4 = (f32[72,512]{1,0:T(8,128)S(1)}, f32[72,512]{1,0:T(8,128)S(1)}, u32[]{:S(2)}, u32[]{:S(2)}) collective-permute-start(f32[72,512]{1,0:T(8,128)S(1)} %collective-permute-done.refs_0_), channel_id=1, source_target_pairs={{0,1},{1,0},{2,3},{3,2},{4,5},{5,4},{6,7},{7,6},{8,9},{9,8},{10,11... | collective-permute-start | bytes 442376 | tf_op jit(solution)/shard_map/ppermute | solution.py:649
  20.9 4.8 %collective-permute-start.5 = (f32[72,512]{1,0:T(8,128)S(1)}, f32[72,512]{1,0:T(8,128)S(1)}, u32[]{:S(2)}, u32[]{:S(2)}) collective-permute-start(f32[72,512]{1,0:T(8,128)S(1)} %collective-permute-done.1.refs_1_), channel_id=1, source_target_pairs={{0,1},{1,0},{2,3},{3,2},{4,5},{5,4},{6,7},{7,6},{8,9},{9,8},{10,11... | collective-permute-start | bytes 442376 | tf_op jit(solution)/shard_map/ppermute | solution.py:649
  21.4 5.0 %collective-permute-start.6 = (f32[72,512]{1,0:T(8,128)S(1)}, f32[72,512]{1,0:T(8,128)S(1)}, u32[]{:S(2)}, u32[]{:S(2)}) collective-permute-start(f32[72,512]{1,0:T(8,128)S(1)} %collective-permute-done.2.refs_2_), channel_id=1, source_target_pairs={{0,1},{1,0},{2,3},{3,2},{4,5},{5,4},{6,7},{7,6},{8,9},{9,8},{10,11... | collective-permute-start | bytes 442376 | tf_op jit(solution)/shard_map/ppermute | solution.py:649
  21.4 5.5 %collective-permute-start.7 = (f32[72,512]{1,0:T(8,128)S(1)}, f32[72,512]{1,0:T(8,128)S(1)}, u32[]{:S(2)}, u32[]{:S(2)}) collective-permute-start(f32[72,512]{1,0:T(8,128)S(1)} %collective-permute-done.3.refs_3_), channel_id=1, source_target_pairs={{0,1},{1,0},{2,3},{3,2},{4,5},{5,4},{6,7},{7,6},{8,9},{9,8},{10,11... | collective-permute-start | bytes 442376 | tf_op jit(solution)/shard_map/ppermute | solution.py:649
  22.1 12.8 %collective-permute-start.9 = (f32[64,512]{1,0:T(8,128)S(1)}, f32[64,512]{1,0:T(8,128)S(1)}, u32[]{:S(2)}, u32[]{:S(2)}) collective-permute-start(f32[64,512]{1,0:T(8,128)S(1)} %get-tuple-element.55), channel_id=1, source_target_pairs={{0,4},{1,13},{2,6},{3,15},{4,0},{5,9},{6,2},{7,11},{8,12},{9,5},{1... | collective-permute-start | bytes 393224 | tf_op jit(solution)/shard_map/ppermute | solution.py:646
  24.5 10.4 %collective-permute-start.10 = (f32[64,512]{1,0:T(8,128)S(1)}, f32[64,512]{1,0:T(8,128)S(1)}, u32[]{:S(2)}, u32[]{:S(2)}) collective-permute-start(f32[64,512]{1,0:T(8,128)S(1)} %get-tuple-element.56), channel_id=1, source_target_pairs={{0,6},{1,15},{2,4},{3,13},{4,2},{5,11},{6,0},{7,9},{8,14},{9,7},{1... | collective-permute-start | bytes 393224 | tf_op jit(solution)/shard_map/ppermute | solution.py:646
  25.7 9.1 %collective-permute-start.11 = (f32[64,512]{1,0:T(8,128)S(1)}, f32[64,512]{1,0:T(8,128)S(1)}, u32[]{:S(2)}, u32[]{:S(2)}) collective-permute-start(f32[64,512]{1,0:T(8,128)S(1)} %get-tuple-element.57), channel_id=1, source_target_pairs={{0,0},{1,9},{2,2},{3,11},{4,4},{5,13},{6,6},{7,15},{8,8},{9,1},{10... | collective-permute-start | bytes 393224 | tf_op jit(solution)/shard_map/ppermute | solution.py:646
  26.4 11.2 %collective-permute-start.12 = (f32[64,512]{1,0:T(8,128)S(1)}, f32[64,512]{1,0:T(8,128)S(1)}, u32[]{:S(2)}, u32[]{:S(2)}) collective-permute-start(f32[64,512]{1,0:T(8,128)S(1)} %get-tuple-element.58), channel_id=1, source_target_pairs={{0,2},{1,11},{2,0},{3,9},{4,6},{5,15},{6,4},{7,13},{8,10},{9,3},{1... | collective-permute-start | bytes 393224 | tf_op jit(solution)/shard_map/ppermute | solution.py:646
  38.1 1.4 %collective-permute-start.15 = (f32[64,512]{1,0:T(8,128)S(1)}, f32[64,512]{1,0:T(8,128)S(1)}, u32[]{:S(2)}, u32[]{:S(2)}) collective-permute-start(f32[64,512]{1,0:T(8,128)S(1)} %collective-permute-done.11.refs_2_), channel_id=1, source_target_pairs={{0,1},{1,0},{2,3},{3,2},{4,5},{5,4},{6,7},{7,6},{8,9},{9,8},{10,11... | collective-permute-start | bytes 393224 | tf_op jit(solution)/shard_map/ppermute | solution.py:649
  42.8 8.5 %collective-permute-start.17 = (f32[136,128]{1,0:T(8,128)S(1)}, f32[136,128]{1,0:T(8,128)S(1)}, u32[]{:S(2)}, u32[]{:S(2)}) collective-permute-start(f32[136,128]{1,0:T(8,128)S(1)} %get-tuple-element.65), channel_id=1, source_target_pairs={{0,8},{8,0},{1,9},{9,1},{2,10},{10,2},{3,11},{11,3},{4,12},{12,4},... | collective-permute-start | bytes 208904 | tf_op jit(solution)/shard_map/ppermute | solution.py:592
  53.4 2.0 %collective-permute-start.18 = (f32[4,64,512]{2,1,0:T(8,128)S(1)}, f32[4,64,512]{2,1,0:T(8,128)S(1)}, u32[]{:S(2)}, u32[]{:S(2)}) collective-permute-start(f32[4,64,512]{2,1,0:T(8,128)S(1)} %get-tuple-element.74), channel_id=1, source_target_pairs={{0,1},{1,0},{2,3},{3,2},{4,5},{5,4},{6,7},{7,6},{8,9},{9,8},{10,11... | collective-permute-start | bytes 1572872 | tf_op jit(solution)/shard_map/ppermute | solution.py:649
  55.5 12.7 %collective-permute-start.19 = (f32[64,512]{1,0:T(8,128)S(1)}, f32[64,512]{1,0:T(8,128)S(1)}, u32[]{:S(2)}, u32[]{:S(2)}) collective-permute-start(f32[64,512]{1,0:T(8,128)S(1)} %get-tuple-element.75), channel_id=1, source_target_pairs={{0,4},{1,13},{2,6},{3,15},{4,0},{5,9},{6,2},{7,11},{8,12},{9,5},{1... | collective-permute-start | bytes 393224 | tf_op jit(solution)/shard_map/ppermute | solution.py:646
  57.9 10.4 %collective-permute-start.20 = (f32[64,512]{1,0:T(8,128)S(1)}, f32[64,512]{1,0:T(8,128)S(1)}, u32[]{:S(2)}, u32[]{:S(2)}) collective-permute-start(f32[64,512]{1,0:T(8,128)S(1)} %get-tuple-element.76), channel_id=1, source_target_pairs={{0,6},{1,15},{2,4},{3,13},{4,2},{5,11},{6,0},{7,9},{8,14},{9,7},{1... | collective-permute-start | bytes 393224 | tf_op jit(solution)/shard_map/ppermute | solution.py:646
  58.6 10.0 %collective-permute-start.21 = (f32[64,512]{1,0:T(8,128)S(1)}, f32[64,512]{1,0:T(8,128)S(1)}, u32[]{:S(2)}, u32[]{:S(2)}) collective-permute-start(f32[64,512]{1,0:T(8,128)S(1)} %get-tuple-element.77), channel_id=1, source_target_pairs={{0,0},{1,9},{2,2},{3,11},{4,4},{5,13},{6,6},{7,15},{8,8},{9,1},{10... | collective-permute-start | bytes 393224 | tf_op jit(solution)/shard_map/ppermute | solution.py:646
  59.3 10.8 %collective-permute-start.22 = (f32[64,512]{1,0:T(8,128)S(1)}, f32[64,512]{1,0:T(8,128)S(1)}, u32[]{:S(2)}, u32[]{:S(2)}) collective-permute-start(f32[64,512]{1,0:T(8,128)S(1)} %get-tuple-element.78), channel_id=1, source_target_pairs={{0,2},{1,11},{2,0},{3,9},{4,6},{5,15},{6,4},{7,13},{8,10},{9,3},{1... | collective-permute-start | bytes 393224 | tf_op jit(solution)/shard_map/ppermute | solution.py:646
  68.1 2.6 %collective-permute-start.23 = (f32[64,512]{1,0:T(8,128)S(1)}, f32[64,512]{1,0:T(8,128)S(1)}, u32[]{:S(2)}, u32[]{:S(2)}) collective-permute-start(f32[64,512]{1,0:T(8,128)S(1)} %collective-permute-done.19.refs_0_), channel_id=1, source_target_pairs={{0,1},{1,0},{2,3},{3,2},{4,5},{5,4},{6,7},{7,6},{8,9},{9,8},{10,11... | collective-permute-start | bytes 393224 | tf_op jit(solution)/shard_map/ppermute | solution.py:649
  68.3 2.4 %collective-permute-start.24 = (f32[64,512]{1,0:T(8,128)S(1)}, f32[64,512]{1,0:T(8,128)S(1)}, u32[]{:S(2)}, u32[]{:S(2)}) collective-permute-start(f32[64,512]{1,0:T(8,128)S(1)} %collective-permute-done.20.refs_1_), channel_id=1, source_target_pairs={{0,1},{1,0},{2,3},{3,2},{4,5},{5,4},{6,7},{7,6},{8,9},{9,8},{10,11... | collective-permute-start | bytes 393224 | tf_op jit(solution)/shard_map/ppermute | solution.py:649
  68.6 2.1 %collective-permute-start.25 = (f32[64,512]{1,0:T(8,128)S(1)}, f32[64,512]{1,0:T(8,128)S(1)}, u32[]{:S(2)}, u32[]{:S(2)}) collective-permute-start(f32[64,512]{1,0:T(8,128)S(1)} %collective-permute-done.21.refs_2_), channel_id=1, source_target_pairs={{0,1},{1,0},{2,3},{3,2},{4,5},{5,4},{6,7},{7,6},{8,9},{9,8},{10,11... | collective-permute-start | bytes 393224 | tf_op jit(solution)/shard_map/ppermute | solution.py:649
  70.1 1.7 %collective-permute-start.26 = (f32[64,512]{1,0:T(8,128)S(1)}, f32[64,512]{1,0:T(8,128)S(1)}, u32[]{:S(2)}, u32[]{:S(2)}) collective-permute-start(f32[64,512]{1,0:T(8,128)S(1)} %collective-permute-done.22.refs_3_), channel_id=1, source_target_pairs={{0,1},{1,0},{2,3},{3,2},{4,5},{5,4},{6,7},{7,6},{8,9},{9,8},{10,11... | collective-permute-start | bytes 393224 | tf_op jit(solution)/shard_map/ppermute | solution.py:649
  (5 other events, 45.1 us)

commit v20 on v19

--- a/solution.py
+++ b/solution.py
@@ -552,7 +552,7 @@
 
 
 def far_first(blocks):
-    return sorted(range(blocks), key=lambda step: -(step * 2 // blocks))
+    return list(reversed(range(blocks)))
 
 
 def final_kernel(blocks, pos_ref, *refs):

time: 74.1 us -> 72.8 us (0.982)
  waiting for transfers between devices: 25 us -> 24.1 us
    ppermute x9, waiting for transfers between devices: 14.5 us -> 13.4 us  [swap(): return lax.ppermute(value, axes, pairs)]
    ppermute x9, starting transfers between devices: 10.7 us -> 11.8 us  [swap(): return lax.ppermute(value, axes, pairs)]
    ppermute x14, starting transfers between devices: 5.56 us -> 4.75 us  [other_core(): return lax.ppermute(value, 'rep', [(0, 1), (1, 0)])]
  transfers between devices with their start and end apart: 27 -> 27, of which waited for: 13 -> 14; matrix products, arithmetic and copies ran while one was open for 0% -> 0% of each run, Pallas kernels for 20% -> 20%
where the time goes in v20:
time: 72.8 us; the launch traced here: 72.7 us
  starting transfers between devices  24.4 us (34%)
  waiting for transfers between devices  24.1 us (33%)
  Pallas kernels  24 us (33%)
    ppermute x9, waiting for transfers between devices, swap(): return lax.ppermute(value, axes, pairs)  13.4 us
    ppermute x9, starting transfers between devices, swap(): return lax.ppermute(value, axes, pairs)  11.8 us
    pallas_call x1, Pallas kernels, body(): pl.pallas_call(functools.partial(near_kernel, layout), out_shape=vm((cols...  6.7 us
    ppermute x3, starting transfers between devices, body(): lax.ppermute(place[step], 'sub', [(i, i ^ stride) for i in range(blocks)])  6.51 us
    ppermute x3, waiting for transfers between devices, body(): lax.ppermute(place[step], 'sub', [(i, i ^ stride) for i in range(blocks)])  6.25 us
    pallas_call x1, Pallas kernels, body(): pl.pallas_call(functools.partial(points_kernel, layout, trees), out_shape...  5.69 us
    ppermute x14, starting transfers between devices, other_core(): return lax.ppermute(value, 'rep', [(0, 1), (1, 0)])  4.75 us
    ppermute x14, waiting for transfers between devices, other_core(): return lax.ppermute(value, 'rep', [(0, 1), (1, 0)])  4.47 us
  transfers between devices with their start and end apart: 27, of which 14 were waited for; matrix products, arithmetic and copies ran while one was open for 0% of the time, Pallas kernels for 20%

profile of v20, /device:TPU:0, one launch (start us, length us, event | category | flops | bytes accessed | tf_op | source)
XLA Modules:
  0.0 72.7 jit_solution(7314277916716344566)
XLA Ops:
  0.0 2.7 %sort_points.1 = (f32[72,512]{1,0:T(8,128)}, f32[8,128]{1,0:T(8,128)}) custom-call(s32[8,128]{1,0:T(8,128)} %bitcast.6, f32[64,1024]{1,0:T(8,128)} %bitcast.5, s32[1,128]{1,0:T(1,128)} %base_ref.1, s32[2,3]{1,0:T(2,128)} %flag_ref.1), custom_call_target="tpu_custom_call" | custom-call | tf_op jit(solution)/shard_map/sort_points/pallas_call | solution.py:628
  2.7 1.6 %collective-permute-start = (f32[72,512]{1,0:T(8,128)}, f32[72,512]{1,0:T(8,128)S(1)}, u32[]{:S(2)}, u32[]{:S(2)}) collective-permute-start(f32[72,512]{1,0:T(8,128)} %get-tuple-element.43), channel_id=1, source_target_pairs={{0,0},{1,9},{2,2},{3,11},{4,4},{5,13},{6,6},{7,15},{8,8},{9,1},{10... | collective-permute-start | bytes 442376 | tf_op jit(solution)/shard_map/ppermute | solution.py:646
  4.3 4.0 %collective-permute-start.2 = (f32[72,512]{1,0:T(8,128)S(1)}, f32[72,512]{1,0:T(8,128)S(1)}, u32[]{:S(2)}, u32[]{:S(2)}) collective-permute-start(f32[72,512]{1,0:T(8,128)S(1)} %collective-permute-done.refs_0_), channel_id=1, source_target_pairs={{0,4},{2,6},{4,0},{6,2},{1,5},{3,7},{5,1},{7,3},{8,12},{10,14},{12... | collective-permute-start | bytes 442376 | tf_op jit(solution)/shard_map/ppermute | solution.py:675
  8.3 1.6 %collective-permute-start.1 = (f32[72,512]{1,0:T(8,128)S(1)}, f32[72,512]{1,0:T(8,128)S(1)}, u32[]{:S(2)}, u32[]{:S(2)}) collective-permute-start(f32[72,512]{1,0:T(8,128)S(1)} %collective-permute-done.refs_0_), channel_id=1, source_target_pairs={{0,2},{2,0},{4,6},{6,4},{1,3},{3,1},{5,7},{7,5},{8,10},{10,8},{12,... | collective-permute-start | bytes 442376 | tf_op jit(solution)/shard_map/ppermute | solution.py:675
  9.9 3.2 %collective-permute-done.2.refs_2_ = f32[72,512]{1,0:T(8,128)S(1)} collective-permute-done((f32[72,512]{1,0:T(8,128)S(1)}, f32[72,512]{1,0:T(8,128)S(1)}, u32[]{:S(2)}, u32[]{:S(2)}) %collective-permute-start.2) | collective-permute-done | bytes 147488 | tf_op jit(solution)/shard_map/ppermute | solution.py:675
  13.2 0.9 %collective-permute-start.3 = (f32[72,512]{1,0:T(8,128)S(1)}, f32[72,512]{1,0:T(8,128)S(1)}, u32[]{:S(2)}, u32[]{:S(2)}) collective-permute-start(f32[72,512]{1,0:T(8,128)S(1)} %collective-permute-done.2.refs_2_), channel_id=1, source_target_pairs={{0,2},{2,0},{4,6},{6,4},{1,3},{3,1},{5,7},{7,5},{8,10},{10,8},{12,... | collective-permute-start | bytes 442376 | tf_op jit(solution)/shard_map/ppermute | solution.py:675
  14.1 1.8 %sort_weights.1 = (f32[4,32,512]{2,1,0:T(8,128)S(1)}, f32[4,32,512]{2,1,0:T(8,128)S(1)}) custom-call(f32[8,128]{1,0:T(8,128)} %get-tuple-element.42.pos_ref, f32[1024,128]{1,0:T(8,128)} %refs_8_.1), custom_call_target="tpu_custom_call" | custom-call | tf_op jit(solution)/shard_map/sort_weights/pallas_call | solution.py:656
  15.9 3.0 %collective-permute-done.3.refs_3_ = f32[72,512]{1,0:T(8,128)S(1)} collective-permute-done((f32[72,512]{1,0:T(8,128)S(1)}, f32[72,512]{1,0:T(8,128)S(1)}, u32[]{:S(2)}, u32[]{:S(2)}) %collective-permute-start.3) | collective-permute-done | bytes 147488 | tf_op jit(solution)/shard_map/ppermute | solution.py:675
  18.9 2.0 %collective-permute-start.8 = (f32[4,32,512]{2,1,0:T(8,128)S(1)}, f32[4,32,512]{2,1,0:T(8,128)S(1)}, u32[]{:S(2)}, u32[]{:S(2)}) collective-permute-start(f32[4,32,512]{2,1,0:T(8,128)S(1)} %get-tuple-element.54), channel_id=1, source_target_pairs={{0,1},{1,0},{2,3},{3,2},{4,5},{5,4},{6,7},{7,6},{8,9},{9,8},{10,11... | collective-permute-start | bytes 786440 | tf_op jit(solution)/shard_map/ppermute | solution.py:649
  22.1 3.5 %collective-permute-start.9 = (f32[64,512]{1,0:T(8,128)S(1)}, f32[64,512]{1,0:T(8,128)S(1)}, u32[]{:S(2)}, u32[]{:S(2)}) collective-permute-start(f32[64,512]{1,0:T(8,128)S(1)} %get-tuple-element.55), channel_id=1, source_target_pairs={{0,6},{1,15},{2,4},{3,13},{4,2},{5,11},{6,0},{7,9},{8,14},{9,7},{1... | collective-permute-start | bytes 393224 | tf_op jit(solution)/shard_map/ppermute | solution.py:646
  25.6 0.9 %collective-permute-start.11 = (f32[64,512]{1,0:T(8,128)S(1)}, f32[64,512]{1,0:T(8,128)S(1)}, u32[]{:S(2)}, u32[]{:S(2)}) collective-permute-start(f32[64,512]{1,0:T(8,128)S(1)} %get-tuple-element.57), channel_id=1, source_target_pairs={{0,2},{1,11},{2,0},{3,9},{4,6},{5,15},{6,4},{7,13},{8,10},{9,3},{1... | collective-permute-start | bytes 393224 | tf_op jit(solution)/shard_map/ppermute | solution.py:646
  27.3 5.7 %tree_points.1 = (bf16[144,4096]{1,0:T(8,128)(2,1)S(1)}, bf16[4096,256]{1,0:T(8,128)(2,1)}, bf16[4,1024,128]{2,1,0:T(8,128)(2,1)}, bf16[896,256]{1,0:T(8,128)(2,...) custom-call(s32[1,8]{1,0:T(1,128)} %count_ref.1, ...), custom_call_target="tpu_custom_call" | custom-call | tf_op jit(solution)/shard_map/tree_points/pallas_call | solution.py:705
  33.0 4.0 %collective-permute-done.10.refs_1_ = f32[64,512]{1,0:T(8,128)S(1)} collective-permute-done((f32[64,512]{1,0:T(8,128)S(1)}, f32[64,512]{1,0:T(8,128)S(1)}, u32[]{:S(2)}, u32[]{:S(2)}) %collective-permute-start.10) | collective-permute-done | bytes 131104 | tf_op jit(solution)/shard_map/ppermute | solution.py:646
  39.2 2.9 %tree_weights.1 = (bf16[64,4096]{1,0:T(8,128)(2,1)S(1)}, bf16[128,896]{1,0:T(8,128)(2,1)S(1)}, f32[136,128]{1,0:T(8,128)S(1)}) custom-call(bf16[4,1024,128]{2,1,0:T(8,128)(2,1)} %get-tuple-element.50.base_hbm, f32[3,256,128]{2,1,0:T(8,128)S(1)} %get-tuple-element.51.upper_tiles_ref, f32[72,128]{1,0:T(8,128)S(1)} %get-tuple-element.52.top_ref, ...), custom_call_target="tpu_custom_call" | custom-call | tf_op jit(solution)/shard_map/tree_weights/pallas_call | solution.py:737
  42.1 1.4 %collective-permute-start.17 = (f32[136,128]{1,0:T(8,128)S(1)}, f32[136,128]{1,0:T(8,128)S(1)}, u32[]{:S(2)}, u32[]{:S(2)}) collective-permute-start(f32[136,128]{1,0:T(8,128)S(1)} %get-tuple-element.65), channel_id=1, source_target_pairs={{0,8},{8,0},{1,9},{9,1},{2,10},{10,2},{3,11},{11,3},{4,12},{12,4},... | collective-permute-start | bytes 208904 | tf_op jit(solution)/shard_map/ppermute | solution.py:592
  43.5 6.7 %near.1.near_ref = f32[64,2048]{1,0:T(8,128)S(1)} custom-call(s32[3,72]{1,0:T(4,128)} %get-tuple-element.70.tiles, bf16[4096,256]{1,0:T(8,128)(2,1)} %get-tuple-element.71.a_hbm, bf16[144,4096]{1,0:T(8,128)(2,1)S(1)} %get-tuple-element.67.tree_ref, bf16[64,4096]{1,0:T(8,128)(2,1)S(1)} %get-tuple-element.72.w_ref), custom_call_target="tpu_custom_call" | custom-call | tf_op jit(solution)/shard_map/near/pallas_call | solution.py:758
  50.2 2.2 %far.1 = (f32[4,64,512]{2,1,0:T(8,128)S(1)}, f32[4,64,512]{2,1,0:T(8,128)S(1)}) custom-call(f32[1,136,128]{2,1,0:T(8,128)S(1)} %bitcast.4, f32[4,1024]{1,0:T(4,128)S(1)} %get-tuple-element.60.slot_ref, f32[4,8,128]{2,1,0:T(8,128)S(1)} %get-tuple-element.66.info_ref, bf16[144,4096]{1,0:T(8,128)(2,1)S(1)} %get-tuple-element.67.tree_ref, ...), custom_call_target="tpu_custom_call" | custom-call | tf_op jit(solution)/shard_map/far/pallas_call | solution.py:775
  52.4 1.9 %collective-permute-done.18.got_ref = f32[4,64,512]{2,1,0:T(8,128)S(1)} collective-permute-done((f32[4,64,512]{2,1,0:T(8,128)S(1)}, f32[4,64,512]{2,1,0:T(8,128)S(1)}, u32[]{:S(2)}, u32[]{:S(2)}) %collective-permute-start.18) | collective-permute-done | bytes 524320 | tf_op jit(solution)/shard_map/ppermute | solution.py:649
  54.4 2.9 %collective-permute-start.19 = (f32[64,512]{1,0:T(8,128)S(1)}, f32[64,512]{1,0:T(8,128)S(1)}, u32[]{:S(2)}, u32[]{:S(2)}) collective-permute-start(f32[64,512]{1,0:T(8,128)S(1)} %get-tuple-element.75), channel_id=1, source_target_pairs={{0,6},{1,15},{2,4},{3,13},{4,2},{5,11},{6,0},{7,9},{8,14},{9,7},{1... | collective-permute-start | bytes 393224 | tf_op jit(solution)/shard_map/ppermute | solution.py:646
  57.3 1.6 %collective-permute-start.21 = (f32[64,512]{1,0:T(8,128)S(1)}, f32[64,512]{1,0:T(8,128)S(1)}, u32[]{:S(2)}, u32[]{:S(2)}) collective-permute-start(f32[64,512]{1,0:T(8,128)S(1)} %get-tuple-element.77), channel_id=1, source_target_pairs={{0,2},{1,11},{2,0},{3,9},{4,6},{5,15},{6,4},{7,13},{8,10},{9,3},{1... | collective-permute-start | bytes 393224 | tf_op jit(solution)/shard_map/ppermute | solution.py:646
  59.5 3.3 %collective-permute-done.19.refs_0_ = f32[64,512]{1,0:T(8,128)S(1)} collective-permute-done((f32[64,512]{1,0:T(8,128)S(1)}, f32[64,512]{1,0:T(8,128)S(1)}, u32[]{:S(2)}, u32[]{:S(2)}) %collective-permute-start.19) | collective-permute-done | bytes 131104 | tf_op jit(solution)/shard_map/ppermute | solution.py:646
  62.8 6.1 %collective-permute-done.20.refs_1_ = f32[64,512]{1,0:T(8,128)S(1)} collective-permute-done((f32[64,512]{1,0:T(8,128)S(1)}, f32[64,512]{1,0:T(8,128)S(1)}, u32[]{:S(2)}, u32[]{:S(2)}) %collective-permute-start.20) | collective-permute-done | bytes 131104 | tf_op jit(solution)/shard_map/ppermute | solution.py:646
  69.5 0.8 %collective-permute-done.24.refs_5_ = f32[64,512]{1,0:T(8,128)S(1)} collective-permute-done((f32[64,512]{1,0:T(8,128)S(1)}, f32[64,512]{1,0:T(8,128)S(1)}, u32[]{:S(2)}, u32[]{:S(2)}) %collective-permute-start.24) | collective-permute-done | bytes 131104 | tf_op jit(solution)/shard_map/ppermute | solution.py:649
  70.7 1.9 %to_input_order.1 = f32[1024,128]{1,0:T(8,128)} custom-call(f32[8,128]{1,0:T(8,128)S(1)} %copy-done.1, f32[64,512]{1,0:T(8,128)S(1)} %collective-permute-done.19.refs_0_, f32[64,512]{1,0:T(8,128)S(1)} %collective-permute-done.20.refs_1_, f32[64,512]{1,0:T(8,128)S(1)} %collective-permute-done.21.refs_2_, f32[64,512]{1,0:T(8,128)S(1)} %collective-permute-done.22.refs_3_, ...), custom_call_target="tpu_custom_call" | custom-call | tf_op jit(solution)/shard_map/to_input_order/pallas_call | solution.py:812
  (43 shorter events, 6.0 us)
Async XLA Ops:
  2.7 1.6 %collective-permute-start = (f32[72,512]{1,0:T(8,128)}, f32[72,512]{1,0:T(8,128)S(1)}, u32[]{:S(2)}, u32[]{:S(2)}) collective-permute-start(f32[72,512]{1,0:T(8,128)} %get-tuple-element.43), channel_id=1, source_target_pairs={{0,0},{1,9},{2,2},{3,11},{4,4},{5,13},{6,6},{7,15},{8,8},{9,1},{10... | collective-permute-start | bytes 442376 | tf_op jit(solution)/shard_map/ppermute | solution.py:646
  4.3 8.8 %collective-permute-start.2 = (f32[72,512]{1,0:T(8,128)S(1)}, f32[72,512]{1,0:T(8,128)S(1)}, u32[]{:S(2)}, u32[]{:S(2)}) collective-permute-start(f32[72,512]{1,0:T(8,128)S(1)} %collective-permute-done.refs_0_), channel_id=1, source_target_pairs={{0,4},{2,6},{4,0},{6,2},{1,5},{3,7},{5,1},{7,3},{8,12},{10,14},{12... | collective-permute-start | bytes 442376 | tf_op jit(solution)/shard_map/ppermute | solution.py:675
  8.3 7.5 %collective-permute-start.1 = (f32[72,512]{1,0:T(8,128)S(1)}, f32[72,512]{1,0:T(8,128)S(1)}, u32[]{:S(2)}, u32[]{:S(2)}) collective-permute-start(f32[72,512]{1,0:T(8,128)S(1)} %collective-permute-done.refs_0_), channel_id=1, source_target_pairs={{0,2},{2,0},{4,6},{6,4},{1,3},{3,1},{5,7},{7,5},{8,10},{10,8},{12,... | collective-permute-start | bytes 442376 | tf_op jit(solution)/shard_map/ppermute | solution.py:675
  13.2 5.7 %collective-permute-start.3 = (f32[72,512]{1,0:T(8,128)S(1)}, f32[72,512]{1,0:T(8,128)S(1)}, u32[]{:S(2)}, u32[]{:S(2)}) collective-permute-start(f32[72,512]{1,0:T(8,128)S(1)} %collective-permute-done.2.refs_2_), channel_id=1, source_target_pairs={{0,2},{2,0},{4,6},{6,4},{1,3},{3,1},{5,7},{7,5},{8,10},{10,8},{12,... | collective-permute-start | bytes 442376 | tf_op jit(solution)/shard_map/ppermute | solution.py:675
  18.9 3.2 %collective-permute-start.8 = (f32[4,32,512]{2,1,0:T(8,128)S(1)}, f32[4,32,512]{2,1,0:T(8,128)S(1)}, u32[]{:S(2)}, u32[]{:S(2)}) collective-permute-start(f32[4,32,512]{2,1,0:T(8,128)S(1)} %get-tuple-element.54), channel_id=1, source_target_pairs={{0,1},{1,0},{2,3},{3,2},{4,5},{5,4},{6,7},{7,6},{8,9},{9,8},{10,11... | collective-permute-start | bytes 786440 | tf_op jit(solution)/shard_map/ppermute | solution.py:649
  20.9 4.7 %collective-permute-start.4 = (f32[72,512]{1,0:T(8,128)S(1)}, f32[72,512]{1,0:T(8,128)S(1)}, u32[]{:S(2)}, u32[]{:S(2)}) collective-permute-start(f32[72,512]{1,0:T(8,128)S(1)} %collective-permute-done.refs_0_), channel_id=1, source_target_pairs={{0,1},{1,0},{2,3},{3,2},{4,5},{5,4},{6,7},{7,6},{8,9},{9,8},{10,11... | collective-permute-start | bytes 442376 | tf_op jit(solution)/shard_map/ppermute | solution.py:649
  20.9 4.7 %collective-permute-start.5 = (f32[72,512]{1,0:T(8,128)S(1)}, f32[72,512]{1,0:T(8,128)S(1)}, u32[]{:S(2)}, u32[]{:S(2)}) collective-permute-start(f32[72,512]{1,0:T(8,128)S(1)} %collective-permute-done.1.refs_1_), channel_id=1, source_target_pairs={{0,1},{1,0},{2,3},{3,2},{4,5},{5,4},{6,7},{7,6},{8,9},{9,8},{10,11... | collective-permute-start | bytes 442376 | tf_op jit(solution)/shard_map/ppermute | solution.py:649
  21.4 5.2 %collective-permute-start.6 = (f32[72,512]{1,0:T(8,128)S(1)}, f32[72,512]{1,0:T(8,128)S(1)}, u32[]{:S(2)}, u32[]{:S(2)}) collective-permute-start(f32[72,512]{1,0:T(8,128)S(1)} %collective-permute-done.2.refs_2_), channel_id=1, source_target_pairs={{0,1},{1,0},{2,3},{3,2},{4,5},{5,4},{6,7},{7,6},{8,9},{9,8},{10,11... | collective-permute-start | bytes 442376 | tf_op jit(solution)/shard_map/ppermute | solution.py:649
  21.4 5.8 %collective-permute-start.7 = (f32[72,512]{1,0:T(8,128)S(1)}, f32[72,512]{1,0:T(8,128)S(1)}, u32[]{:S(2)}, u32[]{:S(2)}) collective-permute-start(f32[72,512]{1,0:T(8,128)S(1)} %collective-permute-done.3.refs_3_), channel_id=1, source_target_pairs={{0,1},{1,0},{2,3},{3,2},{4,5},{5,4},{6,7},{7,6},{8,9},{9,8},{10,11... | collective-permute-start | bytes 442376 | tf_op jit(solution)/shard_map/ppermute | solution.py:649
  22.1 10.8 %collective-permute-start.9 = (f32[64,512]{1,0:T(8,128)S(1)}, f32[64,512]{1,0:T(8,128)S(1)}, u32[]{:S(2)}, u32[]{:S(2)}) collective-permute-start(f32[64,512]{1,0:T(8,128)S(1)} %get-tuple-element.55), channel_id=1, source_target_pairs={{0,6},{1,15},{2,4},{3,13},{4,2},{5,11},{6,0},{7,9},{8,14},{9,7},{1... | collective-permute-start | bytes 393224 | tf_op jit(solution)/shard_map/ppermute | solution.py:646
  25.6 11.4 %collective-permute-start.10 = (f32[64,512]{1,0:T(8,128)S(1)}, f32[64,512]{1,0:T(8,128)S(1)}, u32[]{:S(2)}, u32[]{:S(2)}) collective-permute-start(f32[64,512]{1,0:T(8,128)S(1)} %get-tuple-element.56), channel_id=1, source_target_pairs={{0,4},{1,13},{2,6},{3,15},{4,0},{5,9},{6,2},{7,11},{8,12},{9,5},{1... | collective-permute-start | bytes 393224 | tf_op jit(solution)/shard_map/ppermute | solution.py:646
  25.6 11.4 %collective-permute-start.11 = (f32[64,512]{1,0:T(8,128)S(1)}, f32[64,512]{1,0:T(8,128)S(1)}, u32[]{:S(2)}, u32[]{:S(2)}) collective-permute-start(f32[64,512]{1,0:T(8,128)S(1)} %get-tuple-element.57), channel_id=1, source_target_pairs={{0,2},{1,11},{2,0},{3,9},{4,6},{5,15},{6,4},{7,13},{8,10},{9,3},{1... | collective-permute-start | bytes 393224 | tf_op jit(solution)/shard_map/ppermute | solution.py:646
  26.6 10.4 %collective-permute-start.12 = (f32[64,512]{1,0:T(8,128)S(1)}, f32[64,512]{1,0:T(8,128)S(1)}, u32[]{:S(2)}, u32[]{:S(2)}) collective-permute-start(f32[64,512]{1,0:T(8,128)S(1)} %get-tuple-element.58), channel_id=1, source_target_pairs={{0,0},{1,9},{2,2},{3,11},{4,4},{5,13},{6,6},{7,15},{8,8},{9,1},{10... | collective-permute-start | bytes 393224 | tf_op jit(solution)/shard_map/ppermute | solution.py:646
  37.0 1.4 %collective-permute-start.13 = (f32[64,512]{1,0:T(8,128)S(1)}, f32[64,512]{1,0:T(8,128)S(1)}, u32[]{:S(2)}, u32[]{:S(2)}) collective-permute-start(f32[64,512]{1,0:T(8,128)S(1)} %collective-permute-done.9.refs_0_), channel_id=1, source_target_pairs={{0,1},{1,0},{2,3},{3,2},{4,5},{5,4},{6,7},{7,6},{8,9},{9,8},{10,11... | collective-permute-start | bytes 393224 | tf_op jit(solution)/shard_map/ppermute | solution.py:649
  37.5 1.3 %collective-permute-start.15 = (f32[64,512]{1,0:T(8,128)S(1)}, f32[64,512]{1,0:T(8,128)S(1)}, u32[]{:S(2)}, u32[]{:S(2)}) collective-permute-start(f32[64,512]{1,0:T(8,128)S(1)} %collective-permute-done.11.refs_2_), channel_id=1, source_target_pairs={{0,1},{1,0},{2,3},{3,2},{4,5},{5,4},{6,7},{7,6},{8,9},{9,8},{10,11... | collective-permute-start | bytes 393224 | tf_op jit(solution)/shard_map/ppermute | solution.py:649
  42.1 8.1 %collective-permute-start.17 = (f32[136,128]{1,0:T(8,128)S(1)}, f32[136,128]{1,0:T(8,128)S(1)}, u32[]{:S(2)}, u32[]{:S(2)}) collective-permute-start(f32[136,128]{1,0:T(8,128)S(1)} %get-tuple-element.65), channel_id=1, source_target_pairs={{0,8},{8,0},{1,9},{9,1},{2,10},{10,2},{3,11},{11,3},{4,12},{12,4},... | collective-permute-start | bytes 208904 | tf_op jit(solution)/shard_map/ppermute | solution.py:592
  52.4 2.0 %collective-permute-start.18 = (f32[4,64,512]{2,1,0:T(8,128)S(1)}, f32[4,64,512]{2,1,0:T(8,128)S(1)}, u32[]{:S(2)}, u32[]{:S(2)}) collective-permute-start(f32[4,64,512]{2,1,0:T(8,128)S(1)} %get-tuple-element.74), channel_id=1, source_target_pairs={{0,1},{1,0},{2,3},{3,2},{4,5},{5,4},{6,7},{7,6},{8,9},{9,8},{10,11... | collective-permute-start | bytes 1572872 | tf_op jit(solution)/shard_map/ppermute | solution.py:649
  54.4 8.4 %collective-permute-start.19 = (f32[64,512]{1,0:T(8,128)S(1)}, f32[64,512]{1,0:T(8,128)S(1)}, u32[]{:S(2)}, u32[]{:S(2)}) collective-permute-start(f32[64,512]{1,0:T(8,128)S(1)} %get-tuple-element.75), channel_id=1, source_target_pairs={{0,6},{1,15},{2,4},{3,13},{4,2},{5,11},{6,0},{7,9},{8,14},{9,7},{1... | collective-permute-start | bytes 393224 | tf_op jit(solution)/shard_map/ppermute | solution.py:646
  57.3 11.6 %collective-permute-start.20 = (f32[64,512]{1,0:T(8,128)S(1)}, f32[64,512]{1,0:T(8,128)S(1)}, u32[]{:S(2)}, u32[]{:S(2)}) collective-permute-start(f32[64,512]{1,0:T(8,128)S(1)} %get-tuple-element.76), channel_id=1, source_target_pairs={{0,4},{1,13},{2,6},{3,15},{4,0},{5,9},{6,2},{7,11},{8,12},{9,5},{1... | collective-permute-start | bytes 393224 | tf_op jit(solution)/shard_map/ppermute | solution.py:646
  57.3 11.6 %collective-permute-start.21 = (f32[64,512]{1,0:T(8,128)S(1)}, f32[64,512]{1,0:T(8,128)S(1)}, u32[]{:S(2)}, u32[]{:S(2)}) collective-permute-start(f32[64,512]{1,0:T(8,128)S(1)} %get-tuple-element.77), channel_id=1, source_target_pairs={{0,2},{1,11},{2,0},{3,9},{4,6},{5,15},{6,4},{7,13},{8,10},{9,3},{1... | collective-permute-start | bytes 393224 | tf_op jit(solution)/shard_map/ppermute | solution.py:646
  58.9 10.5 %collective-permute-start.22 = (f32[64,512]{1,0:T(8,128)S(1)}, f32[64,512]{1,0:T(8,128)S(1)}, u32[]{:S(2)}, u32[]{:S(2)}) collective-permute-start(f32[64,512]{1,0:T(8,128)S(1)} %get-tuple-element.78), channel_id=1, source_target_pairs={{0,0},{1,9},{2,2},{3,11},{4,4},{5,13},{6,6},{7,15},{8,8},{9,1},{10... | collective-permute-start | bytes 393224 | tf_op jit(solution)/shard_map/ppermute | solution.py:646
  62.8 6.7 %collective-permute-start.23 = (f32[64,512]{1,0:T(8,128)S(1)}, f32[64,512]{1,0:T(8,128)S(1)}, u32[]{:S(2)}, u32[]{:S(2)}) collective-permute-start(f32[64,512]{1,0:T(8,128)S(1)} %collective-permute-done.19.refs_0_), channel_id=1, source_target_pairs={{0,1},{1,0},{2,3},{3,2},{4,5},{5,4},{6,7},{7,6},{8,9},{9,8},{10,11... | collective-permute-start | bytes 393224 | tf_op jit(solution)/shard_map/ppermute | solution.py:649
  68.9 1.5 %collective-permute-start.25 = (f32[64,512]{1,0:T(8,128)S(1)}, f32[64,512]{1,0:T(8,128)S(1)}, u32[]{:S(2)}, u32[]{:S(2)}) collective-permute-start(f32[64,512]{1,0:T(8,128)S(1)} %collective-permute-done.21.refs_2_), channel_id=1, source_target_pairs={{0,1},{1,0},{2,3},{3,2},{4,5},{5,4},{6,7},{7,6},{8,9},{9,8},{10,11... | collective-permute-start | bytes 393224 | tf_op jit(solution)/shard_map/ppermute | solution.py:649
  69.4 1.3 %collective-permute-start.26 = (f32[64,512]{1,0:T(8,128)S(1)}, f32[64,512]{1,0:T(8,128)S(1)}, u32[]{:S(2)}, u32[]{:S(2)}) collective-permute-start(f32[64,512]{1,0:T(8,128)S(1)} %collective-permute-done.22.refs_3_), channel_id=1, source_target_pairs={{0,1},{1,0},{2,3},{3,2},{4,5},{5,4},{6,7},{7,6},{8,9},{9,8},{10,11... | collective-permute-start | bytes 393224 | tf_op jit(solution)/shard_map/ppermute | solution.py:649
  (5 other events, 45.2 us)

commit v21 on v20

--- a/solution.py
+++ b/solution.py
@@ -675,7 +675,7 @@
                 place[step | stride] = lax.ppermute(place[step], "sub", [(i, i ^ stride) for i in range(blocks)])
             stride //= 2
         kept, sent = sorted_light(pos)
-        place, kept, sent = lax.optimization_barrier((place, kept, sent))
+        tied, kept, sent = lax.optimization_barrier((place[1], kept, sent))
         light = pl.pallas_call(
             join_kernel,
             out_shape=(shaped((cols, part), f32),) * blocks,
@@ -684,6 +684,7 @@
             compiler_params=params(40),
             name="join_cores",
         )(kept, other_core(sent))
+        place, light = lax.optimization_barrier((place, light))
         theirs = {step: other_core(one) for step, one in place.items()}
         place = [place[step] for step in range(blocks)] + [theirs[step] for step in range(blocks)]
         light = [swap(light[step], step) for step in far_first(blocks)]

time: 72.8 us -> 74.5 us (1.023)
  starting transfers between devices: 24.4 us -> 27.4 us
  waiting for transfers between devices: 24.1 us -> 22.7 us
    ppermute x14, starting transfers between devices: 4.75 us -> 7.53 us  [other_core(): return lax.ppermute(value, 'rep', [(0, 1), (1, 0)])]
    ppermute x3, waiting for transfers between devices: 6.25 us -> 4.17 us  [body(): lax.ppermute(place[step], 'sub', [(i, i ^ stride) for i in range(blocks)])]
  transfers between devices with their start and end apart: 27 -> 27, of which waited for: 14 -> 13; matrix products, arithmetic and copies ran while one was open for 0% -> 0% of each run, Pallas kernels for 20% -> 19%
where the time goes in v21:
time: 74.5 us; the launch traced here: 74.2 us
  starting transfers between devices  27.4 us (37%)
  Pallas kernels  24 us (32%)
  waiting for transfers between devices  22.7 us (30%)
    ppermute x9, waiting for transfers between devices, swap(): return lax.ppermute(value, axes, pairs)  13.8 us
    ppermute x9, starting transfers between devices, swap(): return lax.ppermute(value, axes, pairs)  12.5 us
    ppermute x14, starting transfers between devices, other_core(): return lax.ppermute(value, 'rep', [(0, 1), (1, 0)])  7.53 us
    pallas_call x1, Pallas kernels, body(): pl.pallas_call(functools.partial(near_kernel, layout), out_shape=vm((cols...  6.7 us
    ppermute x3, starting transfers between devices, body(): lax.ppermute(place[step], 'sub', [(i, i ^ stride) for i in range(blocks)])  6.23 us
    pallas_call x1, Pallas kernels, body(): pl.pallas_call(functools.partial(points_kernel, layout, trees), out_shape...  5.68 us
    ppermute x14, waiting for transfers between devices, other_core(): return lax.ppermute(value, 'rep', [(0, 1), (1, 0)])  4.74 us
    ppermute x3, waiting for transfers between devices, body(): lax.ppermute(place[step], 'sub', [(i, i ^ stride) for i in range(blocks)])  4.17 us
  transfers between devices with their start and end apart: 27, of which 13 were waited for; matrix products, arithmetic and copies ran while one was open for 0% of the time, Pallas kernels for 19%

profile of v21, /device:TPU:0, one launch (start us, length us, event | category | flops | bytes accessed | tf_op | source)
XLA Modules:
  0.0 74.2 jit_solution(13721986878109223221)
XLA Ops:
  0.0 2.7 %sort_points.1 = (f32[72,512]{1,0:T(8,128)}, f32[8,128]{1,0:T(8,128)}) custom-call(s32[8,128]{1,0:T(8,128)} %bitcast.6, f32[64,1024]{1,0:T(8,128)} %bitcast.5, s32[1,128]{1,0:T(1,128)} %base_ref.1, s32[2,3]{1,0:T(2,128)} %flag_ref.1), custom_call_target="tpu_custom_call" | custom-call | tf_op jit(solution)/shard_map/sort_points/pallas_call | solution.py:628
  2.7 1.6 %collective-permute-start = (f32[72,512]{1,0:T(8,128)}, f32[72,512]{1,0:T(8,128)S(1)}, u32[]{:S(2)}, u32[]{:S(2)}) collective-permute-start(f32[72,512]{1,0:T(8,128)} %get-tuple-element.47), channel_id=1, source_target_pairs={{0,0},{1,9},{2,2},{3,11},{4,4},{5,13},{6,6},{7,15},{8,8},{9,1},{10... | collective-permute-start | bytes 442376 | tf_op jit(solution)/shard_map/ppermute | solution.py:646
  4.3 3.0 %collective-permute-start.1 = (f32[72,512]{1,0:T(8,128)S(1)}, f32[72,512]{1,0:T(8,128)S(1)}, u32[]{:S(2)}, u32[]{:S(2)}) collective-permute-start(f32[72,512]{1,0:T(8,128)S(1)} %collective-permute-done.refs_0_), channel_id=1, source_target_pairs={{0,2},{2,0},{4,6},{6,4},{1,3},{3,1},{5,7},{7,5},{8,10},{10,8},{12,... | collective-permute-start | bytes 442376 | tf_op jit(solution)/shard_map/ppermute | solution.py:675
  7.3 2.6 %collective-permute-start.2 = (f32[72,512]{1,0:T(8,128)S(1)}, f32[72,512]{1,0:T(8,128)S(1)}, u32[]{:S(2)}, u32[]{:S(2)}) collective-permute-start(f32[72,512]{1,0:T(8,128)S(1)} %collective-permute-done.refs_0_), channel_id=1, source_target_pairs={{0,4},{2,6},{4,0},{6,2},{1,5},{3,7},{5,1},{7,3},{8,12},{10,14},{12... | collective-permute-start | bytes 442376 | tf_op jit(solution)/shard_map/ppermute | solution.py:675
  9.9 1.8 %sort_weights.1 = (f32[4,32,512]{2,1,0:T(8,128)S(1)}, f32[4,32,512]{2,1,0:T(8,128)S(1)}) custom-call(f32[8,128]{1,0:T(8,128)} %get-tuple-element.46.pos_ref, f32[1024,128]{1,0:T(8,128)} %refs_8_.1), custom_call_target="tpu_custom_call" | custom-call | tf_op jit(solution)/shard_map/sort_weights/pallas_call | solution.py:656
  11.7 4.2 %collective-permute-start.4 = (f32[4,32,512]{2,1,0:T(8,128)S(1)}, f32[4,32,512]{2,1,0:T(8,128)S(1)}, u32[]{:S(2)}, u32[]{:S(2)}) collective-permute-start(f32[4,32,512]{2,1,0:T(8,128)S(1)} %get-tuple-element.51), channel_id=1, source_target_pairs={{0,1},{1,0},{2,3},{3,2},{4,5},{5,4},{6,7},{7,6},{8,9},{9,8},{10,11... | collective-permute-start | bytes 786440 | tf_op jit(solution)/shard_map/ppermute | solution.py:649
  17.1 4.2 %collective-permute-done.3.refs_3_ = f32[72,512]{1,0:T(8,128)S(1)} collective-permute-done((f32[72,512]{1,0:T(8,128)S(1)}, f32[72,512]{1,0:T(8,128)S(1)}, u32[]{:S(2)}, u32[]{:S(2)}) %collective-permute-start.3) | collective-permute-done | bytes 147488 | tf_op jit(solution)/shard_map/ppermute | solution.py:675
  21.3 1.2 %collective-permute-start.5 = (f32[72,512]{1,0:T(8,128)S(1)}, f32[72,512]{1,0:T(8,128)S(1)}, u32[]{:S(2)}, u32[]{:S(2)}) collective-permute-start(f32[72,512]{1,0:T(8,128)S(1)} %collective-permute-done.refs_0_), channel_id=1, source_target_pairs={{0,1},{1,0},{2,3},{3,2},{4,5},{5,4},{6,7},{7,6},{8,9},{9,8},{10,11... | collective-permute-start | bytes 442376 | tf_op jit(solution)/shard_map/ppermute | solution.py:649
  23.0 4.3 %collective-permute-start.9 = (f32[64,512]{1,0:T(8,128)S(1)}, f32[64,512]{1,0:T(8,128)S(1)}, u32[]{:S(2)}, u32[]{:S(2)}) collective-permute-start(f32[64,512]{1,0:T(8,128)S(1)} %get-tuple-element.63), channel_id=1, source_target_pairs={{0,6},{1,15},{2,4},{3,13},{4,2},{5,11},{6,0},{7,9},{8,14},{9,7},{1... | collective-permute-start | bytes 393224 | tf_op jit(solution)/shard_map/ppermute | solution.py:646
  27.2 0.9 %collective-permute-start.11 = (f32[64,512]{1,0:T(8,128)S(1)}, f32[64,512]{1,0:T(8,128)S(1)}, u32[]{:S(2)}, u32[]{:S(2)}) collective-permute-start(f32[64,512]{1,0:T(8,128)S(1)} %get-tuple-element.65), channel_id=1, source_target_pairs={{0,2},{1,11},{2,0},{3,9},{4,6},{5,15},{6,4},{7,13},{8,10},{9,3},{1... | collective-permute-start | bytes 393224 | tf_op jit(solution)/shard_map/ppermute | solution.py:646
  28.1 0.7 collective-permute-start.12
  28.8 5.7 %tree_points.1 = (bf16[144,4096]{1,0:T(8,128)(2,1)S(1)}, bf16[4096,256]{1,0:T(8,128)(2,1)}, bf16[4,1024,128]{2,1,0:T(8,128)(2,1)}, bf16[896,256]{1,0:T(8,128)(2,...) custom-call(s32[1,8]{1,0:T(1,128)} %count_ref.1, ...), custom_call_target="tpu_custom_call" | custom-call | tf_op jit(solution)/shard_map/tree_points/pallas_call | solution.py:706
  34.5 3.8 %collective-permute-done.10.refs_1_ = f32[64,512]{1,0:T(8,128)S(1)} collective-permute-done((f32[64,512]{1,0:T(8,128)S(1)}, f32[64,512]{1,0:T(8,128)S(1)}, u32[]{:S(2)}, u32[]{:S(2)}) %collective-permute-start.10) | collective-permute-done | bytes 131104 | tf_op jit(solution)/shard_map/ppermute | solution.py:646
  40.3 2.9 %tree_weights.1 = (bf16[64,4096]{1,0:T(8,128)(2,1)S(1)}, bf16[128,896]{1,0:T(8,128)(2,1)S(1)}, f32[136,128]{1,0:T(8,128)S(1)}) custom-call(bf16[4,1024,128]{2,1,0:T(8,128)(2,1)} %get-tuple-element.60.base_hbm, f32[3,256,128]{2,1,0:T(8,128)S(1)} %get-tuple-element.61.upper_tiles_ref, f32[72,128]{1,0:T(8,128)S(1)} %get-tuple-element.62.top_ref, ...), custom_call_target="tpu_custom_call" | custom-call | tf_op jit(solution)/shard_map/tree_weights/pallas_call | solution.py:738
  43.2 1.1 %collective-permute-start.17 = (f32[136,128]{1,0:T(8,128)S(1)}, f32[136,128]{1,0:T(8,128)S(1)}, u32[]{:S(2)}, u32[]{:S(2)}) collective-permute-start(f32[136,128]{1,0:T(8,128)S(1)} %get-tuple-element.73), channel_id=1, source_target_pairs={{0,8},{8,0},{1,9},{9,1},{2,10},{10,2},{3,11},{11,3},{4,12},{12,4},... | collective-permute-start | bytes 208904 | tf_op jit(solution)/shard_map/ppermute | solution.py:592
  44.3 6.7 %near.1.near_ref = f32[64,2048]{1,0:T(8,128)S(1)} custom-call(s32[3,72]{1,0:T(4,128)} %get-tuple-element.78.tiles, bf16[4096,256]{1,0:T(8,128)(2,1)} %get-tuple-element.79.a_hbm, bf16[144,4096]{1,0:T(8,128)(2,1)S(1)} %get-tuple-element.75.tree_ref, bf16[64,4096]{1,0:T(8,128)(2,1)S(1)} %get-tuple-element.80.w_ref), custom_call_target="tpu_custom_call" | custom-call | tf_op jit(solution)/shard_map/near/pallas_call | solution.py:759
  51.0 2.2 %far.1 = (f32[4,64,512]{2,1,0:T(8,128)S(1)}, f32[4,64,512]{2,1,0:T(8,128)S(1)}) custom-call(f32[1,136,128]{2,1,0:T(8,128)S(1)} %bitcast.4, f32[4,1024]{1,0:T(4,128)S(1)} %get-tuple-element.68.slot_ref, f32[4,8,128]{2,1,0:T(8,128)S(1)} %get-tuple-element.74.info_ref, bf16[144,4096]{1,0:T(8,128)(2,1)S(1)} %get-tuple-element.75.tree_ref, ...), custom_call_target="tpu_custom_call" | custom-call | tf_op jit(solution)/shard_map/far/pallas_call | solution.py:776
  53.3 1.9 %collective-permute-done.18.got_ref = f32[4,64,512]{2,1,0:T(8,128)S(1)} collective-permute-done((f32[4,64,512]{2,1,0:T(8,128)S(1)}, f32[4,64,512]{2,1,0:T(8,128)S(1)}, u32[]{:S(2)}, u32[]{:S(2)}) %collective-permute-start.18) | collective-permute-done | bytes 524320 | tf_op jit(solution)/shard_map/ppermute | solution.py:649
  55.3 3.1 %collective-permute-start.19 = (f32[64,512]{1,0:T(8,128)S(1)}, f32[64,512]{1,0:T(8,128)S(1)}, u32[]{:S(2)}, u32[]{:S(2)}) collective-permute-start(f32[64,512]{1,0:T(8,128)S(1)} %get-tuple-element.83), channel_id=1, source_target_pairs={{0,6},{1,15},{2,4},{3,13},{4,2},{5,11},{6,0},{7,9},{8,14},{9,7},{1... | collective-permute-start | bytes 393224 | tf_op jit(solution)/shard_map/ppermute | solution.py:646
  58.4 1.3 %collective-permute-start.21 = (f32[64,512]{1,0:T(8,128)S(1)}, f32[64,512]{1,0:T(8,128)S(1)}, u32[]{:S(2)}, u32[]{:S(2)}) collective-permute-start(f32[64,512]{1,0:T(8,128)S(1)} %get-tuple-element.85), channel_id=1, source_target_pairs={{0,2},{1,11},{2,0},{3,9},{4,6},{5,15},{6,4},{7,13},{8,10},{9,3},{1... | collective-permute-start | bytes 393224 | tf_op jit(solution)/shard_map/ppermute | solution.py:646
  60.4 3.2 %collective-permute-done.19.refs_0_ = f32[64,512]{1,0:T(8,128)S(1)} collective-permute-done((f32[64,512]{1,0:T(8,128)S(1)}, f32[64,512]{1,0:T(8,128)S(1)}, u32[]{:S(2)}, u32[]{:S(2)}) %collective-permute-start.19) | collective-permute-done | bytes 131104 | tf_op jit(solution)/shard_map/ppermute | solution.py:646
  63.6 6.8 %collective-permute-done.20.refs_1_ = f32[64,512]{1,0:T(8,128)S(1)} collective-permute-done((f32[64,512]{1,0:T(8,128)S(1)}, f32[64,512]{1,0:T(8,128)S(1)}, u32[]{:S(2)}, u32[]{:S(2)}) %collective-permute-start.20) | collective-permute-done | bytes 131104 | tf_op jit(solution)/shard_map/ppermute | solution.py:646
  71.0 0.8 %collective-permute-done.24.refs_5_ = f32[64,512]{1,0:T(8,128)S(1)} collective-permute-done((f32[64,512]{1,0:T(8,128)S(1)}, f32[64,512]{1,0:T(8,128)S(1)}, u32[]{:S(2)}, u32[]{:S(2)}) %collective-permute-start.24) | collective-permute-done | bytes 131104 | tf_op jit(solution)/shard_map/ppermute | solution.py:649
  72.3 1.9 %to_input_order.1 = f32[1024,128]{1,0:T(8,128)} custom-call(f32[8,128]{1,0:T(8,128)S(1)} %copy-done.1, f32[64,512]{1,0:T(8,128)S(1)} %collective-permute-done.19.refs_0_, f32[64,512]{1,0:T(8,128)S(1)} %collective-permute-done.20.refs_1_, f32[64,512]{1,0:T(8,128)S(1)} %collective-permute-done.21.refs_2_, f32[64,512]{1,0:T(8,128)S(1)} %collective-permute-done.22.refs_3_, ...), custom_call_target="tpu_custom_call" | custom-call | tf_op jit(solution)/shard_map/to_input_order/pallas_call | solution.py:813
  (43 shorter events, 5.7 us)
Async XLA Ops:
  2.7 1.6 %collective-permute-start = (f32[72,512]{1,0:T(8,128)}, f32[72,512]{1,0:T(8,128)S(1)}, u32[]{:S(2)}, u32[]{:S(2)}) collective-permute-start(f32[72,512]{1,0:T(8,128)} %get-tuple-element.47), channel_id=1, source_target_pairs={{0,0},{1,9},{2,2},{3,11},{4,4},{5,13},{6,6},{7,15},{8,8},{9,1},{10... | collective-permute-start | bytes 442376 | tf_op jit(solution)/shard_map/ppermute | solution.py:646
  4.3 7.4 %collective-permute-start.1 = (f32[72,512]{1,0:T(8,128)S(1)}, f32[72,512]{1,0:T(8,128)S(1)}, u32[]{:S(2)}, u32[]{:S(2)}) collective-permute-start(f32[72,512]{1,0:T(8,128)S(1)} %collective-permute-done.refs_0_), channel_id=1, source_target_pairs={{0,2},{2,0},{4,6},{6,4},{1,3},{3,1},{5,7},{7,5},{8,10},{10,8},{12,... | collective-permute-start | bytes 442376 | tf_op jit(solution)/shard_map/ppermute | solution.py:675
  7.3 8.6 %collective-permute-start.2 = (f32[72,512]{1,0:T(8,128)S(1)}, f32[72,512]{1,0:T(8,128)S(1)}, u32[]{:S(2)}, u32[]{:S(2)}) collective-permute-start(f32[72,512]{1,0:T(8,128)S(1)} %collective-permute-done.refs_0_), channel_id=1, source_target_pairs={{0,4},{2,6},{4,0},{6,2},{1,5},{3,7},{5,1},{7,3},{8,12},{10,14},{12... | collective-permute-start | bytes 442376 | tf_op jit(solution)/shard_map/ppermute | solution.py:675
  11.7 5.3 %collective-permute-start.4 = (f32[4,32,512]{2,1,0:T(8,128)S(1)}, f32[4,32,512]{2,1,0:T(8,128)S(1)}, u32[]{:S(2)}, u32[]{:S(2)}) collective-permute-start(f32[4,32,512]{2,1,0:T(8,128)S(1)} %get-tuple-element.51), channel_id=1, source_target_pairs={{0,1},{1,0},{2,3},{3,2},{4,5},{5,4},{6,7},{7,6},{8,9},{9,8},{10,11... | collective-permute-start | bytes 786440 | tf_op jit(solution)/shard_map/ppermute | solution.py:649
  15.9 5.4 %collective-permute-start.3 = (f32[72,512]{1,0:T(8,128)S(1)}, f32[72,512]{1,0:T(8,128)S(1)}, u32[]{:S(2)}, u32[]{:S(2)}) collective-permute-start(f32[72,512]{1,0:T(8,128)S(1)} %collective-permute-done.2.refs_2_), channel_id=1, source_target_pairs={{0,2},{2,0},{4,6},{6,4},{1,3},{3,1},{5,7},{7,5},{8,10},{10,8},{12,... | collective-permute-start | bytes 442376 | tf_op jit(solution)/shard_map/ppermute | solution.py:675
  21.3 6.0 %collective-permute-start.5 = (f32[72,512]{1,0:T(8,128)S(1)}, f32[72,512]{1,0:T(8,128)S(1)}, u32[]{:S(2)}, u32[]{:S(2)}) collective-permute-start(f32[72,512]{1,0:T(8,128)S(1)} %collective-permute-done.refs_0_), channel_id=1, source_target_pairs={{0,1},{1,0},{2,3},{3,2},{4,5},{5,4},{6,7},{7,6},{8,9},{9,8},{10,11... | collective-permute-start | bytes 442376 | tf_op jit(solution)/shard_map/ppermute | solution.py:649
  22.4 4.8 %collective-permute-start.6 = (f32[72,512]{1,0:T(8,128)S(1)}, f32[72,512]{1,0:T(8,128)S(1)}, u32[]{:S(2)}, u32[]{:S(2)}) collective-permute-start(f32[72,512]{1,0:T(8,128)S(1)} %collective-permute-done.1.refs_1_), channel_id=1, source_target_pairs={{0,1},{1,0},{2,3},{3,2},{4,5},{5,4},{6,7},{7,6},{8,9},{9,8},{10,11... | collective-permute-start | bytes 442376 | tf_op jit(solution)/shard_map/ppermute | solution.py:649
  22.4 5.7 %collective-permute-start.7 = (f32[72,512]{1,0:T(8,128)S(1)}, f32[72,512]{1,0:T(8,128)S(1)}, u32[]{:S(2)}, u32[]{:S(2)}) collective-permute-start(f32[72,512]{1,0:T(8,128)S(1)} %collective-permute-done.2.refs_2_), channel_id=1, source_target_pairs={{0,1},{1,0},{2,3},{3,2},{4,5},{5,4},{6,7},{7,6},{8,9},{9,8},{10,11... | collective-permute-start | bytes 442376 | tf_op jit(solution)/shard_map/ppermute | solution.py:649
  23.0 5.9 %collective-permute-start.8 = (f32[72,512]{1,0:T(8,128)S(1)}, f32[72,512]{1,0:T(8,128)S(1)}, u32[]{:S(2)}, u32[]{:S(2)}) collective-permute-start(f32[72,512]{1,0:T(8,128)S(1)} %collective-permute-done.3.refs_3_), channel_id=1, source_target_pairs={{0,1},{1,0},{2,3},{3,2},{4,5},{5,4},{6,7},{7,6},{8,9},{9,8},{10,11... | collective-permute-start | bytes 442376 | tf_op jit(solution)/shard_map/ppermute | solution.py:649
  23.0 11.6 %collective-permute-start.9 = (f32[64,512]{1,0:T(8,128)S(1)}, f32[64,512]{1,0:T(8,128)S(1)}, u32[]{:S(2)}, u32[]{:S(2)}) collective-permute-start(f32[64,512]{1,0:T(8,128)S(1)} %get-tuple-element.63), channel_id=1, source_target_pairs={{0,6},{1,15},{2,4},{3,13},{4,2},{5,11},{6,0},{7,9},{8,14},{9,7},{1... | collective-permute-start | bytes 393224 | tf_op jit(solution)/shard_map/ppermute | solution.py:646
  27.2 11.0 %collective-permute-start.10 = (f32[64,512]{1,0:T(8,128)S(1)}, f32[64,512]{1,0:T(8,128)S(1)}, u32[]{:S(2)}, u32[]{:S(2)}) collective-permute-start(f32[64,512]{1,0:T(8,128)S(1)} %get-tuple-element.64), channel_id=1, source_target_pairs={{0,4},{1,13},{2,6},{3,15},{4,0},{5,9},{6,2},{7,11},{8,12},{9,5},{1... | collective-permute-start | bytes 393224 | tf_op jit(solution)/shard_map/ppermute | solution.py:646
  27.2 11.0 %collective-permute-start.11 = (f32[64,512]{1,0:T(8,128)S(1)}, f32[64,512]{1,0:T(8,128)S(1)}, u32[]{:S(2)}, u32[]{:S(2)}) collective-permute-start(f32[64,512]{1,0:T(8,128)S(1)} %get-tuple-element.65), channel_id=1, source_target_pairs={{0,2},{1,11},{2,0},{3,9},{4,6},{5,15},{6,4},{7,13},{8,10},{9,3},{1... | collective-permute-start | bytes 393224 | tf_op jit(solution)/shard_map/ppermute | solution.py:646
  28.1 10.1 %collective-permute-start.12 = (f32[64,512]{1,0:T(8,128)S(1)}, f32[64,512]{1,0:T(8,128)S(1)}, u32[]{:S(2)}, u32[]{:S(2)}) collective-permute-start(f32[64,512]{1,0:T(8,128)S(1)} %get-tuple-element.66), channel_id=1, source_target_pairs={{0,0},{1,9},{2,2},{3,11},{4,4},{5,13},{6,6},{7,15},{8,8},{9,1},{10... | collective-permute-start | bytes 393224 | tf_op jit(solution)/shard_map/ppermute | solution.py:646
  38.3 1.4 %collective-permute-start.13 = (f32[64,512]{1,0:T(8,128)S(1)}, f32[64,512]{1,0:T(8,128)S(1)}, u32[]{:S(2)}, u32[]{:S(2)}) collective-permute-start(f32[64,512]{1,0:T(8,128)S(1)} %collective-permute-done.9.refs_0_), channel_id=1, source_target_pairs={{0,1},{1,0},{2,3},{3,2},{4,5},{5,4},{6,7},{7,6},{8,9},{9,8},{10,11... | collective-permute-start | bytes 393224 | tf_op jit(solution)/shard_map/ppermute | solution.py:649
  38.3 1.5 %collective-permute-start.14 = (f32[64,512]{1,0:T(8,128)S(1)}, f32[64,512]{1,0:T(8,128)S(1)}, u32[]{:S(2)}, u32[]{:S(2)}) collective-permute-start(f32[64,512]{1,0:T(8,128)S(1)} %collective-permute-done.10.refs_1_), channel_id=1, source_target_pairs={{0,1},{1,0},{2,3},{3,2},{4,5},{5,4},{6,7},{7,6},{8,9},{9,8},{10,11... | collective-permute-start | bytes 393224 | tf_op jit(solution)/shard_map/ppermute | solution.py:649
  38.9 1.5 %collective-permute-start.16 = (f32[64,512]{1,0:T(8,128)S(1)}, f32[64,512]{1,0:T(8,128)S(1)}, u32[]{:S(2)}, u32[]{:S(2)}) collective-permute-start(f32[64,512]{1,0:T(8,128)S(1)} %collective-permute-done.12.refs_3_), channel_id=1, source_target_pairs={{0,1},{1,0},{2,3},{3,2},{4,5},{5,4},{6,7},{7,6},{8,9},{9,8},{10,11... | collective-permute-start | bytes 393224 | tf_op jit(solution)/shard_map/ppermute | solution.py:649
  43.2 7.8 %collective-permute-start.17 = (f32[136,128]{1,0:T(8,128)S(1)}, f32[136,128]{1,0:T(8,128)S(1)}, u32[]{:S(2)}, u32[]{:S(2)}) collective-permute-start(f32[136,128]{1,0:T(8,128)S(1)} %get-tuple-element.73), channel_id=1, source_target_pairs={{0,8},{8,0},{1,9},{9,1},{2,10},{10,2},{3,11},{11,3},{4,12},{12,4},... | collective-permute-start | bytes 208904 | tf_op jit(solution)/shard_map/ppermute | solution.py:592
  53.2 2.0 %collective-permute-start.18 = (f32[4,64,512]{2,1,0:T(8,128)S(1)}, f32[4,64,512]{2,1,0:T(8,128)S(1)}, u32[]{:S(2)}, u32[]{:S(2)}) collective-permute-start(f32[4,64,512]{2,1,0:T(8,128)S(1)} %get-tuple-element.82), channel_id=1, source_target_pairs={{0,1},{1,0},{2,3},{3,2},{4,5},{5,4},{6,7},{7,6},{8,9},{9,8},{10,11... | collective-permute-start | bytes 1572872 | tf_op jit(solution)/shard_map/ppermute | solution.py:649
  55.3 8.4 %collective-permute-start.19 = (f32[64,512]{1,0:T(8,128)S(1)}, f32[64,512]{1,0:T(8,128)S(1)}, u32[]{:S(2)}, u32[]{:S(2)}) collective-permute-start(f32[64,512]{1,0:T(8,128)S(1)} %get-tuple-element.83), channel_id=1, source_target_pairs={{0,6},{1,15},{2,4},{3,13},{4,2},{5,11},{6,0},{7,9},{8,14},{9,7},{1... | collective-permute-start | bytes 393224 | tf_op jit(solution)/shard_map/ppermute | solution.py:646
  58.4 12.0 %collective-permute-start.20 = (f32[64,512]{1,0:T(8,128)S(1)}, f32[64,512]{1,0:T(8,128)S(1)}, u32[]{:S(2)}, u32[]{:S(2)}) collective-permute-start(f32[64,512]{1,0:T(8,128)S(1)} %get-tuple-element.84), channel_id=1, source_target_pairs={{0,4},{1,13},{2,6},{3,15},{4,0},{5,9},{6,2},{7,11},{8,12},{9,5},{1... | collective-permute-start | bytes 393224 | tf_op jit(solution)/shard_map/ppermute | solution.py:646
  58.4 12.0 %collective-permute-start.21 = (f32[64,512]{1,0:T(8,128)S(1)}, f32[64,512]{1,0:T(8,128)S(1)}, u32[]{:S(2)}, u32[]{:S(2)}) collective-permute-start(f32[64,512]{1,0:T(8,128)S(1)} %get-tuple-element.85), channel_id=1, source_target_pairs={{0,2},{1,11},{2,0},{3,9},{4,6},{5,15},{6,4},{7,13},{8,10},{9,3},{1... | collective-permute-start | bytes 393224 | tf_op jit(solution)/shard_map/ppermute | solution.py:646
  59.7 11.2 %collective-permute-start.22 = (f32[64,512]{1,0:T(8,128)S(1)}, f32[64,512]{1,0:T(8,128)S(1)}, u32[]{:S(2)}, u32[]{:S(2)}) collective-permute-start(f32[64,512]{1,0:T(8,128)S(1)} %get-tuple-element.86), channel_id=1, source_target_pairs={{0,0},{1,9},{2,2},{3,11},{4,4},{5,13},{6,6},{7,15},{8,8},{9,1},{10... | collective-permute-start | bytes 393224 | tf_op jit(solution)/shard_map/ppermute | solution.py:646
  63.6 7.4 %collective-permute-start.23 = (f32[64,512]{1,0:T(8,128)S(1)}, f32[64,512]{1,0:T(8,128)S(1)}, u32[]{:S(2)}, u32[]{:S(2)}) collective-permute-start(f32[64,512]{1,0:T(8,128)S(1)} %collective-permute-done.19.refs_0_), channel_id=1, source_target_pairs={{0,1},{1,0},{2,3},{3,2},{4,5},{5,4},{6,7},{7,6},{8,9},{9,8},{10,11... | collective-permute-start | bytes 393224 | tf_op jit(solution)/shard_map/ppermute | solution.py:649
  70.4 1.5 %collective-permute-start.25 = (f32[64,512]{1,0:T(8,128)S(1)}, f32[64,512]{1,0:T(8,128)S(1)}, u32[]{:S(2)}, u32[]{:S(2)}) collective-permute-start(f32[64,512]{1,0:T(8,128)S(1)} %collective-permute-done.21.refs_2_), channel_id=1, source_target_pairs={{0,1},{1,0},{2,3},{3,2},{4,5},{5,4},{6,7},{7,6},{8,9},{9,8},{10,11... | collective-permute-start | bytes 393224 | tf_op jit(solution)/shard_map/ppermute | solution.py:649
  (5 other events, 46.5 us)

commit v22 on v20

--- a/solution.py
+++ b/solution.py
@@ -256,24 +256,29 @@
 def list_tiles(count_ref, list_ref, tiles, times):
     every = count_ref.shape[1]
 
-    def tally(leaf, filled):
+    def tally(leaf, carry):
         for other in range(every):
-            times[other] = (leaf == other).astype(jnp.int32)
+            times[leaf * every + other] = (leaf == other).astype(jnp.int32)
 
         def add(slot, carry):
-            at = list_ref[leaf, slot]
+            at = leaf * every + list_ref[leaf, slot]
             times[at] = times[at] + 1
             return carry
 
-        lax.fori_loop(0, count_ref[0, leaf], add, 0)
-        for other in range(every):
+        return lax.fori_loop(0, count_ref[0, leaf], add, carry)
+
+    lax.fori_loop(0, every, tally, 0)
+
+    def write(other, filled):
+        for leaf in range(every):
+            many = times[leaf * every + other]
             tiles[0, filled] = leaf
             tiles[1, filled] = other
-            tiles[2, filled] = times[other]
-            filled = filled + (times[other] > 0).astype(jnp.int32)
+            tiles[2, filled] = many
+            filled = filled + (many > 0).astype(jnp.int32)
         return filled
 
-    filled = lax.fori_loop(0, every, tally, jnp.int32(0))
+    filled = lax.fori_loop(0, every, write, jnp.int32(0))
 
     def pad(more, carry):
         tiles[0, more] = 0
@@ -412,10 +417,14 @@
         start, count = start + count, count // 2
 
 
-def near_kernel(layout, tiles, a_hbm, tree_ref, w_ref, acc, a_ref, bt_ref, sem, even, odd, even_tile, odd_tile):
+def near_kernel(layout, tiles, a_hbm, tree_ref, w_ref, acc, a_ref, bt_ref, sems, even, odd, even_tile, odd_tile):
     span = layout.span
-    copy = pltpu.make_async_copy(a_hbm, a_ref, sem)
-    copy.start()
+    size = a_ref.shape[0] // 2
+    copies = []
+    for half in range(2):
+        rows = slice(half * size, (half + 1) * size)
+        copies.append(pltpu.make_async_copy(a_hbm.at[rows], a_ref.at[rows], sems.at[half]))
+        copies[-1].start()
     filled = tiles[0, tiles.shape[1] - 1]
     acc[...] = jnp.zeros_like(acc)
     target_columns(layout, bt_ref, tree_ref)
@@ -429,11 +438,12 @@
         target = aligned(tiles[0, tile] * span, span, span)
         acc[:, target] += tiles[2, tile].astype(f32) * nn(w_ref[:, source], block)
 
-    copy.wait()
+    copies[0].wait()
     exponents(0, even)
     for k in range(2):
         even_tile[k] = jnp.exp(even[k]).astype(bf16)
     exponents(1, odd)
+    copies[1].wait()
 
     def phase(unit, upcoming, ready, finished, previous):
         for k in range(2):
@@ -725,7 +735,7 @@
             vm((COORD, nodes * SK), bf16),
             vm((FEAT, nodes * SK), bf16),
             pltpu.SemaphoreType.DMA((2, blocks)),
-            pltpu.SMEM((leaves,), jnp.int32),
+            pltpu.SMEM((leaves * leaves,), jnp.int32),
         ],
         compiler_params=params(40),
         name="tree_points",
@@ -763,7 +773,7 @@
         scratch_shapes=[
             vm((total, FEAT), bf16),
             vm((FEAT, total // layout.halves), bf16),
-            pltpu.SemaphoreType.DMA(()),
+            pltpu.SemaphoreType.DMA((2,)),
         ]
         + [vm((2, LEAF, layout.span), f32)] * 2
         + [vm((2, LEAF, layout.span), bf16)] * 2,

time: 72.8 us -> 72.5 us (level)
  transfers between devices with their start and end apart: 27 -> 27, of which waited for: 14 -> 14; matrix products, arithmetic and copies ran while one was open for 0% -> 0% of each run, Pallas kernels for 20% -> 19%
where the time goes in v22:
time: 72.5 us; the launch traced here: 72 us
  starting transfers between devices  24.5 us (34%)
  Pallas kernels  23.8 us (33%)
  waiting for transfers between devices  23.6 us (33%)
    ppermute x9, waiting for transfers between devices, swap(): return lax.ppermute(value, axes, pairs)  13 us
    ppermute x9, starting transfers between devices, swap(): return lax.ppermute(value, axes, pairs)  11.8 us
    ppermute x3, starting transfers between devices, body(): lax.ppermute(place[step], 'sub', [(i, i ^ stride) for i in range(blocks)])  6.51 us
    pallas_call x1, Pallas kernels, body(): pl.pallas_call(functools.partial(near_kernel, layout), out_shape=vm((cols...  6.35 us
    ppermute x3, waiting for transfers between devices, body(): lax.ppermute(place[step], 'sub', [(i, i ^ stride) for i in range(blocks)])  6.25 us
    pallas_call x1, Pallas kernels, body(): pl.pallas_call(functools.partial(points_kernel, layout, trees), out_shape...  5.81 us
    ppermute x14, starting transfers between devices, other_core(): return lax.ppermute(value, 'rep', [(0, 1), (1, 0)])  4.81 us
    ppermute x14, waiting for transfers between devices, other_core(): return lax.ppermute(value, 'rep', [(0, 1), (1, 0)])  4.41 us
  transfers between devices with their start and end apart: 27, of which 14 were waited for; matrix products, arithmetic and copies ran while one was open for 0% of the time, Pallas kernels for 19%

profile of v22, /device:TPU:0, one launch (start us, length us, event | category | flops | bytes accessed | tf_op | source)
XLA Modules:
  0.0 72.0 jit_solution(17978480940689118353)
XLA Ops:
  0.0 2.7 %sort_points.1 = (f32[72,512]{1,0:T(8,128)}, f32[8,128]{1,0:T(8,128)}) custom-call(s32[8,128]{1,0:T(8,128)} %bitcast.6, f32[64,1024]{1,0:T(8,128)} %bitcast.5, s32[1,128]{1,0:T(1,128)} %base_ref.1, s32[2,3]{1,0:T(2,128)} %flag_ref.1), custom_call_target="tpu_custom_call" | custom-call | tf_op jit(solution)/shard_map/sort_points/pallas_call | solution.py:638
  2.7 1.6 %collective-permute-start = (f32[72,512]{1,0:T(8,128)}, f32[72,512]{1,0:T(8,128)S(1)}, u32[]{:S(2)}, u32[]{:S(2)}) collective-permute-start(f32[72,512]{1,0:T(8,128)} %get-tuple-element.43), channel_id=1, source_target_pairs={{0,0},{1,9},{2,2},{3,11},{4,4},{5,13},{6,6},{7,15},{8,8},{9,1},{10... | collective-permute-start | bytes 442376 | tf_op jit(solution)/shard_map/ppermute | solution.py:656
  4.3 4.0 %collective-permute-start.2 = (f32[72,512]{1,0:T(8,128)S(1)}, f32[72,512]{1,0:T(8,128)S(1)}, u32[]{:S(2)}, u32[]{:S(2)}) collective-permute-start(f32[72,512]{1,0:T(8,128)S(1)} %collective-permute-done.refs_0_), channel_id=1, source_target_pairs={{0,4},{2,6},{4,0},{6,2},{1,5},{3,7},{5,1},{7,3},{8,12},{10,14},{12... | collective-permute-start | bytes 442376 | tf_op jit(solution)/shard_map/ppermute | solution.py:685
  8.3 1.6 %collective-permute-start.1 = (f32[72,512]{1,0:T(8,128)S(1)}, f32[72,512]{1,0:T(8,128)S(1)}, u32[]{:S(2)}, u32[]{:S(2)}) collective-permute-start(f32[72,512]{1,0:T(8,128)S(1)} %collective-permute-done.refs_0_), channel_id=1, source_target_pairs={{0,2},{2,0},{4,6},{6,4},{1,3},{3,1},{5,7},{7,5},{8,10},{10,8},{12,... | collective-permute-start | bytes 442376 | tf_op jit(solution)/shard_map/ppermute | solution.py:685
  9.9 3.2 %collective-permute-done.2.refs_2_ = f32[72,512]{1,0:T(8,128)S(1)} collective-permute-done((f32[72,512]{1,0:T(8,128)S(1)}, f32[72,512]{1,0:T(8,128)S(1)}, u32[]{:S(2)}, u32[]{:S(2)}) %collective-permute-start.2) | collective-permute-done | bytes 147488 | tf_op jit(solution)/shard_map/ppermute | solution.py:685
  13.2 0.9 %collective-permute-start.3 = (f32[72,512]{1,0:T(8,128)S(1)}, f32[72,512]{1,0:T(8,128)S(1)}, u32[]{:S(2)}, u32[]{:S(2)}) collective-permute-start(f32[72,512]{1,0:T(8,128)S(1)} %collective-permute-done.2.refs_2_), channel_id=1, source_target_pairs={{0,2},{2,0},{4,6},{6,4},{1,3},{3,1},{5,7},{7,5},{8,10},{10,8},{12,... | collective-permute-start | bytes 442376 | tf_op jit(solution)/shard_map/ppermute | solution.py:685
  14.1 1.8 %sort_weights.1 = (f32[4,32,512]{2,1,0:T(8,128)S(1)}, f32[4,32,512]{2,1,0:T(8,128)S(1)}) custom-call(f32[8,128]{1,0:T(8,128)} %get-tuple-element.42.pos_ref, f32[1024,128]{1,0:T(8,128)} %refs_8_.1), custom_call_target="tpu_custom_call" | custom-call | tf_op jit(solution)/shard_map/sort_weights/pallas_call | solution.py:666
  15.9 3.0 %collective-permute-done.3.refs_3_ = f32[72,512]{1,0:T(8,128)S(1)} collective-permute-done((f32[72,512]{1,0:T(8,128)S(1)}, f32[72,512]{1,0:T(8,128)S(1)}, u32[]{:S(2)}, u32[]{:S(2)}) %collective-permute-start.3) | collective-permute-done | bytes 147488 | tf_op jit(solution)/shard_map/ppermute | solution.py:685
  18.9 2.0 %collective-permute-start.8 = (f32[4,32,512]{2,1,0:T(8,128)S(1)}, f32[4,32,512]{2,1,0:T(8,128)S(1)}, u32[]{:S(2)}, u32[]{:S(2)}) collective-permute-start(f32[4,32,512]{2,1,0:T(8,128)S(1)} %get-tuple-element.54), channel_id=1, source_target_pairs={{0,1},{1,0},{2,3},{3,2},{4,5},{5,4},{6,7},{7,6},{8,9},{9,8},{10,11... | collective-permute-start | bytes 786440 | tf_op jit(solution)/shard_map/ppermute | solution.py:659
  22.1 3.5 %collective-permute-start.9 = (f32[64,512]{1,0:T(8,128)S(1)}, f32[64,512]{1,0:T(8,128)S(1)}, u32[]{:S(2)}, u32[]{:S(2)}) collective-permute-start(f32[64,512]{1,0:T(8,128)S(1)} %get-tuple-element.55), channel_id=1, source_target_pairs={{0,6},{1,15},{2,4},{3,13},{4,2},{5,11},{6,0},{7,9},{8,14},{9,7},{1... | collective-permute-start | bytes 393224 | tf_op jit(solution)/shard_map/ppermute | solution.py:656
  25.6 0.9 %collective-permute-start.11 = (f32[64,512]{1,0:T(8,128)S(1)}, f32[64,512]{1,0:T(8,128)S(1)}, u32[]{:S(2)}, u32[]{:S(2)}) collective-permute-start(f32[64,512]{1,0:T(8,128)S(1)} %get-tuple-element.57), channel_id=1, source_target_pairs={{0,2},{1,11},{2,0},{3,9},{4,6},{5,15},{6,4},{7,13},{8,10},{9,3},{1... | collective-permute-start | bytes 393224 | tf_op jit(solution)/shard_map/ppermute | solution.py:656
  27.3 5.8 %tree_points.1 = (bf16[144,4096]{1,0:T(8,128)(2,1)S(1)}, bf16[4096,256]{1,0:T(8,128)(2,1)}, bf16[4,1024,128]{2,1,0:T(8,128)(2,1)}, bf16[896,256]{1,0:T(8,128)(2,...) custom-call(s32[1,8]{1,0:T(1,128)} %count_ref.1, ...), custom_call_target="tpu_custom_call" | custom-call | tf_op jit(solution)/shard_map/tree_points/pallas_call | solution.py:715
  33.1 3.9 %collective-permute-done.10.refs_1_ = f32[64,512]{1,0:T(8,128)S(1)} collective-permute-done((f32[64,512]{1,0:T(8,128)S(1)}, f32[64,512]{1,0:T(8,128)S(1)}, u32[]{:S(2)}, u32[]{:S(2)}) %collective-permute-start.10) | collective-permute-done | bytes 131104 | tf_op jit(solution)/shard_map/ppermute | solution.py:656
  39.2 2.9 %tree_weights.1 = (bf16[64,4096]{1,0:T(8,128)(2,1)S(1)}, bf16[128,896]{1,0:T(8,128)(2,1)S(1)}, f32[136,128]{1,0:T(8,128)S(1)}) custom-call(bf16[4,1024,128]{2,1,0:T(8,128)(2,1)} %get-tuple-element.50.base_hbm, f32[3,256,128]{2,1,0:T(8,128)S(1)} %get-tuple-element.51.upper_tiles_ref, f32[72,128]{1,0:T(8,128)S(1)} %get-tuple-element.52.top_ref, ...), custom_call_target="tpu_custom_call" | custom-call | tf_op jit(solution)/shard_map/tree_weights/pallas_call | solution.py:747
  42.1 1.4 %collective-permute-start.17 = (f32[136,128]{1,0:T(8,128)S(1)}, f32[136,128]{1,0:T(8,128)S(1)}, u32[]{:S(2)}, u32[]{:S(2)}) collective-permute-start(f32[136,128]{1,0:T(8,128)S(1)} %get-tuple-element.65), channel_id=1, source_target_pairs={{0,8},{8,0},{1,9},{9,1},{2,10},{10,2},{3,11},{11,3},{4,12},{12,4},... | collective-permute-start | bytes 208904 | tf_op jit(solution)/shard_map/ppermute | solution.py:602
  43.5 6.3 %near.1.near_ref = f32[64,2048]{1,0:T(8,128)S(1)} custom-call(s32[3,72]{1,0:T(4,128)} %get-tuple-element.70.tiles, bf16[4096,256]{1,0:T(8,128)(2,1)} %get-tuple-element.71.a_hbm, bf16[144,4096]{1,0:T(8,128)(2,1)S(1)} %get-tuple-element.67.tree_ref, bf16[64,4096]{1,0:T(8,128)(2,1)S(1)} %get-tuple-element.72.w_ref), custom_call_target="tpu_custom_call" | custom-call | tf_op jit(solution)/shard_map/near/pallas_call | solution.py:768
  49.8 2.2 %far.1 = (f32[4,64,512]{2,1,0:T(8,128)S(1)}, f32[4,64,512]{2,1,0:T(8,128)S(1)}) custom-call(f32[1,136,128]{2,1,0:T(8,128)S(1)} %bitcast.4, f32[4,1024]{1,0:T(4,128)S(1)} %get-tuple-element.60.slot_ref, f32[4,8,128]{2,1,0:T(8,128)S(1)} %get-tuple-element.66.info_ref, bf16[144,4096]{1,0:T(8,128)(2,1)S(1)} %get-tuple-element.67.tree_ref, ...), custom_call_target="tpu_custom_call" | custom-call | tf_op jit(solution)/shard_map/far/pallas_call | solution.py:785
  52.1 1.9 %collective-permute-done.18.got_ref = f32[4,64,512]{2,1,0:T(8,128)S(1)} collective-permute-done((f32[4,64,512]{2,1,0:T(8,128)S(1)}, f32[4,64,512]{2,1,0:T(8,128)S(1)}, u32[]{:S(2)}, u32[]{:S(2)}) %collective-permute-start.18) | collective-permute-done | bytes 524320 | tf_op jit(solution)/shard_map/ppermute | solution.py:659
  54.1 2.9 %collective-permute-start.19 = (f32[64,512]{1,0:T(8,128)S(1)}, f32[64,512]{1,0:T(8,128)S(1)}, u32[]{:S(2)}, u32[]{:S(2)}) collective-permute-start(f32[64,512]{1,0:T(8,128)S(1)} %get-tuple-element.75), channel_id=1, source_target_pairs={{0,6},{1,15},{2,4},{3,13},{4,2},{5,11},{6,0},{7,9},{8,14},{9,7},{1... | collective-permute-start | bytes 393224 | tf_op jit(solution)/shard_map/ppermute | solution.py:656
  56.9 1.6 %collective-permute-start.21 = (f32[64,512]{1,0:T(8,128)S(1)}, f32[64,512]{1,0:T(8,128)S(1)}, u32[]{:S(2)}, u32[]{:S(2)}) collective-permute-start(f32[64,512]{1,0:T(8,128)S(1)} %get-tuple-element.77), channel_id=1, source_target_pairs={{0,2},{1,11},{2,0},{3,9},{4,6},{5,15},{6,4},{7,13},{8,10},{9,3},{1... | collective-permute-start | bytes 393224 | tf_op jit(solution)/shard_map/ppermute | solution.py:656
  59.2 3.1 %collective-permute-done.19.refs_0_ = f32[64,512]{1,0:T(8,128)S(1)} collective-permute-done((f32[64,512]{1,0:T(8,128)S(1)}, f32[64,512]{1,0:T(8,128)S(1)}, u32[]{:S(2)}, u32[]{:S(2)}) %collective-permute-start.19) | collective-permute-done | bytes 131104 | tf_op jit(solution)/shard_map/ppermute | solution.py:656
  62.3 5.9 %collective-permute-done.20.refs_1_ = f32[64,512]{1,0:T(8,128)S(1)} collective-permute-done((f32[64,512]{1,0:T(8,128)S(1)}, f32[64,512]{1,0:T(8,128)S(1)}, u32[]{:S(2)}, u32[]{:S(2)}) %collective-permute-start.20) | collective-permute-done | bytes 131104 | tf_op jit(solution)/shard_map/ppermute | solution.py:656
  68.9 0.7 collective-permute-done.24.refs_5_
  70.1 1.9 %to_input_order.1 = f32[1024,128]{1,0:T(8,128)} custom-call(f32[8,128]{1,0:T(8,128)S(1)} %copy-done.1, f32[64,512]{1,0:T(8,128)S(1)} %collective-permute-done.19.refs_0_, f32[64,512]{1,0:T(8,128)S(1)} %collective-permute-done.20.refs_1_, f32[64,512]{1,0:T(8,128)S(1)} %collective-permute-done.21.refs_2_, f32[64,512]{1,0:T(8,128)S(1)} %collective-permute-done.22.refs_3_, ...), custom_call_target="tpu_custom_call" | custom-call | tf_op jit(solution)/shard_map/to_input_order/pallas_call | solution.py:822
  (43 shorter events, 6.0 us)
Async XLA Ops:
  2.7 1.6 %collective-permute-start = (f32[72,512]{1,0:T(8,128)}, f32[72,512]{1,0:T(8,128)S(1)}, u32[]{:S(2)}, u32[]{:S(2)}) collective-permute-start(f32[72,512]{1,0:T(8,128)} %get-tuple-element.43), channel_id=1, source_target_pairs={{0,0},{1,9},{2,2},{3,11},{4,4},{5,13},{6,6},{7,15},{8,8},{9,1},{10... | collective-permute-start | bytes 442376 | tf_op jit(solution)/shard_map/ppermute | solution.py:656
  4.3 8.8 %collective-permute-start.2 = (f32[72,512]{1,0:T(8,128)S(1)}, f32[72,512]{1,0:T(8,128)S(1)}, u32[]{:S(2)}, u32[]{:S(2)}) collective-permute-start(f32[72,512]{1,0:T(8,128)S(1)} %collective-permute-done.refs_0_), channel_id=1, source_target_pairs={{0,4},{2,6},{4,0},{6,2},{1,5},{3,7},{5,1},{7,3},{8,12},{10,14},{12... | collective-permute-start | bytes 442376 | tf_op jit(solution)/shard_map/ppermute | solution.py:685
  8.3 7.5 %collective-permute-start.1 = (f32[72,512]{1,0:T(8,128)S(1)}, f32[72,512]{1,0:T(8,128)S(1)}, u32[]{:S(2)}, u32[]{:S(2)}) collective-permute-start(f32[72,512]{1,0:T(8,128)S(1)} %collective-permute-done.refs_0_), channel_id=1, source_target_pairs={{0,2},{2,0},{4,6},{6,4},{1,3},{3,1},{5,7},{7,5},{8,10},{10,8},{12,... | collective-permute-start | bytes 442376 | tf_op jit(solution)/shard_map/ppermute | solution.py:685
  13.2 5.7 %collective-permute-start.3 = (f32[72,512]{1,0:T(8,128)S(1)}, f32[72,512]{1,0:T(8,128)S(1)}, u32[]{:S(2)}, u32[]{:S(2)}) collective-permute-start(f32[72,512]{1,0:T(8,128)S(1)} %collective-permute-done.2.refs_2_), channel_id=1, source_target_pairs={{0,2},{2,0},{4,6},{6,4},{1,3},{3,1},{5,7},{7,5},{8,10},{10,8},{12,... | collective-permute-start | bytes 442376 | tf_op jit(solution)/shard_map/ppermute | solution.py:685
  18.9 3.2 %collective-permute-start.8 = (f32[4,32,512]{2,1,0:T(8,128)S(1)}, f32[4,32,512]{2,1,0:T(8,128)S(1)}, u32[]{:S(2)}, u32[]{:S(2)}) collective-permute-start(f32[4,32,512]{2,1,0:T(8,128)S(1)} %get-tuple-element.54), channel_id=1, source_target_pairs={{0,1},{1,0},{2,3},{3,2},{4,5},{5,4},{6,7},{7,6},{8,9},{9,8},{10,11... | collective-permute-start | bytes 786440 | tf_op jit(solution)/shard_map/ppermute | solution.py:659
  20.9 4.7 %collective-permute-start.4 = (f32[72,512]{1,0:T(8,128)S(1)}, f32[72,512]{1,0:T(8,128)S(1)}, u32[]{:S(2)}, u32[]{:S(2)}) collective-permute-start(f32[72,512]{1,0:T(8,128)S(1)} %collective-permute-done.refs_0_), channel_id=1, source_target_pairs={{0,1},{1,0},{2,3},{3,2},{4,5},{5,4},{6,7},{7,6},{8,9},{9,8},{10,11... | collective-permute-start | bytes 442376 | tf_op jit(solution)/shard_map/ppermute | solution.py:659
  20.9 4.7 %collective-permute-start.5 = (f32[72,512]{1,0:T(8,128)S(1)}, f32[72,512]{1,0:T(8,128)S(1)}, u32[]{:S(2)}, u32[]{:S(2)}) collective-permute-start(f32[72,512]{1,0:T(8,128)S(1)} %collective-permute-done.1.refs_1_), channel_id=1, source_target_pairs={{0,1},{1,0},{2,3},{3,2},{4,5},{5,4},{6,7},{7,6},{8,9},{9,8},{10,11... | collective-permute-start | bytes 442376 | tf_op jit(solution)/shard_map/ppermute | solution.py:659
  21.4 5.2 %collective-permute-start.6 = (f32[72,512]{1,0:T(8,128)S(1)}, f32[72,512]{1,0:T(8,128)S(1)}, u32[]{:S(2)}, u32[]{:S(2)}) collective-permute-start(f32[72,512]{1,0:T(8,128)S(1)} %collective-permute-done.2.refs_2_), channel_id=1, source_target_pairs={{0,1},{1,0},{2,3},{3,2},{4,5},{5,4},{6,7},{7,6},{8,9},{9,8},{10,11... | collective-permute-start | bytes 442376 | tf_op jit(solution)/shard_map/ppermute | solution.py:659
  21.4 5.8 %collective-permute-start.7 = (f32[72,512]{1,0:T(8,128)S(1)}, f32[72,512]{1,0:T(8,128)S(1)}, u32[]{:S(2)}, u32[]{:S(2)}) collective-permute-start(f32[72,512]{1,0:T(8,128)S(1)} %collective-permute-done.3.refs_3_), channel_id=1, source_target_pairs={{0,1},{1,0},{2,3},{3,2},{4,5},{5,4},{6,7},{7,6},{8,9},{9,8},{10,11... | collective-permute-start | bytes 442376 | tf_op jit(solution)/shard_map/ppermute | solution.py:659
  22.1 11.0 %collective-permute-start.9 = (f32[64,512]{1,0:T(8,128)S(1)}, f32[64,512]{1,0:T(8,128)S(1)}, u32[]{:S(2)}, u32[]{:S(2)}) collective-permute-start(f32[64,512]{1,0:T(8,128)S(1)} %get-tuple-element.55), channel_id=1, source_target_pairs={{0,6},{1,15},{2,4},{3,13},{4,2},{5,11},{6,0},{7,9},{8,14},{9,7},{1... | collective-permute-start | bytes 393224 | tf_op jit(solution)/shard_map/ppermute | solution.py:656
  25.6 11.4 %collective-permute-start.10 = (f32[64,512]{1,0:T(8,128)S(1)}, f32[64,512]{1,0:T(8,128)S(1)}, u32[]{:S(2)}, u32[]{:S(2)}) collective-permute-start(f32[64,512]{1,0:T(8,128)S(1)} %get-tuple-element.56), channel_id=1, source_target_pairs={{0,4},{1,13},{2,6},{3,15},{4,0},{5,9},{6,2},{7,11},{8,12},{9,5},{1... | collective-permute-start | bytes 393224 | tf_op jit(solution)/shard_map/ppermute | solution.py:656
  25.6 11.4 %collective-permute-start.11 = (f32[64,512]{1,0:T(8,128)S(1)}, f32[64,512]{1,0:T(8,128)S(1)}, u32[]{:S(2)}, u32[]{:S(2)}) collective-permute-start(f32[64,512]{1,0:T(8,128)S(1)} %get-tuple-element.57), channel_id=1, source_target_pairs={{0,2},{1,11},{2,0},{3,9},{4,6},{5,15},{6,4},{7,13},{8,10},{9,3},{1... | collective-permute-start | bytes 393224 | tf_op jit(solution)/shard_map/ppermute | solution.py:656
  26.6 10.4 %collective-permute-start.12 = (f32[64,512]{1,0:T(8,128)S(1)}, f32[64,512]{1,0:T(8,128)S(1)}, u32[]{:S(2)}, u32[]{:S(2)}) collective-permute-start(f32[64,512]{1,0:T(8,128)S(1)} %get-tuple-element.58), channel_id=1, source_target_pairs={{0,0},{1,9},{2,2},{3,11},{4,4},{5,13},{6,6},{7,15},{8,8},{9,1},{10... | collective-permute-start | bytes 393224 | tf_op jit(solution)/shard_map/ppermute | solution.py:656
  37.0 1.4 %collective-permute-start.13 = (f32[64,512]{1,0:T(8,128)S(1)}, f32[64,512]{1,0:T(8,128)S(1)}, u32[]{:S(2)}, u32[]{:S(2)}) collective-permute-start(f32[64,512]{1,0:T(8,128)S(1)} %collective-permute-done.9.refs_0_), channel_id=1, source_target_pairs={{0,1},{1,0},{2,3},{3,2},{4,5},{5,4},{6,7},{7,6},{8,9},{9,8},{10,11... | collective-permute-start | bytes 393224 | tf_op jit(solution)/shard_map/ppermute | solution.py:659
  37.3 1.3 %collective-permute-start.14 = (f32[64,512]{1,0:T(8,128)S(1)}, f32[64,512]{1,0:T(8,128)S(1)}, u32[]{:S(2)}, u32[]{:S(2)}) collective-permute-start(f32[64,512]{1,0:T(8,128)S(1)} %collective-permute-done.10.refs_1_), channel_id=1, source_target_pairs={{0,1},{1,0},{2,3},{3,2},{4,5},{5,4},{6,7},{7,6},{8,9},{9,8},{10,11... | collective-permute-start | bytes 393224 | tf_op jit(solution)/shard_map/ppermute | solution.py:659
  42.1 7.8 %collective-permute-start.17 = (f32[136,128]{1,0:T(8,128)S(1)}, f32[136,128]{1,0:T(8,128)S(1)}, u32[]{:S(2)}, u32[]{:S(2)}) collective-permute-start(f32[136,128]{1,0:T(8,128)S(1)} %get-tuple-element.65), channel_id=1, source_target_pairs={{0,8},{8,0},{1,9},{9,1},{2,10},{10,2},{3,11},{11,3},{4,12},{12,4},... | collective-permute-start | bytes 208904 | tf_op jit(solution)/shard_map/ppermute | solution.py:602
  52.0 2.0 %collective-permute-start.18 = (f32[4,64,512]{2,1,0:T(8,128)S(1)}, f32[4,64,512]{2,1,0:T(8,128)S(1)}, u32[]{:S(2)}, u32[]{:S(2)}) collective-permute-start(f32[4,64,512]{2,1,0:T(8,128)S(1)} %get-tuple-element.74), channel_id=1, source_target_pairs={{0,1},{1,0},{2,3},{3,2},{4,5},{5,4},{6,7},{7,6},{8,9},{9,8},{10,11... | collective-permute-start | bytes 1572872 | tf_op jit(solution)/shard_map/ppermute | solution.py:659
  54.1 8.2 %collective-permute-start.19 = (f32[64,512]{1,0:T(8,128)S(1)}, f32[64,512]{1,0:T(8,128)S(1)}, u32[]{:S(2)}, u32[]{:S(2)}) collective-permute-start(f32[64,512]{1,0:T(8,128)S(1)} %get-tuple-element.75), channel_id=1, source_target_pairs={{0,6},{1,15},{2,4},{3,13},{4,2},{5,11},{6,0},{7,9},{8,14},{9,7},{1... | collective-permute-start | bytes 393224 | tf_op jit(solution)/shard_map/ppermute | solution.py:656
  56.9 11.3 %collective-permute-start.20 = (f32[64,512]{1,0:T(8,128)S(1)}, f32[64,512]{1,0:T(8,128)S(1)}, u32[]{:S(2)}, u32[]{:S(2)}) collective-permute-start(f32[64,512]{1,0:T(8,128)S(1)} %get-tuple-element.76), channel_id=1, source_target_pairs={{0,4},{1,13},{2,6},{3,15},{4,0},{5,9},{6,2},{7,11},{8,12},{9,5},{1... | collective-permute-start | bytes 393224 | tf_op jit(solution)/shard_map/ppermute | solution.py:656
  56.9 11.4 %collective-permute-start.21 = (f32[64,512]{1,0:T(8,128)S(1)}, f32[64,512]{1,0:T(8,128)S(1)}, u32[]{:S(2)}, u32[]{:S(2)}) collective-permute-start(f32[64,512]{1,0:T(8,128)S(1)} %get-tuple-element.77), channel_id=1, source_target_pairs={{0,2},{1,11},{2,0},{3,9},{4,6},{5,15},{6,4},{7,13},{8,10},{9,3},{1... | collective-permute-start | bytes 393224 | tf_op jit(solution)/shard_map/ppermute | solution.py:656
  58.5 10.2 %collective-permute-start.22 = (f32[64,512]{1,0:T(8,128)S(1)}, f32[64,512]{1,0:T(8,128)S(1)}, u32[]{:S(2)}, u32[]{:S(2)}) collective-permute-start(f32[64,512]{1,0:T(8,128)S(1)} %get-tuple-element.78), channel_id=1, source_target_pairs={{0,0},{1,9},{2,2},{3,11},{4,4},{5,13},{6,6},{7,15},{8,8},{9,1},{10... | collective-permute-start | bytes 393224 | tf_op jit(solution)/shard_map/ppermute | solution.py:656
  62.3 6.6 %collective-permute-start.23 = (f32[64,512]{1,0:T(8,128)S(1)}, f32[64,512]{1,0:T(8,128)S(1)}, u32[]{:S(2)}, u32[]{:S(2)}) collective-permute-start(f32[64,512]{1,0:T(8,128)S(1)} %collective-permute-done.19.refs_0_), channel_id=1, source_target_pairs={{0,1},{1,0},{2,3},{3,2},{4,5},{5,4},{6,7},{7,6},{8,9},{9,8},{10,11... | collective-permute-start | bytes 393224 | tf_op jit(solution)/shard_map/ppermute | solution.py:659
  68.3 1.4 %collective-permute-start.25 = (f32[64,512]{1,0:T(8,128)S(1)}, f32[64,512]{1,0:T(8,128)S(1)}, u32[]{:S(2)}, u32[]{:S(2)}) collective-permute-start(f32[64,512]{1,0:T(8,128)S(1)} %collective-permute-done.21.refs_2_), channel_id=1, source_target_pairs={{0,1},{1,0},{2,3},{3,2},{4,5},{5,4},{6,7},{7,6},{8,9},{9,8},{10,11... | collective-permute-start | bytes 393224 | tf_op jit(solution)/shard_map/ppermute | solution.py:659
  68.7 1.3 %collective-permute-start.26 = (f32[64,512]{1,0:T(8,128)S(1)}, f32[64,512]{1,0:T(8,128)S(1)}, u32[]{:S(2)}, u32[]{:S(2)}) collective-permute-start(f32[64,512]{1,0:T(8,128)S(1)} %collective-permute-done.22.refs_3_), channel_id=1, source_target_pairs={{0,1},{1,0},{2,3},{3,2},{4,5},{5,4},{6,7},{7,6},{8,9},{9,8},{10,11... | collective-permute-start | bytes 393224 | tf_op jit(solution)/shard_map/ppermute | solution.py:659
  (5 other events, 44.6 us)

commit v23 on v22

--- a/solution.py
+++ b/solution.py
@@ -562,7 +562,7 @@
 
 
 def far_first(blocks):
-    return list(reversed(range(blocks)))
+    return list(range(blocks // 2, blocks)) + list(reversed(range(blocks // 2)))
 
 
 def final_kernel(blocks, pos_ref, *refs):

time: 72.5 us -> 73 us (level)
  waiting for transfers between devices: 23.6 us -> 25 us
  starting transfers between devices: 24.5 us -> 23.7 us
    ppermute x9, waiting for transfers between devices: 13 us -> 14.4 us  [swap(): return lax.ppermute(value, axes, pairs)]
    ppermute x9, starting transfers between devices: 11.8 us -> 10.8 us  [swap(): return lax.ppermute(value, axes, pairs)]
  transfers between devices with their start and end apart: 27 -> 27, of which waited for: 14 -> 14; matrix products, arithmetic and copies ran while one was open for 0% -> 0% of each run, Pallas kernels for 19% -> 20%
where the time goes in v23:
time: 73 us; the launch traced here: 72.9 us
  waiting for transfers between devices  25 us (34%)
  Pallas kernels  24.1 us (33%)
  starting transfers between devices  23.7 us (32%)
    ppermute x9, waiting for transfers between devices, swap(): return lax.ppermute(value, axes, pairs)  14.4 us
    ppermute x9, starting transfers between devices, swap(): return lax.ppermute(value, axes, pairs)  10.8 us
    pallas_call x1, Pallas kernels, body(): pl.pallas_call(functools.partial(near_kernel, layout), out_shape=vm((cols...  6.65 us
    ppermute x3, starting transfers between devices, body(): lax.ppermute(place[step], 'sub', [(i, i ^ stride) for i in range(blocks)])  6.51 us
    ppermute x3, waiting for transfers between devices, body(): lax.ppermute(place[step], 'sub', [(i, i ^ stride) for i in range(blocks)])  6.25 us
    pallas_call x1, Pallas kernels, body(): pl.pallas_call(functools.partial(points_kernel, layout, trees), out_shape...  5.8 us
    ppermute x14, starting transfers between devices, other_core(): return lax.ppermute(value, 'rep', [(0, 1), (1, 0)])  5.46 us
    ppermute x14, waiting for transfers between devices, other_core(): return lax.ppermute(value, 'rep', [(0, 1), (1, 0)])  4.39 us
  transfers between devices with their start and end apart: 27, of which 14 were waited for; matrix products, arithmetic and copies ran while one was open for 0% of the time, Pallas kernels for 20%

profile of v23, /device:TPU:0, one launch (start us, length us, event | category | flops | bytes accessed | tf_op | source)
XLA Modules:
  0.0 72.9 jit_solution(14362693204816926514)
XLA Ops:
  0.0 2.7 %sort_points.1 = (f32[72,512]{1,0:T(8,128)}, f32[8,128]{1,0:T(8,128)}) custom-call(s32[8,128]{1,0:T(8,128)} %bitcast.6, f32[64,1024]{1,0:T(8,128)} %bitcast.5, s32[1,128]{1,0:T(1,128)} %base_ref.1, s32[2,3]{1,0:T(2,128)} %flag_ref.1), custom_call_target="tpu_custom_call" | custom-call | tf_op jit(solution)/shard_map/sort_points/pallas_call | solution.py:638
  2.7 1.6 %collective-permute-start = (f32[72,512]{1,0:T(8,128)}, f32[72,512]{1,0:T(8,128)S(1)}, u32[]{:S(2)}, u32[]{:S(2)}) collective-permute-start(f32[72,512]{1,0:T(8,128)} %get-tuple-element.43), channel_id=1, source_target_pairs={{0,0},{1,9},{2,2},{3,11},{4,4},{5,13},{6,6},{7,15},{8,8},{9,1},{10... | collective-permute-start | bytes 442376 | tf_op jit(solution)/shard_map/ppermute | solution.py:656
  4.3 4.0 %collective-permute-start.2 = (f32[72,512]{1,0:T(8,128)S(1)}, f32[72,512]{1,0:T(8,128)S(1)}, u32[]{:S(2)}, u32[]{:S(2)}) collective-permute-start(f32[72,512]{1,0:T(8,128)S(1)} %collective-permute-done.refs_0_), channel_id=1, source_target_pairs={{0,4},{2,6},{4,0},{6,2},{1,5},{3,7},{5,1},{7,3},{8,12},{10,14},{12... | collective-permute-start | bytes 442376 | tf_op jit(solution)/shard_map/ppermute | solution.py:685
  8.3 1.6 %collective-permute-start.1 = (f32[72,512]{1,0:T(8,128)S(1)}, f32[72,512]{1,0:T(8,128)S(1)}, u32[]{:S(2)}, u32[]{:S(2)}) collective-permute-start(f32[72,512]{1,0:T(8,128)S(1)} %collective-permute-done.refs_0_), channel_id=1, source_target_pairs={{0,2},{2,0},{4,6},{6,4},{1,3},{3,1},{5,7},{7,5},{8,10},{10,8},{12,... | collective-permute-start | bytes 442376 | tf_op jit(solution)/shard_map/ppermute | solution.py:685
  9.9 3.2 %collective-permute-done.2.refs_2_ = f32[72,512]{1,0:T(8,128)S(1)} collective-permute-done((f32[72,512]{1,0:T(8,128)S(1)}, f32[72,512]{1,0:T(8,128)S(1)}, u32[]{:S(2)}, u32[]{:S(2)}) %collective-permute-start.2) | collective-permute-done | bytes 147488 | tf_op jit(solution)/shard_map/ppermute | solution.py:685
  13.2 0.9 %collective-permute-start.3 = (f32[72,512]{1,0:T(8,128)S(1)}, f32[72,512]{1,0:T(8,128)S(1)}, u32[]{:S(2)}, u32[]{:S(2)}) collective-permute-start(f32[72,512]{1,0:T(8,128)S(1)} %collective-permute-done.2.refs_2_), channel_id=1, source_target_pairs={{0,2},{2,0},{4,6},{6,4},{1,3},{3,1},{5,7},{7,5},{8,10},{10,8},{12,... | collective-permute-start | bytes 442376 | tf_op jit(solution)/shard_map/ppermute | solution.py:685
  14.1 1.8 %sort_weights.1 = (f32[4,32,512]{2,1,0:T(8,128)S(1)}, f32[4,32,512]{2,1,0:T(8,128)S(1)}) custom-call(f32[8,128]{1,0:T(8,128)} %get-tuple-element.42.pos_ref, f32[1024,128]{1,0:T(8,128)} %refs_8_.1), custom_call_target="tpu_custom_call" | custom-call | tf_op jit(solution)/shard_map/sort_weights/pallas_call | solution.py:666
  15.9 3.0 %collective-permute-done.3.refs_3_ = f32[72,512]{1,0:T(8,128)S(1)} collective-permute-done((f32[72,512]{1,0:T(8,128)S(1)}, f32[72,512]{1,0:T(8,128)S(1)}, u32[]{:S(2)}, u32[]{:S(2)}) %collective-permute-start.3) | collective-permute-done | bytes 147488 | tf_op jit(solution)/shard_map/ppermute | solution.py:685
  18.9 2.0 %collective-permute-start.8 = (f32[4,32,512]{2,1,0:T(8,128)S(1)}, f32[4,32,512]{2,1,0:T(8,128)S(1)}, u32[]{:S(2)}, u32[]{:S(2)}) collective-permute-start(f32[4,32,512]{2,1,0:T(8,128)S(1)} %get-tuple-element.54), channel_id=1, source_target_pairs={{0,1},{1,0},{2,3},{3,2},{4,5},{5,4},{6,7},{7,6},{8,9},{9,8},{10,11... | collective-permute-start | bytes 786440 | tf_op jit(solution)/shard_map/ppermute | solution.py:659
  22.1 2.3 %collective-permute-start.9 = (f32[64,512]{1,0:T(8,128)S(1)}, f32[64,512]{1,0:T(8,128)S(1)}, u32[]{:S(2)}, u32[]{:S(2)}) collective-permute-start(f32[64,512]{1,0:T(8,128)S(1)} %get-tuple-element.55), channel_id=1, source_target_pairs={{0,4},{1,13},{2,6},{3,15},{4,0},{5,9},{6,2},{7,11},{8,12},{9,5},{1... | collective-permute-start | bytes 393224 | tf_op jit(solution)/shard_map/ppermute | solution.py:656
  24.5 1.3 %collective-permute-start.10 = (f32[64,512]{1,0:T(8,128)S(1)}, f32[64,512]{1,0:T(8,128)S(1)}, u32[]{:S(2)}, u32[]{:S(2)}) collective-permute-start(f32[64,512]{1,0:T(8,128)S(1)} %get-tuple-element.56), channel_id=1, source_target_pairs={{0,6},{1,15},{2,4},{3,13},{4,2},{5,11},{6,0},{7,9},{8,14},{9,7},{1... | collective-permute-start | bytes 393224 | tf_op jit(solution)/shard_map/ppermute | solution.py:656
  27.0 5.8 %tree_points.1 = (bf16[144,4096]{1,0:T(8,128)(2,1)S(1)}, bf16[4096,256]{1,0:T(8,128)(2,1)}, bf16[4,1024,128]{2,1,0:T(8,128)(2,1)}, bf16[896,256]{1,0:T(8,128)(2,...) custom-call(s32[1,8]{1,0:T(1,128)} %count_ref.1, ...), custom_call_target="tpu_custom_call" | custom-call | tf_op jit(solution)/shard_map/tree_points/pallas_call | solution.py:715
  32.8 2.1 %collective-permute-done.9.refs_0_ = f32[64,512]{1,0:T(8,128)S(1)} collective-permute-done((f32[64,512]{1,0:T(8,128)S(1)}, f32[64,512]{1,0:T(8,128)S(1)}, u32[]{:S(2)}, u32[]{:S(2)}) %collective-permute-start.9) | collective-permute-done | bytes 131104 | tf_op jit(solution)/shard_map/ppermute | solution.py:656
  34.9 1.9 %collective-permute-done.11.refs_2_ = f32[64,512]{1,0:T(8,128)S(1)} collective-permute-done((f32[64,512]{1,0:T(8,128)S(1)}, f32[64,512]{1,0:T(8,128)S(1)}, u32[]{:S(2)}, u32[]{:S(2)}) %collective-permute-start.11) | collective-permute-done | bytes 131104 | tf_op jit(solution)/shard_map/ppermute | solution.py:656
  39.4 2.9 %tree_weights.1 = (bf16[64,4096]{1,0:T(8,128)(2,1)S(1)}, bf16[128,896]{1,0:T(8,128)(2,1)S(1)}, f32[136,128]{1,0:T(8,128)S(1)}) custom-call(bf16[4,1024,128]{2,1,0:T(8,128)(2,1)} %get-tuple-element.50.base_hbm, f32[3,256,128]{2,1,0:T(8,128)S(1)} %get-tuple-element.51.upper_tiles_ref, f32[72,128]{1,0:T(8,128)S(1)} %get-tuple-element.52.top_ref, ...), custom_call_target="tpu_custom_call" | custom-call | tf_op jit(solution)/shard_map/tree_weights/pallas_call | solution.py:747
  42.3 1.0 %collective-permute-start.17 = (f32[136,128]{1,0:T(8,128)S(1)}, f32[136,128]{1,0:T(8,128)S(1)}, u32[]{:S(2)}, u32[]{:S(2)}) collective-permute-start(f32[136,128]{1,0:T(8,128)S(1)} %get-tuple-element.65), channel_id=1, source_target_pairs={{0,8},{8,0},{1,9},{9,1},{2,10},{10,2},{3,11},{11,3},{4,12},{12,4},... | collective-permute-start | bytes 208904 | tf_op jit(solution)/shard_map/ppermute | solution.py:602
  43.3 6.6 %near.1.near_ref = f32[64,2048]{1,0:T(8,128)S(1)} custom-call(s32[3,72]{1,0:T(4,128)} %get-tuple-element.70.tiles, bf16[4096,256]{1,0:T(8,128)(2,1)} %get-tuple-element.71.a_hbm, bf16[144,4096]{1,0:T(8,128)(2,1)S(1)} %get-tuple-element.67.tree_ref, bf16[64,4096]{1,0:T(8,128)(2,1)S(1)} %get-tuple-element.72.w_ref), custom_call_target="tpu_custom_call" | custom-call | tf_op jit(solution)/shard_map/near/pallas_call | solution.py:768
  50.0 2.2 %far.1 = (f32[4,64,512]{2,1,0:T(8,128)S(1)}, f32[4,64,512]{2,1,0:T(8,128)S(1)}) custom-call(f32[1,136,128]{2,1,0:T(8,128)S(1)} %bitcast.4, f32[4,1024]{1,0:T(4,128)S(1)} %get-tuple-element.60.slot_ref, f32[4,8,128]{2,1,0:T(8,128)S(1)} %get-tuple-element.66.info_ref, bf16[144,4096]{1,0:T(8,128)(2,1)S(1)} %get-tuple-element.67.tree_ref, ...), custom_call_target="tpu_custom_call" | custom-call | tf_op jit(solution)/shard_map/far/pallas_call | solution.py:785
  52.2 1.9 %collective-permute-done.18.got_ref = f32[4,64,512]{2,1,0:T(8,128)S(1)} collective-permute-done((f32[4,64,512]{2,1,0:T(8,128)S(1)}, f32[4,64,512]{2,1,0:T(8,128)S(1)}, u32[]{:S(2)}, u32[]{:S(2)}) %collective-permute-start.18) | collective-permute-done | bytes 524320 | tf_op jit(solution)/shard_map/ppermute | solution.py:659
  54.2 3.1 %collective-permute-start.19 = (f32[64,512]{1,0:T(8,128)S(1)}, f32[64,512]{1,0:T(8,128)S(1)}, u32[]{:S(2)}, u32[]{:S(2)}) collective-permute-start(f32[64,512]{1,0:T(8,128)S(1)} %get-tuple-element.75), channel_id=1, source_target_pairs={{0,4},{1,13},{2,6},{3,15},{4,0},{5,9},{6,2},{7,11},{8,12},{9,5},{1... | collective-permute-start | bytes 393224 | tf_op jit(solution)/shard_map/ppermute | solution.py:656
  58.6 8.7 %collective-permute-done.19.refs_0_ = f32[64,512]{1,0:T(8,128)S(1)} collective-permute-done((f32[64,512]{1,0:T(8,128)S(1)}, f32[64,512]{1,0:T(8,128)S(1)}, u32[]{:S(2)}, u32[]{:S(2)}) %collective-permute-start.19) | collective-permute-done | bytes 131104 | tf_op jit(solution)/shard_map/ppermute | solution.py:656
  67.8 1.6 %collective-permute-done.21.refs_2_ = f32[64,512]{1,0:T(8,128)S(1)} collective-permute-done((f32[64,512]{1,0:T(8,128)S(1)}, f32[64,512]{1,0:T(8,128)S(1)}, u32[]{:S(2)}, u32[]{:S(2)}) %collective-permute-start.21) | collective-permute-done | bytes 131104 | tf_op jit(solution)/shard_map/ppermute | solution.py:656
  70.0 0.8 %collective-permute-done.25.refs_6_ = f32[64,512]{1,0:T(8,128)S(1)} collective-permute-done((f32[64,512]{1,0:T(8,128)S(1)}, f32[64,512]{1,0:T(8,128)S(1)}, u32[]{:S(2)}, u32[]{:S(2)}) %collective-permute-start.25) | collective-permute-done | bytes 131104 | tf_op jit(solution)/shard_map/ppermute | solution.py:659
  71.0 1.9 %to_input_order.1 = f32[1024,128]{1,0:T(8,128)} custom-call(f32[8,128]{1,0:T(8,128)S(1)} %copy-done.1, f32[64,512]{1,0:T(8,128)S(1)} %collective-permute-done.19.refs_0_, f32[64,512]{1,0:T(8,128)S(1)} %collective-permute-done.20.refs_1_, f32[64,512]{1,0:T(8,128)S(1)} %collective-permute-done.21.refs_2_, f32[64,512]{1,0:T(8,128)S(1)} %collective-permute-done.22.refs_3_, ...), custom_call_target="tpu_custom_call" | custom-call | tf_op jit(solution)/shard_map/to_input_order/pallas_call | solution.py:822
  (43 shorter events, 7.7 us)
Async XLA Ops:
  2.7 1.6 %collective-permute-start = (f32[72,512]{1,0:T(8,128)}, f32[72,512]{1,0:T(8,128)S(1)}, u32[]{:S(2)}, u32[]{:S(2)}) collective-permute-start(f32[72,512]{1,0:T(8,128)} %get-tuple-element.43), channel_id=1, source_target_pairs={{0,0},{1,9},{2,2},{3,11},{4,4},{5,13},{6,6},{7,15},{8,8},{9,1},{10... | collective-permute-start | bytes 442376 | tf_op jit(solution)/shard_map/ppermute | solution.py:656
  4.3 8.8 %collective-permute-start.2 = (f32[72,512]{1,0:T(8,128)S(1)}, f32[72,512]{1,0:T(8,128)S(1)}, u32[]{:S(2)}, u32[]{:S(2)}) collective-permute-start(f32[72,512]{1,0:T(8,128)S(1)} %collective-permute-done.refs_0_), channel_id=1, source_target_pairs={{0,4},{2,6},{4,0},{6,2},{1,5},{3,7},{5,1},{7,3},{8,12},{10,14},{12... | collective-permute-start | bytes 442376 | tf_op jit(solution)/shard_map/ppermute | solution.py:685
  8.3 7.5 %collective-permute-start.1 = (f32[72,512]{1,0:T(8,128)S(1)}, f32[72,512]{1,0:T(8,128)S(1)}, u32[]{:S(2)}, u32[]{:S(2)}) collective-permute-start(f32[72,512]{1,0:T(8,128)S(1)} %collective-permute-done.refs_0_), channel_id=1, source_target_pairs={{0,2},{2,0},{4,6},{6,4},{1,3},{3,1},{5,7},{7,5},{8,10},{10,8},{12,... | collective-permute-start | bytes 442376 | tf_op jit(solution)/shard_map/ppermute | solution.py:685
  13.2 5.7 %collective-permute-start.3 = (f32[72,512]{1,0:T(8,128)S(1)}, f32[72,512]{1,0:T(8,128)S(1)}, u32[]{:S(2)}, u32[]{:S(2)}) collective-permute-start(f32[72,512]{1,0:T(8,128)S(1)} %collective-permute-done.2.refs_2_), channel_id=1, source_target_pairs={{0,2},{2,0},{4,6},{6,4},{1,3},{3,1},{5,7},{7,5},{8,10},{10,8},{12,... | collective-permute-start | bytes 442376 | tf_op jit(solution)/shard_map/ppermute | solution.py:685
  18.9 3.2 %collective-permute-start.8 = (f32[4,32,512]{2,1,0:T(8,128)S(1)}, f32[4,32,512]{2,1,0:T(8,128)S(1)}, u32[]{:S(2)}, u32[]{:S(2)}) collective-permute-start(f32[4,32,512]{2,1,0:T(8,128)S(1)} %get-tuple-element.54), channel_id=1, source_target_pairs={{0,1},{1,0},{2,3},{3,2},{4,5},{5,4},{6,7},{7,6},{8,9},{9,8},{10,11... | collective-permute-start | bytes 786440 | tf_op jit(solution)/shard_map/ppermute | solution.py:659
  20.9 3.5 %collective-permute-start.4 = (f32[72,512]{1,0:T(8,128)S(1)}, f32[72,512]{1,0:T(8,128)S(1)}, u32[]{:S(2)}, u32[]{:S(2)}) collective-permute-start(f32[72,512]{1,0:T(8,128)S(1)} %collective-permute-done.refs_0_), channel_id=1, source_target_pairs={{0,1},{1,0},{2,3},{3,2},{4,5},{5,4},{6,7},{7,6},{8,9},{9,8},{10,11... | collective-permute-start | bytes 442376 | tf_op jit(solution)/shard_map/ppermute | solution.py:659
  20.9 4.8 %collective-permute-start.5 = (f32[72,512]{1,0:T(8,128)S(1)}, f32[72,512]{1,0:T(8,128)S(1)}, u32[]{:S(2)}, u32[]{:S(2)}) collective-permute-start(f32[72,512]{1,0:T(8,128)S(1)} %collective-permute-done.1.refs_1_), channel_id=1, source_target_pairs={{0,1},{1,0},{2,3},{3,2},{4,5},{5,4},{6,7},{7,6},{8,9},{9,8},{10,11... | collective-permute-start | bytes 442376 | tf_op jit(solution)/shard_map/ppermute | solution.py:659
  21.4 4.8 %collective-permute-start.6 = (f32[72,512]{1,0:T(8,128)S(1)}, f32[72,512]{1,0:T(8,128)S(1)}, u32[]{:S(2)}, u32[]{:S(2)}) collective-permute-start(f32[72,512]{1,0:T(8,128)S(1)} %collective-permute-done.2.refs_2_), channel_id=1, source_target_pairs={{0,1},{1,0},{2,3},{3,2},{4,5},{5,4},{6,7},{7,6},{8,9},{9,8},{10,11... | collective-permute-start | bytes 442376 | tf_op jit(solution)/shard_map/ppermute | solution.py:659
  21.4 5.5 %collective-permute-start.7 = (f32[72,512]{1,0:T(8,128)S(1)}, f32[72,512]{1,0:T(8,128)S(1)}, u32[]{:S(2)}, u32[]{:S(2)}) collective-permute-start(f32[72,512]{1,0:T(8,128)S(1)} %collective-permute-done.3.refs_3_), channel_id=1, source_target_pairs={{0,1},{1,0},{2,3},{3,2},{4,5},{5,4},{6,7},{7,6},{8,9},{9,8},{10,11... | collective-permute-start | bytes 442376 | tf_op jit(solution)/shard_map/ppermute | solution.py:659
  22.1 12.8 %collective-permute-start.9 = (f32[64,512]{1,0:T(8,128)S(1)}, f32[64,512]{1,0:T(8,128)S(1)}, u32[]{:S(2)}, u32[]{:S(2)}) collective-permute-start(f32[64,512]{1,0:T(8,128)S(1)} %get-tuple-element.55), channel_id=1, source_target_pairs={{0,4},{1,13},{2,6},{3,15},{4,0},{5,9},{6,2},{7,11},{8,12},{9,5},{1... | collective-permute-start | bytes 393224 | tf_op jit(solution)/shard_map/ppermute | solution.py:656
  24.5 10.4 %collective-permute-start.10 = (f32[64,512]{1,0:T(8,128)S(1)}, f32[64,512]{1,0:T(8,128)S(1)}, u32[]{:S(2)}, u32[]{:S(2)}) collective-permute-start(f32[64,512]{1,0:T(8,128)S(1)} %get-tuple-element.56), channel_id=1, source_target_pairs={{0,6},{1,15},{2,4},{3,13},{4,2},{5,11},{6,0},{7,9},{8,14},{9,7},{1... | collective-permute-start | bytes 393224 | tf_op jit(solution)/shard_map/ppermute | solution.py:656
  25.7 11.1 %collective-permute-start.11 = (f32[64,512]{1,0:T(8,128)S(1)}, f32[64,512]{1,0:T(8,128)S(1)}, u32[]{:S(2)}, u32[]{:S(2)}) collective-permute-start(f32[64,512]{1,0:T(8,128)S(1)} %get-tuple-element.57), channel_id=1, source_target_pairs={{0,2},{1,11},{2,0},{3,9},{4,6},{5,15},{6,4},{7,13},{8,10},{9,3},{1... | collective-permute-start | bytes 393224 | tf_op jit(solution)/shard_map/ppermute | solution.py:656
  26.3 10.5 %collective-permute-start.12 = (f32[64,512]{1,0:T(8,128)S(1)}, f32[64,512]{1,0:T(8,128)S(1)}, u32[]{:S(2)}, u32[]{:S(2)}) collective-permute-start(f32[64,512]{1,0:T(8,128)S(1)} %get-tuple-element.58), channel_id=1, source_target_pairs={{0,0},{1,9},{2,2},{3,11},{4,4},{5,13},{6,6},{7,15},{8,8},{9,1},{10... | collective-permute-start | bytes 393224 | tf_op jit(solution)/shard_map/ppermute | solution.py:656
  36.8 1.7 %collective-permute-start.13 = (f32[64,512]{1,0:T(8,128)S(1)}, f32[64,512]{1,0:T(8,128)S(1)}, u32[]{:S(2)}, u32[]{:S(2)}) collective-permute-start(f32[64,512]{1,0:T(8,128)S(1)} %collective-permute-done.9.refs_0_), channel_id=1, source_target_pairs={{0,1},{1,0},{2,3},{3,2},{4,5},{5,4},{6,7},{7,6},{8,9},{9,8},{10,11... | collective-permute-start | bytes 393224 | tf_op jit(solution)/shard_map/ppermute | solution.py:659
  37.6 1.5 %collective-permute-start.15 = (f32[64,512]{1,0:T(8,128)S(1)}, f32[64,512]{1,0:T(8,128)S(1)}, u32[]{:S(2)}, u32[]{:S(2)}) collective-permute-start(f32[64,512]{1,0:T(8,128)S(1)} %collective-permute-done.11.refs_2_), channel_id=1, source_target_pairs={{0,1},{1,0},{2,3},{3,2},{4,5},{5,4},{6,7},{7,6},{8,9},{9,8},{10,11... | collective-permute-start | bytes 393224 | tf_op jit(solution)/shard_map/ppermute | solution.py:659
  42.3 7.7 %collective-permute-start.17 = (f32[136,128]{1,0:T(8,128)S(1)}, f32[136,128]{1,0:T(8,128)S(1)}, u32[]{:S(2)}, u32[]{:S(2)}) collective-permute-start(f32[136,128]{1,0:T(8,128)S(1)} %get-tuple-element.65), channel_id=1, source_target_pairs={{0,8},{8,0},{1,9},{9,1},{2,10},{10,2},{3,11},{11,3},{4,12},{12,4},... | collective-permute-start | bytes 208904 | tf_op jit(solution)/shard_map/ppermute | solution.py:602
  52.2 2.0 %collective-permute-start.18 = (f32[4,64,512]{2,1,0:T(8,128)S(1)}, f32[4,64,512]{2,1,0:T(8,128)S(1)}, u32[]{:S(2)}, u32[]{:S(2)}) collective-permute-start(f32[4,64,512]{2,1,0:T(8,128)S(1)} %get-tuple-element.74), channel_id=1, source_target_pairs={{0,1},{1,0},{2,3},{3,2},{4,5},{5,4},{6,7},{7,6},{8,9},{9,8},{10,11... | collective-permute-start | bytes 1572872 | tf_op jit(solution)/shard_map/ppermute | solution.py:659
  54.2 13.1 %collective-permute-start.19 = (f32[64,512]{1,0:T(8,128)S(1)}, f32[64,512]{1,0:T(8,128)S(1)}, u32[]{:S(2)}, u32[]{:S(2)}) collective-permute-start(f32[64,512]{1,0:T(8,128)S(1)} %get-tuple-element.75), channel_id=1, source_target_pairs={{0,4},{1,13},{2,6},{3,15},{4,0},{5,9},{6,2},{7,11},{8,12},{9,5},{1... | collective-permute-start | bytes 393224 | tf_op jit(solution)/shard_map/ppermute | solution.py:656
  57.3 10.0 %collective-permute-start.20 = (f32[64,512]{1,0:T(8,128)S(1)}, f32[64,512]{1,0:T(8,128)S(1)}, u32[]{:S(2)}, u32[]{:S(2)}) collective-permute-start(f32[64,512]{1,0:T(8,128)S(1)} %get-tuple-element.76), channel_id=1, source_target_pairs={{0,6},{1,15},{2,4},{3,13},{4,2},{5,11},{6,0},{7,9},{8,14},{9,7},{1... | collective-permute-start | bytes 393224 | tf_op jit(solution)/shard_map/ppermute | solution.py:656
  57.9 11.5 %collective-permute-start.21 = (f32[64,512]{1,0:T(8,128)S(1)}, f32[64,512]{1,0:T(8,128)S(1)}, u32[]{:S(2)}, u32[]{:S(2)}) collective-permute-start(f32[64,512]{1,0:T(8,128)S(1)} %get-tuple-element.77), channel_id=1, source_target_pairs={{0,2},{1,11},{2,0},{3,9},{4,6},{5,15},{6,4},{7,13},{8,10},{9,3},{1... | collective-permute-start | bytes 393224 | tf_op jit(solution)/shard_map/ppermute | solution.py:656
  57.9 11.5 %collective-permute-start.22 = (f32[64,512]{1,0:T(8,128)S(1)}, f32[64,512]{1,0:T(8,128)S(1)}, u32[]{:S(2)}, u32[]{:S(2)}) collective-permute-start(f32[64,512]{1,0:T(8,128)S(1)} %get-tuple-element.78), channel_id=1, source_target_pairs={{0,0},{1,9},{2,2},{3,11},{4,4},{5,13},{6,6},{7,15},{8,8},{9,1},{10... | collective-permute-start | bytes 393224 | tf_op jit(solution)/shard_map/ppermute | solution.py:656
  67.3 2.7 %collective-permute-start.23 = (f32[64,512]{1,0:T(8,128)S(1)}, f32[64,512]{1,0:T(8,128)S(1)}, u32[]{:S(2)}, u32[]{:S(2)}) collective-permute-start(f32[64,512]{1,0:T(8,128)S(1)} %collective-permute-done.19.refs_0_), channel_id=1, source_target_pairs={{0,1},{1,0},{2,3},{3,2},{4,5},{5,4},{6,7},{7,6},{8,9},{9,8},{10,11... | collective-permute-start | bytes 393224 | tf_op jit(solution)/shard_map/ppermute | solution.py:659
  67.3 2.7 %collective-permute-start.24 = (f32[64,512]{1,0:T(8,128)S(1)}, f32[64,512]{1,0:T(8,128)S(1)}, u32[]{:S(2)}, u32[]{:S(2)}) collective-permute-start(f32[64,512]{1,0:T(8,128)S(1)} %collective-permute-done.20.refs_1_), channel_id=1, source_target_pairs={{0,1},{1,0},{2,3},{3,2},{4,5},{5,4},{6,7},{7,6},{8,9},{9,8},{10,11... | collective-permute-start | bytes 393224 | tf_op jit(solution)/shard_map/ppermute | solution.py:659
  69.5 1.5 %collective-permute-start.26 = (f32[64,512]{1,0:T(8,128)S(1)}, f32[64,512]{1,0:T(8,128)S(1)}, u32[]{:S(2)}, u32[]{:S(2)}) collective-permute-start(f32[64,512]{1,0:T(8,128)S(1)} %collective-permute-done.22.refs_3_), channel_id=1, source_target_pairs={{0,1},{1,0},{2,3},{3,2},{4,5},{5,4},{6,7},{7,6},{8,9},{9,8},{10,11... | collective-permute-start | bytes 393224 | tf_op jit(solution)/shard_map/ppermute | solution.py:659
  (5 other events, 46.1 us)

commit v24 on v22

--- a/solution.py
+++ b/solution.py
@@ -571,8 +571,13 @@
     rows = chunks * LANES
     width, split = back_refs[0].shape
     width = LANES // blocks if blocks else width
-    for r in range(chunks):
-        spread(perm, slice(r * LANES, (r + 1) * LANES), column(pos_ref[r : r + 1, :]))
+    step = 512
+
+    def make(first):
+        for r in range(first // LANES, (first + step) // LANES):
+            spread(perm, slice(r * LANES, (r + 1) * LANES), column(pos_ref[r : r + 1, :]))
+
+    make(0)
     for g, back_ref in enumerate(back_refs):
         columns, at = 0, slice(0, rows)
         value = back_ref[...]
@@ -583,9 +588,10 @@
         high, low = two(value)
         vals[aligned(columns, width, width), at] = high
         vals[aligned(columns + LANES, width, width), at] = low
-    step = 256
     for s in range(rows // step):
         here = slice(s * step, (s + 1) * step)
+        if (s + 1) * step < rows:
+            make((s + 1) * step)
         moved = nt(perm[here, :], vals[...])
         out_ref[here, :] = ridge * weights_ref[here, :] + moved[:, :LANES] + moved[:, LANES:]
 

time: 72.5 us -> 72.4 us (level)
  transfers between devices with their start and end apart: 27 -> 27, of which waited for: 14 -> 14; matrix products, arithmetic and copies ran while one was open for 0% -> 0% of each run, Pallas kernels for 19% -> 20%
where the time goes in v24:
time: 72.4 us; the launch traced here: 72.3 us
  starting transfers between devices  25 us (35%)
  Pallas kernels  24 us (33%)
  waiting for transfers between devices  23.2 us (32%)
    ppermute x9, waiting for transfers between devices, swap(): return lax.ppermute(value, axes, pairs)  12.7 us
    ppermute x9, starting transfers between devices, swap(): return lax.ppermute(value, axes, pairs)  11.8 us
    pallas_call x1, Pallas kernels, body(): pl.pallas_call(functools.partial(near_kernel, layout), out_shape=vm((cols...  6.64 us
    ppermute x3, starting transfers between devices, body(): lax.ppermute(place[step], 'sub', [(i, i ^ stride) for i in range(blocks)])  6.51 us
    ppermute x3, waiting for transfers between devices, body(): lax.ppermute(place[step], 'sub', [(i, i ^ stride) for i in range(blocks)])  6.25 us
    pallas_call x1, Pallas kernels, body(): pl.pallas_call(functools.partial(points_kernel, layout, trees), out_shape...  5.79 us
    ppermute x14, starting transfers between devices, other_core(): return lax.ppermute(value, 'rep', [(0, 1), (1, 0)])  5.33 us
    ppermute x14, waiting for transfers between devices, other_core(): return lax.ppermute(value, 'rep', [(0, 1), (1, 0)])  4.22 us
  transfers between devices with their start and end apart: 27, of which 14 were waited for; matrix products, arithmetic and copies ran while one was open for 0% of the time, Pallas kernels for 20%

profile of v24, /device:TPU:0, one launch (start us, length us, event | category | flops | bytes accessed | tf_op | source)
XLA Modules:
  0.0 72.3 jit_solution(3336563157453223776)
XLA Ops:
  0.0 2.7 %sort_points.1 = (f32[72,512]{1,0:T(8,128)}, f32[8,128]{1,0:T(8,128)}) custom-call(s32[8,128]{1,0:T(8,128)} %bitcast.6, f32[64,1024]{1,0:T(8,128)} %bitcast.5, s32[1,128]{1,0:T(1,128)} %base_ref.1, s32[2,3]{1,0:T(2,128)} %flag_ref.1), custom_call_target="tpu_custom_call" | custom-call | tf_op jit(solution)/shard_map/sort_points/pallas_call | solution.py:644
  2.7 1.6 %collective-permute-start = (f32[72,512]{1,0:T(8,128)}, f32[72,512]{1,0:T(8,128)S(1)}, u32[]{:S(2)}, u32[]{:S(2)}) collective-permute-start(f32[72,512]{1,0:T(8,128)} %get-tuple-element.43), channel_id=1, source_target_pairs={{0,0},{1,9},{2,2},{3,11},{4,4},{5,13},{6,6},{7,15},{8,8},{9,1},{10... | collective-permute-start | bytes 442376 | tf_op jit(solution)/shard_map/ppermute | solution.py:662
  4.3 4.0 %collective-permute-start.2 = (f32[72,512]{1,0:T(8,128)S(1)}, f32[72,512]{1,0:T(8,128)S(1)}, u32[]{:S(2)}, u32[]{:S(2)}) collective-permute-start(f32[72,512]{1,0:T(8,128)S(1)} %collective-permute-done.refs_0_), channel_id=1, source_target_pairs={{0,4},{2,6},{4,0},{6,2},{1,5},{3,7},{5,1},{7,3},{8,12},{10,14},{12... | collective-permute-start | bytes 442376 | tf_op jit(solution)/shard_map/ppermute | solution.py:691
  8.3 1.6 %collective-permute-start.1 = (f32[72,512]{1,0:T(8,128)S(1)}, f32[72,512]{1,0:T(8,128)S(1)}, u32[]{:S(2)}, u32[]{:S(2)}) collective-permute-start(f32[72,512]{1,0:T(8,128)S(1)} %collective-permute-done.refs_0_), channel_id=1, source_target_pairs={{0,2},{2,0},{4,6},{6,4},{1,3},{3,1},{5,7},{7,5},{8,10},{10,8},{12,... | collective-permute-start | bytes 442376 | tf_op jit(solution)/shard_map/ppermute | solution.py:691
  9.9 3.2 %collective-permute-done.2.refs_2_ = f32[72,512]{1,0:T(8,128)S(1)} collective-permute-done((f32[72,512]{1,0:T(8,128)S(1)}, f32[72,512]{1,0:T(8,128)S(1)}, u32[]{:S(2)}, u32[]{:S(2)}) %collective-permute-start.2) | collective-permute-done | bytes 147488 | tf_op jit(solution)/shard_map/ppermute | solution.py:691
  13.2 0.9 %collective-permute-start.3 = (f32[72,512]{1,0:T(8,128)S(1)}, f32[72,512]{1,0:T(8,128)S(1)}, u32[]{:S(2)}, u32[]{:S(2)}) collective-permute-start(f32[72,512]{1,0:T(8,128)S(1)} %collective-permute-done.2.refs_2_), channel_id=1, source_target_pairs={{0,2},{2,0},{4,6},{6,4},{1,3},{3,1},{5,7},{7,5},{8,10},{10,8},{12,... | collective-permute-start | bytes 442376 | tf_op jit(solution)/shard_map/ppermute | solution.py:691
  14.1 1.8 %sort_weights.1 = (f32[4,32,512]{2,1,0:T(8,128)S(1)}, f32[4,32,512]{2,1,0:T(8,128)S(1)}) custom-call(f32[8,128]{1,0:T(8,128)} %get-tuple-element.42.pos_ref, f32[1024,128]{1,0:T(8,128)} %refs_8_.1), custom_call_target="tpu_custom_call" | custom-call | tf_op jit(solution)/shard_map/sort_weights/pallas_call | solution.py:672
  15.9 3.0 %collective-permute-done.3.refs_3_ = f32[72,512]{1,0:T(8,128)S(1)} collective-permute-done((f32[72,512]{1,0:T(8,128)S(1)}, f32[72,512]{1,0:T(8,128)S(1)}, u32[]{:S(2)}, u32[]{:S(2)}) %collective-permute-start.3) | collective-permute-done | bytes 147488 | tf_op jit(solution)/shard_map/ppermute | solution.py:691
  18.9 2.0 %collective-permute-start.8 = (f32[4,32,512]{2,1,0:T(8,128)S(1)}, f32[4,32,512]{2,1,0:T(8,128)S(1)}, u32[]{:S(2)}, u32[]{:S(2)}) collective-permute-start(f32[4,32,512]{2,1,0:T(8,128)S(1)} %get-tuple-element.54), channel_id=1, source_target_pairs={{0,1},{1,0},{2,3},{3,2},{4,5},{5,4},{6,7},{7,6},{8,9},{9,8},{10,11... | collective-permute-start | bytes 786440 | tf_op jit(solution)/shard_map/ppermute | solution.py:665
  22.1 3.5 %collective-permute-start.9 = (f32[64,512]{1,0:T(8,128)S(1)}, f32[64,512]{1,0:T(8,128)S(1)}, u32[]{:S(2)}, u32[]{:S(2)}) collective-permute-start(f32[64,512]{1,0:T(8,128)S(1)} %get-tuple-element.55), channel_id=1, source_target_pairs={{0,6},{1,15},{2,4},{3,13},{4,2},{5,11},{6,0},{7,9},{8,14},{9,7},{1... | collective-permute-start | bytes 393224 | tf_op jit(solution)/shard_map/ppermute | solution.py:662
  25.6 0.9 %collective-permute-start.11 = (f32[64,512]{1,0:T(8,128)S(1)}, f32[64,512]{1,0:T(8,128)S(1)}, u32[]{:S(2)}, u32[]{:S(2)}) collective-permute-start(f32[64,512]{1,0:T(8,128)S(1)} %get-tuple-element.57), channel_id=1, source_target_pairs={{0,2},{1,11},{2,0},{3,9},{4,6},{5,15},{6,4},{7,13},{8,10},{9,3},{1... | collective-permute-start | bytes 393224 | tf_op jit(solution)/shard_map/ppermute | solution.py:662
  26.6 0.7 collective-permute-start.12
  27.3 5.8 %tree_points.1 = (bf16[144,4096]{1,0:T(8,128)(2,1)S(1)}, bf16[4096,256]{1,0:T(8,128)(2,1)}, bf16[4,1024,128]{2,1,0:T(8,128)(2,1)}, bf16[896,256]{1,0:T(8,128)(2,...) custom-call(s32[1,8]{1,0:T(1,128)} %count_ref.1, ...), custom_call_target="tpu_custom_call" | custom-call | tf_op jit(solution)/shard_map/tree_points/pallas_call | solution.py:721
  33.1 3.9 %collective-permute-done.10.refs_1_ = f32[64,512]{1,0:T(8,128)S(1)} collective-permute-done((f32[64,512]{1,0:T(8,128)S(1)}, f32[64,512]{1,0:T(8,128)S(1)}, u32[]{:S(2)}, u32[]{:S(2)}) %collective-permute-start.10) | collective-permute-done | bytes 131104 | tf_op jit(solution)/shard_map/ppermute | solution.py:662
  39.2 2.9 %tree_weights.1 = (bf16[64,4096]{1,0:T(8,128)(2,1)S(1)}, bf16[128,896]{1,0:T(8,128)(2,1)S(1)}, f32[136,128]{1,0:T(8,128)S(1)}) custom-call(bf16[4,1024,128]{2,1,0:T(8,128)(2,1)} %get-tuple-element.50.base_hbm, f32[3,256,128]{2,1,0:T(8,128)S(1)} %get-tuple-element.51.upper_tiles_ref, f32[72,128]{1,0:T(8,128)S(1)} %get-tuple-element.52.top_ref, ...), custom_call_target="tpu_custom_call" | custom-call | tf_op jit(solution)/shard_map/tree_weights/pallas_call | solution.py:753
  42.1 1.4 %collective-permute-start.17 = (f32[136,128]{1,0:T(8,128)S(1)}, f32[136,128]{1,0:T(8,128)S(1)}, u32[]{:S(2)}, u32[]{:S(2)}) collective-permute-start(f32[136,128]{1,0:T(8,128)S(1)} %get-tuple-element.65), channel_id=1, source_target_pairs={{0,8},{8,0},{1,9},{9,1},{2,10},{10,2},{3,11},{11,3},{4,12},{12,4},... | collective-permute-start | bytes 208904 | tf_op jit(solution)/shard_map/ppermute | solution.py:608
  43.5 6.6 %near.1.near_ref = f32[64,2048]{1,0:T(8,128)S(1)} custom-call(s32[3,72]{1,0:T(4,128)} %get-tuple-element.70.tiles, bf16[4096,256]{1,0:T(8,128)(2,1)} %get-tuple-element.71.a_hbm, bf16[144,4096]{1,0:T(8,128)(2,1)S(1)} %get-tuple-element.67.tree_ref, bf16[64,4096]{1,0:T(8,128)(2,1)S(1)} %get-tuple-element.72.w_ref), custom_call_target="tpu_custom_call" | custom-call | tf_op jit(solution)/shard_map/near/pallas_call | solution.py:774
  50.1 2.2 %far.1 = (f32[4,64,512]{2,1,0:T(8,128)S(1)}, f32[4,64,512]{2,1,0:T(8,128)S(1)}) custom-call(f32[1,136,128]{2,1,0:T(8,128)S(1)} %bitcast.4, f32[4,1024]{1,0:T(4,128)S(1)} %get-tuple-element.60.slot_ref, f32[4,8,128]{2,1,0:T(8,128)S(1)} %get-tuple-element.66.info_ref, bf16[144,4096]{1,0:T(8,128)(2,1)S(1)} %get-tuple-element.67.tree_ref, ...), custom_call_target="tpu_custom_call" | custom-call | tf_op jit(solution)/shard_map/far/pallas_call | solution.py:791
  52.4 1.9 %collective-permute-done.18.got_ref = f32[4,64,512]{2,1,0:T(8,128)S(1)} collective-permute-done((f32[4,64,512]{2,1,0:T(8,128)S(1)}, f32[4,64,512]{2,1,0:T(8,128)S(1)}, u32[]{:S(2)}, u32[]{:S(2)}) %collective-permute-start.18) | collective-permute-done | bytes 524320 | tf_op jit(solution)/shard_map/ppermute | solution.py:665
  54.3 2.9 %collective-permute-start.19 = (f32[64,512]{1,0:T(8,128)S(1)}, f32[64,512]{1,0:T(8,128)S(1)}, u32[]{:S(2)}, u32[]{:S(2)}) collective-permute-start(f32[64,512]{1,0:T(8,128)S(1)} %get-tuple-element.75), channel_id=1, source_target_pairs={{0,6},{1,15},{2,4},{3,13},{4,2},{5,11},{6,0},{7,9},{8,14},{9,7},{1... | collective-permute-start | bytes 393224 | tf_op jit(solution)/shard_map/ppermute | solution.py:662
  57.2 1.6 %collective-permute-start.21 = (f32[64,512]{1,0:T(8,128)S(1)}, f32[64,512]{1,0:T(8,128)S(1)}, u32[]{:S(2)}, u32[]{:S(2)}) collective-permute-start(f32[64,512]{1,0:T(8,128)S(1)} %get-tuple-element.77), channel_id=1, source_target_pairs={{0,2},{1,11},{2,0},{3,9},{4,6},{5,15},{6,4},{7,13},{8,10},{9,3},{1... | collective-permute-start | bytes 393224 | tf_op jit(solution)/shard_map/ppermute | solution.py:662
  59.5 3.2 %collective-permute-done.19.refs_0_ = f32[64,512]{1,0:T(8,128)S(1)} collective-permute-done((f32[64,512]{1,0:T(8,128)S(1)}, f32[64,512]{1,0:T(8,128)S(1)}, u32[]{:S(2)}, u32[]{:S(2)}) %collective-permute-start.19) | collective-permute-done | bytes 131104 | tf_op jit(solution)/shard_map/ppermute | solution.py:662
  62.6 5.6 %collective-permute-done.20.refs_1_ = f32[64,512]{1,0:T(8,128)S(1)} collective-permute-done((f32[64,512]{1,0:T(8,128)S(1)}, f32[64,512]{1,0:T(8,128)S(1)}, u32[]{:S(2)}, u32[]{:S(2)}) %collective-permute-start.20) | collective-permute-done | bytes 131104 | tf_op jit(solution)/shard_map/ppermute | solution.py:662
  70.4 1.9 %to_input_order.1 = f32[1024,128]{1,0:T(8,128)} custom-call(f32[8,128]{1,0:T(8,128)S(1)} %copy-done.1, f32[64,512]{1,0:T(8,128)S(1)} %collective-permute-done.19.refs_0_, f32[64,512]{1,0:T(8,128)S(1)} %collective-permute-done.20.refs_1_, f32[64,512]{1,0:T(8,128)S(1)} %collective-permute-done.21.refs_2_, f32[64,512]{1,0:T(8,128)S(1)} %collective-permute-done.22.refs_3_, ...), custom_call_target="tpu_custom_call" | custom-call | tf_op jit(solution)/shard_map/to_input_order/pallas_call | solution.py:828
  (43 shorter events, 6.4 us)
Async XLA Ops:
  2.7 1.6 %collective-permute-start = (f32[72,512]{1,0:T(8,128)}, f32[72,512]{1,0:T(8,128)S(1)}, u32[]{:S(2)}, u32[]{:S(2)}) collective-permute-start(f32[72,512]{1,0:T(8,128)} %get-tuple-element.43), channel_id=1, source_target_pairs={{0,0},{1,9},{2,2},{3,11},{4,4},{5,13},{6,6},{7,15},{8,8},{9,1},{10... | collective-permute-start | bytes 442376 | tf_op jit(solution)/shard_map/ppermute | solution.py:662
  4.3 8.8 %collective-permute-start.2 = (f32[72,512]{1,0:T(8,128)S(1)}, f32[72,512]{1,0:T(8,128)S(1)}, u32[]{:S(2)}, u32[]{:S(2)}) collective-permute-start(f32[72,512]{1,0:T(8,128)S(1)} %collective-permute-done.refs_0_), channel_id=1, source_target_pairs={{0,4},{2,6},{4,0},{6,2},{1,5},{3,7},{5,1},{7,3},{8,12},{10,14},{12... | collective-permute-start | bytes 442376 | tf_op jit(solution)/shard_map/ppermute | solution.py:691
  8.3 7.5 %collective-permute-start.1 = (f32[72,512]{1,0:T(8,128)S(1)}, f32[72,512]{1,0:T(8,128)S(1)}, u32[]{:S(2)}, u32[]{:S(2)}) collective-permute-start(f32[72,512]{1,0:T(8,128)S(1)} %collective-permute-done.refs_0_), channel_id=1, source_target_pairs={{0,2},{2,0},{4,6},{6,4},{1,3},{3,1},{5,7},{7,5},{8,10},{10,8},{12,... | collective-permute-start | bytes 442376 | tf_op jit(solution)/shard_map/ppermute | solution.py:691
  13.2 5.7 %collective-permute-start.3 = (f32[72,512]{1,0:T(8,128)S(1)}, f32[72,512]{1,0:T(8,128)S(1)}, u32[]{:S(2)}, u32[]{:S(2)}) collective-permute-start(f32[72,512]{1,0:T(8,128)S(1)} %collective-permute-done.2.refs_2_), channel_id=1, source_target_pairs={{0,2},{2,0},{4,6},{6,4},{1,3},{3,1},{5,7},{7,5},{8,10},{10,8},{12,... | collective-permute-start | bytes 442376 | tf_op jit(solution)/shard_map/ppermute | solution.py:691
  18.9 3.2 %collective-permute-start.8 = (f32[4,32,512]{2,1,0:T(8,128)S(1)}, f32[4,32,512]{2,1,0:T(8,128)S(1)}, u32[]{:S(2)}, u32[]{:S(2)}) collective-permute-start(f32[4,32,512]{2,1,0:T(8,128)S(1)} %get-tuple-element.54), channel_id=1, source_target_pairs={{0,1},{1,0},{2,3},{3,2},{4,5},{5,4},{6,7},{7,6},{8,9},{9,8},{10,11... | collective-permute-start | bytes 786440 | tf_op jit(solution)/shard_map/ppermute | solution.py:665
  20.9 4.7 %collective-permute-start.4 = (f32[72,512]{1,0:T(8,128)S(1)}, f32[72,512]{1,0:T(8,128)S(1)}, u32[]{:S(2)}, u32[]{:S(2)}) collective-permute-start(f32[72,512]{1,0:T(8,128)S(1)} %collective-permute-done.refs_0_), channel_id=1, source_target_pairs={{0,1},{1,0},{2,3},{3,2},{4,5},{5,4},{6,7},{7,6},{8,9},{9,8},{10,11... | collective-permute-start | bytes 442376 | tf_op jit(solution)/shard_map/ppermute | solution.py:665
  20.9 4.7 %collective-permute-start.5 = (f32[72,512]{1,0:T(8,128)S(1)}, f32[72,512]{1,0:T(8,128)S(1)}, u32[]{:S(2)}, u32[]{:S(2)}) collective-permute-start(f32[72,512]{1,0:T(8,128)S(1)} %collective-permute-done.1.refs_1_), channel_id=1, source_target_pairs={{0,1},{1,0},{2,3},{3,2},{4,5},{5,4},{6,7},{7,6},{8,9},{9,8},{10,11... | collective-permute-start | bytes 442376 | tf_op jit(solution)/shard_map/ppermute | solution.py:665
  21.4 5.2 %collective-permute-start.6 = (f32[72,512]{1,0:T(8,128)S(1)}, f32[72,512]{1,0:T(8,128)S(1)}, u32[]{:S(2)}, u32[]{:S(2)}) collective-permute-start(f32[72,512]{1,0:T(8,128)S(1)} %collective-permute-done.2.refs_2_), channel_id=1, source_target_pairs={{0,1},{1,0},{2,3},{3,2},{4,5},{5,4},{6,7},{7,6},{8,9},{9,8},{10,11... | collective-permute-start | bytes 442376 | tf_op jit(solution)/shard_map/ppermute | solution.py:665
  21.4 5.8 %collective-permute-start.7 = (f32[72,512]{1,0:T(8,128)S(1)}, f32[72,512]{1,0:T(8,128)S(1)}, u32[]{:S(2)}, u32[]{:S(2)}) collective-permute-start(f32[72,512]{1,0:T(8,128)S(1)} %collective-permute-done.3.refs_3_), channel_id=1, source_target_pairs={{0,1},{1,0},{2,3},{3,2},{4,5},{5,4},{6,7},{7,6},{8,9},{9,8},{10,11... | collective-permute-start | bytes 442376 | tf_op jit(solution)/shard_map/ppermute | solution.py:665
  22.1 10.9 %collective-permute-start.9 = (f32[64,512]{1,0:T(8,128)S(1)}, f32[64,512]{1,0:T(8,128)S(1)}, u32[]{:S(2)}, u32[]{:S(2)}) collective-permute-start(f32[64,512]{1,0:T(8,128)S(1)} %get-tuple-element.55), channel_id=1, source_target_pairs={{0,6},{1,15},{2,4},{3,13},{4,2},{5,11},{6,0},{7,9},{8,14},{9,7},{1... | collective-permute-start | bytes 393224 | tf_op jit(solution)/shard_map/ppermute | solution.py:662
  25.6 11.4 %collective-permute-start.10 = (f32[64,512]{1,0:T(8,128)S(1)}, f32[64,512]{1,0:T(8,128)S(1)}, u32[]{:S(2)}, u32[]{:S(2)}) collective-permute-start(f32[64,512]{1,0:T(8,128)S(1)} %get-tuple-element.56), channel_id=1, source_target_pairs={{0,4},{1,13},{2,6},{3,15},{4,0},{5,9},{6,2},{7,11},{8,12},{9,5},{1... | collective-permute-start | bytes 393224 | tf_op jit(solution)/shard_map/ppermute | solution.py:662
  25.6 11.4 %collective-permute-start.11 = (f32[64,512]{1,0:T(8,128)S(1)}, f32[64,512]{1,0:T(8,128)S(1)}, u32[]{:S(2)}, u32[]{:S(2)}) collective-permute-start(f32[64,512]{1,0:T(8,128)S(1)} %get-tuple-element.57), channel_id=1, source_target_pairs={{0,2},{1,11},{2,0},{3,9},{4,6},{5,15},{6,4},{7,13},{8,10},{9,3},{1... | collective-permute-start | bytes 393224 | tf_op jit(solution)/shard_map/ppermute | solution.py:662
  26.6 10.4 %collective-permute-start.12 = (f32[64,512]{1,0:T(8,128)S(1)}, f32[64,512]{1,0:T(8,128)S(1)}, u32[]{:S(2)}, u32[]{:S(2)}) collective-permute-start(f32[64,512]{1,0:T(8,128)S(1)} %get-tuple-element.58), channel_id=1, source_target_pairs={{0,0},{1,9},{2,2},{3,11},{4,4},{5,13},{6,6},{7,15},{8,8},{9,1},{10... | collective-permute-start | bytes 393224 | tf_op jit(solution)/shard_map/ppermute | solution.py:662
  37.0 1.4 %collective-permute-start.13 = (f32[64,512]{1,0:T(8,128)S(1)}, f32[64,512]{1,0:T(8,128)S(1)}, u32[]{:S(2)}, u32[]{:S(2)}) collective-permute-start(f32[64,512]{1,0:T(8,128)S(1)} %collective-permute-done.9.refs_0_), channel_id=1, source_target_pairs={{0,1},{1,0},{2,3},{3,2},{4,5},{5,4},{6,7},{7,6},{8,9},{9,8},{10,11... | collective-permute-start | bytes 393224 | tf_op jit(solution)/shard_map/ppermute | solution.py:665
  42.1 8.0 %collective-permute-start.17 = (f32[136,128]{1,0:T(8,128)S(1)}, f32[136,128]{1,0:T(8,128)S(1)}, u32[]{:S(2)}, u32[]{:S(2)}) collective-permute-start(f32[136,128]{1,0:T(8,128)S(1)} %get-tuple-element.65), channel_id=1, source_target_pairs={{0,8},{8,0},{1,9},{9,1},{2,10},{10,2},{3,11},{11,3},{4,12},{12,4},... | collective-permute-start | bytes 208904 | tf_op jit(solution)/shard_map/ppermute | solution.py:608
  52.3 2.0 %collective-permute-start.18 = (f32[4,64,512]{2,1,0:T(8,128)S(1)}, f32[4,64,512]{2,1,0:T(8,128)S(1)}, u32[]{:S(2)}, u32[]{:S(2)}) collective-permute-start(f32[4,64,512]{2,1,0:T(8,128)S(1)} %get-tuple-element.74), channel_id=1, source_target_pairs={{0,1},{1,0},{2,3},{3,2},{4,5},{5,4},{6,7},{7,6},{8,9},{9,8},{10,11... | collective-permute-start | bytes 1572872 | tf_op jit(solution)/shard_map/ppermute | solution.py:665
  54.3 8.3 %collective-permute-start.19 = (f32[64,512]{1,0:T(8,128)S(1)}, f32[64,512]{1,0:T(8,128)S(1)}, u32[]{:S(2)}, u32[]{:S(2)}) collective-permute-start(f32[64,512]{1,0:T(8,128)S(1)} %get-tuple-element.75), channel_id=1, source_target_pairs={{0,6},{1,15},{2,4},{3,13},{4,2},{5,11},{6,0},{7,9},{8,14},{9,7},{1... | collective-permute-start | bytes 393224 | tf_op jit(solution)/shard_map/ppermute | solution.py:662
  57.2 11.0 %collective-permute-start.20 = (f32[64,512]{1,0:T(8,128)S(1)}, f32[64,512]{1,0:T(8,128)S(1)}, u32[]{:S(2)}, u32[]{:S(2)}) collective-permute-start(f32[64,512]{1,0:T(8,128)S(1)} %get-tuple-element.76), channel_id=1, source_target_pairs={{0,4},{1,13},{2,6},{3,15},{4,0},{5,9},{6,2},{7,11},{8,12},{9,5},{1... | collective-permute-start | bytes 393224 | tf_op jit(solution)/shard_map/ppermute | solution.py:662
  57.2 11.6 %collective-permute-start.21 = (f32[64,512]{1,0:T(8,128)S(1)}, f32[64,512]{1,0:T(8,128)S(1)}, u32[]{:S(2)}, u32[]{:S(2)}) collective-permute-start(f32[64,512]{1,0:T(8,128)S(1)} %get-tuple-element.77), channel_id=1, source_target_pairs={{0,2},{1,11},{2,0},{3,9},{4,6},{5,15},{6,4},{7,13},{8,10},{9,3},{1... | collective-permute-start | bytes 393224 | tf_op jit(solution)/shard_map/ppermute | solution.py:662
  58.8 10.1 %collective-permute-start.22 = (f32[64,512]{1,0:T(8,128)S(1)}, f32[64,512]{1,0:T(8,128)S(1)}, u32[]{:S(2)}, u32[]{:S(2)}) collective-permute-start(f32[64,512]{1,0:T(8,128)S(1)} %get-tuple-element.78), channel_id=1, source_target_pairs={{0,0},{1,9},{2,2},{3,11},{4,4},{5,13},{6,6},{7,15},{8,8},{9,1},{10... | collective-permute-start | bytes 393224 | tf_op jit(solution)/shard_map/ppermute | solution.py:662
  62.6 6.8 %collective-permute-start.23 = (f32[64,512]{1,0:T(8,128)S(1)}, f32[64,512]{1,0:T(8,128)S(1)}, u32[]{:S(2)}, u32[]{:S(2)}) collective-permute-start(f32[64,512]{1,0:T(8,128)S(1)} %collective-permute-done.19.refs_0_), channel_id=1, source_target_pairs={{0,1},{1,0},{2,3},{3,2},{4,5},{5,4},{6,7},{7,6},{8,9},{9,8},{10,11... | collective-permute-start | bytes 393224 | tf_op jit(solution)/shard_map/ppermute | solution.py:665
  68.2 1.6 %collective-permute-start.24 = (f32[64,512]{1,0:T(8,128)S(1)}, f32[64,512]{1,0:T(8,128)S(1)}, u32[]{:S(2)}, u32[]{:S(2)}) collective-permute-start(f32[64,512]{1,0:T(8,128)S(1)} %collective-permute-done.20.refs_1_), channel_id=1, source_target_pairs={{0,1},{1,0},{2,3},{3,2},{4,5},{5,4},{6,7},{7,6},{8,9},{9,8},{10,11... | collective-permute-start | bytes 393224 | tf_op jit(solution)/shard_map/ppermute | solution.py:665
  68.9 1.3 %collective-permute-start.25 = (f32[64,512]{1,0:T(8,128)S(1)}, f32[64,512]{1,0:T(8,128)S(1)}, u32[]{:S(2)}, u32[]{:S(2)}) collective-permute-start(f32[64,512]{1,0:T(8,128)S(1)} %collective-permute-done.21.refs_2_), channel_id=1, source_target_pairs={{0,1},{1,0},{2,3},{3,2},{4,5},{5,4},{6,7},{7,6},{8,9},{9,8},{10,11... | collective-permute-start | bytes 393224 | tf_op jit(solution)/shard_map/ppermute | solution.py:665
  68.9 1.5 %collective-permute-start.26 = (f32[64,512]{1,0:T(8,128)S(1)}, f32[64,512]{1,0:T(8,128)S(1)}, u32[]{:S(2)}, u32[]{:S(2)}) collective-permute-start(f32[64,512]{1,0:T(8,128)S(1)} %collective-permute-done.22.refs_3_), channel_id=1, source_target_pairs={{0,1},{1,0},{2,3},{3,2},{4,5},{5,4},{6,7},{7,6},{8,9},{9,8},{10,11... | collective-permute-start | bytes 393224 | tf_op jit(solution)/shard_map/ppermute | solution.py:665
  (5 other events, 44.7 us)
